TPU v7x, 32 devices: a whole 2x2x4 slice. The times are simulated.
32 devices in a mesh: groups: 2 (over y), ctx: 4 (over z), exp: 4 (over x, core), rep: 1.
Axes of the slice: x: 2, y: 2, z: 4, core: 2. Of those that a mesh axis runs over, the one named last changes fastest.
Arguments:
- queries: bfloat16 [2, 256, 4096], P('groups', 'ctx', ('exp', 'rep')), parts along dimension 0, may hold values from -16.25 to 16.25
- pages: bfloat16 [2, 2304, 2, 512], P('groups', 'ctx', None, 'exp'), parts along dimension 0, may hold values from -5.2 to 5.2
- cached_lengths: int32 [2, 4], P('groups'), parts along dimension 0, may hold values from 128 to 512
- residual_in: bfloat16 [2, 256, 2048], P('groups', ('ctx', 'exp')), parts along dimension 0, may hold values from -2.390625 to 2.390625
- out_weight: bfloat16 [4096, 2048], P(('exp', 'rep')), may hold values from -0.09375 to 0.09375
- norm_gain: float32 [2048], replicated, may hold values from 0.1 to 1.9
- expert_ids: int32 [2, 256, 8], P('groups', ('ctx', 'exp')), parts along dimension 0, may hold values from 0 to 15, all different within a row; in each aligned block of 16 rows (0 to 15, 16 to 31, ..., all dimensions but the last counted through in order) at most 8 rows name the same one
- route_scores: float32 [2, 256, 8], P('groups', ('ctx', 'exp')), parts along dimension 0, may hold values from 0.05 to 1
- expert_input: bfloat16 [16, 2048, 2, 384], P(('ctx', 'exp'), None, None, 'rep'), may hold values from -0.125 to 0.125
- expert_output: bfloat16 [16, 384, 2048], P(('ctx', 'exp'), 'rep'), may hold values from -0.3125 to 0.3125
Outputs:
- context: bfloat16 [2, 256, 4096], P('groups', 'ctx', ('exp', 'rep')), parts along dimension 0
- layer_out: bfloat16 [2, 256, 2048], P('groups', ('ctx', 'exp', 'rep')), parts along dimension 0
There are 2 independent parts, one for each index of `groups`. A program takes and returns all parts, laid end to end along the dimension named above; an argument that names none is the same for every part. Nothing has to cross between parts.
Inputs may be any that keep to these rules, and one draw needn't show every extreme that they name: `expert_ids`: in every aligned block of 16 positions of one request, no expert is named by more than 8 of the block's rows, and in some blocks one expert by exactly 8; the 8 experts of a row differ.
All inputs are finite; a program needn't handle non-finite values.
Results may differ from a plain program's by a relative error of at most 0.015.
Values may be sent and summed in bfloat16 or wider, within the bound.
No kernel may reach another device: no remote copies, remote signals or barrier semaphores. Data moves between devices by JAX's collectives and lax.ppermute only.
A program may use at most 128 MiB of HBM per device.

v0:
```python
import jax
import jax.numpy as jnp
from jax import lax
from jax.sharding import PartitionSpec as P

HEAD = 128


floor_value = -1e30
norm_epsilon = 1e-06


def normalize(hidden, norm_gain):
    widened = hidden.astype(jnp.float32)
    mean_square = jnp.mean(widened * widened, axis=-1, keepdims=True)
    return (widened * lax.rsqrt(mean_square + norm_epsilon) * norm_gain).astype(jnp.bfloat16)


def attend_piece(query_rows, page_rows, allowed):
    scaling = query_rows.shape[-1] ** (-0.5)
    scores = (
        jnp.einsum(
            "rqhe,rke->rqhk", query_rows, page_rows[:, :, 0], preferred_element_type=jnp.float32
        )
        * scaling
    )
    permitted = allowed[:, :, None, :]
    masked = jnp.where(permitted, scores, floor_value)
    peaks = jnp.max(masked, axis=-1)
    weights = jnp.where(permitted, jnp.exp(masked - peaks[..., None]), 0.0)
    totals = jnp.sum(weights, axis=-1)
    summed = jnp.einsum(
        "rqhk,rke->rqhe",
        weights.astype(jnp.bfloat16),
        page_rows[:, :, 1],
        preferred_element_type=jnp.float32,
    )
    return (peaks, totals, summed)


def merge_partials(earlier, later):
    peaks = jnp.maximum(earlier[0], later[0])
    later_scale = jnp.exp(later[0] - peaks)
    totals = later[1] * later_scale
    summed = later[2] * later_scale[..., None]
    return (peaks, totals, summed)


def rows_mask(row_index, lengths, query_positions, slab_size, fresh_block):
    page_size = slab_size + fresh_block
    page_number = row_index // page_size
    offset = row_index - page_number * page_size
    page_count = lengths.shape[1]
    picker = page_number[None, :] == jnp.arange(page_count, dtype=jnp.int32)[:, None]
    live_length = jnp.sum(jnp.where(picker[None], lengths[:, :, None], 0), axis=1)
    in_cache = (offset < slab_size)[None, :] & (offset[None, :] < live_length)
    fresh_position = page_number * fresh_block + offset - slab_size
    in_fresh = (offset >= slab_size)[None, :] & (
        fresh_position[None, :] <= query_positions[:, None]
    )
    return in_cache[:, None, :] | in_fresh[None, :, :]


def per_device(
    queries,
    pages,
    cached_lengths,
    residual_in,
    out_weight,
    norm_gain,
    expert_ids,
    route_scores,
    expert_input,
    expert_output,
):
    requests, fresh_block, query_width = queries.shape
    local_heads = query_width // HEAD
    core_place = lax.axis_index("rep")
    page_place = lax.axis_index("ctx")
    rep_count = lax.axis_size("rep")
    page_size = pages.shape[1]
    slab_size = page_size - fresh_block
    own_positions = page_place * fresh_block + jnp.arange(fresh_block, dtype=jnp.int32)
    query_rows = queries.reshape(requests, fresh_block, local_heads, HEAD)
    start_state = (
        jnp.full((requests, fresh_block, local_heads), floor_value, jnp.float32),
        jnp.zeros((requests, fresh_block, local_heads), jnp.float32),
        jnp.zeros((requests, fresh_block, local_heads, HEAD), jnp.float32),
    )
    page_piece = lax.all_gather(pages, "ctx", axis=1, tiled=True)
    row_index = jnp.arange(page_piece.shape[1], dtype=jnp.int32)
    allowed = rows_mask(row_index, cached_lengths, own_positions, slab_size, fresh_block)
    peaks, totals, summed = merge_partials(
        start_state, attend_piece(query_rows, page_piece, allowed)
    )
    context = (
        (summed / totals[..., None])
        .astype(jnp.bfloat16)
        .reshape(requests, fresh_block, query_width)
    )
    projected = jnp.dot(
        context.reshape(requests * fresh_block, query_width),
        out_weight,
        preferred_element_type=jnp.float32,
    ).reshape(requests, fresh_block, -1)
    token_block = residual_in.shape[1]
    share_size = token_block // rep_count
    own_share = lax.psum_scatter(
        projected.astype(jnp.bfloat16), ("exp", "rep"), scatter_dimension=1, tiled=True
    ).astype(jnp.float32)
    own_residual = lax.dynamic_slice_in_dim(residual_in, core_place * share_size, share_size, 1)
    own_hidden = (own_residual.astype(jnp.float32) + own_share).astype(jnp.bfloat16)
    normed = lax.all_gather(normalize(own_hidden, norm_gain), "rep", axis=1, tiled=True)
    top_count = expert_ids.shape[2]
    expert_count = lax.axis_size("ctx") * lax.axis_size("exp")
    most_rows = max(2, (token_block * top_count + expert_count - 1) // expert_count)
    capacity = requests * most_rows
    model_width = normed.shape[2]
    token_count = requests * token_block
    flat_ids = expert_ids.reshape(-1)
    row_count = flat_ids.shape[0]
    chosen = (flat_ids[:, None] == jnp.arange(expert_count, dtype=jnp.int32)[None, :]).astype(
        jnp.int32
    )
    earlier_rows = jnp.cumsum(chosen, axis=0) - chosen
    slot_rank = jnp.sum(earlier_rows * chosen, axis=1)
    slot_index = flat_ids * capacity + slot_rank
    slot_onehot = (
        slot_index[:, None] == jnp.arange(expert_count * capacity, dtype=jnp.int32)[None, :]
    ).astype(jnp.bfloat16)
    token_onehot = (
        (jnp.arange(row_count, dtype=jnp.int32) // top_count)[:, None]
        == jnp.arange(token_count, dtype=jnp.int32)[None, :]
    ).astype(jnp.bfloat16)
    placement = jnp.dot(slot_onehot.T, token_onehot, preferred_element_type=jnp.float32).astype(
        jnp.bfloat16
    )
    outgoing = jnp.dot(
        placement, normed.reshape(token_count, model_width), preferred_element_type=jnp.float32
    )
    outgoing = outgoing.astype(jnp.bfloat16).reshape(expert_count, capacity, model_width)
    scores_sum = jnp.sum(route_scores, axis=2, keepdims=True)
    combine = (route_scores / scores_sum).astype(jnp.bfloat16).reshape(-1)
    gathering = jnp.dot(
        (token_onehot * combine[:, None]).T, slot_onehot, preferred_element_type=jnp.float32
    ).astype(jnp.bfloat16)
    gate_up = expert_input[0]
    down_weight = expert_output[0]
    arrived_rows = lax.all_to_all(outgoing, ("ctx", "exp"), split_axis=0, concat_axis=0, tiled=True)
    inner_rows = jnp.einsum(
        "nd,dgh->ngh",
        arrived_rows.reshape(-1, model_width),
        gate_up,
        preferred_element_type=jnp.float32,
    )
    activated = (jax.nn.silu(inner_rows[:, 0]) * inner_rows[:, 1]).astype(jnp.bfloat16)
    result = jnp.dot(activated, down_weight, preferred_element_type=jnp.float32).astype(
        jnp.bfloat16
    )
    returned = lax.all_to_all(
        result.reshape(arrived_rows.shape), ("ctx", "exp"), split_axis=0, concat_axis=0, tiled=True
    )
    mixture = jnp.dot(
        gathering,
        returned.reshape(expert_count * capacity, model_width),
        preferred_element_type=jnp.float32,
    )
    own_mixture = lax.psum_scatter(
        mixture.reshape(requests, token_block, model_width).astype(jnp.bfloat16),
        "rep",
        scatter_dimension=1,
        tiled=True,
    ).astype(jnp.float32)
    layer_out = (own_hidden.astype(jnp.float32) + own_mixture).astype(jnp.bfloat16)
    return (context, layer_out)


def solution(mesh):
    in_specs = (
        P("groups", "ctx", ("exp", "rep")),
        P("groups", "ctx", None, "exp"),
        P("groups", None),
        P("groups", ("ctx", "exp"), None),
        P(("exp", "rep"), None),
        P(),
        P("groups", ("ctx", "exp"), None),
        P("groups", ("ctx", "exp"), None),
        P(("ctx", "exp"), None, None, "rep"),
        P(("ctx", "exp"), "rep", None),
    )
    out_specs = (P("groups", "ctx", ("exp", "rep")), P("groups", ("ctx", "exp", "rep"), None))
    return jax.shard_map(
        per_device, mesh=mesh, in_specs=in_specs, out_specs=out_specs, check_vma=False
    )
```

profile of v0, /device:TPU:0, one launch (start us, length us, event | category | flops | bytes accessed | tf_op | source)
XLA Modules:
  0.0 121.7 jit_solution(10408529155012849360)
XLA Ops:
  7.2 0.0 copy-start
  7.2 0.0 all-gather.2.cloned.1.call-start
  7.2 1.9 %copy.20 = bf16[1,576,2,128]{3,1,2,0:T(8,128)(2,1)} copy(bf16[1,576,2,128]{3,2,1,0:T(2,128)(2,1)} %param.11) | data formatting | bytes 589824 | tf_op args[1]
  9.1 0.0 all-gather.2.cloned.1.call-update
  9.1 0.0 reduce-scatter.2.cloned.1.call-start
  9.2 0.9 copy.24
  10.1 0.8 copy.22
  10.9 0.1 reshape.327
  11.0 0.8 select_reduce_fusion.1
  11.8 0.2 and_or_fusion
  12.0 30.8 %all-gather.2.cloned.1.call-done = bf16[1,2304,2,128]{3,1,2,0:T(8,128)(2,1)} async-done(((bf16[1,576,2,128]{3,1,2,0:T(8,128)(2,1)}), bf16[1,2304,2,128]{3,1,2,0:T(8,128)(2,1)}) %all-gather.2.cloned.1.call-update) | async-done | bytes 1179664 | tf_op jit(solution)/shard_map/all_gather | solution.py:90
  42.8 0.0 copy-start.5
  42.8 2.5 %fusion.70 = (f32[64,8]{1,0:T(8,128)S(1)}, f32[64,8,2304]{2,1,0:T(8,128)S(1)}) fusion(bf16[64,8,128]{2,1,0:T(8,128)(2,1)S(1)} %bitcast.57, bf16[1,2304,2,128]{3,1,2,0:T(8,128)(2,1)} %all-gather.2.cloned.1.call-done, pred[64,2304]{1,0:T(8,128)(4,1)S(1)} %and_or_fusion), kind=kOutput, calls=%fused_computation.88 | convolution fusion | flops 305528320 | bytes 5588992 | tf_op jit(solution)/shard_map/rqhe,rke->rqhk/dot_general | solution.py:22
  45.2 1.3 %fusion.1 = f32[64,8]{1,0:T(8,128)S(1)} fusion(f32[64,8,2304]{2,1,0:T(8,128)S(1)} %get-tuple-element.5, f32[64,8]{1,0:T(8,128)S(1)} %get-tuple-element.4, pred[64,2304]{1,0:T(8,128)(4,1)S(1)} %and_or_fusion), kind=kLoop, calls=%fused_computation.3 | loop fusion | flops 3538432 | bytes 4870144 | tf_op jit(solution)/shard_map/reduce_sum | solution.py:31
  46.5 0.0 copy-start.1
  46.5 0.0 copy-done.5
  46.6 1.1 fusion.24
  47.6 0.0 copy-start.3
  47.7 0.0 copy-start.7
  47.7 1.0 copy-done.1
  48.7 1.5 %fusion.12 = bf16[1,64,2048]{2,1,0:T(8,128)(2,1)} fusion(bf16[1024,2048]{1,0:T(8,128)(2,1)S(1)} %copy-done.1, bf16[8,8,8,128]{3,2,1,0:T(8,128)(2,1)S(1)} %bitcast.56), kind=kOutput, calls=%fused_computation.16 | convolution fusion | flops 268566528 | bytes 4587520 | tf_op jit(solution)/shard_map/dot_general | solution.py:101
  50.2 0.0 reduce-scatter.2.cloned.1.call-update
  50.3 0.1 fusion.41
  50.4 0.2 reduce_window_sum.11
  50.5 0.2 select_reduce_fusion
  50.7 18.9 %reduce-scatter.2.cloned.1.call-done = bf16[1,16,2048]{2,1,0:T(8,128)(2,1)} async-done(((bf16[1,64,2048]{2,1,0:T(8,128)(2,1)}), bf16[1,16,2048]{2,1,0:T(8,128)(2,1)}) %reduce-scatter.2.cloned.1.call-update) | async-done | bytes 65552 | tf_op jit(solution)/shard_map/reduce_scatter | solution.py:108
  69.6 0.0 copy-done.3
  69.6 1.0 fusion.30
  70.6 0.0 copy-done.7
  70.6 2.2 %fusion.10 = bf16[16,8,2048]{2,1,0:T(8,128)(2,1)} fusion(f32[2048]{0:T(1024)S(1)} %copy-done.7, f32[16]{0:T(128)S(1)} %add_rsqrt_fusion, s32[128]{0:T(128)S(1)} %get-tuple-element.9, s32[128]{0:T(128)S(1)} %get-tuple-element.8, bf16[1,16,2048]{2,1,0:T(8,128)(2,1)} %reduce-scatter.2.cloned.1.call-done, bf16[1,16,2048]{2,1,0:T(8,128)(2,1)S(1)} %copy-done.3), kind=kOutput, calls=%fused_computation.13 | convolution fusion | flops 9457664 | bytes 664640 | tf_op jit(solution)/shard_map/dot_general | solution.py:138
  72.8 0.0 copy-start.2
  72.8 19.3 %all_to_all.10 = bf16[16,8,2048]{2,1,0:T(8,128)(2,1)S(1)} all-to-all(bf16[16,8,2048]{2,1,0:T(8,128)(2,1)} %fusion.10), channel_id=1, replica_groups=mesh['groups'=2,'ctx'=4,'exp'=4,'rep'=1] {'ctx','exp'}, dimensions={0} | all-to-all | bytes 1048576 | tf_op jit(solution)/shard_map/all_to_all | solution.py:149
  92.2 0.0 copy-done
  92.2 0.0 copy-start.6
  92.2 0.0 copy-start.4
  92.2 0.6 fusion.3
  92.8 0.0 copy-done.2
  92.8 1.3 %fusion.11 = bf16[16,8,2048]{2,1,0:T(8,128)(2,1)} fusion(bf16[1,384,2048]{2,1,0:T(8,128)(2,1)S(1)} %copy-done.2, f32[128,2,384]{2,0,1:T(8,128)S(1)} %fusion.3), kind=kOutput, calls=%fused_computation.14 | convolution fusion | flops 201883648 | bytes 2490368 | tf_op jit(solution)/shard_map/dot_general | solution.py:157
  94.1 4.2 %all-to-all-start.1 = ((bf16[16,8,2048]{2,1,0:T(8,128)(2,1)}), bf16[16,8,2048]{2,1,0:T(8,128)(2,1)}, u32[]{:S(2)}, u32[]{:S(2)}) async-start(bf16[16,8,2048]{2,1,0:T(8,128)(2,1)} %fusion.11), calls=%async_computation.2 | async-start | bytes 1048576 | tf_op jit(solution)/shard_map/all_to_all | solution.py:160
  98.3 0.0 copy-done.6
  98.4 0.1 copy.21
  98.5 0.1 mul.119
  98.6 0.7 reshape.326
  99.3 13.5 %all-to-all-done.1 = bf16[16,8,2048]{2,1,0:T(8,128)(2,1)} async-done(((bf16[16,8,2048]{2,1,0:T(8,128)(2,1)}), bf16[16,8,2048]{2,1,0:T(8,128)(2,1)}, u32[]{:S(2)}, u32[]{:S(2)}) %all-to-all-start.1) | async-done | bytes 524320 | tf_op jit(solution)/shard_map/all_to_all | solution.py:160
  112.8 0.0 copy-done.4
  112.8 2.1 %fusion.16 = bf16[1,16,2048]{2,1,0:T(8,128)(2,1)} fusion(bf16[16,8,2048]{2,1,0:T(8,128)(2,1)} %all-to-all-done.1, s32[128]{0:T(128)S(1)} %get-tuple-element.9, s32[128]{0:T(128)S(1)} %get-tuple-element.8, bf16[128]{0:T(256)(128)(2,1)S(1)} %mul.119, bf16[1,16,2048]{2,1,0:T(8,128)(2,1)S(1)} %copy-done.4, bf16[1,16,2048]{2,1,0:T(8,128)(2,1)S(1)} %copy-done.3), kind=kOutput, calls=%fused_computation.21 | convolution fusion | flops 9230336 | bytes 722176 | tf_op jit(solution)/shard_map/dot_general | solution.py:163
  (9 shorter events, 0.1 us)
Async XLA Ops:
  7.2 85.0 %copy-start = (bf16[1,2048,2,384]{3,2,1,0:T(2,128)(2,1)S(1)}, bf16[1,2048,2,384]{3,2,1,0:T(2,128)(2,1)}, u32[]{:S(2)}) copy-start(bf16[1,2048,2,384]{3,2,1,0:T(2,128)(2,1)} %param.18) | copy-start | bytes 9437188
  7.2 35.6 %all-gather.2.cloned.1.call-start = ((), (), s32[]{:S(2)}) async-start(), calls=%async_computation.3 | async-start | bytes 1474560 | tf_op jit(solution)/shard_map/all_gather | solution.py:90
  9.1 60.5 %reduce-scatter.2.cloned.1.call-start = ((), (), s32[]{:S(2)}) async-start(), calls=%async_computation.4 | async-start | bytes 327680 | tf_op jit(solution)/shard_map/reduce_scatter | solution.py:108
  42.8 3.8 %copy-start.5 = (bf16[1,2304,2,128]{3,1,2,0:T(8,128)(2,1)S(1)}, bf16[1,2304,2,128]{3,1,2,0:T(8,128)(2,1)}, u32[]{:S(2)}) copy-start(bf16[1,2304,2,128]{3,1,2,0:T(8,128)(2,1)} %all-gather.2.cloned.1.call-done) | copy-start | bytes 3538948
  46.5 2.2 %copy-start.1 = (bf16[1024,2048]{1,0:T(8,128)(2,1)S(1)}, bf16[1024,2048]{1,0:T(8,128)(2,1)}, u32[]{:S(2)}) copy-start(bf16[1024,2048]{1,0:T(8,128)(2,1)} %param.14) | copy-start | bytes 12582916
  47.6 22.0 %copy-start.3 = (bf16[1,16,2048]{2,1,0:T(8,128)(2,1)S(1)}, bf16[1,16,2048]{2,1,0:T(8,128)(2,1)}, u32[]{:S(2)}) copy-start(bf16[1,16,2048]{2,1,0:T(8,128)(2,1)} %param.13) | copy-start | bytes 196612
  47.7 23.0 %copy-start.7 = (f32[2048]{0:T(1024)S(1)}, f32[2048]{0:T(1024)}, u32[]{:S(2)}) copy-start(f32[2048]{0:T(1024)} %param.15) | copy-start | bytes 24580
  72.8 20.0 %copy-start.2 = (bf16[1,384,2048]{2,1,0:T(8,128)(2,1)S(1)}, bf16[1,384,2048]{2,1,0:T(8,128)(2,1)}, u32[]{:S(2)}) copy-start(bf16[1,384,2048]{2,1,0:T(8,128)(2,1)} %param.19) | copy-start | bytes 4718596
  92.2 6.2 %copy-start.6 = (f32[1,16,8]{1,2,0:T(8,128)S(1)}, f32[1,16,8]{1,2,0:T(8,128)}, u32[]{:S(2)}) copy-start(f32[1,16,8]{1,2,0:T(8,128)} %param.17) | copy-start | bytes 1540
  92.2 20.6 %copy-start.4 = (bf16[1,16,2048]{2,1,0:T(8,128)(2,1)S(1)}, bf16[1,16,2048]{2,1,0:T(8,128)(2,1)}, u32[]{:S(2)}) copy-start(bf16[1,16,2048]{2,1,0:T(8,128)(2,1)} %reduce-scatter.2.cloned.1.call-done) | copy-start | bytes 196612
  94.1 18.7 %all-to-all-start.1 = ((bf16[16,8,2048]{2,1,0:T(8,128)(2,1)}), bf16[16,8,2048]{2,1,0:T(8,128)(2,1)}, u32[]{:S(2)}, u32[]{:S(2)}) async-start(bf16[16,8,2048]{2,1,0:T(8,128)(2,1)} %fusion.11), calls=%async_computation.2 | async-start | bytes 1048576 | tf_op jit(solution)/shard_map/all_to_all | solution.py:160
Sparse Core Ops, SparseCore 0:
  9.6 33.1 all-gather.1
  50.4 19.1 reduce-scatter.1
where the time goes:
time: 122 us
  waiting for transfers between devices  63.2 us (52%)
  blocking collectives  19.3 us (16%)
  between operations  14.2 us (12%)
  matrix products  11.3 us (9%)
  local copies, waits for them, and re-layouts  5.62 us (5%)
  starting transfers between devices  4.31 us (4%)
  other arithmetic  3.74 us (3%)
    all_gather x1, waiting for transfers between devices, per_device(): page_piece = lax.all_gather(pages, 'ctx', axis=1, tiled=True)  30.8 us
    all_to_all x1, blocking collectives, per_device(): lax.all_to_all(outgoing, ('ctx', 'exp'), split_axis=0, concat_axis=0, til...  19.3 us
    reduce_scatter x1, waiting for transfers between devices, per_device(): lax.psum_scatter(projected.astype(jnp.bfloat16), ('exp', 'rep'), scatter_...  18.9 us
    all_to_all x1, waiting for transfers between devices, per_device(): lax.all_to_all(result.reshape(arrived_rows.shape), ('ctx', 'exp'), split_...  13.5 us
    unnamed x19, local copies, waits for them, and re-layouts  4.63 us
    all_to_all x1, starting transfers between devices, per_device(): lax.all_to_all(result.reshape(arrived_rows.shape), ('ctx', 'exp'), split_...  4.23 us
    dot_general x1, matrix products, attend_piece(): jnp.einsum('rqhe,rke->rqhk', query_rows, page_rows[:, :, 0], preferred_el...  2.46 us
  transfers between devices with their start and end apart: 3, of which 3 were waited for; matrix products, arithmetic and copies ran while one was open for 3% of the time, Pallas kernels for 0%

commit v1 on v0

v1 whole, which is shorter than its diff:
```python
import functools

import jax
import jax.numpy as jnp
from jax import lax
from jax.experimental import pallas as pl
from jax.experimental.pallas import tpu as pltpu
from jax.sharding import PartitionSpec as P

HEAD = 128

floor_value = -1e30
norm_epsilon = 1e-06


def normalize(hidden, norm_gain):
    widened = hidden.astype(jnp.float32)
    mean_square = jnp.mean(widened * widened, axis=-1, keepdims=True)
    return (widened * lax.rsqrt(mean_square + norm_epsilon) * norm_gain).astype(jnp.bfloat16)


def partner(index, step, count):
    if count & (count - 1) == 0:
        return index ^ step
    return lax.rem(index + step, count)


def swap(value, axis, step):
    count = lax.axis_size(axis)
    pow2 = count & (count - 1) == 0
    pairs = [(i, (i ^ step) if pow2 else (i + step) % count) for i in range(count)]
    return lax.ppermute(value, axis, pairs)


def shift(value, axis, step):
    count = lax.axis_size(axis)
    return lax.ppermute(value, axis, [(i, (i + step) % count) for i in range(count)])


def stack_heads(queries):
    heads = queries.shape[1] // HEAD
    return jnp.concatenate(
        [queries[:, h * HEAD : (h + 1) * HEAD] for h in range(heads)], axis=0
    )


def page_partial(stacked, keys, values, page, length, place, fresh_block):
    rows, page_size = stacked.shape[0], keys.shape[0]
    slab_size = page_size - fresh_block
    scores = lax.dot_general(
        stacked, keys, (((1,), (1,)), ((), ())), preferred_element_type=jnp.float32
    )
    offset = lax.broadcasted_iota(jnp.int32, (fresh_block, page_size), 1)
    position = place * fresh_block + lax.broadcasted_iota(
        jnp.int32, (fresh_block, page_size), 0
    )
    in_cache = (offset < slab_size) & (offset < length)
    in_fresh = (offset >= slab_size) & (page * fresh_block + offset - slab_size <= position)
    bias = jnp.where(in_cache | in_fresh, 0.0, floor_value)
    masked = scores + jnp.concatenate([bias] * (rows // fresh_block), axis=0)
    peak = jnp.max(masked, axis=1, keepdims=True)
    weights = jnp.exp((masked - peak) * (HEAD**-0.5))
    total = jnp.sum(weights, axis=1, keepdims=True)
    summed = jnp.dot(weights.astype(jnp.bfloat16), values, preferred_element_type=jnp.float32)
    return peak, total, summed


def merge(first, second):
    peak = jnp.maximum(first[0], second[0])
    scale_first = jnp.exp((first[0] - peak) * (HEAD**-0.5))
    scale_second = jnp.exp((second[0] - peak) * (HEAD**-0.5))
    return (
        peak,
        first[1] * scale_first + second[1] * scale_second,
        first[2] * scale_first + second[2] * scale_second,
    )


def early_kernel(count, fresh_block, info, queries, *refs):
    pages, (peak_out, total_out, summed_out) = refs[: 2 * count], refs[2 * count :]
    stacked = stack_heads(queries[...])
    state = None
    for number in range(count):
        part = page_partial(
            stacked,
            pages[2 * number][...],
            pages[2 * number + 1][...],
            info[1 + 2 * number],
            info[2 + 2 * number],
            info[0],
            fresh_block,
        )
        state = part if state is None else merge(state, part)
    peak_out[...] = state[0]
    total_out[...] = state[1]
    summed_out[...] = state[2]


def late_kernel(fresh_block, info, queries, keys, values, peak, total, summed, context_out):
    stacked = stack_heads(queries[...])
    part = page_partial(
        stacked, keys[...], values[...], info[1], info[2], info[0], fresh_block
    )
    state = merge((peak[...], total[...], summed[...]), part)
    result = (state[2] / state[1]).astype(jnp.bfloat16)
    for h in range(result.shape[0] // fresh_block):
        context_out[:, h * HEAD : (h + 1) * HEAD] = result[
            h * fresh_block : (h + 1) * fresh_block
        ]


def whole_specs(count):
    return [pl.BlockSpec(memory_space=pltpu.VMEM)] * count


def attention(queries, pages, lengths):
    fresh_block, width = queries.shape
    heads = width // HEAD
    stacked_rows = heads * fresh_block
    place = lax.axis_index("ctx")
    count = lax.axis_size("ctx")
    own_keys, own_values = pages[:, 0], pages[:, 1]
    held = [(place, own_keys, own_values)]
    from_left, from_right = (own_keys, own_values), (own_keys, own_values)
    for step in range(1, (count - 1) // 2 + 1):
        from_left = tuple(shift(part, "ctx", 1) for part in from_left)
        from_right = tuple(shift(part, "ctx", -1) for part in reversed(from_right))[::-1]
        held.append((lax.rem(place - step + count, count), *from_left))
        held.append((lax.rem(place + step, count), *from_right))
    if count % 2 == 0:
        last = (
            lax.rem(place + count // 2, count),
            shift(from_left[0], "ctx", 1),
            shift(from_right[1], "ctx", -1),
        )
    else:
        last = held.pop()

    def info_of(parts):
        numbers = [place]
        for page, _, _ in parts:
            numbers += [page, lax.dynamic_index_in_dim(lengths, page, 0, keepdims=False)]
        return jnp.stack(numbers).astype(jnp.int32)

    smem = pl.BlockSpec(memory_space=pltpu.SMEM)
    column = jax.ShapeDtypeStruct((stacked_rows, 1), jnp.float32)
    limit = pltpu.CompilerParams(vmem_limit_bytes=32 * 1024 * 1024)
    page_flops = 4 * stacked_rows * pages.shape[0] * HEAD

    state = None
    for start in range(0, len(held), 3):
        group = held[start : start + 3]
        operands = [part for _, keys, values in group for part in (keys, values)]
        partial_state = pl.pallas_call(
            functools.partial(early_kernel, len(group), fresh_block),
            out_shape=(column, column, jax.ShapeDtypeStruct((stacked_rows, HEAD), jnp.float32)),
            in_specs=[smem] + whole_specs(1 + len(operands)),
            out_specs=tuple(whole_specs(3)),
            compiler_params=limit,
            cost_estimate=pl.CostEstimate(
                flops=len(group) * page_flops, bytes_accessed=2 << 20, transcendentals=0
            ),
        )(info_of(group), queries, *operands)
        state = partial_state if state is None else merge(state, partial_state)
    return pl.pallas_call(
        functools.partial(late_kernel, fresh_block),
        out_shape=jax.ShapeDtypeStruct(queries.shape, jnp.bfloat16),
        in_specs=[smem] + whole_specs(6),
        out_specs=whole_specs(1)[0],
        compiler_params=limit,
        cost_estimate=pl.CostEstimate(
            flops=page_flops, bytes_accessed=1 << 20, transcendentals=0
        ),
    )(info_of([last]), queries, last[1], last[2], *state)


def scatter_sum(blocks):
    count = lax.axis_size("exp")
    place = lax.axis_index("exp")
    pick = lambda index: lax.dynamic_index_in_dim(blocks, index, 0, keepdims=False)
    arrived = [
        swap(pick(partner(place, step, count)), "exp", step) for step in reversed(range(1, count))
    ]
    total = pick(place).astype(jnp.float32)
    for part in arrived:
        total = total + part.astype(jnp.float32)
    return total


def exp_strides():
    count = lax.axis_size("exp")
    if count & (count - 1) == 0:
        return [1 << bit for bit in range(count.bit_length() - 1)]
    return None


def gather_rows(rows):
    count = lax.axis_size("ctx")
    column = jnp.stack([rows] + [shift(rows, "ctx", step) for step in range(1, count)])
    strides = exp_strides()
    if strides is None:
        parts = [column] + [swap(column, "exp", step) for step in range(1, lax.axis_size("exp"))]
        return jnp.concatenate(parts)
    held = [column]
    for stride in reversed(strides):
        held = held + [swap(part, "exp", stride) for part in held]
    return jnp.concatenate(held)


def give_back(blocks):
    count = lax.axis_size("ctx")
    strides = exp_strides()
    groups = blocks.shape[0] // count
    held = [blocks[i * count : (i + 1) * count] for i in range(groups)]
    if strides is None:
        size = lax.axis_size("exp")
        total = held[0].astype(jnp.float32)
        for step in range(1, size):
            total = total + swap(held[step], "exp", size - step).astype(jnp.float32)
        column = total
    else:
        for stride in strides:
            half = len(held) // 2
            arrived = [swap(part.astype(jnp.bfloat16), "exp", stride) for part in held[half:]]
            held = [
                keep.astype(jnp.float32) + new.astype(jnp.float32)
                for keep, new in zip(held[:half], arrived)
            ]
        column = held[0].astype(jnp.float32)
    sent = column.astype(jnp.bfloat16)
    total = column[0]
    for step in range(1, count):
        total = total + shift(sent[step], "ctx", -step).astype(jnp.float32)
    return total


def per_device(
    queries,
    pages,
    cached_lengths,
    residual_in,
    out_weight,
    norm_gain,
    expert_ids,
    route_scores,
    expert_input,
    expert_output,
):
    requests, fresh_block, query_width = queries.shape
    core_place = lax.axis_index("rep")
    rep_count = lax.axis_size("rep")
    exp_count = lax.axis_size("exp")
    expert_count = lax.axis_size("ctx") * exp_count
    token_block, model_width = residual_in.shape[1:]
    token_count = requests * token_block
    expert = lax.axis_index("ctx") * exp_count + lax.axis_index("exp")

    combine = (route_scores / jnp.sum(route_scores, axis=2, keepdims=True)).astype(jnp.bfloat16)
    named = expert_ids[..., None] == jnp.arange(expert_count, dtype=jnp.int32)
    dense = jnp.sum(jnp.where(named, combine[..., None], 0).astype(jnp.float32), axis=2)
    dense = dense.astype(jnp.bfloat16).reshape(token_count, expert_count)
    all_dense = gather_rows(dense).reshape(-1, expert_count)
    own_column = jnp.arange(expert_count, dtype=jnp.int32) == expert
    own_weight = jnp.sum(jnp.where(own_column, all_dense.astype(jnp.float32), 0.0), axis=1)

    context = jnp.stack(
        [attention(queries[r], pages[r], cached_lengths[r]) for r in range(requests)]
    )
    projected = jnp.dot(
        context.reshape(requests * fresh_block, query_width),
        out_weight,
        preferred_element_type=jnp.float32,
    ).astype(jnp.bfloat16)
    blocks = projected.reshape(requests, exp_count, token_block, model_width)
    blocks = blocks.transpose(1, 0, 2, 3)
    share = scatter_sum(blocks)
    share_size = token_block // rep_count
    if rep_count > 1:
        share = lax.psum_scatter(
            share.astype(jnp.bfloat16), "rep", scatter_dimension=1, tiled=True
        ).astype(jnp.float32)
    own_residual = lax.dynamic_slice_in_dim(residual_in, core_place * share_size, share_size, 1)
    own_hidden = (own_residual.astype(jnp.float32) + share).astype(jnp.bfloat16)
    normed = normalize(own_hidden, norm_gain)
    if rep_count > 1:
        normed = lax.all_gather(normed, "rep", axis=1, tiled=True)

    arrived = gather_rows(normed.reshape(token_count, model_width))
    inner = jnp.einsum(
        "nd,dgh->ngh",
        arrived.reshape(-1, model_width),
        expert_input[0],
        preferred_element_type=jnp.float32,
    )
    activated = (jax.nn.silu(inner[:, 0]) * inner[:, 1]).astype(jnp.bfloat16)
    piece = jnp.dot(activated, expert_output[0], preferred_element_type=jnp.float32)
    piece = piece.astype(jnp.bfloat16).astype(jnp.float32)
    scaled = (piece * own_weight[:, None]).astype(jnp.bfloat16)
    mixture = give_back(scaled.reshape(arrived.shape)).reshape(requests, token_block, model_width)
    if rep_count > 1:
        mixture = lax.psum_scatter(
            mixture.astype(jnp.bfloat16), "rep", scatter_dimension=1, tiled=True
        ).astype(jnp.float32)
    layer_out = (own_hidden.astype(jnp.float32) + mixture).astype(jnp.bfloat16)
    return (context, layer_out)


def solution(mesh):
    in_specs = (
        P("groups", "ctx", ("exp", "rep")),
        P("groups", "ctx", None, "exp"),
        P("groups", None),
        P("groups", ("ctx", "exp"), None),
        P(("exp", "rep"), None),
        P(),
        P("groups", ("ctx", "exp"), None),
        P("groups", ("ctx", "exp"), None),
        P(("ctx", "exp"), None, None, "rep"),
        P(("ctx", "exp"), "rep", None),
    )
    out_specs = (P("groups", "ctx", ("exp", "rep")), P("groups", ("ctx", "exp", "rep"), None))
    return jax.shard_map(
        per_device, mesh=mesh, in_specs=in_specs, out_specs=out_specs, check_vma=False
    )
```

time: 122 us -> 92.7 us (0.76)
  waiting for transfers between devices: 63.2 us -> 37.9 us
  starting transfers between devices: 4.31 us -> 26.8 us
  blocking collectives: 19.3 us -> 0 us
  between operations: 14.2 us -> 0.82 us
  Pallas kernels: 0 us -> 6 us
  matrix products: 11.3 us -> 6.16 us
  local copies, waits for them, and re-layouts: 5.62 us -> 10.4 us
    ppermute x0 -> x27, waiting for transfers between devices: none -> 37.9 us  [the longest x12 22.1 us: swap(): return lax.ppermute(value, axis, pairs)]
    all_gather x1 -> x0, waiting for transfers between devices: 30.8 us -> none  [per_device(): page_piece = lax.all_gather(pages, 'ctx', axis=1, tiled=True)]
    ppermute x0 -> x27, starting transfers between devices: none -> 26.8 us  [the longest x15 20.6 us: shift(): lax.ppermute(value, axis, [(i, (i + step) % count) for i in range(count)])]
    all_to_all x1 -> x0, blocking collectives: 19.3 us -> none  [per_device(): lax.all_to_all(outgoing, ('ctx', 'exp'), split_axis=0, concat_axis=0, til...]
    reduce_scatter x1 -> x0, waiting for transfers between devices: 18.9 us -> none  [per_device(): lax.psum_scatter(projected.astype(jnp.bfloat16), ('exp', 'rep'), scatter_...]
    all_to_all x1 -> x0, waiting for transfers between devices: 13.5 us -> none  [per_device(): lax.all_to_all(result.reshape(arrived_rows.shape), ('ctx', 'exp'), split_...]
    dot_general x6 -> x2, matrix products: 9.76 us -> 3.06 us  [the longest x1 2.33 us: per_device(): jnp.einsum('nd,dgh->ngh', arrived.reshape(-1, model_width), expert_input[...]
    pallas_call x0 -> x2, Pallas kernels: none -> 6 us  [the longest x1 3.17 us: attention(): pl.pallas_call(functools.partial(early_kernel, len(group), fresh_block),...]
  transfers between devices with their start and end apart: 3 -> 27, of which waited for: 3 -> 15; matrix products, arithmetic and copies ran while one was open for 3% -> 13% of each run, Pallas kernels for 0% -> 6%
where the time goes in v1:
time: 92.7 us; the launch traced here: 92.4 us
  waiting for transfers between devices  37.9 us (41%)
  starting transfers between devices  26.8 us (29%)
  local copies, waits for them, and re-layouts  10.4 us (11%)
  matrix products  6.16 us (7%)
  Pallas kernels  6 us (6%)
  other arithmetic  4.33 us (5%)
    ppermute x12, waiting for transfers between devices, swap(): return lax.ppermute(value, axis, pairs)  22.1 us
    ppermute x15, starting transfers between devices, shift(): lax.ppermute(value, axis, [(i, (i + step) % count) for i in range(count)])  20.6 us
    ppermute x15, waiting for transfers between devices, shift(): lax.ppermute(value, axis, [(i, (i + step) % count) for i in range(count)])  15.8 us
    ppermute x12, starting transfers between devices, swap(): return lax.ppermute(value, axis, pairs)  6.2 us
    unnamed x22, local copies, waits for them, and re-layouts  5.28 us
    pallas_call x1, Pallas kernels, attention(): pl.pallas_call(functools.partial(early_kernel, len(group), fresh_block),...  3.17 us
    dot_general x1, matrix products, per_device(): jnp.dot(context.reshape(requests * fresh_block, query_width), out_weight,...  3.11 us
    pallas_call x1, Pallas kernels, attention(): pl.pallas_call(functools.partial(late_kernel, fresh_block), out_shape=jax...  2.83 us
  transfers between devices with their start and end apart: 27, of which 15 were waited for; matrix products, arithmetic and copies ran while one was open for 13% of the time, Pallas kernels for 6%

profile of v1, /device:TPU:0, one launch (start us, length us, event | category | flops | bytes accessed | tf_op | source)
XLA Modules:
  0.0 92.4 jit_solution(5276998614455028627)
XLA Ops:
  0.6 0.9 reduce_sum.42
  1.5 0.8 fusion.25
  2.4 0.8 copy.20
  3.3 5.1 %collective-permute-start.17 = (bf16[16,16]{1,0:T(8,128)(2,1)S(1)}, bf16[16,16]{1,0:T(8,128)(2,1)S(1)}, u32[]{:S(2)}, u32[]{:S(2)}) collective-permute-start(bf16[16,16]{1,0:T(8,128)(2,1)S(1)} %fusion.24), channel_id=1, source_target_pairs={{0,12},{4,0},{8,4},{12,8},{1,13},{5,1},{9,5},{13,9},{2,14},{6,2},{... | collective-permute-start | bytes 1544 | tf_op jit(solution)/shard_map/ppermute | solution.py:37
  8.4 1.0 %collective-permute-start.15 = (bf16[16,16]{1,0:T(8,128)(2,1)S(1)}, bf16[16,16]{1,0:T(8,128)(2,1)S(1)}, u32[]{:S(2)}, u32[]{:S(2)}) collective-permute-start(bf16[16,16]{1,0:T(8,128)(2,1)S(1)} %fusion.24), channel_id=1, source_target_pairs={{0,4},{4,8},{8,12},{12,0},{1,5},{5,9},{9,13},{13,1},{2,6},{6,10},{... | collective-permute-start | bytes 1544 | tf_op jit(solution)/shard_map/ppermute | solution.py:37
  9.4 1.0 %copy.25 = bf16[1,576,2,128]{3,1,2,0:T(8,128)(2,1)S(1)} copy(bf16[1,576,2,128]{3,2,1,0:T(2,128)(2,1)} %param.11) | data formatting | bytes 589824 | tf_op args[1]
  10.4 2.5 %collective-permute-start.4 = (bf16[576,128]{1,0:T(8,128)(2,1)S(1)}, bf16[576,128]{1,0:T(8,128)(2,1)}, u32[]{:S(2)}, u32[]{:S(2)}) collective-permute-start(bf16[576,128]{1,0:T(8,128)(2,1)S(1)} %get-tuple-element.18.refs_1_), channel_id=1, source_target_pairs={{0,4},{4,8},{8,12},{12,0},{1,5},{5,9},{9,13},{13,1},{2,6},{6,10},{... | collective-permute-start | bytes 442376 | tf_op jit(solution)/shard_map/ppermute | solution.py:37
  12.9 1.3 %collective-permute-start.2 = (bf16[576,128]{1,0:T(8,128)(2,1)S(1)}, bf16[576,128]{1,0:T(8,128)(2,1)}, u32[]{:S(2)}, u32[]{:S(2)}) collective-permute-start(bf16[576,128]{1,0:T(8,128)(2,1)S(1)} %get-tuple-element.18.refs_1_), channel_id=1, source_target_pairs={{0,12},{4,0},{8,4},{12,8},{1,13},{5,1},{9,5},{13,9},{2,14},{6,2},{... | collective-permute-start | bytes 442376 | tf_op jit(solution)/shard_map/ppermute | solution.py:37
  14.3 1.5 %constant_dynamic-slice_fusion = (s32[1,1]{1,0:T(1,128)}, s32[1,1]{1,0:T(1,128)}, s32[1,1]{1,0:T(1,128)}, s32[1,1]{1,0:T(1,128)}) fusion(s32[1,4]{1,0:T(1,128)} %param.12, s32[]{:T(128)S(6)} %select_n.47, s32[]{:T(128)S(6)} %select_n.45, s32[]{:T(128)S(6)} %select_n.44, s32[]{:T(128)S(6)} %select_n.46), kind=kLoop, calls=%fused_computation.62 | loop fusion | bytes 48 | tf_op jit(solution)/shard_map/jit(dynamic_index_in_dim)/dynamic_slice | solution.py:142
  15.8 0.7 pad_add_fusion.info
  16.4 1.9 %stack.56.info = s32[7]{0:T(128)S(1)} concatenate(s32[1]{0:T(128)} %bitcast, s32[1]{0:T(128)} %bitcast, s32[1]{0:T(128)} %bitcast.7, s32[1]{0:T(128)} %bitcast.8, s32[1]{0:T(128)} %bitcast.9, s32[1]{0:T(128)} %bitcast.10, s32[1]{0:T(128)} %bitcast.11), dimensions={0} | concatenate | bytes 56 | tf_op jit(solution)/shard_map/stack | solution.py:143
  18.3 1.0 %collective-permute-start.5 = (bf16[576,128]{1,0:T(8,128)(2,1)S(1)}, bf16[576,128]{1,0:T(8,128)(2,1)S(1)}, u32[]{:S(2)}, u32[]{:S(2)}) collective-permute-start(bf16[576,128]{1,0:T(8,128)(2,1)S(1)} %get-tuple-element.19.refs_0_), channel_id=1, source_target_pairs={{0,12},{4,0},{8,4},{12,8},{1,13},{5,1},{9,5},{13,9},{2,14},{6,2},{... | collective-permute-start | bytes 442376 | tf_op jit(solution)/shard_map/ppermute | solution.py:37
  19.4 1.0 %collective-permute-start = (bf16[576,128]{1,0:T(8,128)(2,1)S(1)}, bf16[576,128]{1,0:T(8,128)(2,1)S(1)}, u32[]{:S(2)}, u32[]{:S(2)}) collective-permute-start(bf16[576,128]{1,0:T(8,128)(2,1)S(1)} %get-tuple-element.19.refs_0_), channel_id=1, source_target_pairs={{0,4},{4,8},{8,12},{12,0},{1,5},{5,9},{9,13},{13,1},{2,6},{6,10},{... | collective-permute-start | bytes 442376 | tf_op jit(solution)/shard_map/ppermute | solution.py:37
  20.4 1.6 %collective-permute-start.18 = (bf16[4,16,16]{2,1,0:T(8,128)(2,1)S(1)}, bf16[4,16,16]{2,1,0:T(8,128)(2,1)S(1)}, u32[]{:S(2)}, u32[]{:S(2)}) collective-permute-start(bf16[4,16,16]{2,1,0:T(8,128)(2,1)S(1)} %pad_maximum_fusion.1), channel_id=1, source_target_pairs={{0,2},{1,3},{2,0},{3,1},{4,6},{5,7},{6,4},{7,5},{8,10},{9,11},{10,... | collective-permute-start | bytes 6152 | tf_op jit(solution)/shard_map/ppermute | solution.py:32
  22.0 2.2 %collective-permute-done.18 = bf16[4,16,16]{2,1,0:T(8,128)(2,1)S(1)} collective-permute-done((bf16[4,16,16]{2,1,0:T(8,128)(2,1)S(1)}, bf16[4,16,16]{2,1,0:T(8,128)(2,1)S(1)}, u32[]{:S(2)}, u32[]{:S(2)}) %collective-permute-start.18) | collective-permute-done | bytes 2080 | tf_op jit(solution)/shard_map/ppermute | solution.py:32
  24.2 1.2 %collective-permute-done.19 = bf16[4,16,16]{2,1,0:T(8,128)(2,1)S(1)} collective-permute-done((bf16[4,16,16]{2,1,0:T(8,128)(2,1)S(1)}, bf16[4,16,16]{2,1,0:T(8,128)(2,1)S(1)}, u32[]{:S(2)}, u32[]{:S(2)}) %collective-permute-start.19) | collective-permute-done | bytes 2080 | tf_op jit(solution)/shard_map/ppermute | solution.py:32
  25.6 2.8 %collective-permute-start.3 = (bf16[576,128]{1,0:T(8,128)(2,1)}, bf16[576,128]{1,0:T(8,128)(2,1)S(1)}, u32[]{:S(2)}, u32[]{:S(2)}) collective-permute-start(bf16[576,128]{1,0:T(8,128)(2,1)} %collective-permute-done.2.refs_5_), channel_id=1, source_target_pairs={{0,12},{4,0},{8,4},{12,8},{1,13},{5,1},{9,5},{13,9},{2,14},{6,2},{... | collective-permute-start | bytes 442376 | tf_op jit(solution)/shard_map/ppermute | solution.py:37
  28.4 0.9 copy-done.1
  29.3 3.2 %shard_map.113 = (f32[512,1]{1,0:T(8,128)S(1)}, f32[512,1]{1,0:T(8,128)S(1)}, f32[512,128]{1,0:T(8,128)S(1)}) custom-call(s32[7]{0:T(128)S(1)} %stack.56.info, bf16[64,1024]{1,0:T(8,128)(2,1)S(1)} %bitcast.90, bf16[576,128]{1,0:T(8,128)(2,1)S(1)} %get-tuple-element.19.refs_0_, bf16[576,128]{1,0:T(8,128)(2,1)S(1)} %get-tuple-element.18.refs_1_, ...), custom_call_target="tpu_custom_call" | custom-call | flops 452984832 | bytes 2097152 | tf_op jit(solution)/shard_map/pallas_call | solution.py:154
  32.9 3.2 %collective-permute-done.1.keys = bf16[576,128]{1,0:T(8,128)(2,1)S(1)} collective-permute-done((bf16[576,128]{1,0:T(8,128)(2,1)S(1)}, bf16[576,128]{1,0:T(8,128)(2,1)S(1)}, u32[]{:S(2)}, u32[]{:S(2)}) %collective-permute-start.1) | collective-permute-done | bytes 147488 | tf_op jit(solution)/shard_map/ppermute | solution.py:37
  36.1 2.8 %shard_map.114 = bf16[64,1024]{1,0:T(8,128)(2,1)} custom-call(s32[3]{0:T(128)S(1)} %pad_add_fusion.info, bf16[64,1024]{1,0:T(8,128)(2,1)S(1)} %bitcast.91, bf16[576,128]{1,0:T(8,128)(2,1)S(1)} %collective-permute-done.1.keys, bf16[576,128]{1,0:T(8,128)(2,1)S(1)} %collective-permute-done.3.values, f32[512,1]{1,0:T(8,128)S(1)} %get-tuple-element.5.peak, ...), custom_call_target="tpu_custom_call" | custom-call | flops 150994944 | bytes 1048576 | tf_op jit(solution)/shard_map/pallas_call | solution.py:165
  38.9 3.1 %convolution_convert_fusion.1 = bf16[64,2048]{1,0:T(8,128)(2,1)S(1)} fusion(bf16[64,1024]{1,0:T(8,128)(2,1)} %shard_map.114, bf16[1024,2048]{1,0:T(8,128)(2,1)} %param.14), kind=kOutput, calls=%fused_computation.6 | convolution fusion | flops 268566528 | bytes 4587520 | tf_op jit(solution)/shard_map/dot_general | solution.py:269
  42.6 1.1 %collective-permute-start.7 = (bf16[1,16,2048]{2,1,0:T(8,128)(2,1)S(1)}, bf16[1,16,2048]{2,1,0:T(8,128)(2,1)S(1)}, u32[]{:S(2)}, u32[]{:S(2)}) collective-permute-start(bf16[1,16,2048]{2,1,0:T(8,128)(2,1)S(1)} %get-tuple-element.24), channel_id=1, source_target_pairs={{0,2},{1,3},{2,0},{3,1},{4,6},{5,7},{6,4},{7,5},{8,10},{9,11},{10,... | collective-permute-start | bytes 196616 | tf_op jit(solution)/shard_map/ppermute | solution.py:32
  44.0 2.5 %collective-permute-done.6 = bf16[1,16,2048]{2,1,0:T(8,128)(2,1)S(1)} collective-permute-done((bf16[1,16,2048]{2,1,0:T(8,128)(2,1)S(1)}, bf16[1,16,2048]{2,1,0:T(8,128)(2,1)S(1)}, u32[]{:S(2)}, u32[]{:S(2)}) %collective-permute-start.6) | collective-permute-done | bytes 65568 | tf_op jit(solution)/shard_map/ppermute | solution.py:32
  46.5 1.5 %collective-permute-done.7 = bf16[1,16,2048]{2,1,0:T(8,128)(2,1)S(1)} collective-permute-done((bf16[1,16,2048]{2,1,0:T(8,128)(2,1)S(1)}, bf16[1,16,2048]{2,1,0:T(8,128)(2,1)S(1)}, u32[]{:S(2)}, u32[]{:S(2)}) %collective-permute-start.7) | collective-permute-done | bytes 65568 | tf_op jit(solution)/shard_map/ppermute | solution.py:32
  48.1 0.7 constant_dynamic-update-slice_fusion.6
  48.8 1.6 %collective-permute-start.11 = (bf16[16,2048]{1,0:T(8,128)(2,1)S(1)}, bf16[16,2048]{1,0:T(8,128)(2,1)S(1)}, u32[]{:S(2)}, u32[]{:S(2)}) collective-permute-start(bf16[16,2048]{1,0:T(8,128)(2,1)S(1)} %bitcast.98), channel_id=1, source_target_pairs={{0,12},{4,0},{8,4},{12,8},{1,13},{5,1},{9,5},{13,9},{2,14},{6,2},{... | collective-permute-start | bytes 196616 | tf_op jit(solution)/shard_map/ppermute | solution.py:37
  50.5 1.6 %collective-permute-start.10 = (bf16[16,2048]{1,0:T(8,128)(2,1)S(1)}, bf16[16,2048]{1,0:T(8,128)(2,1)S(1)}, u32[]{:S(2)}, u32[]{:S(2)}) collective-permute-start(bf16[16,2048]{1,0:T(8,128)(2,1)S(1)} %bitcast.99), channel_id=1, source_target_pairs={{0,8},{4,12},{8,0},{12,4},{1,9},{5,13},{9,1},{13,5},{2,10},{6,14},... | collective-permute-start | bytes 196616 | tf_op jit(solution)/shard_map/ppermute | solution.py:37
  52.3 0.8 collective-permute-done.11
  53.1 5.4 %collective-permute-done.10 = bf16[16,2048]{1,0:T(8,128)(2,1)S(1)} collective-permute-done((bf16[16,2048]{1,0:T(8,128)(2,1)S(1)}, bf16[16,2048]{1,0:T(8,128)(2,1)S(1)}, u32[]{:S(2)}, u32[]{:S(2)}) %collective-permute-start.10) | collective-permute-done | bytes 65568 | tf_op jit(solution)/shard_map/ppermute | solution.py:37
  58.7 0.9 %collective-permute-start.12 = (bf16[4,16,2048]{2,1,0:T(8,128)(2,1)S(1)}, bf16[4,16,2048]{2,1,0:T(8,128)(2,1)S(1)}, u32[]{:S(2)}, u32[]{:S(2)}) collective-permute-start(bf16[4,16,2048]{2,1,0:T(8,128)(2,1)S(1)} %pad_maximum_fusion), channel_id=1, source_target_pairs={{0,2},{1,3},{2,0},{3,1},{4,6},{5,7},{6,4},{7,5},{8,10},{9,11},{10,... | collective-permute-start | bytes 786440 | tf_op jit(solution)/shard_map/ppermute | solution.py:32
  59.6 0.6 constant_dynamic-update-slice_fusion.5
  60.2 0.6 constant_dynamic-update-slice_fusion.4
  60.9 0.6 constant_dynamic-update-slice_fusion.3
  61.5 5.9 %collective-permute-done.12 = bf16[4,16,2048]{2,1,0:T(8,128)(2,1)S(1)} collective-permute-done((bf16[4,16,2048]{2,1,0:T(8,128)(2,1)S(1)}, bf16[4,16,2048]{2,1,0:T(8,128)(2,1)S(1)}, u32[]{:S(2)}, u32[]{:S(2)}) %collective-permute-start.12) | collective-permute-done | bytes 262176 | tf_op jit(solution)/shard_map/ppermute | solution.py:32
  67.4 0.7 constant_dynamic-update-slice_fusion.2
  68.1 0.7 constant_dynamic-update-slice_fusion.1
  68.9 0.7 constant_dynamic-update-slice_fusion
  69.7 2.3 %fusion = f32[256,2,384]{2,0,1:T(8,128)S(1)} fusion(bf16[256,2048,1]{1,0,2:T(8,128)(2,1)} %bitcast.110, bf16[2048,2,384]{2,1,0:T(2,128)(2,1)S(1)} %bitcast.89), kind=kOutput, calls=%fused_computation | convolution fusion | flops 805306368 | bytes 4980736 | tf_op jit(solution)/shard_map/nd,dgh->ngh/dot_general | solution.py:289
  72.0 0.7 fusion.4
  73.4 1.1 %collective-permute-done.22 = bf16[4,16,2048]{2,1,0:T(8,128)(2,1)S(1)} collective-permute-done((bf16[4,16,2048]{2,1,0:T(8,128)(2,1)S(1)}, bf16[4,16,2048]{2,1,0:T(8,128)(2,1)S(1)}, u32[]{:S(2)}, u32[]{:S(2)}) %collective-permute-start.22) | collective-permute-done | bytes 262176 | tf_op jit(solution)/shard_map/ppermute | solution.py:32
  74.6 0.9 %collective-permute-start.23 = (bf16[4,16,2048]{2,1,0:T(8,128)(2,1)S(1)}, bf16[4,16,2048]{2,1,0:T(8,128)(2,1)S(1)}, u32[]{:S(2)}, u32[]{:S(2)}) collective-permute-start(bf16[4,16,2048]{2,1,0:T(8,128)(2,1)S(1)} %fusion.6), channel_id=1, source_target_pairs={{0,2},{1,3},{2,0},{3,1},{4,6},{5,7},{6,4},{7,5},{8,10},{9,11},{10,... | collective-permute-start | bytes 786440 | tf_op jit(solution)/shard_map/ppermute | solution.py:32
  75.5 7.7 %collective-permute-done.23 = bf16[4,16,2048]{2,1,0:T(8,128)(2,1)S(1)} collective-permute-done((bf16[4,16,2048]{2,1,0:T(8,128)(2,1)S(1)}, bf16[4,16,2048]{2,1,0:T(8,128)(2,1)S(1)}, u32[]{:S(2)}, u32[]{:S(2)}) %collective-permute-start.23) | collective-permute-done | bytes 262176 | tf_op jit(solution)/shard_map/ppermute | solution.py:32
  83.8 1.6 %collective-permute-start.26 = (bf16[16,2048]{1,0:T(8,128)(2,1)S(1)}, bf16[16,2048]{1,0:T(8,128)(2,1)S(1)}, u32[]{:S(2)}, u32[]{:S(2)}) collective-permute-start(bf16[16,2048]{1,0:T(8,128)(2,1)S(1)} %get-tuple-element.21), channel_id=1, source_target_pairs={{0,4},{4,8},{8,12},{12,0},{1,5},{5,9},{9,13},{13,1},{2,6},{6,10},{... | collective-permute-start | bytes 196616 | tf_op jit(solution)/shard_map/ppermute | solution.py:37
  85.8 2.6 %collective-permute-done.24 = bf16[16,2048]{1,0:T(8,128)(2,1)S(1)} collective-permute-done((bf16[16,2048]{1,0:T(8,128)(2,1)S(1)}, bf16[16,2048]{1,0:T(8,128)(2,1)S(1)}, u32[]{:S(2)}, u32[]{:S(2)}) %collective-permute-start.24) | collective-permute-done | bytes 65568 | tf_op jit(solution)/shard_map/ppermute | solution.py:37
  88.4 1.5 %collective-permute-done.26 = bf16[16,2048]{1,0:T(8,128)(2,1)S(1)} collective-permute-done((bf16[16,2048]{1,0:T(8,128)(2,1)S(1)}, bf16[16,2048]{1,0:T(8,128)(2,1)S(1)}, u32[]{:S(2)}, u32[]{:S(2)}) %collective-permute-start.26) | collective-permute-done | bytes 65568 | tf_op jit(solution)/shard_map/ppermute | solution.py:37
  89.9 1.9 %collective-permute-done.25 = bf16[16,2048]{1,0:T(8,128)(2,1)S(1)} collective-permute-done((bf16[16,2048]{1,0:T(8,128)(2,1)S(1)}, bf16[16,2048]{1,0:T(8,128)(2,1)S(1)}, u32[]{:S(2)}, u32[]{:S(2)}) %collective-permute-start.25) | collective-permute-done | bytes 65568 | tf_op jit(solution)/shard_map/ppermute | solution.py:37
  91.7 0.7 fusion.14
  (58 shorter events, 4.0 us)
Async XLA Ops:
  0.6 69.0 %copy-start = (bf16[1,2048,2,384]{3,2,1,0:T(2,128)(2,1)S(1)}, bf16[1,2048,2,384]{3,2,1,0:T(2,128)(2,1)}, u32[]{:S(2)}) copy-start(bf16[1,2048,2,384]{3,2,1,0:T(2,128)(2,1)} %param.18) | copy-start | bytes 9437188
  3.3 15.1 %collective-permute-start.17 = (bf16[16,16]{1,0:T(8,128)(2,1)S(1)}, bf16[16,16]{1,0:T(8,128)(2,1)S(1)}, u32[]{:S(2)}, u32[]{:S(2)}) collective-permute-start(bf16[16,16]{1,0:T(8,128)(2,1)S(1)} %fusion.24), channel_id=1, source_target_pairs={{0,12},{4,0},{8,4},{12,8},{1,13},{5,1},{9,5},{13,9},{2,14},{6,2},{... | collective-permute-start | bytes 1544 | tf_op jit(solution)/shard_map/ppermute | solution.py:37
  8.4 11.0 %collective-permute-start.16 = (bf16[16,16]{1,0:T(8,128)(2,1)S(1)}, bf16[16,16]{1,0:T(8,128)(2,1)S(1)}, u32[]{:S(2)}, u32[]{:S(2)}) collective-permute-start(bf16[16,16]{1,0:T(8,128)(2,1)S(1)} %fusion.24), channel_id=1, source_target_pairs={{0,8},{4,12},{8,0},{12,4},{1,9},{5,13},{9,1},{13,5},{2,10},{6,14},... | collective-permute-start | bytes 1544 | tf_op jit(solution)/shard_map/ppermute | solution.py:37
  8.4 12.0 %collective-permute-start.15 = (bf16[16,16]{1,0:T(8,128)(2,1)S(1)}, bf16[16,16]{1,0:T(8,128)(2,1)S(1)}, u32[]{:S(2)}, u32[]{:S(2)}) collective-permute-start(bf16[16,16]{1,0:T(8,128)(2,1)S(1)} %fusion.24), channel_id=1, source_target_pairs={{0,4},{4,8},{8,12},{12,0},{1,5},{5,9},{9,13},{13,1},{2,6},{6,10},{... | collective-permute-start | bytes 1544 | tf_op jit(solution)/shard_map/ppermute | solution.py:37
  10.4 18.0 %collective-permute-start.4 = (bf16[576,128]{1,0:T(8,128)(2,1)S(1)}, bf16[576,128]{1,0:T(8,128)(2,1)}, u32[]{:S(2)}, u32[]{:S(2)}) collective-permute-start(bf16[576,128]{1,0:T(8,128)(2,1)S(1)} %get-tuple-element.18.refs_1_), channel_id=1, source_target_pairs={{0,4},{4,8},{8,12},{12,0},{1,5},{5,9},{9,13},{13,1},{2,6},{6,10},{... | collective-permute-start | bytes 442376 | tf_op jit(solution)/shard_map/ppermute | solution.py:37
  12.9 12.6 %collective-permute-start.2 = (bf16[576,128]{1,0:T(8,128)(2,1)S(1)}, bf16[576,128]{1,0:T(8,128)(2,1)}, u32[]{:S(2)}, u32[]{:S(2)}) collective-permute-start(bf16[576,128]{1,0:T(8,128)(2,1)S(1)} %get-tuple-element.18.refs_1_), channel_id=1, source_target_pairs={{0,12},{4,0},{8,4},{12,8},{1,13},{5,1},{9,5},{13,9},{2,14},{6,2},{... | collective-permute-start | bytes 442376 | tf_op jit(solution)/shard_map/ppermute | solution.py:37
  18.3 10.1 %collective-permute-start.5 = (bf16[576,128]{1,0:T(8,128)(2,1)S(1)}, bf16[576,128]{1,0:T(8,128)(2,1)S(1)}, u32[]{:S(2)}, u32[]{:S(2)}) collective-permute-start(bf16[576,128]{1,0:T(8,128)(2,1)S(1)} %get-tuple-element.19.refs_0_), channel_id=1, source_target_pairs={{0,12},{4,0},{8,4},{12,8},{1,13},{5,1},{9,5},{13,9},{2,14},{6,2},{... | collective-permute-start | bytes 442376 | tf_op jit(solution)/shard_map/ppermute | solution.py:37
  19.4 9.0 %collective-permute-start = (bf16[576,128]{1,0:T(8,128)(2,1)S(1)}, bf16[576,128]{1,0:T(8,128)(2,1)S(1)}, u32[]{:S(2)}, u32[]{:S(2)}) collective-permute-start(bf16[576,128]{1,0:T(8,128)(2,1)S(1)} %get-tuple-element.19.refs_0_), channel_id=1, source_target_pairs={{0,4},{4,8},{8,12},{12,0},{1,5},{5,9},{9,13},{13,1},{2,6},{6,10},{... | collective-permute-start | bytes 442376 | tf_op jit(solution)/shard_map/ppermute | solution.py:37
  20.4 3.8 %collective-permute-start.18 = (bf16[4,16,16]{2,1,0:T(8,128)(2,1)S(1)}, bf16[4,16,16]{2,1,0:T(8,128)(2,1)S(1)}, u32[]{:S(2)}, u32[]{:S(2)}) collective-permute-start(bf16[4,16,16]{2,1,0:T(8,128)(2,1)S(1)} %pad_maximum_fusion.1), channel_id=1, source_target_pairs={{0,2},{1,3},{2,0},{3,1},{4,6},{5,7},{6,4},{7,5},{8,10},{9,11},{10,... | collective-permute-start | bytes 6152 | tf_op jit(solution)/shard_map/ppermute | solution.py:32
  24.2 1.2 %collective-permute-start.19 = (bf16[4,16,16]{2,1,0:T(8,128)(2,1)S(1)}, bf16[4,16,16]{2,1,0:T(8,128)(2,1)S(1)}, u32[]{:S(2)}, u32[]{:S(2)}) collective-permute-start(bf16[4,16,16]{2,1,0:T(8,128)(2,1)S(1)} %pad_maximum_fusion.1), channel_id=1, source_target_pairs={{0,1},{1,0},{2,3},{3,2},{4,5},{5,4},{6,7},{7,6},{8,9},{9,8},{10,11... | collective-permute-start | bytes 6152 | tf_op jit(solution)/shard_map/ppermute | solution.py:32
  25.4 18.6 %collective-permute-start.20 = (bf16[4,16,16]{2,1,0:T(8,128)(2,1)S(1)}, bf16[4,16,16]{2,1,0:T(8,128)(2,1)S(1)}, u32[]{:S(2)}, u32[]{:S(2)}) collective-permute-start(bf16[4,16,16]{2,1,0:T(8,128)(2,1)S(1)} %collective-permute-done.18), channel_id=1, source_target_pairs={{0,1},{1,0},{2,3},{3,2},{4,5},{5,4},{6,7},{7,6},{8,9},{9,8},{10,11... | collective-permute-start | bytes 6152 | tf_op jit(solution)/shard_map/ppermute | solution.py:32
  25.6 7.4 %collective-permute-start.3 = (bf16[576,128]{1,0:T(8,128)(2,1)}, bf16[576,128]{1,0:T(8,128)(2,1)S(1)}, u32[]{:S(2)}, u32[]{:S(2)}) collective-permute-start(bf16[576,128]{1,0:T(8,128)(2,1)} %collective-permute-done.2.refs_5_), channel_id=1, source_target_pairs={{0,12},{4,0},{8,4},{12,8},{1,13},{5,1},{9,5},{13,9},{2,14},{6,2},{... | collective-permute-start | bytes 442376 | tf_op jit(solution)/shard_map/ppermute | solution.py:37
  28.4 7.7 %collective-permute-start.1 = (bf16[576,128]{1,0:T(8,128)(2,1)S(1)}, bf16[576,128]{1,0:T(8,128)(2,1)S(1)}, u32[]{:S(2)}, u32[]{:S(2)}) collective-permute-start(bf16[576,128]{1,0:T(8,128)(2,1)S(1)} %collective-permute-done.refs_2_), channel_id=1, source_target_pairs={{0,4},{4,8},{8,12},{12,0},{1,5},{5,9},{9,13},{13,1},{2,6},{6,10},{... | collective-permute-start | bytes 442376 | tf_op jit(solution)/shard_map/ppermute | solution.py:37
  28.4 0.9 copy-start.1
  36.1 11.8 %copy-start.2 = (bf16[1,16,2048]{2,1,0:T(8,128)(2,1)S(1)}, bf16[1,16,2048]{2,1,0:T(8,128)(2,1)}, u32[]{:S(2)}) copy-start(bf16[1,16,2048]{2,1,0:T(8,128)(2,1)} %param.13) | copy-start | bytes 196612
  36.1 12.0 %copy-start.3 = (f32[2048]{0:T(1024)S(1)}, f32[2048]{0:T(1024)}, u32[]{:S(2)}) copy-start(f32[2048]{0:T(1024)} %param.15) | copy-start | bytes 24580
  42.1 4.4 %collective-permute-start.6 = (bf16[1,16,2048]{2,1,0:T(8,128)(2,1)S(1)}, bf16[1,16,2048]{2,1,0:T(8,128)(2,1)S(1)}, u32[]{:S(2)}, u32[]{:S(2)}) collective-permute-start(bf16[1,16,2048]{2,1,0:T(8,128)(2,1)S(1)} %get-tuple-element.23), channel_id=1, source_target_pairs={{0,3},{1,2},{2,1},{3,0},{4,7},{5,6},{6,5},{7,4},{8,11},{9,10},{10,... | collective-permute-start | bytes 196616 | tf_op jit(solution)/shard_map/ppermute | solution.py:32
  42.6 5.4 %collective-permute-start.7 = (bf16[1,16,2048]{2,1,0:T(8,128)(2,1)S(1)}, bf16[1,16,2048]{2,1,0:T(8,128)(2,1)S(1)}, u32[]{:S(2)}, u32[]{:S(2)}) collective-permute-start(bf16[1,16,2048]{2,1,0:T(8,128)(2,1)S(1)} %get-tuple-element.24), channel_id=1, source_target_pairs={{0,2},{1,3},{2,0},{3,1},{4,6},{5,7},{6,4},{7,5},{8,10},{9,11},{10,... | collective-permute-start | bytes 196616 | tf_op jit(solution)/shard_map/ppermute | solution.py:32
  43.7 4.2 %collective-permute-start.8 = (bf16[1,16,2048]{2,1,0:T(8,128)(2,1)S(1)}, bf16[1,16,2048]{2,1,0:T(8,128)(2,1)S(1)}, u32[]{:S(2)}, u32[]{:S(2)}) collective-permute-start(bf16[1,16,2048]{2,1,0:T(8,128)(2,1)S(1)} %get-tuple-element.25), channel_id=1, source_target_pairs={{0,1},{1,0},{2,3},{3,2},{4,5},{5,4},{6,7},{7,6},{8,9},{9,8},{10,11... | collective-permute-start | bytes 196616 | tf_op jit(solution)/shard_map/ppermute | solution.py:32
  48.8 4.3 %collective-permute-start.11 = (bf16[16,2048]{1,0:T(8,128)(2,1)S(1)}, bf16[16,2048]{1,0:T(8,128)(2,1)S(1)}, u32[]{:S(2)}, u32[]{:S(2)}) collective-permute-start(bf16[16,2048]{1,0:T(8,128)(2,1)S(1)} %bitcast.98), channel_id=1, source_target_pairs={{0,12},{4,0},{8,4},{12,8},{1,13},{5,1},{9,5},{13,9},{2,14},{6,2},{... | collective-permute-start | bytes 196616 | tf_op jit(solution)/shard_map/ppermute | solution.py:37
  50.5 8.1 %collective-permute-start.10 = (bf16[16,2048]{1,0:T(8,128)(2,1)S(1)}, bf16[16,2048]{1,0:T(8,128)(2,1)S(1)}, u32[]{:S(2)}, u32[]{:S(2)}) collective-permute-start(bf16[16,2048]{1,0:T(8,128)(2,1)S(1)} %bitcast.99), channel_id=1, source_target_pairs={{0,8},{4,12},{8,0},{12,4},{1,9},{5,13},{9,1},{13,5},{2,10},{6,14},... | collective-permute-start | bytes 196616 | tf_op jit(solution)/shard_map/ppermute | solution.py:37
  52.1 6.5 %collective-permute-start.9 = (bf16[16,2048]{1,0:T(8,128)(2,1)S(1)}, bf16[16,2048]{1,0:T(8,128)(2,1)S(1)}, u32[]{:S(2)}, u32[]{:S(2)}) collective-permute-start(bf16[16,2048]{1,0:T(8,128)(2,1)S(1)} %bitcast.100), channel_id=1, source_target_pairs={{0,4},{4,8},{8,12},{12,0},{1,5},{5,9},{9,13},{13,1},{2,6},{6,10},{... | collective-permute-start | bytes 196616 | tf_op jit(solution)/shard_map/ppermute | solution.py:37
  58.6 9.5 %collective-permute-start.13 = (bf16[4,16,2048]{2,1,0:T(8,128)(2,1)S(1)}, bf16[4,16,2048]{2,1,0:T(8,128)(2,1)S(1)}, u32[]{:S(2)}, u32[]{:S(2)}) collective-permute-start(bf16[4,16,2048]{2,1,0:T(8,128)(2,1)S(1)} %pad_maximum_fusion), channel_id=1, source_target_pairs={{0,1},{1,0},{2,3},{3,2},{4,5},{5,4},{6,7},{7,6},{8,9},{9,8},{10,11... | collective-permute-start | bytes 786440 | tf_op jit(solution)/shard_map/ppermute | solution.py:32
  58.7 8.7 %collective-permute-start.12 = (bf16[4,16,2048]{2,1,0:T(8,128)(2,1)S(1)}, bf16[4,16,2048]{2,1,0:T(8,128)(2,1)S(1)}, u32[]{:S(2)}, u32[]{:S(2)}) collective-permute-start(bf16[4,16,2048]{2,1,0:T(8,128)(2,1)S(1)} %pad_maximum_fusion), channel_id=1, source_target_pairs={{0,2},{1,3},{2,0},{3,1},{4,6},{5,7},{6,4},{7,5},{8,10},{9,11},{10,... | collective-permute-start | bytes 786440 | tf_op jit(solution)/shard_map/ppermute | solution.py:32
  67.4 1.5 %collective-permute-start.14 = (bf16[4,16,2048]{2,1,0:T(8,128)(2,1)S(1)}, bf16[4,16,2048]{2,1,0:T(8,128)(2,1)S(1)}, u32[]{:S(2)}, u32[]{:S(2)}) collective-permute-start(bf16[4,16,2048]{2,1,0:T(8,128)(2,1)S(1)} %collective-permute-done.12), channel_id=1, source_target_pairs={{0,1},{1,0},{2,3},{3,2},{4,5},{5,4},{6,7},{7,6},{8,9},{9,8},{10,11... | collective-permute-start | bytes 786440 | tf_op jit(solution)/shard_map/ppermute | solution.py:32
  69.7 2.3 %copy-start.4 = (bf16[1,384,2048]{2,1,0:T(8,128)(2,1)S(1)}, bf16[1,384,2048]{2,1,0:T(8,128)(2,1)}, u32[]{:S(2)}) copy-start(bf16[1,384,2048]{2,1,0:T(8,128)(2,1)} %param.19) | copy-start | bytes 4718596
  72.8 1.7 %collective-permute-start.22 = (bf16[4,16,2048]{2,1,0:T(8,128)(2,1)S(1)}, bf16[4,16,2048]{2,1,0:T(8,128)(2,1)S(1)}, u32[]{:S(2)}, u32[]{:S(2)}) collective-permute-start(bf16[4,16,2048]{2,1,0:T(8,128)(2,1)S(1)} %bitcast.105), channel_id=1, source_target_pairs={{0,1},{1,0},{2,3},{3,2},{4,5},{5,4},{6,7},{7,6},{8,9},{9,8},{10,11... | collective-permute-start | bytes 786440 | tf_op jit(solution)/shard_map/ppermute | solution.py:32
  73.3 2.2 %collective-permute-start.21 = (bf16[4,16,2048]{2,1,0:T(8,128)(2,1)S(1)}, bf16[4,16,2048]{2,1,0:T(8,128)(2,1)S(1)}, u32[]{:S(2)}, u32[]{:S(2)}) collective-permute-start(bf16[4,16,2048]{2,1,0:T(8,128)(2,1)S(1)} %bitcast.104), channel_id=1, source_target_pairs={{0,1},{1,0},{2,3},{3,2},{4,5},{5,4},{6,7},{7,6},{8,9},{9,8},{10,11... | collective-permute-start | bytes 786440 | tf_op jit(solution)/shard_map/ppermute | solution.py:32
  74.6 8.7 %collective-permute-start.23 = (bf16[4,16,2048]{2,1,0:T(8,128)(2,1)S(1)}, bf16[4,16,2048]{2,1,0:T(8,128)(2,1)S(1)}, u32[]{:S(2)}, u32[]{:S(2)}) collective-permute-start(bf16[4,16,2048]{2,1,0:T(8,128)(2,1)S(1)} %fusion.6), channel_id=1, source_target_pairs={{0,2},{1,3},{2,0},{3,1},{4,6},{5,7},{6,4},{7,5},{8,10},{9,11},{10,... | collective-permute-start | bytes 786440 | tf_op jit(solution)/shard_map/ppermute | solution.py:32
  83.3 5.1 %collective-permute-start.24 = (bf16[16,2048]{1,0:T(8,128)(2,1)S(1)}, bf16[16,2048]{1,0:T(8,128)(2,1)S(1)}, u32[]{:S(2)}, u32[]{:S(2)}) collective-permute-start(bf16[16,2048]{1,0:T(8,128)(2,1)S(1)} %get-tuple-element.20), channel_id=1, source_target_pairs={{0,12},{4,0},{8,4},{12,8},{1,13},{5,1},{9,5},{13,9},{2,14},{6,2},{... | collective-permute-start | bytes 196616 | tf_op jit(solution)/shard_map/ppermute | solution.py:37
  83.8 6.1 %collective-permute-start.26 = (bf16[16,2048]{1,0:T(8,128)(2,1)S(1)}, bf16[16,2048]{1,0:T(8,128)(2,1)S(1)}, u32[]{:S(2)}, u32[]{:S(2)}) collective-permute-start(bf16[16,2048]{1,0:T(8,128)(2,1)S(1)} %get-tuple-element.21), channel_id=1, source_target_pairs={{0,4},{4,8},{8,12},{12,0},{1,5},{5,9},{9,13},{13,1},{2,6},{6,10},{... | collective-permute-start | bytes 196616 | tf_op jit(solution)/shard_map/ppermute | solution.py:37
  85.4 6.3 %collective-permute-start.25 = (bf16[16,2048]{1,0:T(8,128)(2,1)S(1)}, bf16[16,2048]{1,0:T(8,128)(2,1)S(1)}, u32[]{:S(2)}, u32[]{:S(2)}) collective-permute-start(bf16[16,2048]{1,0:T(8,128)(2,1)S(1)} %get-tuple-element.22), channel_id=1, source_target_pairs={{0,8},{4,12},{8,0},{12,4},{1,9},{5,13},{9,1},{13,5},{2,10},{6,14},... | collective-permute-start | bytes 196616 | tf_op jit(solution)/shard_map/ppermute | solution.py:37

commit v2 on v1

v2 whole, which is shorter than its diff:
```python
import functools
import math

import jax
import jax.numpy as jnp
from jax import lax
from jax.experimental import pallas as pl
from jax.experimental.pallas import tpu as pltpu
from jax.sharding import PartitionSpec as P

HEAD = 128

floor_value = -1e30
norm_epsilon = 1e-06


def normalize(hidden, norm_gain):
    widened = hidden.astype(jnp.float32)
    mean_square = jnp.mean(widened * widened, axis=-1, keepdims=True)
    return (widened * lax.rsqrt(mean_square + norm_epsilon) * norm_gain).astype(jnp.bfloat16)


def strides(count):
    assert count & (count - 1) == 0
    return [1 << bit for bit in reversed(range(count.bit_length() - 1))]


def swap(value, axis, stride):
    return lax.ppermute(value, axis, [(i, i ^ stride) for i in range(lax.axis_size(axis))])


def shift(value, axis, step):
    count = lax.axis_size(axis)
    return lax.ppermute(value, axis, [(i, (i + step) % count) for i in range(count)])


def whole_specs(count):
    return [pl.BlockSpec(memory_space=pltpu.VMEM)] * count


SMEM_SPEC = pl.BlockSpec(memory_space=pltpu.SMEM)
LIMIT = pltpu.CompilerParams(vmem_limit_bytes=16 * 1024 * 1024)


def stack_heads(queries):
    heads = queries.shape[1] // HEAD
    return jnp.concatenate(
        [queries[:, h * HEAD : (h + 1) * HEAD] for h in range(heads)], axis=0
    )


def page_partial(stacked, keys, values, page, length, place, fresh_block):
    rows, page_size = stacked.shape[0], keys.shape[0]
    slab_size = page_size - fresh_block
    scores = lax.dot_general(
        keys, stacked, (((1,), (1,)), ((), ())), preferred_element_type=jnp.float32
    )
    lanes = HEAD if HEAD % fresh_block == 0 and rows % HEAD == 0 else rows
    offset = lax.broadcasted_iota(jnp.int32, (slab_size, lanes), 0)
    fresh = page * fresh_block + lax.broadcasted_iota(jnp.int32, (fresh_block, lanes), 0)
    lane = lax.broadcasted_iota(jnp.int32, (fresh_block, lanes), 1)
    position = place * fresh_block + lax.rem(lane, fresh_block)
    bias = jnp.concatenate(
        [
            jnp.where(offset < length, 0.0, floor_value),
            jnp.where(fresh <= position, 0.0, floor_value),
        ],
        axis=0,
    )
    masked = scores + jnp.concatenate([bias] * (rows // lanes), axis=1)
    peak = jnp.max(masked, axis=0, keepdims=True)
    weights = jnp.exp((masked - peak) * (HEAD**-0.5))
    total = jnp.sum(weights, axis=0, keepdims=True)
    summed = lax.dot_general(
        values,
        weights.astype(jnp.bfloat16),
        (((0,), (0,)), ((), ())),
        preferred_element_type=jnp.float32,
    )
    return peak, total, summed


def merge(first, second):
    peak = jnp.maximum(first[0], second[0])
    scale_first = jnp.exp((first[0] - peak) * (HEAD**-0.5))
    scale_second = jnp.exp((second[0] - peak) * (HEAD**-0.5))
    return (
        peak,
        first[1] * scale_first + second[1] * scale_second,
        first[2] * scale_first + second[2] * scale_second,
    )


def page_at(offset):
    count = lax.axis_size("ctx")
    return lax.rem(lax.axis_index("ctx") + offset + count, count)


def early_kernel(offsets, fresh_block, lengths, queries, *refs):
    count = len(offsets)
    pages, (peak_out, total_out, summed_out) = refs[: 2 * count], refs[2 * count :]
    stacked = stack_heads(queries[...])
    place = lax.axis_index("ctx")
    state = None
    for number, offset in enumerate(offsets):
        page = page_at(offset)
        part = page_partial(
            stacked,
            pages[2 * number][...],
            pages[2 * number + 1][...],
            page,
            lengths[page],
            place,
            fresh_block,
        )
        state = part if state is None else merge(state, part)
    peak_out[...] = state[0]
    total_out[...] = state[1]
    summed_out[...] = state[2]


def late_kernel(
    offset,
    fresh_block,
    lengths,
    queries,
    keys,
    values,
    peak,
    total,
    summed,
    weight_hbm,
    context_out,
    own_out,
    *rest,
):
    sent_outs, (weight, blocks, sem) = rest[:-3], rest[-3:]
    copy = pltpu.make_async_copy(weight_hbm, weight, sem)
    copy.start()
    page = page_at(offset)
    part = page_partial(
        stack_heads(queries[...]),
        keys[...],
        values[...],
        page,
        lengths[page],
        lax.axis_index("ctx"),
        fresh_block,
    )
    state = merge((peak[...], total[...], summed[...]), part)
    result = jnp.transpose(state[2] / state[1])
    context = jnp.concatenate(
        [
            result[h * fresh_block : (h + 1) * fresh_block]
            for h in range(result.shape[0] // fresh_block)
        ],
        axis=1,
    ).astype(jnp.bfloat16)
    context_out[...] = context
    copy.wait()
    blocks[...] = jnp.dot(context, weight[...], preferred_element_type=jnp.float32)
    place = lax.axis_index("exp")
    size = own_out.shape[0]
    pick = lambda index: blocks[pl.ds(pl.multiple_of(index * size, size), size), :]
    own_out[...] = pick(place)
    for step, out in enumerate(sent_outs, 1):
        out[...] = pick(place ^ step).astype(jnp.bfloat16)


def attention(queries, pages, lengths, out_weight, token_block):
    fresh_block, width = queries.shape
    rows = width // HEAD * fresh_block
    count = lax.axis_size("ctx")
    exp_count = lax.axis_size("exp")
    model_width = out_weight.shape[1]
    own_keys, own_values = pages[:, 0], pages[:, 1]
    held = [(0, own_keys, own_values)]
    left_keys, left_values = own_keys, own_values
    right_keys, right_values = own_keys, own_values
    for step in range(1, (count - 1) // 2 + 1):
        left_keys = shift(left_keys, "ctx", 1)
        right_values = shift(right_values, "ctx", -1)
        left_values = shift(left_values, "ctx", 1)
        right_keys = shift(right_keys, "ctx", -1)
        held.append((-step, left_keys, left_values))
        held.append((step, right_keys, right_values))
    if count % 2 == 0:
        last = (count // 2, shift(left_keys, "ctx", 1), shift(right_values, "ctx", -1))
    else:
        last = held.pop()
    page_flops = 4 * rows * pages.shape[0] * HEAD
    line = jax.ShapeDtypeStruct((1, rows), jnp.float32)
    state = None
    for start in range(0, len(held), 3):
        group = held[start : start + 3]
        operands = [part for _, keys, values in group for part in (keys, values)]
        partial_state = pl.pallas_call(
            functools.partial(early_kernel, [offset for offset, _, _ in group], fresh_block),
            out_shape=(line, line, jax.ShapeDtypeStruct((HEAD, rows), jnp.float32)),
            in_specs=[SMEM_SPEC] + whole_specs(1 + len(operands)),
            out_specs=tuple(whole_specs(3)),
            compiler_params=LIMIT,
            cost_estimate=pl.CostEstimate(
                flops=len(group) * page_flops, bytes_accessed=2 << 20, transcendentals=0
            ),
        )(lengths, queries, *operands)
        state = partial_state if state is None else merge(state, partial_state)
    block = jax.ShapeDtypeStruct((token_block, model_width), jnp.bfloat16)
    outs = pl.pallas_call(
        functools.partial(late_kernel, last[0], fresh_block),
        out_shape=(
            jax.ShapeDtypeStruct(queries.shape, jnp.bfloat16),
            jax.ShapeDtypeStruct(block.shape, jnp.float32),
        )
        + (block,) * (exp_count - 1),
        in_specs=[SMEM_SPEC] + whole_specs(6) + [pl.BlockSpec(memory_space=pl.ANY)],
        out_specs=tuple(whole_specs(1 + exp_count)),
        scratch_shapes=[
            pltpu.VMEM(out_weight.shape, jnp.bfloat16),
            pltpu.VMEM((fresh_block, model_width), jnp.float32),
            pltpu.SemaphoreType.DMA,
        ],
        compiler_params=LIMIT,
        cost_estimate=pl.CostEstimate(
            flops=page_flops + 2 * fresh_block * width * model_width,
            bytes_accessed=6 << 20,
            transcendentals=0,
        ),
    )(lengths, queries, last[1], last[2], *state, out_weight)
    return outs[0], outs[1], outs[2:], left_keys


def split_kernel(tile, source, target):
    half = source.shape[3]

    def body(number, carry):
        rows = pl.ds(pl.multiple_of(number * tile, tile), tile)
        target[rows, :half] = source[0, rows, 0, :]
        target[rows, half:] = source[0, rows, 1, :]
        return carry

    lax.fori_loop(0, source.shape[1] // tile, body, 0)


def split_gate_up(expert_input):
    _, width, _, hidden = expert_input.shape
    return pl.pallas_call(
        functools.partial(split_kernel, math.gcd(width, 128)),
        out_shape=jax.ShapeDtypeStruct((width, 2 * hidden), jnp.bfloat16),
        in_specs=whole_specs(1),
        out_specs=whole_specs(1)[0],
        compiler_params=LIMIT,
        cost_estimate=pl.CostEstimate(flops=0, bytes_accessed=6 << 20, transcendentals=0),
    )(expert_input)


def expert_kernel(*refs):
    pieces, (gate_up, down, scale, keep_out, send_out) = refs[:-5], refs[-5:]
    rows = jnp.concatenate([piece[...] for piece in pieces], axis=0)
    inner = jnp.dot(rows, gate_up[...], preferred_element_type=jnp.float32)
    hidden = inner.shape[1] // 2
    gate, up = inner[:, :hidden], inner[:, hidden:]
    activated = (gate / (1.0 + jnp.exp(-gate)) * up).astype(jnp.bfloat16)
    result = jnp.dot(activated, down[0], preferred_element_type=jnp.float32)
    result = result.astype(jnp.bfloat16).astype(jnp.float32) * scale[...]
    half = keep_out.shape[0]
    keep_out[...] = result[:half]
    send_out[...] = result[half:].astype(jnp.bfloat16)


def expert_apply(pieces, gate_up, down, scale):
    rows = sum(piece.shape[0] for piece in pieces)
    width, hidden = down.shape[2], down.shape[1]
    half = (rows // 2, width)
    return pl.pallas_call(
        expert_kernel,
        out_shape=(
            jax.ShapeDtypeStruct(half, jnp.float32),
            jax.ShapeDtypeStruct(half, jnp.bfloat16),
        ),
        in_specs=whole_specs(len(pieces) + 3),
        out_specs=tuple(whole_specs(2)),
        compiler_params=LIMIT,
        cost_estimate=pl.CostEstimate(
            flops=6 * rows * width * hidden, bytes_accessed=6 << 20, transcendentals=0
        ),
    )(*pieces, gate_up, down, scale)


def gather_column(rows):
    for stride in strides(lax.axis_size("ctx")):
        rows = jnp.concatenate([rows, swap(rows, "ctx", stride)], axis=0)
    return rows


def gather_pieces(rows):
    pieces = [gather_column(rows)]
    for stride in strides(lax.axis_size("exp")):
        pieces = pieces + [swap(piece, "exp", stride) for piece in pieces]
    return pieces


def give_back(keep, send):
    exchanges = [("exp", stride) for stride in reversed(strides(lax.axis_size("exp")))]
    exchanges += [("ctx", stride) for stride in reversed(strides(lax.axis_size("ctx")))]
    for number, (axis, stride) in enumerate(exchanges):
        total = keep + swap(send, axis, stride).astype(jnp.float32)
        if number + 1 == len(exchanges):
            return total
        half = total.shape[0] // 2
        keep, send = total[:half], total[half:].astype(jnp.bfloat16)


def per_device(
    queries,
    pages,
    cached_lengths,
    residual_in,
    out_weight,
    norm_gain,
    expert_ids,
    route_scores,
    expert_input,
    expert_output,
):
    requests = queries.shape[0]
    core_place = lax.axis_index("rep")
    rep_count = lax.axis_size("rep")
    exp_count = lax.axis_size("exp")
    expert_count = lax.axis_size("ctx") * exp_count
    token_block, model_width = residual_in.shape[1:]
    token_count = requests * token_block
    expert = lax.axis_index("ctx") * exp_count + lax.axis_index("exp")

    contexts, owns, sents = [], [], []
    for r in range(requests):
        context, own, sent, arrived_keys = attention(
            queries[r], pages[r], cached_lengths[r], out_weight, token_block
        )
        contexts.append(context)
        owns.append(own)
        sents.append(sent)
    context = jnp.stack(contexts)

    route_scores, expert_ids, expert_input, _ = lax.optimization_barrier(
        (route_scores, expert_ids, expert_input, arrived_keys)
    )
    combine = (route_scores / jnp.sum(route_scores, axis=2, keepdims=True)).astype(jnp.bfloat16)
    named = expert_ids[..., None] == jnp.arange(expert_count, dtype=jnp.int32)
    dense = jnp.sum(jnp.where(named, combine[..., None], 0).astype(jnp.float32), axis=2)
    dense = dense.astype(jnp.bfloat16).reshape(token_count, expert_count)
    dense = gather_column(dense)
    for stride in strides(exp_count):
        dense = jnp.concatenate([dense, swap(dense, "exp", stride)], axis=0)
    own_column = jnp.arange(expert_count, dtype=jnp.int32) == expert
    own_weight = jnp.sum(jnp.where(own_column, dense.astype(jnp.float32), 0.0), axis=1)
    own_weight = own_weight.reshape(-1, token_count)
    gate_up = split_gate_up(expert_input)

    share = jnp.stack(owns)
    for step in range(1, exp_count):
        blocks = jnp.stack([sent[step - 1] for sent in sents])
        share = share + swap(blocks, "exp", step).astype(jnp.float32)
    share_size = token_block // rep_count
    if rep_count > 1:
        share = lax.psum_scatter(
            share.astype(jnp.bfloat16), "rep", scatter_dimension=1, tiled=True
        ).astype(jnp.float32)
    own_residual = lax.dynamic_slice_in_dim(residual_in, core_place * share_size, share_size, 1)
    own_hidden = (own_residual.astype(jnp.float32) + share).astype(jnp.bfloat16)
    normed = normalize(own_hidden, norm_gain)
    if rep_count > 1:
        normed = lax.all_gather(normed, "rep", axis=1, tiled=True)
    normed = normed.reshape(token_count, model_width)

    parts = 2 if token_count % 16 == 0 else 1
    size = token_count // parts
    returned = []
    for part in range(parts):
        rows = slice(part * size, (part + 1) * size)
        pieces = gather_pieces(normed[rows])
        scale = own_weight[:, rows].reshape(-1, 1)
        returned.append(give_back(*expert_apply(pieces, gate_up, expert_output, scale)))
    mixture = jnp.concatenate(returned, axis=0).reshape(requests, token_block, model_width)
    if rep_count > 1:
        mixture = lax.psum_scatter(
            mixture.astype(jnp.bfloat16), "rep", scatter_dimension=1, tiled=True
        ).astype(jnp.float32)
    layer_out = (own_hidden.astype(jnp.float32) + mixture).astype(jnp.bfloat16)
    return (context, layer_out)


def solution(mesh):
    in_specs = (
        P("groups", "ctx", ("exp", "rep")),
        P("groups", "ctx", None, "exp"),
        P("groups", None),
        P("groups", ("ctx", "exp"), None),
        P(("exp", "rep"), None),
        P(),
        P("groups", ("ctx", "exp"), None),
        P("groups", ("ctx", "exp"), None),
        P(("ctx", "exp"), None, None, "rep"),
        P(("ctx", "exp"), "rep", None),
    )
    out_specs = (P("groups", "ctx", ("exp", "rep")), P("groups", ("ctx", "exp", "rep"), None))
    return jax.shard_map(
        per_device, mesh=mesh, in_specs=in_specs, out_specs=out_specs, check_vma=False
    )
```

time: 92.7 us -> 99 us (1.068)
  Pallas kernels: 6 us -> 17.6 us
  waiting for transfers between devices: 37.9 us -> 30.9 us
  matrix products: 6.16 us -> 0 us
  other arithmetic: 4.33 us -> 8.23 us
  starting transfers between devices: 26.8 us -> 29.5 us
    pallas_call x2 -> x5, Pallas kernels: 6 us -> 17.6 us  [the longest x1 7.34 us: split_gate_up(): pl.pallas_call(functools.partial(split_kernel, math.gcd(width, 128)), out...]
    ppermute x15 -> x6, waiting for transfers between devices: 15.8 us -> 4.67 us  [shift(): lax.ppermute(value, axis, [(i, (i + step) % count) for i in range(count)])]
    ppermute x12 -> x25, starting transfers between devices: 6.2 us -> 16.7 us  [swap(): lax.ppermute(value, axis, [(i, i ^ stride) for i in range(lax.axis_size(a...]
    ppermute x15 -> x6, starting transfers between devices: 20.6 us -> 12.8 us  [shift(): lax.ppermute(value, axis, [(i, (i + step) % count) for i in range(count)])]
    dot_general x3 -> x0, matrix products: 6.16 us -> none  [the longest x1 3.11 us: per_device(): jnp.dot(context.reshape(requests * fresh_block, query_width), out_weight,...]
    ppermute x12 -> x25, waiting for transfers between devices: 22.1 us -> 26.3 us  [swap(): lax.ppermute(value, axis, [(i, i ^ stride) for i in range(lax.axis_size(a...]
    unnamed x22 -> x23, local copies, waits for them, and re-layouts: 5.28 us -> 8.37 us
    another operation x1 -> x0, local copies, waits for them, and re-layouts: 1.89 us -> none  [info_of(): return jnp.stack(numbers).astype(jnp.int32)]
  transfers between devices with their start and end apart: 27 -> 31, of which waited for: 15 -> 14; matrix products, arithmetic and copies ran while one was open for 13% -> 9% of each run, Pallas kernels for 6% -> 18%
where the time goes in v2:
time: 99 us; the launch traced here: 98.4 us
  waiting for transfers between devices  30.9 us (31%)
  starting transfers between devices  29.5 us (30%)
  Pallas kernels  17.6 us (18%)
  local copies, waits for them, and re-layouts  11.2 us (11%)
  other arithmetic  8.23 us (8%)
    ppermute x25, waiting for transfers between devices, swap(): lax.ppermute(value, axis, [(i, i ^ stride) for i in range(lax.axis_size(a...  26.3 us
    ppermute x25, starting transfers between devices, swap(): lax.ppermute(value, axis, [(i, i ^ stride) for i in range(lax.axis_size(a...  16.7 us
    ppermute x6, starting transfers between devices, shift(): lax.ppermute(value, axis, [(i, (i + step) % count) for i in range(count)])  12.8 us
    unnamed x23, local copies, waits for them, and re-layouts  8.37 us
    pallas_call x1, Pallas kernels, split_gate_up(): pl.pallas_call(functools.partial(split_kernel, math.gcd(width, 128)), out...  7.34 us
    pallas_call x2, Pallas kernels, expert_apply(): pl.pallas_call(expert_kernel, out_shape=(jax.ShapeDtypeStruct(half, jnp.f...  5.08 us
    ppermute x6, waiting for transfers between devices, shift(): lax.ppermute(value, axis, [(i, (i + step) % count) for i in range(count)])  4.67 us
    pallas_call x1, Pallas kernels, attention(): pl.pallas_call(functools.partial(early_kernel, [offset for offset, _, _ i...  2.58 us
  transfers between devices with their start and end apart: 31, of which 14 were waited for; matrix products, arithmetic and copies ran while one was open for 9% of the time, Pallas kernels for 18%

profile of v2, /device:TPU:0, one launch (start us, length us, event | category | flops | bytes accessed | tf_op | source)
XLA Modules:
  0.0 98.4 jit_solution(7606921434854874339)
XLA Ops:
  0.6 1.0 %copy.42 = bf16[1,576,2,128]{3,1,2,0:T(8,128)(2,1)S(1)} copy(bf16[1,576,2,128]{3,2,1,0:T(2,128)(2,1)} %param.11) | data formatting | bytes 589824 | tf_op args[1]
  1.7 3.1 %collective-permute-start = (bf16[576,128]{1,0:T(8,128)(2,1)S(1)}, bf16[576,128]{1,0:T(8,128)(2,1)S(1)}, u32[]{:S(2)}, u32[]{:S(2)}) collective-permute-start(bf16[576,128]{1,0:T(8,128)(2,1)S(1)} %get-tuple-element.35.refs_0_), channel_id=1, source_target_pairs={{0,4},{4,8},{8,12},{12,0},{1,5},{5,9},{9,13},{13,1},{2,6},{6,10},{... | collective-permute-start | bytes 442376 | tf_op jit(solution)/shard_map/ppermute | solution.py:34
  4.7 2.1 %collective-permute-start.2 = (bf16[576,128]{1,0:T(8,128)(2,1)S(1)}, bf16[576,128]{1,0:T(8,128)(2,1)S(1)}, u32[]{:S(2)}, u32[]{:S(2)}) collective-permute-start(bf16[576,128]{1,0:T(8,128)(2,1)S(1)} %get-tuple-element.34.refs_1_), channel_id=1, source_target_pairs={{0,12},{4,0},{8,4},{12,8},{1,13},{5,1},{9,5},{13,9},{2,14},{6,2},{... | collective-permute-start | bytes 442376 | tf_op jit(solution)/shard_map/ppermute | solution.py:34
  6.8 4.7 %collective-permute-done.refs_2_ = bf16[576,128]{1,0:T(8,128)(2,1)S(1)} collective-permute-done((bf16[576,128]{1,0:T(8,128)(2,1)S(1)}, bf16[576,128]{1,0:T(8,128)(2,1)S(1)}, u32[]{:S(2)}, u32[]{:S(2)}) %collective-permute-start) | collective-permute-done | bytes 147488 | tf_op jit(solution)/shard_map/ppermute | solution.py:34
  11.5 0.8 copy.28
  12.2 0.7 reduce_sum.40
  12.9 0.7 fusion.10
  13.8 3.1 %collective-permute-start.14 = (bf16[16,16]{1,0:T(8,128)(2,1)S(1)}, bf16[16,16]{1,0:T(8,128)(2,1)S(1)}, u32[]{:S(2)}, u32[]{:S(2)}) collective-permute-start(bf16[16,16]{1,0:T(8,128)(2,1)S(1)} %fusion.9), channel_id=1, source_target_pairs={{0,8},{4,12},{8,0},{12,4},{1,9},{5,13},{9,1},{13,5},{2,10},{6,14},... | collective-permute-start | bytes 1544 | tf_op jit(solution)/shard_map/ppermute | solution.py:29
  16.9 1.6 %collective-permute-start.4 = (bf16[576,128]{1,0:T(8,128)(2,1)S(1)}, bf16[576,128]{1,0:T(8,128)(2,1)S(1)}, u32[]{:S(2)}, u32[]{:S(2)}) collective-permute-start(bf16[576,128]{1,0:T(8,128)(2,1)S(1)} %get-tuple-element.34.refs_1_), channel_id=1, source_target_pairs={{0,4},{4,8},{8,12},{12,0},{1,5},{5,9},{9,13},{13,1},{2,6},{6,10},{... | collective-permute-start | bytes 442376 | tf_op jit(solution)/shard_map/ppermute | solution.py:34
  18.5 2.2 %collective-permute-start.5 = (bf16[576,128]{1,0:T(8,128)(2,1)S(1)}, bf16[576,128]{1,0:T(8,128)(2,1)S(1)}, u32[]{:S(2)}, u32[]{:S(2)}) collective-permute-start(bf16[576,128]{1,0:T(8,128)(2,1)S(1)} %get-tuple-element.35.refs_0_), channel_id=1, source_target_pairs={{0,12},{4,0},{8,4},{12,8},{1,13},{5,1},{9,5},{13,9},{2,14},{6,2},{... | collective-permute-start | bytes 442376 | tf_op jit(solution)/shard_map/ppermute | solution.py:34
  20.9 2.0 %collective-permute-start.1 = (bf16[576,128]{1,0:T(8,128)(2,1)S(1)}, bf16[576,128]{1,0:T(8,128)(2,1)S(1)}, u32[]{:S(2)}, u32[]{:S(2)}) collective-permute-start(bf16[576,128]{1,0:T(8,128)(2,1)S(1)} %collective-permute-done.refs_2_), channel_id=1, source_target_pairs={{0,4},{4,8},{8,12},{12,0},{1,5},{5,9},{9,13},{13,1},{2,6},{6,10},{... | collective-permute-start | bytes 442376 | tf_op jit(solution)/shard_map/ppermute | solution.py:34
  22.9 1.8 %collective-permute-start.3 = (bf16[576,128]{1,0:T(8,128)(2,1)S(1)}, bf16[576,128]{1,0:T(8,128)(2,1)S(1)}, u32[]{:S(2)}, u32[]{:S(2)}) collective-permute-start(bf16[576,128]{1,0:T(8,128)(2,1)S(1)} %collective-permute-done.2.refs_5_), channel_id=1, source_target_pairs={{0,12},{4,0},{8,4},{12,8},{1,13},{5,1},{9,5},{13,9},{2,14},{6,2},{... | collective-permute-start | bytes 442376 | tf_op jit(solution)/shard_map/ppermute | solution.py:34
  24.8 1.5 %collective-permute-done.15 = bf16[32,16]{1,0:T(8,128)(2,1)S(1)} collective-permute-done((bf16[32,16]{1,0:T(8,128)(2,1)S(1)}, bf16[32,16]{1,0:T(8,128)(2,1)S(1)}, u32[]{:S(2)}, u32[]{:S(2)}) %collective-permute-start.15) | collective-permute-done | bytes 1056 | tf_op jit(solution)/shard_map/ppermute | solution.py:29
  26.5 1.5 %collective-permute-start.16 = (bf16[64,16]{0,1:T(8,128)(2,1)S(1)}, bf16[64,16]{0,1:T(8,128)(2,1)S(1)}, u32[]{:S(2)}, u32[]{:S(2)}) collective-permute-start(bf16[64,16]{0,1:T(8,128)(2,1)S(1)} %pad_maximum_fusion.5), channel_id=1, source_target_pairs={{0,2},{1,3},{2,0},{3,1},{4,6},{5,7},{6,4},{7,5},{8,10},{9,11},{10,... | collective-permute-start | bytes 6152 | tf_op jit(solution)/shard_map/ppermute | solution.py:29
  28.0 0.9 copy-done.6
  29.6 2.6 %shard_map.113 = (f32[1,512]{1,0:T(1,128)S(1)}, f32[1,512]{1,0:T(1,128)S(1)}, f32[128,512]{1,0:T(8,128)S(1)}) custom-call(s32[4]{0:T(128)S(1)} %bitcast.37, bf16[64,1024]{1,0:T(8,128)(2,1)S(1)} %bitcast.35, bf16[576,128]{1,0:T(8,128)(2,1)S(1)} %get-tuple-element.35.refs_0_, bf16[576,128]{1,0:T(8,128)(2,1)S(1)} %get-tuple-element.34.refs_1_, ...), custom_call_target="tpu_custom_call" | custom-call | flops 452984832 | bytes 2097152 | tf_op jit(solution)/shard_map/pallas_call | solution.py:197
  32.3 2.2 %copy-done.2 = bf16[1024,2048]{1,0:T(8,128)(2,1)S(1)} copy-done((bf16[1024,2048]{1,0:T(8,128)(2,1)S(1)}, bf16[1024,2048]{1,0:T(8,128)(2,1)}, u32[]{:S(2)}) %copy-start.2) | copy-done | bytes 4194328
  34.5 2.5 %shard_map.114 = (bf16[64,1024]{1,0:T(8,128)(2,1)}, f32[16,2048]{1,0:T(8,128)S(1)}, bf16[16,2048]{1,0:T(8,128)(2,1)S(1)}, bf16[16,2048]{1,0:T(8,128)(2,1)S(1)}, bf16[16,2048]{1,0:T(8,128)(2,1)S(1)}) custom-call(s32[4]{0:T(128)S(1)} %bitcast.38, bf16[64,1024]{1,0:T(8,128)(2,1)S(1)} %bitcast.36, bf16[576,128]{1,0:T(8,128)(2,1)S(1)} %collective-permute-done.1.keys, ...), custom_call_target="tpu_custom_call" | custom-call | flops 419430400 | bytes 6291456 | tf_op jit(solution)/shard_map/pallas_call | solution.py:209
  37.7 1.5 %collective-permute-start.7 = (bf16[1,16,2048]{2,1,0:T(8,128)(2,1)S(1)}, bf16[1,16,2048]{2,1,0:T(8,128)(2,1)}, u32[]{:S(2)}, u32[]{:S(2)}) collective-permute-start(bf16[1,16,2048]{2,1,0:T(8,128)(2,1)S(1)} %bitcast.40), channel_id=1, source_target_pairs={{0,2},{1,3},{2,0},{3,1},{4,6},{5,7},{6,4},{7,5},{8,10},{9,11},{10,... | collective-permute-start | bytes 196616 | tf_op jit(solution)/shard_map/ppermute | solution.py:29
  39.8 7.3 %shard_map.115.refs_4_ = bf16[2048,768]{1,0:T(8,128)(2,1)S(1)} custom-call(bf16[1,2048,2,384]{3,2,1,0:T(2,128)(2,1)S(1)} %copy-done.3), custom_call_target="tpu_custom_call" | custom-call | bytes 6291456 | tf_op jit(solution)/shard_map/pallas_call | solution.py:247
  47.2 1.4 %concatenate.37 = bf16[256,16]{0,1:T(8,128)(2,1)} concatenate(bf16[16,16]{0,1:T(8,128)(2,1)S(1)} %copy.36, bf16[16,16]{0,1:T(8,128)(2,1)S(1)} %copy.37, bf16[32,16]{0,1:T(8,128)(2,1)S(1)} %copy.38, bf16[64,16]{0,1:T(8,128)(2,1)S(1)} %collective-permute-done.16, bf16[128,16]{0,1:T(8,128)(2,1)} %collective-permute-done.17), dimensions={0} | concatenate | bytes 16384 | tf_op jit(solution)/shard_map/concatenate | solution.py:354
  48.5 1.1 %fusion = (f32[16]{0:T(128)S(1)}, bf16[1,16,2048]{2,1,0:T(8,128)(2,1)S(1)}) fusion(bf16[1,16,2048]{2,1,0:T(8,128)(2,1)} %collective-permute-done.8, bf16[1,16,2048]{2,1,0:T(8,128)(2,1)} %collective-permute-done.7, bf16[1,16,2048]{2,1,0:T(8,128)(2,1)} %collective-permute-done.6, f32[16,2048]{1,0:T(8,128)S(1)} %get-tuple-element.21, ...), kind=kLoop, calls=%fused_computation.12 | loop fusion | flops 393200 | bytes 458816 | tf_op jit(solution)/shard_map/reduce_sum | solution.py:19
  49.6 0.8 fusion.2
  50.4 1.0 %collective-permute-start.22 = (bf16[8,2048]{1,0:T(8,128)(2,1)S(1)}, bf16[8,2048]{1,0:T(8,128)(2,1)S(1)}, u32[]{:S(2)}, u32[]{:S(2)}) collective-permute-start(bf16[8,2048]{1,0:T(8,128)(2,1)S(1)} %get-tuple-element.37), channel_id=1, source_target_pairs={{0,8},{4,12},{8,0},{12,4},{1,9},{5,13},{9,1},{13,5},{2,10},{6,14},... | collective-permute-start | bytes 98312 | tf_op jit(solution)/shard_map/ppermute | solution.py:29
  51.5 0.8 select_reduce_fusion
  52.3 2.0 %collective-permute-start.9 = (bf16[8,2048]{1,0:T(8,128)(2,1)S(1)}, bf16[8,2048]{1,0:T(8,128)(2,1)S(1)}, u32[]{:S(2)}, u32[]{:S(2)}) collective-permute-start(bf16[8,2048]{1,0:T(8,128)(2,1)S(1)} %get-tuple-element.36), channel_id=1, source_target_pairs={{0,8},{4,12},{8,0},{12,4},{1,9},{5,13},{9,1},{13,5},{2,10},{6,14},... | collective-permute-start | bytes 98312 | tf_op jit(solution)/shard_map/ppermute | solution.py:29
  54.3 1.6 %collective-permute-done.22 = bf16[8,2048]{1,0:T(8,128)(2,1)S(1)} collective-permute-done((bf16[8,2048]{1,0:T(8,128)(2,1)S(1)}, bf16[8,2048]{1,0:T(8,128)(2,1)S(1)}, u32[]{:S(2)}, u32[]{:S(2)}) %collective-permute-start.22) | collective-permute-done | bytes 32800 | tf_op jit(solution)/shard_map/ppermute | solution.py:29
  55.9 1.4 %collective-permute-done.9 = bf16[8,2048]{1,0:T(8,128)(2,1)S(1)} collective-permute-done((bf16[8,2048]{1,0:T(8,128)(2,1)S(1)}, bf16[8,2048]{1,0:T(8,128)(2,1)S(1)}, u32[]{:S(2)}, u32[]{:S(2)}) %collective-permute-start.9) | collective-permute-done | bytes 32800 | tf_op jit(solution)/shard_map/ppermute | solution.py:29
  58.5 1.6 %collective-permute-done.23 = bf16[16,2048]{1,0:T(8,128)(2,1)S(1)} collective-permute-done((bf16[16,2048]{1,0:T(8,128)(2,1)S(1)}, bf16[16,2048]{1,0:T(8,128)(2,1)S(1)}, u32[]{:S(2)}, u32[]{:S(2)}) %collective-permute-start.23) | collective-permute-done | bytes 65568 | tf_op jit(solution)/shard_map/ppermute | solution.py:29
  60.2 1.1 %collective-permute-start.24 = (bf16[32,2048]{1,0:T(8,128)(2,1)S(1)}, bf16[32,2048]{1,0:T(8,128)(2,1)}, u32[]{:S(2)}, u32[]{:S(2)}) collective-permute-start(bf16[32,2048]{1,0:T(8,128)(2,1)S(1)} %pad_maximum_fusion.1.refs_0_), channel_id=1, source_target_pairs={{0,2},{1,3},{2,0},{3,1},{4,6},{5,7},{6,4},{7,5},{8,10},{9,11},{10,... | collective-permute-start | bytes 393224 | tf_op jit(solution)/shard_map/ppermute | solution.py:29
  61.4 3.8 %collective-permute-done.24.refs_1_ = bf16[32,2048]{1,0:T(8,128)(2,1)} collective-permute-done((bf16[32,2048]{1,0:T(8,128)(2,1)S(1)}, bf16[32,2048]{1,0:T(8,128)(2,1)}, u32[]{:S(2)}, u32[]{:S(2)}) %collective-permute-start.24) | collective-permute-done | bytes 131104 | tf_op jit(solution)/shard_map/ppermute | solution.py:29
  65.3 0.9 pad_maximum_fusion.refs_0_
  66.2 1.1 %collective-permute-start.11 = (bf16[32,2048]{1,0:T(8,128)(2,1)S(1)}, bf16[32,2048]{1,0:T(8,128)(2,1)}, u32[]{:S(2)}, u32[]{:S(2)}) collective-permute-start(bf16[32,2048]{1,0:T(8,128)(2,1)S(1)} %pad_maximum_fusion.refs_0_), channel_id=1, source_target_pairs={{0,2},{1,3},{2,0},{3,1},{4,6},{5,7},{6,4},{7,5},{8,10},{9,11},{10,... | collective-permute-start | bytes 393224 | tf_op jit(solution)/shard_map/ppermute | solution.py:29
  67.2 1.4 %copy-done = bf16[1,384,2048]{2,1,0:T(8,128)(2,1)S(1)} copy-done((bf16[1,384,2048]{2,1,0:T(8,128)(2,1)S(1)}, bf16[1,384,2048]{2,1,0:T(8,128)(2,1)}, u32[]{:S(2)}) %copy-start) | copy-done | bytes 1572888
  68.6 2.8 %shard_map.117 = (f32[64,2048]{1,0:T(8,128)S(1)}, bf16[64,2048]{1,0:T(8,128)(2,1)}) custom-call(bf16[32,2048]{1,0:T(8,128)(2,1)S(1)} %pad_maximum_fusion.1.refs_0_, bf16[32,2048]{1,0:T(8,128)(2,1)} %collective-permute-done.24.refs_1_, bf16[32,2048]{1,0:T(8,128)(2,1)S(1)} %collective-permute-done.25.refs_2_, ...), custom_call_target="tpu_custom_call" | custom-call | flops 603979776 | bytes 6291456 | tf_op jit(solution)/shard_map/pallas_call | solution.py:275
  71.5 0.8 copy-done.4
  73.1 0.9 collective-permute-done.12.refs_2_
  74.5 1.4 %copy-done.1 = bf16[1,384,2048]{2,1,0:T(8,128)(2,1)S(1)} copy-done((bf16[1,384,2048]{2,1,0:T(8,128)(2,1)S(1)}, bf16[1,384,2048]{2,1,0:T(8,128)(2,1)}, u32[]{:S(2)}) %copy-start.1) | copy-done | bytes 1572888
  75.9 2.2 %shard_map.116 = (f32[64,2048]{1,0:T(8,128)S(1)}, bf16[64,2048]{1,0:T(8,128)(2,1)S(1)}) custom-call(bf16[32,2048]{1,0:T(8,128)(2,1)S(1)} %pad_maximum_fusion.refs_0_, bf16[32,2048]{1,0:T(8,128)(2,1)} %collective-permute-done.11.refs_1_, bf16[32,2048]{1,0:T(8,128)(2,1)S(1)} %collective-permute-done.12.refs_2_, ...), custom_call_target="tpu_custom_call" | custom-call | flops 603979776 | bytes 6291456 | tf_op jit(solution)/shard_map/pallas_call | solution.py:275
  78.5 1.0 %convert_add_fusion = f32[64,2048]{1,0:T(8,128)S(1)} fusion(f32[64,2048]{1,0:T(8,128)S(1)} %copy-done.5, bf16[64,2048]{1,0:T(8,128)(2,1)} %collective-permute-done.27), kind=kLoop, calls=%fused_computation | loop fusion | flops 262144 | bytes 1310720 | tf_op jit(solution)/shard_map/add | solution.py:307
  79.5 1.1 %collective-permute-start.28 = (bf16[32,2048]{1,0:T(8,128)(2,1)S(1)}, bf16[32,2048]{1,0:T(8,128)(2,1)S(1)}, u32[]{:S(2)}, u32[]{:S(2)}) collective-permute-start(bf16[32,2048]{1,0:T(8,128)(2,1)S(1)} %slice.120), channel_id=1, source_target_pairs={{0,2},{1,3},{2,0},{3,1},{4,6},{5,7},{6,4},{7,5},{8,10},{9,11},{10,... | collective-permute-start | bytes 393224 | tf_op jit(solution)/shard_map/ppermute | solution.py:29
  80.7 1.0 %collective-permute-start.19 = (bf16[32,2048]{1,0:T(8,128)(2,1)S(1)}, bf16[32,2048]{1,0:T(8,128)(2,1)S(1)}, u32[]{:S(2)}, u32[]{:S(2)}) collective-permute-start(bf16[32,2048]{1,0:T(8,128)(2,1)S(1)} %slice.121), channel_id=1, source_target_pairs={{0,2},{1,3},{2,0},{3,1},{4,6},{5,7},{6,4},{7,5},{8,10},{9,11},{10,... | collective-permute-start | bytes 393224 | tf_op jit(solution)/shard_map/ppermute | solution.py:29
  81.8 4.1 %collective-permute-done.28 = bf16[32,2048]{1,0:T(8,128)(2,1)S(1)} collective-permute-done((bf16[32,2048]{1,0:T(8,128)(2,1)S(1)}, bf16[32,2048]{1,0:T(8,128)(2,1)S(1)}, u32[]{:S(2)}, u32[]{:S(2)}) %collective-permute-start.28) | collective-permute-done | bytes 131104 | tf_op jit(solution)/shard_map/ppermute | solution.py:29
  86.0 2.0 %collective-permute-done.19 = bf16[32,2048]{1,0:T(8,128)(2,1)S(1)} collective-permute-done((bf16[32,2048]{1,0:T(8,128)(2,1)S(1)}, bf16[32,2048]{1,0:T(8,128)(2,1)S(1)}, u32[]{:S(2)}, u32[]{:S(2)}) %collective-permute-start.19) | collective-permute-done | bytes 131104 | tf_op jit(solution)/shard_map/ppermute | solution.py:29
  88.2 2.2 %collective-permute-done.29 = bf16[16,2048]{1,0:T(8,128)(2,1)S(1)} collective-permute-done((bf16[16,2048]{1,0:T(8,128)(2,1)S(1)}, bf16[16,2048]{1,0:T(8,128)(2,1)S(1)}, u32[]{:S(2)}, u32[]{:S(2)}) %collective-permute-start.29) | collective-permute-done | bytes 65568 | tf_op jit(solution)/shard_map/ppermute | solution.py:29
  90.5 2.3 %collective-permute-done.20 = bf16[16,2048]{1,0:T(8,128)(2,1)S(1)} collective-permute-done((bf16[16,2048]{1,0:T(8,128)(2,1)S(1)}, bf16[16,2048]{1,0:T(8,128)(2,1)S(1)}, u32[]{:S(2)}, u32[]{:S(2)}) %collective-permute-start.20) | collective-permute-done | bytes 65568 | tf_op jit(solution)/shard_map/ppermute | solution.py:29
  93.5 2.0 %collective-permute-done.30 = bf16[8,2048]{1,0:T(8,128)(2,1)S(1)} collective-permute-done((bf16[8,2048]{1,0:T(8,128)(2,1)S(1)}, bf16[8,2048]{1,0:T(8,128)(2,1)S(1)}, u32[]{:S(2)}, u32[]{:S(2)}) %collective-permute-start.30) | collective-permute-done | bytes 32800 | tf_op jit(solution)/shard_map/ppermute | solution.py:29
  95.5 2.2 %collective-permute-done.21 = bf16[8,2048]{1,0:T(8,128)(2,1)S(1)} collective-permute-done((bf16[8,2048]{1,0:T(8,128)(2,1)S(1)}, bf16[8,2048]{1,0:T(8,128)(2,1)S(1)}, u32[]{:S(2)}, u32[]{:S(2)}) %collective-permute-start.21) | collective-permute-done | bytes 32800 | tf_op jit(solution)/shard_map/ppermute | solution.py:29
  (84 shorter events, 7.7 us)
Async XLA Ops:
  1.7 9.8 %collective-permute-start = (bf16[576,128]{1,0:T(8,128)(2,1)S(1)}, bf16[576,128]{1,0:T(8,128)(2,1)S(1)}, u32[]{:S(2)}, u32[]{:S(2)}) collective-permute-start(bf16[576,128]{1,0:T(8,128)(2,1)S(1)} %get-tuple-element.35.refs_0_), channel_id=1, source_target_pairs={{0,4},{4,8},{8,12},{12,0},{1,5},{5,9},{9,13},{13,1},{2,6},{6,10},{... | collective-permute-start | bytes 442376 | tf_op jit(solution)/shard_map/ppermute | solution.py:34
  4.7 18.2 %collective-permute-start.2 = (bf16[576,128]{1,0:T(8,128)(2,1)S(1)}, bf16[576,128]{1,0:T(8,128)(2,1)S(1)}, u32[]{:S(2)}, u32[]{:S(2)}) collective-permute-start(bf16[576,128]{1,0:T(8,128)(2,1)S(1)} %get-tuple-element.34.refs_1_), channel_id=1, source_target_pairs={{0,12},{4,0},{8,4},{12,8},{1,13},{5,1},{9,5},{13,9},{2,14},{6,2},{... | collective-permute-start | bytes 442376 | tf_op jit(solution)/shard_map/ppermute | solution.py:34
  13.8 6.9 %collective-permute-start.14 = (bf16[16,16]{1,0:T(8,128)(2,1)S(1)}, bf16[16,16]{1,0:T(8,128)(2,1)S(1)}, u32[]{:S(2)}, u32[]{:S(2)}) collective-permute-start(bf16[16,16]{1,0:T(8,128)(2,1)S(1)} %fusion.9), channel_id=1, source_target_pairs={{0,8},{4,12},{8,0},{12,4},{1,9},{5,13},{9,1},{13,5},{2,10},{6,14},... | collective-permute-start | bytes 1544 | tf_op jit(solution)/shard_map/ppermute | solution.py:29
  16.9 11.1 %collective-permute-start.4 = (bf16[576,128]{1,0:T(8,128)(2,1)S(1)}, bf16[576,128]{1,0:T(8,128)(2,1)S(1)}, u32[]{:S(2)}, u32[]{:S(2)}) collective-permute-start(bf16[576,128]{1,0:T(8,128)(2,1)S(1)} %get-tuple-element.34.refs_1_), channel_id=1, source_target_pairs={{0,4},{4,8},{8,12},{12,0},{1,5},{5,9},{9,13},{13,1},{2,6},{6,10},{... | collective-permute-start | bytes 442376 | tf_op jit(solution)/shard_map/ppermute | solution.py:34
  18.5 9.5 %collective-permute-start.5 = (bf16[576,128]{1,0:T(8,128)(2,1)S(1)}, bf16[576,128]{1,0:T(8,128)(2,1)S(1)}, u32[]{:S(2)}, u32[]{:S(2)}) collective-permute-start(bf16[576,128]{1,0:T(8,128)(2,1)S(1)} %get-tuple-element.35.refs_0_), channel_id=1, source_target_pairs={{0,12},{4,0},{8,4},{12,8},{1,13},{5,1},{9,5},{13,9},{2,14},{6,2},{... | collective-permute-start | bytes 442376 | tf_op jit(solution)/shard_map/ppermute | solution.py:34
  20.8 5.6 %collective-permute-start.15 = (bf16[32,16]{1,0:T(8,128)(2,1)S(1)}, bf16[32,16]{1,0:T(8,128)(2,1)S(1)}, u32[]{:S(2)}, u32[]{:S(2)}) collective-permute-start(bf16[32,16]{1,0:T(8,128)(2,1)S(1)} %pad_maximum_fusion.4), channel_id=1, source_target_pairs={{0,4},{4,0},{8,12},{12,8},{1,5},{5,1},{9,13},{13,9},{2,6},{6,2},{1... | collective-permute-start | bytes 3080 | tf_op jit(solution)/shard_map/ppermute | solution.py:29
  20.9 11.4 %collective-permute-start.1 = (bf16[576,128]{1,0:T(8,128)(2,1)S(1)}, bf16[576,128]{1,0:T(8,128)(2,1)S(1)}, u32[]{:S(2)}, u32[]{:S(2)}) collective-permute-start(bf16[576,128]{1,0:T(8,128)(2,1)S(1)} %collective-permute-done.refs_2_), channel_id=1, source_target_pairs={{0,4},{4,8},{8,12},{12,0},{1,5},{5,9},{9,13},{13,1},{2,6},{6,10},{... | collective-permute-start | bytes 442376 | tf_op jit(solution)/shard_map/ppermute | solution.py:34
  22.9 9.4 %collective-permute-start.3 = (bf16[576,128]{1,0:T(8,128)(2,1)S(1)}, bf16[576,128]{1,0:T(8,128)(2,1)S(1)}, u32[]{:S(2)}, u32[]{:S(2)}) collective-permute-start(bf16[576,128]{1,0:T(8,128)(2,1)S(1)} %collective-permute-done.2.refs_5_), channel_id=1, source_target_pairs={{0,12},{4,0},{8,4},{12,8},{1,13},{5,1},{9,5},{13,9},{2,14},{6,2},{... | collective-permute-start | bytes 442376 | tf_op jit(solution)/shard_map/ppermute | solution.py:34
  26.5 5.7 %collective-permute-start.16 = (bf16[64,16]{0,1:T(8,128)(2,1)S(1)}, bf16[64,16]{0,1:T(8,128)(2,1)S(1)}, u32[]{:S(2)}, u32[]{:S(2)}) collective-permute-start(bf16[64,16]{0,1:T(8,128)(2,1)S(1)} %pad_maximum_fusion.5), channel_id=1, source_target_pairs={{0,2},{1,3},{2,0},{3,1},{4,6},{5,7},{6,4},{7,5},{8,10},{9,11},{10,... | collective-permute-start | bytes 6152 | tf_op jit(solution)/shard_map/ppermute | solution.py:29
  28.0 0.9 copy-start.6
  28.9 0.7 copy-start.7
  32.3 14.9 %collective-permute-start.17 = (bf16[128,16]{0,1:T(8,128)(2,1)S(1)}, bf16[128,16]{0,1:T(8,128)(2,1)}, u32[]{:S(2)}, u32[]{:S(2)}) collective-permute-start(bf16[128,16]{0,1:T(8,128)(2,1)S(1)} %pad_maximum_fusion.6), channel_id=1, source_target_pairs={{0,1},{1,0},{2,3},{3,2},{4,5},{5,4},{6,7},{7,6},{8,9},{9,8},{10,11... | collective-permute-start | bytes 12296 | tf_op jit(solution)/shard_map/ppermute | solution.py:29
  32.3 2.2 %copy-start.2 = (bf16[1024,2048]{1,0:T(8,128)(2,1)S(1)}, bf16[1024,2048]{1,0:T(8,128)(2,1)}, u32[]{:S(2)}) copy-start(bf16[1024,2048]{1,0:T(8,128)(2,1)} %weight_hbm.1) | copy-start | bytes 12582916
  34.5 5.3 %copy-start.3 = (bf16[1,2048,2,384]{3,2,1,0:T(2,128)(2,1)S(1)}, bf16[1,2048,2,384]{3,2,1,0:T(2,128)(2,1)}, u32[]{:S(2)}) copy-start(bf16[1,2048,2,384]{3,2,1,0:T(2,128)(2,1)} %source) | copy-start | bytes 9437188
  37.1 11.5 %collective-permute-start.8 = (bf16[1,16,2048]{2,1,0:T(8,128)(2,1)S(1)}, bf16[1,16,2048]{2,1,0:T(8,128)(2,1)}, u32[]{:S(2)}, u32[]{:S(2)}) collective-permute-start(bf16[1,16,2048]{2,1,0:T(8,128)(2,1)S(1)} %bitcast.41), channel_id=1, source_target_pairs={{0,3},{1,2},{2,1},{3,0},{4,7},{5,6},{6,5},{7,4},{8,11},{9,10},{10,... | collective-permute-start | bytes 196616 | tf_op jit(solution)/shard_map/ppermute | solution.py:29
  37.7 10.8 %collective-permute-start.7 = (bf16[1,16,2048]{2,1,0:T(8,128)(2,1)S(1)}, bf16[1,16,2048]{2,1,0:T(8,128)(2,1)}, u32[]{:S(2)}, u32[]{:S(2)}) collective-permute-start(bf16[1,16,2048]{2,1,0:T(8,128)(2,1)S(1)} %bitcast.40), channel_id=1, source_target_pairs={{0,2},{1,3},{2,0},{3,1},{4,6},{5,7},{6,4},{7,5},{8,10},{9,11},{10,... | collective-permute-start | bytes 196616 | tf_op jit(solution)/shard_map/ppermute | solution.py:29
  39.2 9.3 %collective-permute-start.6 = (bf16[1,16,2048]{2,1,0:T(8,128)(2,1)S(1)}, bf16[1,16,2048]{2,1,0:T(8,128)(2,1)}, u32[]{:S(2)}, u32[]{:S(2)}) collective-permute-start(bf16[1,16,2048]{2,1,0:T(8,128)(2,1)S(1)} %bitcast.39), channel_id=1, source_target_pairs={{0,1},{1,0},{2,3},{3,2},{4,5},{5,4},{6,7},{7,6},{8,9},{9,8},{10,11... | collective-permute-start | bytes 196616 | tf_op jit(solution)/shard_map/ppermute | solution.py:29
  39.8 8.7 %copy-start.10 = (bf16[1,16,2048]{2,1,0:T(8,128)(2,1)S(1)}, bf16[1,16,2048]{2,1,0:T(8,128)(2,1)}, u32[]{:S(2)}) copy-start(bf16[1,16,2048]{2,1,0:T(8,128)(2,1)} %param.13) | copy-start | bytes 196612
  50.4 14.9 %copy-start.8 = (bf16[8,2048]{1,0:T(8,128)(2,1)}, bf16[8,2048]{1,0:T(8,128)(2,1)S(1)}, u32[]{:S(2)}) copy-start(bf16[8,2048]{1,0:T(8,128)(2,1)S(1)} %get-tuple-element.36) | copy-start | bytes 98308
  50.4 5.4 %collective-permute-start.22 = (bf16[8,2048]{1,0:T(8,128)(2,1)S(1)}, bf16[8,2048]{1,0:T(8,128)(2,1)S(1)}, u32[]{:S(2)}, u32[]{:S(2)}) collective-permute-start(bf16[8,2048]{1,0:T(8,128)(2,1)S(1)} %get-tuple-element.37), channel_id=1, source_target_pairs={{0,8},{4,12},{8,0},{12,4},{1,9},{5,13},{9,1},{13,5},{2,10},{6,14},... | collective-permute-start | bytes 98312 | tf_op jit(solution)/shard_map/ppermute | solution.py:29
  52.3 4.9 %collective-permute-start.9 = (bf16[8,2048]{1,0:T(8,128)(2,1)S(1)}, bf16[8,2048]{1,0:T(8,128)(2,1)S(1)}, u32[]{:S(2)}, u32[]{:S(2)}) collective-permute-start(bf16[8,2048]{1,0:T(8,128)(2,1)S(1)} %get-tuple-element.36), channel_id=1, source_target_pairs={{0,8},{4,12},{8,0},{12,4},{1,9},{5,13},{9,1},{13,5},{2,10},{6,14},... | collective-permute-start | bytes 98312 | tf_op jit(solution)/shard_map/ppermute | solution.py:29
  55.9 4.3 %collective-permute-start.23 = (bf16[16,2048]{1,0:T(8,128)(2,1)S(1)}, bf16[16,2048]{1,0:T(8,128)(2,1)S(1)}, u32[]{:S(2)}, u32[]{:S(2)}) collective-permute-start(bf16[16,2048]{1,0:T(8,128)(2,1)S(1)} %pad_maximum_fusion.3), channel_id=1, source_target_pairs={{0,4},{4,0},{8,12},{12,8},{1,5},{5,1},{9,13},{13,9},{2,6},{6,2},{1... | collective-permute-start | bytes 196616 | tf_op jit(solution)/shard_map/ppermute | solution.py:29
  57.3 4.0 %copy-start.9 = (bf16[8,2048]{1,0:T(8,128)(2,1)}, bf16[8,2048]{1,0:T(8,128)(2,1)S(1)}, u32[]{:S(2)}) copy-start(bf16[8,2048]{1,0:T(8,128)(2,1)S(1)} %collective-permute-done.9) | copy-start | bytes 98308
  57.9 7.4 %collective-permute-start.10 = (bf16[16,2048]{1,0:T(8,128)(2,1)}, bf16[16,2048]{1,0:T(8,128)(2,1)}, u32[]{:S(2)}, u32[]{:S(2)}) collective-permute-start(bf16[16,2048]{1,0:T(8,128)(2,1)} %pad_maximum_fusion.2), channel_id=1, source_target_pairs={{0,4},{4,0},{8,12},{12,8},{1,5},{5,1},{9,13},{13,9},{2,6},{6,2},{1... | collective-permute-start | bytes 196616 | tf_op jit(solution)/shard_map/ppermute | solution.py:29
  60.2 5.1 %collective-permute-start.24 = (bf16[32,2048]{1,0:T(8,128)(2,1)S(1)}, bf16[32,2048]{1,0:T(8,128)(2,1)}, u32[]{:S(2)}, u32[]{:S(2)}) collective-permute-start(bf16[32,2048]{1,0:T(8,128)(2,1)S(1)} %pad_maximum_fusion.1.refs_0_), channel_id=1, source_target_pairs={{0,2},{1,3},{2,0},{3,1},{4,6},{5,7},{6,4},{7,5},{8,10},{9,11},{10,... | collective-permute-start | bytes 393224 | tf_op jit(solution)/shard_map/ppermute | solution.py:29
  61.4 5.9 %collective-permute-start.25 = (bf16[32,2048]{1,0:T(8,128)(2,1)S(1)}, bf16[32,2048]{1,0:T(8,128)(2,1)S(1)}, u32[]{:S(2)}, u32[]{:S(2)}) collective-permute-start(bf16[32,2048]{1,0:T(8,128)(2,1)S(1)} %pad_maximum_fusion.1.refs_0_), channel_id=1, source_target_pairs={{0,1},{1,0},{2,3},{3,2},{4,5},{5,4},{6,7},{7,6},{8,9},{9,8},{10,11... | collective-permute-start | bytes 393224 | tf_op jit(solution)/shard_map/ppermute | solution.py:29
  65.3 1.9 %collective-permute-start.26 = (bf16[32,2048]{1,0:T(8,128)(2,1)}, bf16[32,2048]{1,0:T(8,128)(2,1)S(1)}, u32[]{:S(2)}, u32[]{:S(2)}) collective-permute-start(bf16[32,2048]{1,0:T(8,128)(2,1)} %collective-permute-done.24.refs_1_), channel_id=1, source_target_pairs={{0,1},{1,0},{2,3},{3,2},{4,5},{5,4},{6,7},{7,6},{8,9},{9,8},{10,11... | collective-permute-start | bytes 393224 | tf_op jit(solution)/shard_map/ppermute | solution.py:29
  66.2 6.6 %collective-permute-start.11 = (bf16[32,2048]{1,0:T(8,128)(2,1)S(1)}, bf16[32,2048]{1,0:T(8,128)(2,1)}, u32[]{:S(2)}, u32[]{:S(2)}) collective-permute-start(bf16[32,2048]{1,0:T(8,128)(2,1)S(1)} %pad_maximum_fusion.refs_0_), channel_id=1, source_target_pairs={{0,2},{1,3},{2,0},{3,1},{4,6},{5,7},{6,4},{7,5},{8,10},{9,11},{10,... | collective-permute-start | bytes 393224 | tf_op jit(solution)/shard_map/ppermute | solution.py:29
  67.2 1.4 %copy-start = (bf16[1,384,2048]{2,1,0:T(8,128)(2,1)S(1)}, bf16[1,384,2048]{2,1,0:T(8,128)(2,1)}, u32[]{:S(2)}) copy-start(bf16[1,384,2048]{2,1,0:T(8,128)(2,1)} %refs_5_.3) | copy-start | bytes 4718596
  71.5 0.8 copy-start.4
  72.3 6.2 %collective-permute-start.27 = (bf16[64,2048]{1,0:T(8,128)(2,1)}, bf16[64,2048]{1,0:T(8,128)(2,1)}, u32[]{:S(2)}, u32[]{:S(2)}) collective-permute-start(bf16[64,2048]{1,0:T(8,128)(2,1)} %get-tuple-element.31), channel_id=1, source_target_pairs={{0,1},{1,0},{2,3},{3,2},{4,5},{5,4},{6,7},{7,6},{8,9},{9,8},{10,11... | collective-permute-start | bytes 786440 | tf_op jit(solution)/shard_map/ppermute | solution.py:29
  72.5 1.5 %collective-permute-start.12 = (bf16[32,2048]{1,0:T(8,128)(2,1)S(1)}, bf16[32,2048]{1,0:T(8,128)(2,1)S(1)}, u32[]{:S(2)}, u32[]{:S(2)}) collective-permute-start(bf16[32,2048]{1,0:T(8,128)(2,1)S(1)} %pad_maximum_fusion.refs_0_), channel_id=1, source_target_pairs={{0,1},{1,0},{2,3},{3,2},{4,5},{5,4},{6,7},{7,6},{8,9},{9,8},{10,11... | collective-permute-start | bytes 393224 | tf_op jit(solution)/shard_map/ppermute | solution.py:29
  72.8 1.7 %collective-permute-start.13 = (bf16[32,2048]{1,0:T(8,128)(2,1)}, bf16[32,2048]{1,0:T(8,128)(2,1)}, u32[]{:S(2)}, u32[]{:S(2)}) collective-permute-start(bf16[32,2048]{1,0:T(8,128)(2,1)} %collective-permute-done.11.refs_1_), channel_id=1, source_target_pairs={{0,1},{1,0},{2,3},{3,2},{4,5},{5,4},{6,7},{7,6},{8,9},{9,8},{10,11... | collective-permute-start | bytes 393224 | tf_op jit(solution)/shard_map/ppermute | solution.py:29
  74.5 1.4 %copy-start.1 = (bf16[1,384,2048]{2,1,0:T(8,128)(2,1)S(1)}, bf16[1,384,2048]{2,1,0:T(8,128)(2,1)}, u32[]{:S(2)}) copy-start(bf16[1,384,2048]{2,1,0:T(8,128)(2,1)} %refs_5_.3) | copy-start | bytes 4718596
  75.9 2.6 %copy-start.5 = (f32[64,2048]{1,0:T(8,128)S(1)}, f32[64,2048]{1,0:T(8,128)}, u32[]{:S(2)}) copy-start(f32[64,2048]{1,0:T(8,128)} %copy-done.4) | copy-start | bytes 1572868
  78.2 2.5 %collective-permute-start.18 = (bf16[64,2048]{1,0:T(8,128)(2,1)S(1)}, bf16[64,2048]{1,0:T(8,128)(2,1)S(1)}, u32[]{:S(2)}, u32[]{:S(2)}) collective-permute-start(bf16[64,2048]{1,0:T(8,128)(2,1)S(1)} %get-tuple-element.29), channel_id=1, source_target_pairs={{0,1},{1,0},{2,3},{3,2},{4,5},{5,4},{6,7},{7,6},{8,9},{9,8},{10,11... | collective-permute-start | bytes 786440 | tf_op jit(solution)/shard_map/ppermute | solution.py:29
  79.5 6.4 %collective-permute-start.28 = (bf16[32,2048]{1,0:T(8,128)(2,1)S(1)}, bf16[32,2048]{1,0:T(8,128)(2,1)S(1)}, u32[]{:S(2)}, u32[]{:S(2)}) collective-permute-start(bf16[32,2048]{1,0:T(8,128)(2,1)S(1)} %slice.120), channel_id=1, source_target_pairs={{0,2},{1,3},{2,0},{3,1},{4,6},{5,7},{6,4},{7,5},{8,10},{9,11},{10,... | collective-permute-start | bytes 393224 | tf_op jit(solution)/shard_map/ppermute | solution.py:29
  80.7 7.3 %collective-permute-start.19 = (bf16[32,2048]{1,0:T(8,128)(2,1)S(1)}, bf16[32,2048]{1,0:T(8,128)(2,1)S(1)}, u32[]{:S(2)}, u32[]{:S(2)}) collective-permute-start(bf16[32,2048]{1,0:T(8,128)(2,1)S(1)} %slice.121), channel_id=1, source_target_pairs={{0,2},{1,3},{2,0},{3,1},{4,6},{5,7},{6,4},{7,5},{8,10},{9,11},{10,... | collective-permute-start | bytes 393224 | tf_op jit(solution)/shard_map/ppermute | solution.py:29
  86.0 4.4 %collective-permute-start.29 = (bf16[16,2048]{1,0:T(8,128)(2,1)S(1)}, bf16[16,2048]{1,0:T(8,128)(2,1)S(1)}, u32[]{:S(2)}, u32[]{:S(2)}) collective-permute-start(bf16[16,2048]{1,0:T(8,128)(2,1)S(1)} %slice.122), channel_id=1, source_target_pairs={{0,4},{4,0},{8,12},{12,8},{1,5},{5,1},{9,13},{13,9},{2,6},{6,2},{1... | collective-permute-start | bytes 196616 | tf_op jit(solution)/shard_map/ppermute | solution.py:29
  88.1 4.7 %collective-permute-start.20 = (bf16[16,2048]{1,0:T(8,128)(2,1)S(1)}, bf16[16,2048]{1,0:T(8,128)(2,1)S(1)}, u32[]{:S(2)}, u32[]{:S(2)}) collective-permute-start(bf16[16,2048]{1,0:T(8,128)(2,1)S(1)} %slice.123), channel_id=1, source_target_pairs={{0,4},{4,0},{8,12},{12,8},{1,5},{5,1},{9,13},{13,9},{2,6},{6,2},{1... | collective-permute-start | bytes 196616 | tf_op jit(solution)/shard_map/ppermute | solution.py:29
  90.4 5.1 %collective-permute-start.30 = (bf16[8,2048]{1,0:T(8,128)(2,1)S(1)}, bf16[8,2048]{1,0:T(8,128)(2,1)S(1)}, u32[]{:S(2)}, u32[]{:S(2)}) collective-permute-start(bf16[8,2048]{1,0:T(8,128)(2,1)S(1)} %slice.124), channel_id=1, source_target_pairs={{0,8},{4,12},{8,0},{12,4},{1,9},{5,13},{9,1},{13,5},{2,10},{6,14},... | collective-permute-start | bytes 98312 | tf_op jit(solution)/shard_map/ppermute | solution.py:29
  92.8 4.9 %collective-permute-start.21 = (bf16[8,2048]{1,0:T(8,128)(2,1)S(1)}, bf16[8,2048]{1,0:T(8,128)(2,1)S(1)}, u32[]{:S(2)}, u32[]{:S(2)}) collective-permute-start(bf16[8,2048]{1,0:T(8,128)(2,1)S(1)} %slice.125), channel_id=1, source_target_pairs={{0,8},{4,12},{8,0},{12,4},{1,9},{5,13},{9,1},{13,5},{2,10},{6,14},... | collective-permute-start | bytes 98312 | tf_op jit(solution)/shard_map/ppermute | solution.py:29

commit v3 on v2

v3 whole, which is shorter than its diff:
```python
import functools

import jax
import jax.numpy as jnp
from jax import lax
from jax.experimental import pallas as pl
from jax.experimental.pallas import tpu as pltpu
from jax.sharding import PartitionSpec as P

HEAD = 128

floor_value = -1e30
norm_epsilon = 1e-06


def normalize(hidden, norm_gain):
    widened = hidden.astype(jnp.float32)
    mean_square = jnp.mean(widened * widened, axis=-1, keepdims=True)
    return (widened * lax.rsqrt(mean_square + norm_epsilon) * norm_gain).astype(jnp.bfloat16)


def strides(count):
    assert count & (count - 1) == 0
    return [1 << bit for bit in reversed(range(count.bit_length() - 1))]


def swap(value, axis, stride):
    return lax.ppermute(value, axis, [(i, i ^ stride) for i in range(lax.axis_size(axis))])


def shift(value, axis, step):
    count = lax.axis_size(axis)
    return lax.ppermute(value, axis, [(i, (i + step) % count) for i in range(count)])


def whole_specs(count):
    return [pl.BlockSpec(memory_space=pltpu.VMEM)] * count


SMEM_SPEC = pl.BlockSpec(memory_space=pltpu.SMEM)
LIMIT = pltpu.CompilerParams(vmem_limit_bytes=16 * 1024 * 1024)


def stack_heads(queries):
    heads = queries.shape[1] // HEAD
    return jnp.concatenate(
        [queries[:, h * HEAD : (h + 1) * HEAD] for h in range(heads)], axis=0
    )


def page_partial(stacked, keys, values, page, length, place, fresh_block):
    rows, page_size = stacked.shape[0], keys.shape[0]
    slab_size = page_size - fresh_block
    scores = lax.dot_general(
        keys, stacked, (((1,), (1,)), ((), ())), preferred_element_type=jnp.float32
    )
    lanes = HEAD if HEAD % fresh_block == 0 and rows % HEAD == 0 else rows
    offset = lax.broadcasted_iota(jnp.int32, (slab_size, lanes), 0)
    fresh = page * fresh_block + lax.broadcasted_iota(jnp.int32, (fresh_block, lanes), 0)
    lane = lax.broadcasted_iota(jnp.int32, (fresh_block, lanes), 1)
    position = place * fresh_block + lax.rem(lane, fresh_block)
    bias = jnp.concatenate(
        [
            jnp.where(offset < length, 0.0, floor_value),
            jnp.where(fresh <= position, 0.0, floor_value),
        ],
        axis=0,
    )
    masked = scores + jnp.concatenate([bias] * (rows // lanes), axis=1)
    peak = jnp.max(masked, axis=0, keepdims=True)
    weights = jnp.exp((masked - peak) * (HEAD**-0.5))
    total = jnp.sum(weights, axis=0, keepdims=True)
    summed = lax.dot_general(
        values,
        weights.astype(jnp.bfloat16),
        (((0,), (0,)), ((), ())),
        preferred_element_type=jnp.float32,
    )
    return peak, total, summed


def merge(first, second):
    peak = jnp.maximum(first[0], second[0])
    scale_first = jnp.exp((first[0] - peak) * (HEAD**-0.5))
    scale_second = jnp.exp((second[0] - peak) * (HEAD**-0.5))
    return (
        peak,
        first[1] * scale_first + second[1] * scale_second,
        first[2] * scale_first + second[2] * scale_second,
    )


def page_at(offset):
    count = lax.axis_size("ctx")
    return lax.rem(lax.axis_index("ctx") + offset + count, count)


def early_kernel(offsets, last, fresh_block, lengths, queries, *refs):
    count = len(offsets)
    pages, (peak_out, total_out, summed_out, length_out) = refs[: 2 * count], refs[-4:]
    length_out[...] = jnp.full(length_out.shape, lengths[page_at(last)], jnp.int32)
    stacked = stack_heads(queries[...])
    place = lax.axis_index("ctx")
    state = None
    for number, offset in enumerate(offsets):
        page = page_at(offset)
        part = page_partial(
            stacked,
            pages[2 * number][...],
            pages[2 * number + 1][...],
            page,
            lengths[page],
            place,
            fresh_block,
        )
        state = part if state is None else merge(state, part)
    peak_out[...] = state[0]
    total_out[...] = state[1]
    summed_out[...] = state[2]


def late_kernel(
    offset,
    fresh_block,
    queries,
    keys,
    values,
    peak,
    total,
    summed,
    length,
    weight,
    context_out,
    own_out,
    *rest,
):
    sent_outs, blocks = rest[:-1], rest[-1]
    page = page_at(offset)
    part = page_partial(
        stack_heads(queries[...]),
        keys[...],
        values[...],
        page,
        length[...],
        lax.axis_index("ctx"),
        fresh_block,
    )
    state = merge((peak[...], total[...], summed[...]), part)
    result = jnp.transpose(state[2] / state[1])
    context = jnp.concatenate(
        [
            result[h * fresh_block : (h + 1) * fresh_block]
            for h in range(result.shape[0] // fresh_block)
        ],
        axis=1,
    ).astype(jnp.bfloat16)
    context_out[...] = context
    blocks[...] = jnp.dot(context, weight[...], preferred_element_type=jnp.float32)
    place = lax.axis_index("exp")
    size = own_out.shape[0]
    pick = lambda index: blocks[pl.ds(pl.multiple_of(index * size, size), size), :]
    own_out[...] = pick(place)
    for step, out in enumerate(sent_outs, 1):
        out[...] = pick(place ^ step).astype(jnp.bfloat16)


def attention(queries, pages, lengths, out_weight, token_block, later):
    fresh_block, width = queries.shape
    rows = width // HEAD * fresh_block
    count = lax.axis_size("ctx")
    exp_count = lax.axis_size("exp")
    model_width = out_weight.shape[1]
    own_keys, own_values = pages[:, 0], pages[:, 1]
    held = [(0, own_keys, own_values)]
    left_keys, left_values = own_keys, own_values
    right_keys, right_values = own_keys, own_values
    for step in range(1, (count - 1) // 2 + 1):
        left_keys = shift(left_keys, "ctx", 1)
        right_values = shift(right_values, "ctx", -1)
        left_values = shift(left_values, "ctx", 1)
        right_keys = shift(right_keys, "ctx", -1)
        held.append((-step, left_keys, left_values))
        held.append((step, right_keys, right_values))
    if count % 2 == 0:
        last = (count // 2, shift(left_keys, "ctx", 1), shift(right_values, "ctx", -1))
    else:
        last = held.pop()
    page_flops = 4 * rows * pages.shape[0] * HEAD
    line = jax.ShapeDtypeStruct((1, rows), jnp.float32)
    state = None
    for start in range(0, len(held), 3):
        group = held[start : start + 3]
        operands = [part for _, keys, values in group for part in (keys, values)]
        held_operands = () if start else (out_weight, *later)
        partial_state = pl.pallas_call(
            functools.partial(
                early_kernel, [offset for offset, _, _ in group], last[0], fresh_block
            ),
            out_shape=(
                line,
                line,
                jax.ShapeDtypeStruct((HEAD, rows), jnp.float32),
                jax.ShapeDtypeStruct((1, HEAD), jnp.int32),
            ),
            in_specs=[SMEM_SPEC]
            + whole_specs(1 + len(operands))
            + [pl.BlockSpec(memory_space=pl.ANY)] * len(held_operands),
            out_specs=tuple(whole_specs(4)),
            compiler_params=LIMIT,
            cost_estimate=pl.CostEstimate(
                flops=len(group) * page_flops, bytes_accessed=2 << 20, transcendentals=0
            ),
        )(lengths, queries, *operands, *held_operands)
        partial_state, length = partial_state[:3], partial_state[3]
        state = partial_state if state is None else merge(state, partial_state)
    block = jax.ShapeDtypeStruct((token_block, model_width), jnp.bfloat16)
    outs = pl.pallas_call(
        functools.partial(late_kernel, last[0], fresh_block),
        out_shape=(
            jax.ShapeDtypeStruct(queries.shape, jnp.bfloat16),
            jax.ShapeDtypeStruct(block.shape, jnp.float32),
        )
        + (block,) * (exp_count - 1),
        in_specs=whole_specs(8),
        out_specs=tuple(whole_specs(1 + exp_count)),
        scratch_shapes=[pltpu.VMEM((fresh_block, model_width), jnp.float32)],
        compiler_params=LIMIT,
        cost_estimate=pl.CostEstimate(
            flops=page_flops + 2 * fresh_block * width * model_width,
            bytes_accessed=6 << 20,
            transcendentals=0,
        ),
    )(queries, last[1], last[2], *state, length, out_weight)
    return outs[0], outs[1], outs[2:]


def finish_kernel(count, *refs):
    parts, (residual, gain, ids, scores, hidden_out, sent_out) = refs[:count], refs[count:]
    total = residual[...].astype(jnp.float32)
    for part in parts:
        total = total + part[...].astype(jnp.float32)
    hidden = total.astype(jnp.bfloat16)
    hidden_out[...] = hidden
    width = hidden.shape[1]
    sent_out[:, :width] = normalize(hidden, gain[...])
    chosen = scores[...]
    combine = (chosen / jnp.sum(chosen, axis=1, keepdims=True)).astype(jnp.bfloat16)
    combine = combine.astype(jnp.float32)
    tokens, choices = chosen.shape
    expert = lax.broadcasted_iota(jnp.int32, (tokens, sent_out.shape[1] - width), 1)
    dense = jnp.zeros(expert.shape, jnp.float32)
    for k in range(choices):
        dense = dense + jnp.where(ids[:, k : k + 1] == expert, combine[:, k : k + 1], 0.0)
    sent_out[:, width:] = dense.astype(jnp.bfloat16)


def finish(parts, residual, norm_gain, ids, scores, expert_count):
    tokens, width = residual.shape
    lanes = -(-expert_count // 128) * 128
    return pl.pallas_call(
        functools.partial(finish_kernel, len(parts)),
        out_shape=(
            jax.ShapeDtypeStruct((tokens, width), jnp.bfloat16),
            jax.ShapeDtypeStruct((tokens, width + lanes), jnp.bfloat16),
        ),
        in_specs=whole_specs(len(parts) + 4),
        out_specs=tuple(whole_specs(2)),
        compiler_params=LIMIT,
        cost_estimate=pl.CostEstimate(
            flops=8 * residual.size, bytes_accessed=1 << 19, transcendentals=0
        ),
    )(*parts, residual, norm_gain[None], ids, scores)


def down_kernel(inner, rows, down, out):
    expert = lax.axis_index("ctx") * lax.axis_size("exp") + lax.axis_index("exp")
    gate = inner[0]
    activated = (gate / (1.0 + jnp.exp(-gate)) * inner[1]).astype(jnp.bfloat16)
    piece = jnp.dot(activated, down[0], preferred_element_type=jnp.float32)
    dense = rows[:, out.shape[1] :].astype(jnp.float32)
    lane = lax.broadcasted_iota(jnp.int32, dense.shape, 1)
    scale = jnp.sum(jnp.where(lane == expert, dense, 0.0), axis=1, keepdims=True)
    out[...] = (piece.astype(jnp.bfloat16).astype(jnp.float32) * scale).astype(out.dtype)


def expert_apply(rows, gate_up, down, kind):
    _, hidden, width = down.shape
    inner = jnp.einsum(
        "nd,dgh->gnh", rows[:, :width], gate_up[0], preferred_element_type=jnp.float32
    )
    return pl.pallas_call(
        down_kernel,
        out_shape=jax.ShapeDtypeStruct((rows.shape[0], width), kind),
        in_specs=whole_specs(3),
        out_specs=whole_specs(1)[0],
        compiler_params=LIMIT,
        cost_estimate=pl.CostEstimate(
            flops=2 * rows.shape[0] * width * hidden, bytes_accessed=2 << 20, transcendentals=0
        ),
    )(inner, rows, down)


def gather_near(rows, near):
    pieces = [rows]
    for stride in near:
        pieces = pieces + [swap(piece, "exp", stride) for piece in pieces]
    return pieces


def return_near(values, near):
    for stride in reversed(near):
        half = len(values) // 2
        values = [
            keep.astype(jnp.float32)
            + swap(send.astype(jnp.bfloat16), "exp", stride).astype(jnp.float32)
            for keep, send in zip(values[:half], values[half:])
        ]
    return values[0].astype(jnp.float32)


def mixture_of(rows, gate_up, down):
    tokens = rows.shape[0]
    ctx_count = lax.axis_size("ctx")
    exp_strides = strides(lax.axis_size("exp"))
    far, near = exp_strides[:1], exp_strides[1:]

    blocks = {0: rows}
    for offset in reversed(range(1, ctx_count)):
        blocks[offset] = swap(rows, "ctx", offset)
    half = ctx_count // 2
    chunks = [list(range(half, ctx_count)), list(range(half))] if half else [[0]]
    sent = [jnp.concatenate([blocks[offset] for offset in chunk], axis=0) for chunk in chunks]

    def results(pieces):
        half = (len(pieces) + 1) // 2
        kinds = [jnp.float32] * half + [jnp.bfloat16] * (len(pieces) - half)
        values = [expert_apply(piece, gate_up, down, kind) for piece, kind in zip(pieces, kinds)]
        return return_near(values, near)

    crossed = [[swap(piece, "exp", stride) for stride in far] for piece in sent]
    totals = {}
    for chunk, home, away in zip(chunks, sent, crossed):
        value = results(gather_near(home, near))
        for piece in away:
            other = results(gather_near(piece, near)).astype(jnp.bfloat16)
            value = value + swap(other, "exp", far[0]).astype(jnp.float32)
        for position, offset in enumerate(chunk):
            totals[offset] = value[position * tokens : (position + 1) * tokens]
    total = totals[0]
    for offset in reversed(range(1, ctx_count)):
        total = total + swap(totals[offset].astype(jnp.bfloat16), "ctx", offset).astype(jnp.float32)
    return total


def per_device(
    queries,
    pages,
    cached_lengths,
    residual_in,
    out_weight,
    norm_gain,
    expert_ids,
    route_scores,
    expert_input,
    expert_output,
):
    requests = queries.shape[0]
    core_place = lax.axis_index("rep")
    rep_count = lax.axis_size("rep")
    exp_count = lax.axis_size("exp")
    expert_count = lax.axis_size("ctx") * exp_count
    token_block, model_width = residual_in.shape[1:]
    token_count = requests * token_block

    contexts, owns, sents = [], [], []
    for r in range(requests):
        context, own, sent = attention(
            queries[r],
            pages[r],
            cached_lengths[r],
            out_weight,
            token_block,
            (residual_in, norm_gain, expert_output, expert_ids, route_scores),
        )
        contexts.append(context)
        owns.append(own)
        sents.append(sent)
    context = jnp.stack(contexts)

    parts = [jnp.concatenate(owns, axis=0)]
    for step in range(1, exp_count):
        blocks = jnp.concatenate([sent[step - 1] for sent in sents], axis=0)
        parts.append(swap(blocks, "exp", step))
    residual, ids, scores = residual_in, expert_ids, route_scores
    if rep_count > 1:
        share_size = token_block // rep_count
        share = sum(part.astype(jnp.float32) for part in parts).astype(jnp.bfloat16)
        share = share.reshape(requests, token_block, model_width)
        share = lax.psum_scatter(share, "rep", scatter_dimension=1, tiled=True)
        parts = [share.reshape(-1, model_width)]
        residual, ids, scores = (
            lax.dynamic_slice_in_dim(whole, core_place * share_size, share_size, 1)
            for whole in (residual, ids, scores)
        )
    own_hidden, normed = finish(
        parts,
        residual.reshape(-1, model_width),
        norm_gain,
        ids.reshape(-1, ids.shape[2]),
        scores.reshape(-1, ids.shape[2]),
        expert_count,
    )
    own_hidden = own_hidden.reshape(requests, -1, model_width)
    if rep_count > 1:
        normed = normed.reshape(requests, share_size, -1)
        normed = lax.all_gather(normed, "rep", axis=1, tiled=True)
        normed = normed.reshape(token_count, -1)

    mixture = mixture_of(normed, expert_input, expert_output)
    mixture = mixture.reshape(requests, token_block, model_width)
    if rep_count > 1:
        mixture = lax.psum_scatter(
            mixture.astype(jnp.bfloat16), "rep", scatter_dimension=1, tiled=True
        ).astype(jnp.float32)
    layer_out = (own_hidden.astype(jnp.float32) + mixture).astype(jnp.bfloat16)
    return (context, layer_out)


def solution(mesh):
    in_specs = (
        P("groups", "ctx", ("exp", "rep")),
        P("groups", "ctx", None, "exp"),
        P("groups", None),
        P("groups", ("ctx", "exp"), None),
        P(("exp", "rep"), None),
        P(),
        P("groups", ("ctx", "exp"), None),
        P("groups", ("ctx", "exp"), None),
        P(("ctx", "exp"), None, None, "rep"),
        P(("ctx", "exp"), "rep", None),
    )
    out_specs = (P("groups", "ctx", ("exp", "rep")), P("groups", ("ctx", "exp", "rep"), None))
    return jax.shard_map(
        per_device, mesh=mesh, in_specs=in_specs, out_specs=out_specs, check_vma=False
    )
```

time: 99 us -> 79.9 us (0.81)
  waiting for transfers between devices: 30.9 us -> 21 us
  Pallas kernels: 17.6 us -> 9.99 us
  other arithmetic: 8.23 us -> 0.85 us
  matrix products: 0 us -> 5.16 us
  local copies, waits for them, and re-layouts: 11.2 us -> 12.3 us
    ppermute x25 -> x21, waiting for transfers between devices: 26.3 us -> 15.7 us  [swap(): lax.ppermute(value, axis, [(i, i ^ stride) for i in range(lax.axis_size(a...]
    pallas_call x3 -> x9, Pallas kernels: 12.4 us -> 3.38 us  [the longest x8 3.19 us: expert_apply(): pl.pallas_call(down_kernel, out_shape=jax.ShapeDtypeStruct((rows.shape[0]...]
    dot_general x0 -> x8, matrix products: none -> 5.16 us  [expert_apply(): jnp.einsum('nd,dgh->gnh', rows[:, :width], gate_up[0], preferred_element_...]
    reduce_sum x4 -> x0, other arithmetic: 2.68 us -> none  [the longest x1 1.07 us: normalize(): mean_square = jnp.mean(widened * widened, axis=-1, keepdims=True)]
    reshape x3 -> x2, local copies, waits for them, and re-layouts: 0.23 us -> 2.11 us  [the longest x1 1.35 us: per_device(): scores.reshape(-1, ids.shape[2])]
    unnamed x23 -> x29, local copies, waits for them, and re-layouts: 8.37 us -> 10.1 us
    concatenate x7 -> x0, other arithmetic: 1.7 us -> none  [the longest x6 1.61 us: gather_column(): rows = jnp.concatenate([rows, swap(rows, 'ctx', stride)], axis=0)]
    concatenate x1 -> x2, local copies, waits for them, and re-layouts: 1.36 us -> 0.03 us  [mixture_of(): jnp.concatenate([blocks[offset] for offset in chunk], axis=0)]
  transfers between devices with their start and end apart: 31 -> 27, of which waited for: 14 -> 10; matrix products, arithmetic and copies ran while one was open for 9% -> 11% of each run, Pallas kernels for 18% -> 8%
where the time goes in v3:
time: 79.9 us; the launch traced here: 79.4 us
  starting transfers between devices  29.3 us (37%)
  waiting for transfers between devices  21 us (26%)
  local copies, waits for them, and re-layouts  12.3 us (15%)
  Pallas kernels  9.99 us (13%)
  matrix products  5.16 us (6%)
  between operations  0.88 us (1%)
  other arithmetic  0.85 us (1%)
    ppermute x21, starting transfers between devices, swap(): lax.ppermute(value, axis, [(i, i ^ stride) for i in range(lax.axis_size(a...  16.6 us
    ppermute x21, waiting for transfers between devices, swap(): lax.ppermute(value, axis, [(i, i ^ stride) for i in range(lax.axis_size(a...  15.7 us
    ppermute x6, starting transfers between devices, shift(): lax.ppermute(value, axis, [(i, (i + step) % count) for i in range(count)])  12.7 us
    unnamed x29, local copies, waits for them, and re-layouts  10.1 us
    ppermute x6, waiting for transfers between devices, shift(): lax.ppermute(value, axis, [(i, (i + step) % count) for i in range(count)])  5.35 us
    dot_general x8, matrix products, expert_apply(): jnp.einsum('nd,dgh->gnh', rows[:, :width], gate_up[0], preferred_element_...  5.16 us
    pallas_call x1, Pallas kernels, attention(): pl.pallas_call(functools.partial(early_kernel, [offset for offset, _, _ i...  3.32 us
    pallas_call x1, Pallas kernels, attention(): pl.pallas_call(functools.partial(late_kernel, last[0], fresh_block), out_...  3.3 us
  transfers between devices with their start and end apart: 27, of which 10 were waited for; matrix products, arithmetic and copies ran while one was open for 11% of the time, Pallas kernels for 8%

profile of v3, /device:TPU:0, one launch (start us, length us, event | category | flops | bytes accessed | tf_op | source)
XLA Modules:
  0.0 79.4 jit_solution(15908856997848178910)
XLA Ops:
  0.6 1.2 %copy.42 = bf16[1,576,2,128]{3,1,2,0:T(8,128)(2,1)S(1)} copy(bf16[1,576,2,128]{3,2,1,0:T(2,128)(2,1)} %param.11) | data formatting | bytes 589824 | tf_op args[1]
  1.8 3.1 %collective-permute-start = (bf16[576,128]{1,0:T(8,128)(2,1)S(1)}, bf16[576,128]{1,0:T(8,128)(2,1)}, u32[]{:S(2)}, u32[]{:S(2)}) collective-permute-start(bf16[576,128]{1,0:T(8,128)(2,1)S(1)} %get-tuple-element.25.refs_0_), channel_id=1, source_target_pairs={{0,4},{4,8},{8,12},{12,0},{1,5},{5,9},{9,13},{13,1},{2,6},{6,10},{... | collective-permute-start | bytes 442376 | tf_op jit(solution)/shard_map/ppermute | solution.py:33
  4.9 2.1 %collective-permute-start.2 = (bf16[576,128]{1,0:T(8,128)(2,1)S(1)}, bf16[576,128]{1,0:T(8,128)(2,1)}, u32[]{:S(2)}, u32[]{:S(2)}) collective-permute-start(bf16[576,128]{1,0:T(8,128)(2,1)S(1)} %get-tuple-element.24.refs_1_), channel_id=1, source_target_pairs={{0,12},{4,0},{8,4},{12,8},{1,13},{5,1},{9,5},{13,9},{2,14},{6,2},{... | collective-permute-start | bytes 442376 | tf_op jit(solution)/shard_map/ppermute | solution.py:33
  7.0 3.8 %collective-permute-start.5 = (bf16[576,128]{1,0:T(8,128)(2,1)S(1)}, bf16[576,128]{1,0:T(8,128)(2,1)}, u32[]{:S(2)}, u32[]{:S(2)}) collective-permute-start(bf16[576,128]{1,0:T(8,128)(2,1)S(1)} %get-tuple-element.25.refs_0_), channel_id=1, source_target_pairs={{0,12},{4,0},{8,4},{12,8},{1,13},{5,1},{9,5},{13,9},{2,14},{6,2},{... | collective-permute-start | bytes 442376 | tf_op jit(solution)/shard_map/ppermute | solution.py:33
  10.8 0.9 %collective-permute-done.refs_2_ = bf16[576,128]{1,0:T(8,128)(2,1)} collective-permute-done((bf16[576,128]{1,0:T(8,128)(2,1)S(1)}, bf16[576,128]{1,0:T(8,128)(2,1)}, u32[]{:S(2)}, u32[]{:S(2)}) %collective-permute-start) | collective-permute-done | bytes 147488 | tf_op jit(solution)/shard_map/ppermute | solution.py:33
  11.8 1.8 %collective-permute-start.1 = (bf16[576,128]{1,0:T(8,128)(2,1)}, bf16[576,128]{1,0:T(8,128)(2,1)}, u32[]{:S(2)}, u32[]{:S(2)}) collective-permute-start(bf16[576,128]{1,0:T(8,128)(2,1)} %collective-permute-done.refs_2_), channel_id=1, source_target_pairs={{0,4},{4,8},{8,12},{12,0},{1,5},{5,9},{9,13},{13,1},{2,6},{6,10},{... | collective-permute-start | bytes 442376 | tf_op jit(solution)/shard_map/ppermute | solution.py:33
  13.6 1.5 %collective-permute-done.2.refs_5_ = bf16[576,128]{1,0:T(8,128)(2,1)} collective-permute-done((bf16[576,128]{1,0:T(8,128)(2,1)S(1)}, bf16[576,128]{1,0:T(8,128)(2,1)}, u32[]{:S(2)}, u32[]{:S(2)}) %collective-permute-start.2) | collective-permute-done | bytes 147488 | tf_op jit(solution)/shard_map/ppermute | solution.py:33
  15.1 1.9 %collective-permute-start.3 = (bf16[576,128]{1,0:T(8,128)(2,1)}, bf16[576,128]{1,0:T(8,128)(2,1)}, u32[]{:S(2)}, u32[]{:S(2)}) collective-permute-start(bf16[576,128]{1,0:T(8,128)(2,1)} %collective-permute-done.2.refs_5_), channel_id=1, source_target_pairs={{0,12},{4,0},{8,4},{12,8},{1,13},{5,1},{9,5},{13,9},{2,14},{6,2},{... | collective-permute-start | bytes 442376 | tf_op jit(solution)/shard_map/ppermute | solution.py:33
  16.9 0.8 copy.13.refs_10_
  17.7 0.8 copy.14.refs_11_
  18.5 2.9 %collective-permute-done.5.refs_4_ = bf16[576,128]{1,0:T(8,128)(2,1)} collective-permute-done((bf16[576,128]{1,0:T(8,128)(2,1)S(1)}, bf16[576,128]{1,0:T(8,128)(2,1)}, u32[]{:S(2)}, u32[]{:S(2)}) %collective-permute-start.5) | collective-permute-done | bytes 147488 | tf_op jit(solution)/shard_map/ppermute | solution.py:33
  21.4 1.4 %copy-done.1 = bf16[1,384,2048]{2,1,0:T(8,128)(2,1)S(1)} copy-done((bf16[1,384,2048]{2,1,0:T(8,128)(2,1)S(1)}, bf16[1,384,2048]{2,1,0:T(8,128)(2,1)}, u32[]{:S(2)}) %copy-start.1) | copy-done | bytes 1572888
  22.8 2.2 %copy-done.3 = bf16[1024,2048]{1,0:T(8,128)(2,1)S(1)} copy-done((bf16[1024,2048]{1,0:T(8,128)(2,1)S(1)}, bf16[1024,2048]{1,0:T(8,128)(2,1)}, u32[]{:S(2)}) %copy-start.3) | copy-done | bytes 4194328
  25.0 0.9 %copy-done.5 = bf16[1,64,1024]{2,1,0:T(8,128)(2,1)S(1)} copy-done((bf16[1,64,1024]{2,1,0:T(8,128)(2,1)S(1)}, bf16[1,64,1024]{2,1,0:T(8,128)(2,1)}, u32[]{:S(2)}) %copy-start.5) | copy-done | bytes 131096
  25.9 0.8 %copy-done.6 = bf16[1,16,2048]{2,1,0:T(8,128)(2,1)S(1)} copy-done((bf16[1,16,2048]{2,1,0:T(8,128)(2,1)S(1)}, bf16[1,16,2048]{2,1,0:T(8,128)(2,1)}, u32[]{:S(2)}) %copy-start.6) | copy-done | bytes 65560
  26.7 0.7 copy-done.8
  27.4 0.7 copy-done.11
  28.1 3.3 %shard_map.113 = (f32[1,512]{1,0:T(1,128)S(1)}, f32[1,512]{1,0:T(1,128)S(1)}, f32[128,512]{1,0:T(8,128)S(1)}, s32[1,128]{1,0:T(1,128)S(1)}) custom-call(s32[4]{0:T(128)S(1)} %bitcast.69, bf16[64,1024]{1,0:T(8,128)(2,1)S(1)} %bitcast.65, bf16[576,128]{1,0:T(8,128)(2,1)S(1)} %get-tuple-element.25.refs_0_, bf16[576,128]{1,0:T(8,128)(2,1)S(1)} %get-tuple-element.24.refs_1_, ...), custom_call_target="tpu_custom_call" | custom-call | flops 452984832 | bytes 2097152 | tf_op jit(solution)/shard_map/pallas_call | solution.py:195
  31.4 3.3 %shard_map.114 = (bf16[64,1024]{1,0:T(8,128)(2,1)}, f32[16,2048]{1,0:T(8,128)S(1)}, bf16[16,2048]{1,0:T(8,128)(2,1)}, bf16[16,2048]{1,0:T(8,128)(2,1)}, bf16[16,2048]{1,0:T(8,128)(2,1)}) custom-call(bf16[64,1024]{1,0:T(8,128)(2,1)S(1)} %bitcast.66, bf16[576,128]{1,0:T(8,128)(2,1)} %collective-permute-done.1.keys, ...), custom_call_target="tpu_custom_call" | custom-call | flops 419430400 | bytes 6291456 | tf_op jit(solution)/shard_map/pallas_call | solution.py:217
  34.7 1.7 %collective-permute-start.7 = (bf16[16,2048]{1,0:T(8,128)(2,1)}, bf16[16,2048]{1,0:T(8,128)(2,1)S(1)}, u32[]{:S(2)}, u32[]{:S(2)}) collective-permute-start(bf16[16,2048]{1,0:T(8,128)(2,1)} %get-tuple-element.20), channel_id=1, source_target_pairs={{0,2},{1,3},{2,0},{3,1},{4,6},{5,7},{6,4},{7,5},{8,10},{9,11},{10,... | collective-permute-start | bytes 196616 | tf_op jit(solution)/shard_map/ppermute | solution.py:28
  36.6 0.8 copy.15.refs_6_
  37.4 1.3 %copy.16.refs_7_ = f32[16,8]{1,0:T(8,128)} copy(f32[16,8]{0,1:T(8,128)} %bitcast.72) | data formatting | bytes 1024 | tf_op jit(solution)/shard_map/reshape | solution.py:410
  38.7 0.7 collective-permute-done.7.refs_2_
  39.5 1.3 %collective-permute-done.8.refs_3_ = bf16[16,2048]{1,0:T(8,128)(2,1)S(1)} collective-permute-done((bf16[16,2048]{1,0:T(8,128)(2,1)}, bf16[16,2048]{1,0:T(8,128)(2,1)S(1)}, u32[]{:S(2)}, u32[]{:S(2)}) %collective-permute-start.8) | collective-permute-done | bytes 65568 | tf_op jit(solution)/shard_map/ppermute | solution.py:28
  40.8 0.7 copy-done.10
  41.7 0.8 collective-permute-start.16
  42.4 2.2 %collective-permute-start.17 = (bf16[16,2176]{1,0:T(8,128)(2,1)S(1)}, bf16[16,2176]{1,0:T(8,128)(2,1)S(1)}, u32[]{:S(2)}, u32[]{:S(2)}) collective-permute-start(bf16[16,2176]{1,0:T(8,128)(2,1)S(1)} %get-tuple-element.23), channel_id=1, source_target_pairs={{0,12},{4,8},{8,4},{12,0},{1,13},{5,9},{9,5},{13,1},{2,14},{6,10},... | collective-permute-start | bytes 208904 | tf_op jit(solution)/shard_map/ppermute | solution.py:28
  44.6 0.6 collective-permute-start.9
  45.2 4.7 %collective-permute-done.16 = bf16[16,2176]{1,0:T(8,128)(2,1)S(1)} collective-permute-done((bf16[16,2176]{1,0:T(8,128)(2,1)S(1)}, bf16[16,2176]{1,0:T(8,128)(2,1)S(1)}, u32[]{:S(2)}, u32[]{:S(2)}) %collective-permute-start.16) | collective-permute-done | bytes 69664 | tf_op jit(solution)/shard_map/ppermute | solution.py:28
  50.0 1.6 %collective-permute-start.20 = (bf16[32,2176]{1,0:T(8,128)(2,1)S(1)}, bf16[32,2176]{1,0:T(8,128)(2,1)S(1)}, u32[]{:S(2)}, u32[]{:S(2)}) collective-permute-start(bf16[32,2176]{1,0:T(8,128)(2,1)S(1)} %constant_dynamic-update-slice_fusion.2.rows), channel_id=1, source_target_pairs={{0,2},{1,3},{2,0},{3,1},{4,6},{5,7},{6,4},{7,5},{8,10},{9,11},{10,... | collective-permute-start | bytes 417800 | tf_op jit(solution)/shard_map/ppermute | solution.py:28
  51.6 0.6 convolution_bitcast_fusion.3.inner
  52.5 0.6 convolution_bitcast_fusion.7.inner
  54.5 0.6 convolution_bitcast_fusion.2.inner
  55.7 0.6 convolution_bitcast_fusion.6.inner
  57.3 0.6 convolution_bitcast_fusion.1.inner
  58.0 1.1 %collective-permute-done.12.rows = bf16[32,2176]{1,0:T(8,128)(2,1)S(1)} collective-permute-done((bf16[32,2176]{1,0:T(8,128)(2,1)S(1)}, bf16[32,2176]{1,0:T(8,128)(2,1)S(1)}, u32[]{:S(2)}, u32[]{:S(2)}) %collective-permute-start.12) | collective-permute-done | bytes 139296 | tf_op jit(solution)/shard_map/ppermute | solution.py:28
  59.1 0.6 convolution_bitcast_fusion.5.inner
  60.5 0.6 convolution_bitcast_fusion.inner
  62.2 0.6 convolution_bitcast_fusion.4.inner
  63.4 1.6 %collective-permute-start.23 = (bf16[32,2048]{1,0:T(8,128)(2,1)S(1)}, bf16[32,2048]{1,0:T(8,128)(2,1)S(1)}, u32[]{:S(2)}, u32[]{:S(2)}) collective-permute-start(bf16[32,2048]{1,0:T(8,128)(2,1)S(1)} %add_convert_fusion.1), channel_id=1, source_target_pairs={{0,2},{1,3},{2,0},{3,1},{4,6},{5,7},{6,4},{7,5},{8,10},{9,11},{10,... | collective-permute-start | bytes 393224 | tf_op jit(solution)/shard_map/ppermute | solution.py:28
  65.0 1.3 %collective-permute-start.15 = (bf16[32,2048]{1,0:T(8,128)(2,1)S(1)}, bf16[32,2048]{1,0:T(8,128)(2,1)S(1)}, u32[]{:S(2)}, u32[]{:S(2)}) collective-permute-start(bf16[32,2048]{1,0:T(8,128)(2,1)S(1)} %add_convert_fusion.2), channel_id=1, source_target_pairs={{0,2},{1,3},{2,0},{3,1},{4,6},{5,7},{6,4},{7,5},{8,10},{9,11},{10,... | collective-permute-start | bytes 393224 | tf_op jit(solution)/shard_map/ppermute | solution.py:28
  66.3 3.5 %collective-permute-done.23 = bf16[32,2048]{1,0:T(8,128)(2,1)S(1)} collective-permute-done((bf16[32,2048]{1,0:T(8,128)(2,1)S(1)}, bf16[32,2048]{1,0:T(8,128)(2,1)S(1)}, u32[]{:S(2)}, u32[]{:S(2)}) %collective-permute-start.23) | collective-permute-done | bytes 131104 | tf_op jit(solution)/shard_map/ppermute | solution.py:28
  69.8 1.7 %collective-permute-start.24 = (bf16[16,2048]{1,0:T(8,128)(2,1)S(1)}, bf16[16,2048]{1,0:T(8,128)(2,1)S(1)}, u32[]{:S(2)}, u32[]{:S(2)}) collective-permute-start(bf16[16,2048]{1,0:T(8,128)(2,1)S(1)} %get-tuple-element.26), channel_id=1, source_target_pairs={{0,12},{4,8},{8,4},{12,0},{1,13},{5,9},{9,5},{13,1},{2,14},{6,10},... | collective-permute-start | bytes 196616 | tf_op jit(solution)/shard_map/ppermute | solution.py:28
  71.5 1.8 %collective-permute-start.25 = (bf16[16,2048]{1,0:T(8,128)(2,1)S(1)}, bf16[16,2048]{1,0:T(8,128)(2,1)S(1)}, u32[]{:S(2)}, u32[]{:S(2)}) collective-permute-start(bf16[16,2048]{1,0:T(8,128)(2,1)S(1)} %get-tuple-element.27), channel_id=1, source_target_pairs={{0,8},{4,12},{8,0},{12,4},{1,9},{5,13},{9,1},{13,5},{2,10},{6,14},... | collective-permute-start | bytes 196616 | tf_op jit(solution)/shard_map/ppermute | solution.py:28
  73.3 1.1 %collective-permute-start.26 = (bf16[16,2048]{1,0:T(8,128)(2,1)S(1)}, bf16[16,2048]{1,0:T(8,128)(2,1)S(1)}, u32[]{:S(2)}, u32[]{:S(2)}) collective-permute-start(bf16[16,2048]{1,0:T(8,128)(2,1)S(1)} %slice.103), channel_id=1, source_target_pairs={{0,4},{4,0},{8,12},{12,8},{1,5},{5,1},{9,13},{13,9},{2,6},{6,2},{1... | collective-permute-start | bytes 196616 | tf_op jit(solution)/shard_map/ppermute | solution.py:28
  74.4 1.7 %collective-permute-done.24 = bf16[16,2048]{1,0:T(8,128)(2,1)S(1)} collective-permute-done((bf16[16,2048]{1,0:T(8,128)(2,1)S(1)}, bf16[16,2048]{1,0:T(8,128)(2,1)S(1)}, u32[]{:S(2)}, u32[]{:S(2)}) %collective-permute-start.24) | collective-permute-done | bytes 65568 | tf_op jit(solution)/shard_map/ppermute | solution.py:28
  76.0 2.7 %collective-permute-done.25 = bf16[16,2048]{1,0:T(8,128)(2,1)S(1)} collective-permute-done((bf16[16,2048]{1,0:T(8,128)(2,1)S(1)}, bf16[16,2048]{1,0:T(8,128)(2,1)S(1)}, u32[]{:S(2)}, u32[]{:S(2)}) %collective-permute-start.25) | collective-permute-done | bytes 65568 | tf_op jit(solution)/shard_map/ppermute | solution.py:28
  78.8 0.7 fusion.12
  (66 shorter events, 6.1 us)
Async XLA Ops:
  0.6 50.9 %copy-start = (bf16[1,2048,2,384]{3,2,1,0:T(2,128)(2,1)S(1)}, bf16[1,2048,2,384]{3,2,1,0:T(2,128)(2,1)}, u32[]{:S(2)}) copy-start(bf16[1,2048,2,384]{3,2,1,0:T(2,128)(2,1)} %param.18) | copy-start | bytes 9437188
  1.8 9.9 %collective-permute-start = (bf16[576,128]{1,0:T(8,128)(2,1)S(1)}, bf16[576,128]{1,0:T(8,128)(2,1)}, u32[]{:S(2)}, u32[]{:S(2)}) collective-permute-start(bf16[576,128]{1,0:T(8,128)(2,1)S(1)} %get-tuple-element.25.refs_0_), channel_id=1, source_target_pairs={{0,4},{4,8},{8,12},{12,0},{1,5},{5,9},{9,13},{13,1},{2,6},{6,10},{... | collective-permute-start | bytes 442376 | tf_op jit(solution)/shard_map/ppermute | solution.py:33
  4.9 10.2 %collective-permute-start.2 = (bf16[576,128]{1,0:T(8,128)(2,1)S(1)}, bf16[576,128]{1,0:T(8,128)(2,1)}, u32[]{:S(2)}, u32[]{:S(2)}) collective-permute-start(bf16[576,128]{1,0:T(8,128)(2,1)S(1)} %get-tuple-element.24.refs_1_), channel_id=1, source_target_pairs={{0,12},{4,0},{8,4},{12,8},{1,13},{5,1},{9,5},{13,9},{2,14},{6,2},{... | collective-permute-start | bytes 442376 | tf_op jit(solution)/shard_map/ppermute | solution.py:33
  7.0 11.5 %collective-permute-start.4 = (bf16[576,128]{1,0:T(8,128)(2,1)S(1)}, bf16[576,128]{1,0:T(8,128)(2,1)}, u32[]{:S(2)}, u32[]{:S(2)}) collective-permute-start(bf16[576,128]{1,0:T(8,128)(2,1)S(1)} %get-tuple-element.24.refs_1_), channel_id=1, source_target_pairs={{0,4},{4,8},{8,12},{12,0},{1,5},{5,9},{9,13},{13,1},{2,6},{6,10},{... | collective-permute-start | bytes 442376 | tf_op jit(solution)/shard_map/ppermute | solution.py:33
  7.0 14.4 %collective-permute-start.5 = (bf16[576,128]{1,0:T(8,128)(2,1)S(1)}, bf16[576,128]{1,0:T(8,128)(2,1)}, u32[]{:S(2)}, u32[]{:S(2)}) collective-permute-start(bf16[576,128]{1,0:T(8,128)(2,1)S(1)} %get-tuple-element.25.refs_0_), channel_id=1, source_target_pairs={{0,12},{4,0},{8,4},{12,8},{1,13},{5,1},{9,5},{13,9},{2,14},{6,2},{... | collective-permute-start | bytes 442376 | tf_op jit(solution)/shard_map/ppermute | solution.py:33
  11.8 19.6 %collective-permute-start.1 = (bf16[576,128]{1,0:T(8,128)(2,1)}, bf16[576,128]{1,0:T(8,128)(2,1)}, u32[]{:S(2)}, u32[]{:S(2)}) collective-permute-start(bf16[576,128]{1,0:T(8,128)(2,1)} %collective-permute-done.refs_2_), channel_id=1, source_target_pairs={{0,4},{4,8},{8,12},{12,0},{1,5},{5,9},{9,13},{13,1},{2,6},{6,10},{... | collective-permute-start | bytes 442376 | tf_op jit(solution)/shard_map/ppermute | solution.py:33
  15.1 16.3 %collective-permute-start.3 = (bf16[576,128]{1,0:T(8,128)(2,1)}, bf16[576,128]{1,0:T(8,128)(2,1)}, u32[]{:S(2)}, u32[]{:S(2)}) collective-permute-start(bf16[576,128]{1,0:T(8,128)(2,1)} %collective-permute-done.2.refs_5_), channel_id=1, source_target_pairs={{0,12},{4,0},{8,4},{12,8},{1,13},{5,1},{9,5},{13,9},{2,14},{6,2},{... | collective-permute-start | bytes 442376 | tf_op jit(solution)/shard_map/ppermute | solution.py:33
  21.4 1.4 %copy-start.1 = (bf16[1,384,2048]{2,1,0:T(8,128)(2,1)S(1)}, bf16[1,384,2048]{2,1,0:T(8,128)(2,1)}, u32[]{:S(2)}) copy-start(bf16[1,384,2048]{2,1,0:T(8,128)(2,1)} %down.15) | copy-start | bytes 4718596
  22.8 2.2 %copy-start.3 = (bf16[1024,2048]{1,0:T(8,128)(2,1)S(1)}, bf16[1024,2048]{1,0:T(8,128)(2,1)}, u32[]{:S(2)}) copy-start(bf16[1024,2048]{1,0:T(8,128)(2,1)} %weight.1) | copy-start | bytes 12582916
  25.0 0.9 %copy-start.5 = (bf16[1,64,1024]{2,1,0:T(8,128)(2,1)S(1)}, bf16[1,64,1024]{2,1,0:T(8,128)(2,1)}, u32[]{:S(2)}) copy-start(bf16[1,64,1024]{2,1,0:T(8,128)(2,1)} %param.10) | copy-start | bytes 393220
  25.9 0.8 %copy-start.6 = (bf16[1,16,2048]{2,1,0:T(8,128)(2,1)S(1)}, bf16[1,16,2048]{2,1,0:T(8,128)(2,1)}, u32[]{:S(2)}) copy-start(bf16[1,16,2048]{2,1,0:T(8,128)(2,1)} %refs_7_.1) | copy-start | bytes 196612
  26.7 0.7 copy-start.8
  27.4 0.7 copy-start.11
  28.1 3.4 %copy-start.4 = (bf16[1024,2048]{1,0:T(8,128)(2,1)S(1)}, bf16[1024,2048]{1,0:T(8,128)(2,1)}, u32[]{:S(2)}) copy-start(bf16[1024,2048]{1,0:T(8,128)(2,1)} %weight.1) | copy-start | bytes 12582916
  31.4 9.4 %copy-start.7 = (bf16[1,16,2048]{2,1,0:T(8,128)(2,1)S(1)}, bf16[1,16,2048]{2,1,0:T(8,128)(2,1)}, u32[]{:S(2)}) copy-start(bf16[1,16,2048]{2,1,0:T(8,128)(2,1)} %refs_7_.1) | copy-start | bytes 196612
  31.4 9.4 %copy-start.9 = (f32[2048]{0:T(1024)S(1)}, f32[2048]{0:T(1024)}, u32[]{:S(2)}) copy-start(f32[2048]{0:T(1024)} %refs_8_.1) | copy-start | bytes 24580
  34.7 4.0 %collective-permute-start.6 = (bf16[16,2048]{1,0:T(8,128)(2,1)}, bf16[16,2048]{1,0:T(8,128)(2,1)S(1)}, u32[]{:S(2)}, u32[]{:S(2)}) collective-permute-start(bf16[16,2048]{1,0:T(8,128)(2,1)} %get-tuple-element.19), channel_id=1, source_target_pairs={{0,1},{1,0},{2,3},{3,2},{4,5},{5,4},{6,7},{7,6},{8,9},{9,8},{10,11... | collective-permute-start | bytes 196616 | tf_op jit(solution)/shard_map/ppermute | solution.py:28
  34.7 4.7 %collective-permute-start.7 = (bf16[16,2048]{1,0:T(8,128)(2,1)}, bf16[16,2048]{1,0:T(8,128)(2,1)S(1)}, u32[]{:S(2)}, u32[]{:S(2)}) collective-permute-start(bf16[16,2048]{1,0:T(8,128)(2,1)} %get-tuple-element.20), channel_id=1, source_target_pairs={{0,2},{1,3},{2,0},{3,1},{4,6},{5,7},{6,4},{7,5},{8,10},{9,11},{10,... | collective-permute-start | bytes 196616 | tf_op jit(solution)/shard_map/ppermute | solution.py:28
  36.5 4.3 %collective-permute-start.8 = (bf16[16,2048]{1,0:T(8,128)(2,1)}, bf16[16,2048]{1,0:T(8,128)(2,1)S(1)}, u32[]{:S(2)}, u32[]{:S(2)}) collective-permute-start(bf16[16,2048]{1,0:T(8,128)(2,1)} %get-tuple-element.21), channel_id=1, source_target_pairs={{0,3},{1,2},{2,1},{3,0},{4,7},{5,6},{6,5},{7,4},{8,11},{9,10},{10,... | collective-permute-start | bytes 196616 | tf_op jit(solution)/shard_map/ppermute | solution.py:28
  40.8 0.7 copy-start.10
  41.7 8.2 %collective-permute-start.16 = (bf16[16,2176]{1,0:T(8,128)(2,1)S(1)}, bf16[16,2176]{1,0:T(8,128)(2,1)S(1)}, u32[]{:S(2)}, u32[]{:S(2)}) collective-permute-start(bf16[16,2176]{1,0:T(8,128)(2,1)S(1)} %get-tuple-element.23), channel_id=1, source_target_pairs={{0,8},{4,12},{8,0},{12,4},{1,9},{5,13},{9,1},{13,5},{2,10},{6,14},... | collective-permute-start | bytes 208904 | tf_op jit(solution)/shard_map/ppermute | solution.py:28
  42.4 7.5 %collective-permute-start.17 = (bf16[16,2176]{1,0:T(8,128)(2,1)S(1)}, bf16[16,2176]{1,0:T(8,128)(2,1)S(1)}, u32[]{:S(2)}, u32[]{:S(2)}) collective-permute-start(bf16[16,2176]{1,0:T(8,128)(2,1)S(1)} %get-tuple-element.23), channel_id=1, source_target_pairs={{0,12},{4,8},{8,4},{12,0},{1,13},{5,9},{9,5},{13,1},{2,14},{6,10},... | collective-permute-start | bytes 208904 | tf_op jit(solution)/shard_map/ppermute | solution.py:28
  44.6 7.6 %collective-permute-start.9 = (bf16[16,2176]{1,0:T(8,128)(2,1)S(1)}, bf16[16,2176]{1,0:T(8,128)(2,1)S(1)}, u32[]{:S(2)}, u32[]{:S(2)}) collective-permute-start(bf16[16,2176]{1,0:T(8,128)(2,1)S(1)} %get-tuple-element.23), channel_id=1, source_target_pairs={{0,4},{4,0},{8,12},{12,8},{1,5},{5,1},{9,13},{13,9},{2,6},{6,2},{1... | collective-permute-start | bytes 208904 | tf_op jit(solution)/shard_map/ppermute | solution.py:28
  49.9 4.5 %collective-permute-start.18 = (bf16[32,2176]{1,0:T(8,128)(2,1)S(1)}, bf16[32,2176]{1,0:T(8,128)(2,1)S(1)}, u32[]{:S(2)}, u32[]{:S(2)}) collective-permute-start(bf16[32,2176]{1,0:T(8,128)(2,1)S(1)} %constant_dynamic-update-slice_fusion.2.rows), channel_id=1, source_target_pairs={{0,1},{1,0},{2,3},{3,2},{4,5},{5,4},{6,7},{7,6},{8,9},{9,8},{10,11... | collective-permute-start | bytes 417800 | tf_op jit(solution)/shard_map/ppermute | solution.py:28
  50.0 7.2 %collective-permute-start.20 = (bf16[32,2176]{1,0:T(8,128)(2,1)S(1)}, bf16[32,2176]{1,0:T(8,128)(2,1)S(1)}, u32[]{:S(2)}, u32[]{:S(2)}) collective-permute-start(bf16[32,2176]{1,0:T(8,128)(2,1)S(1)} %constant_dynamic-update-slice_fusion.2.rows), channel_id=1, source_target_pairs={{0,2},{1,3},{2,0},{3,1},{4,6},{5,7},{6,4},{7,5},{8,10},{9,11},{10,... | collective-permute-start | bytes 417800 | tf_op jit(solution)/shard_map/ppermute | solution.py:28
  51.6 2.1 %copy-start.2 = (bf16[1,384,2048]{2,1,0:T(8,128)(2,1)S(1)}, bf16[1,384,2048]{2,1,0:T(8,128)(2,1)}, u32[]{:S(2)}) copy-start(bf16[1,384,2048]{2,1,0:T(8,128)(2,1)} %down.15) | copy-start | bytes 4718596
  52.2 3.4 %collective-permute-start.10 = (bf16[32,2176]{1,0:T(8,128)(2,1)S(1)}, bf16[32,2176]{1,0:T(8,128)(2,1)S(1)}, u32[]{:S(2)}, u32[]{:S(2)}) collective-permute-start(bf16[32,2176]{1,0:T(8,128)(2,1)S(1)} %constant_dynamic-update-slice_fusion.rows), channel_id=1, source_target_pairs={{0,1},{1,0},{2,3},{3,2},{4,5},{5,4},{6,7},{7,6},{8,9},{9,8},{10,11... | collective-permute-start | bytes 417800 | tf_op jit(solution)/shard_map/ppermute | solution.py:28
  53.1 6.0 %collective-permute-start.12 = (bf16[32,2176]{1,0:T(8,128)(2,1)S(1)}, bf16[32,2176]{1,0:T(8,128)(2,1)S(1)}, u32[]{:S(2)}, u32[]{:S(2)}) collective-permute-start(bf16[32,2176]{1,0:T(8,128)(2,1)S(1)} %constant_dynamic-update-slice_fusion.rows), channel_id=1, source_target_pairs={{0,2},{1,3},{2,0},{3,1},{4,6},{5,7},{6,4},{7,5},{8,10},{9,11},{10,... | collective-permute-start | bytes 417800 | tf_op jit(solution)/shard_map/ppermute | solution.py:28
  55.5 10.7 %collective-permute-start.19 = (bf16[32,2048]{1,0:T(8,128)(2,1)S(1)}, bf16[32,2048]{1,0:T(8,128)(2,1)S(1)}, u32[]{:S(2)}, u32[]{:S(2)}) collective-permute-start(bf16[32,2048]{1,0:T(8,128)(2,1)S(1)} %shard_map.121), channel_id=1, source_target_pairs={{0,1},{1,0},{2,3},{3,2},{4,5},{5,4},{6,7},{7,6},{8,9},{9,8},{10,11... | collective-permute-start | bytes 393224 | tf_op jit(solution)/shard_map/ppermute | solution.py:28
  56.7 16.5 %collective-permute-start.11 = (bf16[32,2048]{1,0:T(8,128)(2,1)S(1)}, bf16[32,2048]{1,0:T(8,128)(2,1)S(1)}, u32[]{:S(2)}, u32[]{:S(2)}) collective-permute-start(bf16[32,2048]{1,0:T(8,128)(2,1)S(1)} %shard_map.117), channel_id=1, source_target_pairs={{0,1},{1,0},{2,3},{3,2},{4,5},{5,4},{6,7},{7,6},{8,9},{9,8},{10,11... | collective-permute-start | bytes 393224 | tf_op jit(solution)/shard_map/ppermute | solution.py:28
  57.2 3.3 %collective-permute-start.21 = (bf16[32,2176]{1,0:T(8,128)(2,1)S(1)}, bf16[32,2176]{1,0:T(8,128)(2,1)S(1)}, u32[]{:S(2)}, u32[]{:S(2)}) collective-permute-start(bf16[32,2176]{1,0:T(8,128)(2,1)S(1)} %collective-permute-done.20.rows), channel_id=1, source_target_pairs={{0,1},{1,0},{2,3},{3,2},{4,5},{5,4},{6,7},{7,6},{8,9},{9,8},{10,11... | collective-permute-start | bytes 417800 | tf_op jit(solution)/shard_map/ppermute | solution.py:28
  59.1 3.1 %collective-permute-start.13 = (bf16[32,2176]{1,0:T(8,128)(2,1)S(1)}, bf16[32,2176]{1,0:T(8,128)(2,1)S(1)}, u32[]{:S(2)}, u32[]{:S(2)}) collective-permute-start(bf16[32,2176]{1,0:T(8,128)(2,1)S(1)} %collective-permute-done.12.rows), channel_id=1, source_target_pairs={{0,1},{1,0},{2,3},{3,2},{4,5},{5,4},{6,7},{7,6},{8,9},{9,8},{10,11... | collective-permute-start | bytes 417800 | tf_op jit(solution)/shard_map/ppermute | solution.py:28
  61.6 1.7 %collective-permute-start.22 = (bf16[32,2048]{1,0:T(8,128)(2,1)S(1)}, bf16[32,2048]{1,0:T(8,128)(2,1)S(1)}, u32[]{:S(2)}, u32[]{:S(2)}) collective-permute-start(bf16[32,2048]{1,0:T(8,128)(2,1)S(1)} %shard_map.123), channel_id=1, source_target_pairs={{0,1},{1,0},{2,3},{3,2},{4,5},{5,4},{6,7},{7,6},{8,9},{9,8},{10,11... | collective-permute-start | bytes 393224 | tf_op jit(solution)/shard_map/ppermute | solution.py:28
  63.2 1.7 %collective-permute-start.14 = (bf16[32,2048]{1,0:T(8,128)(2,1)S(1)}, bf16[32,2048]{1,0:T(8,128)(2,1)S(1)}, u32[]{:S(2)}, u32[]{:S(2)}) collective-permute-start(bf16[32,2048]{1,0:T(8,128)(2,1)S(1)} %shard_map.119), channel_id=1, source_target_pairs={{0,1},{1,0},{2,3},{3,2},{4,5},{5,4},{6,7},{7,6},{8,9},{9,8},{10,11... | collective-permute-start | bytes 393224 | tf_op jit(solution)/shard_map/ppermute | solution.py:28
  63.4 6.4 %collective-permute-start.23 = (bf16[32,2048]{1,0:T(8,128)(2,1)S(1)}, bf16[32,2048]{1,0:T(8,128)(2,1)S(1)}, u32[]{:S(2)}, u32[]{:S(2)}) collective-permute-start(bf16[32,2048]{1,0:T(8,128)(2,1)S(1)} %add_convert_fusion.1), channel_id=1, source_target_pairs={{0,2},{1,3},{2,0},{3,1},{4,6},{5,7},{6,4},{7,5},{8,10},{9,11},{10,... | collective-permute-start | bytes 393224 | tf_op jit(solution)/shard_map/ppermute | solution.py:28
  65.0 8.3 %collective-permute-start.15 = (bf16[32,2048]{1,0:T(8,128)(2,1)S(1)}, bf16[32,2048]{1,0:T(8,128)(2,1)S(1)}, u32[]{:S(2)}, u32[]{:S(2)}) collective-permute-start(bf16[32,2048]{1,0:T(8,128)(2,1)S(1)} %add_convert_fusion.2), channel_id=1, source_target_pairs={{0,2},{1,3},{2,0},{3,1},{4,6},{5,7},{6,4},{7,5},{8,10},{9,11},{10,... | collective-permute-start | bytes 393224 | tf_op jit(solution)/shard_map/ppermute | solution.py:28
  69.8 6.3 %collective-permute-start.24 = (bf16[16,2048]{1,0:T(8,128)(2,1)S(1)}, bf16[16,2048]{1,0:T(8,128)(2,1)S(1)}, u32[]{:S(2)}, u32[]{:S(2)}) collective-permute-start(bf16[16,2048]{1,0:T(8,128)(2,1)S(1)} %get-tuple-element.26), channel_id=1, source_target_pairs={{0,12},{4,8},{8,4},{12,0},{1,13},{5,9},{9,5},{13,1},{2,14},{6,10},... | collective-permute-start | bytes 196616 | tf_op jit(solution)/shard_map/ppermute | solution.py:28
  71.5 7.2 %collective-permute-start.25 = (bf16[16,2048]{1,0:T(8,128)(2,1)S(1)}, bf16[16,2048]{1,0:T(8,128)(2,1)S(1)}, u32[]{:S(2)}, u32[]{:S(2)}) collective-permute-start(bf16[16,2048]{1,0:T(8,128)(2,1)S(1)} %get-tuple-element.27), channel_id=1, source_target_pairs={{0,8},{4,12},{8,0},{12,4},{1,9},{5,13},{9,1},{13,5},{2,10},{6,14},... | collective-permute-start | bytes 196616 | tf_op jit(solution)/shard_map/ppermute | solution.py:28
  73.3 5.4 %collective-permute-start.26 = (bf16[16,2048]{1,0:T(8,128)(2,1)S(1)}, bf16[16,2048]{1,0:T(8,128)(2,1)S(1)}, u32[]{:S(2)}, u32[]{:S(2)}) collective-permute-start(bf16[16,2048]{1,0:T(8,128)(2,1)S(1)} %slice.103), channel_id=1, source_target_pairs={{0,4},{4,0},{8,12},{12,8},{1,5},{5,1},{9,13},{13,9},{2,6},{6,2},{1... | collective-permute-start | bytes 196616 | tf_op jit(solution)/shard_map/ppermute | solution.py:28

commit v4 on v3

--- a/solution.py
+++ b/solution.py
@@ -38,7 +38,7 @@
 
 
 SMEM_SPEC = pl.BlockSpec(memory_space=pltpu.SMEM)
-LIMIT = pltpu.CompilerParams(vmem_limit_bytes=16 * 1024 * 1024)
+LIMIT = pltpu.CompilerParams(vmem_limit_bytes=12 * 1024 * 1024)
 
 
 def stack_heads(queries):
@@ -95,28 +95,43 @@
     return lax.rem(lax.axis_index("ctx") + offset + count, count)
 
 
-def early_kernel(offsets, last, fresh_block, lengths, queries, *refs):
+def first_kernel(fresh_block, count, lengths, queries, keys, values, *refs):
+    peak_out, total_out, summed_out, lengths_out = refs[-4:]
+    for offset in range(count):
+        lengths_out[offset : offset + 1, :] = jnp.full(
+            (1, lengths_out.shape[1]), lengths[page_at(offset)], jnp.int32
+        )
+    place = lax.axis_index("ctx")
+    peak_out[...], total_out[...], summed_out[...] = page_partial(
+        stack_heads(queries[...]),
+        keys[...],
+        values[...],
+        place,
+        lengths[place],
+        place,
+        fresh_block,
+    )
+
+
+def middle_kernel(offsets, fresh_block, queries, lengths, *refs):
     count = len(offsets)
-    pages, (peak_out, total_out, summed_out, length_out) = refs[: 2 * count], refs[-4:]
-    length_out[...] = jnp.full(length_out.shape, lengths[page_at(last)], jnp.int32)
+    pages, (peak, total, summed) = refs[: 2 * count], refs[2 * count : 2 * count + 3]
+    outs = refs[2 * count + 3 :]
     stacked = stack_heads(queries[...])
-    place = lax.axis_index("ctx")
-    state = None
+    state = (peak[...], total[...], summed[...])
     for number, offset in enumerate(offsets):
-        page = page_at(offset)
         part = page_partial(
             stacked,
             pages[2 * number][...],
             pages[2 * number + 1][...],
-            page,
-            lengths[page],
-            place,
+            page_at(offset),
+            lengths[offset : offset + 1, :],
+            lax.axis_index("ctx"),
             fresh_block,
         )
-        state = part if state is None else merge(state, part)
-    peak_out[...] = state[0]
-    total_out[...] = state[1]
-    summed_out[...] = state[2]
+        state = merge(state, part)
+    for out, value in zip(outs, state):
+        out[...] = value
 
 
 def late_kernel(
@@ -125,10 +140,10 @@
     queries,
     keys,
     values,
+    lengths,
     peak,
     total,
     summed,
-    length,
     weight,
     context_out,
     own_out,
@@ -141,7 +156,7 @@
         keys[...],
         values[...],
         page,
-        length[...],
+        lengths[offset : offset + 1, :],
         lax.axis_index("ctx"),
         fresh_block,
     )
@@ -171,7 +186,7 @@
     exp_count = lax.axis_size("exp")
     model_width = out_weight.shape[1]
     own_keys, own_values = pages[:, 0], pages[:, 1]
-    held = [(0, own_keys, own_values)]
+    held = []
     left_keys, left_values = own_keys, own_values
     right_keys, right_values = own_keys, own_values
     for step in range(1, (count - 1) // 2 + 1):
@@ -179,7 +194,7 @@
         right_values = shift(right_values, "ctx", -1)
         left_values = shift(left_values, "ctx", 1)
         right_keys = shift(right_keys, "ctx", -1)
-        held.append((-step, left_keys, left_values))
+        held.append((count - step, left_keys, left_values))
         held.append((step, right_keys, right_values))
     if count % 2 == 0:
         last = (count // 2, shift(left_keys, "ctx", 1), shift(right_values, "ctx", -1))
@@ -187,32 +202,32 @@
         last = held.pop()
     page_flops = 4 * rows * pages.shape[0] * HEAD
     line = jax.ShapeDtypeStruct((1, rows), jnp.float32)
-    state = None
-    for start in range(0, len(held), 3):
-        group = held[start : start + 3]
+    partial_shape = (line, line, jax.ShapeDtypeStruct((HEAD, rows), jnp.float32))
+    *state, page_lengths = pl.pallas_call(
+        functools.partial(first_kernel, fresh_block, count),
+        out_shape=partial_shape + (jax.ShapeDtypeStruct((count, HEAD), jnp.int32),),
+        in_specs=[SMEM_SPEC]
+        + whole_specs(3)
+        + [pl.BlockSpec(memory_space=pl.ANY)] * (1 + len(later)),
+        out_specs=tuple(whole_specs(4)),
+        compiler_params=LIMIT,
+        cost_estimate=pl.CostEstimate(
+            flops=16 * page_flops, bytes_accessed=8 << 20, transcendentals=0
+        ),
+    )(lengths, queries, own_keys, own_values, out_weight, *later)
+    for start in range(0, len(held), 2):
+        group = held[start : start + 2]
         operands = [part for _, keys, values in group for part in (keys, values)]
-        held_operands = () if start else (out_weight, *later)
-        partial_state = pl.pallas_call(
-            functools.partial(
-                early_kernel, [offset for offset, _, _ in group], last[0], fresh_block
-            ),
-            out_shape=(
-                line,
-                line,
-                jax.ShapeDtypeStruct((HEAD, rows), jnp.float32),
-                jax.ShapeDtypeStruct((1, HEAD), jnp.int32),
-            ),
-            in_specs=[SMEM_SPEC]
-            + whole_specs(1 + len(operands))
-            + [pl.BlockSpec(memory_space=pl.ANY)] * len(held_operands),
-            out_specs=tuple(whole_specs(4)),
+        state = pl.pallas_call(
+            functools.partial(middle_kernel, [offset for offset, _, _ in group], fresh_block),
+            out_shape=partial_shape,
+            in_specs=whole_specs(5 + len(operands)),
+            out_specs=tuple(whole_specs(3)),
             compiler_params=LIMIT,
             cost_estimate=pl.CostEstimate(
                 flops=len(group) * page_flops, bytes_accessed=2 << 20, transcendentals=0
             ),
-        )(lengths, queries, *operands, *held_operands)
-        partial_state, length = partial_state[:3], partial_state[3]
-        state = partial_state if state is None else merge(state, partial_state)
+        )(queries, page_lengths, *operands, *state)
     block = jax.ShapeDtypeStruct((token_block, model_width), jnp.bfloat16)
     outs = pl.pallas_call(
         functools.partial(late_kernel, last[0], fresh_block),
@@ -230,7 +245,7 @@
             bytes_accessed=6 << 20,
             transcendentals=0,
         ),
-    )(queries, last[1], last[2], *state, length, out_weight)
+    )(queries, last[1], last[2], page_lengths, *state, out_weight)
     return outs[0], outs[1], outs[2:]
 
 
@@ -243,7 +258,8 @@
     hidden_out[...] = hidden
     width = hidden.shape[1]
     sent_out[:, :width] = normalize(hidden, gain[...])
-    chosen = scores[...]
+    chosen = jnp.transpose(scores[...])
+    ids = jnp.transpose(ids[...])
     combine = (chosen / jnp.sum(chosen, axis=1, keepdims=True)).astype(jnp.bfloat16)
     combine = combine.astype(jnp.float32)
     tokens, choices = chosen.shape
@@ -325,10 +341,10 @@
     far, near = exp_strides[:1], exp_strides[1:]
 
     blocks = {0: rows}
-    for offset in reversed(range(1, ctx_count)):
+    for offset in range(1, ctx_count):
         blocks[offset] = swap(rows, "ctx", offset)
     half = ctx_count // 2
-    chunks = [list(range(half, ctx_count)), list(range(half))] if half else [[0]]
+    chunks = [list(range(half)), list(range(half, ctx_count))] if half else [[0]]
     sent = [jnp.concatenate([blocks[offset] for offset in chunk], axis=0) for chunk in chunks]
 
     def results(pieces):
@@ -337,7 +353,11 @@
         values = [expert_apply(piece, gate_up, down, kind) for piece, kind in zip(pieces, kinds)]
         return return_near(values, near)
 
-    crossed = [[swap(piece, "exp", stride) for stride in far] for piece in sent]
+    crossed = []
+    for number, piece in enumerate(sent):
+        if crossed:
+            piece, crossed[-1] = lax.optimization_barrier((piece, crossed[-1]))
+        crossed.append([swap(piece, "exp", stride) for stride in far])
     totals = {}
     for chunk, home, away in zip(chunks, sent, crossed):
         value = results(gather_near(home, near))
@@ -380,7 +400,7 @@
             cached_lengths[r],
             out_weight,
             token_block,
-            (residual_in, norm_gain, expert_output, expert_ids, route_scores),
+            (expert_output,),
         )
         contexts.append(context)
         owns.append(own)
@@ -406,8 +426,8 @@
         parts,
         residual.reshape(-1, model_width),
         norm_gain,
-        ids.reshape(-1, ids.shape[2]),
-        scores.reshape(-1, ids.shape[2]),
+        ids.reshape(-1, ids.shape[2]).T,
+        scores.reshape(-1, ids.shape[2]).T,
         expert_count,
     )
     own_hidden = own_hidden.reshape(requests, -1, model_width)

time: 79.9 us -> 74.2 us (0.929)
  local copies, waits for them, and re-layouts: 12.3 us -> 6.52 us
  starting transfers between devices: 29.3 us -> 31 us
  Pallas kernels: 9.99 us -> 8.32 us
    unnamed x29 -> x27, local copies, waits for them, and re-layouts: 10.1 us -> 6.46 us
    reshape x2 -> x0, local copies, waits for them, and re-layouts: 2.11 us -> none  [the longest x1 1.35 us: per_device(): scores.reshape(-1, ids.shape[2])]
    ppermute x21, waiting for transfers between devices: 15.7 us -> 17.7 us  [swap(): lax.ppermute(value, axis, [(i, i ^ stride) for i in range(lax.axis_size(a...]
    ppermute x6, waiting for transfers between devices: 5.35 us -> 3.41 us  [shift(): lax.ppermute(value, axis, [(i, (i + step) % count) for i in range(count)])]
    ppermute x21, starting transfers between devices: 16.6 us -> 18.3 us  [swap(): lax.ppermute(value, axis, [(i, i ^ stride) for i in range(lax.axis_size(a...]
    pallas_call x1, Pallas kernels: 3.3 us -> 2.16 us  [attention(): pl.pallas_call(functools.partial(late_kernel, last[0], fresh_block), out_...]
    pallas_call x1 -> x2, Pallas kernels: 3.32 us -> 2.74 us  [the longest x1 1.43 us: attention(): pl.pallas_call(functools.partial(middle_kernel, [offset for offset, _, _...]
  transfers between devices with their start and end apart: 27 -> 27, of which waited for: 10 -> 10; matrix products, arithmetic and copies ran while one was open for 11% -> 7% of each run, Pallas kernels for 8% -> 8%
where the time goes in v4:
time: 74.2 us; the launch traced here: 74 us
  starting transfers between devices  31 us (42%)
  waiting for transfers between devices  21.1 us (28%)
  Pallas kernels  8.32 us (11%)
  local copies, waits for them, and re-layouts  6.52 us (9%)
  matrix products  5.18 us (7%)
  between operations  0.95 us (1%)
  other arithmetic  0.81 us (1%)
    ppermute x21, starting transfers between devices, swap(): lax.ppermute(value, axis, [(i, i ^ stride) for i in range(lax.axis_size(a...  18.3 us
    ppermute x21, waiting for transfers between devices, swap(): lax.ppermute(value, axis, [(i, i ^ stride) for i in range(lax.axis_size(a...  17.7 us
    ppermute x6, starting transfers between devices, shift(): lax.ppermute(value, axis, [(i, (i + step) % count) for i in range(count)])  12.8 us
    unnamed x27, local copies, waits for them, and re-layouts  6.46 us
    dot_general x8, matrix products, expert_apply(): jnp.einsum('nd,dgh->gnh', rows[:, :width], gate_up[0], preferred_element_...  5.18 us
    ppermute x6, waiting for transfers between devices, shift(): lax.ppermute(value, axis, [(i, (i + step) % count) for i in range(count)])  3.41 us
    pallas_call x8, Pallas kernels, expert_apply(): pl.pallas_call(down_kernel, out_shape=jax.ShapeDtypeStruct((rows.shape[0]...  3.17 us
    pallas_call x1, Pallas kernels, attention(): pl.pallas_call(functools.partial(late_kernel, last[0], fresh_block), out_...  2.16 us
  transfers between devices with their start and end apart: 27, of which 10 were waited for; matrix products, arithmetic and copies ran while one was open for 7% of the time, Pallas kernels for 8%

profile of v4, /device:TPU:0, one launch (start us, length us, event | category | flops | bytes accessed | tf_op | source)
XLA Modules:
  0.0 74.0 jit_solution(5305890160005771986)
XLA Ops:
  0.6 1.2 %copy.38 = bf16[1,576,2,128]{3,1,2,0:T(8,128)(2,1)S(1)} copy(bf16[1,576,2,128]{3,2,1,0:T(2,128)(2,1)} %param.11) | data formatting | bytes 589824 | tf_op args[1]
  1.8 3.1 %collective-permute-start = (bf16[576,128]{1,0:T(8,128)(2,1)S(1)}, bf16[576,128]{1,0:T(8,128)(2,1)S(1)}, u32[]{:S(2)}, u32[]{:S(2)}) collective-permute-start(bf16[576,128]{1,0:T(8,128)(2,1)S(1)} %get-tuple-element.35.keys), channel_id=1, source_target_pairs={{0,4},{4,8},{8,12},{12,0},{1,5},{5,9},{9,13},{13,1},{2,6},{6,10},{... | collective-permute-start | bytes 442376 | tf_op jit(solution)/shard_map/ppermute | solution.py:33
  4.9 2.1 %collective-permute-start.2 = (bf16[576,128]{1,0:T(8,128)(2,1)S(1)}, bf16[576,128]{1,0:T(8,128)(2,1)S(1)}, u32[]{:S(2)}, u32[]{:S(2)}) collective-permute-start(bf16[576,128]{1,0:T(8,128)(2,1)S(1)} %get-tuple-element.34.values), channel_id=1, source_target_pairs={{0,12},{4,0},{8,4},{12,8},{1,13},{5,1},{9,5},{13,9},{2,14},{6,2},{... | collective-permute-start | bytes 442376 | tf_op jit(solution)/shard_map/ppermute | solution.py:33
  7.0 3.8 %collective-permute-start.5 = (bf16[576,128]{1,0:T(8,128)(2,1)S(1)}, bf16[576,128]{1,0:T(8,128)(2,1)S(1)}, u32[]{:S(2)}, u32[]{:S(2)}) collective-permute-start(bf16[576,128]{1,0:T(8,128)(2,1)S(1)} %get-tuple-element.35.keys), channel_id=1, source_target_pairs={{0,12},{4,0},{8,4},{12,8},{1,13},{5,1},{9,5},{13,9},{2,14},{6,2},{... | collective-permute-start | bytes 442376 | tf_op jit(solution)/shard_map/ppermute | solution.py:33
  10.8 0.8 %collective-permute-done.refs_0_ = bf16[576,128]{1,0:T(8,128)(2,1)S(1)} collective-permute-done((bf16[576,128]{1,0:T(8,128)(2,1)S(1)}, bf16[576,128]{1,0:T(8,128)(2,1)S(1)}, u32[]{:S(2)}, u32[]{:S(2)}) %collective-permute-start) | collective-permute-done | bytes 147488 | tf_op jit(solution)/shard_map/ppermute | solution.py:33
  11.7 1.9 %collective-permute-start.1 = (bf16[576,128]{1,0:T(8,128)(2,1)S(1)}, bf16[576,128]{1,0:T(8,128)(2,1)S(1)}, u32[]{:S(2)}, u32[]{:S(2)}) collective-permute-start(bf16[576,128]{1,0:T(8,128)(2,1)S(1)} %collective-permute-done.refs_0_), channel_id=1, source_target_pairs={{0,4},{4,8},{8,12},{12,0},{1,5},{5,9},{9,13},{13,1},{2,6},{6,10},{... | collective-permute-start | bytes 442376 | tf_op jit(solution)/shard_map/ppermute | solution.py:33
  13.6 1.4 %collective-permute-done.2.refs_3_ = bf16[576,128]{1,0:T(8,128)(2,1)S(1)} collective-permute-done((bf16[576,128]{1,0:T(8,128)(2,1)S(1)}, bf16[576,128]{1,0:T(8,128)(2,1)S(1)}, u32[]{:S(2)}, u32[]{:S(2)}) %collective-permute-start.2) | collective-permute-done | bytes 147488 | tf_op jit(solution)/shard_map/ppermute | solution.py:33
  15.0 1.9 %collective-permute-start.3 = (bf16[576,128]{1,0:T(8,128)(2,1)S(1)}, bf16[576,128]{1,0:T(8,128)(2,1)S(1)}, u32[]{:S(2)}, u32[]{:S(2)}) collective-permute-start(bf16[576,128]{1,0:T(8,128)(2,1)S(1)} %collective-permute-done.2.refs_3_), channel_id=1, source_target_pairs={{0,12},{4,0},{8,4},{12,8},{1,13},{5,1},{9,5},{13,9},{2,14},{6,2},{... | collective-permute-start | bytes 442376 | tf_op jit(solution)/shard_map/ppermute | solution.py:33
  16.8 1.4 %copy-done.1 = bf16[1,384,2048]{2,1,0:T(8,128)(2,1)S(1)} copy-done((bf16[1,384,2048]{2,1,0:T(8,128)(2,1)S(1)}, bf16[1,384,2048]{2,1,0:T(8,128)(2,1)}, u32[]{:S(2)}) %copy-start.1) | copy-done | bytes 1572888
  18.2 2.2 %copy-done.3 = bf16[1024,2048]{1,0:T(8,128)(2,1)S(1)} copy-done((bf16[1024,2048]{1,0:T(8,128)(2,1)S(1)}, bf16[1024,2048]{1,0:T(8,128)(2,1)}, u32[]{:S(2)}) %copy-start.3) | copy-done | bytes 4194328
  20.4 0.9 %copy-done.5 = bf16[1,64,1024]{2,1,0:T(8,128)(2,1)S(1)} copy-done((bf16[1,64,1024]{2,1,0:T(8,128)(2,1)S(1)}, bf16[1,64,1024]{2,1,0:T(8,128)(2,1)}, u32[]{:S(2)}) %copy-start.5) | copy-done | bytes 131096
  21.3 0.7 copy-done.11
  22.0 1.3 %shard_map.113 = (f32[1,512]{1,0:T(1,128)S(1)}, f32[1,512]{1,0:T(1,128)S(1)}, f32[128,512]{1,0:T(8,128)S(1)}, s32[4,128]{1,0:T(4,128)S(1)}) custom-call(s32[4]{0:T(128)S(1)} %bitcast.76, bf16[64,1024]{1,0:T(8,128)(2,1)S(1)} %bitcast.69, bf16[576,128]{1,0:T(8,128)(2,1)S(1)} %get-tuple-element.35.keys, bf16[576,128]{1,0:T(8,128)(2,1)S(1)} %get-tuple-element.34.values, ...), custom_call_target="tpu_custom_call" | custom-call | flops 2415919104 | bytes 8388608 | tf_op jit(solution)/shard_map/pallas_call | solution.py:206
  23.4 1.4 %shard_map.114 = (f32[1,512]{1,0:T(1,128)S(1)}, f32[1,512]{1,0:T(1,128)S(1)}, f32[128,512]{1,0:T(8,128)S(1)}) custom-call(bf16[64,1024]{1,0:T(8,128)(2,1)S(1)} %bitcast.70, s32[4,128]{1,0:T(4,128)S(1)} %get-tuple-element.18.lengths, bf16[576,128]{1,0:T(8,128)(2,1)S(1)} %collective-permute-done.refs_0_, bf16[576,128]{1,0:T(8,128)(2,1)S(1)} %collective-permute-done.4.refs_1_, ...), custom_call_target="tpu_custom_call" | custom-call | flops 301989888 | bytes 2097152 | tf_op jit(solution)/shard_map/pallas_call | solution.py:221
  24.8 1.2 %collective-permute-done.3.values = bf16[576,128]{1,0:T(8,128)(2,1)S(1)} collective-permute-done((bf16[576,128]{1,0:T(8,128)(2,1)S(1)}, bf16[576,128]{1,0:T(8,128)(2,1)S(1)}, u32[]{:S(2)}, u32[]{:S(2)}) %collective-permute-start.3) | collective-permute-done | bytes 147488 | tf_op jit(solution)/shard_map/ppermute | solution.py:33
  26.0 2.2 %shard_map.115 = (bf16[64,1024]{1,0:T(8,128)(2,1)}, f32[16,2048]{1,0:T(8,128)S(1)}, bf16[16,2048]{1,0:T(8,128)(2,1)S(1)}, bf16[16,2048]{1,0:T(8,128)(2,1)S(1)}, bf16[16,2048]{1,0:T(8,128)(2,1)S(1)}) custom-call(bf16[64,1024]{1,0:T(8,128)(2,1)S(1)} %bitcast.71, bf16[576,128]{1,0:T(8,128)(2,1)S(1)} %collective-permute-done.1.keys, ...), custom_call_target="tpu_custom_call" | custom-call | flops 419430400 | bytes 6291456 | tf_op jit(solution)/shard_map/pallas_call | solution.py:232
  28.2 1.5 %collective-permute-start.7 = (bf16[16,2048]{1,0:T(8,128)(2,1)S(1)}, bf16[16,2048]{1,0:T(8,128)(2,1)S(1)}, u32[]{:S(2)}, u32[]{:S(2)}) collective-permute-start(bf16[16,2048]{1,0:T(8,128)(2,1)S(1)} %get-tuple-element.28), channel_id=1, source_target_pairs={{0,2},{1,3},{2,0},{3,1},{4,6},{5,7},{6,4},{7,5},{8,10},{9,11},{10,... | collective-permute-start | bytes 196616 | tf_op jit(solution)/shard_map/ppermute | solution.py:28
  30.0 2.7 %collective-permute-done.7.refs_2_ = bf16[16,2048]{1,0:T(8,128)(2,1)S(1)} collective-permute-done((bf16[16,2048]{1,0:T(8,128)(2,1)S(1)}, bf16[16,2048]{1,0:T(8,128)(2,1)S(1)}, u32[]{:S(2)}, u32[]{:S(2)}) %collective-permute-start.7) | collective-permute-done | bytes 65568 | tf_op jit(solution)/shard_map/ppermute | solution.py:28
  32.7 1.1 %collective-permute-done.8.refs_3_ = bf16[16,2048]{1,0:T(8,128)(2,1)S(1)} collective-permute-done((bf16[16,2048]{1,0:T(8,128)(2,1)S(1)}, bf16[16,2048]{1,0:T(8,128)(2,1)S(1)}, u32[]{:S(2)}, u32[]{:S(2)}) %collective-permute-start.8) | collective-permute-done | bytes 65568 | tf_op jit(solution)/shard_map/ppermute | solution.py:28
  34.1 1.2 %collective-permute-start.9 = (bf16[16,2176]{1,0:T(8,128)(2,1)S(1)}, bf16[16,2176]{1,0:T(8,128)(2,1)S(1)}, u32[]{:S(2)}, u32[]{:S(2)}) collective-permute-start(bf16[16,2176]{1,0:T(8,128)(2,1)S(1)} %get-tuple-element.31), channel_id=1, source_target_pairs={{0,4},{4,0},{8,12},{12,8},{1,5},{5,1},{9,13},{13,9},{2,6},{6,2},{1... | collective-permute-start | bytes 208904 | tf_op jit(solution)/shard_map/ppermute | solution.py:28
  35.3 1.8 %collective-permute-start.12 = (bf16[16,2176]{1,0:T(8,128)(2,1)S(1)}, bf16[16,2176]{1,0:T(8,128)(2,1)S(1)}, u32[]{:S(2)}, u32[]{:S(2)}) collective-permute-start(bf16[16,2176]{1,0:T(8,128)(2,1)S(1)} %get-tuple-element.31), channel_id=1, source_target_pairs={{0,8},{4,12},{8,0},{12,4},{1,9},{5,13},{9,1},{13,5},{2,10},{6,14},... | collective-permute-start | bytes 208904 | tf_op jit(solution)/shard_map/ppermute | solution.py:28
  37.0 1.5 %collective-permute-start.13 = (bf16[16,2176]{1,0:T(8,128)(2,1)S(1)}, bf16[16,2176]{1,0:T(8,128)(2,1)S(1)}, u32[]{:S(2)}, u32[]{:S(2)}) collective-permute-start(bf16[16,2176]{1,0:T(8,128)(2,1)S(1)} %get-tuple-element.31), channel_id=1, source_target_pairs={{0,12},{4,8},{8,4},{12,0},{1,13},{5,9},{9,5},{13,1},{2,14},{6,10},... | collective-permute-start | bytes 208904 | tf_op jit(solution)/shard_map/ppermute | solution.py:28
  38.6 1.5 %collective-permute-start.14 = (bf16[32,2176]{1,0:T(8,128)(2,1)S(1)}, bf16[32,2176]{1,0:T(8,128)(2,1)S(1)}, u32[]{:S(2)}, u32[]{:S(2)}) collective-permute-start(bf16[32,2176]{1,0:T(8,128)(2,1)S(1)} %constant_dynamic-update-slice_fusion.rows), channel_id=1, source_target_pairs={{0,2},{1,3},{2,0},{3,1},{4,6},{5,7},{6,4},{7,5},{8,10},{9,11},{10,... | collective-permute-start | bytes 417800 | tf_op jit(solution)/shard_map/ppermute | solution.py:28
  40.0 3.7 %collective-permute-done.12 = bf16[16,2176]{1,0:T(8,128)(2,1)S(1)} collective-permute-done((bf16[16,2176]{1,0:T(8,128)(2,1)S(1)}, bf16[16,2176]{1,0:T(8,128)(2,1)S(1)}, u32[]{:S(2)}, u32[]{:S(2)}) %collective-permute-start.12) | collective-permute-done | bytes 69664 | tf_op jit(solution)/shard_map/ppermute | solution.py:28
  43.8 0.6 convolution_bitcast_fusion.3.inner
  44.4 0.7 convolution_bitcast_fusion.7.inner
  46.0 0.6 collective-permute-start.15
  46.6 0.6 convolution_bitcast_fusion.5.inner
  47.2 1.4 %collective-permute-start.20 = (bf16[32,2176]{1,0:T(8,128)(2,1)S(1)}, bf16[32,2176]{1,0:T(8,128)(2,1)S(1)}, u32[]{:S(2)}, u32[]{:S(2)}) collective-permute-start(bf16[32,2176]{1,0:T(8,128)(2,1)S(1)} %constant_dynamic-update-slice_fusion.2.rows), channel_id=1, source_target_pairs={{0,2},{1,3},{2,0},{3,1},{4,6},{5,7},{6,4},{7,5},{8,10},{9,11},{10,... | collective-permute-start | bytes 417800 | tf_op jit(solution)/shard_map/ppermute | solution.py:28
  48.6 0.6 convolution_bitcast_fusion.2.inner
  49.2 0.4 shard_map.122
  49.7 0.6 convolution_bitcast_fusion.6.inner
  50.4 0.4 shard_map.118
  50.8 0.6 collective-permute-start.11
  51.7 0.6 convolution_bitcast_fusion.4.inner
  52.4 0.4 shard_map.120
  52.9 0.5 collective-permute-start.21
  53.4 0.6 convolution_bitcast_fusion.1.inner
  54.4 0.6 convolution_bitcast_fusion.inner
  55.9 1.1 %collective-permute-start.17 = (bf16[32,2048]{1,0:T(8,128)(2,1)S(1)}, bf16[32,2048]{1,0:T(8,128)(2,1)S(1)}, u32[]{:S(2)}, u32[]{:S(2)}) collective-permute-start(bf16[32,2048]{1,0:T(8,128)(2,1)S(1)} %add_convert_fusion.2), channel_id=1, source_target_pairs={{0,2},{1,3},{2,0},{3,1},{4,6},{5,7},{6,4},{7,5},{8,10},{9,11},{10,... | collective-permute-start | bytes 393224 | tf_op jit(solution)/shard_map/ppermute | solution.py:28
  57.0 1.1 %collective-permute-start.23 = (bf16[32,2048]{1,0:T(8,128)(2,1)S(1)}, bf16[32,2048]{1,0:T(8,128)(2,1)S(1)}, u32[]{:S(2)}, u32[]{:S(2)}) collective-permute-start(bf16[32,2048]{1,0:T(8,128)(2,1)S(1)} %add_convert_fusion.1), channel_id=1, source_target_pairs={{0,2},{1,3},{2,0},{3,1},{4,6},{5,7},{6,4},{7,5},{8,10},{9,11},{10,... | collective-permute-start | bytes 393224 | tf_op jit(solution)/shard_map/ppermute | solution.py:28
  58.1 4.2 %collective-permute-done.17 = bf16[32,2048]{1,0:T(8,128)(2,1)S(1)} collective-permute-done((bf16[32,2048]{1,0:T(8,128)(2,1)S(1)}, bf16[32,2048]{1,0:T(8,128)(2,1)S(1)}, u32[]{:S(2)}, u32[]{:S(2)}) %collective-permute-start.17) | collective-permute-done | bytes 131104 | tf_op jit(solution)/shard_map/ppermute | solution.py:28
  62.3 1.7 %collective-permute-start.26 = (bf16[16,2048]{1,0:T(8,128)(2,1)S(1)}, bf16[16,2048]{1,0:T(8,128)(2,1)S(1)}, u32[]{:S(2)}, u32[]{:S(2)}) collective-permute-start(bf16[16,2048]{1,0:T(8,128)(2,1)S(1)} %slice.104), channel_id=1, source_target_pairs={{0,4},{4,0},{8,12},{12,8},{1,5},{5,1},{9,13},{13,9},{2,6},{6,2},{1... | collective-permute-start | bytes 196616 | tf_op jit(solution)/shard_map/ppermute | solution.py:28
  64.4 2.2 %collective-permute-start.24 = (bf16[16,2048]{1,0:T(8,128)(2,1)S(1)}, bf16[16,2048]{1,0:T(8,128)(2,1)S(1)}, u32[]{:S(2)}, u32[]{:S(2)}) collective-permute-start(bf16[16,2048]{1,0:T(8,128)(2,1)S(1)} %get-tuple-element.36), channel_id=1, source_target_pairs={{0,12},{4,8},{8,4},{12,0},{1,13},{5,9},{9,5},{13,1},{2,14},{6,10},... | collective-permute-start | bytes 196616 | tf_op jit(solution)/shard_map/ppermute | solution.py:28
  66.6 0.9 %collective-permute-start.25 = (bf16[16,2048]{1,0:T(8,128)(2,1)S(1)}, bf16[16,2048]{1,0:T(8,128)(2,1)S(1)}, u32[]{:S(2)}, u32[]{:S(2)}) collective-permute-start(bf16[16,2048]{1,0:T(8,128)(2,1)S(1)} %get-tuple-element.37), channel_id=1, source_target_pairs={{0,8},{4,12},{8,0},{12,4},{1,9},{5,13},{9,1},{13,5},{2,10},{6,14},... | collective-permute-start | bytes 196616 | tf_op jit(solution)/shard_map/ppermute | solution.py:28
  67.5 3.0 %collective-permute-done.24 = bf16[16,2048]{1,0:T(8,128)(2,1)S(1)} collective-permute-done((bf16[16,2048]{1,0:T(8,128)(2,1)S(1)}, bf16[16,2048]{1,0:T(8,128)(2,1)S(1)}, u32[]{:S(2)}, u32[]{:S(2)}) %collective-permute-start.24) | collective-permute-done | bytes 65568 | tf_op jit(solution)/shard_map/ppermute | solution.py:28
  70.6 2.7 %collective-permute-done.25 = bf16[16,2048]{1,0:T(8,128)(2,1)S(1)} collective-permute-done((bf16[16,2048]{1,0:T(8,128)(2,1)S(1)}, bf16[16,2048]{1,0:T(8,128)(2,1)S(1)}, u32[]{:S(2)}, u32[]{:S(2)}) %collective-permute-start.25) | collective-permute-done | bytes 65568 | tf_op jit(solution)/shard_map/ppermute | solution.py:28
  73.3 0.7 fusion.14
  (63 shorter events, 4.0 us)
Async XLA Ops:
  0.6 43.1 %copy-start = (bf16[1,2048,2,384]{3,2,1,0:T(2,128)(2,1)S(1)}, bf16[1,2048,2,384]{3,2,1,0:T(2,128)(2,1)}, u32[]{:S(2)}) copy-start(bf16[1,2048,2,384]{3,2,1,0:T(2,128)(2,1)} %param.18) | copy-start | bytes 9437188
  1.8 9.8 %collective-permute-start = (bf16[576,128]{1,0:T(8,128)(2,1)S(1)}, bf16[576,128]{1,0:T(8,128)(2,1)S(1)}, u32[]{:S(2)}, u32[]{:S(2)}) collective-permute-start(bf16[576,128]{1,0:T(8,128)(2,1)S(1)} %get-tuple-element.35.keys), channel_id=1, source_target_pairs={{0,4},{4,8},{8,12},{12,0},{1,5},{5,9},{9,13},{13,1},{2,6},{6,10},{... | collective-permute-start | bytes 442376 | tf_op jit(solution)/shard_map/ppermute | solution.py:33
  4.9 10.1 %collective-permute-start.2 = (bf16[576,128]{1,0:T(8,128)(2,1)S(1)}, bf16[576,128]{1,0:T(8,128)(2,1)S(1)}, u32[]{:S(2)}, u32[]{:S(2)}) collective-permute-start(bf16[576,128]{1,0:T(8,128)(2,1)S(1)} %get-tuple-element.34.values), channel_id=1, source_target_pairs={{0,12},{4,0},{8,4},{12,8},{1,13},{5,1},{9,5},{13,9},{2,14},{6,2},{... | collective-permute-start | bytes 442376 | tf_op jit(solution)/shard_map/ppermute | solution.py:33
  7.0 16.4 %collective-permute-start.4 = (bf16[576,128]{1,0:T(8,128)(2,1)S(1)}, bf16[576,128]{1,0:T(8,128)(2,1)S(1)}, u32[]{:S(2)}, u32[]{:S(2)}) collective-permute-start(bf16[576,128]{1,0:T(8,128)(2,1)S(1)} %get-tuple-element.34.values), channel_id=1, source_target_pairs={{0,4},{4,8},{8,12},{12,0},{1,5},{5,9},{9,13},{13,1},{2,6},{6,10},{... | collective-permute-start | bytes 442376 | tf_op jit(solution)/shard_map/ppermute | solution.py:33
  7.0 16.4 %collective-permute-start.5 = (bf16[576,128]{1,0:T(8,128)(2,1)S(1)}, bf16[576,128]{1,0:T(8,128)(2,1)S(1)}, u32[]{:S(2)}, u32[]{:S(2)}) collective-permute-start(bf16[576,128]{1,0:T(8,128)(2,1)S(1)} %get-tuple-element.35.keys), channel_id=1, source_target_pairs={{0,12},{4,0},{8,4},{12,8},{1,13},{5,1},{9,5},{13,9},{2,14},{6,2},{... | collective-permute-start | bytes 442376 | tf_op jit(solution)/shard_map/ppermute | solution.py:33
  11.7 13.2 %collective-permute-start.1 = (bf16[576,128]{1,0:T(8,128)(2,1)S(1)}, bf16[576,128]{1,0:T(8,128)(2,1)S(1)}, u32[]{:S(2)}, u32[]{:S(2)}) collective-permute-start(bf16[576,128]{1,0:T(8,128)(2,1)S(1)} %collective-permute-done.refs_0_), channel_id=1, source_target_pairs={{0,4},{4,8},{8,12},{12,0},{1,5},{5,9},{9,13},{13,1},{2,6},{6,10},{... | collective-permute-start | bytes 442376 | tf_op jit(solution)/shard_map/ppermute | solution.py:33
  15.0 11.0 %collective-permute-start.3 = (bf16[576,128]{1,0:T(8,128)(2,1)S(1)}, bf16[576,128]{1,0:T(8,128)(2,1)S(1)}, u32[]{:S(2)}, u32[]{:S(2)}) collective-permute-start(bf16[576,128]{1,0:T(8,128)(2,1)S(1)} %collective-permute-done.2.refs_3_), channel_id=1, source_target_pairs={{0,12},{4,0},{8,4},{12,8},{1,13},{5,1},{9,5},{13,9},{2,14},{6,2},{... | collective-permute-start | bytes 442376 | tf_op jit(solution)/shard_map/ppermute | solution.py:33
  16.8 1.4 %copy-start.1 = (bf16[1,384,2048]{2,1,0:T(8,128)(2,1)S(1)}, bf16[1,384,2048]{2,1,0:T(8,128)(2,1)}, u32[]{:S(2)}) copy-start(bf16[1,384,2048]{2,1,0:T(8,128)(2,1)} %down.15) | copy-start | bytes 4718596
  18.2 2.2 %copy-start.3 = (bf16[1024,2048]{1,0:T(8,128)(2,1)S(1)}, bf16[1024,2048]{1,0:T(8,128)(2,1)}, u32[]{:S(2)}) copy-start(bf16[1024,2048]{1,0:T(8,128)(2,1)} %weight.1) | copy-start | bytes 12582916
  20.4 0.9 %copy-start.5 = (bf16[1,64,1024]{2,1,0:T(8,128)(2,1)S(1)}, bf16[1,64,1024]{2,1,0:T(8,128)(2,1)}, u32[]{:S(2)}) copy-start(bf16[1,64,1024]{2,1,0:T(8,128)(2,1)} %param.10) | copy-start | bytes 393220
  21.3 0.7 copy-start.11
  22.0 1.4 %copy-start.6 = (bf16[1,64,1024]{2,1,0:T(8,128)(2,1)S(1)}, bf16[1,64,1024]{2,1,0:T(8,128)(2,1)}, u32[]{:S(2)}) copy-start(bf16[1,64,1024]{2,1,0:T(8,128)(2,1)} %param.10) | copy-start | bytes 393220
  22.0 4.0 %copy-start.4 = (bf16[1024,2048]{1,0:T(8,128)(2,1)S(1)}, bf16[1024,2048]{1,0:T(8,128)(2,1)}, u32[]{:S(2)}) copy-start(bf16[1024,2048]{1,0:T(8,128)(2,1)} %weight.1) | copy-start | bytes 12582916
  23.3 10.5 %copy-start.7 = (bf16[1,16,2048]{2,1,0:T(8,128)(2,1)S(1)}, bf16[1,16,2048]{2,1,0:T(8,128)(2,1)}, u32[]{:S(2)}) copy-start(bf16[1,16,2048]{2,1,0:T(8,128)(2,1)} %param.13) | copy-start | bytes 196612
  23.3 10.5 %copy-start.8 = (f32[2048]{0:T(1024)S(1)}, f32[2048]{0:T(1024)}, u32[]{:S(2)}) copy-start(f32[2048]{0:T(1024)} %param.15) | copy-start | bytes 24580
  23.3 10.5 %copy-start.9 = (s32[1,16,8]{1,2,0:T(8,128)S(1)}, s32[1,16,8]{1,2,0:T(8,128)}, u32[]{:S(2)}) copy-start(s32[1,16,8]{1,2,0:T(8,128)} %param.16) | copy-start | bytes 1540
  23.3 10.5 %copy-start.10 = (f32[1,16,8]{1,2,0:T(8,128)S(1)}, f32[1,16,8]{1,2,0:T(8,128)}, u32[]{:S(2)}) copy-start(f32[1,16,8]{1,2,0:T(8,128)} %param.17) | copy-start | bytes 1540
  28.2 1.9 %collective-permute-start.6 = (bf16[16,2048]{1,0:T(8,128)(2,1)S(1)}, bf16[16,2048]{1,0:T(8,128)(2,1)S(1)}, u32[]{:S(2)}, u32[]{:S(2)}) collective-permute-start(bf16[16,2048]{1,0:T(8,128)(2,1)S(1)} %get-tuple-element.27), channel_id=1, source_target_pairs={{0,1},{1,0},{2,3},{3,2},{4,5},{5,4},{6,7},{7,6},{8,9},{9,8},{10,11... | collective-permute-start | bytes 196616 | tf_op jit(solution)/shard_map/ppermute | solution.py:28
  28.2 4.5 %collective-permute-start.7 = (bf16[16,2048]{1,0:T(8,128)(2,1)S(1)}, bf16[16,2048]{1,0:T(8,128)(2,1)S(1)}, u32[]{:S(2)}, u32[]{:S(2)}) collective-permute-start(bf16[16,2048]{1,0:T(8,128)(2,1)S(1)} %get-tuple-element.28), channel_id=1, source_target_pairs={{0,2},{1,3},{2,0},{3,1},{4,6},{5,7},{6,4},{7,5},{8,10},{9,11},{10,... | collective-permute-start | bytes 196616 | tf_op jit(solution)/shard_map/ppermute | solution.py:28
  29.7 4.1 %collective-permute-start.8 = (bf16[16,2048]{1,0:T(8,128)(2,1)S(1)}, bf16[16,2048]{1,0:T(8,128)(2,1)S(1)}, u32[]{:S(2)}, u32[]{:S(2)}) collective-permute-start(bf16[16,2048]{1,0:T(8,128)(2,1)S(1)} %get-tuple-element.29), channel_id=1, source_target_pairs={{0,3},{1,2},{2,1},{3,0},{4,7},{5,6},{6,5},{7,4},{8,11},{9,10},{10,... | collective-permute-start | bytes 196616 | tf_op jit(solution)/shard_map/ppermute | solution.py:28
  34.1 4.5 %collective-permute-start.9 = (bf16[16,2176]{1,0:T(8,128)(2,1)S(1)}, bf16[16,2176]{1,0:T(8,128)(2,1)S(1)}, u32[]{:S(2)}, u32[]{:S(2)}) collective-permute-start(bf16[16,2176]{1,0:T(8,128)(2,1)S(1)} %get-tuple-element.31), channel_id=1, source_target_pairs={{0,4},{4,0},{8,12},{12,8},{1,5},{5,1},{9,13},{13,9},{2,6},{6,2},{1... | collective-permute-start | bytes 208904 | tf_op jit(solution)/shard_map/ppermute | solution.py:28
  35.3 8.4 %collective-permute-start.12 = (bf16[16,2176]{1,0:T(8,128)(2,1)S(1)}, bf16[16,2176]{1,0:T(8,128)(2,1)S(1)}, u32[]{:S(2)}, u32[]{:S(2)}) collective-permute-start(bf16[16,2176]{1,0:T(8,128)(2,1)S(1)} %get-tuple-element.31), channel_id=1, source_target_pairs={{0,8},{4,12},{8,0},{12,4},{1,9},{5,13},{9,1},{13,5},{2,10},{6,14},... | collective-permute-start | bytes 208904 | tf_op jit(solution)/shard_map/ppermute | solution.py:28
  37.0 6.6 %collective-permute-start.13 = (bf16[16,2176]{1,0:T(8,128)(2,1)S(1)}, bf16[16,2176]{1,0:T(8,128)(2,1)S(1)}, u32[]{:S(2)}, u32[]{:S(2)}) collective-permute-start(bf16[16,2176]{1,0:T(8,128)(2,1)S(1)} %get-tuple-element.31), channel_id=1, source_target_pairs={{0,12},{4,8},{8,4},{12,0},{1,13},{5,9},{9,5},{13,1},{2,14},{6,10},... | collective-permute-start | bytes 208904 | tf_op jit(solution)/shard_map/ppermute | solution.py:28
  38.6 7.4 %collective-permute-start.14 = (bf16[32,2176]{1,0:T(8,128)(2,1)S(1)}, bf16[32,2176]{1,0:T(8,128)(2,1)S(1)}, u32[]{:S(2)}, u32[]{:S(2)}) collective-permute-start(bf16[32,2176]{1,0:T(8,128)(2,1)S(1)} %constant_dynamic-update-slice_fusion.rows), channel_id=1, source_target_pairs={{0,2},{1,3},{2,0},{3,1},{4,6},{5,7},{6,4},{7,5},{8,10},{9,11},{10,... | collective-permute-start | bytes 417800 | tf_op jit(solution)/shard_map/ppermute | solution.py:28
  40.0 9.7 %collective-permute-start.10 = (bf16[32,2176]{1,0:T(8,128)(2,1)S(1)}, bf16[32,2176]{1,0:T(8,128)(2,1)S(1)}, u32[]{:S(2)}, u32[]{:S(2)}) collective-permute-start(bf16[32,2176]{1,0:T(8,128)(2,1)S(1)} %constant_dynamic-update-slice_fusion.rows), channel_id=1, source_target_pairs={{0,1},{1,0},{2,3},{3,2},{4,5},{5,4},{6,7},{7,6},{8,9},{9,8},{10,11... | collective-permute-start | bytes 417800 | tf_op jit(solution)/shard_map/ppermute | solution.py:28
  43.7 4.9 %collective-permute-start.18 = (bf16[32,2176]{1,0:T(8,128)(2,1)S(1)}, bf16[32,2176]{1,0:T(8,128)(2,1)S(1)}, u32[]{:S(2)}, u32[]{:S(2)}) collective-permute-start(bf16[32,2176]{1,0:T(8,128)(2,1)S(1)} %constant_dynamic-update-slice_fusion.2.rows), channel_id=1, source_target_pairs={{0,1},{1,0},{2,3},{3,2},{4,5},{5,4},{6,7},{7,6},{8,9},{9,8},{10,11... | collective-permute-start | bytes 417800 | tf_op jit(solution)/shard_map/ppermute | solution.py:28
  43.8 1.4 %copy-start.2 = (bf16[1,384,2048]{2,1,0:T(8,128)(2,1)S(1)}, bf16[1,384,2048]{2,1,0:T(8,128)(2,1)}, u32[]{:S(2)}) copy-start(bf16[1,384,2048]{2,1,0:T(8,128)(2,1)} %down.15) | copy-start | bytes 4718596
  46.0 5.7 %collective-permute-start.15 = (bf16[32,2176]{1,0:T(8,128)(2,1)S(1)}, bf16[32,2176]{1,0:T(8,128)(2,1)S(1)}, u32[]{:S(2)}, u32[]{:S(2)}) collective-permute-start(bf16[32,2176]{1,0:T(8,128)(2,1)S(1)} %collective-permute-done.14.rows), channel_id=1, source_target_pairs={{0,1},{1,0},{2,3},{3,2},{4,5},{5,4},{6,7},{7,6},{8,9},{9,8},{10,11... | collective-permute-start | bytes 417800 | tf_op jit(solution)/shard_map/ppermute | solution.py:28
  47.2 5.7 %collective-permute-start.20 = (bf16[32,2176]{1,0:T(8,128)(2,1)S(1)}, bf16[32,2176]{1,0:T(8,128)(2,1)S(1)}, u32[]{:S(2)}, u32[]{:S(2)}) collective-permute-start(bf16[32,2176]{1,0:T(8,128)(2,1)S(1)} %constant_dynamic-update-slice_fusion.2.rows), channel_id=1, source_target_pairs={{0,2},{1,3},{2,0},{3,1},{4,6},{5,7},{6,4},{7,5},{8,10},{9,11},{10,... | collective-permute-start | bytes 417800 | tf_op jit(solution)/shard_map/ppermute | solution.py:28
  49.6 14.4 %collective-permute-start.19 = (bf16[32,2048]{1,0:T(8,128)(2,1)S(1)}, bf16[32,2048]{1,0:T(8,128)(2,1)S(1)}, u32[]{:S(2)}, u32[]{:S(2)}) collective-permute-start(bf16[32,2048]{1,0:T(8,128)(2,1)S(1)} %shard_map.122), channel_id=1, source_target_pairs={{0,1},{1,0},{2,3},{3,2},{4,5},{5,4},{6,7},{7,6},{8,9},{9,8},{10,11... | collective-permute-start | bytes 393224 | tf_op jit(solution)/shard_map/ppermute | solution.py:28
  50.8 7.3 %collective-permute-start.11 = (bf16[32,2048]{1,0:T(8,128)(2,1)S(1)}, bf16[32,2048]{1,0:T(8,128)(2,1)S(1)}, u32[]{:S(2)}, u32[]{:S(2)}) collective-permute-start(bf16[32,2048]{1,0:T(8,128)(2,1)S(1)} %shard_map.118), channel_id=1, source_target_pairs={{0,1},{1,0},{2,3},{3,2},{4,5},{5,4},{6,7},{7,6},{8,9},{9,8},{10,11... | collective-permute-start | bytes 393224 | tf_op jit(solution)/shard_map/ppermute | solution.py:28
  52.8 3.1 %collective-permute-start.16 = (bf16[32,2048]{1,0:T(8,128)(2,1)S(1)}, bf16[32,2048]{1,0:T(8,128)(2,1)S(1)}, u32[]{:S(2)}, u32[]{:S(2)}) collective-permute-start(bf16[32,2048]{1,0:T(8,128)(2,1)S(1)} %shard_map.120), channel_id=1, source_target_pairs={{0,1},{1,0},{2,3},{3,2},{4,5},{5,4},{6,7},{7,6},{8,9},{9,8},{10,11... | collective-permute-start | bytes 393224 | tf_op jit(solution)/shard_map/ppermute | solution.py:28
  52.9 1.5 %collective-permute-start.21 = (bf16[32,2176]{1,0:T(8,128)(2,1)S(1)}, bf16[32,2176]{1,0:T(8,128)(2,1)S(1)}, u32[]{:S(2)}, u32[]{:S(2)}) collective-permute-start(bf16[32,2176]{1,0:T(8,128)(2,1)S(1)} %collective-permute-done.20.rows), channel_id=1, source_target_pairs={{0,1},{1,0},{2,3},{3,2},{4,5},{5,4},{6,7},{7,6},{8,9},{9,8},{10,11... | collective-permute-start | bytes 417800 | tf_op jit(solution)/shard_map/ppermute | solution.py:28
  55.5 1.5 %collective-permute-start.22 = (bf16[32,2048]{1,0:T(8,128)(2,1)S(1)}, bf16[32,2048]{1,0:T(8,128)(2,1)S(1)}, u32[]{:S(2)}, u32[]{:S(2)}) collective-permute-start(bf16[32,2048]{1,0:T(8,128)(2,1)S(1)} %shard_map.124), channel_id=1, source_target_pairs={{0,1},{1,0},{2,3},{3,2},{4,5},{5,4},{6,7},{7,6},{8,9},{9,8},{10,11... | collective-permute-start | bytes 393224 | tf_op jit(solution)/shard_map/ppermute | solution.py:28
  55.9 6.4 %collective-permute-start.17 = (bf16[32,2048]{1,0:T(8,128)(2,1)S(1)}, bf16[32,2048]{1,0:T(8,128)(2,1)S(1)}, u32[]{:S(2)}, u32[]{:S(2)}) collective-permute-start(bf16[32,2048]{1,0:T(8,128)(2,1)S(1)} %add_convert_fusion.2), channel_id=1, source_target_pairs={{0,2},{1,3},{2,0},{3,1},{4,6},{5,7},{6,4},{7,5},{8,10},{9,11},{10,... | collective-permute-start | bytes 393224 | tf_op jit(solution)/shard_map/ppermute | solution.py:28
  57.0 7.4 %collective-permute-start.23 = (bf16[32,2048]{1,0:T(8,128)(2,1)S(1)}, bf16[32,2048]{1,0:T(8,128)(2,1)S(1)}, u32[]{:S(2)}, u32[]{:S(2)}) collective-permute-start(bf16[32,2048]{1,0:T(8,128)(2,1)S(1)} %add_convert_fusion.1), channel_id=1, source_target_pairs={{0,2},{1,3},{2,0},{3,1},{4,6},{5,7},{6,4},{7,5},{8,10},{9,11},{10,... | collective-permute-start | bytes 393224 | tf_op jit(solution)/shard_map/ppermute | solution.py:28
  62.3 5.2 %collective-permute-start.26 = (bf16[16,2048]{1,0:T(8,128)(2,1)S(1)}, bf16[16,2048]{1,0:T(8,128)(2,1)S(1)}, u32[]{:S(2)}, u32[]{:S(2)}) collective-permute-start(bf16[16,2048]{1,0:T(8,128)(2,1)S(1)} %slice.104), channel_id=1, source_target_pairs={{0,4},{4,0},{8,12},{12,8},{1,5},{5,1},{9,13},{13,9},{2,6},{6,2},{1... | collective-permute-start | bytes 196616 | tf_op jit(solution)/shard_map/ppermute | solution.py:28
  64.4 6.2 %collective-permute-start.24 = (bf16[16,2048]{1,0:T(8,128)(2,1)S(1)}, bf16[16,2048]{1,0:T(8,128)(2,1)S(1)}, u32[]{:S(2)}, u32[]{:S(2)}) collective-permute-start(bf16[16,2048]{1,0:T(8,128)(2,1)S(1)} %get-tuple-element.36), channel_id=1, source_target_pairs={{0,12},{4,8},{8,4},{12,0},{1,13},{5,9},{9,5},{13,1},{2,14},{6,10},... | collective-permute-start | bytes 196616 | tf_op jit(solution)/shard_map/ppermute | solution.py:28
  66.6 6.7 %collective-permute-start.25 = (bf16[16,2048]{1,0:T(8,128)(2,1)S(1)}, bf16[16,2048]{1,0:T(8,128)(2,1)S(1)}, u32[]{:S(2)}, u32[]{:S(2)}) collective-permute-start(bf16[16,2048]{1,0:T(8,128)(2,1)S(1)} %get-tuple-element.37), channel_id=1, source_target_pairs={{0,8},{4,12},{8,0},{12,4},{1,9},{5,13},{9,1},{13,5},{2,10},{6,14},... | collective-permute-start | bytes 196616 | tf_op jit(solution)/shard_map/ppermute | solution.py:28

commit v5 on v4

--- a/solution.py
+++ b/solution.py
@@ -288,87 +288,100 @@
     )(*parts, residual, norm_gain[None], ids, scores)
 
 
-def down_kernel(inner, rows, down, out):
+def down_kernel(inner, rows, down, keep_out, *send_out):
     expert = lax.axis_index("ctx") * lax.axis_size("exp") + lax.axis_index("exp")
     gate = inner[0]
     activated = (gate / (1.0 + jnp.exp(-gate)) * inner[1]).astype(jnp.bfloat16)
     piece = jnp.dot(activated, down[0], preferred_element_type=jnp.float32)
-    dense = rows[:, out.shape[1] :].astype(jnp.float32)
+    dense = rows[:, piece.shape[1] :].astype(jnp.float32)
     lane = lax.broadcasted_iota(jnp.int32, dense.shape, 1)
     scale = jnp.sum(jnp.where(lane == expert, dense, 0.0), axis=1, keepdims=True)
-    out[...] = (piece.astype(jnp.bfloat16).astype(jnp.float32) * scale).astype(out.dtype)
-
-
-def expert_apply(rows, gate_up, down, kind):
+    result = piece.astype(jnp.bfloat16).astype(jnp.float32) * scale
+    size = keep_out.shape[0]
+    keep_out[...] = result[:size]
+    for out in send_out:
+        out[...] = result[size:].astype(jnp.bfloat16)
+
+
+def expert_apply(rows, gate_up, down, size):
     _, hidden, width = down.shape
+    total = rows.shape[0]
+    half = max(size, total // 2)
     inner = jnp.einsum(
         "nd,dgh->gnh", rows[:, :width], gate_up[0], preferred_element_type=jnp.float32
     )
-    return pl.pallas_call(
+    shapes = [jax.ShapeDtypeStruct((half, width), jnp.float32)]
+    if total > half:
+        shapes.append(jax.ShapeDtypeStruct((total - half, width), jnp.bfloat16))
+    outs = pl.pallas_call(
         down_kernel,
-        out_shape=jax.ShapeDtypeStruct((rows.shape[0], width), kind),
+        out_shape=shapes,
         in_specs=whole_specs(3),
-        out_specs=whole_specs(1)[0],
+        out_specs=whole_specs(len(shapes)),
         compiler_params=LIMIT,
         cost_estimate=pl.CostEstimate(
-            flops=2 * rows.shape[0] * width * hidden, bytes_accessed=2 << 20, transcendentals=0
+            flops=2 * total * width * hidden, bytes_accessed=2 << 20, transcendentals=0
         ),
     )(inner, rows, down)
-
-
-def gather_near(rows, near):
-    pieces = [rows]
-    for stride in near:
-        pieces = pieces + [swap(piece, "exp", stride) for piece in pieces]
-    return pieces
-
-
-def return_near(values, near):
+    return outs[0], (outs[1] if total > half else None)
+
+
+def return_near(keep, send, near):
     for stride in reversed(near):
-        half = len(values) // 2
-        values = [
-            keep.astype(jnp.float32)
-            + swap(send.astype(jnp.bfloat16), "exp", stride).astype(jnp.float32)
-            for keep, send in zip(values[:half], values[half:])
-        ]
-    return values[0].astype(jnp.float32)
+        keep = keep + swap(send, "exp", stride).astype(jnp.float32)
+        half = keep.shape[0] // 2
+        if stride != near[0]:
+            keep, send = keep[:half], keep[half:].astype(jnp.bfloat16)
+    return keep
 
 
 def mixture_of(rows, gate_up, down):
     tokens = rows.shape[0]
-    ctx_count = lax.axis_size("ctx")
+    ctx_strides = strides(lax.axis_size("ctx"))
     exp_strides = strides(lax.axis_size("exp"))
     far, near = exp_strides[:1], exp_strides[1:]
 
-    blocks = {0: rows}
-    for offset in range(1, ctx_count):
-        blocks[offset] = swap(rows, "ctx", offset)
-    half = ctx_count // 2
-    chunks = [list(range(half)), list(range(half, ctx_count))] if half else [[0]]
-    sent = [jnp.concatenate([blocks[offset] for offset in chunk], axis=0) for chunk in chunks]
-
-    def results(pieces):
-        half = (len(pieces) + 1) // 2
-        kinds = [jnp.float32] * half + [jnp.bfloat16] * (len(pieces) - half)
-        values = [expert_apply(piece, gate_up, down, kind) for piece, kind in zip(pieces, kinds)]
-        return return_near(values, near)
-
-    crossed = []
-    for number, piece in enumerate(sent):
-        if crossed:
-            piece, crossed[-1] = lax.optimization_barrier((piece, crossed[-1]))
-        crossed.append([swap(piece, "exp", stride) for stride in far])
-    totals = {}
-    for chunk, home, away in zip(chunks, sent, crossed):
-        value = results(gather_near(home, near))
-        for piece in away:
-            other = results(gather_near(piece, near)).astype(jnp.bfloat16)
+    offsets, chunks, sent = [0], [], rows
+    for stride in ctx_strides[:-1]:
+        sent = jnp.concatenate([sent, swap(sent, "ctx", stride)], axis=0)
+        offsets = offsets + [offset ^ stride for offset in offsets]
+    chunks = [(offsets, sent)]
+    for stride in ctx_strides[-1:]:
+        chunks.append(([offset ^ stride for offset in offsets], swap(sent, "ctx", stride)))
+
+    def gather(piece):
+        held = [piece]
+        for stride in near:
+            held = held + [swap(part, "exp", stride) for part in held]
+        return jnp.concatenate(held, axis=0)
+
+    def results(held, size):
+        return return_near(*expert_apply(held, gate_up, down, size), near)
+
+    size = sent.shape[0]
+    crossed = [
+        [gather(swap(piece, "exp", stride)) for stride in far] for _, piece in chunks
+    ]
+    everything = jnp.concatenate([piece for _, piece in chunks], axis=0)
+    everything, crossed[0] = lax.optimization_barrier((everything, crossed[0]))
+    home = results(gather(everything), size * len(chunks))
+    homes = lax.optimization_barrier(
+        [home[number * size : (number + 1) * size] for number in range(len(chunks))]
+    )
+    total, arrived = None, []
+    for (offsets, _), value, away in zip(chunks, homes, crossed):
+        for part in away:
+            other = results(part, size).astype(jnp.bfloat16)
             value = value + swap(other, "exp", far[0]).astype(jnp.float32)
-        for position, offset in enumerate(chunk):
-            totals[offset] = value[position * tokens : (position + 1) * tokens]
-    total = totals[0]
-    for offset in reversed(range(1, ctx_count)):
-        total = total + swap(totals[offset].astype(jnp.bfloat16), "ctx", offset).astype(jnp.float32)
+        value, arrived = lax.optimization_barrier((value, arrived))
+        for position, offset in enumerate(offsets):
+            block = value[position * tokens : (position + 1) * tokens]
+            if offset == 0:
+                total = block
+            else:
+                arrived.append(swap(block.astype(jnp.bfloat16), "ctx", offset))
+    for block in arrived:
+        total = total + block.astype(jnp.float32)
     return total
 
 

time: 74.2 us -> 72.5 us (0.977)
  waiting for transfers between devices: 21.1 us -> 29.8 us
  starting transfers between devices: 31 us -> 25.7 us
  matrix products: 5.18 us -> 1.95 us
  Pallas kernels: 8.32 us -> 6.42 us
    ppermute x21 -> x18, waiting for transfers between devices: 17.7 us -> 27.3 us  [swap(): lax.ppermute(value, axis, [(i, i ^ stride) for i in range(lax.axis_size(a...]
    ppermute x21 -> x18, starting transfers between devices: 18.3 us -> 11.3 us  [swap(): lax.ppermute(value, axis, [(i, i ^ stride) for i in range(lax.axis_size(a...]
    dot_general x8 -> x3, matrix products: 5.18 us -> 1.95 us  [expert_apply(): jnp.einsum('nd,dgh->gnh', rows[:, :width], gate_up[0], preferred_element_...]
    pallas_call x8 -> x3, Pallas kernels: 3.17 us -> 1.27 us  [expert_apply(): pl.pallas_call(down_kernel, out_shape=shapes, in_specs=whole_specs(3), ou...]
    ppermute x6, starting transfers between devices: 12.8 us -> 14.4 us  [shift(): lax.ppermute(value, axis, [(i, (i + step) % count) for i in range(count)])]
    ppermute x6, waiting for transfers between devices: 3.41 us -> 2.54 us  [shift(): lax.ppermute(value, axis, [(i, (i + step) % count) for i in range(count)])]
    unnamed x27 -> x28, local copies, waits for them, and re-layouts: 6.46 us -> 6.39 us
  transfers between devices with their start and end apart: 27 -> 24, of which waited for: 10 -> 15; matrix products, arithmetic and copies ran while one was open for 7% -> 3% of each run, Pallas kernels for 8% -> 6%
where the time goes in v5:
time: 72.5 us; the launch traced here: 72.2 us
  waiting for transfers between devices  29.8 us (41%)
  starting transfers between devices  25.7 us (35%)
  local copies, waits for them, and re-layouts  6.52 us (9%)
  Pallas kernels  6.42 us (9%)
  matrix products  1.95 us (3%)
  between operations  0.92 us (1%)
  other arithmetic  0.91 us (1%)
    ppermute x18, waiting for transfers between devices, swap(): lax.ppermute(value, axis, [(i, i ^ stride) for i in range(lax.axis_size(a...  27.3 us
    ppermute x6, starting transfers between devices, shift(): lax.ppermute(value, axis, [(i, (i + step) % count) for i in range(count)])  14.4 us
    ppermute x18, starting transfers between devices, swap(): lax.ppermute(value, axis, [(i, i ^ stride) for i in range(lax.axis_size(a...  11.3 us
    unnamed x28, local copies, waits for them, and re-layouts  6.39 us
    ppermute x6, waiting for transfers between devices, shift(): lax.ppermute(value, axis, [(i, (i + step) % count) for i in range(count)])  2.54 us
    pallas_call x1, Pallas kernels, attention(): pl.pallas_call(functools.partial(late_kernel, last[0], fresh_block), out_...  2.16 us
    dot_general x3, matrix products, expert_apply(): jnp.einsum('nd,dgh->gnh', rows[:, :width], gate_up[0], preferred_element_...  1.95 us
  transfers between devices with their start and end apart: 24, of which 15 were waited for; matrix products, arithmetic and copies ran while one was open for 3% of the time, Pallas kernels for 6%

profile of v5, /device:TPU:0, one launch (start us, length us, event | category | flops | bytes accessed | tf_op | source)
XLA Modules:
  0.0 72.2 jit_solution(17675709580883028789)
XLA Ops:
  0.6 1.2 %copy.29 = bf16[1,576,2,128]{3,1,2,0:T(8,128)(2,1)S(1)} copy(bf16[1,576,2,128]{3,2,1,0:T(2,128)(2,1)} %param.11) | data formatting | bytes 589824 | tf_op args[1]
  1.8 5.1 %collective-permute-start.2 = (bf16[576,128]{1,0:T(8,128)(2,1)S(1)}, bf16[576,128]{1,0:T(8,128)(2,1)S(1)}, u32[]{:S(2)}, u32[]{:S(2)}) collective-permute-start(bf16[576,128]{1,0:T(8,128)(2,1)S(1)} %get-tuple-element.56.values), channel_id=1, source_target_pairs={{0,12},{4,0},{8,4},{12,8},{1,13},{5,1},{9,5},{13,9},{2,14},{6,2},{... | collective-permute-start | bytes 442376 | tf_op jit(solution)/shard_map/ppermute | solution.py:33
  6.9 3.9 %collective-permute-start.5 = (bf16[576,128]{1,0:T(8,128)(2,1)S(1)}, bf16[576,128]{1,0:T(8,128)(2,1)S(1)}, u32[]{:S(2)}, u32[]{:S(2)}) collective-permute-start(bf16[576,128]{1,0:T(8,128)(2,1)S(1)} %get-tuple-element.57.keys), channel_id=1, source_target_pairs={{0,12},{4,0},{8,4},{12,8},{1,13},{5,1},{9,5},{13,9},{2,14},{6,2},{... | collective-permute-start | bytes 442376 | tf_op jit(solution)/shard_map/ppermute | solution.py:33
  10.8 0.4 collective-permute-done.2.refs_3_
  11.2 4.3 %collective-permute-start.3 = (bf16[576,128]{1,0:T(8,128)(2,1)S(1)}, bf16[576,128]{1,0:T(8,128)(2,1)S(1)}, u32[]{:S(2)}, u32[]{:S(2)}) collective-permute-start(bf16[576,128]{1,0:T(8,128)(2,1)S(1)} %collective-permute-done.2.refs_3_), channel_id=1, source_target_pairs={{0,12},{4,0},{8,4},{12,8},{1,13},{5,1},{9,5},{13,9},{2,14},{6,2},{... | collective-permute-start | bytes 442376 | tf_op jit(solution)/shard_map/ppermute | solution.py:33
  15.5 0.2 collective-permute-done.refs_0_
  15.7 1.2 %collective-permute-start.1 = (bf16[576,128]{1,0:T(8,128)(2,1)S(1)}, bf16[576,128]{1,0:T(8,128)(2,1)S(1)}, u32[]{:S(2)}, u32[]{:S(2)}) collective-permute-start(bf16[576,128]{1,0:T(8,128)(2,1)S(1)} %collective-permute-done.refs_0_), channel_id=1, source_target_pairs={{0,4},{4,8},{8,12},{12,0},{1,5},{5,9},{9,13},{13,1},{2,6},{6,10},{... | collective-permute-start | bytes 442376 | tf_op jit(solution)/shard_map/ppermute | solution.py:33
  16.8 1.4 %copy-done.1 = bf16[1,384,2048]{2,1,0:T(8,128)(2,1)S(1)} copy-done((bf16[1,384,2048]{2,1,0:T(8,128)(2,1)S(1)}, bf16[1,384,2048]{2,1,0:T(8,128)(2,1)}, u32[]{:S(2)}) %copy-start.1) | copy-done | bytes 1572888
  18.2 2.2 %copy-done.3 = bf16[1024,2048]{1,0:T(8,128)(2,1)S(1)} copy-done((bf16[1024,2048]{1,0:T(8,128)(2,1)S(1)}, bf16[1024,2048]{1,0:T(8,128)(2,1)}, u32[]{:S(2)}) %copy-start.3) | copy-done | bytes 4194328
  20.4 0.9 %copy-done.5 = bf16[1,64,1024]{2,1,0:T(8,128)(2,1)S(1)} copy-done((bf16[1,64,1024]{2,1,0:T(8,128)(2,1)S(1)}, bf16[1,64,1024]{2,1,0:T(8,128)(2,1)}, u32[]{:S(2)}) %copy-start.5) | copy-done | bytes 131096
  21.3 0.7 copy-done.11
  22.0 1.3 %shard_map.113 = (f32[1,512]{1,0:T(1,128)S(1)}, f32[1,512]{1,0:T(1,128)S(1)}, f32[128,512]{1,0:T(8,128)S(1)}, s32[4,128]{1,0:T(4,128)S(1)}) custom-call(s32[4]{0:T(128)S(1)} %bitcast.46, bf16[64,1024]{1,0:T(8,128)(2,1)S(1)} %bitcast.39, bf16[576,128]{1,0:T(8,128)(2,1)S(1)} %get-tuple-element.57.keys, bf16[576,128]{1,0:T(8,128)(2,1)S(1)} %get-tuple-element.56.values, ...), custom_call_target="tpu_custom_call" | custom-call | flops 2415919104 | bytes 8388608 | tf_op jit(solution)/shard_map/pallas_call | solution.py:206
  23.4 1.4 %shard_map.114 = (f32[1,512]{1,0:T(1,128)S(1)}, f32[1,512]{1,0:T(1,128)S(1)}, f32[128,512]{1,0:T(8,128)S(1)}) custom-call(bf16[64,1024]{1,0:T(8,128)(2,1)S(1)} %bitcast.40, s32[4,128]{1,0:T(4,128)S(1)} %get-tuple-element.28.lengths, bf16[576,128]{1,0:T(8,128)(2,1)S(1)} %collective-permute-done.refs_0_, bf16[576,128]{1,0:T(8,128)(2,1)S(1)} %collective-permute-done.4.refs_1_, ...), custom_call_target="tpu_custom_call" | custom-call | flops 301989888 | bytes 2097152 | tf_op jit(solution)/shard_map/pallas_call | solution.py:221
  24.8 1.9 %collective-permute-done.1.keys = bf16[576,128]{1,0:T(8,128)(2,1)S(1)} collective-permute-done((bf16[576,128]{1,0:T(8,128)(2,1)S(1)}, bf16[576,128]{1,0:T(8,128)(2,1)S(1)}, u32[]{:S(2)}, u32[]{:S(2)}) %collective-permute-start.1) | collective-permute-done | bytes 147488 | tf_op jit(solution)/shard_map/ppermute | solution.py:33
  26.8 2.2 %shard_map.115 = (bf16[64,1024]{1,0:T(8,128)(2,1)}, f32[16,2048]{1,0:T(8,128)S(1)}, bf16[16,2048]{1,0:T(8,128)(2,1)S(1)}, bf16[16,2048]{1,0:T(8,128)(2,1)S(1)}, bf16[16,2048]{1,0:T(8,128)(2,1)S(1)}) custom-call(bf16[64,1024]{1,0:T(8,128)(2,1)S(1)} %bitcast.41, bf16[576,128]{1,0:T(8,128)(2,1)S(1)} %collective-permute-done.1.keys, ...), custom_call_target="tpu_custom_call" | custom-call | flops 419430400 | bytes 6291456 | tf_op jit(solution)/shard_map/pallas_call | solution.py:232
  29.0 1.5 %collective-permute-start.7 = (bf16[16,2048]{1,0:T(8,128)(2,1)S(1)}, bf16[16,2048]{1,0:T(8,128)(2,1)S(1)}, u32[]{:S(2)}, u32[]{:S(2)}) collective-permute-start(bf16[16,2048]{1,0:T(8,128)(2,1)S(1)} %get-tuple-element.38), channel_id=1, source_target_pairs={{0,2},{1,3},{2,0},{3,1},{4,6},{5,7},{6,4},{7,5},{8,10},{9,11},{10,... | collective-permute-start | bytes 196616 | tf_op jit(solution)/shard_map/ppermute | solution.py:28
  30.4 0.4 collective-permute-start.8
  30.8 2.7 %collective-permute-done.7.refs_2_ = bf16[16,2048]{1,0:T(8,128)(2,1)S(1)} collective-permute-done((bf16[16,2048]{1,0:T(8,128)(2,1)S(1)}, bf16[16,2048]{1,0:T(8,128)(2,1)S(1)}, u32[]{:S(2)}, u32[]{:S(2)}) %collective-permute-start.7) | collective-permute-done | bytes 65568 | tf_op jit(solution)/shard_map/ppermute | solution.py:28
  33.5 1.1 %collective-permute-done.8.refs_3_ = bf16[16,2048]{1,0:T(8,128)(2,1)S(1)} collective-permute-done((bf16[16,2048]{1,0:T(8,128)(2,1)S(1)}, bf16[16,2048]{1,0:T(8,128)(2,1)S(1)}, u32[]{:S(2)}, u32[]{:S(2)}) %collective-permute-start.8) | collective-permute-done | bytes 65568 | tf_op jit(solution)/shard_map/ppermute | solution.py:28
  34.6 0.3 shard_map.116
  34.9 0.8 %collective-permute-start.9 = (bf16[16,2176]{1,0:T(8,128)(2,1)S(1)}, bf16[16,2176]{1,0:T(8,128)(2,1)S(1)}, u32[]{:S(2)}, u32[]{:S(2)}) collective-permute-start(bf16[16,2176]{1,0:T(8,128)(2,1)S(1)} %get-tuple-element.41), channel_id=1, source_target_pairs={{0,8},{4,12},{8,0},{12,4},{1,9},{5,13},{9,1},{13,5},{2,10},{6,14},... | collective-permute-start | bytes 208904 | tf_op jit(solution)/shard_map/ppermute | solution.py:28
  35.6 6.0 %collective-permute-done.9 = bf16[16,2176]{1,0:T(8,128)(2,1)S(1)} collective-permute-done((bf16[16,2176]{1,0:T(8,128)(2,1)S(1)}, bf16[16,2176]{1,0:T(8,128)(2,1)S(1)}, u32[]{:S(2)}, u32[]{:S(2)}) %collective-permute-start.9) | collective-permute-done | bytes 69664 | tf_op jit(solution)/shard_map/ppermute | solution.py:28
  41.6 1.5 %collective-permute-start.11 = (bf16[32,2176]{1,0:T(8,128)(2,1)S(1)}, bf16[32,2176]{1,0:T(8,128)(2,1)S(1)}, u32[]{:S(2)}, u32[]{:S(2)}) collective-permute-start(bf16[32,2176]{1,0:T(8,128)(2,1)S(1)} %constant_dynamic-update-slice_fusion), channel_id=1, source_target_pairs={{0,2},{1,3},{2,0},{3,1},{4,6},{5,7},{6,4},{7,5},{8,10},{9,11},{10,... | collective-permute-start | bytes 417800 | tf_op jit(solution)/shard_map/ppermute | solution.py:28
  43.1 0.2 collective-permute-start.10
  43.3 3.4 %collective-permute-done.11 = bf16[32,2176]{1,0:T(8,128)(2,1)S(1)} collective-permute-done((bf16[32,2176]{1,0:T(8,128)(2,1)S(1)}, bf16[32,2176]{1,0:T(8,128)(2,1)S(1)}, u32[]{:S(2)}, u32[]{:S(2)}) %collective-permute-start.11) | collective-permute-done | bytes 139296 | tf_op jit(solution)/shard_map/ppermute | solution.py:28
  46.8 1.4 %collective-permute-done.10 = bf16[32,2176]{1,0:T(8,128)(2,1)S(1)} collective-permute-done((bf16[32,2176]{1,0:T(8,128)(2,1)S(1)}, bf16[32,2176]{1,0:T(8,128)(2,1)S(1)}, u32[]{:S(2)}, u32[]{:S(2)}) %collective-permute-start.10) | collective-permute-done | bytes 139296 | tf_op jit(solution)/shard_map/ppermute | solution.py:28
  48.2 0.7 collective-permute-start.17
  49.0 0.7 fusion.9.inner
  49.7 0.4 shard_map.118
  50.1 0.6 collective-permute-start.15
  50.7 2.6 %collective-permute-done.17 = bf16[32,2176]{1,0:T(8,128)(2,1)S(1)} collective-permute-done((bf16[32,2176]{1,0:T(8,128)(2,1)S(1)}, bf16[32,2176]{1,0:T(8,128)(2,1)S(1)}, u32[]{:S(2)}, u32[]{:S(2)}) %collective-permute-start.17) | collective-permute-done | bytes 139296 | tf_op jit(solution)/shard_map/ppermute | solution.py:28
  53.4 1.1 %collective-permute-start.16 = (bf16[32,2048]{1,0:T(8,128)(2,1)S(1)}, bf16[32,2048]{1,0:T(8,128)(2,1)S(1)}, u32[]{:S(2)}, u32[]{:S(2)}) collective-permute-start(bf16[32,2048]{1,0:T(8,128)(2,1)S(1)} %add_convert_fusion.1), channel_id=1, source_target_pairs={{0,2},{1,3},{2,0},{3,1},{4,6},{5,7},{6,4},{7,5},{8,10},{9,11},{10,... | collective-permute-start | bytes 393224 | tf_op jit(solution)/shard_map/ppermute | solution.py:28
  54.5 0.2 collective-permute-done.18
  54.7 0.7 fusion.12.inner
  55.4 0.4 shard_map.119
  55.8 0.2 collective-permute-start.19
  56.0 0.6 fusion.6.inner
  56.6 0.5 shard_map.117
  57.1 0.4 collective-permute-start.14
  57.6 1.1 %collective-permute-start.20 = (bf16[32,2048]{1,0:T(8,128)(2,1)S(1)}, bf16[32,2048]{1,0:T(8,128)(2,1)S(1)}, u32[]{:S(2)}, u32[]{:S(2)}) collective-permute-start(bf16[32,2048]{1,0:T(8,128)(2,1)S(1)} %add_convert_fusion), channel_id=1, source_target_pairs={{0,2},{1,3},{2,0},{3,1},{4,6},{5,7},{6,4},{7,5},{8,10},{9,11},{10,... | collective-permute-start | bytes 393224 | tf_op jit(solution)/shard_map/ppermute | solution.py:28
  58.8 0.5 collective-permute-done.16
  59.4 0.7 %collective-permute-start.21 = (bf16[16,2048]{1,0:T(8,128)(2,1)S(1)}, bf16[16,2048]{1,0:T(8,128)(2,1)S(1)}, u32[]{:S(2)}, u32[]{:S(2)}) collective-permute-start(bf16[16,2048]{1,0:T(8,128)(2,1)S(1)} %slice.79), channel_id=1, source_target_pairs={{0,8},{4,12},{8,0},{12,4},{1,9},{5,13},{9,1},{13,5},{2,10},{6,14},... | collective-permute-start | bytes 196616 | tf_op jit(solution)/shard_map/ppermute | solution.py:28
  60.1 3.0 %collective-permute-done.20 = bf16[32,2048]{1,0:T(8,128)(2,1)S(1)} collective-permute-done((bf16[32,2048]{1,0:T(8,128)(2,1)S(1)}, bf16[32,2048]{1,0:T(8,128)(2,1)S(1)}, u32[]{:S(2)}, u32[]{:S(2)}) %collective-permute-start.20) | collective-permute-done | bytes 131104 | tf_op jit(solution)/shard_map/ppermute | solution.py:28
  63.2 2.0 %collective-permute-done.21 = bf16[16,2048]{1,0:T(8,128)(2,1)S(1)} collective-permute-done((bf16[16,2048]{1,0:T(8,128)(2,1)S(1)}, bf16[16,2048]{1,0:T(8,128)(2,1)S(1)}, u32[]{:S(2)}, u32[]{:S(2)}) %collective-permute-start.21) | collective-permute-done | bytes 65568 | tf_op jit(solution)/shard_map/ppermute | solution.py:28
  65.3 2.0 %collective-permute-start.23 = (bf16[16,2048]{1,0:T(8,128)(2,1)S(1)}, bf16[16,2048]{1,0:T(8,128)(2,1)S(1)}, u32[]{:S(2)}, u32[]{:S(2)}) collective-permute-start(bf16[16,2048]{1,0:T(8,128)(2,1)S(1)} %get-tuple-element.59), channel_id=1, source_target_pairs={{0,12},{4,8},{8,4},{12,0},{1,13},{5,9},{9,5},{13,1},{2,14},{6,10},... | collective-permute-start | bytes 196616 | tf_op jit(solution)/shard_map/ppermute | solution.py:28
  67.3 3.0 %collective-permute-done.22 = bf16[16,2048]{1,0:T(8,128)(2,1)S(1)} collective-permute-done((bf16[16,2048]{1,0:T(8,128)(2,1)S(1)}, bf16[16,2048]{1,0:T(8,128)(2,1)S(1)}, u32[]{:S(2)}, u32[]{:S(2)}) %collective-permute-start.22) | collective-permute-done | bytes 65568 | tf_op jit(solution)/shard_map/ppermute | solution.py:28
  70.3 1.3 %collective-permute-done.23 = bf16[16,2048]{1,0:T(8,128)(2,1)S(1)} collective-permute-done((bf16[16,2048]{1,0:T(8,128)(2,1)S(1)}, bf16[16,2048]{1,0:T(8,128)(2,1)S(1)}, u32[]{:S(2)}, u32[]{:S(2)}) %collective-permute-start.23) | collective-permute-done | bytes 65568 | tf_op jit(solution)/shard_map/ppermute | solution.py:28
  71.6 0.7 fusion.21
  (53 shorter events, 0.7 us)
Async XLA Ops:
  0.6 48.4 %copy-start = (bf16[1,2048,2,384]{3,2,1,0:T(2,128)(2,1)S(1)}, bf16[1,2048,2,384]{3,2,1,0:T(2,128)(2,1)}, u32[]{:S(2)}) copy-start(bf16[1,2048,2,384]{3,2,1,0:T(2,128)(2,1)} %param.18) | copy-start | bytes 9437188
  1.8 9.4 %collective-permute-start.2 = (bf16[576,128]{1,0:T(8,128)(2,1)S(1)}, bf16[576,128]{1,0:T(8,128)(2,1)S(1)}, u32[]{:S(2)}, u32[]{:S(2)}) collective-permute-start(bf16[576,128]{1,0:T(8,128)(2,1)S(1)} %get-tuple-element.56.values), channel_id=1, source_target_pairs={{0,12},{4,0},{8,4},{12,8},{1,13},{5,1},{9,5},{13,9},{2,14},{6,2},{... | collective-permute-start | bytes 442376 | tf_op jit(solution)/shard_map/ppermute | solution.py:33
  6.9 8.7 %collective-permute-start = (bf16[576,128]{1,0:T(8,128)(2,1)S(1)}, bf16[576,128]{1,0:T(8,128)(2,1)S(1)}, u32[]{:S(2)}, u32[]{:S(2)}) collective-permute-start(bf16[576,128]{1,0:T(8,128)(2,1)S(1)} %get-tuple-element.57.keys), channel_id=1, source_target_pairs={{0,4},{4,8},{8,12},{12,0},{1,5},{5,9},{9,13},{13,1},{2,6},{6,10},{... | collective-permute-start | bytes 442376 | tf_op jit(solution)/shard_map/ppermute | solution.py:33
  6.9 16.4 %collective-permute-start.4 = (bf16[576,128]{1,0:T(8,128)(2,1)S(1)}, bf16[576,128]{1,0:T(8,128)(2,1)S(1)}, u32[]{:S(2)}, u32[]{:S(2)}) collective-permute-start(bf16[576,128]{1,0:T(8,128)(2,1)S(1)} %get-tuple-element.56.values), channel_id=1, source_target_pairs={{0,4},{4,8},{8,12},{12,0},{1,5},{5,9},{9,13},{13,1},{2,6},{6,10},{... | collective-permute-start | bytes 442376 | tf_op jit(solution)/shard_map/ppermute | solution.py:33
  6.9 16.4 %collective-permute-start.5 = (bf16[576,128]{1,0:T(8,128)(2,1)S(1)}, bf16[576,128]{1,0:T(8,128)(2,1)S(1)}, u32[]{:S(2)}, u32[]{:S(2)}) collective-permute-start(bf16[576,128]{1,0:T(8,128)(2,1)S(1)} %get-tuple-element.57.keys), channel_id=1, source_target_pairs={{0,12},{4,0},{8,4},{12,8},{1,13},{5,1},{9,5},{13,9},{2,14},{6,2},{... | collective-permute-start | bytes 442376 | tf_op jit(solution)/shard_map/ppermute | solution.py:33
  11.2 13.6 %collective-permute-start.3 = (bf16[576,128]{1,0:T(8,128)(2,1)S(1)}, bf16[576,128]{1,0:T(8,128)(2,1)S(1)}, u32[]{:S(2)}, u32[]{:S(2)}) collective-permute-start(bf16[576,128]{1,0:T(8,128)(2,1)S(1)} %collective-permute-done.2.refs_3_), channel_id=1, source_target_pairs={{0,12},{4,0},{8,4},{12,8},{1,13},{5,1},{9,5},{13,9},{2,14},{6,2},{... | collective-permute-start | bytes 442376 | tf_op jit(solution)/shard_map/ppermute | solution.py:33
  15.7 11.1 %collective-permute-start.1 = (bf16[576,128]{1,0:T(8,128)(2,1)S(1)}, bf16[576,128]{1,0:T(8,128)(2,1)S(1)}, u32[]{:S(2)}, u32[]{:S(2)}) collective-permute-start(bf16[576,128]{1,0:T(8,128)(2,1)S(1)} %collective-permute-done.refs_0_), channel_id=1, source_target_pairs={{0,4},{4,8},{8,12},{12,0},{1,5},{5,9},{9,13},{13,1},{2,6},{6,10},{... | collective-permute-start | bytes 442376 | tf_op jit(solution)/shard_map/ppermute | solution.py:33
  16.8 1.4 %copy-start.1 = (bf16[1,384,2048]{2,1,0:T(8,128)(2,1)S(1)}, bf16[1,384,2048]{2,1,0:T(8,128)(2,1)}, u32[]{:S(2)}) copy-start(bf16[1,384,2048]{2,1,0:T(8,128)(2,1)} %down.5) | copy-start | bytes 4718596
  18.2 2.2 %copy-start.3 = (bf16[1024,2048]{1,0:T(8,128)(2,1)S(1)}, bf16[1024,2048]{1,0:T(8,128)(2,1)}, u32[]{:S(2)}) copy-start(bf16[1024,2048]{1,0:T(8,128)(2,1)} %weight.1) | copy-start | bytes 12582916
  20.4 0.9 %copy-start.5 = (bf16[1,64,1024]{2,1,0:T(8,128)(2,1)S(1)}, bf16[1,64,1024]{2,1,0:T(8,128)(2,1)}, u32[]{:S(2)}) copy-start(bf16[1,64,1024]{2,1,0:T(8,128)(2,1)} %param.10) | copy-start | bytes 393220
  21.3 0.7 copy-start.11
  22.0 1.4 %copy-start.6 = (bf16[1,64,1024]{2,1,0:T(8,128)(2,1)S(1)}, bf16[1,64,1024]{2,1,0:T(8,128)(2,1)}, u32[]{:S(2)}) copy-start(bf16[1,64,1024]{2,1,0:T(8,128)(2,1)} %param.10) | copy-start | bytes 393220
  22.0 4.8 %copy-start.4 = (bf16[1024,2048]{1,0:T(8,128)(2,1)S(1)}, bf16[1024,2048]{1,0:T(8,128)(2,1)}, u32[]{:S(2)}) copy-start(bf16[1024,2048]{1,0:T(8,128)(2,1)} %weight.1) | copy-start | bytes 12582916
  23.3 11.3 %copy-start.7 = (bf16[1,16,2048]{2,1,0:T(8,128)(2,1)S(1)}, bf16[1,16,2048]{2,1,0:T(8,128)(2,1)}, u32[]{:S(2)}) copy-start(bf16[1,16,2048]{2,1,0:T(8,128)(2,1)} %param.13) | copy-start | bytes 196612
  23.3 11.3 %copy-start.8 = (f32[2048]{0:T(1024)S(1)}, f32[2048]{0:T(1024)}, u32[]{:S(2)}) copy-start(f32[2048]{0:T(1024)} %param.15) | copy-start | bytes 24580
  23.3 11.2 %copy-start.9 = (s32[1,16,8]{1,2,0:T(8,128)S(1)}, s32[1,16,8]{1,2,0:T(8,128)}, u32[]{:S(2)}) copy-start(s32[1,16,8]{1,2,0:T(8,128)} %param.16) | copy-start | bytes 1540
  23.3 11.2 %copy-start.10 = (f32[1,16,8]{1,2,0:T(8,128)S(1)}, f32[1,16,8]{1,2,0:T(8,128)}, u32[]{:S(2)}) copy-start(f32[1,16,8]{1,2,0:T(8,128)} %param.17) | copy-start | bytes 1540
  29.0 1.9 %collective-permute-start.6 = (bf16[16,2048]{1,0:T(8,128)(2,1)S(1)}, bf16[16,2048]{1,0:T(8,128)(2,1)S(1)}, u32[]{:S(2)}, u32[]{:S(2)}) collective-permute-start(bf16[16,2048]{1,0:T(8,128)(2,1)S(1)} %get-tuple-element.37), channel_id=1, source_target_pairs={{0,1},{1,0},{2,3},{3,2},{4,5},{5,4},{6,7},{7,6},{8,9},{9,8},{10,11... | collective-permute-start | bytes 196616 | tf_op jit(solution)/shard_map/ppermute | solution.py:28
  29.0 4.5 %collective-permute-start.7 = (bf16[16,2048]{1,0:T(8,128)(2,1)S(1)}, bf16[16,2048]{1,0:T(8,128)(2,1)S(1)}, u32[]{:S(2)}, u32[]{:S(2)}) collective-permute-start(bf16[16,2048]{1,0:T(8,128)(2,1)S(1)} %get-tuple-element.38), channel_id=1, source_target_pairs={{0,2},{1,3},{2,0},{3,1},{4,6},{5,7},{6,4},{7,5},{8,10},{9,11},{10,... | collective-permute-start | bytes 196616 | tf_op jit(solution)/shard_map/ppermute | solution.py:28
  30.4 4.1 %collective-permute-start.8 = (bf16[16,2048]{1,0:T(8,128)(2,1)S(1)}, bf16[16,2048]{1,0:T(8,128)(2,1)S(1)}, u32[]{:S(2)}, u32[]{:S(2)}) collective-permute-start(bf16[16,2048]{1,0:T(8,128)(2,1)S(1)} %get-tuple-element.39), channel_id=1, source_target_pairs={{0,3},{1,2},{2,1},{3,0},{4,7},{5,6},{6,5},{7,4},{8,11},{9,10},{10,... | collective-permute-start | bytes 196616 | tf_op jit(solution)/shard_map/ppermute | solution.py:28
  34.6 15.1 %copy-start.2 = (bf16[1,384,2048]{2,1,0:T(8,128)(2,1)S(1)}, bf16[1,384,2048]{2,1,0:T(8,128)(2,1)}, u32[]{:S(2)}) copy-start(bf16[1,384,2048]{2,1,0:T(8,128)(2,1)} %down.5) | copy-start | bytes 4718596
  34.9 6.8 %collective-permute-start.9 = (bf16[16,2176]{1,0:T(8,128)(2,1)S(1)}, bf16[16,2176]{1,0:T(8,128)(2,1)S(1)}, u32[]{:S(2)}, u32[]{:S(2)}) collective-permute-start(bf16[16,2176]{1,0:T(8,128)(2,1)S(1)} %get-tuple-element.41), channel_id=1, source_target_pairs={{0,8},{4,12},{8,0},{12,4},{1,9},{5,13},{9,1},{13,5},{2,10},{6,14},... | collective-permute-start | bytes 208904 | tf_op jit(solution)/shard_map/ppermute | solution.py:28
  41.6 5.1 %collective-permute-start.11 = (bf16[32,2176]{1,0:T(8,128)(2,1)S(1)}, bf16[32,2176]{1,0:T(8,128)(2,1)S(1)}, u32[]{:S(2)}, u32[]{:S(2)}) collective-permute-start(bf16[32,2176]{1,0:T(8,128)(2,1)S(1)} %constant_dynamic-update-slice_fusion), channel_id=1, source_target_pairs={{0,2},{1,3},{2,0},{3,1},{4,6},{5,7},{6,4},{7,5},{8,10},{9,11},{10,... | collective-permute-start | bytes 417800 | tf_op jit(solution)/shard_map/ppermute | solution.py:28
  43.1 5.1 %collective-permute-start.10 = (bf16[32,2176]{1,0:T(8,128)(2,1)S(1)}, bf16[32,2176]{1,0:T(8,128)(2,1)S(1)}, u32[]{:S(2)}, u32[]{:S(2)}) collective-permute-start(bf16[32,2176]{1,0:T(8,128)(2,1)S(1)} %constant_dynamic-update-slice_fusion), channel_id=1, source_target_pairs={{0,4},{4,0},{8,12},{12,8},{1,5},{5,1},{9,13},{13,9},{2,6},{6,2},{1... | collective-permute-start | bytes 417800 | tf_op jit(solution)/shard_map/ppermute | solution.py:28
  46.8 2.1 %collective-permute-start.12 = (bf16[32,2176]{1,0:T(8,128)(2,1)S(1)}, bf16[32,2176]{1,0:T(8,128)(2,1)S(1)}, u32[]{:S(2)}, u32[]{:S(2)}) collective-permute-start(bf16[32,2176]{1,0:T(8,128)(2,1)S(1)} %collective-permute-done.11), channel_id=1, source_target_pairs={{0,1},{1,0},{2,3},{3,2},{4,5},{5,4},{6,7},{7,6},{8,9},{9,8},{10,11... | collective-permute-start | bytes 417800 | tf_op jit(solution)/shard_map/ppermute | solution.py:28
  48.2 5.1 %collective-permute-start.17 = (bf16[32,2176]{1,0:T(8,128)(2,1)S(1)}, bf16[32,2176]{1,0:T(8,128)(2,1)S(1)}, u32[]{:S(2)}, u32[]{:S(2)}) collective-permute-start(bf16[32,2176]{1,0:T(8,128)(2,1)S(1)} %collective-permute-done.10), channel_id=1, source_target_pairs={{0,2},{1,3},{2,0},{3,1},{4,6},{5,7},{6,4},{7,5},{8,10},{9,11},{10,... | collective-permute-start | bytes 417800 | tf_op jit(solution)/shard_map/ppermute | solution.py:28
  48.9 7.1 %collective-permute-start.13 = (bf16[64,2176]{1,0:T(8,128)(2,1)S(1)}, bf16[64,2176]{1,0:T(8,128)(2,1)S(1)}, u32[]{:S(2)}, u32[]{:S(2)}) collective-permute-start(bf16[64,2176]{1,0:T(8,128)(2,1)S(1)} %pad_maximum_fusion), channel_id=1, source_target_pairs={{0,1},{1,0},{2,3},{3,2},{4,5},{5,4},{6,7},{7,6},{8,9},{9,8},{10,11... | collective-permute-start | bytes 835592 | tf_op jit(solution)/shard_map/ppermute | solution.py:28
  50.1 3.2 %collective-permute-start.15 = (bf16[32,2048]{1,0:T(8,128)(2,1)S(1)}, bf16[32,2048]{1,0:T(8,128)(2,1)S(1)}, u32[]{:S(2)}, u32[]{:S(2)}) collective-permute-start(bf16[32,2048]{1,0:T(8,128)(2,1)S(1)} %get-tuple-element.48), channel_id=1, source_target_pairs={{0,1},{1,0},{2,3},{3,2},{4,5},{5,4},{6,7},{7,6},{8,9},{9,8},{10,11... | collective-permute-start | bytes 393224 | tf_op jit(solution)/shard_map/ppermute | solution.py:28
  53.3 1.4 %collective-permute-start.18 = (bf16[32,2176]{1,0:T(8,128)(2,1)S(1)}, bf16[32,2176]{1,0:T(8,128)(2,1)S(1)}, u32[]{:S(2)}, u32[]{:S(2)}) collective-permute-start(bf16[32,2176]{1,0:T(8,128)(2,1)S(1)} %collective-permute-done.17), channel_id=1, source_target_pairs={{0,1},{1,0},{2,3},{3,2},{4,5},{5,4},{6,7},{7,6},{8,9},{9,8},{10,11... | collective-permute-start | bytes 417800 | tf_op jit(solution)/shard_map/ppermute | solution.py:28
  53.4 6.0 %collective-permute-start.16 = (bf16[32,2048]{1,0:T(8,128)(2,1)S(1)}, bf16[32,2048]{1,0:T(8,128)(2,1)S(1)}, u32[]{:S(2)}, u32[]{:S(2)}) collective-permute-start(bf16[32,2048]{1,0:T(8,128)(2,1)S(1)} %add_convert_fusion.1), channel_id=1, source_target_pairs={{0,2},{1,3},{2,0},{3,1},{4,6},{5,7},{6,4},{7,5},{8,10},{9,11},{10,... | collective-permute-start | bytes 393224 | tf_op jit(solution)/shard_map/ppermute | solution.py:28
  55.8 1.8 %collective-permute-start.19 = (bf16[32,2048]{1,0:T(8,128)(2,1)S(1)}, bf16[32,2048]{1,0:T(8,128)(2,1)S(1)}, u32[]{:S(2)}, u32[]{:S(2)}) collective-permute-start(bf16[32,2048]{1,0:T(8,128)(2,1)S(1)} %get-tuple-element.51), channel_id=1, source_target_pairs={{0,1},{1,0},{2,3},{3,2},{4,5},{5,4},{6,7},{7,6},{8,9},{9,8},{10,11... | collective-permute-start | bytes 393224 | tf_op jit(solution)/shard_map/ppermute | solution.py:28
  57.1 1.6 %collective-permute-start.14 = (bf16[64,2048]{1,0:T(8,128)(2,1)S(1)}, bf16[64,2048]{1,0:T(8,128)(2,1)S(1)}, u32[]{:S(2)}, u32[]{:S(2)}) collective-permute-start(bf16[64,2048]{1,0:T(8,128)(2,1)S(1)} %get-tuple-element.44), channel_id=1, source_target_pairs={{0,1},{1,0},{2,3},{3,2},{4,5},{5,4},{6,7},{7,6},{8,9},{9,8},{10,11... | collective-permute-start | bytes 786440 | tf_op jit(solution)/shard_map/ppermute | solution.py:28
  57.6 5.6 %collective-permute-start.20 = (bf16[32,2048]{1,0:T(8,128)(2,1)S(1)}, bf16[32,2048]{1,0:T(8,128)(2,1)S(1)}, u32[]{:S(2)}, u32[]{:S(2)}) collective-permute-start(bf16[32,2048]{1,0:T(8,128)(2,1)S(1)} %add_convert_fusion), channel_id=1, source_target_pairs={{0,2},{1,3},{2,0},{3,1},{4,6},{5,7},{6,4},{7,5},{8,10},{9,11},{10,... | collective-permute-start | bytes 393224 | tf_op jit(solution)/shard_map/ppermute | solution.py:28
  59.4 5.9 %collective-permute-start.21 = (bf16[16,2048]{1,0:T(8,128)(2,1)S(1)}, bf16[16,2048]{1,0:T(8,128)(2,1)S(1)}, u32[]{:S(2)}, u32[]{:S(2)}) collective-permute-start(bf16[16,2048]{1,0:T(8,128)(2,1)S(1)} %slice.79), channel_id=1, source_target_pairs={{0,8},{4,12},{8,0},{12,4},{1,9},{5,13},{9,1},{13,5},{2,10},{6,14},... | collective-permute-start | bytes 196616 | tf_op jit(solution)/shard_map/ppermute | solution.py:28
  65.3 5.0 %collective-permute-start.22 = (bf16[16,2048]{1,0:T(8,128)(2,1)S(1)}, bf16[16,2048]{1,0:T(8,128)(2,1)S(1)}, u32[]{:S(2)}, u32[]{:S(2)}) collective-permute-start(bf16[16,2048]{1,0:T(8,128)(2,1)S(1)} %get-tuple-element.58), channel_id=1, source_target_pairs={{0,4},{4,0},{8,12},{12,8},{1,5},{5,1},{9,13},{13,9},{2,6},{6,2},{1... | collective-permute-start | bytes 196616 | tf_op jit(solution)/shard_map/ppermute | solution.py:28
  65.3 6.2 %collective-permute-start.23 = (bf16[16,2048]{1,0:T(8,128)(2,1)S(1)}, bf16[16,2048]{1,0:T(8,128)(2,1)S(1)}, u32[]{:S(2)}, u32[]{:S(2)}) collective-permute-start(bf16[16,2048]{1,0:T(8,128)(2,1)S(1)} %get-tuple-element.59), channel_id=1, source_target_pairs={{0,12},{4,8},{8,4},{12,0},{1,13},{5,9},{9,5},{13,1},{2,14},{6,10},... | collective-permute-start | bytes 196616 | tf_op jit(solution)/shard_map/ppermute | solution.py:28

commit v6 on v5

--- a/solution.py
+++ b/solution.py
@@ -335,19 +335,16 @@
     return keep
 
 
+def chunks_of(count):
+    chunks = [range(0, count, 2), range(1, count, 4), range(3, count, 4)]
+    return [list(chunk) for chunk in chunks if len(chunk)]
+
+
 def mixture_of(rows, gate_up, down):
     tokens = rows.shape[0]
-    ctx_strides = strides(lax.axis_size("ctx"))
     exp_strides = strides(lax.axis_size("exp"))
     far, near = exp_strides[:1], exp_strides[1:]
-
-    offsets, chunks, sent = [0], [], rows
-    for stride in ctx_strides[:-1]:
-        sent = jnp.concatenate([sent, swap(sent, "ctx", stride)], axis=0)
-        offsets = offsets + [offset ^ stride for offset in offsets]
-    chunks = [(offsets, sent)]
-    for stride in ctx_strides[-1:]:
-        chunks.append(([offset ^ stride for offset in offsets], swap(sent, "ctx", stride)))
+    chunks = chunks_of(lax.axis_size("ctx"))
 
     def gather(piece):
         held = [piece]
@@ -358,23 +355,32 @@
     def results(held, size):
         return return_near(*expert_apply(held, gate_up, down, size), near)
 
-    size = sent.shape[0]
-    crossed = [
-        [gather(swap(piece, "exp", stride)) for stride in far] for _, piece in chunks
-    ]
-    everything = jnp.concatenate([piece for _, piece in chunks], axis=0)
-    everything, crossed[0] = lax.optimization_barrier((everything, crossed[0]))
-    home = results(gather(everything), size * len(chunks))
-    homes = lax.optimization_barrier(
-        [home[number * size : (number + 1) * size] for number in range(len(chunks))]
-    )
+    sent = []
+    for chunk in chunks:
+        blocks = [rows if offset == 0 else swap(rows, "ctx", offset) for offset in chunk]
+        sent.append(jnp.concatenate(blocks, axis=0))
+    crossed = []
+    for piece in sent:
+        arrived = [swap(piece, "exp", stride) for stride in far]
+        if crossed:
+            arrived, _ = lax.optimization_barrier((arrived, crossed[-1]))
+        crossed.append([gather(part) for part in arrived])
+    everything = jnp.concatenate(sent, axis=0)
+    everything, _ = lax.optimization_barrier((everything, crossed[0]))
+    home = results(gather(everything), everything.shape[0])
+    homes, start = [], 0
+    for piece in sent:
+        homes.append(home[start : start + piece.shape[0]])
+        start += piece.shape[0]
+    homes = lax.optimization_barrier(homes)
     total, arrived = None, []
-    for (offsets, _), value, away in zip(chunks, homes, crossed):
+    for chunk, value, away in zip(chunks, homes, crossed):
         for part in away:
-            other = results(part, size).astype(jnp.bfloat16)
+            other = results(part, value.shape[0]).astype(jnp.bfloat16)
             value = value + swap(other, "exp", far[0]).astype(jnp.float32)
-        value, arrived = lax.optimization_barrier((value, arrived))
-        for position, offset in enumerate(offsets):
+        if arrived:
+            value, _ = lax.optimization_barrier((value, arrived[0]))
+        for position, offset in enumerate(chunk):
             block = value[position * tokens : (position + 1) * tokens]
             if offset == 0:
                 total = block

time: 72.5 us -> 74.2 us (1.023)
  starting transfers between devices: 25.7 us -> 32.3 us
  waiting for transfers between devices: 29.8 us -> 23.9 us
    ppermute x18 -> x23, starting transfers between devices: 11.3 us -> 17.9 us  [swap(): lax.ppermute(value, axis, [(i, i ^ stride) for i in range(lax.axis_size(a...]
    ppermute x18 -> x23, waiting for transfers between devices: 27.3 us -> 21.4 us  [swap(): lax.ppermute(value, axis, [(i, i ^ stride) for i in range(lax.axis_size(a...]
    dot_general x3 -> x4, matrix products: 1.95 us -> 2.57 us  [expert_apply(): jnp.einsum('nd,dgh->gnh', rows[:, :width], gate_up[0], preferred_element_...]
    pallas_call x3 -> x4, Pallas kernels: 1.27 us -> 1.68 us  [expert_apply(): pl.pallas_call(down_kernel, out_shape=shapes, in_specs=whole_specs(3), ou...]
    unnamed x28 -> x29, local copies, waits for them, and re-layouts: 6.39 us -> 6.4 us
  transfers between devices with their start and end apart: 24 -> 29, of which waited for: 15 -> 14; matrix products, arithmetic and copies ran while one was open for 3% -> 4% of each run, Pallas kernels for 6% -> 6%
where the time goes in v6:
time: 74.2 us; the launch traced here: 74 us
  starting transfers between devices  32.3 us (44%)
  waiting for transfers between devices  23.9 us (32%)
  Pallas kernels  6.84 us (9%)
  local copies, waits for them, and re-layouts  6.53 us (9%)
  matrix products  2.57 us (3%)
  between operations  0.95 us (1%)
  other arithmetic  0.89 us (1%)
    ppermute x23, waiting for transfers between devices, swap(): lax.ppermute(value, axis, [(i, i ^ stride) for i in range(lax.axis_size(a...  21.4 us
    ppermute x23, starting transfers between devices, swap(): lax.ppermute(value, axis, [(i, i ^ stride) for i in range(lax.axis_size(a...  17.9 us
    ppermute x6, starting transfers between devices, shift(): lax.ppermute(value, axis, [(i, (i + step) % count) for i in range(count)])  14.4 us
    unnamed x29, local copies, waits for them, and re-layouts  6.4 us
    dot_general x4, matrix products, expert_apply(): jnp.einsum('nd,dgh->gnh', rows[:, :width], gate_up[0], preferred_element_...  2.57 us
    ppermute x6, waiting for transfers between devices, shift(): lax.ppermute(value, axis, [(i, (i + step) % count) for i in range(count)])  2.54 us
    pallas_call x1, Pallas kernels, attention(): pl.pallas_call(functools.partial(late_kernel, last[0], fresh_block), out_...  2.16 us
    pallas_call x4, Pallas kernels, expert_apply(): pl.pallas_call(down_kernel, out_shape=shapes, in_specs=whole_specs(3), ou...  1.68 us
  transfers between devices with their start and end apart: 29, of which 14 were waited for; matrix products, arithmetic and copies ran while one was open for 4% of the time, Pallas kernels for 6%

profile of v6, /device:TPU:0, one launch (start us, length us, event | category | flops | bytes accessed | tf_op | source)
XLA Modules:
  0.0 74.0 jit_solution(4254062377633723924)
XLA Ops:
  0.6 1.2 %copy.34 = bf16[1,576,2,128]{3,1,2,0:T(8,128)(2,1)S(1)} copy(bf16[1,576,2,128]{3,2,1,0:T(2,128)(2,1)} %param.11) | data formatting | bytes 589824 | tf_op args[1]
  1.8 5.1 %collective-permute-start.2 = (bf16[576,128]{1,0:T(8,128)(2,1)S(1)}, bf16[576,128]{1,0:T(8,128)(2,1)S(1)}, u32[]{:S(2)}, u32[]{:S(2)}) collective-permute-start(bf16[576,128]{1,0:T(8,128)(2,1)S(1)} %get-tuple-element.64.values), channel_id=1, source_target_pairs={{0,12},{4,0},{8,4},{12,8},{1,13},{5,1},{9,5},{13,9},{2,14},{6,2},{... | collective-permute-start | bytes 442376 | tf_op jit(solution)/shard_map/ppermute | solution.py:33
  6.9 3.9 %collective-permute-start.5 = (bf16[576,128]{1,0:T(8,128)(2,1)S(1)}, bf16[576,128]{1,0:T(8,128)(2,1)S(1)}, u32[]{:S(2)}, u32[]{:S(2)}) collective-permute-start(bf16[576,128]{1,0:T(8,128)(2,1)S(1)} %get-tuple-element.65.keys), channel_id=1, source_target_pairs={{0,12},{4,0},{8,4},{12,8},{1,13},{5,1},{9,5},{13,9},{2,14},{6,2},{... | collective-permute-start | bytes 442376 | tf_op jit(solution)/shard_map/ppermute | solution.py:33
  10.8 0.4 collective-permute-done.2.refs_3_
  11.2 4.3 %collective-permute-start.3 = (bf16[576,128]{1,0:T(8,128)(2,1)S(1)}, bf16[576,128]{1,0:T(8,128)(2,1)S(1)}, u32[]{:S(2)}, u32[]{:S(2)}) collective-permute-start(bf16[576,128]{1,0:T(8,128)(2,1)S(1)} %collective-permute-done.2.refs_3_), channel_id=1, source_target_pairs={{0,12},{4,0},{8,4},{12,8},{1,13},{5,1},{9,5},{13,9},{2,14},{6,2},{... | collective-permute-start | bytes 442376 | tf_op jit(solution)/shard_map/ppermute | solution.py:33
  15.7 1.2 %collective-permute-start.1 = (bf16[576,128]{1,0:T(8,128)(2,1)S(1)}, bf16[576,128]{1,0:T(8,128)(2,1)S(1)}, u32[]{:S(2)}, u32[]{:S(2)}) collective-permute-start(bf16[576,128]{1,0:T(8,128)(2,1)S(1)} %collective-permute-done.refs_0_), channel_id=1, source_target_pairs={{0,4},{4,8},{8,12},{12,0},{1,5},{5,9},{9,13},{13,1},{2,6},{6,10},{... | collective-permute-start | bytes 442376 | tf_op jit(solution)/shard_map/ppermute | solution.py:33
  16.8 1.4 %copy-done.1 = bf16[1,384,2048]{2,1,0:T(8,128)(2,1)S(1)} copy-done((bf16[1,384,2048]{2,1,0:T(8,128)(2,1)S(1)}, bf16[1,384,2048]{2,1,0:T(8,128)(2,1)}, u32[]{:S(2)}) %copy-start.1) | copy-done | bytes 1572888
  18.2 2.2 %copy-done.3 = bf16[1024,2048]{1,0:T(8,128)(2,1)S(1)} copy-done((bf16[1024,2048]{1,0:T(8,128)(2,1)S(1)}, bf16[1024,2048]{1,0:T(8,128)(2,1)}, u32[]{:S(2)}) %copy-start.3) | copy-done | bytes 4194328
  20.4 0.9 %copy-done.5 = bf16[1,64,1024]{2,1,0:T(8,128)(2,1)S(1)} copy-done((bf16[1,64,1024]{2,1,0:T(8,128)(2,1)S(1)}, bf16[1,64,1024]{2,1,0:T(8,128)(2,1)}, u32[]{:S(2)}) %copy-start.5) | copy-done | bytes 131096
  21.3 0.7 copy-done.11
  22.0 1.3 %shard_map.113 = (f32[1,512]{1,0:T(1,128)S(1)}, f32[1,512]{1,0:T(1,128)S(1)}, f32[128,512]{1,0:T(8,128)S(1)}, s32[4,128]{1,0:T(4,128)S(1)}) custom-call(s32[4]{0:T(128)S(1)} %bitcast.52, bf16[64,1024]{1,0:T(8,128)(2,1)S(1)} %bitcast.45, bf16[576,128]{1,0:T(8,128)(2,1)S(1)} %get-tuple-element.65.keys, bf16[576,128]{1,0:T(8,128)(2,1)S(1)} %get-tuple-element.64.values, ...), custom_call_target="tpu_custom_call" | custom-call | flops 2415919104 | bytes 8388608 | tf_op jit(solution)/shard_map/pallas_call | solution.py:206
  23.4 1.4 %shard_map.114 = (f32[1,512]{1,0:T(1,128)S(1)}, f32[1,512]{1,0:T(1,128)S(1)}, f32[128,512]{1,0:T(8,128)S(1)}) custom-call(bf16[64,1024]{1,0:T(8,128)(2,1)S(1)} %bitcast.46, s32[4,128]{1,0:T(4,128)S(1)} %get-tuple-element.32.lengths, bf16[576,128]{1,0:T(8,128)(2,1)S(1)} %collective-permute-done.refs_0_, bf16[576,128]{1,0:T(8,128)(2,1)S(1)} %collective-permute-done.4.refs_1_, ...), custom_call_target="tpu_custom_call" | custom-call | flops 301989888 | bytes 2097152 | tf_op jit(solution)/shard_map/pallas_call | solution.py:221
  24.8 1.9 %collective-permute-done.1.keys = bf16[576,128]{1,0:T(8,128)(2,1)S(1)} collective-permute-done((bf16[576,128]{1,0:T(8,128)(2,1)S(1)}, bf16[576,128]{1,0:T(8,128)(2,1)S(1)}, u32[]{:S(2)}, u32[]{:S(2)}) %collective-permute-start.1) | collective-permute-done | bytes 147488 | tf_op jit(solution)/shard_map/ppermute | solution.py:33
  26.8 2.2 %shard_map.115 = (bf16[64,1024]{1,0:T(8,128)(2,1)}, f32[16,2048]{1,0:T(8,128)S(1)}, bf16[16,2048]{1,0:T(8,128)(2,1)S(1)}, bf16[16,2048]{1,0:T(8,128)(2,1)S(1)}, bf16[16,2048]{1,0:T(8,128)(2,1)S(1)}) custom-call(bf16[64,1024]{1,0:T(8,128)(2,1)S(1)} %bitcast.47, bf16[576,128]{1,0:T(8,128)(2,1)S(1)} %collective-permute-done.1.keys, ...), custom_call_target="tpu_custom_call" | custom-call | flops 419430400 | bytes 6291456 | tf_op jit(solution)/shard_map/pallas_call | solution.py:232
  29.0 1.5 %collective-permute-start.7 = (bf16[16,2048]{1,0:T(8,128)(2,1)S(1)}, bf16[16,2048]{1,0:T(8,128)(2,1)S(1)}, u32[]{:S(2)}, u32[]{:S(2)}) collective-permute-start(bf16[16,2048]{1,0:T(8,128)(2,1)S(1)} %get-tuple-element.42), channel_id=1, source_target_pairs={{0,2},{1,3},{2,0},{3,1},{4,6},{5,7},{6,4},{7,5},{8,10},{9,11},{10,... | collective-permute-start | bytes 196616 | tf_op jit(solution)/shard_map/ppermute | solution.py:28
  30.4 0.4 collective-permute-start.8
  30.8 2.7 %collective-permute-done.7.refs_2_ = bf16[16,2048]{1,0:T(8,128)(2,1)S(1)} collective-permute-done((bf16[16,2048]{1,0:T(8,128)(2,1)S(1)}, bf16[16,2048]{1,0:T(8,128)(2,1)S(1)}, u32[]{:S(2)}, u32[]{:S(2)}) %collective-permute-start.7) | collective-permute-done | bytes 65568 | tf_op jit(solution)/shard_map/ppermute | solution.py:28
  33.5 1.1 %collective-permute-done.8.refs_3_ = bf16[16,2048]{1,0:T(8,128)(2,1)S(1)} collective-permute-done((bf16[16,2048]{1,0:T(8,128)(2,1)S(1)}, bf16[16,2048]{1,0:T(8,128)(2,1)S(1)}, u32[]{:S(2)}, u32[]{:S(2)}) %collective-permute-start.8) | collective-permute-done | bytes 65568 | tf_op jit(solution)/shard_map/ppermute | solution.py:28
  34.6 0.3 shard_map.116
  34.9 0.8 %collective-permute-start.9 = (bf16[16,2176]{1,0:T(8,128)(2,1)S(1)}, bf16[16,2176]{1,0:T(8,128)(2,1)S(1)}, u32[]{:S(2)}, u32[]{:S(2)}) collective-permute-start(bf16[16,2176]{1,0:T(8,128)(2,1)S(1)} %get-tuple-element.45), channel_id=1, source_target_pairs={{0,8},{4,12},{8,0},{12,4},{1,9},{5,13},{9,1},{13,5},{2,10},{6,14},... | collective-permute-start | bytes 208904 | tf_op jit(solution)/shard_map/ppermute | solution.py:28
  35.6 3.3 %collective-permute-start.11 = (bf16[16,2176]{1,0:T(8,128)(2,1)S(1)}, bf16[16,2176]{1,0:T(8,128)(2,1)S(1)}, u32[]{:S(2)}, u32[]{:S(2)}) collective-permute-start(bf16[16,2176]{1,0:T(8,128)(2,1)S(1)} %get-tuple-element.45), channel_id=1, source_target_pairs={{0,12},{4,8},{8,4},{12,0},{1,13},{5,9},{9,5},{13,1},{2,14},{6,10},... | collective-permute-start | bytes 208904 | tf_op jit(solution)/shard_map/ppermute | solution.py:28
  38.9 4.8 %collective-permute-done.9 = bf16[16,2176]{1,0:T(8,128)(2,1)S(1)} collective-permute-done((bf16[16,2176]{1,0:T(8,128)(2,1)S(1)}, bf16[16,2176]{1,0:T(8,128)(2,1)S(1)}, u32[]{:S(2)}, u32[]{:S(2)}) %collective-permute-start.9) | collective-permute-done | bytes 69664 | tf_op jit(solution)/shard_map/ppermute | solution.py:28
  43.8 1.5 %collective-permute-start.12 = (bf16[32,2176]{1,0:T(8,128)(2,1)S(1)}, bf16[32,2176]{1,0:T(8,128)(2,1)S(1)}, u32[]{:S(2)}, u32[]{:S(2)}) collective-permute-start(bf16[32,2176]{1,0:T(8,128)(2,1)S(1)} %pad_maximum_fusion.1), channel_id=1, source_target_pairs={{0,2},{1,3},{2,0},{3,1},{4,6},{5,7},{6,4},{7,5},{8,10},{9,11},{10,... | collective-permute-start | bytes 417800 | tf_op jit(solution)/shard_map/ppermute | solution.py:28
  45.3 0.6 collective-permute-start.24
  45.9 1.5 %collective-permute-start.19 = (bf16[16,2176]{1,0:T(8,128)(2,1)S(1)}, bf16[16,2176]{1,0:T(8,128)(2,1)S(1)}, u32[]{:S(2)}, u32[]{:S(2)}) collective-permute-start(bf16[16,2176]{1,0:T(8,128)(2,1)S(1)} %collective-permute-done.10), channel_id=1, source_target_pairs={{0,2},{1,3},{2,0},{3,1},{4,6},{5,7},{6,4},{7,5},{8,10},{9,11},{10,... | collective-permute-start | bytes 208904 | tf_op jit(solution)/shard_map/ppermute | solution.py:28
  47.4 1.5 %collective-permute-done.12 = bf16[32,2176]{1,0:T(8,128)(2,1)S(1)} collective-permute-done((bf16[32,2176]{1,0:T(8,128)(2,1)S(1)}, bf16[32,2176]{1,0:T(8,128)(2,1)S(1)}, u32[]{:S(2)}, u32[]{:S(2)}) %collective-permute-start.12) | collective-permute-done | bytes 139296 | tf_op jit(solution)/shard_map/ppermute | solution.py:28
  48.9 1.3 %collective-permute-done.13 = bf16[32,2176]{1,0:T(8,128)(2,1)S(1)} collective-permute-done((bf16[32,2176]{1,0:T(8,128)(2,1)S(1)}, bf16[32,2176]{1,0:T(8,128)(2,1)S(1)}, u32[]{:S(2)}, u32[]{:S(2)}) %collective-permute-start.13) | collective-permute-done | bytes 139296 | tf_op jit(solution)/shard_map/ppermute | solution.py:28
  50.5 0.4 collective-permute-start.14
  50.9 0.7 fusion.11.inner
  51.6 0.4 shard_map.118
  52.3 0.5 collective-permute-start.25
  52.7 0.6 fusion.14.inner
  53.4 0.4 shard_map.119
  54.0 1.5 %collective-permute-start.17 = (bf16[32,2048]{1,0:T(8,128)(2,1)S(1)}, bf16[32,2048]{1,0:T(8,128)(2,1)S(1)}, u32[]{:S(2)}, u32[]{:S(2)}) collective-permute-start(bf16[32,2048]{1,0:T(8,128)(2,1)S(1)} %add_convert_fusion), channel_id=1, source_target_pairs={{0,2},{1,3},{2,0},{3,1},{4,6},{5,7},{6,4},{7,5},{8,10},{9,11},{10,... | collective-permute-start | bytes 393224 | tf_op jit(solution)/shard_map/ppermute | solution.py:28
  55.5 1.1 %collective-permute-start.22 = (bf16[16,2048]{1,0:T(8,128)(2,1)S(1)}, bf16[16,2048]{1,0:T(8,128)(2,1)S(1)}, u32[]{:S(2)}, u32[]{:S(2)}) collective-permute-start(bf16[16,2048]{1,0:T(8,128)(2,1)S(1)} %add_convert_fusion.2), channel_id=1, source_target_pairs={{0,2},{1,3},{2,0},{3,1},{4,6},{5,7},{6,4},{7,5},{8,10},{9,11},{10,... | collective-permute-start | bytes 196616 | tf_op jit(solution)/shard_map/ppermute | solution.py:28
  56.7 0.6 fusion.17.inner
  57.3 0.4 shard_map.120
  57.8 0.6 fusion.8.inner
  58.5 0.5 shard_map.117
  58.9 0.5 collective-permute-start.15
  59.5 1.0 %collective-permute-start.27 = (bf16[16,2048]{1,0:T(8,128)(2,1)S(1)}, bf16[16,2048]{1,0:T(8,128)(2,1)S(1)}, u32[]{:S(2)}, u32[]{:S(2)}) collective-permute-start(bf16[16,2048]{1,0:T(8,128)(2,1)S(1)} %add_convert_fusion.1), channel_id=1, source_target_pairs={{0,2},{1,3},{2,0},{3,1},{4,6},{5,7},{6,4},{7,5},{8,10},{9,11},{10,... | collective-permute-start | bytes 196616 | tf_op jit(solution)/shard_map/ppermute | solution.py:28
  60.8 1.0 %collective-permute-start.18 = (bf16[16,2048]{1,0:T(8,128)(2,1)S(1)}, bf16[16,2048]{1,0:T(8,128)(2,1)S(1)}, u32[]{:S(2)}, u32[]{:S(2)}) collective-permute-start(bf16[16,2048]{1,0:T(8,128)(2,1)S(1)} %slice.78), channel_id=1, source_target_pairs={{0,8},{4,12},{8,0},{12,4},{1,9},{5,13},{9,1},{13,5},{2,10},{6,14},... | collective-permute-start | bytes 196616 | tf_op jit(solution)/shard_map/ppermute | solution.py:28
  61.8 2.0 %collective-permute-done.27 = bf16[16,2048]{1,0:T(8,128)(2,1)S(1)} collective-permute-done((bf16[16,2048]{1,0:T(8,128)(2,1)S(1)}, bf16[16,2048]{1,0:T(8,128)(2,1)S(1)}, u32[]{:S(2)}, u32[]{:S(2)}) %collective-permute-start.27) | collective-permute-done | bytes 65568 | tf_op jit(solution)/shard_map/ppermute | solution.py:28
  63.9 3.3 %collective-permute-done.18 = bf16[16,2048]{1,0:T(8,128)(2,1)S(1)} collective-permute-done((bf16[16,2048]{1,0:T(8,128)(2,1)S(1)}, bf16[16,2048]{1,0:T(8,128)(2,1)S(1)}, u32[]{:S(2)}, u32[]{:S(2)}) %collective-permute-start.18) | collective-permute-done | bytes 65568 | tf_op jit(solution)/shard_map/ppermute | solution.py:28
  67.2 1.8 %collective-permute-start.28 = (bf16[16,2048]{1,0:T(8,128)(2,1)S(1)}, bf16[16,2048]{1,0:T(8,128)(2,1)S(1)}, u32[]{:S(2)}, u32[]{:S(2)}) collective-permute-start(bf16[16,2048]{1,0:T(8,128)(2,1)S(1)} %get-tuple-element.61), channel_id=1, source_target_pairs={{0,12},{4,8},{8,4},{12,0},{1,13},{5,9},{9,5},{13,1},{2,14},{6,10},... | collective-permute-start | bytes 196616 | tf_op jit(solution)/shard_map/ppermute | solution.py:28
  69.0 2.4 %collective-permute-done.23 = bf16[16,2048]{1,0:T(8,128)(2,1)S(1)} collective-permute-done((bf16[16,2048]{1,0:T(8,128)(2,1)S(1)}, bf16[16,2048]{1,0:T(8,128)(2,1)S(1)}, u32[]{:S(2)}, u32[]{:S(2)}) %collective-permute-start.23) | collective-permute-done | bytes 65568 | tf_op jit(solution)/shard_map/ppermute | solution.py:28
  71.5 1.9 %collective-permute-done.28 = bf16[16,2048]{1,0:T(8,128)(2,1)S(1)} collective-permute-done((bf16[16,2048]{1,0:T(8,128)(2,1)S(1)}, bf16[16,2048]{1,0:T(8,128)(2,1)S(1)}, u32[]{:S(2)}, u32[]{:S(2)}) %collective-permute-start.28) | collective-permute-done | bytes 65568 | tf_op jit(solution)/shard_map/ppermute | solution.py:28
  73.3 0.7 fusion.24
  (68 shorter events, 1.4 us)
Async XLA Ops:
  0.6 50.3 %copy-start = (bf16[1,2048,2,384]{3,2,1,0:T(2,128)(2,1)S(1)}, bf16[1,2048,2,384]{3,2,1,0:T(2,128)(2,1)}, u32[]{:S(2)}) copy-start(bf16[1,2048,2,384]{3,2,1,0:T(2,128)(2,1)} %param.18) | copy-start | bytes 9437188
  1.8 9.4 %collective-permute-start.2 = (bf16[576,128]{1,0:T(8,128)(2,1)S(1)}, bf16[576,128]{1,0:T(8,128)(2,1)S(1)}, u32[]{:S(2)}, u32[]{:S(2)}) collective-permute-start(bf16[576,128]{1,0:T(8,128)(2,1)S(1)} %get-tuple-element.64.values), channel_id=1, source_target_pairs={{0,12},{4,0},{8,4},{12,8},{1,13},{5,1},{9,5},{13,9},{2,14},{6,2},{... | collective-permute-start | bytes 442376 | tf_op jit(solution)/shard_map/ppermute | solution.py:33
  6.9 8.7 %collective-permute-start = (bf16[576,128]{1,0:T(8,128)(2,1)S(1)}, bf16[576,128]{1,0:T(8,128)(2,1)S(1)}, u32[]{:S(2)}, u32[]{:S(2)}) collective-permute-start(bf16[576,128]{1,0:T(8,128)(2,1)S(1)} %get-tuple-element.65.keys), channel_id=1, source_target_pairs={{0,4},{4,8},{8,12},{12,0},{1,5},{5,9},{9,13},{13,1},{2,6},{6,10},{... | collective-permute-start | bytes 442376 | tf_op jit(solution)/shard_map/ppermute | solution.py:33
  6.9 16.4 %collective-permute-start.4 = (bf16[576,128]{1,0:T(8,128)(2,1)S(1)}, bf16[576,128]{1,0:T(8,128)(2,1)S(1)}, u32[]{:S(2)}, u32[]{:S(2)}) collective-permute-start(bf16[576,128]{1,0:T(8,128)(2,1)S(1)} %get-tuple-element.64.values), channel_id=1, source_target_pairs={{0,4},{4,8},{8,12},{12,0},{1,5},{5,9},{9,13},{13,1},{2,6},{6,10},{... | collective-permute-start | bytes 442376 | tf_op jit(solution)/shard_map/ppermute | solution.py:33
  6.9 16.4 %collective-permute-start.5 = (bf16[576,128]{1,0:T(8,128)(2,1)S(1)}, bf16[576,128]{1,0:T(8,128)(2,1)S(1)}, u32[]{:S(2)}, u32[]{:S(2)}) collective-permute-start(bf16[576,128]{1,0:T(8,128)(2,1)S(1)} %get-tuple-element.65.keys), channel_id=1, source_target_pairs={{0,12},{4,0},{8,4},{12,8},{1,13},{5,1},{9,5},{13,9},{2,14},{6,2},{... | collective-permute-start | bytes 442376 | tf_op jit(solution)/shard_map/ppermute | solution.py:33
  11.2 13.6 %collective-permute-start.3 = (bf16[576,128]{1,0:T(8,128)(2,1)S(1)}, bf16[576,128]{1,0:T(8,128)(2,1)S(1)}, u32[]{:S(2)}, u32[]{:S(2)}) collective-permute-start(bf16[576,128]{1,0:T(8,128)(2,1)S(1)} %collective-permute-done.2.refs_3_), channel_id=1, source_target_pairs={{0,12},{4,0},{8,4},{12,8},{1,13},{5,1},{9,5},{13,9},{2,14},{6,2},{... | collective-permute-start | bytes 442376 | tf_op jit(solution)/shard_map/ppermute | solution.py:33
  15.7 11.1 %collective-permute-start.1 = (bf16[576,128]{1,0:T(8,128)(2,1)S(1)}, bf16[576,128]{1,0:T(8,128)(2,1)S(1)}, u32[]{:S(2)}, u32[]{:S(2)}) collective-permute-start(bf16[576,128]{1,0:T(8,128)(2,1)S(1)} %collective-permute-done.refs_0_), channel_id=1, source_target_pairs={{0,4},{4,8},{8,12},{12,0},{1,5},{5,9},{9,13},{13,1},{2,6},{6,10},{... | collective-permute-start | bytes 442376 | tf_op jit(solution)/shard_map/ppermute | solution.py:33
  16.8 1.4 %copy-start.1 = (bf16[1,384,2048]{2,1,0:T(8,128)(2,1)S(1)}, bf16[1,384,2048]{2,1,0:T(8,128)(2,1)}, u32[]{:S(2)}) copy-start(bf16[1,384,2048]{2,1,0:T(8,128)(2,1)} %down.7) | copy-start | bytes 4718596
  18.2 2.2 %copy-start.3 = (bf16[1024,2048]{1,0:T(8,128)(2,1)S(1)}, bf16[1024,2048]{1,0:T(8,128)(2,1)}, u32[]{:S(2)}) copy-start(bf16[1024,2048]{1,0:T(8,128)(2,1)} %weight.1) | copy-start | bytes 12582916
  20.4 0.9 %copy-start.5 = (bf16[1,64,1024]{2,1,0:T(8,128)(2,1)S(1)}, bf16[1,64,1024]{2,1,0:T(8,128)(2,1)}, u32[]{:S(2)}) copy-start(bf16[1,64,1024]{2,1,0:T(8,128)(2,1)} %param.10) | copy-start | bytes 393220
  21.3 0.7 copy-start.11
  22.0 1.4 %copy-start.6 = (bf16[1,64,1024]{2,1,0:T(8,128)(2,1)S(1)}, bf16[1,64,1024]{2,1,0:T(8,128)(2,1)}, u32[]{:S(2)}) copy-start(bf16[1,64,1024]{2,1,0:T(8,128)(2,1)} %param.10) | copy-start | bytes 393220
  22.0 4.8 %copy-start.4 = (bf16[1024,2048]{1,0:T(8,128)(2,1)S(1)}, bf16[1024,2048]{1,0:T(8,128)(2,1)}, u32[]{:S(2)}) copy-start(bf16[1024,2048]{1,0:T(8,128)(2,1)} %weight.1) | copy-start | bytes 12582916
  23.3 11.3 %copy-start.7 = (bf16[1,16,2048]{2,1,0:T(8,128)(2,1)S(1)}, bf16[1,16,2048]{2,1,0:T(8,128)(2,1)}, u32[]{:S(2)}) copy-start(bf16[1,16,2048]{2,1,0:T(8,128)(2,1)} %param.13) | copy-start | bytes 196612
  23.3 11.3 %copy-start.8 = (f32[2048]{0:T(1024)S(1)}, f32[2048]{0:T(1024)}, u32[]{:S(2)}) copy-start(f32[2048]{0:T(1024)} %param.15) | copy-start | bytes 24580
  23.3 11.2 %copy-start.9 = (s32[1,16,8]{1,2,0:T(8,128)S(1)}, s32[1,16,8]{1,2,0:T(8,128)}, u32[]{:S(2)}) copy-start(s32[1,16,8]{1,2,0:T(8,128)} %param.16) | copy-start | bytes 1540
  23.3 11.2 %copy-start.10 = (f32[1,16,8]{1,2,0:T(8,128)S(1)}, f32[1,16,8]{1,2,0:T(8,128)}, u32[]{:S(2)}) copy-start(f32[1,16,8]{1,2,0:T(8,128)} %param.17) | copy-start | bytes 1540
  29.0 1.9 %collective-permute-start.6 = (bf16[16,2048]{1,0:T(8,128)(2,1)S(1)}, bf16[16,2048]{1,0:T(8,128)(2,1)S(1)}, u32[]{:S(2)}, u32[]{:S(2)}) collective-permute-start(bf16[16,2048]{1,0:T(8,128)(2,1)S(1)} %get-tuple-element.41), channel_id=1, source_target_pairs={{0,1},{1,0},{2,3},{3,2},{4,5},{5,4},{6,7},{7,6},{8,9},{9,8},{10,11... | collective-permute-start | bytes 196616 | tf_op jit(solution)/shard_map/ppermute | solution.py:28
  29.0 4.5 %collective-permute-start.7 = (bf16[16,2048]{1,0:T(8,128)(2,1)S(1)}, bf16[16,2048]{1,0:T(8,128)(2,1)S(1)}, u32[]{:S(2)}, u32[]{:S(2)}) collective-permute-start(bf16[16,2048]{1,0:T(8,128)(2,1)S(1)} %get-tuple-element.42), channel_id=1, source_target_pairs={{0,2},{1,3},{2,0},{3,1},{4,6},{5,7},{6,4},{7,5},{8,10},{9,11},{10,... | collective-permute-start | bytes 196616 | tf_op jit(solution)/shard_map/ppermute | solution.py:28
  30.4 4.1 %collective-permute-start.8 = (bf16[16,2048]{1,0:T(8,128)(2,1)S(1)}, bf16[16,2048]{1,0:T(8,128)(2,1)S(1)}, u32[]{:S(2)}, u32[]{:S(2)}) collective-permute-start(bf16[16,2048]{1,0:T(8,128)(2,1)S(1)} %get-tuple-element.43), channel_id=1, source_target_pairs={{0,3},{1,2},{2,1},{3,0},{4,7},{5,6},{6,5},{7,4},{8,11},{9,10},{10,... | collective-permute-start | bytes 196616 | tf_op jit(solution)/shard_map/ppermute | solution.py:28
  34.6 17.0 %copy-start.2 = (bf16[1,384,2048]{2,1,0:T(8,128)(2,1)S(1)}, bf16[1,384,2048]{2,1,0:T(8,128)(2,1)}, u32[]{:S(2)}) copy-start(bf16[1,384,2048]{2,1,0:T(8,128)(2,1)} %down.7) | copy-start | bytes 4718596
  34.9 8.9 %collective-permute-start.9 = (bf16[16,2176]{1,0:T(8,128)(2,1)S(1)}, bf16[16,2176]{1,0:T(8,128)(2,1)S(1)}, u32[]{:S(2)}, u32[]{:S(2)}) collective-permute-start(bf16[16,2176]{1,0:T(8,128)(2,1)S(1)} %get-tuple-element.45), channel_id=1, source_target_pairs={{0,8},{4,12},{8,0},{12,4},{1,9},{5,13},{9,1},{13,5},{2,10},{6,14},... | collective-permute-start | bytes 208904 | tf_op jit(solution)/shard_map/ppermute | solution.py:28
  35.6 9.7 %collective-permute-start.11 = (bf16[16,2176]{1,0:T(8,128)(2,1)S(1)}, bf16[16,2176]{1,0:T(8,128)(2,1)S(1)}, u32[]{:S(2)}, u32[]{:S(2)}) collective-permute-start(bf16[16,2176]{1,0:T(8,128)(2,1)S(1)} %get-tuple-element.45), channel_id=1, source_target_pairs={{0,12},{4,8},{8,4},{12,0},{1,13},{5,9},{9,5},{13,1},{2,14},{6,10},... | collective-permute-start | bytes 208904 | tf_op jit(solution)/shard_map/ppermute | solution.py:28
  38.9 7.0 %collective-permute-start.10 = (bf16[16,2176]{1,0:T(8,128)(2,1)S(1)}, bf16[16,2176]{1,0:T(8,128)(2,1)S(1)}, u32[]{:S(2)}, u32[]{:S(2)}) collective-permute-start(bf16[16,2176]{1,0:T(8,128)(2,1)S(1)} %get-tuple-element.45), channel_id=1, source_target_pairs={{0,4},{4,0},{8,12},{12,8},{1,5},{5,1},{9,13},{13,9},{2,6},{6,2},{1... | collective-permute-start | bytes 208904 | tf_op jit(solution)/shard_map/ppermute | solution.py:28
  43.8 5.1 %collective-permute-start.12 = (bf16[32,2176]{1,0:T(8,128)(2,1)S(1)}, bf16[32,2176]{1,0:T(8,128)(2,1)S(1)}, u32[]{:S(2)}, u32[]{:S(2)}) collective-permute-start(bf16[32,2176]{1,0:T(8,128)(2,1)S(1)} %pad_maximum_fusion.1), channel_id=1, source_target_pairs={{0,2},{1,3},{2,0},{3,1},{4,6},{5,7},{6,4},{7,5},{8,10},{9,11},{10,... | collective-permute-start | bytes 417800 | tf_op jit(solution)/shard_map/ppermute | solution.py:28
  45.3 6.9 %collective-permute-start.24 = (bf16[16,2176]{1,0:T(8,128)(2,1)S(1)}, bf16[16,2176]{1,0:T(8,128)(2,1)S(1)}, u32[]{:S(2)}, u32[]{:S(2)}) collective-permute-start(bf16[16,2176]{1,0:T(8,128)(2,1)S(1)} %collective-permute-done.11), channel_id=1, source_target_pairs={{0,2},{1,3},{2,0},{3,1},{4,6},{5,7},{6,4},{7,5},{8,10},{9,11},{10,... | collective-permute-start | bytes 208904 | tf_op jit(solution)/shard_map/ppermute | solution.py:28
  45.9 4.5 %collective-permute-start.19 = (bf16[16,2176]{1,0:T(8,128)(2,1)S(1)}, bf16[16,2176]{1,0:T(8,128)(2,1)S(1)}, u32[]{:S(2)}, u32[]{:S(2)}) collective-permute-start(bf16[16,2176]{1,0:T(8,128)(2,1)S(1)} %collective-permute-done.10), channel_id=1, source_target_pairs={{0,2},{1,3},{2,0},{3,1},{4,6},{5,7},{6,4},{7,5},{8,10},{9,11},{10,... | collective-permute-start | bytes 208904 | tf_op jit(solution)/shard_map/ppermute | solution.py:28
  48.9 1.4 %collective-permute-start.13 = (bf16[32,2176]{1,0:T(8,128)(2,1)S(1)}, bf16[32,2176]{1,0:T(8,128)(2,1)S(1)}, u32[]{:S(2)}, u32[]{:S(2)}) collective-permute-start(bf16[32,2176]{1,0:T(8,128)(2,1)S(1)} %collective-permute-done.12), channel_id=1, source_target_pairs={{0,1},{1,0},{2,3},{3,2},{4,5},{5,4},{6,7},{7,6},{8,9},{9,8},{10,11... | collective-permute-start | bytes 417800 | tf_op jit(solution)/shard_map/ppermute | solution.py:28
  50.4 1.8 %collective-permute-start.20 = (bf16[16,2176]{1,0:T(8,128)(2,1)S(1)}, bf16[16,2176]{1,0:T(8,128)(2,1)S(1)}, u32[]{:S(2)}, u32[]{:S(2)}) collective-permute-start(bf16[16,2176]{1,0:T(8,128)(2,1)S(1)} %collective-permute-done.19), channel_id=1, source_target_pairs={{0,1},{1,0},{2,3},{3,2},{4,5},{5,4},{6,7},{7,6},{8,9},{9,8},{10,11... | collective-permute-start | bytes 208904 | tf_op jit(solution)/shard_map/ppermute | solution.py:28
  50.5 7.3 %collective-permute-start.14 = (bf16[64,2176]{1,0:T(8,128)(2,1)S(1)}, bf16[64,2176]{1,0:T(8,128)(2,1)S(1)}, u32[]{:S(2)}, u32[]{:S(2)}) collective-permute-start(bf16[64,2176]{1,0:T(8,128)(2,1)S(1)} %pad_maximum_fusion), channel_id=1, source_target_pairs={{0,1},{1,0},{2,3},{3,2},{4,5},{5,4},{6,7},{7,6},{8,9},{9,8},{10,11... | collective-permute-start | bytes 835592 | tf_op jit(solution)/shard_map/ppermute | solution.py:28
  52.1 1.9 %collective-permute-start.16 = (bf16[32,2048]{1,0:T(8,128)(2,1)S(1)}, bf16[32,2048]{1,0:T(8,128)(2,1)S(1)}, u32[]{:S(2)}, u32[]{:S(2)}) collective-permute-start(bf16[32,2048]{1,0:T(8,128)(2,1)S(1)} %get-tuple-element.51), channel_id=1, source_target_pairs={{0,1},{1,0},{2,3},{3,2},{4,5},{5,4},{6,7},{7,6},{8,9},{9,8},{10,11... | collective-permute-start | bytes 393224 | tf_op jit(solution)/shard_map/ppermute | solution.py:28
  52.3 4.4 %collective-permute-start.25 = (bf16[16,2176]{1,0:T(8,128)(2,1)S(1)}, bf16[16,2176]{1,0:T(8,128)(2,1)S(1)}, u32[]{:S(2)}, u32[]{:S(2)}) collective-permute-start(bf16[16,2176]{1,0:T(8,128)(2,1)S(1)} %collective-permute-done.24), channel_id=1, source_target_pairs={{0,1},{1,0},{2,3},{3,2},{4,5},{5,4},{6,7},{7,6},{8,9},{9,8},{10,11... | collective-permute-start | bytes 208904 | tf_op jit(solution)/shard_map/ppermute | solution.py:28
  53.8 1.7 %collective-permute-start.21 = (bf16[16,2048]{1,0:T(8,128)(2,1)S(1)}, bf16[16,2048]{1,0:T(8,128)(2,1)S(1)}, u32[]{:S(2)}, u32[]{:S(2)}) collective-permute-start(bf16[16,2048]{1,0:T(8,128)(2,1)S(1)} %get-tuple-element.55), channel_id=1, source_target_pairs={{0,1},{1,0},{2,3},{3,2},{4,5},{5,4},{6,7},{7,6},{8,9},{9,8},{10,11... | collective-permute-start | bytes 196616 | tf_op jit(solution)/shard_map/ppermute | solution.py:28
  54.0 6.8 %collective-permute-start.17 = (bf16[32,2048]{1,0:T(8,128)(2,1)S(1)}, bf16[32,2048]{1,0:T(8,128)(2,1)S(1)}, u32[]{:S(2)}, u32[]{:S(2)}) collective-permute-start(bf16[32,2048]{1,0:T(8,128)(2,1)S(1)} %add_convert_fusion), channel_id=1, source_target_pairs={{0,2},{1,3},{2,0},{3,1},{4,6},{5,7},{6,4},{7,5},{8,10},{9,11},{10,... | collective-permute-start | bytes 393224 | tf_op jit(solution)/shard_map/ppermute | solution.py:28
  55.5 6.3 %collective-permute-start.22 = (bf16[16,2048]{1,0:T(8,128)(2,1)S(1)}, bf16[16,2048]{1,0:T(8,128)(2,1)S(1)}, u32[]{:S(2)}, u32[]{:S(2)}) collective-permute-start(bf16[16,2048]{1,0:T(8,128)(2,1)S(1)} %add_convert_fusion.2), channel_id=1, source_target_pairs={{0,2},{1,3},{2,0},{3,1},{4,6},{5,7},{6,4},{7,5},{8,10},{9,11},{10,... | collective-permute-start | bytes 196616 | tf_op jit(solution)/shard_map/ppermute | solution.py:28
  57.7 1.8 %collective-permute-start.26 = (bf16[16,2048]{1,0:T(8,128)(2,1)S(1)}, bf16[16,2048]{1,0:T(8,128)(2,1)S(1)}, u32[]{:S(2)}, u32[]{:S(2)}) collective-permute-start(bf16[16,2048]{1,0:T(8,128)(2,1)S(1)} %get-tuple-element.60), channel_id=1, source_target_pairs={{0,1},{1,0},{2,3},{3,2},{4,5},{5,4},{6,7},{7,6},{8,9},{9,8},{10,11... | collective-permute-start | bytes 196616 | tf_op jit(solution)/shard_map/ppermute | solution.py:28
  58.9 1.7 %collective-permute-start.15 = (bf16[64,2048]{1,0:T(8,128)(2,1)S(1)}, bf16[64,2048]{1,0:T(8,128)(2,1)S(1)}, u32[]{:S(2)}, u32[]{:S(2)}) collective-permute-start(bf16[64,2048]{1,0:T(8,128)(2,1)S(1)} %get-tuple-element.48), channel_id=1, source_target_pairs={{0,1},{1,0},{2,3},{3,2},{4,5},{5,4},{6,7},{7,6},{8,9},{9,8},{10,11... | collective-permute-start | bytes 786440 | tf_op jit(solution)/shard_map/ppermute | solution.py:28
  59.5 4.3 %collective-permute-start.27 = (bf16[16,2048]{1,0:T(8,128)(2,1)S(1)}, bf16[16,2048]{1,0:T(8,128)(2,1)S(1)}, u32[]{:S(2)}, u32[]{:S(2)}) collective-permute-start(bf16[16,2048]{1,0:T(8,128)(2,1)S(1)} %add_convert_fusion.1), channel_id=1, source_target_pairs={{0,2},{1,3},{2,0},{3,1},{4,6},{5,7},{6,4},{7,5},{8,10},{9,11},{10,... | collective-permute-start | bytes 196616 | tf_op jit(solution)/shard_map/ppermute | solution.py:28
  60.8 6.4 %collective-permute-start.18 = (bf16[16,2048]{1,0:T(8,128)(2,1)S(1)}, bf16[16,2048]{1,0:T(8,128)(2,1)S(1)}, u32[]{:S(2)}, u32[]{:S(2)}) collective-permute-start(bf16[16,2048]{1,0:T(8,128)(2,1)S(1)} %slice.78), channel_id=1, source_target_pairs={{0,8},{4,12},{8,0},{12,4},{1,9},{5,13},{9,1},{13,5},{2,10},{6,14},... | collective-permute-start | bytes 196616 | tf_op jit(solution)/shard_map/ppermute | solution.py:28
  67.2 4.3 %collective-permute-start.23 = (bf16[16,2048]{1,0:T(8,128)(2,1)S(1)}, bf16[16,2048]{1,0:T(8,128)(2,1)S(1)}, u32[]{:S(2)}, u32[]{:S(2)}) collective-permute-start(bf16[16,2048]{1,0:T(8,128)(2,1)S(1)} %get-tuple-element.56), channel_id=1, source_target_pairs={{0,4},{4,0},{8,12},{12,8},{1,5},{5,1},{9,13},{13,9},{2,6},{6,2},{1... | collective-permute-start | bytes 196616 | tf_op jit(solution)/shard_map/ppermute | solution.py:28
  67.2 6.1 %collective-permute-start.28 = (bf16[16,2048]{1,0:T(8,128)(2,1)S(1)}, bf16[16,2048]{1,0:T(8,128)(2,1)S(1)}, u32[]{:S(2)}, u32[]{:S(2)}) collective-permute-start(bf16[16,2048]{1,0:T(8,128)(2,1)S(1)} %get-tuple-element.61), channel_id=1, source_target_pairs={{0,12},{4,8},{8,4},{12,0},{1,13},{5,9},{9,5},{13,1},{2,14},{6,10},... | collective-permute-start | bytes 196616 | tf_op jit(solution)/shard_map/ppermute | solution.py:28

commit v7 on v6

--- a/solution.py
+++ b/solution.py
@@ -336,7 +336,7 @@
 
 
 def chunks_of(count):
-    chunks = [range(0, count, 2), range(1, count, 4), range(3, count, 4)]
+    chunks = [range((count + 1) // 2), range((count + 1) // 2, count)]
     return [list(chunk) for chunk in chunks if len(chunk)]
 
 
@@ -361,9 +361,9 @@
         sent.append(jnp.concatenate(blocks, axis=0))
     crossed = []
     for piece in sent:
+        if crossed:
+            piece, _ = lax.optimization_barrier((piece, arrived))
         arrived = [swap(piece, "exp", stride) for stride in far]
-        if crossed:
-            arrived, _ = lax.optimization_barrier((arrived, crossed[-1]))
         crossed.append([gather(part) for part in arrived])
     everything = jnp.concatenate(sent, axis=0)
     everything, _ = lax.optimization_barrier((everything, crossed[0]))

time: 74.2 us -> 69.5 us (0.937)
  waiting for transfers between devices: 23.9 us -> 20.7 us
    ppermute x23 -> x19, waiting for transfers between devices: 21.4 us -> 18.2 us  [swap(): lax.ppermute(value, axis, [(i, i ^ stride) for i in range(lax.axis_size(a...]
    dot_general x4 -> x3, matrix products: 2.57 us -> 1.95 us  [expert_apply(): jnp.einsum('nd,dgh->gnh', rows[:, :width], gate_up[0], preferred_element_...]
    ppermute x23 -> x19, starting transfers between devices: 17.9 us -> 17.4 us  [swap(): lax.ppermute(value, axis, [(i, i ^ stride) for i in range(lax.axis_size(a...]
    pallas_call x4 -> x3, Pallas kernels: 1.68 us -> 1.26 us  [expert_apply(): pl.pallas_call(down_kernel, out_shape=shapes, in_specs=whole_specs(3), ou...]
    unnamed x29 -> x28, local copies, waits for them, and re-layouts: 6.4 us -> 6.4 us
  transfers between devices with their start and end apart: 29 -> 25, of which waited for: 14 -> 15; matrix products, arithmetic and copies ran while one was open for 4% -> 3% of each run, Pallas kernels for 6% -> 6%
where the time goes in v7:
time: 69.5 us; the launch traced here: 69.3 us
  starting transfers between devices  31.8 us (46%)
  waiting for transfers between devices  20.7 us (30%)
  local copies, waits for them, and re-layouts  6.53 us (9%)
  Pallas kernels  6.42 us (9%)
  matrix products  1.95 us (3%)
  between operations  0.92 us (1%)
  other arithmetic  0.91 us (1%)
    ppermute x19, waiting for transfers between devices, swap(): lax.ppermute(value, axis, [(i, i ^ stride) for i in range(lax.axis_size(a...  18.2 us
    ppermute x19, starting transfers between devices, swap(): lax.ppermute(value, axis, [(i, i ^ stride) for i in range(lax.axis_size(a...  17.4 us
    ppermute x6, starting transfers between devices, shift(): lax.ppermute(value, axis, [(i, (i + step) % count) for i in range(count)])  14.4 us
    unnamed x28, local copies, waits for them, and re-layouts  6.4 us
    ppermute x6, waiting for transfers between devices, shift(): lax.ppermute(value, axis, [(i, (i + step) % count) for i in range(count)])  2.54 us
    pallas_call x1, Pallas kernels, attention(): pl.pallas_call(functools.partial(late_kernel, last[0], fresh_block), out_...  2.16 us
    dot_general x3, matrix products, expert_apply(): jnp.einsum('nd,dgh->gnh', rows[:, :width], gate_up[0], preferred_element_...  1.95 us
    pallas_call x1, Pallas kernels, attention(): pl.pallas_call(functools.partial(middle_kernel, [offset for offset, _, _...  1.43 us
  transfers between devices with their start and end apart: 25, of which 15 were waited for; matrix products, arithmetic and copies ran while one was open for 3% of the time, Pallas kernels for 6%

profile of v7, /device:TPU:0, one launch (start us, length us, event | category | flops | bytes accessed | tf_op | source)
XLA Modules:
  0.0 69.3 jit_solution(18217837036683562633)
XLA Ops:
  0.6 1.2 %copy.29 = bf16[1,576,2,128]{3,1,2,0:T(8,128)(2,1)S(1)} copy(bf16[1,576,2,128]{3,2,1,0:T(2,128)(2,1)} %param.11) | data formatting | bytes 589824 | tf_op args[1]
  1.8 5.1 %collective-permute-start.2 = (bf16[576,128]{1,0:T(8,128)(2,1)S(1)}, bf16[576,128]{1,0:T(8,128)(2,1)S(1)}, u32[]{:S(2)}, u32[]{:S(2)}) collective-permute-start(bf16[576,128]{1,0:T(8,128)(2,1)S(1)} %get-tuple-element.54.values), channel_id=1, source_target_pairs={{0,12},{4,0},{8,4},{12,8},{1,13},{5,1},{9,5},{13,9},{2,14},{6,2},{... | collective-permute-start | bytes 442376 | tf_op jit(solution)/shard_map/ppermute | solution.py:33
  6.9 3.9 %collective-permute-start.5 = (bf16[576,128]{1,0:T(8,128)(2,1)S(1)}, bf16[576,128]{1,0:T(8,128)(2,1)S(1)}, u32[]{:S(2)}, u32[]{:S(2)}) collective-permute-start(bf16[576,128]{1,0:T(8,128)(2,1)S(1)} %get-tuple-element.55.keys), channel_id=1, source_target_pairs={{0,12},{4,0},{8,4},{12,8},{1,13},{5,1},{9,5},{13,9},{2,14},{6,2},{... | collective-permute-start | bytes 442376 | tf_op jit(solution)/shard_map/ppermute | solution.py:33
  10.8 0.4 collective-permute-done.2.refs_3_
  11.2 4.3 %collective-permute-start.3 = (bf16[576,128]{1,0:T(8,128)(2,1)S(1)}, bf16[576,128]{1,0:T(8,128)(2,1)S(1)}, u32[]{:S(2)}, u32[]{:S(2)}) collective-permute-start(bf16[576,128]{1,0:T(8,128)(2,1)S(1)} %collective-permute-done.2.refs_3_), channel_id=1, source_target_pairs={{0,12},{4,0},{8,4},{12,8},{1,13},{5,1},{9,5},{13,9},{2,14},{6,2},{... | collective-permute-start | bytes 442376 | tf_op jit(solution)/shard_map/ppermute | solution.py:33
  15.7 1.2 %collective-permute-start.1 = (bf16[576,128]{1,0:T(8,128)(2,1)S(1)}, bf16[576,128]{1,0:T(8,128)(2,1)S(1)}, u32[]{:S(2)}, u32[]{:S(2)}) collective-permute-start(bf16[576,128]{1,0:T(8,128)(2,1)S(1)} %collective-permute-done.refs_0_), channel_id=1, source_target_pairs={{0,4},{4,8},{8,12},{12,0},{1,5},{5,9},{9,13},{13,1},{2,6},{6,10},{... | collective-permute-start | bytes 442376 | tf_op jit(solution)/shard_map/ppermute | solution.py:33
  16.8 1.4 %copy-done.1 = bf16[1,384,2048]{2,1,0:T(8,128)(2,1)S(1)} copy-done((bf16[1,384,2048]{2,1,0:T(8,128)(2,1)S(1)}, bf16[1,384,2048]{2,1,0:T(8,128)(2,1)}, u32[]{:S(2)}) %copy-start.1) | copy-done | bytes 1572888
  18.2 2.2 %copy-done.3 = bf16[1024,2048]{1,0:T(8,128)(2,1)S(1)} copy-done((bf16[1024,2048]{1,0:T(8,128)(2,1)S(1)}, bf16[1024,2048]{1,0:T(8,128)(2,1)}, u32[]{:S(2)}) %copy-start.3) | copy-done | bytes 4194328
  20.4 0.9 %copy-done.5 = bf16[1,64,1024]{2,1,0:T(8,128)(2,1)S(1)} copy-done((bf16[1,64,1024]{2,1,0:T(8,128)(2,1)S(1)}, bf16[1,64,1024]{2,1,0:T(8,128)(2,1)}, u32[]{:S(2)}) %copy-start.5) | copy-done | bytes 131096
  21.3 0.7 copy-done.11
  22.0 1.3 %shard_map.113 = (f32[1,512]{1,0:T(1,128)S(1)}, f32[1,512]{1,0:T(1,128)S(1)}, f32[128,512]{1,0:T(8,128)S(1)}, s32[4,128]{1,0:T(4,128)S(1)}) custom-call(s32[4]{0:T(128)S(1)} %bitcast.46, bf16[64,1024]{1,0:T(8,128)(2,1)S(1)} %bitcast.39, bf16[576,128]{1,0:T(8,128)(2,1)S(1)} %get-tuple-element.55.keys, bf16[576,128]{1,0:T(8,128)(2,1)S(1)} %get-tuple-element.54.values, ...), custom_call_target="tpu_custom_call" | custom-call | flops 2415919104 | bytes 8388608 | tf_op jit(solution)/shard_map/pallas_call | solution.py:206
  23.4 1.4 %shard_map.114 = (f32[1,512]{1,0:T(1,128)S(1)}, f32[1,512]{1,0:T(1,128)S(1)}, f32[128,512]{1,0:T(8,128)S(1)}) custom-call(bf16[64,1024]{1,0:T(8,128)(2,1)S(1)} %bitcast.40, s32[4,128]{1,0:T(4,128)S(1)} %get-tuple-element.27.lengths, bf16[576,128]{1,0:T(8,128)(2,1)S(1)} %collective-permute-done.refs_0_, bf16[576,128]{1,0:T(8,128)(2,1)S(1)} %collective-permute-done.4.refs_1_, ...), custom_call_target="tpu_custom_call" | custom-call | flops 301989888 | bytes 2097152 | tf_op jit(solution)/shard_map/pallas_call | solution.py:221
  24.8 1.9 %collective-permute-done.1.keys = bf16[576,128]{1,0:T(8,128)(2,1)S(1)} collective-permute-done((bf16[576,128]{1,0:T(8,128)(2,1)S(1)}, bf16[576,128]{1,0:T(8,128)(2,1)S(1)}, u32[]{:S(2)}, u32[]{:S(2)}) %collective-permute-start.1) | collective-permute-done | bytes 147488 | tf_op jit(solution)/shard_map/ppermute | solution.py:33
  26.8 2.2 %shard_map.115 = (bf16[64,1024]{1,0:T(8,128)(2,1)}, f32[16,2048]{1,0:T(8,128)S(1)}, bf16[16,2048]{1,0:T(8,128)(2,1)S(1)}, bf16[16,2048]{1,0:T(8,128)(2,1)S(1)}, bf16[16,2048]{1,0:T(8,128)(2,1)S(1)}) custom-call(bf16[64,1024]{1,0:T(8,128)(2,1)S(1)} %bitcast.41, bf16[576,128]{1,0:T(8,128)(2,1)S(1)} %collective-permute-done.1.keys, ...), custom_call_target="tpu_custom_call" | custom-call | flops 419430400 | bytes 6291456 | tf_op jit(solution)/shard_map/pallas_call | solution.py:232
  29.0 1.5 %collective-permute-start.7 = (bf16[16,2048]{1,0:T(8,128)(2,1)S(1)}, bf16[16,2048]{1,0:T(8,128)(2,1)S(1)}, u32[]{:S(2)}, u32[]{:S(2)}) collective-permute-start(bf16[16,2048]{1,0:T(8,128)(2,1)S(1)} %get-tuple-element.37), channel_id=1, source_target_pairs={{0,2},{1,3},{2,0},{3,1},{4,6},{5,7},{6,4},{7,5},{8,10},{9,11},{10,... | collective-permute-start | bytes 196616 | tf_op jit(solution)/shard_map/ppermute | solution.py:28
  30.4 0.4 collective-permute-start.8
  30.8 2.7 %collective-permute-done.7.refs_2_ = bf16[16,2048]{1,0:T(8,128)(2,1)S(1)} collective-permute-done((bf16[16,2048]{1,0:T(8,128)(2,1)S(1)}, bf16[16,2048]{1,0:T(8,128)(2,1)S(1)}, u32[]{:S(2)}, u32[]{:S(2)}) %collective-permute-start.7) | collective-permute-done | bytes 65568 | tf_op jit(solution)/shard_map/ppermute | solution.py:28
  33.5 1.1 %collective-permute-done.8.refs_3_ = bf16[16,2048]{1,0:T(8,128)(2,1)S(1)} collective-permute-done((bf16[16,2048]{1,0:T(8,128)(2,1)S(1)}, bf16[16,2048]{1,0:T(8,128)(2,1)S(1)}, u32[]{:S(2)}, u32[]{:S(2)}) %collective-permute-start.8) | collective-permute-done | bytes 65568 | tf_op jit(solution)/shard_map/ppermute | solution.py:28
  34.9 1.7 %collective-permute-start.9 = (bf16[16,2176]{1,0:T(8,128)(2,1)S(1)}, bf16[16,2176]{1,0:T(8,128)(2,1)S(1)}, u32[]{:S(2)}, u32[]{:S(2)}) collective-permute-start(bf16[16,2176]{1,0:T(8,128)(2,1)S(1)} %get-tuple-element.40), channel_id=1, source_target_pairs={{0,4},{4,0},{8,12},{12,8},{1,5},{5,1},{9,13},{13,9},{2,6},{6,2},{1... | collective-permute-start | bytes 208904 | tf_op jit(solution)/shard_map/ppermute | solution.py:28
  36.6 0.5 collective-permute-start.11
  37.1 1.3 %collective-permute-start.10 = (bf16[16,2176]{1,0:T(8,128)(2,1)S(1)}, bf16[16,2176]{1,0:T(8,128)(2,1)S(1)}, u32[]{:S(2)}, u32[]{:S(2)}) collective-permute-start(bf16[16,2176]{1,0:T(8,128)(2,1)S(1)} %get-tuple-element.40), channel_id=1, source_target_pairs={{0,8},{4,12},{8,0},{12,4},{1,9},{5,13},{9,1},{13,5},{2,10},{6,14},... | collective-permute-start | bytes 208904 | tf_op jit(solution)/shard_map/ppermute | solution.py:28
  38.4 0.8 %collective-permute-done.9 = bf16[16,2176]{1,0:T(8,128)(2,1)S(1)} collective-permute-done((bf16[16,2176]{1,0:T(8,128)(2,1)S(1)}, bf16[16,2176]{1,0:T(8,128)(2,1)S(1)}, u32[]{:S(2)}, u32[]{:S(2)}) %collective-permute-start.9) | collective-permute-done | bytes 69664 | tf_op jit(solution)/shard_map/ppermute | solution.py:28
  39.2 1.5 %collective-permute-start.12 = (bf16[32,2176]{1,0:T(8,128)(2,1)S(1)}, bf16[32,2176]{1,0:T(8,128)(2,1)S(1)}, u32[]{:S(2)}, u32[]{:S(2)}) collective-permute-start(bf16[32,2176]{1,0:T(8,128)(2,1)S(1)} %pad_maximum_fusion.1), channel_id=1, source_target_pairs={{0,2},{1,3},{2,0},{3,1},{4,6},{5,7},{6,4},{7,5},{8,10},{9,11},{10,... | collective-permute-start | bytes 417800 | tf_op jit(solution)/shard_map/ppermute | solution.py:28
  40.7 2.4 %collective-permute-done.11 = bf16[16,2176]{1,0:T(8,128)(2,1)S(1)} collective-permute-done((bf16[16,2176]{1,0:T(8,128)(2,1)S(1)}, bf16[16,2176]{1,0:T(8,128)(2,1)S(1)}, u32[]{:S(2)}, u32[]{:S(2)}) %collective-permute-start.11) | collective-permute-done | bytes 69664 | tf_op jit(solution)/shard_map/ppermute | solution.py:28
  43.1 2.1 %collective-permute-done.10 = bf16[16,2176]{1,0:T(8,128)(2,1)S(1)} collective-permute-done((bf16[16,2176]{1,0:T(8,128)(2,1)S(1)}, bf16[16,2176]{1,0:T(8,128)(2,1)S(1)}, u32[]{:S(2)}, u32[]{:S(2)}) %collective-permute-start.10) | collective-permute-done | bytes 69664 | tf_op jit(solution)/shard_map/ppermute | solution.py:28
  45.2 1.5 %collective-permute-start.19 = (bf16[32,2176]{1,0:T(8,128)(2,1)S(1)}, bf16[32,2176]{1,0:T(8,128)(2,1)S(1)}, u32[]{:S(2)}, u32[]{:S(2)}) collective-permute-start(bf16[32,2176]{1,0:T(8,128)(2,1)S(1)} %pad_maximum_fusion.2), channel_id=1, source_target_pairs={{0,2},{1,3},{2,0},{3,1},{4,6},{5,7},{6,4},{7,5},{8,10},{9,11},{10,... | collective-permute-start | bytes 417800 | tf_op jit(solution)/shard_map/ppermute | solution.py:28
  46.7 1.3 %collective-permute-done.13 = bf16[32,2176]{1,0:T(8,128)(2,1)S(1)} collective-permute-done((bf16[32,2176]{1,0:T(8,128)(2,1)S(1)}, bf16[32,2176]{1,0:T(8,128)(2,1)S(1)}, u32[]{:S(2)}, u32[]{:S(2)}) %collective-permute-start.13) | collective-permute-done | bytes 139296 | tf_op jit(solution)/shard_map/ppermute | solution.py:28
  48.3 0.7 fusion.9.inner
  49.0 0.4 shard_map.118
  49.4 0.4 collective-permute-start.16
  49.8 0.6 collective-permute-done.19
  50.4 0.4 collective-permute-done.16
  50.9 1.2 %collective-permute-start.17 = (bf16[32,2048]{1,0:T(8,128)(2,1)S(1)}, bf16[32,2048]{1,0:T(8,128)(2,1)S(1)}, u32[]{:S(2)}, u32[]{:S(2)}) collective-permute-start(bf16[32,2048]{1,0:T(8,128)(2,1)S(1)} %add_convert_fusion.1), channel_id=1, source_target_pairs={{0,2},{1,3},{2,0},{3,1},{4,6},{5,7},{6,4},{7,5},{8,10},{9,11},{10,... | collective-permute-start | bytes 393224 | tf_op jit(solution)/shard_map/ppermute | solution.py:28
  52.1 0.7 fusion.12.inner
  52.7 0.4 shard_map.119
  53.1 0.3 collective-permute-start.21
  53.5 0.6 fusion.6.inner
  54.1 0.5 shard_map.117
  54.6 0.3 collective-permute-start.15
  54.9 1.3 %collective-permute-start.22 = (bf16[32,2048]{1,0:T(8,128)(2,1)S(1)}, bf16[32,2048]{1,0:T(8,128)(2,1)S(1)}, u32[]{:S(2)}, u32[]{:S(2)}) collective-permute-start(bf16[32,2048]{1,0:T(8,128)(2,1)S(1)} %add_convert_fusion), channel_id=1, source_target_pairs={{0,2},{1,3},{2,0},{3,1},{4,6},{5,7},{6,4},{7,5},{8,10},{9,11},{10,... | collective-permute-start | bytes 393224 | tf_op jit(solution)/shard_map/ppermute | solution.py:28
  56.3 0.4 collective-permute-done.17
  56.7 1.5 %collective-permute-start.18 = (bf16[16,2048]{1,0:T(8,128)(2,1)S(1)}, bf16[16,2048]{1,0:T(8,128)(2,1)S(1)}, u32[]{:S(2)}, u32[]{:S(2)}) collective-permute-start(bf16[16,2048]{1,0:T(8,128)(2,1)S(1)} %slice.78), channel_id=1, source_target_pairs={{0,4},{4,0},{8,12},{12,8},{1,5},{5,1},{9,13},{13,9},{2,6},{6,2},{1... | collective-permute-start | bytes 196616 | tf_op jit(solution)/shard_map/ppermute | solution.py:28
  58.2 2.4 %collective-permute-done.22 = bf16[32,2048]{1,0:T(8,128)(2,1)S(1)} collective-permute-done((bf16[32,2048]{1,0:T(8,128)(2,1)S(1)}, bf16[32,2048]{1,0:T(8,128)(2,1)S(1)}, u32[]{:S(2)}, u32[]{:S(2)}) %collective-permute-start.22) | collective-permute-done | bytes 131104 | tf_op jit(solution)/shard_map/ppermute | solution.py:28
  60.7 0.4 collective-permute-done.18
  61.1 0.9 %collective-permute-start.23 = (bf16[16,2048]{1,0:T(8,128)(2,1)S(1)}, bf16[16,2048]{1,0:T(8,128)(2,1)S(1)}, u32[]{:S(2)}, u32[]{:S(2)}) collective-permute-start(bf16[16,2048]{1,0:T(8,128)(2,1)S(1)} %get-tuple-element.56), channel_id=1, source_target_pairs={{0,8},{4,12},{8,0},{12,4},{1,9},{5,13},{9,1},{13,5},{2,10},{6,14},... | collective-permute-start | bytes 196616 | tf_op jit(solution)/shard_map/ppermute | solution.py:28
  62.0 2.9 %collective-permute-start.24 = (bf16[16,2048]{1,0:T(8,128)(2,1)S(1)}, bf16[16,2048]{1,0:T(8,128)(2,1)S(1)}, u32[]{:S(2)}, u32[]{:S(2)}) collective-permute-start(bf16[16,2048]{1,0:T(8,128)(2,1)S(1)} %get-tuple-element.57), channel_id=1, source_target_pairs={{0,12},{4,8},{8,4},{12,0},{1,13},{5,9},{9,5},{13,1},{2,14},{6,10},... | collective-permute-start | bytes 196616 | tf_op jit(solution)/shard_map/ppermute | solution.py:28
  64.9 3.7 %collective-permute-done.23 = bf16[16,2048]{1,0:T(8,128)(2,1)S(1)} collective-permute-done((bf16[16,2048]{1,0:T(8,128)(2,1)S(1)}, bf16[16,2048]{1,0:T(8,128)(2,1)S(1)}, u32[]{:S(2)}, u32[]{:S(2)}) %collective-permute-start.23) | collective-permute-done | bytes 65568 | tf_op jit(solution)/shard_map/ppermute | solution.py:28
  68.6 0.7 fusion.19
  (56 shorter events, 1.2 us)
Async XLA Ops:
  0.6 47.7 %copy-start = (bf16[1,2048,2,384]{3,2,1,0:T(2,128)(2,1)S(1)}, bf16[1,2048,2,384]{3,2,1,0:T(2,128)(2,1)}, u32[]{:S(2)}) copy-start(bf16[1,2048,2,384]{3,2,1,0:T(2,128)(2,1)} %param.18) | copy-start | bytes 9437188
  1.8 9.4 %collective-permute-start.2 = (bf16[576,128]{1,0:T(8,128)(2,1)S(1)}, bf16[576,128]{1,0:T(8,128)(2,1)S(1)}, u32[]{:S(2)}, u32[]{:S(2)}) collective-permute-start(bf16[576,128]{1,0:T(8,128)(2,1)S(1)} %get-tuple-element.54.values), channel_id=1, source_target_pairs={{0,12},{4,0},{8,4},{12,8},{1,13},{5,1},{9,5},{13,9},{2,14},{6,2},{... | collective-permute-start | bytes 442376 | tf_op jit(solution)/shard_map/ppermute | solution.py:33
  6.9 8.7 %collective-permute-start = (bf16[576,128]{1,0:T(8,128)(2,1)S(1)}, bf16[576,128]{1,0:T(8,128)(2,1)S(1)}, u32[]{:S(2)}, u32[]{:S(2)}) collective-permute-start(bf16[576,128]{1,0:T(8,128)(2,1)S(1)} %get-tuple-element.55.keys), channel_id=1, source_target_pairs={{0,4},{4,8},{8,12},{12,0},{1,5},{5,9},{9,13},{13,1},{2,6},{6,10},{... | collective-permute-start | bytes 442376 | tf_op jit(solution)/shard_map/ppermute | solution.py:33
  6.9 16.4 %collective-permute-start.4 = (bf16[576,128]{1,0:T(8,128)(2,1)S(1)}, bf16[576,128]{1,0:T(8,128)(2,1)S(1)}, u32[]{:S(2)}, u32[]{:S(2)}) collective-permute-start(bf16[576,128]{1,0:T(8,128)(2,1)S(1)} %get-tuple-element.54.values), channel_id=1, source_target_pairs={{0,4},{4,8},{8,12},{12,0},{1,5},{5,9},{9,13},{13,1},{2,6},{6,10},{... | collective-permute-start | bytes 442376 | tf_op jit(solution)/shard_map/ppermute | solution.py:33
  6.9 16.4 %collective-permute-start.5 = (bf16[576,128]{1,0:T(8,128)(2,1)S(1)}, bf16[576,128]{1,0:T(8,128)(2,1)S(1)}, u32[]{:S(2)}, u32[]{:S(2)}) collective-permute-start(bf16[576,128]{1,0:T(8,128)(2,1)S(1)} %get-tuple-element.55.keys), channel_id=1, source_target_pairs={{0,12},{4,0},{8,4},{12,8},{1,13},{5,1},{9,5},{13,9},{2,14},{6,2},{... | collective-permute-start | bytes 442376 | tf_op jit(solution)/shard_map/ppermute | solution.py:33
  11.2 13.6 %collective-permute-start.3 = (bf16[576,128]{1,0:T(8,128)(2,1)S(1)}, bf16[576,128]{1,0:T(8,128)(2,1)S(1)}, u32[]{:S(2)}, u32[]{:S(2)}) collective-permute-start(bf16[576,128]{1,0:T(8,128)(2,1)S(1)} %collective-permute-done.2.refs_3_), channel_id=1, source_target_pairs={{0,12},{4,0},{8,4},{12,8},{1,13},{5,1},{9,5},{13,9},{2,14},{6,2},{... | collective-permute-start | bytes 442376 | tf_op jit(solution)/shard_map/ppermute | solution.py:33
  15.7 11.1 %collective-permute-start.1 = (bf16[576,128]{1,0:T(8,128)(2,1)S(1)}, bf16[576,128]{1,0:T(8,128)(2,1)S(1)}, u32[]{:S(2)}, u32[]{:S(2)}) collective-permute-start(bf16[576,128]{1,0:T(8,128)(2,1)S(1)} %collective-permute-done.refs_0_), channel_id=1, source_target_pairs={{0,4},{4,8},{8,12},{12,0},{1,5},{5,9},{9,13},{13,1},{2,6},{6,10},{... | collective-permute-start | bytes 442376 | tf_op jit(solution)/shard_map/ppermute | solution.py:33
  16.8 1.4 %copy-start.1 = (bf16[1,384,2048]{2,1,0:T(8,128)(2,1)S(1)}, bf16[1,384,2048]{2,1,0:T(8,128)(2,1)}, u32[]{:S(2)}) copy-start(bf16[1,384,2048]{2,1,0:T(8,128)(2,1)} %down.5) | copy-start | bytes 4718596
  18.2 2.2 %copy-start.3 = (bf16[1024,2048]{1,0:T(8,128)(2,1)S(1)}, bf16[1024,2048]{1,0:T(8,128)(2,1)}, u32[]{:S(2)}) copy-start(bf16[1024,2048]{1,0:T(8,128)(2,1)} %weight.1) | copy-start | bytes 12582916
  20.4 0.9 %copy-start.5 = (bf16[1,64,1024]{2,1,0:T(8,128)(2,1)S(1)}, bf16[1,64,1024]{2,1,0:T(8,128)(2,1)}, u32[]{:S(2)}) copy-start(bf16[1,64,1024]{2,1,0:T(8,128)(2,1)} %param.10) | copy-start | bytes 393220
  21.3 0.7 copy-start.11
  22.0 1.4 %copy-start.6 = (bf16[1,64,1024]{2,1,0:T(8,128)(2,1)S(1)}, bf16[1,64,1024]{2,1,0:T(8,128)(2,1)}, u32[]{:S(2)}) copy-start(bf16[1,64,1024]{2,1,0:T(8,128)(2,1)} %param.10) | copy-start | bytes 393220
  22.0 4.8 %copy-start.4 = (bf16[1024,2048]{1,0:T(8,128)(2,1)S(1)}, bf16[1024,2048]{1,0:T(8,128)(2,1)}, u32[]{:S(2)}) copy-start(bf16[1024,2048]{1,0:T(8,128)(2,1)} %weight.1) | copy-start | bytes 12582916
  23.3 11.3 %copy-start.7 = (bf16[1,16,2048]{2,1,0:T(8,128)(2,1)S(1)}, bf16[1,16,2048]{2,1,0:T(8,128)(2,1)}, u32[]{:S(2)}) copy-start(bf16[1,16,2048]{2,1,0:T(8,128)(2,1)} %param.13) | copy-start | bytes 196612
  23.3 11.3 %copy-start.8 = (f32[2048]{0:T(1024)S(1)}, f32[2048]{0:T(1024)}, u32[]{:S(2)}) copy-start(f32[2048]{0:T(1024)} %param.15) | copy-start | bytes 24580
  23.3 11.2 %copy-start.9 = (s32[1,16,8]{1,2,0:T(8,128)S(1)}, s32[1,16,8]{1,2,0:T(8,128)}, u32[]{:S(2)}) copy-start(s32[1,16,8]{1,2,0:T(8,128)} %param.16) | copy-start | bytes 1540
  23.3 11.2 %copy-start.10 = (f32[1,16,8]{1,2,0:T(8,128)S(1)}, f32[1,16,8]{1,2,0:T(8,128)}, u32[]{:S(2)}) copy-start(f32[1,16,8]{1,2,0:T(8,128)} %param.17) | copy-start | bytes 1540
  29.0 1.9 %collective-permute-start.6 = (bf16[16,2048]{1,0:T(8,128)(2,1)S(1)}, bf16[16,2048]{1,0:T(8,128)(2,1)S(1)}, u32[]{:S(2)}, u32[]{:S(2)}) collective-permute-start(bf16[16,2048]{1,0:T(8,128)(2,1)S(1)} %get-tuple-element.36), channel_id=1, source_target_pairs={{0,1},{1,0},{2,3},{3,2},{4,5},{5,4},{6,7},{7,6},{8,9},{9,8},{10,11... | collective-permute-start | bytes 196616 | tf_op jit(solution)/shard_map/ppermute | solution.py:28
  29.0 4.5 %collective-permute-start.7 = (bf16[16,2048]{1,0:T(8,128)(2,1)S(1)}, bf16[16,2048]{1,0:T(8,128)(2,1)S(1)}, u32[]{:S(2)}, u32[]{:S(2)}) collective-permute-start(bf16[16,2048]{1,0:T(8,128)(2,1)S(1)} %get-tuple-element.37), channel_id=1, source_target_pairs={{0,2},{1,3},{2,0},{3,1},{4,6},{5,7},{6,4},{7,5},{8,10},{9,11},{10,... | collective-permute-start | bytes 196616 | tf_op jit(solution)/shard_map/ppermute | solution.py:28
  30.4 4.1 %collective-permute-start.8 = (bf16[16,2048]{1,0:T(8,128)(2,1)S(1)}, bf16[16,2048]{1,0:T(8,128)(2,1)S(1)}, u32[]{:S(2)}, u32[]{:S(2)}) collective-permute-start(bf16[16,2048]{1,0:T(8,128)(2,1)S(1)} %get-tuple-element.38), channel_id=1, source_target_pairs={{0,3},{1,2},{2,1},{3,0},{4,7},{5,6},{6,5},{7,4},{8,11},{9,10},{10,... | collective-permute-start | bytes 196616 | tf_op jit(solution)/shard_map/ppermute | solution.py:28
  34.8 14.1 %copy-start.2 = (bf16[1,384,2048]{2,1,0:T(8,128)(2,1)S(1)}, bf16[1,384,2048]{2,1,0:T(8,128)(2,1)}, u32[]{:S(2)}) copy-start(bf16[1,384,2048]{2,1,0:T(8,128)(2,1)} %down.5) | copy-start | bytes 4718596
  34.9 4.4 %collective-permute-start.9 = (bf16[16,2176]{1,0:T(8,128)(2,1)S(1)}, bf16[16,2176]{1,0:T(8,128)(2,1)S(1)}, u32[]{:S(2)}, u32[]{:S(2)}) collective-permute-start(bf16[16,2176]{1,0:T(8,128)(2,1)S(1)} %get-tuple-element.40), channel_id=1, source_target_pairs={{0,4},{4,0},{8,12},{12,8},{1,5},{5,1},{9,13},{13,9},{2,6},{6,2},{1... | collective-permute-start | bytes 208904 | tf_op jit(solution)/shard_map/ppermute | solution.py:28
  36.6 6.6 %collective-permute-start.11 = (bf16[16,2176]{1,0:T(8,128)(2,1)S(1)}, bf16[16,2176]{1,0:T(8,128)(2,1)S(1)}, u32[]{:S(2)}, u32[]{:S(2)}) collective-permute-start(bf16[16,2176]{1,0:T(8,128)(2,1)S(1)} %get-tuple-element.40), channel_id=1, source_target_pairs={{0,12},{4,8},{8,4},{12,0},{1,13},{5,9},{9,5},{13,1},{2,14},{6,10},... | collective-permute-start | bytes 208904 | tf_op jit(solution)/shard_map/ppermute | solution.py:28
  37.1 8.1 %collective-permute-start.10 = (bf16[16,2176]{1,0:T(8,128)(2,1)S(1)}, bf16[16,2176]{1,0:T(8,128)(2,1)S(1)}, u32[]{:S(2)}, u32[]{:S(2)}) collective-permute-start(bf16[16,2176]{1,0:T(8,128)(2,1)S(1)} %get-tuple-element.40), channel_id=1, source_target_pairs={{0,8},{4,12},{8,0},{12,4},{1,9},{5,13},{9,1},{13,5},{2,10},{6,14},... | collective-permute-start | bytes 208904 | tf_op jit(solution)/shard_map/ppermute | solution.py:28
  39.2 6.0 %collective-permute-start.12 = (bf16[32,2176]{1,0:T(8,128)(2,1)S(1)}, bf16[32,2176]{1,0:T(8,128)(2,1)S(1)}, u32[]{:S(2)}, u32[]{:S(2)}) collective-permute-start(bf16[32,2176]{1,0:T(8,128)(2,1)S(1)} %pad_maximum_fusion.1), channel_id=1, source_target_pairs={{0,2},{1,3},{2,0},{3,1},{4,6},{5,7},{6,4},{7,5},{8,10},{9,11},{10,... | collective-permute-start | bytes 417800 | tf_op jit(solution)/shard_map/ppermute | solution.py:28
  45.2 5.2 %collective-permute-start.19 = (bf16[32,2176]{1,0:T(8,128)(2,1)S(1)}, bf16[32,2176]{1,0:T(8,128)(2,1)S(1)}, u32[]{:S(2)}, u32[]{:S(2)}) collective-permute-start(bf16[32,2176]{1,0:T(8,128)(2,1)S(1)} %pad_maximum_fusion.2), channel_id=1, source_target_pairs={{0,2},{1,3},{2,0},{3,1},{4,6},{5,7},{6,4},{7,5},{8,10},{9,11},{10,... | collective-permute-start | bytes 417800 | tf_op jit(solution)/shard_map/ppermute | solution.py:28
  46.7 1.4 %collective-permute-start.13 = (bf16[32,2176]{1,0:T(8,128)(2,1)S(1)}, bf16[32,2176]{1,0:T(8,128)(2,1)S(1)}, u32[]{:S(2)}, u32[]{:S(2)}) collective-permute-start(bf16[32,2176]{1,0:T(8,128)(2,1)S(1)} %collective-permute-done.12), channel_id=1, source_target_pairs={{0,1},{1,0},{2,3},{3,2},{4,5},{5,4},{6,7},{7,6},{8,9},{9,8},{10,11... | collective-permute-start | bytes 417800 | tf_op jit(solution)/shard_map/ppermute | solution.py:28
  48.1 5.4 %collective-permute-start.14 = (bf16[64,2176]{1,0:T(8,128)(2,1)S(1)}, bf16[64,2176]{1,0:T(8,128)(2,1)S(1)}, u32[]{:S(2)}, u32[]{:S(2)}) collective-permute-start(bf16[64,2176]{1,0:T(8,128)(2,1)S(1)} %pad_maximum_fusion), channel_id=1, source_target_pairs={{0,1},{1,0},{2,3},{3,2},{4,5},{5,4},{6,7},{7,6},{8,9},{9,8},{10,11... | collective-permute-start | bytes 835592 | tf_op jit(solution)/shard_map/ppermute | solution.py:28
  49.4 1.4 %collective-permute-start.16 = (bf16[32,2048]{1,0:T(8,128)(2,1)S(1)}, bf16[32,2048]{1,0:T(8,128)(2,1)S(1)}, u32[]{:S(2)}, u32[]{:S(2)}) collective-permute-start(bf16[32,2048]{1,0:T(8,128)(2,1)S(1)} %get-tuple-element.46), channel_id=1, source_target_pairs={{0,1},{1,0},{2,3},{3,2},{4,5},{5,4},{6,7},{7,6},{8,9},{9,8},{10,11... | collective-permute-start | bytes 393224 | tf_op jit(solution)/shard_map/ppermute | solution.py:28
  50.4 1.6 %collective-permute-start.20 = (bf16[32,2176]{1,0:T(8,128)(2,1)S(1)}, bf16[32,2176]{1,0:T(8,128)(2,1)S(1)}, u32[]{:S(2)}, u32[]{:S(2)}) collective-permute-start(bf16[32,2176]{1,0:T(8,128)(2,1)S(1)} %collective-permute-done.19), channel_id=1, source_target_pairs={{0,1},{1,0},{2,3},{3,2},{4,5},{5,4},{6,7},{7,6},{8,9},{9,8},{10,11... | collective-permute-start | bytes 417800 | tf_op jit(solution)/shard_map/ppermute | solution.py:28
  50.9 5.8 %collective-permute-start.17 = (bf16[32,2048]{1,0:T(8,128)(2,1)S(1)}, bf16[32,2048]{1,0:T(8,128)(2,1)S(1)}, u32[]{:S(2)}, u32[]{:S(2)}) collective-permute-start(bf16[32,2048]{1,0:T(8,128)(2,1)S(1)} %add_convert_fusion.1), channel_id=1, source_target_pairs={{0,2},{1,3},{2,0},{3,1},{4,6},{5,7},{6,4},{7,5},{8,10},{9,11},{10,... | collective-permute-start | bytes 393224 | tf_op jit(solution)/shard_map/ppermute | solution.py:28
  53.1 1.8 %collective-permute-start.21 = (bf16[32,2048]{1,0:T(8,128)(2,1)S(1)}, bf16[32,2048]{1,0:T(8,128)(2,1)S(1)}, u32[]{:S(2)}, u32[]{:S(2)}) collective-permute-start(bf16[32,2048]{1,0:T(8,128)(2,1)S(1)} %get-tuple-element.50), channel_id=1, source_target_pairs={{0,1},{1,0},{2,3},{3,2},{4,5},{5,4},{6,7},{7,6},{8,9},{9,8},{10,11... | collective-permute-start | bytes 393224 | tf_op jit(solution)/shard_map/ppermute | solution.py:28
  54.6 1.7 %collective-permute-start.15 = (bf16[64,2048]{1,0:T(8,128)(2,1)S(1)}, bf16[64,2048]{1,0:T(8,128)(2,1)S(1)}, u32[]{:S(2)}, u32[]{:S(2)}) collective-permute-start(bf16[64,2048]{1,0:T(8,128)(2,1)S(1)} %get-tuple-element.43), channel_id=1, source_target_pairs={{0,1},{1,0},{2,3},{3,2},{4,5},{5,4},{6,7},{7,6},{8,9},{9,8},{10,11... | collective-permute-start | bytes 786440 | tf_op jit(solution)/shard_map/ppermute | solution.py:28
  54.9 5.7 %collective-permute-start.22 = (bf16[32,2048]{1,0:T(8,128)(2,1)S(1)}, bf16[32,2048]{1,0:T(8,128)(2,1)S(1)}, u32[]{:S(2)}, u32[]{:S(2)}) collective-permute-start(bf16[32,2048]{1,0:T(8,128)(2,1)S(1)} %add_convert_fusion), channel_id=1, source_target_pairs={{0,2},{1,3},{2,0},{3,1},{4,6},{5,7},{6,4},{7,5},{8,10},{9,11},{10,... | collective-permute-start | bytes 393224 | tf_op jit(solution)/shard_map/ppermute | solution.py:28
  56.7 4.3 %collective-permute-start.18 = (bf16[16,2048]{1,0:T(8,128)(2,1)S(1)}, bf16[16,2048]{1,0:T(8,128)(2,1)S(1)}, u32[]{:S(2)}, u32[]{:S(2)}) collective-permute-start(bf16[16,2048]{1,0:T(8,128)(2,1)S(1)} %slice.78), channel_id=1, source_target_pairs={{0,4},{4,0},{8,12},{12,8},{1,5},{5,1},{9,13},{13,9},{2,6},{6,2},{1... | collective-permute-start | bytes 196616 | tf_op jit(solution)/shard_map/ppermute | solution.py:28
  61.1 7.5 %collective-permute-start.23 = (bf16[16,2048]{1,0:T(8,128)(2,1)S(1)}, bf16[16,2048]{1,0:T(8,128)(2,1)S(1)}, u32[]{:S(2)}, u32[]{:S(2)}) collective-permute-start(bf16[16,2048]{1,0:T(8,128)(2,1)S(1)} %get-tuple-element.56), channel_id=1, source_target_pairs={{0,8},{4,12},{8,0},{12,4},{1,9},{5,13},{9,1},{13,5},{2,10},{6,14},... | collective-permute-start | bytes 196616 | tf_op jit(solution)/shard_map/ppermute | solution.py:28
  62.0 6.6 %collective-permute-start.24 = (bf16[16,2048]{1,0:T(8,128)(2,1)S(1)}, bf16[16,2048]{1,0:T(8,128)(2,1)S(1)}, u32[]{:S(2)}, u32[]{:S(2)}) collective-permute-start(bf16[16,2048]{1,0:T(8,128)(2,1)S(1)} %get-tuple-element.57), channel_id=1, source_target_pairs={{0,12},{4,8},{8,4},{12,0},{1,13},{5,9},{9,5},{13,1},{2,14},{6,10},... | collective-permute-start | bytes 196616 | tf_op jit(solution)/shard_map/ppermute | solution.py:28

commit v8 on v7

--- a/solution.py
+++ b/solution.py
@@ -288,7 +288,7 @@
     )(*parts, residual, norm_gain[None], ids, scores)
 
 
-def down_kernel(inner, rows, down, keep_out, *send_out):
+def down_kernel(inner, rows, down, *outs):
     expert = lax.axis_index("ctx") * lax.axis_size("exp") + lax.axis_index("exp")
     gate = inner[0]
     activated = (gate / (1.0 + jnp.exp(-gate)) * inner[1]).astype(jnp.bfloat16)
@@ -297,22 +297,27 @@
     lane = lax.broadcasted_iota(jnp.int32, dense.shape, 1)
     scale = jnp.sum(jnp.where(lane == expert, dense, 0.0), axis=1, keepdims=True)
     result = piece.astype(jnp.bfloat16).astype(jnp.float32) * scale
-    size = keep_out.shape[0]
-    keep_out[...] = result[:size]
-    for out in send_out:
-        out[...] = result[size:].astype(jnp.bfloat16)
-
-
-def expert_apply(rows, gate_up, down, size):
+    start = 0
+    for out in outs:
+        out[...] = result[start : start + out.shape[0]].astype(out.dtype)
+        start += out.shape[0]
+
+
+def expert_apply(groups, gate_up, down, split):
     _, hidden, width = down.shape
+    rows = jnp.concatenate(groups, axis=0)
     total = rows.shape[0]
-    half = max(size, total // 2)
     inner = jnp.einsum(
         "nd,dgh->gnh", rows[:, :width], gate_up[0], preferred_element_type=jnp.float32
     )
-    shapes = [jax.ShapeDtypeStruct((half, width), jnp.float32)]
-    if total > half:
-        shapes.append(jax.ShapeDtypeStruct((total - half, width), jnp.bfloat16))
+    shapes = []
+    for group in groups:
+        size = group.shape[0]
+        if split:
+            shapes.append(jax.ShapeDtypeStruct((size // 2, width), jnp.float32))
+            shapes.append(jax.ShapeDtypeStruct((size // 2, width), jnp.bfloat16))
+        else:
+            shapes.append(jax.ShapeDtypeStruct((size, width), jnp.float32))
     outs = pl.pallas_call(
         down_kernel,
         out_shape=shapes,
@@ -323,7 +328,7 @@
             flops=2 * total * width * hidden, bytes_accessed=2 << 20, transcendentals=0
         ),
     )(inner, rows, down)
-    return outs[0], (outs[1] if total > half else None)
+    return list(zip(outs[::2], outs[1::2])) if split else [(out, None) for out in outs]
 
 
 def return_near(keep, send, near):
@@ -352,36 +357,60 @@
             held = held + [swap(part, "exp", stride) for part in held]
         return jnp.concatenate(held, axis=0)
 
-    def results(held, size):
-        return return_near(*expert_apply(held, gate_up, down, size), near)
-
-    sent = []
-    for chunk in chunks:
-        blocks = [rows if offset == 0 else swap(rows, "ctx", offset) for offset in chunk]
-        sent.append(jnp.concatenate(blocks, axis=0))
+    sent = [
+        {offset: rows if offset == 0 else swap(rows, "ctx", offset) for offset in chunk}
+        for chunk in chunks
+    ]
+    joined = [jnp.concatenate(list(blocks.values()), axis=0) for blocks in sent]
+
+    def cross(number):
+        if not far:
+            return None
+        if number == 0:
+            return swap(joined[0], "exp", far[0])
+        blocks = list(sent[number].values())
+        blocks[0], _ = lax.optimization_barrier((blocks[0], crossed[0]))
+        return jnp.concatenate([swap(block, "exp", far[0]) for block in blocks], axis=0)
+
     crossed = []
-    for piece in sent:
-        if crossed:
-            piece, _ = lax.optimization_barrier((piece, arrived))
-        arrived = [swap(piece, "exp", stride) for stride in far]
-        crossed.append([gather(part) for part in arrived])
-    everything = jnp.concatenate(sent, axis=0)
+    for number in range(len(chunks)):
+        crossed.append(cross(number))
+    groups = [[] if piece is None else [gather(piece)] for piece in crossed]
+    everything = jnp.concatenate(joined, axis=0)
     everything, _ = lax.optimization_barrier((everything, crossed[0]))
-    home = results(gather(everything), everything.shape[0])
+    groups[-1].append(gather(everything))
+    values = [
+        [return_near(*pair, near) for pair in expert_apply(held, gate_up, down, bool(near))]
+        if held
+        else []
+        for held in groups
+    ]
+    home = values[-1].pop()
     homes, start = [], 0
-    for piece in sent:
+    for piece in joined:
         homes.append(home[start : start + piece.shape[0]])
         start += piece.shape[0]
     homes = lax.optimization_barrier(homes)
     total, arrived = None, []
-    for chunk, value, away in zip(chunks, homes, crossed):
-        for part in away:
-            other = results(part, value.shape[0]).astype(jnp.bfloat16)
-            value = value + swap(other, "exp", far[0]).astype(jnp.float32)
+    for number, (chunk, value, others) in enumerate(zip(chunks, homes, values)):
+        size = value.shape[0]
+        blocks = [value[low : low + tokens] for low in range(0, size, tokens)]
+        for other in others:
+            other = other.astype(jnp.bfloat16)
+            if number == 0:
+                other = swap(other, "exp", far[0])
+                others = [other[low : low + tokens] for low in range(0, size, tokens)]
+            else:
+                others = [
+                    swap(other[low : low + tokens], "exp", far[0])
+                    for low in range(0, size, tokens)
+                ]
+            blocks = [
+                block + other.astype(jnp.float32) for block, other in zip(blocks, others)
+            ]
         if arrived:
-            value, _ = lax.optimization_barrier((value, arrived[0]))
-        for position, offset in enumerate(chunk):
-            block = value[position * tokens : (position + 1) * tokens]
+            blocks[-1], _ = lax.optimization_barrier((blocks[-1], arrived[0]))
+        for offset, block in zip(chunk, blocks):
             if offset == 0:
                 total = block
             else:

time: 69.5 us -> 70.8 us (1.019)
  starting transfers between devices: 31.8 us -> 33.6 us
    ppermute x19 -> x21, starting transfers between devices: 17.4 us -> 19.2 us  [swap(): lax.ppermute(value, axis, [(i, i ^ stride) for i in range(lax.axis_size(a...]
    dot_general x3 -> x2, matrix products: 1.95 us -> 1.5 us  [expert_apply(): jnp.einsum('nd,dgh->gnh', rows[:, :width], gate_up[0], preferred_element_...]
    ppermute x19 -> x21, waiting for transfers between devices: 18.2 us -> 18.4 us  [swap(): lax.ppermute(value, axis, [(i, i ^ stride) for i in range(lax.axis_size(a...]
    unnamed x28 -> x30, local copies, waits for them, and re-layouts: 6.4 us -> 6.43 us
  transfers between devices with their start and end apart: 25 -> 27, of which waited for: 15 -> 14; matrix products, arithmetic and copies ran while one was open for 3% -> 3% of each run, Pallas kernels for 6% -> 5%
where the time goes in v8:
time: 70.8 us; the launch traced here: 70.6 us
  starting transfers between devices  33.6 us (47%)
  waiting for transfers between devices  20.9 us (30%)
  local copies, waits for them, and re-layouts  6.54 us (9%)
  Pallas kernels  6.16 us (9%)
  matrix products  1.5 us (2%)
  between operations  0.94 us (1%)
  other arithmetic  0.89 us (1%)
    ppermute x21, starting transfers between devices, swap(): lax.ppermute(value, axis, [(i, i ^ stride) for i in range(lax.axis_size(a...  19.2 us
    ppermute x21, waiting for transfers between devices, swap(): lax.ppermute(value, axis, [(i, i ^ stride) for i in range(lax.axis_size(a...  18.4 us
    ppermute x6, starting transfers between devices, shift(): lax.ppermute(value, axis, [(i, (i + step) % count) for i in range(count)])  14.4 us
    unnamed x30, local copies, waits for them, and re-layouts  6.43 us
    ppermute x6, waiting for transfers between devices, shift(): lax.ppermute(value, axis, [(i, (i + step) % count) for i in range(count)])  2.54 us
    pallas_call x1, Pallas kernels, attention(): pl.pallas_call(functools.partial(late_kernel, last[0], fresh_block), out_...  2.16 us
    dot_general x2, matrix products, expert_apply(): jnp.einsum('nd,dgh->gnh', rows[:, :width], gate_up[0], preferred_element_...  1.5 us
    pallas_call x1, Pallas kernels, attention(): pl.pallas_call(functools.partial(middle_kernel, [offset for offset, _, _...  1.43 us
  transfers between devices with their start and end apart: 27, of which 14 were waited for; matrix products, arithmetic and copies ran while one was open for 3% of the time, Pallas kernels for 5%

profile of v8, /device:TPU:0, one launch (start us, length us, event | category | flops | bytes accessed | tf_op | source)
XLA Modules:
  0.0 70.6 jit_solution(7210421163382167611)
XLA Ops:
  0.6 1.2 %copy.24 = bf16[1,576,2,128]{3,1,2,0:T(8,128)(2,1)S(1)} copy(bf16[1,576,2,128]{3,2,1,0:T(2,128)(2,1)} %param.11) | data formatting | bytes 589824 | tf_op args[1]
  1.8 5.1 %collective-permute-start.2 = (bf16[576,128]{1,0:T(8,128)(2,1)S(1)}, bf16[576,128]{1,0:T(8,128)(2,1)S(1)}, u32[]{:S(2)}, u32[]{:S(2)}) collective-permute-start(bf16[576,128]{1,0:T(8,128)(2,1)S(1)} %get-tuple-element.54.values), channel_id=1, source_target_pairs={{0,12},{4,0},{8,4},{12,8},{1,13},{5,1},{9,5},{13,9},{2,14},{6,2},{... | collective-permute-start | bytes 442376 | tf_op jit(solution)/shard_map/ppermute | solution.py:33
  6.9 3.9 %collective-permute-start.5 = (bf16[576,128]{1,0:T(8,128)(2,1)S(1)}, bf16[576,128]{1,0:T(8,128)(2,1)S(1)}, u32[]{:S(2)}, u32[]{:S(2)}) collective-permute-start(bf16[576,128]{1,0:T(8,128)(2,1)S(1)} %get-tuple-element.55.keys), channel_id=1, source_target_pairs={{0,12},{4,0},{8,4},{12,8},{1,13},{5,1},{9,5},{13,9},{2,14},{6,2},{... | collective-permute-start | bytes 442376 | tf_op jit(solution)/shard_map/ppermute | solution.py:33
  10.8 0.4 collective-permute-done.2.refs_3_
  11.2 4.3 %collective-permute-start.3 = (bf16[576,128]{1,0:T(8,128)(2,1)S(1)}, bf16[576,128]{1,0:T(8,128)(2,1)S(1)}, u32[]{:S(2)}, u32[]{:S(2)}) collective-permute-start(bf16[576,128]{1,0:T(8,128)(2,1)S(1)} %collective-permute-done.2.refs_3_), channel_id=1, source_target_pairs={{0,12},{4,0},{8,4},{12,8},{1,13},{5,1},{9,5},{13,9},{2,14},{6,2},{... | collective-permute-start | bytes 442376 | tf_op jit(solution)/shard_map/ppermute | solution.py:33
  15.7 1.2 %collective-permute-start.1 = (bf16[576,128]{1,0:T(8,128)(2,1)S(1)}, bf16[576,128]{1,0:T(8,128)(2,1)S(1)}, u32[]{:S(2)}, u32[]{:S(2)}) collective-permute-start(bf16[576,128]{1,0:T(8,128)(2,1)S(1)} %collective-permute-done.refs_0_), channel_id=1, source_target_pairs={{0,4},{4,8},{8,12},{12,0},{1,5},{5,9},{9,13},{13,1},{2,6},{6,10},{... | collective-permute-start | bytes 442376 | tf_op jit(solution)/shard_map/ppermute | solution.py:33
  16.8 1.4 %copy-done.1 = bf16[1,384,2048]{2,1,0:T(8,128)(2,1)S(1)} copy-done((bf16[1,384,2048]{2,1,0:T(8,128)(2,1)S(1)}, bf16[1,384,2048]{2,1,0:T(8,128)(2,1)}, u32[]{:S(2)}) %copy-start.1) | copy-done | bytes 1572888
  18.2 2.2 %copy-done.3 = bf16[1024,2048]{1,0:T(8,128)(2,1)S(1)} copy-done((bf16[1024,2048]{1,0:T(8,128)(2,1)S(1)}, bf16[1024,2048]{1,0:T(8,128)(2,1)}, u32[]{:S(2)}) %copy-start.3) | copy-done | bytes 4194328
  20.4 0.9 %copy-done.5 = bf16[1,64,1024]{2,1,0:T(8,128)(2,1)S(1)} copy-done((bf16[1,64,1024]{2,1,0:T(8,128)(2,1)S(1)}, bf16[1,64,1024]{2,1,0:T(8,128)(2,1)}, u32[]{:S(2)}) %copy-start.5) | copy-done | bytes 131096
  21.3 0.7 copy-done.11
  22.0 1.3 %shard_map.113 = (f32[1,512]{1,0:T(1,128)S(1)}, f32[1,512]{1,0:T(1,128)S(1)}, f32[128,512]{1,0:T(8,128)S(1)}, s32[4,128]{1,0:T(4,128)S(1)}) custom-call(s32[4]{0:T(128)S(1)} %bitcast.40, bf16[64,1024]{1,0:T(8,128)(2,1)S(1)} %bitcast.33, bf16[576,128]{1,0:T(8,128)(2,1)S(1)} %get-tuple-element.55.keys, bf16[576,128]{1,0:T(8,128)(2,1)S(1)} %get-tuple-element.54.values, ...), custom_call_target="tpu_custom_call" | custom-call | flops 2415919104 | bytes 8388608 | tf_op jit(solution)/shard_map/pallas_call | solution.py:206
  23.4 1.4 %shard_map.114 = (f32[1,512]{1,0:T(1,128)S(1)}, f32[1,512]{1,0:T(1,128)S(1)}, f32[128,512]{1,0:T(8,128)S(1)}) custom-call(bf16[64,1024]{1,0:T(8,128)(2,1)S(1)} %bitcast.34, s32[4,128]{1,0:T(4,128)S(1)} %get-tuple-element.27.lengths, bf16[576,128]{1,0:T(8,128)(2,1)S(1)} %collective-permute-done.refs_0_, bf16[576,128]{1,0:T(8,128)(2,1)S(1)} %collective-permute-done.4.refs_1_, ...), custom_call_target="tpu_custom_call" | custom-call | flops 301989888 | bytes 2097152 | tf_op jit(solution)/shard_map/pallas_call | solution.py:221
  24.8 1.9 %collective-permute-done.1.keys = bf16[576,128]{1,0:T(8,128)(2,1)S(1)} collective-permute-done((bf16[576,128]{1,0:T(8,128)(2,1)S(1)}, bf16[576,128]{1,0:T(8,128)(2,1)S(1)}, u32[]{:S(2)}, u32[]{:S(2)}) %collective-permute-start.1) | collective-permute-done | bytes 147488 | tf_op jit(solution)/shard_map/ppermute | solution.py:33
  26.8 2.2 %shard_map.115 = (bf16[64,1024]{1,0:T(8,128)(2,1)}, f32[16,2048]{1,0:T(8,128)S(1)}, bf16[16,2048]{1,0:T(8,128)(2,1)S(1)}, bf16[16,2048]{1,0:T(8,128)(2,1)S(1)}, bf16[16,2048]{1,0:T(8,128)(2,1)S(1)}) custom-call(bf16[64,1024]{1,0:T(8,128)(2,1)S(1)} %bitcast.35, bf16[576,128]{1,0:T(8,128)(2,1)S(1)} %collective-permute-done.1.keys, ...), custom_call_target="tpu_custom_call" | custom-call | flops 419430400 | bytes 6291456 | tf_op jit(solution)/shard_map/pallas_call | solution.py:232
  29.0 1.5 %collective-permute-start.7 = (bf16[16,2048]{1,0:T(8,128)(2,1)S(1)}, bf16[16,2048]{1,0:T(8,128)(2,1)S(1)}, u32[]{:S(2)}, u32[]{:S(2)}) collective-permute-start(bf16[16,2048]{1,0:T(8,128)(2,1)S(1)} %get-tuple-element.37), channel_id=1, source_target_pairs={{0,2},{1,3},{2,0},{3,1},{4,6},{5,7},{6,4},{7,5},{8,10},{9,11},{10,... | collective-permute-start | bytes 196616 | tf_op jit(solution)/shard_map/ppermute | solution.py:28
  30.4 0.4 collective-permute-start.8
  30.8 2.7 %collective-permute-done.7.refs_2_ = bf16[16,2048]{1,0:T(8,128)(2,1)S(1)} collective-permute-done((bf16[16,2048]{1,0:T(8,128)(2,1)S(1)}, bf16[16,2048]{1,0:T(8,128)(2,1)S(1)}, u32[]{:S(2)}, u32[]{:S(2)}) %collective-permute-start.7) | collective-permute-done | bytes 65568 | tf_op jit(solution)/shard_map/ppermute | solution.py:28
  33.5 1.1 %collective-permute-done.8.refs_3_ = bf16[16,2048]{1,0:T(8,128)(2,1)S(1)} collective-permute-done((bf16[16,2048]{1,0:T(8,128)(2,1)S(1)}, bf16[16,2048]{1,0:T(8,128)(2,1)S(1)}, u32[]{:S(2)}, u32[]{:S(2)}) %collective-permute-start.8) | collective-permute-done | bytes 65568 | tf_op jit(solution)/shard_map/ppermute | solution.py:28
  34.6 0.3 shard_map.116
  34.9 1.7 %collective-permute-start.10 = (bf16[16,2176]{1,0:T(8,128)(2,1)S(1)}, bf16[16,2176]{1,0:T(8,128)(2,1)S(1)}, u32[]{:S(2)}, u32[]{:S(2)}) collective-permute-start(bf16[16,2176]{1,0:T(8,128)(2,1)S(1)} %get-tuple-element.40), channel_id=1, source_target_pairs={{0,4},{4,0},{8,12},{12,8},{1,5},{5,1},{9,13},{13,9},{2,6},{6,2},{1... | collective-permute-start | bytes 208904 | tf_op jit(solution)/shard_map/ppermute | solution.py:28
  36.6 0.5 collective-permute-start.13
  37.1 1.3 %collective-permute-start.9 = (bf16[16,2176]{1,0:T(8,128)(2,1)S(1)}, bf16[16,2176]{1,0:T(8,128)(2,1)S(1)}, u32[]{:S(2)}, u32[]{:S(2)}) collective-permute-start(bf16[16,2176]{1,0:T(8,128)(2,1)S(1)} %get-tuple-element.40), channel_id=1, source_target_pairs={{0,8},{4,12},{8,0},{12,4},{1,9},{5,13},{9,1},{13,5},{2,10},{6,14},... | collective-permute-start | bytes 208904 | tf_op jit(solution)/shard_map/ppermute | solution.py:28
  38.4 0.8 %collective-permute-done.10 = bf16[16,2176]{1,0:T(8,128)(2,1)S(1)} collective-permute-done((bf16[16,2176]{1,0:T(8,128)(2,1)S(1)}, bf16[16,2176]{1,0:T(8,128)(2,1)S(1)}, u32[]{:S(2)}, u32[]{:S(2)}) %collective-permute-start.10) | collective-permute-done | bytes 69664 | tf_op jit(solution)/shard_map/ppermute | solution.py:28
  39.2 1.5 %collective-permute-start.11 = (bf16[32,2176]{1,0:T(8,128)(2,1)S(1)}, bf16[32,2176]{1,0:T(8,128)(2,1)S(1)}, u32[]{:S(2)}, u32[]{:S(2)}) collective-permute-start(bf16[32,2176]{1,0:T(8,128)(2,1)S(1)} %pad_maximum_fusion.1), channel_id=1, source_target_pairs={{0,2},{1,3},{2,0},{3,1},{4,6},{5,7},{6,4},{7,5},{8,10},{9,11},{10,... | collective-permute-start | bytes 417800 | tf_op jit(solution)/shard_map/ppermute | solution.py:28
  40.7 2.4 %collective-permute-done.13 = bf16[16,2176]{1,0:T(8,128)(2,1)S(1)} collective-permute-done((bf16[16,2176]{1,0:T(8,128)(2,1)S(1)}, bf16[16,2176]{1,0:T(8,128)(2,1)S(1)}, u32[]{:S(2)}, u32[]{:S(2)}) %collective-permute-start.13) | collective-permute-done | bytes 69664 | tf_op jit(solution)/shard_map/ppermute | solution.py:28
  43.1 1.5 %collective-permute-start.14 = (bf16[16,2176]{1,0:T(8,128)(2,1)S(1)}, bf16[16,2176]{1,0:T(8,128)(2,1)S(1)}, u32[]{:S(2)}, u32[]{:S(2)}) collective-permute-start(bf16[16,2176]{1,0:T(8,128)(2,1)S(1)} %collective-permute-done.13), channel_id=1, source_target_pairs={{0,2},{1,3},{2,0},{3,1},{4,6},{5,7},{6,4},{7,5},{8,10},{9,11},{10,... | collective-permute-start | bytes 208904 | tf_op jit(solution)/shard_map/ppermute | solution.py:28
  44.6 0.6 collective-permute-done.9
  45.2 1.5 %collective-permute-start.12 = (bf16[16,2176]{1,0:T(8,128)(2,1)S(1)}, bf16[16,2176]{1,0:T(8,128)(2,1)S(1)}, u32[]{:S(2)}, u32[]{:S(2)}) collective-permute-start(bf16[16,2176]{1,0:T(8,128)(2,1)S(1)} %collective-permute-done.9), channel_id=1, source_target_pairs={{0,2},{1,3},{2,0},{3,1},{4,6},{5,7},{6,4},{7,5},{8,10},{9,11},{10,... | collective-permute-start | bytes 208904 | tf_op jit(solution)/shard_map/ppermute | solution.py:28
  46.7 0.5 collective-permute-start.18
  47.2 0.3 collective-permute-done.14
  47.5 2.1 %collective-permute-done.12 = bf16[16,2176]{1,0:T(8,128)(2,1)S(1)} collective-permute-done((bf16[16,2176]{1,0:T(8,128)(2,1)S(1)}, bf16[16,2176]{1,0:T(8,128)(2,1)S(1)}, u32[]{:S(2)}, u32[]{:S(2)}) %collective-permute-start.12) | collective-permute-done | bytes 69664 | tf_op jit(solution)/shard_map/ppermute | solution.py:28
  49.8 0.7 fusion.7.inner
  50.4 0.4 shard_map.118
  50.9 0.6 collective-permute-start.19
  51.5 0.8 %fusion.4.inner = f32[2,192,384]{2,1,0:T(8,128)S(1)} fusion(bf16[2048,2,384]{2,1,0:T(2,128)(2,1)S(1)} %bitcast.31, bf16[192,2176]{1,0:T(8,128)(2,1)S(1)} %constant_dynamic-update-slice_fusion.rows), kind=kOutput, calls=%fused_computation.4 | convolution fusion | flops 603979776 | bytes 4521984 | tf_op jit(solution)/shard_map/nd,dgh->gnh/dot_general | solution.py:310
  52.3 0.6 shard_map.117
  53.1 1.5 %collective-permute-start.20 = (bf16[32,2048]{1,0:T(8,128)(2,1)S(1)}, bf16[32,2048]{1,0:T(8,128)(2,1)S(1)}, u32[]{:S(2)}, u32[]{:S(2)}) collective-permute-start(bf16[32,2048]{1,0:T(8,128)(2,1)S(1)} %add_convert_fusion.1), channel_id=1, source_target_pairs={{0,2},{1,3},{2,0},{3,1},{4,6},{5,7},{6,4},{7,5},{8,10},{9,11},{10,... | collective-permute-start | bytes 393224 | tf_op jit(solution)/shard_map/ppermute | solution.py:28
  54.5 0.2 collective-permute-start.17
  54.8 1.1 %collective-permute-start.23 = (bf16[16,2048]{1,0:T(8,128)(2,1)S(1)}, bf16[16,2048]{1,0:T(8,128)(2,1)S(1)}, u32[]{:S(2)}, u32[]{:S(2)}) collective-permute-start(bf16[16,2048]{1,0:T(8,128)(2,1)S(1)} %get-tuple-element.56), channel_id=1, source_target_pairs={{0,2},{1,3},{2,0},{3,1},{4,6},{5,7},{6,4},{7,5},{8,10},{9,11},{10,... | collective-permute-start | bytes 196616 | tf_op jit(solution)/shard_map/ppermute | solution.py:28
  55.9 1.0 %collective-permute-start.25 = (bf16[16,2048]{1,0:T(8,128)(2,1)S(1)}, bf16[16,2048]{1,0:T(8,128)(2,1)S(1)}, u32[]{:S(2)}, u32[]{:S(2)}) collective-permute-start(bf16[16,2048]{1,0:T(8,128)(2,1)S(1)} %get-tuple-element.57), channel_id=1, source_target_pairs={{0,2},{1,3},{2,0},{3,1},{4,6},{5,7},{6,4},{7,5},{8,10},{9,11},{10,... | collective-permute-start | bytes 196616 | tf_op jit(solution)/shard_map/ppermute | solution.py:28
  57.0 2.4 %collective-permute-done.20 = bf16[32,2048]{1,0:T(8,128)(2,1)S(1)} collective-permute-done((bf16[32,2048]{1,0:T(8,128)(2,1)S(1)}, bf16[32,2048]{1,0:T(8,128)(2,1)S(1)}, u32[]{:S(2)}, u32[]{:S(2)}) %collective-permute-start.20) | collective-permute-done | bytes 131104 | tf_op jit(solution)/shard_map/ppermute | solution.py:28
  59.5 1.5 %collective-permute-start.21 = (bf16[16,2048]{1,0:T(8,128)(2,1)S(1)}, bf16[16,2048]{1,0:T(8,128)(2,1)S(1)}, u32[]{:S(2)}, u32[]{:S(2)}) collective-permute-start(bf16[16,2048]{1,0:T(8,128)(2,1)S(1)} %add_convert_fusion.4), channel_id=1, source_target_pairs={{0,4},{4,0},{8,12},{12,8},{1,5},{5,1},{9,13},{13,9},{2,6},{6,2},{1... | collective-permute-start | bytes 196616 | tf_op jit(solution)/shard_map/ppermute | solution.py:28
  61.0 1.0 %collective-permute-start.24 = (bf16[16,2048]{1,0:T(8,128)(2,1)S(1)}, bf16[16,2048]{1,0:T(8,128)(2,1)S(1)}, u32[]{:S(2)}, u32[]{:S(2)}) collective-permute-start(bf16[16,2048]{1,0:T(8,128)(2,1)S(1)} %add_convert_fusion.3), channel_id=1, source_target_pairs={{0,8},{4,12},{8,0},{12,4},{1,9},{5,13},{9,1},{13,5},{2,10},{6,14},... | collective-permute-start | bytes 196616 | tf_op jit(solution)/shard_map/ppermute | solution.py:28
  62.0 1.8 %collective-permute-done.21 = bf16[16,2048]{1,0:T(8,128)(2,1)S(1)} collective-permute-done((bf16[16,2048]{1,0:T(8,128)(2,1)S(1)}, bf16[16,2048]{1,0:T(8,128)(2,1)S(1)}, u32[]{:S(2)}, u32[]{:S(2)}) %collective-permute-start.21) | collective-permute-done | bytes 65568 | tf_op jit(solution)/shard_map/ppermute | solution.py:28
  63.8 1.8 %collective-permute-start.26 = (bf16[16,2048]{1,0:T(8,128)(2,1)S(1)}, bf16[16,2048]{1,0:T(8,128)(2,1)S(1)}, u32[]{:S(2)}, u32[]{:S(2)}) collective-permute-start(bf16[16,2048]{1,0:T(8,128)(2,1)S(1)} %convert_add_fusion.1), channel_id=1, source_target_pairs={{0,12},{4,8},{8,4},{12,0},{1,13},{5,9},{9,5},{13,1},{2,14},{6,10},... | collective-permute-start | bytes 196616 | tf_op jit(solution)/shard_map/ppermute | solution.py:28
  65.6 2.6 %collective-permute-done.24 = bf16[16,2048]{1,0:T(8,128)(2,1)S(1)} collective-permute-done((bf16[16,2048]{1,0:T(8,128)(2,1)S(1)}, bf16[16,2048]{1,0:T(8,128)(2,1)S(1)}, u32[]{:S(2)}, u32[]{:S(2)}) %collective-permute-start.24) | collective-permute-done | bytes 65568 | tf_op jit(solution)/shard_map/ppermute | solution.py:28
  68.2 1.6 %collective-permute-done.26 = bf16[16,2048]{1,0:T(8,128)(2,1)S(1)} collective-permute-done((bf16[16,2048]{1,0:T(8,128)(2,1)S(1)}, bf16[16,2048]{1,0:T(8,128)(2,1)S(1)}, u32[]{:S(2)}, u32[]{:S(2)}) %collective-permute-start.26) | collective-permute-done | bytes 65568 | tf_op jit(solution)/shard_map/ppermute | solution.py:28
  69.9 0.7 fusion.10
  (59 shorter events, 0.9 us)
Async XLA Ops:
  0.6 49.1 %copy-start = (bf16[1,2048,2,384]{3,2,1,0:T(2,128)(2,1)S(1)}, bf16[1,2048,2,384]{3,2,1,0:T(2,128)(2,1)}, u32[]{:S(2)}) copy-start(bf16[1,2048,2,384]{3,2,1,0:T(2,128)(2,1)} %param.18) | copy-start | bytes 9437188
  1.8 9.4 %collective-permute-start.2 = (bf16[576,128]{1,0:T(8,128)(2,1)S(1)}, bf16[576,128]{1,0:T(8,128)(2,1)S(1)}, u32[]{:S(2)}, u32[]{:S(2)}) collective-permute-start(bf16[576,128]{1,0:T(8,128)(2,1)S(1)} %get-tuple-element.54.values), channel_id=1, source_target_pairs={{0,12},{4,0},{8,4},{12,8},{1,13},{5,1},{9,5},{13,9},{2,14},{6,2},{... | collective-permute-start | bytes 442376 | tf_op jit(solution)/shard_map/ppermute | solution.py:33
  6.9 8.7 %collective-permute-start = (bf16[576,128]{1,0:T(8,128)(2,1)S(1)}, bf16[576,128]{1,0:T(8,128)(2,1)S(1)}, u32[]{:S(2)}, u32[]{:S(2)}) collective-permute-start(bf16[576,128]{1,0:T(8,128)(2,1)S(1)} %get-tuple-element.55.keys), channel_id=1, source_target_pairs={{0,4},{4,8},{8,12},{12,0},{1,5},{5,9},{9,13},{13,1},{2,6},{6,10},{... | collective-permute-start | bytes 442376 | tf_op jit(solution)/shard_map/ppermute | solution.py:33
  6.9 16.4 %collective-permute-start.4 = (bf16[576,128]{1,0:T(8,128)(2,1)S(1)}, bf16[576,128]{1,0:T(8,128)(2,1)S(1)}, u32[]{:S(2)}, u32[]{:S(2)}) collective-permute-start(bf16[576,128]{1,0:T(8,128)(2,1)S(1)} %get-tuple-element.54.values), channel_id=1, source_target_pairs={{0,4},{4,8},{8,12},{12,0},{1,5},{5,9},{9,13},{13,1},{2,6},{6,10},{... | collective-permute-start | bytes 442376 | tf_op jit(solution)/shard_map/ppermute | solution.py:33
  6.9 16.4 %collective-permute-start.5 = (bf16[576,128]{1,0:T(8,128)(2,1)S(1)}, bf16[576,128]{1,0:T(8,128)(2,1)S(1)}, u32[]{:S(2)}, u32[]{:S(2)}) collective-permute-start(bf16[576,128]{1,0:T(8,128)(2,1)S(1)} %get-tuple-element.55.keys), channel_id=1, source_target_pairs={{0,12},{4,0},{8,4},{12,8},{1,13},{5,1},{9,5},{13,9},{2,14},{6,2},{... | collective-permute-start | bytes 442376 | tf_op jit(solution)/shard_map/ppermute | solution.py:33
  11.2 13.6 %collective-permute-start.3 = (bf16[576,128]{1,0:T(8,128)(2,1)S(1)}, bf16[576,128]{1,0:T(8,128)(2,1)S(1)}, u32[]{:S(2)}, u32[]{:S(2)}) collective-permute-start(bf16[576,128]{1,0:T(8,128)(2,1)S(1)} %collective-permute-done.2.refs_3_), channel_id=1, source_target_pairs={{0,12},{4,0},{8,4},{12,8},{1,13},{5,1},{9,5},{13,9},{2,14},{6,2},{... | collective-permute-start | bytes 442376 | tf_op jit(solution)/shard_map/ppermute | solution.py:33
  15.7 11.1 %collective-permute-start.1 = (bf16[576,128]{1,0:T(8,128)(2,1)S(1)}, bf16[576,128]{1,0:T(8,128)(2,1)S(1)}, u32[]{:S(2)}, u32[]{:S(2)}) collective-permute-start(bf16[576,128]{1,0:T(8,128)(2,1)S(1)} %collective-permute-done.refs_0_), channel_id=1, source_target_pairs={{0,4},{4,8},{8,12},{12,0},{1,5},{5,9},{9,13},{13,1},{2,6},{6,10},{... | collective-permute-start | bytes 442376 | tf_op jit(solution)/shard_map/ppermute | solution.py:33
  16.8 1.4 %copy-start.1 = (bf16[1,384,2048]{2,1,0:T(8,128)(2,1)S(1)}, bf16[1,384,2048]{2,1,0:T(8,128)(2,1)}, u32[]{:S(2)}) copy-start(bf16[1,384,2048]{2,1,0:T(8,128)(2,1)} %down.3) | copy-start | bytes 4718596
  18.2 2.2 %copy-start.3 = (bf16[1024,2048]{1,0:T(8,128)(2,1)S(1)}, bf16[1024,2048]{1,0:T(8,128)(2,1)}, u32[]{:S(2)}) copy-start(bf16[1024,2048]{1,0:T(8,128)(2,1)} %weight.1) | copy-start | bytes 12582916
  20.4 0.9 %copy-start.5 = (bf16[1,64,1024]{2,1,0:T(8,128)(2,1)S(1)}, bf16[1,64,1024]{2,1,0:T(8,128)(2,1)}, u32[]{:S(2)}) copy-start(bf16[1,64,1024]{2,1,0:T(8,128)(2,1)} %param.10) | copy-start | bytes 393220
  21.3 0.7 copy-start.11
  22.0 1.4 %copy-start.6 = (bf16[1,64,1024]{2,1,0:T(8,128)(2,1)S(1)}, bf16[1,64,1024]{2,1,0:T(8,128)(2,1)}, u32[]{:S(2)}) copy-start(bf16[1,64,1024]{2,1,0:T(8,128)(2,1)} %param.10) | copy-start | bytes 393220
  22.0 4.8 %copy-start.4 = (bf16[1024,2048]{1,0:T(8,128)(2,1)S(1)}, bf16[1024,2048]{1,0:T(8,128)(2,1)}, u32[]{:S(2)}) copy-start(bf16[1024,2048]{1,0:T(8,128)(2,1)} %weight.1) | copy-start | bytes 12582916
  23.3 11.3 %copy-start.7 = (bf16[1,16,2048]{2,1,0:T(8,128)(2,1)S(1)}, bf16[1,16,2048]{2,1,0:T(8,128)(2,1)}, u32[]{:S(2)}) copy-start(bf16[1,16,2048]{2,1,0:T(8,128)(2,1)} %param.13) | copy-start | bytes 196612
  23.3 11.3 %copy-start.8 = (f32[2048]{0:T(1024)S(1)}, f32[2048]{0:T(1024)}, u32[]{:S(2)}) copy-start(f32[2048]{0:T(1024)} %param.15) | copy-start | bytes 24580
  23.3 11.2 %copy-start.9 = (s32[1,16,8]{1,2,0:T(8,128)S(1)}, s32[1,16,8]{1,2,0:T(8,128)}, u32[]{:S(2)}) copy-start(s32[1,16,8]{1,2,0:T(8,128)} %param.16) | copy-start | bytes 1540
  23.3 11.2 %copy-start.10 = (f32[1,16,8]{1,2,0:T(8,128)S(1)}, f32[1,16,8]{1,2,0:T(8,128)}, u32[]{:S(2)}) copy-start(f32[1,16,8]{1,2,0:T(8,128)} %param.17) | copy-start | bytes 1540
  29.0 1.9 %collective-permute-start.6 = (bf16[16,2048]{1,0:T(8,128)(2,1)S(1)}, bf16[16,2048]{1,0:T(8,128)(2,1)S(1)}, u32[]{:S(2)}, u32[]{:S(2)}) collective-permute-start(bf16[16,2048]{1,0:T(8,128)(2,1)S(1)} %get-tuple-element.36), channel_id=1, source_target_pairs={{0,1},{1,0},{2,3},{3,2},{4,5},{5,4},{6,7},{7,6},{8,9},{9,8},{10,11... | collective-permute-start | bytes 196616 | tf_op jit(solution)/shard_map/ppermute | solution.py:28
  29.0 4.5 %collective-permute-start.7 = (bf16[16,2048]{1,0:T(8,128)(2,1)S(1)}, bf16[16,2048]{1,0:T(8,128)(2,1)S(1)}, u32[]{:S(2)}, u32[]{:S(2)}) collective-permute-start(bf16[16,2048]{1,0:T(8,128)(2,1)S(1)} %get-tuple-element.37), channel_id=1, source_target_pairs={{0,2},{1,3},{2,0},{3,1},{4,6},{5,7},{6,4},{7,5},{8,10},{9,11},{10,... | collective-permute-start | bytes 196616 | tf_op jit(solution)/shard_map/ppermute | solution.py:28
  30.4 4.1 %collective-permute-start.8 = (bf16[16,2048]{1,0:T(8,128)(2,1)S(1)}, bf16[16,2048]{1,0:T(8,128)(2,1)S(1)}, u32[]{:S(2)}, u32[]{:S(2)}) collective-permute-start(bf16[16,2048]{1,0:T(8,128)(2,1)S(1)} %get-tuple-element.38), channel_id=1, source_target_pairs={{0,3},{1,2},{2,1},{3,0},{4,7},{5,6},{6,5},{7,4},{8,11},{9,10},{10,... | collective-permute-start | bytes 196616 | tf_op jit(solution)/shard_map/ppermute | solution.py:28
  34.6 15.8 %copy-start.2 = (bf16[1,384,2048]{2,1,0:T(8,128)(2,1)S(1)}, bf16[1,384,2048]{2,1,0:T(8,128)(2,1)}, u32[]{:S(2)}) copy-start(bf16[1,384,2048]{2,1,0:T(8,128)(2,1)} %down.3) | copy-start | bytes 4718596
  34.9 4.4 %collective-permute-start.10 = (bf16[16,2176]{1,0:T(8,128)(2,1)S(1)}, bf16[16,2176]{1,0:T(8,128)(2,1)S(1)}, u32[]{:S(2)}, u32[]{:S(2)}) collective-permute-start(bf16[16,2176]{1,0:T(8,128)(2,1)S(1)} %get-tuple-element.40), channel_id=1, source_target_pairs={{0,4},{4,0},{8,12},{12,8},{1,5},{5,1},{9,13},{13,9},{2,6},{6,2},{1... | collective-permute-start | bytes 208904 | tf_op jit(solution)/shard_map/ppermute | solution.py:28
  36.6 6.6 %collective-permute-start.13 = (bf16[16,2176]{1,0:T(8,128)(2,1)S(1)}, bf16[16,2176]{1,0:T(8,128)(2,1)S(1)}, u32[]{:S(2)}, u32[]{:S(2)}) collective-permute-start(bf16[16,2176]{1,0:T(8,128)(2,1)S(1)} %get-tuple-element.40), channel_id=1, source_target_pairs={{0,12},{4,8},{8,4},{12,0},{1,13},{5,9},{9,5},{13,1},{2,14},{6,10},... | collective-permute-start | bytes 208904 | tf_op jit(solution)/shard_map/ppermute | solution.py:28
  37.1 8.1 %collective-permute-start.9 = (bf16[16,2176]{1,0:T(8,128)(2,1)S(1)}, bf16[16,2176]{1,0:T(8,128)(2,1)S(1)}, u32[]{:S(2)}, u32[]{:S(2)}) collective-permute-start(bf16[16,2176]{1,0:T(8,128)(2,1)S(1)} %get-tuple-element.40), channel_id=1, source_target_pairs={{0,8},{4,12},{8,0},{12,4},{1,9},{5,13},{9,1},{13,5},{2,10},{6,14},... | collective-permute-start | bytes 208904 | tf_op jit(solution)/shard_map/ppermute | solution.py:28
  39.2 6.0 %collective-permute-start.11 = (bf16[32,2176]{1,0:T(8,128)(2,1)S(1)}, bf16[32,2176]{1,0:T(8,128)(2,1)S(1)}, u32[]{:S(2)}, u32[]{:S(2)}) collective-permute-start(bf16[32,2176]{1,0:T(8,128)(2,1)S(1)} %pad_maximum_fusion.1), channel_id=1, source_target_pairs={{0,2},{1,3},{2,0},{3,1},{4,6},{5,7},{6,4},{7,5},{8,10},{9,11},{10,... | collective-permute-start | bytes 417800 | tf_op jit(solution)/shard_map/ppermute | solution.py:28
  43.1 4.4 %collective-permute-start.14 = (bf16[16,2176]{1,0:T(8,128)(2,1)S(1)}, bf16[16,2176]{1,0:T(8,128)(2,1)S(1)}, u32[]{:S(2)}, u32[]{:S(2)}) collective-permute-start(bf16[16,2176]{1,0:T(8,128)(2,1)S(1)} %collective-permute-done.13), channel_id=1, source_target_pairs={{0,2},{1,3},{2,0},{3,1},{4,6},{5,7},{6,4},{7,5},{8,10},{9,11},{10,... | collective-permute-start | bytes 208904 | tf_op jit(solution)/shard_map/ppermute | solution.py:28
  45.2 4.4 %collective-permute-start.12 = (bf16[16,2176]{1,0:T(8,128)(2,1)S(1)}, bf16[16,2176]{1,0:T(8,128)(2,1)S(1)}, u32[]{:S(2)}, u32[]{:S(2)}) collective-permute-start(bf16[16,2176]{1,0:T(8,128)(2,1)S(1)} %collective-permute-done.9), channel_id=1, source_target_pairs={{0,2},{1,3},{2,0},{3,1},{4,6},{5,7},{6,4},{7,5},{8,10},{9,11},{10,... | collective-permute-start | bytes 208904 | tf_op jit(solution)/shard_map/ppermute | solution.py:28
  46.7 4.8 %collective-permute-start.16 = (bf16[64,2176]{1,0:T(8,128)(2,1)S(1)}, bf16[64,2176]{1,0:T(8,128)(2,1)S(1)}, u32[]{:S(2)}, u32[]{:S(2)}) collective-permute-start(bf16[64,2176]{1,0:T(8,128)(2,1)S(1)} %pad_maximum_fusion), channel_id=1, source_target_pairs={{0,1},{1,0},{2,3},{3,2},{4,5},{5,4},{6,7},{7,6},{8,9},{9,8},{10,11... | collective-permute-start | bytes 835592 | tf_op jit(solution)/shard_map/ppermute | solution.py:28
  46.7 3.0 %collective-permute-start.18 = (bf16[32,2176]{1,0:T(8,128)(2,1)S(1)}, bf16[32,2176]{1,0:T(8,128)(2,1)S(1)}, u32[]{:S(2)}, u32[]{:S(2)}) collective-permute-start(bf16[32,2176]{1,0:T(8,128)(2,1)S(1)} %collective-permute-done.11), channel_id=1, source_target_pairs={{0,1},{1,0},{2,3},{3,2},{4,5},{5,4},{6,7},{7,6},{8,9},{9,8},{10,11... | collective-permute-start | bytes 417800 | tf_op jit(solution)/shard_map/ppermute | solution.py:28
  49.6 1.8 %collective-permute-start.15 = (bf16[32,2176]{1,0:T(8,128)(2,1)S(1)}, bf16[32,2176]{1,0:T(8,128)(2,1)S(1)}, u32[]{:S(2)}, u32[]{:S(2)}) collective-permute-start(bf16[32,2176]{1,0:T(8,128)(2,1)S(1)} %pad_maximum_fusion.2), channel_id=1, source_target_pairs={{0,1},{1,0},{2,3},{3,2},{4,5},{5,4},{6,7},{7,6},{8,9},{9,8},{10,11... | collective-permute-start | bytes 417800 | tf_op jit(solution)/shard_map/ppermute | solution.py:28
  50.9 2.2 %collective-permute-start.19 = (bf16[32,2048]{1,0:T(8,128)(2,1)S(1)}, bf16[32,2048]{1,0:T(8,128)(2,1)S(1)}, u32[]{:S(2)}, u32[]{:S(2)}) collective-permute-start(bf16[32,2048]{1,0:T(8,128)(2,1)S(1)} %get-tuple-element.47), channel_id=1, source_target_pairs={{0,1},{1,0},{2,3},{3,2},{4,5},{5,4},{6,7},{7,6},{8,9},{9,8},{10,11... | collective-permute-start | bytes 393224 | tf_op jit(solution)/shard_map/ppermute | solution.py:28
  53.0 1.8 %collective-permute-start.22 = (bf16[32,2048]{1,0:T(8,128)(2,1)S(1)}, bf16[32,2048]{1,0:T(8,128)(2,1)S(1)}, u32[]{:S(2)}, u32[]{:S(2)}) collective-permute-start(bf16[32,2048]{1,0:T(8,128)(2,1)S(1)} %get-tuple-element.50), channel_id=1, source_target_pairs={{0,1},{1,0},{2,3},{3,2},{4,5},{5,4},{6,7},{7,6},{8,9},{9,8},{10,11... | collective-permute-start | bytes 393224 | tf_op jit(solution)/shard_map/ppermute | solution.py:28
  53.1 6.4 %collective-permute-start.20 = (bf16[32,2048]{1,0:T(8,128)(2,1)S(1)}, bf16[32,2048]{1,0:T(8,128)(2,1)S(1)}, u32[]{:S(2)}, u32[]{:S(2)}) collective-permute-start(bf16[32,2048]{1,0:T(8,128)(2,1)S(1)} %add_convert_fusion.1), channel_id=1, source_target_pairs={{0,2},{1,3},{2,0},{3,1},{4,6},{5,7},{6,4},{7,5},{8,10},{9,11},{10,... | collective-permute-start | bytes 393224 | tf_op jit(solution)/shard_map/ppermute | solution.py:28
  54.5 2.4 %collective-permute-start.17 = (bf16[64,2048]{1,0:T(8,128)(2,1)S(1)}, bf16[64,2048]{1,0:T(8,128)(2,1)S(1)}, u32[]{:S(2)}, u32[]{:S(2)}) collective-permute-start(bf16[64,2048]{1,0:T(8,128)(2,1)S(1)} %get-tuple-element.44), channel_id=1, source_target_pairs={{0,1},{1,0},{2,3},{3,2},{4,5},{5,4},{6,7},{7,6},{8,9},{9,8},{10,11... | collective-permute-start | bytes 786440 | tf_op jit(solution)/shard_map/ppermute | solution.py:28
  54.8 6.2 %collective-permute-start.23 = (bf16[16,2048]{1,0:T(8,128)(2,1)S(1)}, bf16[16,2048]{1,0:T(8,128)(2,1)S(1)}, u32[]{:S(2)}, u32[]{:S(2)}) collective-permute-start(bf16[16,2048]{1,0:T(8,128)(2,1)S(1)} %get-tuple-element.56), channel_id=1, source_target_pairs={{0,2},{1,3},{2,0},{3,1},{4,6},{5,7},{6,4},{7,5},{8,10},{9,11},{10,... | collective-permute-start | bytes 196616 | tf_op jit(solution)/shard_map/ppermute | solution.py:28
  55.9 6.1 %collective-permute-start.25 = (bf16[16,2048]{1,0:T(8,128)(2,1)S(1)}, bf16[16,2048]{1,0:T(8,128)(2,1)S(1)}, u32[]{:S(2)}, u32[]{:S(2)}) collective-permute-start(bf16[16,2048]{1,0:T(8,128)(2,1)S(1)} %get-tuple-element.57), channel_id=1, source_target_pairs={{0,2},{1,3},{2,0},{3,1},{4,6},{5,7},{6,4},{7,5},{8,10},{9,11},{10,... | collective-permute-start | bytes 196616 | tf_op jit(solution)/shard_map/ppermute | solution.py:28
  59.5 4.3 %collective-permute-start.21 = (bf16[16,2048]{1,0:T(8,128)(2,1)S(1)}, bf16[16,2048]{1,0:T(8,128)(2,1)S(1)}, u32[]{:S(2)}, u32[]{:S(2)}) collective-permute-start(bf16[16,2048]{1,0:T(8,128)(2,1)S(1)} %add_convert_fusion.4), channel_id=1, source_target_pairs={{0,4},{4,0},{8,12},{12,8},{1,5},{5,1},{9,13},{13,9},{2,6},{6,2},{1... | collective-permute-start | bytes 196616 | tf_op jit(solution)/shard_map/ppermute | solution.py:28
  61.0 7.2 %collective-permute-start.24 = (bf16[16,2048]{1,0:T(8,128)(2,1)S(1)}, bf16[16,2048]{1,0:T(8,128)(2,1)S(1)}, u32[]{:S(2)}, u32[]{:S(2)}) collective-permute-start(bf16[16,2048]{1,0:T(8,128)(2,1)S(1)} %add_convert_fusion.3), channel_id=1, source_target_pairs={{0,8},{4,12},{8,0},{12,4},{1,9},{5,13},{9,1},{13,5},{2,10},{6,14},... | collective-permute-start | bytes 196616 | tf_op jit(solution)/shard_map/ppermute | solution.py:28
  63.8 6.1 %collective-permute-start.26 = (bf16[16,2048]{1,0:T(8,128)(2,1)S(1)}, bf16[16,2048]{1,0:T(8,128)(2,1)S(1)}, u32[]{:S(2)}, u32[]{:S(2)}) collective-permute-start(bf16[16,2048]{1,0:T(8,128)(2,1)S(1)} %convert_add_fusion.1), channel_id=1, source_target_pairs={{0,12},{4,8},{8,4},{12,0},{1,13},{5,9},{9,5},{13,1},{2,14},{6,10},... | collective-permute-start | bytes 196616 | tf_op jit(solution)/shard_map/ppermute | solution.py:28

commit v9 on v7

--- a/solution.py
+++ b/solution.py
@@ -137,6 +137,7 @@
 def late_kernel(
     offset,
     fresh_block,
+    sent_count,
     queries,
     keys,
     values,
@@ -145,11 +146,10 @@
     total,
     summed,
     weight,
-    context_out,
-    own_out,
     *rest,
 ):
-    sent_outs, blocks = rest[:-1], rest[-1]
+    context_out, own_out = rest[-sent_count - 3 : -sent_count - 1]
+    sent_outs, blocks = rest[-sent_count - 1 : -1], rest[-1]
     page = page_at(offset)
     part = page_partial(
         stack_heads(queries[...]),
@@ -179,7 +179,7 @@
         out[...] = pick(place ^ step).astype(jnp.bfloat16)
 
 
-def attention(queries, pages, lengths, out_weight, token_block, later):
+def attention(queries, pages, lengths, out_weight, token_block, later, swapped):
     fresh_block, width = queries.shape
     rows = width // HEAD * fresh_block
     count = lax.axis_size("ctx")
@@ -230,13 +230,13 @@
         )(queries, page_lengths, *operands, *state)
     block = jax.ShapeDtypeStruct((token_block, model_width), jnp.bfloat16)
     outs = pl.pallas_call(
-        functools.partial(late_kernel, last[0], fresh_block),
+        functools.partial(late_kernel, last[0], fresh_block, exp_count - 1),
         out_shape=(
             jax.ShapeDtypeStruct(queries.shape, jnp.bfloat16),
             jax.ShapeDtypeStruct(block.shape, jnp.float32),
         )
         + (block,) * (exp_count - 1),
-        in_specs=whole_specs(8),
+        in_specs=whole_specs(8) + [pl.BlockSpec(memory_space=pl.ANY)] * len(swapped),
         out_specs=tuple(whole_specs(1 + exp_count)),
         scratch_shapes=[pltpu.VMEM((fresh_block, model_width), jnp.float32)],
         compiler_params=LIMIT,
@@ -245,7 +245,7 @@
             bytes_accessed=6 << 20,
             transcendentals=0,
         ),
-    )(queries, last[1], last[2], page_lengths, *state, out_weight)
+    )(queries, last[1], last[2], page_lengths, *state, out_weight, *swapped)
     return outs[0], outs[1], outs[2:]
 
 
@@ -288,98 +288,91 @@
     )(*parts, residual, norm_gain[None], ids, scores)
 
 
-def down_kernel(inner, rows, down, keep_out, *send_out):
-    expert = lax.axis_index("ctx") * lax.axis_size("exp") + lax.axis_index("exp")
-    gate = inner[0]
-    activated = (gate / (1.0 + jnp.exp(-gate)) * inner[1]).astype(jnp.bfloat16)
-    piece = jnp.dot(activated, down[0], preferred_element_type=jnp.float32)
-    dense = rows[:, piece.shape[1] :].astype(jnp.float32)
+def down_kernel(offsets, rows, *refs):
+    count = len(offsets)
+    inners, downs, outs = refs[:count], refs[count : 2 * count], refs[2 * count :]
+    dense = rows[:, outs[0].shape[1] :].astype(jnp.float32)
     lane = lax.broadcasted_iota(jnp.int32, dense.shape, 1)
-    scale = jnp.sum(jnp.where(lane == expert, dense, 0.0), axis=1, keepdims=True)
-    result = piece.astype(jnp.bfloat16).astype(jnp.float32) * scale
-    size = keep_out.shape[0]
-    keep_out[...] = result[:size]
-    for out in send_out:
-        out[...] = result[size:].astype(jnp.bfloat16)
-
-
-def expert_apply(rows, gate_up, down, size):
-    _, hidden, width = down.shape
-    total = rows.shape[0]
-    half = max(size, total // 2)
-    inner = jnp.einsum(
-        "nd,dgh->gnh", rows[:, :width], gate_up[0], preferred_element_type=jnp.float32
-    )
-    shapes = [jax.ShapeDtypeStruct((half, width), jnp.float32)]
-    if total > half:
-        shapes.append(jax.ShapeDtypeStruct((total - half, width), jnp.bfloat16))
-    outs = pl.pallas_call(
-        down_kernel,
-        out_shape=shapes,
-        in_specs=whole_specs(3),
-        out_specs=whole_specs(len(shapes)),
+    base = lax.axis_index("ctx") * lax.axis_size("exp")
+    total = 0.0
+    for offset, inner, down in zip(offsets, inners, downs):
+        gate = inner[0]
+        activated = (gate / (1.0 + jnp.exp(-gate)) * inner[1]).astype(jnp.bfloat16)
+        piece = jnp.dot(activated, down[0], preferred_element_type=jnp.float32)
+        expert = base + (lax.axis_index("exp") ^ offset)
+        scale = jnp.sum(jnp.where(lane == expert, dense, 0.0), axis=1, keepdims=True)
+        total = total + piece.astype(jnp.bfloat16).astype(jnp.float32) * scale
+    start = 0
+    for out in outs:
+        out[...] = total[start : start + out.shape[0]].astype(out.dtype)
+        start += out.shape[0]
+
+
+def expert_apply(groups, kinds, weights):
+    count = len(weights)
+    rows = jnp.concatenate(groups, axis=0)
+    _, hidden, width = weights[0][2].shape
+    inners = [
+        jnp.einsum("nd,dgh->gnh", rows[:, :width], gate_up[0], preferred_element_type=jnp.float32)
+        for _, gate_up, _ in weights
+    ]
+
+    return pl.pallas_call(
+        functools.partial(down_kernel, [offset for offset, _, _ in weights]),
+        out_shape=[
+            jax.ShapeDtypeStruct((group.shape[0], width), kind)
+            for group, kind in zip(groups, kinds)
+        ],
+        in_specs=whole_specs(1 + 2 * count),
+        out_specs=whole_specs(len(groups)),
         compiler_params=LIMIT,
         cost_estimate=pl.CostEstimate(
-            flops=2 * total * width * hidden, bytes_accessed=2 << 20, transcendentals=0
+            flops=2 * count * rows.shape[0] * width * hidden,
+            bytes_accessed=2 << 20,
+            transcendentals=0,
         ),
-    )(inner, rows, down)
-    return outs[0], (outs[1] if total > half else None)
-
-
-def return_near(keep, send, near):
-    for stride in reversed(near):
-        keep = keep + swap(send, "exp", stride).astype(jnp.float32)
-        half = keep.shape[0] // 2
-        if stride != near[0]:
-            keep, send = keep[:half], keep[half:].astype(jnp.bfloat16)
-    return keep
+    )(rows, *inners, *[down for _, _, down in weights])
+
+
+def near_weights(gate_up, down):
+    held = [(0, gate_up, down)]
+    for stride in strides(lax.axis_size("exp"))[1:]:
+        held = held + [
+            (offset ^ stride, swap(first, "exp", stride), swap(second, "exp", stride))
+            for offset, first, second in held
+        ]
+    return held
 
 
 def chunks_of(count):
-    chunks = [range((count + 1) // 2), range((count + 1) // 2, count)]
+    chunks = [range((count + 1) // 2, count), range((count + 1) // 2)]
     return [list(chunk) for chunk in chunks if len(chunk)]
 
 
-def mixture_of(rows, gate_up, down):
+def mixture_of(rows, weights):
     tokens = rows.shape[0]
-    exp_strides = strides(lax.axis_size("exp"))
-    far, near = exp_strides[:1], exp_strides[1:]
+    far = strides(lax.axis_size("exp"))[:1]
     chunks = chunks_of(lax.axis_size("ctx"))
 
-    def gather(piece):
-        held = [piece]
-        for stride in near:
-            held = held + [swap(part, "exp", stride) for part in held]
-        return jnp.concatenate(held, axis=0)
-
-    def results(held, size):
-        return return_near(*expert_apply(held, gate_up, down, size), near)
-
-    sent = []
-    for chunk in chunks:
-        blocks = [rows if offset == 0 else swap(rows, "ctx", offset) for offset in chunk]
-        sent.append(jnp.concatenate(blocks, axis=0))
+    joined = [
+        jnp.concatenate(
+            [rows if offset == 0 else swap(rows, "ctx", offset) for offset in chunk], axis=0
+        )
+        for chunk in chunks
+    ]
     crossed = []
-    for piece in sent:
-        if crossed:
-            piece, _ = lax.optimization_barrier((piece, arrived))
-        arrived = [swap(piece, "exp", stride) for stride in far]
-        crossed.append([gather(part) for part in arrived])
-    everything = jnp.concatenate(sent, axis=0)
-    everything, _ = lax.optimization_barrier((everything, crossed[0]))
-    home = results(gather(everything), everything.shape[0])
-    homes, start = [], 0
-    for piece in sent:
-        homes.append(home[start : start + piece.shape[0]])
-        start += piece.shape[0]
-    homes = lax.optimization_barrier(homes)
+    for piece in joined if far else []:
+        crossed.append(swap(piece, "exp", far[0]))
+    *homes, first = expert_apply(
+        joined + (crossed or joined)[:1], [jnp.float32] * len(joined) + [jnp.bfloat16], weights
+    )
     total, arrived = None, []
-    for chunk, value, away in zip(chunks, homes, crossed):
-        for part in away:
-            other = results(part, value.shape[0]).astype(jnp.bfloat16)
+    for number, (chunk, value) in enumerate(zip(chunks, homes)):
+        if far:
+            other = first
+            if number:
+                (other,) = expert_apply(crossed[number : number + 1], [jnp.bfloat16], weights)
             value = value + swap(other, "exp", far[0]).astype(jnp.float32)
-        if arrived:
-            value, _ = lax.optimization_barrier((value, arrived[0]))
         for position, offset in enumerate(chunk):
             block = value[position * tokens : (position + 1) * tokens]
             if offset == 0:
@@ -411,6 +404,8 @@
     token_block, model_width = residual_in.shape[1:]
     token_count = requests * token_block
 
+    weights = near_weights(expert_input, expert_output)
+    swapped = [part for _, *pair in weights[1:] for part in pair]
     contexts, owns, sents = [], [], []
     for r in range(requests):
         context, own, sent = attention(
@@ -420,6 +415,7 @@
             out_weight,
             token_block,
             (expert_output,),
+            swapped if r == 0 else (),
         )
         contexts.append(context)
         owns.append(own)
@@ -455,7 +451,7 @@
         normed = lax.all_gather(normed, "rep", axis=1, tiled=True)
         normed = normed.reshape(token_count, -1)
 
-    mixture = mixture_of(normed, expert_input, expert_output)
+    mixture = mixture_of(normed, weights)
     mixture = mixture.reshape(requests, token_block, model_width)
     if rep_count > 1:
         mixture = lax.psum_scatter(

time: 69.5 us -> 67.6 us (0.973)
  starting transfers between devices: 31.8 us -> 26.7 us
  waiting for transfers between devices: 20.7 us -> 23.5 us
    ppermute x6, waiting for transfers between devices: 2.54 us -> 5.5 us  [shift(): lax.ppermute(value, axis, [(i, (i + step) % count) for i in range(count)])]
    ppermute x6, starting transfers between devices: 14.4 us -> 11.6 us  [shift(): lax.ppermute(value, axis, [(i, (i + step) % count) for i in range(count)])]
    ppermute x19 -> x15, starting transfers between devices: 17.4 us -> 15.1 us  [swap(): lax.ppermute(value, axis, [(i, i ^ stride) for i in range(lax.axis_size(a...]
    dot_general x3 -> x4, matrix products: 1.95 us -> 2.58 us  [expert_apply(): jnp.einsum('nd,dgh->gnh', rows[:, :width], gate_up[0], preferred_element_...]
    ppermute x19 -> x15, waiting for transfers between devices: 18.2 us -> 18 us  [swap(): lax.ppermute(value, axis, [(i, i ^ stride) for i in range(lax.axis_size(a...]
    pallas_call x4 -> x3, Pallas kernels: 3.42 us -> 3.59 us  [the longest x1 2.17 us: attention(): pl.pallas_call(functools.partial(late_kernel, last[0], fresh_block, exp_c...]
    unnamed x28 -> x29, local copies, waits for them, and re-layouts: 6.4 us -> 6.33 us
  transfers between devices with their start and end apart: 25 -> 21, of which waited for: 15 -> 11; matrix products, arithmetic and copies ran while one was open for 3% -> 6% of each run, Pallas kernels for 6% -> 6%
where the time goes in v9:
time: 67.6 us; the launch traced here: 67.3 us
  starting transfers between devices  26.7 us (39%)
  waiting for transfers between devices  23.5 us (35%)
  Pallas kernels  6.57 us (10%)
  local copies, waits for them, and re-layouts  6.39 us (9%)
  matrix products  2.58 us (4%)
  between operations  0.85 us (1%)
  other arithmetic  0.74 us (1%)
    ppermute x15, waiting for transfers between devices, swap(): lax.ppermute(value, axis, [(i, i ^ stride) for i in range(lax.axis_size(a...  18 us
    ppermute x15, starting transfers between devices, swap(): lax.ppermute(value, axis, [(i, i ^ stride) for i in range(lax.axis_size(a...  15.1 us
    ppermute x6, starting transfers between devices, shift(): lax.ppermute(value, axis, [(i, (i + step) % count) for i in range(count)])  11.6 us
    unnamed x29, local copies, waits for them, and re-layouts  6.33 us
    ppermute x6, waiting for transfers between devices, shift(): lax.ppermute(value, axis, [(i, (i + step) % count) for i in range(count)])  5.5 us
    dot_general x4, matrix products, expert_apply(): jnp.einsum('nd,dgh->gnh', rows[:, :width], gate_up[0], preferred_element_...  2.58 us
    pallas_call x1, Pallas kernels, attention(): pl.pallas_call(functools.partial(late_kernel, last[0], fresh_block, exp_c...  2.17 us
    pallas_call x1, Pallas kernels, attention(): pl.pallas_call(functools.partial(middle_kernel, [offset for offset, _, _...  1.43 us
  transfers between devices with their start and end apart: 21, of which 11 were waited for; matrix products, arithmetic and copies ran while one was open for 6% of the time, Pallas kernels for 6%

profile of v9, /device:TPU:0, one launch (start us, length us, event | category | flops | bytes accessed | tf_op | source)
XLA Modules:
  0.0 67.3 jit_solution(1580644038983506595)
XLA Ops:
  0.6 0.5 collective-permute-start.6
  1.1 0.1 collective-permute-start.7
  1.2 1.0 %copy.34 = bf16[1,576,2,128]{3,1,2,0:T(8,128)(2,1)S(1)} copy(bf16[1,576,2,128]{3,2,1,0:T(2,128)(2,1)} %param.11) | data formatting | bytes 589824 | tf_op args[1]
  2.3 3.1 %collective-permute-start.4 = (bf16[576,128]{1,0:T(8,128)(2,1)S(1)}, bf16[576,128]{1,0:T(8,128)(2,1)S(1)}, u32[]{:S(2)}, u32[]{:S(2)}) collective-permute-start(bf16[576,128]{1,0:T(8,128)(2,1)S(1)} %get-tuple-element.36.values), channel_id=1, source_target_pairs={{0,4},{4,8},{8,12},{12,0},{1,5},{5,9},{9,13},{13,1},{2,6},{6,10},{... | collective-permute-start | bytes 442376 | tf_op jit(solution)/shard_map/ppermute | solution.py:33
  5.3 2.1 %collective-permute-start.2 = (bf16[576,128]{1,0:T(8,128)(2,1)S(1)}, bf16[576,128]{1,0:T(8,128)(2,1)S(1)}, u32[]{:S(2)}, u32[]{:S(2)}) collective-permute-start(bf16[576,128]{1,0:T(8,128)(2,1)S(1)} %get-tuple-element.36.values), channel_id=1, source_target_pairs={{0,12},{4,0},{8,4},{12,8},{1,13},{5,1},{9,5},{13,9},{2,14},{6,2},{... | collective-permute-start | bytes 442376 | tf_op jit(solution)/shard_map/ppermute | solution.py:33
  7.4 4.6 %collective-permute-done.4.refs_1_ = bf16[576,128]{1,0:T(8,128)(2,1)S(1)} collective-permute-done((bf16[576,128]{1,0:T(8,128)(2,1)S(1)}, bf16[576,128]{1,0:T(8,128)(2,1)S(1)}, u32[]{:S(2)}, u32[]{:S(2)}) %collective-permute-start.4) | collective-permute-done | bytes 147488 | tf_op jit(solution)/shard_map/ppermute | solution.py:33
  12.0 5.2 %collective-permute-start.5 = (bf16[576,128]{1,0:T(8,128)(2,1)S(1)}, bf16[576,128]{1,0:T(8,128)(2,1)S(1)}, u32[]{:S(2)}, u32[]{:S(2)}) collective-permute-start(bf16[576,128]{1,0:T(8,128)(2,1)S(1)} %get-tuple-element.37.keys), channel_id=1, source_target_pairs={{0,12},{4,0},{8,4},{12,8},{1,13},{5,1},{9,5},{13,9},{2,14},{6,2},{... | collective-permute-start | bytes 442376 | tf_op jit(solution)/shard_map/ppermute | solution.py:33
  17.2 0.5 collective-permute-start.3
  17.7 0.7 %collective-permute-done.refs_0_ = bf16[576,128]{1,0:T(8,128)(2,1)S(1)} collective-permute-done((bf16[576,128]{1,0:T(8,128)(2,1)S(1)}, bf16[576,128]{1,0:T(8,128)(2,1)S(1)}, u32[]{:S(2)}, u32[]{:S(2)}) %collective-permute-start) | collective-permute-done | bytes 147488 | tf_op jit(solution)/shard_map/ppermute | solution.py:33
  18.4 0.8 %collective-permute-start.1 = (bf16[576,128]{1,0:T(8,128)(2,1)S(1)}, bf16[576,128]{1,0:T(8,128)(2,1)S(1)}, u32[]{:S(2)}, u32[]{:S(2)}) collective-permute-start(bf16[576,128]{1,0:T(8,128)(2,1)S(1)} %collective-permute-done.refs_0_), channel_id=1, source_target_pairs={{0,4},{4,8},{8,12},{12,0},{1,5},{5,9},{9,13},{13,1},{2,6},{6,10},{... | collective-permute-start | bytes 442376 | tf_op jit(solution)/shard_map/ppermute | solution.py:33
  19.2 1.4 %copy-done = bf16[1,384,2048]{2,1,0:T(8,128)(2,1)S(1)} copy-done((bf16[1,384,2048]{2,1,0:T(8,128)(2,1)S(1)}, bf16[1,384,2048]{2,1,0:T(8,128)(2,1)}, u32[]{:S(2)}) %copy-start) | copy-done | bytes 1572888
  20.7 2.2 %copy-done.2 = bf16[1024,2048]{1,0:T(8,128)(2,1)S(1)} copy-done((bf16[1024,2048]{1,0:T(8,128)(2,1)S(1)}, bf16[1024,2048]{1,0:T(8,128)(2,1)}, u32[]{:S(2)}) %copy-start.2) | copy-done | bytes 4194328
  22.8 0.9 %copy-done.4 = bf16[1,64,1024]{2,1,0:T(8,128)(2,1)S(1)} copy-done((bf16[1,64,1024]{2,1,0:T(8,128)(2,1)S(1)}, bf16[1,64,1024]{2,1,0:T(8,128)(2,1)}, u32[]{:S(2)}) %copy-start.4) | copy-done | bytes 131096
  23.7 0.7 copy-done.10
  24.4 1.3 %shard_map.113 = (f32[1,512]{1,0:T(1,128)S(1)}, f32[1,512]{1,0:T(1,128)S(1)}, f32[128,512]{1,0:T(8,128)S(1)}, s32[4,128]{1,0:T(4,128)S(1)}) custom-call(s32[4]{0:T(128)S(1)} %bitcast.47, bf16[64,1024]{1,0:T(8,128)(2,1)S(1)} %bitcast.40, bf16[576,128]{1,0:T(8,128)(2,1)S(1)} %get-tuple-element.37.keys, bf16[576,128]{1,0:T(8,128)(2,1)S(1)} %get-tuple-element.36.values, ...), custom_call_target="tpu_custom_call" | custom-call | flops 2415919104 | bytes 8388608 | tf_op jit(solution)/shard_map/pallas_call | solution.py:206
  25.7 1.4 %shard_map.114 = (f32[1,512]{1,0:T(1,128)S(1)}, f32[1,512]{1,0:T(1,128)S(1)}, f32[128,512]{1,0:T(8,128)S(1)}) custom-call(bf16[64,1024]{1,0:T(8,128)(2,1)S(1)} %bitcast.41, s32[4,128]{1,0:T(4,128)S(1)} %get-tuple-element.19.lengths, bf16[576,128]{1,0:T(8,128)(2,1)S(1)} %collective-permute-done.refs_0_, bf16[576,128]{1,0:T(8,128)(2,1)S(1)} %collective-permute-done.4.refs_1_, ...), custom_call_target="tpu_custom_call" | custom-call | flops 301989888 | bytes 2097152 | tf_op jit(solution)/shard_map/pallas_call | solution.py:221
  27.2 0.1 collective-permute-done.1.keys
  27.3 0.0 copy-start.6
  27.3 0.0 copy-start.7
  27.4 2.2 %shard_map.115 = (bf16[64,1024]{1,0:T(8,128)(2,1)}, f32[16,2048]{1,0:T(8,128)S(1)}, bf16[16,2048]{1,0:T(8,128)(2,1)S(1)}, bf16[16,2048]{1,0:T(8,128)(2,1)S(1)}, bf16[16,2048]{1,0:T(8,128)(2,1)S(1)}) custom-call(bf16[64,1024]{1,0:T(8,128)(2,1)S(1)} %bitcast.42, bf16[576,128]{1,0:T(8,128)(2,1)S(1)} %collective-permute-done.1.keys, ...), custom_call_target="tpu_custom_call" | custom-call | flops 419430400 | bytes 6291456 | tf_op jit(solution)/shard_map/pallas_call | solution.py:232
  29.6 1.5 %collective-permute-start.9 = (bf16[16,2048]{1,0:T(8,128)(2,1)S(1)}, bf16[16,2048]{1,0:T(8,128)(2,1)S(1)}, u32[]{:S(2)}, u32[]{:S(2)}) collective-permute-start(bf16[16,2048]{1,0:T(8,128)(2,1)S(1)} %get-tuple-element.29), channel_id=1, source_target_pairs={{0,2},{1,3},{2,0},{3,1},{4,6},{5,7},{6,4},{7,5},{8,10},{9,11},{10,... | collective-permute-start | bytes 196616 | tf_op jit(solution)/shard_map/ppermute | solution.py:28
  31.0 0.4 collective-permute-start.10
  31.4 2.7 %collective-permute-done.9.refs_2_ = bf16[16,2048]{1,0:T(8,128)(2,1)S(1)} collective-permute-done((bf16[16,2048]{1,0:T(8,128)(2,1)S(1)}, bf16[16,2048]{1,0:T(8,128)(2,1)S(1)}, u32[]{:S(2)}, u32[]{:S(2)}) %collective-permute-start.9) | collective-permute-done | bytes 65568 | tf_op jit(solution)/shard_map/ppermute | solution.py:28
  34.1 1.1 %collective-permute-done.10.refs_3_ = bf16[16,2048]{1,0:T(8,128)(2,1)S(1)} collective-permute-done((bf16[16,2048]{1,0:T(8,128)(2,1)S(1)}, bf16[16,2048]{1,0:T(8,128)(2,1)S(1)}, u32[]{:S(2)}, u32[]{:S(2)}) %collective-permute-start.10) | collective-permute-done | bytes 65568 | tf_op jit(solution)/shard_map/ppermute | solution.py:28
  35.2 0.3 shard_map.116
  35.5 0.6 collective-permute-start.13
  36.1 4.8 %collective-permute-start.12 = (bf16[16,2176]{1,0:T(8,128)(2,1)S(1)}, bf16[16,2176]{1,0:T(8,128)(2,1)S(1)}, u32[]{:S(2)}, u32[]{:S(2)}) collective-permute-start(bf16[16,2176]{1,0:T(8,128)(2,1)S(1)} %get-tuple-element.32), channel_id=1, source_target_pairs={{0,12},{4,8},{8,4},{12,0},{1,13},{5,9},{9,5},{13,1},{2,14},{6,10},... | collective-permute-start | bytes 208904 | tf_op jit(solution)/shard_map/ppermute | solution.py:28
  40.9 1.5 %collective-permute-start.15 = (bf16[32,2176]{1,0:T(8,128)(2,1)S(1)}, bf16[32,2176]{1,0:T(8,128)(2,1)S(1)}, u32[]{:S(2)}, u32[]{:S(2)}) collective-permute-start(bf16[32,2176]{1,0:T(8,128)(2,1)S(1)} %pad_maximum_fusion.1), channel_id=1, source_target_pairs={{0,2},{1,3},{2,0},{3,1},{4,6},{5,7},{6,4},{7,5},{8,10},{9,11},{10,... | collective-permute-start | bytes 417800 | tf_op jit(solution)/shard_map/ppermute | solution.py:28
  42.3 3.0 %collective-permute-done.12 = bf16[16,2176]{1,0:T(8,128)(2,1)S(1)} collective-permute-done((bf16[16,2176]{1,0:T(8,128)(2,1)S(1)}, bf16[16,2176]{1,0:T(8,128)(2,1)S(1)}, u32[]{:S(2)}, u32[]{:S(2)}) %collective-permute-start.12) | collective-permute-done | bytes 69664 | tf_op jit(solution)/shard_map/ppermute | solution.py:28
  45.4 2.1 %collective-permute-done.11 = bf16[16,2176]{1,0:T(8,128)(2,1)S(1)} collective-permute-done((bf16[16,2176]{1,0:T(8,128)(2,1)S(1)}, bf16[16,2176]{1,0:T(8,128)(2,1)S(1)}, u32[]{:S(2)}, u32[]{:S(2)}) %collective-permute-start.11) | collective-permute-done | bytes 69664 | tf_op jit(solution)/shard_map/ppermute | solution.py:28
  47.5 1.6 %collective-permute-start.14 = (bf16[32,2176]{1,0:T(8,128)(2,1)S(1)}, bf16[32,2176]{1,0:T(8,128)(2,1)S(1)}, u32[]{:S(2)}, u32[]{:S(2)}) collective-permute-start(bf16[32,2176]{1,0:T(8,128)(2,1)S(1)} %pad_maximum_fusion), channel_id=1, source_target_pairs={{0,2},{1,3},{2,0},{3,1},{4,6},{5,7},{6,4},{7,5},{8,10},{9,11},{10,... | collective-permute-start | bytes 417800 | tf_op jit(solution)/shard_map/ppermute | solution.py:28
  49.2 0.6 fusion.17.refs_1_
  49.8 0.7 fusion.14.refs_0_
  50.5 0.1 copy-done.1
  50.6 0.7 %shard_map.118 = bf16[32,2048]{1,0:T(8,128)(2,1)S(1)} custom-call(bf16[32,2176]{1,0:T(8,128)(2,1)S(1)} %collective-permute-done.15.rows, f32[2,32,384]{2,1,0:T(8,128)S(1)} %fusion.14.refs_0_, f32[2,32,384]{2,1,0:T(8,128)S(1)} %fusion.17.refs_1_, bf16[1,384,2048]{2,1,0:T(8,128)(2,1)S(1)} %copy-done.1, ...), custom_call_target="tpu_custom_call" | custom-call | flops 100663296 | bytes 2097152 | tf_op jit(solution)/shard_map/pallas_call | solution.py:320
  51.2 0.6 collective-permute-start.16
  51.8 1.4 %collective-permute-done.14 = bf16[32,2176]{1,0:T(8,128)(2,1)S(1)} collective-permute-done((bf16[32,2176]{1,0:T(8,128)(2,1)S(1)}, bf16[32,2176]{1,0:T(8,128)(2,1)S(1)}, u32[]{:S(2)}, u32[]{:S(2)}) %collective-permute-start.14) | collective-permute-done | bytes 139296 | tf_op jit(solution)/shard_map/ppermute | solution.py:28
  53.2 0.6 fusion.11.refs_1_
  53.8 0.6 fusion.8.refs_0_
  54.5 0.7 %shard_map.117 = (f32[32,2048]{1,0:T(8,128)S(1)}, f32[32,2048]{1,0:T(8,128)S(1)}, bf16[32,2048]{1,0:T(8,128)(2,1)S(1)}) custom-call(bf16[96,2176]{1,0:T(8,128)(2,1)S(1)} %constant_dynamic-update-slice_fusion.rows, f32[2,96,384]{2,1,0:T(8,128)S(1)} %fusion.8.refs_0_, f32[2,96,384]{2,1,0:T(8,128)S(1)} %fusion.11.refs_1_, bf16[1,384,2048]{2,1,0:T(8,128)(2,1)S(1)} %copy-done.1, ...), custom_call_target="tpu_custom_call" | custom-call | flops 301989888 | bytes 2097152 | tf_op jit(solution)/shard_map/pallas_call | solution.py:320
  55.2 2.0 %collective-permute-start.17 = (bf16[32,2048]{1,0:T(8,128)(2,1)S(1)}, bf16[32,2048]{1,0:T(8,128)(2,1)S(1)}, u32[]{:S(2)}, u32[]{:S(2)}) collective-permute-start(bf16[32,2048]{1,0:T(8,128)(2,1)S(1)} %get-tuple-element.35), channel_id=1, source_target_pairs={{0,2},{1,3},{2,0},{3,1},{4,6},{5,7},{6,4},{7,5},{8,10},{9,11},{10,... | collective-permute-start | bytes 393224 | tf_op jit(solution)/shard_map/ppermute | solution.py:28
  57.3 0.1 collective-permute-start.20
  57.4 2.9 %collective-permute-done.17 = bf16[32,2048]{1,0:T(8,128)(2,1)S(1)} collective-permute-done((bf16[32,2048]{1,0:T(8,128)(2,1)S(1)}, bf16[32,2048]{1,0:T(8,128)(2,1)S(1)}, u32[]{:S(2)}, u32[]{:S(2)}) %collective-permute-start.17) | collective-permute-done | bytes 131104 | tf_op jit(solution)/shard_map/ppermute | solution.py:28
  60.3 0.1 collective-permute-start.18
  60.4 1.5 %collective-permute-start.19 = (bf16[16,2048]{1,0:T(8,128)(2,1)S(1)}, bf16[16,2048]{1,0:T(8,128)(2,1)S(1)}, u32[]{:S(2)}, u32[]{:S(2)}) collective-permute-start(bf16[16,2048]{1,0:T(8,128)(2,1)S(1)} %get-tuple-element.39), channel_id=1, source_target_pairs={{0,12},{4,8},{8,4},{12,0},{1,13},{5,9},{9,5},{13,1},{2,14},{6,10},... | collective-permute-start | bytes 196616 | tf_op jit(solution)/shard_map/ppermute | solution.py:28
  61.9 3.7 %collective-permute-done.18 = bf16[16,2048]{1,0:T(8,128)(2,1)S(1)} collective-permute-done((bf16[16,2048]{1,0:T(8,128)(2,1)S(1)}, bf16[16,2048]{1,0:T(8,128)(2,1)S(1)}, u32[]{:S(2)}, u32[]{:S(2)}) %collective-permute-start.18) | collective-permute-done | bytes 65568 | tf_op jit(solution)/shard_map/ppermute | solution.py:28
  65.5 1.1 %collective-permute-done.19 = bf16[16,2048]{1,0:T(8,128)(2,1)S(1)} collective-permute-done((bf16[16,2048]{1,0:T(8,128)(2,1)S(1)}, bf16[16,2048]{1,0:T(8,128)(2,1)S(1)}, u32[]{:S(2)}, u32[]{:S(2)}) %collective-permute-start.19) | collective-permute-done | bytes 65568 | tf_op jit(solution)/shard_map/ppermute | solution.py:28
  66.6 0.7 fusion.24
  (42 shorter events, 0.2 us)
Async XLA Ops:
  0.6 26.7 %collective-permute-start.6 = (bf16[1,2048,2,384]{3,2,1,0:T(2,128)(2,1)}, bf16[1,2048,2,384]{3,2,1,0:T(2,128)(2,1)S(1)}, u32[]{:S(2)}, u32[]{:S(2)}) collective-permute-start(bf16[1,2048,2,384]{3,2,1,0:T(2,128)(2,1)} %param.18), channel_id=1, source_target_pairs={{0,1},{1,0},{2,3},{3,2},{4,5},{5,4},{6,7},{7,6},{8,9},{9,8},{10,11... | collective-permute-start | bytes 9437192 | tf_op jit(solution)/shard_map/ppermute | solution.py:28
  1.1 26.2 %collective-permute-start.7 = (bf16[1,384,2048]{2,1,0:T(8,128)(2,1)}, bf16[1,384,2048]{2,1,0:T(8,128)(2,1)S(1)}, u32[]{:S(2)}, u32[]{:S(2)}) collective-permute-start(bf16[1,384,2048]{2,1,0:T(8,128)(2,1)} %refs_2_.3), channel_id=1, source_target_pairs={{0,1},{1,0},{2,3},{3,2},{4,5},{5,4},{6,7},{7,6},{8,9},{9,8},{10,11... | collective-permute-start | bytes 4718600 | tf_op jit(solution)/shard_map/ppermute | solution.py:28
  2.3 9.8 %collective-permute-start.4 = (bf16[576,128]{1,0:T(8,128)(2,1)S(1)}, bf16[576,128]{1,0:T(8,128)(2,1)S(1)}, u32[]{:S(2)}, u32[]{:S(2)}) collective-permute-start(bf16[576,128]{1,0:T(8,128)(2,1)S(1)} %get-tuple-element.36.values), channel_id=1, source_target_pairs={{0,4},{4,8},{8,12},{12,0},{1,5},{5,9},{9,13},{13,1},{2,6},{6,10},{... | collective-permute-start | bytes 442376 | tf_op jit(solution)/shard_map/ppermute | solution.py:33
  5.3 11.9 %collective-permute-start.2 = (bf16[576,128]{1,0:T(8,128)(2,1)S(1)}, bf16[576,128]{1,0:T(8,128)(2,1)S(1)}, u32[]{:S(2)}, u32[]{:S(2)}) collective-permute-start(bf16[576,128]{1,0:T(8,128)(2,1)S(1)} %get-tuple-element.36.values), channel_id=1, source_target_pairs={{0,12},{4,0},{8,4},{12,8},{1,13},{5,1},{9,5},{13,9},{2,14},{6,2},{... | collective-permute-start | bytes 442376 | tf_op jit(solution)/shard_map/ppermute | solution.py:33
  7.4 11.0 %collective-permute-start = (bf16[576,128]{1,0:T(8,128)(2,1)S(1)}, bf16[576,128]{1,0:T(8,128)(2,1)S(1)}, u32[]{:S(2)}, u32[]{:S(2)}) collective-permute-start(bf16[576,128]{1,0:T(8,128)(2,1)S(1)} %get-tuple-element.37.keys), channel_id=1, source_target_pairs={{0,4},{4,8},{8,12},{12,0},{1,5},{5,9},{9,13},{13,1},{2,6},{6,10},{... | collective-permute-start | bytes 442376 | tf_op jit(solution)/shard_map/ppermute | solution.py:33
  12.0 13.7 %collective-permute-start.5 = (bf16[576,128]{1,0:T(8,128)(2,1)S(1)}, bf16[576,128]{1,0:T(8,128)(2,1)S(1)}, u32[]{:S(2)}, u32[]{:S(2)}) collective-permute-start(bf16[576,128]{1,0:T(8,128)(2,1)S(1)} %get-tuple-element.37.keys), channel_id=1, source_target_pairs={{0,12},{4,0},{8,4},{12,8},{1,13},{5,1},{9,5},{13,9},{2,14},{6,2},{... | collective-permute-start | bytes 442376 | tf_op jit(solution)/shard_map/ppermute | solution.py:33
  17.2 10.0 %collective-permute-start.3 = (bf16[576,128]{1,0:T(8,128)(2,1)S(1)}, bf16[576,128]{1,0:T(8,128)(2,1)S(1)}, u32[]{:S(2)}, u32[]{:S(2)}) collective-permute-start(bf16[576,128]{1,0:T(8,128)(2,1)S(1)} %collective-permute-done.2.refs_3_), channel_id=1, source_target_pairs={{0,12},{4,0},{8,4},{12,8},{1,13},{5,1},{9,5},{13,9},{2,14},{6,2},{... | collective-permute-start | bytes 442376 | tf_op jit(solution)/shard_map/ppermute | solution.py:33
  18.4 8.9 %collective-permute-start.1 = (bf16[576,128]{1,0:T(8,128)(2,1)S(1)}, bf16[576,128]{1,0:T(8,128)(2,1)S(1)}, u32[]{:S(2)}, u32[]{:S(2)}) collective-permute-start(bf16[576,128]{1,0:T(8,128)(2,1)S(1)} %collective-permute-done.refs_0_), channel_id=1, source_target_pairs={{0,4},{4,8},{8,12},{12,0},{1,5},{5,9},{9,13},{13,1},{2,6},{6,10},{... | collective-permute-start | bytes 442376 | tf_op jit(solution)/shard_map/ppermute | solution.py:33
  19.2 1.4 %copy-start = (bf16[1,384,2048]{2,1,0:T(8,128)(2,1)S(1)}, bf16[1,384,2048]{2,1,0:T(8,128)(2,1)}, u32[]{:S(2)}) copy-start(bf16[1,384,2048]{2,1,0:T(8,128)(2,1)} %refs_2_.3) | copy-start | bytes 4718596
  20.6 2.2 %copy-start.2 = (bf16[1024,2048]{1,0:T(8,128)(2,1)S(1)}, bf16[1024,2048]{1,0:T(8,128)(2,1)}, u32[]{:S(2)}) copy-start(bf16[1024,2048]{1,0:T(8,128)(2,1)} %weight.1) | copy-start | bytes 12582916
  22.8 0.9 %copy-start.4 = (bf16[1,64,1024]{2,1,0:T(8,128)(2,1)S(1)}, bf16[1,64,1024]{2,1,0:T(8,128)(2,1)}, u32[]{:S(2)}) copy-start(bf16[1,64,1024]{2,1,0:T(8,128)(2,1)} %param.10) | copy-start | bytes 393220
  23.7 0.7 copy-start.10
  24.4 1.3 %copy-start.5 = (bf16[1,64,1024]{2,1,0:T(8,128)(2,1)S(1)}, bf16[1,64,1024]{2,1,0:T(8,128)(2,1)}, u32[]{:S(2)}) copy-start(bf16[1,64,1024]{2,1,0:T(8,128)(2,1)} %param.10) | copy-start | bytes 393220
  24.4 2.9 %copy-start.3 = (bf16[1024,2048]{1,0:T(8,128)(2,1)S(1)}, bf16[1024,2048]{1,0:T(8,128)(2,1)}, u32[]{:S(2)}) copy-start(bf16[1024,2048]{1,0:T(8,128)(2,1)} %weight.1) | copy-start | bytes 12582916
  27.3 7.8 %copy-start.6 = (bf16[1,16,2048]{2,1,0:T(8,128)(2,1)S(1)}, bf16[1,16,2048]{2,1,0:T(8,128)(2,1)}, u32[]{:S(2)}) copy-start(bf16[1,16,2048]{2,1,0:T(8,128)(2,1)} %param.13) | copy-start | bytes 196612
  27.3 7.8 %copy-start.7 = (f32[2048]{0:T(1024)S(1)}, f32[2048]{0:T(1024)}, u32[]{:S(2)}) copy-start(f32[2048]{0:T(1024)} %param.15) | copy-start | bytes 24580
  27.4 7.8 %copy-start.8 = (s32[1,16,8]{1,2,0:T(8,128)S(1)}, s32[1,16,8]{1,2,0:T(8,128)}, u32[]{:S(2)}) copy-start(s32[1,16,8]{1,2,0:T(8,128)} %param.16) | copy-start | bytes 1540
  27.4 7.8 %copy-start.9 = (f32[1,16,8]{1,2,0:T(8,128)S(1)}, f32[1,16,8]{1,2,0:T(8,128)}, u32[]{:S(2)}) copy-start(f32[1,16,8]{1,2,0:T(8,128)} %param.17) | copy-start | bytes 1540
  29.5 20.3 %copy-start.11 = (bf16[1,2048,2,384]{3,2,1,0:T(2,128)(2,1)S(1)}, bf16[1,2048,2,384]{3,2,1,0:T(2,128)(2,1)}, u32[]{:S(2)}) copy-start(bf16[1,2048,2,384]{3,2,1,0:T(2,128)(2,1)} %param.18) | copy-start | bytes 9437188
  29.6 1.9 %collective-permute-start.8 = (bf16[16,2048]{1,0:T(8,128)(2,1)S(1)}, bf16[16,2048]{1,0:T(8,128)(2,1)S(1)}, u32[]{:S(2)}, u32[]{:S(2)}) collective-permute-start(bf16[16,2048]{1,0:T(8,128)(2,1)S(1)} %get-tuple-element.28), channel_id=1, source_target_pairs={{0,1},{1,0},{2,3},{3,2},{4,5},{5,4},{6,7},{7,6},{8,9},{9,8},{10,11... | collective-permute-start | bytes 196616 | tf_op jit(solution)/shard_map/ppermute | solution.py:28
  29.6 4.5 %collective-permute-start.9 = (bf16[16,2048]{1,0:T(8,128)(2,1)S(1)}, bf16[16,2048]{1,0:T(8,128)(2,1)S(1)}, u32[]{:S(2)}, u32[]{:S(2)}) collective-permute-start(bf16[16,2048]{1,0:T(8,128)(2,1)S(1)} %get-tuple-element.29), channel_id=1, source_target_pairs={{0,2},{1,3},{2,0},{3,1},{4,6},{5,7},{6,4},{7,5},{8,10},{9,11},{10,... | collective-permute-start | bytes 196616 | tf_op jit(solution)/shard_map/ppermute | solution.py:28
  31.0 4.1 %collective-permute-start.10 = (bf16[16,2048]{1,0:T(8,128)(2,1)S(1)}, bf16[16,2048]{1,0:T(8,128)(2,1)S(1)}, u32[]{:S(2)}, u32[]{:S(2)}) collective-permute-start(bf16[16,2048]{1,0:T(8,128)(2,1)S(1)} %get-tuple-element.30), channel_id=1, source_target_pairs={{0,3},{1,2},{2,1},{3,0},{4,7},{5,6},{6,5},{7,4},{8,11},{9,10},{10,... | collective-permute-start | bytes 196616 | tf_op jit(solution)/shard_map/ppermute | solution.py:28
  35.5 5.4 %collective-permute-start.13 = (bf16[16,2176]{1,0:T(8,128)(2,1)S(1)}, bf16[16,2176]{1,0:T(8,128)(2,1)S(1)}, u32[]{:S(2)}, u32[]{:S(2)}) collective-permute-start(bf16[16,2176]{1,0:T(8,128)(2,1)S(1)} %get-tuple-element.32), channel_id=1, source_target_pairs={{0,4},{4,0},{8,12},{12,8},{1,5},{5,1},{9,13},{13,9},{2,6},{6,2},{1... | collective-permute-start | bytes 208904 | tf_op jit(solution)/shard_map/ppermute | solution.py:28
  36.1 9.3 %collective-permute-start.12 = (bf16[16,2176]{1,0:T(8,128)(2,1)S(1)}, bf16[16,2176]{1,0:T(8,128)(2,1)S(1)}, u32[]{:S(2)}, u32[]{:S(2)}) collective-permute-start(bf16[16,2176]{1,0:T(8,128)(2,1)S(1)} %get-tuple-element.32), channel_id=1, source_target_pairs={{0,12},{4,8},{8,4},{12,0},{1,13},{5,9},{9,5},{13,1},{2,14},{6,10},... | collective-permute-start | bytes 208904 | tf_op jit(solution)/shard_map/ppermute | solution.py:28
  40.9 6.7 %collective-permute-start.11 = (bf16[16,2176]{1,0:T(8,128)(2,1)S(1)}, bf16[16,2176]{1,0:T(8,128)(2,1)S(1)}, u32[]{:S(2)}, u32[]{:S(2)}) collective-permute-start(bf16[16,2176]{1,0:T(8,128)(2,1)S(1)} %get-tuple-element.32), channel_id=1, source_target_pairs={{0,8},{4,12},{8,0},{12,4},{1,9},{5,13},{9,1},{13,5},{2,10},{6,14},... | collective-permute-start | bytes 208904 | tf_op jit(solution)/shard_map/ppermute | solution.py:28
  40.9 8.3 %collective-permute-start.15 = (bf16[32,2176]{1,0:T(8,128)(2,1)S(1)}, bf16[32,2176]{1,0:T(8,128)(2,1)S(1)}, u32[]{:S(2)}, u32[]{:S(2)}) collective-permute-start(bf16[32,2176]{1,0:T(8,128)(2,1)S(1)} %pad_maximum_fusion.1), channel_id=1, source_target_pairs={{0,2},{1,3},{2,0},{3,1},{4,6},{5,7},{6,4},{7,5},{8,10},{9,11},{10,... | collective-permute-start | bytes 417800 | tf_op jit(solution)/shard_map/ppermute | solution.py:28
  47.5 5.7 %collective-permute-start.14 = (bf16[32,2176]{1,0:T(8,128)(2,1)S(1)}, bf16[32,2176]{1,0:T(8,128)(2,1)S(1)}, u32[]{:S(2)}, u32[]{:S(2)}) collective-permute-start(bf16[32,2176]{1,0:T(8,128)(2,1)S(1)} %pad_maximum_fusion), channel_id=1, source_target_pairs={{0,2},{1,3},{2,0},{3,1},{4,6},{5,7},{6,4},{7,5},{8,10},{9,11},{10,... | collective-permute-start | bytes 417800 | tf_op jit(solution)/shard_map/ppermute | solution.py:28
  49.1 1.4 %copy-start.1 = (bf16[1,384,2048]{2,1,0:T(8,128)(2,1)S(1)}, bf16[1,384,2048]{2,1,0:T(8,128)(2,1)}, u32[]{:S(2)}) copy-start(bf16[1,384,2048]{2,1,0:T(8,128)(2,1)} %refs_2_.3) | copy-start | bytes 4718596
  51.2 6.0 %collective-permute-start.16 = (bf16[32,2048]{1,0:T(8,128)(2,1)S(1)}, bf16[32,2048]{1,0:T(8,128)(2,1)S(1)}, u32[]{:S(2)}, u32[]{:S(2)}) collective-permute-start(bf16[32,2048]{1,0:T(8,128)(2,1)S(1)} %shard_map.118), channel_id=1, source_target_pairs={{0,2},{1,3},{2,0},{3,1},{4,6},{5,7},{6,4},{7,5},{8,10},{9,11},{10,... | collective-permute-start | bytes 393224 | tf_op jit(solution)/shard_map/ppermute | solution.py:28
  55.2 5.0 %collective-permute-start.17 = (bf16[32,2048]{1,0:T(8,128)(2,1)S(1)}, bf16[32,2048]{1,0:T(8,128)(2,1)S(1)}, u32[]{:S(2)}, u32[]{:S(2)}) collective-permute-start(bf16[32,2048]{1,0:T(8,128)(2,1)S(1)} %get-tuple-element.35), channel_id=1, source_target_pairs={{0,2},{1,3},{2,0},{3,1},{4,6},{5,7},{6,4},{7,5},{8,10},{9,11},{10,... | collective-permute-start | bytes 393224 | tf_op jit(solution)/shard_map/ppermute | solution.py:28
  57.3 4.6 %collective-permute-start.20 = (bf16[16,2048]{1,0:T(8,128)(2,1)S(1)}, bf16[16,2048]{1,0:T(8,128)(2,1)S(1)}, u32[]{:S(2)}, u32[]{:S(2)}) collective-permute-start(bf16[16,2048]{1,0:T(8,128)(2,1)S(1)} %slice.65), channel_id=1, source_target_pairs={{0,4},{4,0},{8,12},{12,8},{1,5},{5,1},{9,13},{13,9},{2,6},{6,2},{1... | collective-permute-start | bytes 196616 | tf_op jit(solution)/shard_map/ppermute | solution.py:28
  60.3 5.2 %collective-permute-start.18 = (bf16[16,2048]{1,0:T(8,128)(2,1)S(1)}, bf16[16,2048]{1,0:T(8,128)(2,1)S(1)}, u32[]{:S(2)}, u32[]{:S(2)}) collective-permute-start(bf16[16,2048]{1,0:T(8,128)(2,1)S(1)} %get-tuple-element.38), channel_id=1, source_target_pairs={{0,8},{4,12},{8,0},{12,4},{1,9},{5,13},{9,1},{13,5},{2,10},{6,14},... | collective-permute-start | bytes 196616 | tf_op jit(solution)/shard_map/ppermute | solution.py:28
  60.4 6.2 %collective-permute-start.19 = (bf16[16,2048]{1,0:T(8,128)(2,1)S(1)}, bf16[16,2048]{1,0:T(8,128)(2,1)S(1)}, u32[]{:S(2)}, u32[]{:S(2)}) collective-permute-start(bf16[16,2048]{1,0:T(8,128)(2,1)S(1)} %get-tuple-element.39), channel_id=1, source_target_pairs={{0,12},{4,8},{8,4},{12,0},{1,13},{5,9},{9,5},{13,1},{2,14},{6,10},... | collective-permute-start | bytes 196616 | tf_op jit(solution)/shard_map/ppermute | solution.py:28

commit v10 on v9

--- a/solution.py
+++ b/solution.py
@@ -90,16 +90,66 @@
     )
 
 
-def page_at(offset):
+def ring_page(offset):
     count = lax.axis_size("ctx")
     return lax.rem(lax.axis_index("ctx") + offset + count, count)
 
 
-def first_kernel(fresh_block, count, lengths, queries, keys, values, *refs):
+def at_end():
+    place = lax.axis_index("ctx")
+    return (place == 0) | (place == lax.axis_size("ctx") - 1)
+
+
+def line_page(at_ends, inside):
+    place = lax.axis_index("ctx")
+    return jnp.where(at_end(), place ^ at_ends, place ^ inside)
+
+
+def page_order():
+    count = lax.axis_size("ctx")
+    if count == 4:
+        return [functools.partial(line_page, *pair) for pair in ((1, 1), (2, 3), (3, 2))]
+    steps = [sign * step for step in range(1, (count - 1) // 2 + 1) for sign in (-1, 1)]
+    return [functools.partial(ring_page, step) for step in steps + [count // 2] * (1 - count % 2)]
+
+
+def ring_pages(keys, values):
+    count = lax.axis_size("ctx")
+    held = []
+    left_keys, left_values, right_keys, right_values = keys, values, keys, values
+    for step in range(1, (count - 1) // 2 + 1):
+        left_keys = shift(left_keys, "ctx", 1)
+        right_values = shift(right_values, "ctx", -1)
+        left_values = shift(left_values, "ctx", 1)
+        right_keys = shift(right_keys, "ctx", -1)
+        held.append([(left_keys, left_values)])
+        held.append([(right_keys, right_values)])
+    if count % 2 == 0:
+        held.append([(shift(left_keys, "ctx", 1), shift(right_values, "ctx", -1))])
+    return held
+
+
+def line_pages(keys, values, weight_held, own_done):
+    send = lambda part, pairs: lax.ppermute(part, "ctx", pairs)
+    after = lambda part, other: lax.optimization_barrier((part, other))[0]
+    across, outward = [(1, 2), (2, 1)], [(1, 0), (2, 3)]
+    beside = [send(part, [(0, 1), (1, 0), (2, 3), (3, 2)]) for part in (keys, values)]
+    middle = [send(part, across) for part in (keys, values)]
+    handed = [send(after(middle[0], weight_held), outward), send(middle[1], outward)]
+    farther = [send(part, across) for part in beside]
+    last = [send(after(farther[0], own_done), outward), send(farther[1], outward)]
+    return [[beside], [handed, middle], [last, farther]]
+
+
+def hold_kernel(weight, out):
+    out[...] = jnp.zeros(out.shape, out.dtype)
+
+
+def first_kernel(fresh_block, pages, lengths, queries, keys, values, *refs):
     peak_out, total_out, summed_out, lengths_out = refs[-4:]
-    for offset in range(count):
-        lengths_out[offset : offset + 1, :] = jnp.full(
-            (1, lengths_out.shape[1]), lengths[page_at(offset)], jnp.int32
+    for row, page in enumerate(pages):
+        lengths_out[row : row + 1, :] = jnp.full(
+            (1, lengths_out.shape[1]), lengths[page()], jnp.int32
         )
     place = lax.axis_index("ctx")
     peak_out[...], total_out[...], summed_out[...] = page_partial(
@@ -113,19 +163,26 @@
     )
 
 
-def middle_kernel(offsets, fresh_block, queries, lengths, *refs):
-    count = len(offsets)
-    pages, (peak, total, summed) = refs[: 2 * count], refs[2 * count : 2 * count + 3]
-    outs = refs[2 * count + 3 :]
+def page_refs(ways, refs):
+    keys, values = refs[0][...], refs[1][...]
+    if ways == 2:
+        keys = jnp.where(at_end(), keys, refs[2][...])
+        values = jnp.where(at_end(), values, refs[3][...])
+    return keys, values, refs[2 * ways :]
+
+
+def middle_kernel(row, parts, fresh_block, queries, lengths, *refs):
     stacked = stack_heads(queries[...])
+    (peak, total, summed), refs, outs = refs[:3], refs[3:-3], refs[-3:]
     state = (peak[...], total[...], summed[...])
-    for number, offset in enumerate(offsets):
+    for number, (page, ways) in enumerate(parts):
+        keys, values, refs = page_refs(ways, refs)
         part = page_partial(
             stacked,
-            pages[2 * number][...],
-            pages[2 * number + 1][...],
-            page_at(offset),
-            lengths[offset : offset + 1, :],
+            keys,
+            values,
+            page(),
+            lengths[row + number : row + number + 1, :],
             lax.axis_index("ctx"),
             fresh_block,
         )
@@ -134,29 +191,17 @@
         out[...] = value
 
 
-def late_kernel(
-    offset,
-    fresh_block,
-    sent_count,
-    queries,
-    keys,
-    values,
-    lengths,
-    peak,
-    total,
-    summed,
-    weight,
-    *rest,
-):
-    context_out, own_out = rest[-sent_count - 3 : -sent_count - 1]
-    sent_outs, blocks = rest[-sent_count - 1 : -1], rest[-1]
-    page = page_at(offset)
+def late_kernel(row, part, fresh_block, sent_count, queries, lengths, peak, total, summed, *refs):
+    page, ways = part
+    keys, values, refs = page_refs(ways, refs)
+    weight = refs[0]
+    context_out, own_out, *sent_outs, blocks = refs[-sent_count - 3 :]
     part = page_partial(
         stack_heads(queries[...]),
-        keys[...],
-        values[...],
-        page,
-        lengths[offset : offset + 1, :],
+        keys,
+        values,
+        page(),
+        lengths[row : row + 1, :],
         lax.axis_index("ctx"),
         fresh_block,
     )
@@ -179,47 +224,51 @@
         out[...] = pick(place ^ step).astype(jnp.bfloat16)
 
 
-def attention(queries, pages, lengths, out_weight, token_block, later, swapped):
+def attention(queries, pages, lengths, out_weight, token_block, swapped):
     fresh_block, width = queries.shape
     rows = width // HEAD * fresh_block
     count = lax.axis_size("ctx")
     exp_count = lax.axis_size("exp")
     model_width = out_weight.shape[1]
     own_keys, own_values = pages[:, 0], pages[:, 1]
-    held = []
-    left_keys, left_values = own_keys, own_values
-    right_keys, right_values = own_keys, own_values
-    for step in range(1, (count - 1) // 2 + 1):
-        left_keys = shift(left_keys, "ctx", 1)
-        right_values = shift(right_values, "ctx", -1)
-        left_values = shift(left_values, "ctx", 1)
-        right_keys = shift(right_keys, "ctx", -1)
-        held.append((count - step, left_keys, left_values))
-        held.append((step, right_keys, right_values))
-    if count % 2 == 0:
-        last = (count // 2, shift(left_keys, "ctx", 1), shift(right_values, "ctx", -1))
-    else:
-        last = held.pop()
+    order = page_order()
+    anywhere = pl.BlockSpec(memory_space=pl.ANY)
+    weight_held = pl.pallas_call(
+        hold_kernel,
+        out_shape=jax.ShapeDtypeStruct((8, HEAD), jnp.float32),
+        in_specs=[anywhere],
+        out_specs=whole_specs(1)[0],
+        compiler_params=LIMIT,
+        cost_estimate=pl.CostEstimate(flops=0, bytes_accessed=4 << 20, transcendentals=0),
+    )(out_weight)
     page_flops = 4 * rows * pages.shape[0] * HEAD
     line = jax.ShapeDtypeStruct((1, rows), jnp.float32)
     partial_shape = (line, line, jax.ShapeDtypeStruct((HEAD, rows), jnp.float32))
     *state, page_lengths = pl.pallas_call(
-        functools.partial(first_kernel, fresh_block, count),
-        out_shape=partial_shape + (jax.ShapeDtypeStruct((count, HEAD), jnp.int32),),
-        in_specs=[SMEM_SPEC]
-        + whole_specs(3)
-        + [pl.BlockSpec(memory_space=pl.ANY)] * (1 + len(later)),
+        functools.partial(first_kernel, fresh_block, order),
+        out_shape=partial_shape + (jax.ShapeDtypeStruct((len(order), HEAD), jnp.int32),),
+        in_specs=[SMEM_SPEC] + whole_specs(3) + [anywhere],
         out_specs=tuple(whole_specs(4)),
         compiler_params=LIMIT,
         cost_estimate=pl.CostEstimate(
             flops=16 * page_flops, bytes_accessed=8 << 20, transcendentals=0
         ),
-    )(lengths, queries, own_keys, own_values, out_weight, *later)
-    for start in range(0, len(held), 2):
-        group = held[start : start + 2]
-        operands = [part for _, keys, values in group for part in (keys, values)]
+    )(lengths, queries, own_keys, own_values, weight_held)
+    if count == 4:
+        sources = line_pages(own_keys, own_values, weight_held, page_lengths)
+    else:
+        sources = ring_pages(own_keys, own_values)
+    held = list(zip(order, sources))
+    for start in range(0, len(held) - 1, 2):
+        group = held[start : min(start + 2, len(held) - 1)]
+        operands = [part for _, sources in group for pair in sources for part in pair]
         state = pl.pallas_call(
-            functools.partial(middle_kernel, [offset for offset, _, _ in group], fresh_block),
+            functools.partial(
+                middle_kernel,
+                start,
+                [(page, len(sources)) for page, sources in group],
+                fresh_block,
+            ),
             out_shape=partial_shape,
             in_specs=whole_specs(5 + len(operands)),
             out_specs=tuple(whole_specs(3)),
@@ -227,16 +276,21 @@
             cost_estimate=pl.CostEstimate(
                 flops=len(group) * page_flops, bytes_accessed=2 << 20, transcendentals=0
             ),
-        )(queries, page_lengths, *operands, *state)
+        )(queries, page_lengths, *state, *operands)
+    page, sources = held[-1]
+    operands = [part for pair in sources for part in pair]
     block = jax.ShapeDtypeStruct((token_block, model_width), jnp.bfloat16)
     outs = pl.pallas_call(
-        functools.partial(late_kernel, last[0], fresh_block, exp_count - 1),
+        functools.partial(
+            late_kernel, len(held) - 1, (page, len(sources)), fresh_block, exp_count - 1
+        ),
         out_shape=(
             jax.ShapeDtypeStruct(queries.shape, jnp.bfloat16),
             jax.ShapeDtypeStruct(block.shape, jnp.float32),
         )
         + (block,) * (exp_count - 1),
-        in_specs=whole_specs(8) + [pl.BlockSpec(memory_space=pl.ANY)] * len(swapped),
+        in_specs=whole_specs(6 + len(operands))
+        + [anywhere] * len(swapped),
         out_specs=tuple(whole_specs(1 + exp_count)),
         scratch_shapes=[pltpu.VMEM((fresh_block, model_width), jnp.float32)],
         compiler_params=LIMIT,
@@ -245,7 +299,7 @@
             bytes_accessed=6 << 20,
             transcendentals=0,
         ),
-    )(queries, last[1], last[2], page_lengths, *state, out_weight, *swapped)
+    )(queries, page_lengths, *state, *operands, out_weight, *swapped)
     return outs[0], outs[1], outs[2:]
 
 
@@ -414,7 +468,6 @@
             cached_lengths[r],
             out_weight,
             token_block,
-            (expert_output,),
             swapped if r == 0 else (),
         )
         contexts.append(context)

time: 67.6 us -> 74.3 us (1.099)
  starting transfers between devices: 26.7 us -> 31.9 us
  waiting for transfers between devices: 23.5 us -> 27.6 us
  local copies, waits for them, and re-layouts: 6.39 us -> 3.42 us
    ppermute x6 -> x10, starting transfers between devices: 11.6 us -> 17.2 us  [line_pages(): send = lambda part, pairs: lax.ppermute(part, 'ctx', pairs)]
    ppermute x6 -> x10, waiting for transfers between devices: 5.5 us -> 10.6 us  [line_pages(): send = lambda part, pairs: lax.ppermute(part, 'ctx', pairs)]
    unnamed x29 -> x25, local copies, waits for them, and re-layouts: 6.33 us -> 3.37 us
    ppermute x15, waiting for transfers between devices: 18 us -> 17 us  [swap(): lax.ppermute(value, axis, [(i, i ^ stride) for i in range(lax.axis_size(a...]
    pallas_call x3 -> x4, Pallas kernels: 4.9 us -> 5.03 us  [the longest x1 2.23 us: attention(): pl.pallas_call(functools.partial(late_kernel, len(held) - 1, (page, len(s...]
  transfers between devices with their start and end apart: 21 -> 25, of which waited for: 11 -> 13; matrix products, arithmetic and copies ran while one was open for 6% -> 5% of each run, Pallas kernels for 6% -> 6%
where the time goes in v10:
time: 74.3 us; the launch traced here: 74 us
  starting transfers between devices  31.9 us (43%)
  waiting for transfers between devices  27.6 us (37%)
  Pallas kernels  6.7 us (9%)
  local copies, waits for them, and re-layouts  3.42 us (5%)
  matrix products  2.58 us (3%)
  between operations  0.96 us (1%)
  other arithmetic  0.75 us (1%)
    ppermute x10, starting transfers between devices, line_pages(): send = lambda part, pairs: lax.ppermute(part, 'ctx', pairs)  17.2 us
    ppermute x15, waiting for transfers between devices, swap(): lax.ppermute(value, axis, [(i, i ^ stride) for i in range(lax.axis_size(a...  17 us
    ppermute x15, starting transfers between devices, swap(): lax.ppermute(value, axis, [(i, i ^ stride) for i in range(lax.axis_size(a...  14.7 us
    ppermute x10, waiting for transfers between devices, line_pages(): send = lambda part, pairs: lax.ppermute(part, 'ctx', pairs)  10.6 us
    unnamed x25, local copies, waits for them, and re-layouts  3.37 us
    dot_general x4, matrix products, expert_apply(): jnp.einsum('nd,dgh->gnh', rows[:, :width], gate_up[0], preferred_element_...  2.58 us
    pallas_call x1, Pallas kernels, attention(): pl.pallas_call(functools.partial(late_kernel, len(held) - 1, (page, len(s...  2.23 us
  transfers between devices with their start and end apart: 25, of which 13 were waited for; matrix products, arithmetic and copies ran while one was open for 5% of the time, Pallas kernels for 6%

profile of v10, /device:TPU:0, one launch (start us, length us, event | category | flops | bytes accessed | tf_op | source)
XLA Modules:
  0.0 74.0 jit_solution(532603785535437768)
XLA Ops:
  0.6 0.5 collective-permute-start.10
  1.2 1.0 %copy.34 = bf16[1,576,2,128]{3,1,2,0:T(8,128)(2,1)S(1)} copy(bf16[1,576,2,128]{3,2,1,0:T(2,128)(2,1)} %param.11) | data formatting | bytes 589824 | tf_op args[1]
  2.3 0.7 collective-permute-start.2
  3.0 5.9 %collective-permute-start = (bf16[576,128]{1,0:T(8,128)(2,1)S(1)}, bf16[576,128]{1,0:T(8,128)(2,1)S(1)}, u32[]{:S(2)}, u32[]{:S(2)}) collective-permute-start(bf16[576,128]{1,0:T(8,128)(2,1)S(1)} %get-tuple-element.41.keys), channel_id=1, source_target_pairs={{0,4},{4,0},{8,12},{12,8},{1,5},{5,1},{9,13},{13,9},{2,6},{6,2},{1... | collective-permute-start | bytes 442376 | tf_op jit(solution)/shard_map/ppermute | solution.py:133
  8.8 0.7 collective-permute-start.4
  9.5 3.5 %collective-permute-start.1 = (bf16[576,128]{1,0:T(8,128)(2,1)S(1)}, bf16[576,128]{1,0:T(8,128)(2,1)S(1)}, u32[]{:S(2)}, u32[]{:S(2)}) collective-permute-start(bf16[576,128]{1,0:T(8,128)(2,1)S(1)} %get-tuple-element.40.values), channel_id=1, source_target_pairs={{0,4},{4,0},{8,12},{12,8},{1,5},{5,1},{9,13},{13,9},{2,6},{6,2},{1... | collective-permute-start | bytes 442376 | tf_op jit(solution)/shard_map/ppermute | solution.py:133
  13.0 0.7 collective-permute-start.6
  13.7 2.2 %copy-done = bf16[1024,2048]{1,0:T(8,128)(2,1)S(1)} copy-done((bf16[1024,2048]{1,0:T(8,128)(2,1)S(1)}, bf16[1024,2048]{1,0:T(8,128)(2,1)}, u32[]{:S(2)}) %copy-start) | copy-done | bytes 4194328
  15.9 1.3 %collective-permute-start.3 = (bf16[576,128]{1,0:T(8,128)(2,1)S(1)}, bf16[576,128]{1,0:T(8,128)(2,1)S(1)}, u32[]{:S(2)}, u32[]{:S(2)}) collective-permute-start(bf16[576,128]{1,0:T(8,128)(2,1)S(1)} %collective-permute-done.2.refs_7_), channel_id=1, source_target_pairs={{4,0},{8,12},{5,1},{9,13},{6,2},{10,14},{7,3},{11,15},{20,16},{24,... | collective-permute-start | bytes 442376 | tf_op jit(solution)/shard_map/ppermute | solution.py:133
  17.2 1.3 %collective-permute-start.5 = (bf16[576,128]{1,0:T(8,128)(2,1)S(1)}, bf16[576,128]{1,0:T(8,128)(2,1)S(1)}, u32[]{:S(2)}, u32[]{:S(2)}) collective-permute-start(bf16[576,128]{1,0:T(8,128)(2,1)S(1)} %collective-permute-done.4.refs_8_), channel_id=1, source_target_pairs={{4,0},{8,12},{5,1},{9,13},{6,2},{10,14},{7,3},{11,15},{20,16},{24,... | collective-permute-start | bytes 442376 | tf_op jit(solution)/shard_map/ppermute | solution.py:133
  18.5 0.7 collective-permute-start.8
  19.2 1.3 %shard_map.114 = (f32[1,512]{1,0:T(1,128)S(1)}, f32[1,512]{1,0:T(1,128)S(1)}, f32[128,512]{1,0:T(8,128)S(1)}, s32[3,128]{1,0:T(4,128)S(1)}) custom-call(s32[4]{0:T(128)S(1)} %bitcast.47, bf16[64,1024]{1,0:T(8,128)(2,1)S(1)} %bitcast.40, bf16[576,128]{1,0:T(8,128)(2,1)S(1)} %get-tuple-element.41.keys, bf16[576,128]{1,0:T(8,128)(2,1)S(1)} %get-tuple-element.40.values, ...), custom_call_target="tpu_custom_call" | custom-call | flops 2415919104 | bytes 8388608 | tf_op jit(solution)/shard_map/pallas_call | solution.py:247
  20.5 1.3 %collective-permute-start.9 = (bf16[576,128]{1,0:T(8,128)(2,1)S(1)}, bf16[576,128]{1,0:T(8,128)(2,1)S(1)}, u32[]{:S(2)}, u32[]{:S(2)}) collective-permute-start(bf16[576,128]{1,0:T(8,128)(2,1)S(1)} %collective-permute-done.8.refs_3_), channel_id=1, source_target_pairs={{4,0},{8,12},{5,1},{9,13},{6,2},{10,14},{7,3},{11,15},{20,16},{24,... | collective-permute-start | bytes 442376 | tf_op jit(solution)/shard_map/ppermute | solution.py:133
  21.8 4.3 %collective-permute-done.5.refs_6_ = bf16[576,128]{1,0:T(8,128)(2,1)S(1)} collective-permute-done((bf16[576,128]{1,0:T(8,128)(2,1)S(1)}, bf16[576,128]{1,0:T(8,128)(2,1)S(1)}, u32[]{:S(2)}, u32[]{:S(2)}) %collective-permute-start.5) | collective-permute-done | bytes 147488 | tf_op jit(solution)/shard_map/ppermute | solution.py:133
  26.1 1.3 %collective-permute-start.7 = (bf16[576,128]{1,0:T(8,128)(2,1)S(1)}, bf16[576,128]{1,0:T(8,128)(2,1)S(1)}, u32[]{:S(2)}, u32[]{:S(2)}) collective-permute-start(bf16[576,128]{1,0:T(8,128)(2,1)S(1)} %collective-permute-done.6.refs_2_), channel_id=1, source_target_pairs={{4,0},{8,12},{5,1},{9,13},{6,2},{10,14},{7,3},{11,15},{20,16},{24,... | collective-permute-start | bytes 442376 | tf_op jit(solution)/shard_map/ppermute | solution.py:133
  27.4 1.5 %shard_map.115 = (f32[1,512]{1,0:T(1,128)S(1)}, f32[1,512]{1,0:T(1,128)S(1)}, f32[128,512]{1,0:T(8,128)S(1)}) custom-call(bf16[64,1024]{1,0:T(8,128)(2,1)S(1)} %bitcast.41, s32[3,128]{1,0:T(4,128)S(1)} %get-tuple-element.21.lengths, f32[1,512]{1,0:T(1,128)S(1)} %get-tuple-element.22.refs_0_, f32[1,512]{1,0:T(1,128)S(1)} %get-tuple-element.23.refs_1_, ...), custom_call_target="tpu_custom_call" | custom-call | flops 301989888 | bytes 2097152 | tf_op jit(solution)/shard_map/pallas_call | solution.py:265
  28.9 4.7 %collective-permute-done.9.refs_1_ = bf16[576,128]{1,0:T(8,128)(2,1)S(1)} collective-permute-done((bf16[576,128]{1,0:T(8,128)(2,1)S(1)}, bf16[576,128]{1,0:T(8,128)(2,1)S(1)}, u32[]{:S(2)}, u32[]{:S(2)}) %collective-permute-start.9) | collective-permute-done | bytes 147488 | tf_op jit(solution)/shard_map/ppermute | solution.py:133
  33.6 1.6 %collective-permute-done.7.refs_0_ = bf16[576,128]{1,0:T(8,128)(2,1)S(1)} collective-permute-done((bf16[576,128]{1,0:T(8,128)(2,1)S(1)}, bf16[576,128]{1,0:T(8,128)(2,1)S(1)}, u32[]{:S(2)}, u32[]{:S(2)}) %collective-permute-start.7) | collective-permute-done | bytes 147488 | tf_op jit(solution)/shard_map/ppermute | solution.py:133
  35.3 2.2 %shard_map.116 = (bf16[64,1024]{1,0:T(8,128)(2,1)}, f32[16,2048]{1,0:T(8,128)S(1)}, bf16[16,2048]{1,0:T(8,128)(2,1)S(1)}, bf16[16,2048]{1,0:T(8,128)(2,1)S(1)}, bf16[16,2048]{1,0:T(8,128)(2,1)S(1)}) custom-call(bf16[64,1024]{1,0:T(8,128)(2,1)S(1)} %bitcast.42, s32[3,128]{1,0:T(4,128)S(1)} %get-tuple-element.21.lengths, f32[1,512]{1,0:T(1,128)S(1)} %get-tuple-element.26.peak, ...), custom_call_target="tpu_custom_call" | custom-call | flops 419430400 | bytes 6291456 | tf_op jit(solution)/shard_map/pallas_call | solution.py:283
  37.5 1.5 %collective-permute-start.13 = (bf16[16,2048]{1,0:T(8,128)(2,1)S(1)}, bf16[16,2048]{1,0:T(8,128)(2,1)S(1)}, u32[]{:S(2)}, u32[]{:S(2)}) collective-permute-start(bf16[16,2048]{1,0:T(8,128)(2,1)S(1)} %get-tuple-element.33), channel_id=1, source_target_pairs={{0,2},{1,3},{2,0},{3,1},{4,6},{5,7},{6,4},{7,5},{8,10},{9,11},{10,... | collective-permute-start | bytes 196616 | tf_op jit(solution)/shard_map/ppermute | solution.py:28
  39.0 0.4 collective-permute-start.14
  39.4 2.7 %collective-permute-done.13.refs_2_ = bf16[16,2048]{1,0:T(8,128)(2,1)S(1)} collective-permute-done((bf16[16,2048]{1,0:T(8,128)(2,1)S(1)}, bf16[16,2048]{1,0:T(8,128)(2,1)S(1)}, u32[]{:S(2)}, u32[]{:S(2)}) %collective-permute-start.13) | collective-permute-done | bytes 65568 | tf_op jit(solution)/shard_map/ppermute | solution.py:28
  42.0 1.1 %collective-permute-done.14.refs_3_ = bf16[16,2048]{1,0:T(8,128)(2,1)S(1)} collective-permute-done((bf16[16,2048]{1,0:T(8,128)(2,1)S(1)}, bf16[16,2048]{1,0:T(8,128)(2,1)S(1)}, u32[]{:S(2)}, u32[]{:S(2)}) %collective-permute-start.14) | collective-permute-done | bytes 65568 | tf_op jit(solution)/shard_map/ppermute | solution.py:28
  43.1 0.3 shard_map.117
  43.5 2.4 %collective-permute-start.16 = (bf16[16,2176]{1,0:T(8,128)(2,1)S(1)}, bf16[16,2176]{1,0:T(8,128)(2,1)S(1)}, u32[]{:S(2)}, u32[]{:S(2)}) collective-permute-start(bf16[16,2176]{1,0:T(8,128)(2,1)S(1)} %get-tuple-element.36), channel_id=1, source_target_pairs={{0,12},{4,8},{8,4},{12,0},{1,13},{5,9},{9,5},{13,1},{2,14},{6,10},... | collective-permute-start | bytes 208904 | tf_op jit(solution)/shard_map/ppermute | solution.py:28
  45.8 1.1 %collective-permute-start.15 = (bf16[16,2176]{1,0:T(8,128)(2,1)S(1)}, bf16[16,2176]{1,0:T(8,128)(2,1)S(1)}, u32[]{:S(2)}, u32[]{:S(2)}) collective-permute-start(bf16[16,2176]{1,0:T(8,128)(2,1)S(1)} %get-tuple-element.36), channel_id=1, source_target_pairs={{0,8},{4,12},{8,0},{12,4},{1,9},{5,13},{9,1},{13,5},{2,10},{6,14},... | collective-permute-start | bytes 208904 | tf_op jit(solution)/shard_map/ppermute | solution.py:28
  46.9 0.8 %collective-permute-done.17 = bf16[16,2176]{1,0:T(8,128)(2,1)S(1)} collective-permute-done((bf16[16,2176]{1,0:T(8,128)(2,1)S(1)}, bf16[16,2176]{1,0:T(8,128)(2,1)S(1)}, u32[]{:S(2)}, u32[]{:S(2)}) %collective-permute-start.17) | collective-permute-done | bytes 69664 | tf_op jit(solution)/shard_map/ppermute | solution.py:28
  47.8 1.5 %collective-permute-start.19 = (bf16[32,2176]{1,0:T(8,128)(2,1)S(1)}, bf16[32,2176]{1,0:T(8,128)(2,1)S(1)}, u32[]{:S(2)}, u32[]{:S(2)}) collective-permute-start(bf16[32,2176]{1,0:T(8,128)(2,1)S(1)} %pad_maximum_fusion.1), channel_id=1, source_target_pairs={{0,2},{1,3},{2,0},{3,1},{4,6},{5,7},{6,4},{7,5},{8,10},{9,11},{10,... | collective-permute-start | bytes 417800 | tf_op jit(solution)/shard_map/ppermute | solution.py:28
  49.2 0.9 %collective-permute-done.16 = bf16[16,2176]{1,0:T(8,128)(2,1)S(1)} collective-permute-done((bf16[16,2176]{1,0:T(8,128)(2,1)S(1)}, bf16[16,2176]{1,0:T(8,128)(2,1)S(1)}, u32[]{:S(2)}, u32[]{:S(2)}) %collective-permute-start.16) | collective-permute-done | bytes 69664 | tf_op jit(solution)/shard_map/ppermute | solution.py:28
  50.2 3.3 %collective-permute-done.15 = bf16[16,2176]{1,0:T(8,128)(2,1)S(1)} collective-permute-done((bf16[16,2176]{1,0:T(8,128)(2,1)S(1)}, bf16[16,2176]{1,0:T(8,128)(2,1)S(1)}, u32[]{:S(2)}, u32[]{:S(2)}) %collective-permute-start.15) | collective-permute-done | bytes 69664 | tf_op jit(solution)/shard_map/ppermute | solution.py:28
  53.4 1.5 %collective-permute-start.18 = (bf16[32,2176]{1,0:T(8,128)(2,1)S(1)}, bf16[32,2176]{1,0:T(8,128)(2,1)S(1)}, u32[]{:S(2)}, u32[]{:S(2)}) collective-permute-start(bf16[32,2176]{1,0:T(8,128)(2,1)S(1)} %pad_maximum_fusion), channel_id=1, source_target_pairs={{0,2},{1,3},{2,0},{3,1},{4,6},{5,7},{6,4},{7,5},{8,10},{9,11},{10,... | collective-permute-start | bytes 417800 | tf_op jit(solution)/shard_map/ppermute | solution.py:28
  55.1 0.6 fusion.17.refs_1_
  55.7 0.7 fusion.14.refs_0_
  56.5 0.7 shard_map.119
  57.1 0.6 collective-permute-start.20
  57.7 0.8 %collective-permute-done.18 = bf16[32,2176]{1,0:T(8,128)(2,1)S(1)} collective-permute-done((bf16[32,2176]{1,0:T(8,128)(2,1)S(1)}, bf16[32,2176]{1,0:T(8,128)(2,1)S(1)}, u32[]{:S(2)}, u32[]{:S(2)}) %collective-permute-start.18) | collective-permute-done | bytes 139296 | tf_op jit(solution)/shard_map/ppermute | solution.py:28
  58.6 0.6 fusion.11.refs_1_
  59.2 0.6 fusion.8.refs_0_
  59.9 0.8 %shard_map.118 = (f32[32,2048]{1,0:T(8,128)S(1)}, f32[32,2048]{1,0:T(8,128)S(1)}, bf16[32,2048]{1,0:T(8,128)(2,1)S(1)}) custom-call(bf16[96,2176]{1,0:T(8,128)(2,1)S(1)} %constant_dynamic-update-slice_fusion.rows, f32[2,96,384]{2,1,0:T(8,128)S(1)} %fusion.8.refs_0_, f32[2,96,384]{2,1,0:T(8,128)S(1)} %fusion.11.refs_1_, bf16[1,384,2048]{2,1,0:T(8,128)(2,1)S(1)} %copy-done.2, ...), custom_call_target="tpu_custom_call" | custom-call | flops 301989888 | bytes 2097152 | tf_op jit(solution)/shard_map/pallas_call | solution.py:374
  60.6 2.1 %collective-permute-start.21 = (bf16[32,2048]{1,0:T(8,128)(2,1)S(1)}, bf16[32,2048]{1,0:T(8,128)(2,1)S(1)}, u32[]{:S(2)}, u32[]{:S(2)}) collective-permute-start(bf16[32,2048]{1,0:T(8,128)(2,1)S(1)} %get-tuple-element.39), channel_id=1, source_target_pairs={{0,2},{1,3},{2,0},{3,1},{4,6},{5,7},{6,4},{7,5},{8,10},{9,11},{10,... | collective-permute-start | bytes 393224 | tf_op jit(solution)/shard_map/ppermute | solution.py:28
  62.7 0.1 collective-permute-done.20
  62.9 0.2 collective-permute-start.24
  63.1 2.6 %collective-permute-done.21 = bf16[32,2048]{1,0:T(8,128)(2,1)S(1)} collective-permute-done((bf16[32,2048]{1,0:T(8,128)(2,1)S(1)}, bf16[32,2048]{1,0:T(8,128)(2,1)S(1)}, u32[]{:S(2)}, u32[]{:S(2)}) %collective-permute-start.21) | collective-permute-done | bytes 131104 | tf_op jit(solution)/shard_map/ppermute | solution.py:28
  65.7 1.4 %collective-permute-start.22 = (bf16[16,2048]{1,0:T(8,128)(2,1)S(1)}, bf16[16,2048]{1,0:T(8,128)(2,1)S(1)}, u32[]{:S(2)}, u32[]{:S(2)}) collective-permute-start(bf16[16,2048]{1,0:T(8,128)(2,1)S(1)} %get-tuple-element.42), channel_id=1, source_target_pairs={{0,8},{4,12},{8,0},{12,4},{1,9},{5,13},{9,1},{13,5},{2,10},{6,14},... | collective-permute-start | bytes 196616 | tf_op jit(solution)/shard_map/ppermute | solution.py:28
  67.1 1.4 %collective-permute-start.23 = (bf16[16,2048]{1,0:T(8,128)(2,1)S(1)}, bf16[16,2048]{1,0:T(8,128)(2,1)S(1)}, u32[]{:S(2)}, u32[]{:S(2)}) collective-permute-start(bf16[16,2048]{1,0:T(8,128)(2,1)S(1)} %get-tuple-element.43), channel_id=1, source_target_pairs={{0,12},{4,8},{8,4},{12,0},{1,13},{5,9},{9,5},{13,1},{2,14},{6,10},... | collective-permute-start | bytes 196616 | tf_op jit(solution)/shard_map/ppermute | solution.py:28
  68.5 2.9 %collective-permute-done.22 = bf16[16,2048]{1,0:T(8,128)(2,1)S(1)} collective-permute-done((bf16[16,2048]{1,0:T(8,128)(2,1)S(1)}, bf16[16,2048]{1,0:T(8,128)(2,1)S(1)}, u32[]{:S(2)}, u32[]{:S(2)}) %collective-permute-start.22) | collective-permute-done | bytes 65568 | tf_op jit(solution)/shard_map/ppermute | solution.py:28
  71.4 1.9 %collective-permute-done.23 = bf16[16,2048]{1,0:T(8,128)(2,1)S(1)} collective-permute-done((bf16[16,2048]{1,0:T(8,128)(2,1)S(1)}, bf16[16,2048]{1,0:T(8,128)(2,1)S(1)}, u32[]{:S(2)}, u32[]{:S(2)}) %collective-permute-start.23) | collective-permute-done | bytes 65568 | tf_op jit(solution)/shard_map/ppermute | solution.py:28
  73.3 0.7 fusion.24
  (47 shorter events, 0.5 us)
Async XLA Ops:
  0.6 18.5 %copy-start.8 = (s32[1,4]{1,0:T(1,128)S(1)}, s32[1,4]{1,0:T(1,128)}, u32[]{:S(2)}) copy-start(s32[1,4]{1,0:T(1,128)} %param.12) | copy-start | bytes 52
  0.6 18.5 %copy-start.3 = (bf16[1,64,1024]{2,1,0:T(8,128)(2,1)S(1)}, bf16[1,64,1024]{2,1,0:T(8,128)(2,1)}, u32[]{:S(2)}) copy-start(bf16[1,64,1024]{2,1,0:T(8,128)(2,1)} %param.10) | copy-start | bytes 393220
  0.6 34.6 %collective-permute-start.10 = (bf16[1,2048,2,384]{3,2,1,0:T(2,128)(2,1)}, bf16[1,2048,2,384]{3,2,1,0:T(2,128)(2,1)S(1)}, u32[]{:S(2)}, u32[]{:S(2)}) collective-permute-start(bf16[1,2048,2,384]{3,2,1,0:T(2,128)(2,1)} %param.18), channel_id=1, source_target_pairs={{0,1},{1,0},{2,3},{3,2},{4,5},{5,4},{6,7},{7,6},{8,9},{9,8},{10,11... | collective-permute-start | bytes 9437192 | tf_op jit(solution)/shard_map/ppermute | solution.py:28
  1.2 34.0 %collective-permute-start.11 = (bf16[1,384,2048]{2,1,0:T(8,128)(2,1)}, bf16[1,384,2048]{2,1,0:T(8,128)(2,1)S(1)}, u32[]{:S(2)}, u32[]{:S(2)}) collective-permute-start(bf16[1,384,2048]{2,1,0:T(8,128)(2,1)} %refs_2_.3), channel_id=1, source_target_pairs={{0,1},{1,0},{2,3},{3,2},{4,5},{5,4},{6,7},{7,6},{8,9},{9,8},{10,11... | collective-permute-start | bytes 4718600 | tf_op jit(solution)/shard_map/ppermute | solution.py:28
  2.3 7.2 %collective-permute-start.2 = (bf16[576,128]{1,0:T(8,128)(2,1)S(1)}, bf16[576,128]{1,0:T(8,128)(2,1)S(1)}, u32[]{:S(2)}, u32[]{:S(2)}) collective-permute-start(bf16[576,128]{1,0:T(8,128)(2,1)S(1)} %get-tuple-element.41.keys), channel_id=1, source_target_pairs={{4,8},{8,4},{5,9},{9,5},{6,10},{10,6},{7,11},{11,7},{20,24},{24,20... | collective-permute-start | bytes 442376 | tf_op jit(solution)/shard_map/ppermute | solution.py:133
  3.0 10.1 %collective-permute-start = (bf16[576,128]{1,0:T(8,128)(2,1)S(1)}, bf16[576,128]{1,0:T(8,128)(2,1)S(1)}, u32[]{:S(2)}, u32[]{:S(2)}) collective-permute-start(bf16[576,128]{1,0:T(8,128)(2,1)S(1)} %get-tuple-element.41.keys), channel_id=1, source_target_pairs={{0,4},{4,0},{8,12},{12,8},{1,5},{5,1},{9,13},{13,9},{2,6},{6,2},{1... | collective-permute-start | bytes 442376 | tf_op jit(solution)/shard_map/ppermute | solution.py:133
  8.8 7.0 %collective-permute-start.4 = (bf16[576,128]{1,0:T(8,128)(2,1)S(1)}, bf16[576,128]{1,0:T(8,128)(2,1)S(1)}, u32[]{:S(2)}, u32[]{:S(2)}) collective-permute-start(bf16[576,128]{1,0:T(8,128)(2,1)S(1)} %get-tuple-element.40.values), channel_id=1, source_target_pairs={{4,8},{8,4},{5,9},{9,5},{6,10},{10,6},{7,11},{11,7},{20,24},{24,20... | collective-permute-start | bytes 442376 | tf_op jit(solution)/shard_map/ppermute | solution.py:133
  9.5 7.7 %collective-permute-start.1 = (bf16[576,128]{1,0:T(8,128)(2,1)S(1)}, bf16[576,128]{1,0:T(8,128)(2,1)S(1)}, u32[]{:S(2)}, u32[]{:S(2)}) collective-permute-start(bf16[576,128]{1,0:T(8,128)(2,1)S(1)} %get-tuple-element.40.values), channel_id=1, source_target_pairs={{0,4},{4,0},{8,12},{12,8},{1,5},{5,1},{9,13},{13,9},{2,6},{6,2},{1... | collective-permute-start | bytes 442376 | tf_op jit(solution)/shard_map/ppermute | solution.py:133
  13.0 5.5 %collective-permute-start.6 = (bf16[576,128]{1,0:T(8,128)(2,1)S(1)}, bf16[576,128]{1,0:T(8,128)(2,1)S(1)}, u32[]{:S(2)}, u32[]{:S(2)}) collective-permute-start(bf16[576,128]{1,0:T(8,128)(2,1)S(1)} %collective-permute-done.refs_3_), channel_id=1, source_target_pairs={{4,8},{8,4},{5,9},{9,5},{6,10},{10,6},{7,11},{11,7},{20,24},{24,20... | collective-permute-start | bytes 442376 | tf_op jit(solution)/shard_map/ppermute | solution.py:133
  13.7 2.2 %copy-start = (bf16[1024,2048]{1,0:T(8,128)(2,1)S(1)}, bf16[1024,2048]{1,0:T(8,128)(2,1)}, u32[]{:S(2)}) copy-start(bf16[1024,2048]{1,0:T(8,128)(2,1)} %refs_4_.1) | copy-start | bytes 12582916
  15.9 11.5 %collective-permute-start.3 = (bf16[576,128]{1,0:T(8,128)(2,1)S(1)}, bf16[576,128]{1,0:T(8,128)(2,1)S(1)}, u32[]{:S(2)}, u32[]{:S(2)}) collective-permute-start(bf16[576,128]{1,0:T(8,128)(2,1)S(1)} %collective-permute-done.2.refs_7_), channel_id=1, source_target_pairs={{4,0},{8,12},{5,1},{9,13},{6,2},{10,14},{7,3},{11,15},{20,16},{24,... | collective-permute-start | bytes 442376 | tf_op jit(solution)/shard_map/ppermute | solution.py:133
  17.2 8.9 %collective-permute-start.5 = (bf16[576,128]{1,0:T(8,128)(2,1)S(1)}, bf16[576,128]{1,0:T(8,128)(2,1)S(1)}, u32[]{:S(2)}, u32[]{:S(2)}) collective-permute-start(bf16[576,128]{1,0:T(8,128)(2,1)S(1)} %collective-permute-done.4.refs_8_), channel_id=1, source_target_pairs={{4,0},{8,12},{5,1},{9,13},{6,2},{10,14},{7,3},{11,15},{20,16},{24,... | collective-permute-start | bytes 442376 | tf_op jit(solution)/shard_map/ppermute | solution.py:133
  18.5 2.0 %collective-permute-start.8 = (bf16[576,128]{1,0:T(8,128)(2,1)S(1)}, bf16[576,128]{1,0:T(8,128)(2,1)S(1)}, u32[]{:S(2)}, u32[]{:S(2)}) collective-permute-start(bf16[576,128]{1,0:T(8,128)(2,1)S(1)} %collective-permute-done.1.refs_4_), channel_id=1, source_target_pairs={{4,8},{8,4},{5,9},{9,5},{6,10},{10,6},{7,11},{11,7},{20,24},{24,20... | collective-permute-start | bytes 442376 | tf_op jit(solution)/shard_map/ppermute | solution.py:133
  19.2 16.0 %copy-start.1 = (bf16[1024,2048]{1,0:T(8,128)(2,1)S(1)}, bf16[1024,2048]{1,0:T(8,128)(2,1)}, u32[]{:S(2)}) copy-start(bf16[1024,2048]{1,0:T(8,128)(2,1)} %refs_4_.1) | copy-start | bytes 12582916
  20.5 13.1 %collective-permute-start.9 = (bf16[576,128]{1,0:T(8,128)(2,1)S(1)}, bf16[576,128]{1,0:T(8,128)(2,1)S(1)}, u32[]{:S(2)}, u32[]{:S(2)}) collective-permute-start(bf16[576,128]{1,0:T(8,128)(2,1)S(1)} %collective-permute-done.8.refs_3_), channel_id=1, source_target_pairs={{4,0},{8,12},{5,1},{9,13},{6,2},{10,14},{7,3},{11,15},{20,16},{24,... | collective-permute-start | bytes 442376 | tf_op jit(solution)/shard_map/ppermute | solution.py:133
  26.1 9.1 %collective-permute-start.7 = (bf16[576,128]{1,0:T(8,128)(2,1)S(1)}, bf16[576,128]{1,0:T(8,128)(2,1)S(1)}, u32[]{:S(2)}, u32[]{:S(2)}) collective-permute-start(bf16[576,128]{1,0:T(8,128)(2,1)S(1)} %collective-permute-done.6.refs_2_), channel_id=1, source_target_pairs={{4,0},{8,12},{5,1},{9,13},{6,2},{10,14},{7,3},{11,15},{20,16},{24,... | collective-permute-start | bytes 442376 | tf_op jit(solution)/shard_map/ppermute | solution.py:133
  35.2 7.9 %copy-start.4 = (bf16[1,16,2048]{2,1,0:T(8,128)(2,1)S(1)}, bf16[1,16,2048]{2,1,0:T(8,128)(2,1)}, u32[]{:S(2)}) copy-start(bf16[1,16,2048]{2,1,0:T(8,128)(2,1)} %param.13) | copy-start | bytes 196612
  35.2 7.9 %copy-start.5 = (f32[2048]{0:T(1024)S(1)}, f32[2048]{0:T(1024)}, u32[]{:S(2)}) copy-start(f32[2048]{0:T(1024)} %param.15) | copy-start | bytes 24580
  35.2 7.9 %copy-start.6 = (s32[1,16,8]{1,2,0:T(8,128)S(1)}, s32[1,16,8]{1,2,0:T(8,128)}, u32[]{:S(2)}) copy-start(s32[1,16,8]{1,2,0:T(8,128)} %param.16) | copy-start | bytes 1540
  35.2 7.9 %copy-start.7 = (f32[1,16,8]{1,2,0:T(8,128)S(1)}, f32[1,16,8]{1,2,0:T(8,128)}, u32[]{:S(2)}) copy-start(f32[1,16,8]{1,2,0:T(8,128)} %param.17) | copy-start | bytes 1540
  37.5 18.2 %copy-start.9 = (bf16[1,2048,2,384]{3,2,1,0:T(2,128)(2,1)S(1)}, bf16[1,2048,2,384]{3,2,1,0:T(2,128)(2,1)}, u32[]{:S(2)}) copy-start(bf16[1,2048,2,384]{3,2,1,0:T(2,128)(2,1)} %param.18) | copy-start | bytes 9437188
  37.5 1.9 %collective-permute-start.12 = (bf16[16,2048]{1,0:T(8,128)(2,1)S(1)}, bf16[16,2048]{1,0:T(8,128)(2,1)S(1)}, u32[]{:S(2)}, u32[]{:S(2)}) collective-permute-start(bf16[16,2048]{1,0:T(8,128)(2,1)S(1)} %get-tuple-element.32), channel_id=1, source_target_pairs={{0,1},{1,0},{2,3},{3,2},{4,5},{5,4},{6,7},{7,6},{8,9},{9,8},{10,11... | collective-permute-start | bytes 196616 | tf_op jit(solution)/shard_map/ppermute | solution.py:28
  37.5 4.5 %collective-permute-start.13 = (bf16[16,2048]{1,0:T(8,128)(2,1)S(1)}, bf16[16,2048]{1,0:T(8,128)(2,1)S(1)}, u32[]{:S(2)}, u32[]{:S(2)}) collective-permute-start(bf16[16,2048]{1,0:T(8,128)(2,1)S(1)} %get-tuple-element.33), channel_id=1, source_target_pairs={{0,2},{1,3},{2,0},{3,1},{4,6},{5,7},{6,4},{7,5},{8,10},{9,11},{10,... | collective-permute-start | bytes 196616 | tf_op jit(solution)/shard_map/ppermute | solution.py:28
  39.0 4.1 %collective-permute-start.14 = (bf16[16,2048]{1,0:T(8,128)(2,1)S(1)}, bf16[16,2048]{1,0:T(8,128)(2,1)S(1)}, u32[]{:S(2)}, u32[]{:S(2)}) collective-permute-start(bf16[16,2048]{1,0:T(8,128)(2,1)S(1)} %get-tuple-element.34), channel_id=1, source_target_pairs={{0,3},{1,2},{2,1},{3,0},{4,7},{5,6},{6,5},{7,4},{8,11},{9,10},{10,... | collective-permute-start | bytes 196616 | tf_op jit(solution)/shard_map/ppermute | solution.py:28
  43.4 4.4 %collective-permute-start.17 = (bf16[16,2176]{1,0:T(8,128)(2,1)S(1)}, bf16[16,2176]{1,0:T(8,128)(2,1)S(1)}, u32[]{:S(2)}, u32[]{:S(2)}) collective-permute-start(bf16[16,2176]{1,0:T(8,128)(2,1)S(1)} %get-tuple-element.36), channel_id=1, source_target_pairs={{0,4},{4,0},{8,12},{12,8},{1,5},{5,1},{9,13},{13,9},{2,6},{6,2},{1... | collective-permute-start | bytes 208904 | tf_op jit(solution)/shard_map/ppermute | solution.py:28
  43.5 6.7 %collective-permute-start.16 = (bf16[16,2176]{1,0:T(8,128)(2,1)S(1)}, bf16[16,2176]{1,0:T(8,128)(2,1)S(1)}, u32[]{:S(2)}, u32[]{:S(2)}) collective-permute-start(bf16[16,2176]{1,0:T(8,128)(2,1)S(1)} %get-tuple-element.36), channel_id=1, source_target_pairs={{0,12},{4,8},{8,4},{12,0},{1,13},{5,9},{9,5},{13,1},{2,14},{6,10},... | collective-permute-start | bytes 208904 | tf_op jit(solution)/shard_map/ppermute | solution.py:28
  45.8 7.6 %collective-permute-start.15 = (bf16[16,2176]{1,0:T(8,128)(2,1)S(1)}, bf16[16,2176]{1,0:T(8,128)(2,1)S(1)}, u32[]{:S(2)}, u32[]{:S(2)}) collective-permute-start(bf16[16,2176]{1,0:T(8,128)(2,1)S(1)} %get-tuple-element.36), channel_id=1, source_target_pairs={{0,8},{4,12},{8,0},{12,4},{1,9},{5,13},{9,1},{13,5},{2,10},{6,14},... | collective-permute-start | bytes 208904 | tf_op jit(solution)/shard_map/ppermute | solution.py:28
  47.8 7.3 %collective-permute-start.19 = (bf16[32,2176]{1,0:T(8,128)(2,1)S(1)}, bf16[32,2176]{1,0:T(8,128)(2,1)S(1)}, u32[]{:S(2)}, u32[]{:S(2)}) collective-permute-start(bf16[32,2176]{1,0:T(8,128)(2,1)S(1)} %pad_maximum_fusion.1), channel_id=1, source_target_pairs={{0,2},{1,3},{2,0},{3,1},{4,6},{5,7},{6,4},{7,5},{8,10},{9,11},{10,... | collective-permute-start | bytes 417800 | tf_op jit(solution)/shard_map/ppermute | solution.py:28
  53.4 5.1 %collective-permute-start.18 = (bf16[32,2176]{1,0:T(8,128)(2,1)S(1)}, bf16[32,2176]{1,0:T(8,128)(2,1)S(1)}, u32[]{:S(2)}, u32[]{:S(2)}) collective-permute-start(bf16[32,2176]{1,0:T(8,128)(2,1)S(1)} %pad_maximum_fusion), channel_id=1, source_target_pairs={{0,2},{1,3},{2,0},{3,1},{4,6},{5,7},{6,4},{7,5},{8,10},{9,11},{10,... | collective-permute-start | bytes 417800 | tf_op jit(solution)/shard_map/ppermute | solution.py:28
  55.1 1.4 %copy-start.2 = (bf16[1,384,2048]{2,1,0:T(8,128)(2,1)S(1)}, bf16[1,384,2048]{2,1,0:T(8,128)(2,1)}, u32[]{:S(2)}) copy-start(bf16[1,384,2048]{2,1,0:T(8,128)(2,1)} %refs_2_.3) | copy-start | bytes 4718596
  57.1 5.7 %collective-permute-start.20 = (bf16[32,2048]{1,0:T(8,128)(2,1)S(1)}, bf16[32,2048]{1,0:T(8,128)(2,1)S(1)}, u32[]{:S(2)}, u32[]{:S(2)}) collective-permute-start(bf16[32,2048]{1,0:T(8,128)(2,1)S(1)} %shard_map.119), channel_id=1, source_target_pairs={{0,2},{1,3},{2,0},{3,1},{4,6},{5,7},{6,4},{7,5},{8,10},{9,11},{10,... | collective-permute-start | bytes 393224 | tf_op jit(solution)/shard_map/ppermute | solution.py:28
  60.6 5.1 %collective-permute-start.21 = (bf16[32,2048]{1,0:T(8,128)(2,1)S(1)}, bf16[32,2048]{1,0:T(8,128)(2,1)S(1)}, u32[]{:S(2)}, u32[]{:S(2)}) collective-permute-start(bf16[32,2048]{1,0:T(8,128)(2,1)S(1)} %get-tuple-element.39), channel_id=1, source_target_pairs={{0,2},{1,3},{2,0},{3,1},{4,6},{5,7},{6,4},{7,5},{8,10},{9,11},{10,... | collective-permute-start | bytes 393224 | tf_op jit(solution)/shard_map/ppermute | solution.py:28
  62.9 5.6 %collective-permute-start.24 = (bf16[16,2048]{1,0:T(8,128)(2,1)S(1)}, bf16[16,2048]{1,0:T(8,128)(2,1)S(1)}, u32[]{:S(2)}, u32[]{:S(2)}) collective-permute-start(bf16[16,2048]{1,0:T(8,128)(2,1)S(1)} %slice.65), channel_id=1, source_target_pairs={{0,4},{4,0},{8,12},{12,8},{1,5},{5,1},{9,13},{13,9},{2,6},{6,2},{1... | collective-permute-start | bytes 196616 | tf_op jit(solution)/shard_map/ppermute | solution.py:28
  65.7 5.6 %collective-permute-start.22 = (bf16[16,2048]{1,0:T(8,128)(2,1)S(1)}, bf16[16,2048]{1,0:T(8,128)(2,1)S(1)}, u32[]{:S(2)}, u32[]{:S(2)}) collective-permute-start(bf16[16,2048]{1,0:T(8,128)(2,1)S(1)} %get-tuple-element.42), channel_id=1, source_target_pairs={{0,8},{4,12},{8,0},{12,4},{1,9},{5,13},{9,1},{13,5},{2,10},{6,14},... | collective-permute-start | bytes 196616 | tf_op jit(solution)/shard_map/ppermute | solution.py:28
  67.1 6.2 %collective-permute-start.23 = (bf16[16,2048]{1,0:T(8,128)(2,1)S(1)}, bf16[16,2048]{1,0:T(8,128)(2,1)S(1)}, u32[]{:S(2)}, u32[]{:S(2)}) collective-permute-start(bf16[16,2048]{1,0:T(8,128)(2,1)S(1)} %get-tuple-element.43), channel_id=1, source_target_pairs={{0,12},{4,8},{8,4},{12,0},{1,13},{5,9},{9,5},{13,1},{2,14},{6,10},... | collective-permute-start | bytes 196616 | tf_op jit(solution)/shard_map/ppermute | solution.py:28

commit v11 on v9

--- a/solution.py
+++ b/solution.py
@@ -179,7 +179,7 @@
         out[...] = pick(place ^ step).astype(jnp.bfloat16)
 
 
-def attention(queries, pages, lengths, out_weight, token_block, later, swapped):
+def attention(queries, pages, lengths, out_weight, token_block):
     fresh_block, width = queries.shape
     rows = width // HEAD * fresh_block
     count = lax.axis_size("ctx")
@@ -208,13 +208,13 @@
         out_shape=partial_shape + (jax.ShapeDtypeStruct((count, HEAD), jnp.int32),),
         in_specs=[SMEM_SPEC]
         + whole_specs(3)
-        + [pl.BlockSpec(memory_space=pl.ANY)] * (1 + len(later)),
+        + [pl.BlockSpec(memory_space=pl.ANY)],
         out_specs=tuple(whole_specs(4)),
         compiler_params=LIMIT,
         cost_estimate=pl.CostEstimate(
             flops=16 * page_flops, bytes_accessed=8 << 20, transcendentals=0
         ),
-    )(lengths, queries, own_keys, own_values, out_weight, *later)
+    )(lengths, queries, own_keys, own_values, out_weight)
     for start in range(0, len(held), 2):
         group = held[start : start + 2]
         operands = [part for _, keys, values in group for part in (keys, values)]
@@ -236,7 +236,7 @@
             jax.ShapeDtypeStruct(block.shape, jnp.float32),
         )
         + (block,) * (exp_count - 1),
-        in_specs=whole_specs(8) + [pl.BlockSpec(memory_space=pl.ANY)] * len(swapped),
+        in_specs=whole_specs(8),
         out_specs=tuple(whole_specs(1 + exp_count)),
         scratch_shapes=[pltpu.VMEM((fresh_block, model_width), jnp.float32)],
         compiler_params=LIMIT,
@@ -245,12 +245,16 @@
             bytes_accessed=6 << 20,
             transcendentals=0,
         ),
-    )(queries, last[1], last[2], page_lengths, *state, out_weight, *swapped)
-    return outs[0], outs[1], outs[2:]
+    )(queries, last[1], last[2], page_lengths, *state, out_weight)
+    return outs[0], outs[1], outs[2:], state[0]
 
 
 def finish_kernel(count, *refs):
-    parts, (residual, gain, ids, scores, hidden_out, sent_out) = refs[:count], refs[count:]
+    parts, (residual, gain, ids, scores), (hidden_out, sent_out) = (
+        refs[:count],
+        refs[count : count + 4],
+        refs[-2:],
+    )
     total = residual[...].astype(jnp.float32)
     for part in parts:
         total = total + part[...].astype(jnp.float32)
@@ -270,7 +274,7 @@
     sent_out[:, width:] = dense.astype(jnp.bfloat16)
 
 
-def finish(parts, residual, norm_gain, ids, scores, expert_count):
+def finish(parts, swapped, residual, norm_gain, ids, scores, expert_count):
     tokens, width = residual.shape
     lanes = -(-expert_count // 128) * 128
     return pl.pallas_call(
@@ -279,13 +283,14 @@
             jax.ShapeDtypeStruct((tokens, width), jnp.bfloat16),
             jax.ShapeDtypeStruct((tokens, width + lanes), jnp.bfloat16),
         ),
-        in_specs=whole_specs(len(parts) + 4),
+        in_specs=whole_specs(len(parts) + 4)
+        + [pl.BlockSpec(memory_space=pl.ANY)] * len(swapped),
         out_specs=tuple(whole_specs(2)),
         compiler_params=LIMIT,
         cost_estimate=pl.CostEstimate(
             flops=8 * residual.size, bytes_accessed=1 << 19, transcendentals=0
         ),
-    )(*parts, residual, norm_gain[None], ids, scores)
+    )(*parts, residual, norm_gain[None], ids, scores, *swapped)
 
 
 def down_kernel(offsets, rows, *refs):
@@ -334,13 +339,10 @@
     )(rows, *inners, *[down for _, _, down in weights])
 
 
-def near_weights(gate_up, down):
-    held = [(0, gate_up, down)]
+def near_parts(part):
+    held = [(0, part)]
     for stride in strides(lax.axis_size("exp"))[1:]:
-        held = held + [
-            (offset ^ stride, swap(first, "exp", stride), swap(second, "exp", stride))
-            for offset, first, second in held
-        ]
+        held = held + [(offset ^ stride, swap(first, "exp", stride)) for offset, first in held]
     return held
 
 
@@ -404,23 +406,23 @@
     token_block, model_width = residual_in.shape[1:]
     token_count = requests * token_block
 
-    weights = near_weights(expert_input, expert_output)
-    swapped = [part for _, *pair in weights[1:] for part in pair]
+    gate_ups = near_parts(expert_input)
     contexts, owns, sents = [], [], []
     for r in range(requests):
-        context, own, sent = attention(
+        context, own, sent, arrived = attention(
             queries[r],
             pages[r],
             cached_lengths[r],
             out_weight,
             token_block,
-            (expert_output,),
-            swapped if r == 0 else (),
         )
         contexts.append(context)
         owns.append(own)
         sents.append(sent)
     context = jnp.stack(contexts)
+    downs = near_parts(lax.optimization_barrier((expert_output, owns[-1]))[0])
+    weights = [(offset, first, down) for (offset, first), (_, down) in zip(gate_ups, downs)]
+    swapped = [part for _, *pair in weights[1:] for part in pair]
 
     parts = [jnp.concatenate(owns, axis=0)]
     for step in range(1, exp_count):
@@ -439,6 +441,7 @@
         )
     own_hidden, normed = finish(
         parts,
+        swapped,
         residual.reshape(-1, model_width),
         norm_gain,
         ids.reshape(-1, ids.shape[2]).T,

time: 67.6 us -> 66.3 us (0.981)
  local copies, waits for them, and re-layouts: 6.39 us -> 4.89 us
    ppermute x6, starting transfers between devices: 11.6 us -> 14 us  [shift(): lax.ppermute(value, axis, [(i, (i + step) % count) for i in range(count)])]
    ppermute x15, starting transfers between devices: 15.1 us -> 13.3 us  [swap(): lax.ppermute(value, axis, [(i, i ^ stride) for i in range(lax.axis_size(a...]
    unnamed x29 -> x27, local copies, waits for them, and re-layouts: 6.33 us -> 4.83 us
    ppermute x6, waiting for transfers between devices: 5.5 us -> 4.56 us  [shift(): lax.ppermute(value, axis, [(i, (i + step) % count) for i in range(count)])]
  transfers between devices with their start and end apart: 21 -> 21, of which waited for: 11 -> 14; matrix products, arithmetic and copies ran while one was open for 6% -> 6% of each run, Pallas kernels for 6% -> 10%
where the time goes in v11:
time: 66.3 us; the launch traced here: 66.1 us
  starting transfers between devices  27.3 us (41%)
  waiting for transfers between devices  23.2 us (35%)
  Pallas kernels  6.59 us (10%)
  local copies, waits for them, and re-layouts  4.89 us (7%)
  matrix products  2.57 us (4%)
  between operations  0.85 us (1%)
  other arithmetic  0.76 us (1%)
    ppermute x15, waiting for transfers between devices, swap(): lax.ppermute(value, axis, [(i, i ^ stride) for i in range(lax.axis_size(a...  18.6 us
    ppermute x6, starting transfers between devices, shift(): lax.ppermute(value, axis, [(i, (i + step) % count) for i in range(count)])  14 us
    ppermute x15, starting transfers between devices, swap(): lax.ppermute(value, axis, [(i, i ^ stride) for i in range(lax.axis_size(a...  13.3 us
    unnamed x27, local copies, waits for them, and re-layouts  4.83 us
    ppermute x6, waiting for transfers between devices, shift(): lax.ppermute(value, axis, [(i, (i + step) % count) for i in range(count)])  4.56 us
    dot_general x4, matrix products, expert_apply(): jnp.einsum('nd,dgh->gnh', rows[:, :width], gate_up[0], preferred_element_...  2.57 us
    pallas_call x1, Pallas kernels, attention(): pl.pallas_call(functools.partial(late_kernel, last[0], fresh_block, exp_c...  2.16 us
    pallas_call x2, Pallas kernels, expert_apply(): pl.pallas_call(functools.partial(down_kernel, [offset for offset, _, _ in...  1.44 us
  transfers between devices with their start and end apart: 21, of which 14 were waited for; matrix products, arithmetic and copies ran while one was open for 6% of the time, Pallas kernels for 10%

profile of v11, /device:TPU:0, one launch (start us, length us, event | category | flops | bytes accessed | tf_op | source)
XLA Modules:
  0.0 66.1 jit_solution(10872217655475312064)
XLA Ops:
  0.6 0.5 collective-permute-start.9
  1.1 1.0 %copy.34 = bf16[1,576,2,128]{3,1,2,0:T(8,128)(2,1)S(1)} copy(bf16[1,576,2,128]{3,2,1,0:T(2,128)(2,1)} %param.11) | data formatting | bytes 589824 | tf_op args[1]
  2.2 4.7 %collective-permute-start.2 = (bf16[576,128]{1,0:T(8,128)(2,1)S(1)}, bf16[576,128]{1,0:T(8,128)(2,1)S(1)}, u32[]{:S(2)}, u32[]{:S(2)}) collective-permute-start(bf16[576,128]{1,0:T(8,128)(2,1)S(1)} %get-tuple-element.38.values), channel_id=1, source_target_pairs={{0,12},{4,0},{8,4},{12,8},{1,13},{5,1},{9,5},{13,9},{2,14},{6,2},{... | collective-permute-start | bytes 442376 | tf_op jit(solution)/shard_map/ppermute | solution.py:33
  6.9 3.9 %collective-permute-start.5 = (bf16[576,128]{1,0:T(8,128)(2,1)S(1)}, bf16[576,128]{1,0:T(8,128)(2,1)S(1)}, u32[]{:S(2)}, u32[]{:S(2)}) collective-permute-start(bf16[576,128]{1,0:T(8,128)(2,1)S(1)} %get-tuple-element.39.keys), channel_id=1, source_target_pairs={{0,12},{4,0},{8,4},{12,8},{1,13},{5,1},{9,5},{13,9},{2,14},{6,2},{... | collective-permute-start | bytes 442376 | tf_op jit(solution)/shard_map/ppermute | solution.py:33
  10.7 0.3 collective-permute-done.2.refs_3_
  11.1 4.3 %collective-permute-start.3 = (bf16[576,128]{1,0:T(8,128)(2,1)S(1)}, bf16[576,128]{1,0:T(8,128)(2,1)S(1)}, u32[]{:S(2)}, u32[]{:S(2)}) collective-permute-start(bf16[576,128]{1,0:T(8,128)(2,1)S(1)} %collective-permute-done.2.refs_3_), channel_id=1, source_target_pairs={{0,12},{4,0},{8,4},{12,8},{1,13},{5,1},{9,5},{13,9},{2,14},{6,2},{... | collective-permute-start | bytes 442376 | tf_op jit(solution)/shard_map/ppermute | solution.py:33
  15.3 0.1 collective-permute-done.refs_0_
  15.5 1.2 %collective-permute-start.1 = (bf16[576,128]{1,0:T(8,128)(2,1)S(1)}, bf16[576,128]{1,0:T(8,128)(2,1)S(1)}, u32[]{:S(2)}, u32[]{:S(2)}) collective-permute-start(bf16[576,128]{1,0:T(8,128)(2,1)S(1)} %collective-permute-done.refs_0_), channel_id=1, source_target_pairs={{0,4},{4,8},{8,12},{12,0},{1,5},{5,9},{9,13},{13,1},{2,6},{6,10},{... | collective-permute-start | bytes 442376 | tf_op jit(solution)/shard_map/ppermute | solution.py:33
  16.7 2.2 %copy-done.1 = bf16[1024,2048]{1,0:T(8,128)(2,1)S(1)} copy-done((bf16[1024,2048]{1,0:T(8,128)(2,1)S(1)}, bf16[1024,2048]{1,0:T(8,128)(2,1)}, u32[]{:S(2)}) %copy-start.1) | copy-done | bytes 4194328
  18.9 0.9 %copy-done.3 = bf16[1,64,1024]{2,1,0:T(8,128)(2,1)S(1)} copy-done((bf16[1,64,1024]{2,1,0:T(8,128)(2,1)S(1)}, bf16[1,64,1024]{2,1,0:T(8,128)(2,1)}, u32[]{:S(2)}) %copy-start.3) | copy-done | bytes 131096
  19.8 0.7 copy-done.9
  20.4 1.3 %shard_map.113 = (f32[1,512]{1,0:T(1,128)S(1)}, f32[1,512]{1,0:T(1,128)S(1)}, f32[128,512]{1,0:T(8,128)S(1)}, s32[4,128]{1,0:T(4,128)S(1)}) custom-call(s32[4]{0:T(128)S(1)} %bitcast.47, bf16[64,1024]{1,0:T(8,128)(2,1)S(1)} %bitcast.40, bf16[576,128]{1,0:T(8,128)(2,1)S(1)} %get-tuple-element.39.keys, bf16[576,128]{1,0:T(8,128)(2,1)S(1)} %get-tuple-element.38.values, ...), custom_call_target="tpu_custom_call" | custom-call | flops 2415919104 | bytes 8388608 | tf_op jit(solution)/shard_map/pallas_call | solution.py:206
  21.8 0.0 copy-start.5
  21.8 0.0 copy-start.6
  21.9 1.4 %shard_map.114 = (f32[1,512]{1,0:T(1,128)S(1)}, f32[1,512]{1,0:T(1,128)S(1)}, f32[128,512]{1,0:T(8,128)S(1)}) custom-call(bf16[64,1024]{1,0:T(8,128)(2,1)S(1)} %bitcast.41, s32[4,128]{1,0:T(4,128)S(1)} %get-tuple-element.20.lengths, bf16[576,128]{1,0:T(8,128)(2,1)S(1)} %collective-permute-done.refs_0_, bf16[576,128]{1,0:T(8,128)(2,1)S(1)} %collective-permute-done.4.refs_1_, ...), custom_call_target="tpu_custom_call" | custom-call | flops 301989888 | bytes 2097152 | tf_op jit(solution)/shard_map/pallas_call | solution.py:221
  23.3 0.4 collective-permute-done.3.values
  23.7 3.6 %collective-permute-done.1.keys = bf16[576,128]{1,0:T(8,128)(2,1)S(1)} collective-permute-done((bf16[576,128]{1,0:T(8,128)(2,1)S(1)}, bf16[576,128]{1,0:T(8,128)(2,1)S(1)}, u32[]{:S(2)}, u32[]{:S(2)}) %collective-permute-start.1) | collective-permute-done | bytes 147488 | tf_op jit(solution)/shard_map/ppermute | solution.py:33
  27.4 2.2 %shard_map.115 = (bf16[64,1024]{1,0:T(8,128)(2,1)}, f32[16,2048]{1,0:T(8,128)S(1)}, bf16[16,2048]{1,0:T(8,128)(2,1)S(1)}, bf16[16,2048]{1,0:T(8,128)(2,1)S(1)}, bf16[16,2048]{1,0:T(8,128)(2,1)S(1)}) custom-call(bf16[64,1024]{1,0:T(8,128)(2,1)S(1)} %bitcast.42, bf16[576,128]{1,0:T(8,128)(2,1)S(1)} %collective-permute-done.1.keys, ...), custom_call_target="tpu_custom_call" | custom-call | flops 419430400 | bytes 6291456 | tf_op jit(solution)/shard_map/pallas_call | solution.py:232
  29.5 0.5 collective-permute-start.6
  30.0 1.5 %collective-permute-start.7 = (bf16[16,2048]{1,0:T(8,128)(2,1)S(1)}, bf16[16,2048]{1,0:T(8,128)(2,1)S(1)}, u32[]{:S(2)}, u32[]{:S(2)}) collective-permute-start(bf16[16,2048]{1,0:T(8,128)(2,1)S(1)} %get-tuple-element.30), channel_id=1, source_target_pairs={{0,2},{1,3},{2,0},{3,1},{4,6},{5,7},{6,4},{7,5},{8,10},{9,11},{10,... | collective-permute-start | bytes 196616 | tf_op jit(solution)/shard_map/ppermute | solution.py:28
  31.5 1.5 %collective-permute-done.6.refs_1_ = bf16[16,2048]{1,0:T(8,128)(2,1)S(1)} collective-permute-done((bf16[16,2048]{1,0:T(8,128)(2,1)S(1)}, bf16[16,2048]{1,0:T(8,128)(2,1)S(1)}, u32[]{:S(2)}, u32[]{:S(2)}) %collective-permute-start.6) | collective-permute-done | bytes 65568 | tf_op jit(solution)/shard_map/ppermute | solution.py:28
  33.0 1.3 %collective-permute-done.7.refs_2_ = bf16[16,2048]{1,0:T(8,128)(2,1)S(1)} collective-permute-done((bf16[16,2048]{1,0:T(8,128)(2,1)S(1)}, bf16[16,2048]{1,0:T(8,128)(2,1)S(1)}, u32[]{:S(2)}, u32[]{:S(2)}) %collective-permute-start.7) | collective-permute-done | bytes 65568 | tf_op jit(solution)/shard_map/ppermute | solution.py:28
  34.3 1.5 %collective-permute-done.8.refs_3_ = bf16[16,2048]{1,0:T(8,128)(2,1)S(1)} collective-permute-done((bf16[16,2048]{1,0:T(8,128)(2,1)S(1)}, bf16[16,2048]{1,0:T(8,128)(2,1)S(1)}, u32[]{:S(2)}, u32[]{:S(2)}) %collective-permute-start.8) | collective-permute-done | bytes 65568 | tf_op jit(solution)/shard_map/ppermute | solution.py:28
  35.9 0.3 shard_map.116
  36.1 1.7 %collective-permute-start.13 = (bf16[16,2176]{1,0:T(8,128)(2,1)S(1)}, bf16[16,2176]{1,0:T(8,128)(2,1)S(1)}, u32[]{:S(2)}, u32[]{:S(2)}) collective-permute-start(bf16[16,2176]{1,0:T(8,128)(2,1)S(1)} %get-tuple-element.34), channel_id=1, source_target_pairs={{0,4},{4,0},{8,12},{12,8},{1,5},{5,1},{9,13},{13,9},{2,6},{6,2},{1... | collective-permute-start | bytes 208904 | tf_op jit(solution)/shard_map/ppermute | solution.py:28
  37.8 0.5 collective-permute-start.12
  38.4 1.3 %collective-permute-start.11 = (bf16[16,2176]{1,0:T(8,128)(2,1)S(1)}, bf16[16,2176]{1,0:T(8,128)(2,1)S(1)}, u32[]{:S(2)}, u32[]{:S(2)}) collective-permute-start(bf16[16,2176]{1,0:T(8,128)(2,1)S(1)} %get-tuple-element.34), channel_id=1, source_target_pairs={{0,8},{4,12},{8,0},{12,4},{1,9},{5,13},{9,1},{13,5},{2,10},{6,14},... | collective-permute-start | bytes 208904 | tf_op jit(solution)/shard_map/ppermute | solution.py:28
  39.7 0.8 %collective-permute-done.13 = bf16[16,2176]{1,0:T(8,128)(2,1)S(1)} collective-permute-done((bf16[16,2176]{1,0:T(8,128)(2,1)S(1)}, bf16[16,2176]{1,0:T(8,128)(2,1)S(1)}, u32[]{:S(2)}, u32[]{:S(2)}) %collective-permute-start.13) | collective-permute-done | bytes 69664 | tf_op jit(solution)/shard_map/ppermute | solution.py:28
  40.5 1.0 %collective-permute-start.15 = (bf16[32,2176]{1,0:T(8,128)(2,1)S(1)}, bf16[32,2176]{1,0:T(8,128)(2,1)S(1)}, u32[]{:S(2)}, u32[]{:S(2)}) collective-permute-start(bf16[32,2176]{1,0:T(8,128)(2,1)S(1)} %pad_maximum_fusion.1), channel_id=1, source_target_pairs={{0,2},{1,3},{2,0},{3,1},{4,6},{5,7},{6,4},{7,5},{8,10},{9,11},{10,... | collective-permute-start | bytes 417800 | tf_op jit(solution)/shard_map/ppermute | solution.py:28
  41.5 2.8 %collective-permute-done.12 = bf16[16,2176]{1,0:T(8,128)(2,1)S(1)} collective-permute-done((bf16[16,2176]{1,0:T(8,128)(2,1)S(1)}, bf16[16,2176]{1,0:T(8,128)(2,1)S(1)}, u32[]{:S(2)}, u32[]{:S(2)}) %collective-permute-start.12) | collective-permute-done | bytes 69664 | tf_op jit(solution)/shard_map/ppermute | solution.py:28
  44.3 2.1 %collective-permute-done.11 = bf16[16,2176]{1,0:T(8,128)(2,1)S(1)} collective-permute-done((bf16[16,2176]{1,0:T(8,128)(2,1)S(1)}, bf16[16,2176]{1,0:T(8,128)(2,1)S(1)}, u32[]{:S(2)}, u32[]{:S(2)}) %collective-permute-start.11) | collective-permute-done | bytes 69664 | tf_op jit(solution)/shard_map/ppermute | solution.py:28
  46.5 0.7 %collective-permute-start.14 = (bf16[32,2176]{1,0:T(8,128)(2,1)S(1)}, bf16[32,2176]{1,0:T(8,128)(2,1)S(1)}, u32[]{:S(2)}, u32[]{:S(2)}) collective-permute-start(bf16[32,2176]{1,0:T(8,128)(2,1)S(1)} %pad_maximum_fusion), channel_id=1, source_target_pairs={{0,2},{1,3},{2,0},{3,1},{4,6},{5,7},{6,4},{7,5},{8,10},{9,11},{10,... | collective-permute-start | bytes 417800 | tf_op jit(solution)/shard_map/ppermute | solution.py:28
  47.2 0.6 fusion.17.refs_1_
  47.9 0.7 fusion.14.refs_0_
  48.6 0.7 %shard_map.118 = bf16[32,2048]{1,0:T(8,128)(2,1)S(1)} custom-call(bf16[32,2176]{1,0:T(8,128)(2,1)S(1)} %collective-permute-done.15.rows, f32[2,32,384]{2,1,0:T(8,128)S(1)} %fusion.14.refs_0_, f32[2,32,384]{2,1,0:T(8,128)S(1)} %fusion.17.refs_1_, bf16[1,384,2048]{2,1,0:T(8,128)(2,1)S(1)} %copy-done, ...), custom_call_target="tpu_custom_call" | custom-call | flops 100663296 | bytes 2097152 | tf_op jit(solution)/shard_map/pallas_call | solution.py:325
  49.2 1.4 %collective-permute-start.16 = (bf16[32,2048]{1,0:T(8,128)(2,1)S(1)}, bf16[32,2048]{1,0:T(8,128)(2,1)S(1)}, u32[]{:S(2)}, u32[]{:S(2)}) collective-permute-start(bf16[32,2048]{1,0:T(8,128)(2,1)S(1)} %shard_map.118), channel_id=1, source_target_pairs={{0,2},{1,3},{2,0},{3,1},{4,6},{5,7},{6,4},{7,5},{8,10},{9,11},{10,... | collective-permute-start | bytes 393224 | tf_op jit(solution)/shard_map/ppermute | solution.py:28
  50.7 1.3 %collective-permute-done.14 = bf16[32,2176]{1,0:T(8,128)(2,1)S(1)} collective-permute-done((bf16[32,2176]{1,0:T(8,128)(2,1)S(1)}, bf16[32,2176]{1,0:T(8,128)(2,1)S(1)}, u32[]{:S(2)}, u32[]{:S(2)}) %collective-permute-start.14) | collective-permute-done | bytes 139296 | tf_op jit(solution)/shard_map/ppermute | solution.py:28
  52.0 0.6 fusion.11.refs_1_
  52.7 0.6 fusion.8.refs_0_
  53.3 0.8 %shard_map.117 = (f32[32,2048]{1,0:T(8,128)S(1)}, f32[32,2048]{1,0:T(8,128)S(1)}, bf16[32,2048]{1,0:T(8,128)(2,1)S(1)}) custom-call(bf16[96,2176]{1,0:T(8,128)(2,1)S(1)} %constant_dynamic-update-slice_fusion.rows, f32[2,96,384]{2,1,0:T(8,128)S(1)} %fusion.8.refs_0_, f32[2,96,384]{2,1,0:T(8,128)S(1)} %fusion.11.refs_1_, bf16[1,384,2048]{2,1,0:T(8,128)(2,1)S(1)} %copy-done, ...), custom_call_target="tpu_custom_call" | custom-call | flops 301989888 | bytes 2097152 | tf_op jit(solution)/shard_map/pallas_call | solution.py:325
  54.1 0.4 collective-permute-start.17
  54.5 1.6 %collective-permute-start.20 = (bf16[16,2048]{1,0:T(8,128)(2,1)S(1)}, bf16[16,2048]{1,0:T(8,128)(2,1)S(1)}, u32[]{:S(2)}, u32[]{:S(2)}) collective-permute-start(bf16[16,2048]{1,0:T(8,128)(2,1)S(1)} %slice.65), channel_id=1, source_target_pairs={{0,4},{4,0},{8,12},{12,8},{1,5},{5,1},{9,13},{13,9},{2,6},{6,2},{1... | collective-permute-start | bytes 196616 | tf_op jit(solution)/shard_map/ppermute | solution.py:28
  56.1 3.0 %collective-permute-done.17 = bf16[32,2048]{1,0:T(8,128)(2,1)S(1)} collective-permute-done((bf16[32,2048]{1,0:T(8,128)(2,1)S(1)}, bf16[32,2048]{1,0:T(8,128)(2,1)S(1)}, u32[]{:S(2)}, u32[]{:S(2)}) %collective-permute-start.17) | collective-permute-done | bytes 131104 | tf_op jit(solution)/shard_map/ppermute | solution.py:28
  59.2 0.1 collective-permute-start.18
  59.2 2.0 %collective-permute-start.19 = (bf16[16,2048]{1,0:T(8,128)(2,1)S(1)}, bf16[16,2048]{1,0:T(8,128)(2,1)S(1)}, u32[]{:S(2)}, u32[]{:S(2)}) collective-permute-start(bf16[16,2048]{1,0:T(8,128)(2,1)S(1)} %get-tuple-element.41), channel_id=1, source_target_pairs={{0,12},{4,8},{8,4},{12,0},{1,13},{5,9},{9,5},{13,1},{2,14},{6,10},... | collective-permute-start | bytes 196616 | tf_op jit(solution)/shard_map/ppermute | solution.py:28
  61.2 3.2 %collective-permute-done.18 = bf16[16,2048]{1,0:T(8,128)(2,1)S(1)} collective-permute-done((bf16[16,2048]{1,0:T(8,128)(2,1)S(1)}, bf16[16,2048]{1,0:T(8,128)(2,1)S(1)}, u32[]{:S(2)}, u32[]{:S(2)}) %collective-permute-start.18) | collective-permute-done | bytes 65568 | tf_op jit(solution)/shard_map/ppermute | solution.py:28
  64.4 1.0 %collective-permute-done.19 = bf16[16,2048]{1,0:T(8,128)(2,1)S(1)} collective-permute-done((bf16[16,2048]{1,0:T(8,128)(2,1)S(1)}, bf16[16,2048]{1,0:T(8,128)(2,1)S(1)}, u32[]{:S(2)}, u32[]{:S(2)}) %collective-permute-start.19) | collective-permute-done | bytes 65568 | tf_op jit(solution)/shard_map/ppermute | solution.py:28
  65.4 0.7 %fusion.24 = bf16[1,16,2048]{2,1,0:T(8,128)(2,1)} fusion(bf16[16,2048]{1,0:T(8,128)(2,1)S(1)} %collective-permute-done.20, bf16[16,2048]{1,0:T(8,128)(2,1)S(1)} %collective-permute-done.19, bf16[16,2048]{1,0:T(8,128)(2,1)S(1)} %collective-permute-done.18, f32[32,2048]{1,0:T(8,128)S(1)} %convert_add_fusion, bf16[16,2048]{1,0:T(8,128)(2,1)S(1)} %get-tuple-element.33), kind=kLoop, calls=%fused_computation.27 | loop fusion | flops 294912 | bytes 458752 | tf_op jit(solution)/shard_map/convert_element_type | solution.py:463
  (40 shorter events, 0.3 us)
Async XLA Ops:
  0.6 35.2 %collective-permute-start.9 = (bf16[1,2048,2,384]{3,2,1,0:T(2,128)(2,1)}, bf16[1,2048,2,384]{3,2,1,0:T(2,128)(2,1)S(1)}, u32[]{:S(2)}, u32[]{:S(2)}) collective-permute-start(bf16[1,2048,2,384]{3,2,1,0:T(2,128)(2,1)} %param.18), channel_id=1, source_target_pairs={{0,1},{1,0},{2,3},{3,2},{4,5},{5,4},{6,7},{7,6},{8,9},{9,8},{10,11... | collective-permute-start | bytes 9437192 | tf_op jit(solution)/shard_map/ppermute | solution.py:28
  2.2 8.9 %collective-permute-start.2 = (bf16[576,128]{1,0:T(8,128)(2,1)S(1)}, bf16[576,128]{1,0:T(8,128)(2,1)S(1)}, u32[]{:S(2)}, u32[]{:S(2)}) collective-permute-start(bf16[576,128]{1,0:T(8,128)(2,1)S(1)} %get-tuple-element.38.values), channel_id=1, source_target_pairs={{0,12},{4,0},{8,4},{12,8},{1,13},{5,1},{9,5},{13,9},{2,14},{6,2},{... | collective-permute-start | bytes 442376 | tf_op jit(solution)/shard_map/ppermute | solution.py:33
  6.8 8.6 %collective-permute-start = (bf16[576,128]{1,0:T(8,128)(2,1)S(1)}, bf16[576,128]{1,0:T(8,128)(2,1)S(1)}, u32[]{:S(2)}, u32[]{:S(2)}) collective-permute-start(bf16[576,128]{1,0:T(8,128)(2,1)S(1)} %get-tuple-element.39.keys), channel_id=1, source_target_pairs={{0,4},{4,8},{8,12},{12,0},{1,5},{5,9},{9,13},{13,1},{2,6},{6,10},{... | collective-permute-start | bytes 442376 | tf_op jit(solution)/shard_map/ppermute | solution.py:33
  6.8 15.0 %collective-permute-start.4 = (bf16[576,128]{1,0:T(8,128)(2,1)S(1)}, bf16[576,128]{1,0:T(8,128)(2,1)S(1)}, u32[]{:S(2)}, u32[]{:S(2)}) collective-permute-start(bf16[576,128]{1,0:T(8,128)(2,1)S(1)} %get-tuple-element.38.values), channel_id=1, source_target_pairs={{0,4},{4,8},{8,12},{12,0},{1,5},{5,9},{9,13},{13,1},{2,6},{6,10},{... | collective-permute-start | bytes 442376 | tf_op jit(solution)/shard_map/ppermute | solution.py:33
  6.9 15.0 %collective-permute-start.5 = (bf16[576,128]{1,0:T(8,128)(2,1)S(1)}, bf16[576,128]{1,0:T(8,128)(2,1)S(1)}, u32[]{:S(2)}, u32[]{:S(2)}) collective-permute-start(bf16[576,128]{1,0:T(8,128)(2,1)S(1)} %get-tuple-element.39.keys), channel_id=1, source_target_pairs={{0,12},{4,0},{8,4},{12,8},{1,13},{5,1},{9,5},{13,9},{2,14},{6,2},{... | collective-permute-start | bytes 442376 | tf_op jit(solution)/shard_map/ppermute | solution.py:33
  11.1 12.7 %collective-permute-start.3 = (bf16[576,128]{1,0:T(8,128)(2,1)S(1)}, bf16[576,128]{1,0:T(8,128)(2,1)S(1)}, u32[]{:S(2)}, u32[]{:S(2)}) collective-permute-start(bf16[576,128]{1,0:T(8,128)(2,1)S(1)} %collective-permute-done.2.refs_3_), channel_id=1, source_target_pairs={{0,12},{4,0},{8,4},{12,8},{1,13},{5,1},{9,5},{13,9},{2,14},{6,2},{... | collective-permute-start | bytes 442376 | tf_op jit(solution)/shard_map/ppermute | solution.py:33
  15.5 11.9 %collective-permute-start.1 = (bf16[576,128]{1,0:T(8,128)(2,1)S(1)}, bf16[576,128]{1,0:T(8,128)(2,1)S(1)}, u32[]{:S(2)}, u32[]{:S(2)}) collective-permute-start(bf16[576,128]{1,0:T(8,128)(2,1)S(1)} %collective-permute-done.refs_0_), channel_id=1, source_target_pairs={{0,4},{4,8},{8,12},{12,0},{1,5},{5,9},{9,13},{13,1},{2,6},{6,10},{... | collective-permute-start | bytes 442376 | tf_op jit(solution)/shard_map/ppermute | solution.py:33
  16.7 2.2 %copy-start.1 = (bf16[1024,2048]{1,0:T(8,128)(2,1)S(1)}, bf16[1024,2048]{1,0:T(8,128)(2,1)}, u32[]{:S(2)}) copy-start(bf16[1024,2048]{1,0:T(8,128)(2,1)} %weight.1) | copy-start | bytes 12582916
  18.9 0.9 %copy-start.3 = (bf16[1,64,1024]{2,1,0:T(8,128)(2,1)S(1)}, bf16[1,64,1024]{2,1,0:T(8,128)(2,1)}, u32[]{:S(2)}) copy-start(bf16[1,64,1024]{2,1,0:T(8,128)(2,1)} %param.10) | copy-start | bytes 393220
  19.8 0.7 copy-start.9
  20.4 1.4 %copy-start.4 = (bf16[1,64,1024]{2,1,0:T(8,128)(2,1)S(1)}, bf16[1,64,1024]{2,1,0:T(8,128)(2,1)}, u32[]{:S(2)}) copy-start(bf16[1,64,1024]{2,1,0:T(8,128)(2,1)} %param.10) | copy-start | bytes 393220
  20.4 6.9 %copy-start.2 = (bf16[1024,2048]{1,0:T(8,128)(2,1)S(1)}, bf16[1024,2048]{1,0:T(8,128)(2,1)}, u32[]{:S(2)}) copy-start(bf16[1024,2048]{1,0:T(8,128)(2,1)} %weight.1) | copy-start | bytes 12582916
  21.8 7.8 %copy-start = (bf16[1,384,2048]{2,1,0:T(8,128)(2,1)S(1)}, bf16[1,384,2048]{2,1,0:T(8,128)(2,1)}, u32[]{:S(2)}) copy-start(bf16[1,384,2048]{2,1,0:T(8,128)(2,1)} %refs_2_.1) | copy-start | bytes 4718596
  21.8 14.1 %copy-start.5 = (bf16[1,16,2048]{2,1,0:T(8,128)(2,1)S(1)}, bf16[1,16,2048]{2,1,0:T(8,128)(2,1)}, u32[]{:S(2)}) copy-start(bf16[1,16,2048]{2,1,0:T(8,128)(2,1)} %param.13) | copy-start | bytes 196612
  21.8 14.1 %copy-start.6 = (f32[2048]{0:T(1024)S(1)}, f32[2048]{0:T(1024)}, u32[]{:S(2)}) copy-start(f32[2048]{0:T(1024)} %param.15) | copy-start | bytes 24580
  21.8 14.1 %copy-start.7 = (s32[1,16,8]{1,2,0:T(8,128)S(1)}, s32[1,16,8]{1,2,0:T(8,128)}, u32[]{:S(2)}) copy-start(s32[1,16,8]{1,2,0:T(8,128)} %param.16) | copy-start | bytes 1540
  21.8 14.1 %copy-start.8 = (f32[1,16,8]{1,2,0:T(8,128)S(1)}, f32[1,16,8]{1,2,0:T(8,128)}, u32[]{:S(2)}) copy-start(f32[1,16,8]{1,2,0:T(8,128)} %param.17) | copy-start | bytes 1540
  29.5 6.3 %collective-permute-start.10 = (bf16[1,384,2048]{2,1,0:T(8,128)(2,1)S(1)}, bf16[1,384,2048]{2,1,0:T(8,128)(2,1)S(1)}, u32[]{:S(2)}, u32[]{:S(2)}) collective-permute-start(bf16[1,384,2048]{2,1,0:T(8,128)(2,1)S(1)} %copy-done), channel_id=1, source_target_pairs={{0,1},{1,0},{2,3},{3,2},{4,5},{5,4},{6,7},{7,6},{8,9},{9,8},{10,11... | collective-permute-start | bytes 4718600 | tf_op jit(solution)/shard_map/ppermute | solution.py:28
  29.5 3.5 %collective-permute-start.6 = (bf16[16,2048]{1,0:T(8,128)(2,1)S(1)}, bf16[16,2048]{1,0:T(8,128)(2,1)S(1)}, u32[]{:S(2)}, u32[]{:S(2)}) collective-permute-start(bf16[16,2048]{1,0:T(8,128)(2,1)S(1)} %get-tuple-element.29), channel_id=1, source_target_pairs={{0,1},{1,0},{2,3},{3,2},{4,5},{5,4},{6,7},{7,6},{8,9},{9,8},{10,11... | collective-permute-start | bytes 196616 | tf_op jit(solution)/shard_map/ppermute | solution.py:28
  30.0 4.3 %collective-permute-start.7 = (bf16[16,2048]{1,0:T(8,128)(2,1)S(1)}, bf16[16,2048]{1,0:T(8,128)(2,1)S(1)}, u32[]{:S(2)}, u32[]{:S(2)}) collective-permute-start(bf16[16,2048]{1,0:T(8,128)(2,1)S(1)} %get-tuple-element.30), channel_id=1, source_target_pairs={{0,2},{1,3},{2,0},{3,1},{4,6},{5,7},{6,4},{7,5},{8,10},{9,11},{10,... | collective-permute-start | bytes 196616 | tf_op jit(solution)/shard_map/ppermute | solution.py:28
  31.5 4.3 %collective-permute-start.8 = (bf16[16,2048]{1,0:T(8,128)(2,1)S(1)}, bf16[16,2048]{1,0:T(8,128)(2,1)S(1)}, u32[]{:S(2)}, u32[]{:S(2)}) collective-permute-start(bf16[16,2048]{1,0:T(8,128)(2,1)S(1)} %get-tuple-element.31), channel_id=1, source_target_pairs={{0,3},{1,2},{2,1},{3,0},{4,7},{5,6},{6,5},{7,4},{8,11},{9,10},{10,... | collective-permute-start | bytes 196616 | tf_op jit(solution)/shard_map/ppermute | solution.py:28
  36.1 11.8 %copy-start.10 = (bf16[1,2048,2,384]{3,2,1,0:T(2,128)(2,1)S(1)}, bf16[1,2048,2,384]{3,2,1,0:T(2,128)(2,1)}, u32[]{:S(2)}) copy-start(bf16[1,2048,2,384]{3,2,1,0:T(2,128)(2,1)} %param.18) | copy-start | bytes 9437188
  36.1 4.4 %collective-permute-start.13 = (bf16[16,2176]{1,0:T(8,128)(2,1)S(1)}, bf16[16,2176]{1,0:T(8,128)(2,1)S(1)}, u32[]{:S(2)}, u32[]{:S(2)}) collective-permute-start(bf16[16,2176]{1,0:T(8,128)(2,1)S(1)} %get-tuple-element.34), channel_id=1, source_target_pairs={{0,4},{4,0},{8,12},{12,8},{1,5},{5,1},{9,13},{13,9},{2,6},{6,2},{1... | collective-permute-start | bytes 208904 | tf_op jit(solution)/shard_map/ppermute | solution.py:28
  37.8 6.5 %collective-permute-start.12 = (bf16[16,2176]{1,0:T(8,128)(2,1)S(1)}, bf16[16,2176]{1,0:T(8,128)(2,1)S(1)}, u32[]{:S(2)}, u32[]{:S(2)}) collective-permute-start(bf16[16,2176]{1,0:T(8,128)(2,1)S(1)} %get-tuple-element.34), channel_id=1, source_target_pairs={{0,12},{4,8},{8,4},{12,0},{1,13},{5,9},{9,5},{13,1},{2,14},{6,10},... | collective-permute-start | bytes 208904 | tf_op jit(solution)/shard_map/ppermute | solution.py:28
  38.4 8.1 %collective-permute-start.11 = (bf16[16,2176]{1,0:T(8,128)(2,1)S(1)}, bf16[16,2176]{1,0:T(8,128)(2,1)S(1)}, u32[]{:S(2)}, u32[]{:S(2)}) collective-permute-start(bf16[16,2176]{1,0:T(8,128)(2,1)S(1)} %get-tuple-element.34), channel_id=1, source_target_pairs={{0,8},{4,12},{8,0},{12,4},{1,9},{5,13},{9,1},{13,5},{2,10},{6,14},... | collective-permute-start | bytes 208904 | tf_op jit(solution)/shard_map/ppermute | solution.py:28
  40.5 6.7 %collective-permute-start.15 = (bf16[32,2176]{1,0:T(8,128)(2,1)S(1)}, bf16[32,2176]{1,0:T(8,128)(2,1)S(1)}, u32[]{:S(2)}, u32[]{:S(2)}) collective-permute-start(bf16[32,2176]{1,0:T(8,128)(2,1)S(1)} %pad_maximum_fusion.1), channel_id=1, source_target_pairs={{0,2},{1,3},{2,0},{3,1},{4,6},{5,7},{6,4},{7,5},{8,10},{9,11},{10,... | collective-permute-start | bytes 417800 | tf_op jit(solution)/shard_map/ppermute | solution.py:28
  46.5 5.5 %collective-permute-start.14 = (bf16[32,2176]{1,0:T(8,128)(2,1)S(1)}, bf16[32,2176]{1,0:T(8,128)(2,1)S(1)}, u32[]{:S(2)}, u32[]{:S(2)}) collective-permute-start(bf16[32,2176]{1,0:T(8,128)(2,1)S(1)} %pad_maximum_fusion), channel_id=1, source_target_pairs={{0,2},{1,3},{2,0},{3,1},{4,6},{5,7},{6,4},{7,5},{8,10},{9,11},{10,... | collective-permute-start | bytes 417800 | tf_op jit(solution)/shard_map/ppermute | solution.py:28
  49.2 5.2 %collective-permute-start.16 = (bf16[32,2048]{1,0:T(8,128)(2,1)S(1)}, bf16[32,2048]{1,0:T(8,128)(2,1)S(1)}, u32[]{:S(2)}, u32[]{:S(2)}) collective-permute-start(bf16[32,2048]{1,0:T(8,128)(2,1)S(1)} %shard_map.118), channel_id=1, source_target_pairs={{0,2},{1,3},{2,0},{3,1},{4,6},{5,7},{6,4},{7,5},{8,10},{9,11},{10,... | collective-permute-start | bytes 393224 | tf_op jit(solution)/shard_map/ppermute | solution.py:28
  54.1 5.0 %collective-permute-start.17 = (bf16[32,2048]{1,0:T(8,128)(2,1)S(1)}, bf16[32,2048]{1,0:T(8,128)(2,1)S(1)}, u32[]{:S(2)}, u32[]{:S(2)}) collective-permute-start(bf16[32,2048]{1,0:T(8,128)(2,1)S(1)} %get-tuple-element.37), channel_id=1, source_target_pairs={{0,2},{1,3},{2,0},{3,1},{4,6},{5,7},{6,4},{7,5},{8,10},{9,11},{10,... | collective-permute-start | bytes 393224 | tf_op jit(solution)/shard_map/ppermute | solution.py:28
  54.5 6.7 %collective-permute-start.20 = (bf16[16,2048]{1,0:T(8,128)(2,1)S(1)}, bf16[16,2048]{1,0:T(8,128)(2,1)S(1)}, u32[]{:S(2)}, u32[]{:S(2)}) collective-permute-start(bf16[16,2048]{1,0:T(8,128)(2,1)S(1)} %slice.65), channel_id=1, source_target_pairs={{0,4},{4,0},{8,12},{12,8},{1,5},{5,1},{9,13},{13,9},{2,6},{6,2},{1... | collective-permute-start | bytes 196616 | tf_op jit(solution)/shard_map/ppermute | solution.py:28
  59.2 5.2 %collective-permute-start.18 = (bf16[16,2048]{1,0:T(8,128)(2,1)S(1)}, bf16[16,2048]{1,0:T(8,128)(2,1)S(1)}, u32[]{:S(2)}, u32[]{:S(2)}) collective-permute-start(bf16[16,2048]{1,0:T(8,128)(2,1)S(1)} %get-tuple-element.40), channel_id=1, source_target_pairs={{0,8},{4,12},{8,0},{12,4},{1,9},{5,13},{9,1},{13,5},{2,10},{6,14},... | collective-permute-start | bytes 196616 | tf_op jit(solution)/shard_map/ppermute | solution.py:28
  59.2 6.2 %collective-permute-start.19 = (bf16[16,2048]{1,0:T(8,128)(2,1)S(1)}, bf16[16,2048]{1,0:T(8,128)(2,1)S(1)}, u32[]{:S(2)}, u32[]{:S(2)}) collective-permute-start(bf16[16,2048]{1,0:T(8,128)(2,1)S(1)} %get-tuple-element.41), channel_id=1, source_target_pairs={{0,12},{4,8},{8,4},{12,0},{1,13},{5,9},{9,5},{13,1},{2,14},{6,10},... | collective-permute-start | bytes 196616 | tf_op jit(solution)/shard_map/ppermute | solution.py:28

commit v12 on v11

--- a/solution.py
+++ b/solution.py
@@ -22,6 +22,13 @@
 def strides(count):
     assert count & (count - 1) == 0
     return [1 << bit for bit in reversed(range(count.bit_length() - 1))]
+
+
+def sum_order(held):
+    offsets = [0]
+    for stride in held:
+        offsets = offsets + [offset ^ stride for offset in offsets]
+    return offsets
 
 
 def swap(value, axis, stride):
@@ -137,7 +144,6 @@
 def late_kernel(
     offset,
     fresh_block,
-    sent_count,
     queries,
     keys,
     values,
@@ -146,10 +152,11 @@
     total,
     summed,
     weight,
+    context_out,
+    keep_out,
     *rest,
 ):
-    context_out, own_out = rest[-sent_count - 3 : -sent_count - 1]
-    sent_outs, blocks = rest[-sent_count - 1 : -1], rest[-1]
+    send_out, blocks = rest[:-1], rest[-1]
     page = page_at(offset)
     part = page_partial(
         stack_heads(queries[...]),
@@ -172,11 +179,17 @@
     context_out[...] = context
     blocks[...] = jnp.dot(context, weight[...], preferred_element_type=jnp.float32)
     place = lax.axis_index("exp")
-    size = own_out.shape[0]
-    pick = lambda index: blocks[pl.ds(pl.multiple_of(index * size, size), size), :]
-    own_out[...] = pick(place)
-    for step, out in enumerate(sent_outs, 1):
-        out[...] = pick(place ^ step).astype(jnp.bfloat16)
+    offsets = sum_order(strides(lax.axis_size("exp")))
+    size = blocks.shape[0] // len(offsets)
+    half = keep_out.shape[0] // size
+    for number, offset in enumerate(offsets):
+        index = place ^ offset
+        value = blocks[pl.ds(pl.multiple_of(index * size, size), size), :]
+        if number < half:
+            keep_out[number * size : (number + 1) * size, :] = value
+        else:
+            low = (number - half) * size
+            send_out[0][low : low + size, :] = value.astype(jnp.bfloat16)
 
 
 def attention(queries, pages, lengths, out_weight, token_block):
@@ -228,16 +241,18 @@
                 flops=len(group) * page_flops, bytes_accessed=2 << 20, transcendentals=0
             ),
         )(queries, page_lengths, *operands, *state)
-    block = jax.ShapeDtypeStruct((token_block, model_width), jnp.bfloat16)
+    half = (max(1, exp_count // 2) * token_block, model_width)
+    shapes = [
+        jax.ShapeDtypeStruct(queries.shape, jnp.bfloat16),
+        jax.ShapeDtypeStruct(half, jnp.float32),
+    ]
+    if exp_count > 1:
+        shapes.append(jax.ShapeDtypeStruct(half, jnp.bfloat16))
     outs = pl.pallas_call(
-        functools.partial(late_kernel, last[0], fresh_block, exp_count - 1),
-        out_shape=(
-            jax.ShapeDtypeStruct(queries.shape, jnp.bfloat16),
-            jax.ShapeDtypeStruct(block.shape, jnp.float32),
-        )
-        + (block,) * (exp_count - 1),
+        functools.partial(late_kernel, last[0], fresh_block),
+        out_shape=shapes,
         in_specs=whole_specs(8),
-        out_specs=tuple(whole_specs(1 + exp_count)),
+        out_specs=whole_specs(len(shapes)),
         scratch_shapes=[pltpu.VMEM((fresh_block, model_width), jnp.float32)],
         compiler_params=LIMIT,
         cost_estimate=pl.CostEstimate(
@@ -246,7 +261,7 @@
             transcendentals=0,
         ),
     )(queries, last[1], last[2], page_lengths, *state, out_weight)
-    return outs[0], outs[1], outs[2:], state[0]
+    return outs[0], outs[1], outs[2:]
 
 
 def finish_kernel(count, *refs):
@@ -407,9 +422,9 @@
     token_count = requests * token_block
 
     gate_ups = near_parts(expert_input)
-    contexts, owns, sents = [], [], []
+    contexts, keeps, sends = [], [], []
     for r in range(requests):
-        context, own, sent, arrived = attention(
+        context, keep, send = attention(
             queries[r],
             pages[r],
             cached_lengths[r],
@@ -417,17 +432,24 @@
             token_block,
         )
         contexts.append(context)
-        owns.append(own)
-        sents.append(sent)
+        keeps.append(keep)
+        sends.extend(send)
     context = jnp.stack(contexts)
-    downs = near_parts(lax.optimization_barrier((expert_output, owns[-1]))[0])
+
+    by_block = lambda values: [value.reshape(-1, token_block, model_width) for value in values]
+    parts = [jnp.stack(by_block(keeps), axis=1)]
+    send = jnp.stack(by_block(sends), axis=1) if sends else None
+    for stride in reversed(strides(exp_count)):
+        arrived = swap(send, "exp", stride)
+        if parts[0].shape[0] > 1:
+            total = parts[0] + arrived.astype(jnp.float32)
+            half = total.shape[0] // 2
+            parts, send = [total[:half]], total[half:].astype(jnp.bfloat16)
+        else:
+            parts = [parts[0], arrived]
+    downs = near_parts(lax.optimization_barrier((expert_output, parts[0]))[0])
     weights = [(offset, first, down) for (offset, first), (_, down) in zip(gate_ups, downs)]
-    swapped = [part for _, *pair in weights[1:] for part in pair]
-
-    parts = [jnp.concatenate(owns, axis=0)]
-    for step in range(1, exp_count):
-        blocks = jnp.concatenate([sent[step - 1] for sent in sents], axis=0)
-        parts.append(swap(blocks, "exp", step))
+    parts = [part.reshape(-1, model_width) for part in parts]
     residual, ids, scores = residual_in, expert_ids, route_scores
     if rep_count > 1:
         share_size = token_block // rep_count
@@ -441,7 +463,7 @@
         )
     own_hidden, normed = finish(
         parts,
-        swapped,
+        [first for _, first in gate_ups[1:]],
         residual.reshape(-1, model_width),
         norm_gain,
         ids.reshape(-1, ids.shape[2]).T,

time: 66.3 us -> 65.8 us (level)
  waiting for transfers between devices: 23.2 us -> 22 us
    ppermute x15 -> x14, waiting for transfers between devices: 18.6 us -> 17.5 us  [swap(): lax.ppermute(value, axis, [(i, i ^ stride) for i in range(lax.axis_size(a...]
    ppermute x15 -> x14, starting transfers between devices: 13.3 us -> 13.8 us  [swap(): lax.ppermute(value, axis, [(i, i ^ stride) for i in range(lax.axis_size(a...]
  transfers between devices with their start and end apart: 21 -> 20, of which waited for: 14 -> 13; matrix products, arithmetic and copies ran while one was open for 6% -> 6% of each run, Pallas kernels for 10% -> 10%
where the time goes in v12:
time: 65.8 us; the launch traced here: 65.6 us
  starting transfers between devices  27.9 us (42%)
  waiting for transfers between devices  22 us (33%)
  Pallas kernels  6.57 us (10%)
  local copies, waits for them, and re-layouts  4.91 us (7%)
  matrix products  2.59 us (4%)
  between operations  0.87 us (1%)
  other arithmetic  0.78 us (1%)
    ppermute x14, waiting for transfers between devices, swap(): lax.ppermute(value, axis, [(i, i ^ stride) for i in range(lax.axis_size(a...  17.5 us
    ppermute x6, starting transfers between devices, shift(): lax.ppermute(value, axis, [(i, (i + step) % count) for i in range(count)])  14 us
    ppermute x14, starting transfers between devices, swap(): lax.ppermute(value, axis, [(i, i ^ stride) for i in range(lax.axis_size(a...  13.8 us
    unnamed x27, local copies, waits for them, and re-layouts  4.83 us
    ppermute x6, waiting for transfers between devices, shift(): lax.ppermute(value, axis, [(i, (i + step) % count) for i in range(count)])  4.58 us
    dot_general x4, matrix products, expert_apply(): jnp.einsum('nd,dgh->gnh', rows[:, :width], gate_up[0], preferred_element_...  2.59 us
    pallas_call x1, Pallas kernels, attention(): pl.pallas_call(functools.partial(late_kernel, last[0], fresh_block), out_...  2.15 us
    pallas_call x2, Pallas kernels, expert_apply(): pl.pallas_call(functools.partial(down_kernel, [offset for offset, _, _ in...  1.44 us
  transfers between devices with their start and end apart: 20, of which 13 were waited for; matrix products, arithmetic and copies ran while one was open for 6% of the time, Pallas kernels for 10%

profile of v12, /device:TPU:0, one launch (start us, length us, event | category | flops | bytes accessed | tf_op | source)
XLA Modules:
  0.0 65.6 jit_solution(3840080544735367016)
XLA Ops:
  0.6 0.5 collective-permute-start.8
  1.1 1.0 %copy.34 = bf16[1,576,2,128]{3,1,2,0:T(8,128)(2,1)S(1)} copy(bf16[1,576,2,128]{3,2,1,0:T(2,128)(2,1)} %param.11) | data formatting | bytes 589824 | tf_op args[1]
  2.2 4.7 %collective-permute-start.2 = (bf16[576,128]{1,0:T(8,128)(2,1)S(1)}, bf16[576,128]{1,0:T(8,128)(2,1)S(1)}, u32[]{:S(2)}, u32[]{:S(2)}) collective-permute-start(bf16[576,128]{1,0:T(8,128)(2,1)S(1)} %get-tuple-element.34.values), channel_id=1, source_target_pairs={{0,12},{4,0},{8,4},{12,8},{1,13},{5,1},{9,5},{13,9},{2,14},{6,2},{... | collective-permute-start | bytes 442376 | tf_op jit(solution)/shard_map/ppermute | solution.py:40
  6.9 3.9 %collective-permute-start.5 = (bf16[576,128]{1,0:T(8,128)(2,1)S(1)}, bf16[576,128]{1,0:T(8,128)(2,1)S(1)}, u32[]{:S(2)}, u32[]{:S(2)}) collective-permute-start(bf16[576,128]{1,0:T(8,128)(2,1)S(1)} %get-tuple-element.35.keys), channel_id=1, source_target_pairs={{0,12},{4,0},{8,4},{12,8},{1,13},{5,1},{9,5},{13,9},{2,14},{6,2},{... | collective-permute-start | bytes 442376 | tf_op jit(solution)/shard_map/ppermute | solution.py:40
  10.7 0.3 collective-permute-done.2.refs_3_
  11.1 4.3 %collective-permute-start.3 = (bf16[576,128]{1,0:T(8,128)(2,1)S(1)}, bf16[576,128]{1,0:T(8,128)(2,1)S(1)}, u32[]{:S(2)}, u32[]{:S(2)}) collective-permute-start(bf16[576,128]{1,0:T(8,128)(2,1)S(1)} %collective-permute-done.2.refs_3_), channel_id=1, source_target_pairs={{0,12},{4,0},{8,4},{12,8},{1,13},{5,1},{9,5},{13,9},{2,14},{6,2},{... | collective-permute-start | bytes 442376 | tf_op jit(solution)/shard_map/ppermute | solution.py:40
  15.3 0.1 collective-permute-done.refs_0_
  15.5 1.2 %collective-permute-start.1 = (bf16[576,128]{1,0:T(8,128)(2,1)S(1)}, bf16[576,128]{1,0:T(8,128)(2,1)S(1)}, u32[]{:S(2)}, u32[]{:S(2)}) collective-permute-start(bf16[576,128]{1,0:T(8,128)(2,1)S(1)} %collective-permute-done.refs_0_), channel_id=1, source_target_pairs={{0,4},{4,8},{8,12},{12,0},{1,5},{5,9},{9,13},{13,1},{2,6},{6,10},{... | collective-permute-start | bytes 442376 | tf_op jit(solution)/shard_map/ppermute | solution.py:40
  16.7 2.2 %copy-done.1 = bf16[1024,2048]{1,0:T(8,128)(2,1)S(1)} copy-done((bf16[1024,2048]{1,0:T(8,128)(2,1)S(1)}, bf16[1024,2048]{1,0:T(8,128)(2,1)}, u32[]{:S(2)}) %copy-start.1) | copy-done | bytes 4194328
  18.9 0.9 %copy-done.3 = bf16[1,64,1024]{2,1,0:T(8,128)(2,1)S(1)} copy-done((bf16[1,64,1024]{2,1,0:T(8,128)(2,1)S(1)}, bf16[1,64,1024]{2,1,0:T(8,128)(2,1)}, u32[]{:S(2)}) %copy-start.3) | copy-done | bytes 131096
  19.8 0.7 copy-done.9
  20.4 1.3 %shard_map.113 = (f32[1,512]{1,0:T(1,128)S(1)}, f32[1,512]{1,0:T(1,128)S(1)}, f32[128,512]{1,0:T(8,128)S(1)}, s32[4,128]{1,0:T(4,128)S(1)}) custom-call(s32[4]{0:T(128)S(1)} %bitcast.55, bf16[64,1024]{1,0:T(8,128)(2,1)S(1)} %bitcast.46, bf16[576,128]{1,0:T(8,128)(2,1)S(1)} %get-tuple-element.35.keys, bf16[576,128]{1,0:T(8,128)(2,1)S(1)} %get-tuple-element.34.values, ...), custom_call_target="tpu_custom_call" | custom-call | flops 2415919104 | bytes 8388608 | tf_op jit(solution)/shard_map/pallas_call | solution.py:219
  21.8 1.4 %shard_map.114 = (f32[1,512]{1,0:T(1,128)S(1)}, f32[1,512]{1,0:T(1,128)S(1)}, f32[128,512]{1,0:T(8,128)S(1)}) custom-call(bf16[64,1024]{1,0:T(8,128)(2,1)S(1)} %bitcast.47, s32[4,128]{1,0:T(4,128)S(1)} %get-tuple-element.18.lengths, bf16[576,128]{1,0:T(8,128)(2,1)S(1)} %collective-permute-done.refs_0_, bf16[576,128]{1,0:T(8,128)(2,1)S(1)} %collective-permute-done.4.refs_1_, ...), custom_call_target="tpu_custom_call" | custom-call | flops 301989888 | bytes 2097152 | tf_op jit(solution)/shard_map/pallas_call | solution.py:234
  23.2 0.0 copy-start.5
  23.2 0.0 copy-start.6
  23.3 0.0 copy-start.7
  23.3 0.0 copy-start.8
  23.3 0.5 collective-permute-done.3.values
  23.7 3.6 %collective-permute-done.1.keys = bf16[576,128]{1,0:T(8,128)(2,1)S(1)} collective-permute-done((bf16[576,128]{1,0:T(8,128)(2,1)S(1)}, bf16[576,128]{1,0:T(8,128)(2,1)S(1)}, u32[]{:S(2)}, u32[]{:S(2)}) %collective-permute-start.1) | collective-permute-done | bytes 147488 | tf_op jit(solution)/shard_map/ppermute | solution.py:40
  27.4 2.2 %shard_map.115 = (bf16[64,1024]{1,0:T(8,128)(2,1)}, f32[32,2048]{1,0:T(8,128)S(1)}, bf16[32,2048]{1,0:T(8,128)(2,1)S(1)}) custom-call(bf16[64,1024]{1,0:T(8,128)(2,1)S(1)} %bitcast.48, bf16[576,128]{1,0:T(8,128)(2,1)S(1)} %collective-permute-done.1.keys, bf16[576,128]{1,0:T(8,128)(2,1)S(1)} %collective-permute-done.3.values, ...), custom_call_target="tpu_custom_call" | custom-call | flops 419430400 | bytes 6291456 | tf_op jit(solution)/shard_map/pallas_call | solution.py:251
  29.5 1.3 %collective-permute-done.6 = bf16[2,1,16,2048]{3,2,1,0:T(8,128)(2,1)S(1)} collective-permute-done((bf16[2,1,16,2048]{3,2,1,0:T(8,128)(2,1)S(1)}, bf16[2,1,16,2048]{3,2,1,0:T(8,128)(2,1)S(1)}, u32[]{:S(2)}, u32[]{:S(2)}) %collective-permute-start.6) | collective-permute-done | bytes 131104 | tf_op jit(solution)/shard_map/ppermute | solution.py:35
  30.9 1.6 %collective-permute-start.7 = (bf16[1,1,16,2048]{3,2,1,0:T(8,128)(2,1)S(1)}, bf16[1,1,16,2048]{3,2,1,0:T(8,128)(2,1)S(1)}, u32[]{:S(2)}, u32[]{:S(2)}) collective-permute-start(bf16[1,1,16,2048]{3,2,1,0:T(8,128)(2,1)S(1)} %slice.79), channel_id=1, source_target_pairs={{0,2},{1,3},{2,0},{3,1},{4,6},{5,7},{6,4},{7,5},{8,10},{9,11},{10,... | collective-permute-start | bytes 196616 | tf_op jit(solution)/shard_map/ppermute | solution.py:35
  32.5 2.7 %collective-permute-done.7 = bf16[1,1,16,2048]{3,2,1,0:T(8,128)(2,1)S(1)} collective-permute-done((bf16[1,1,16,2048]{3,2,1,0:T(8,128)(2,1)S(1)}, bf16[1,1,16,2048]{3,2,1,0:T(8,128)(2,1)S(1)}, u32[]{:S(2)}, u32[]{:S(2)}) %collective-permute-start.7) | collective-permute-done | bytes 65568 | tf_op jit(solution)/shard_map/ppermute | solution.py:35
  35.3 0.2 shard_map.116
  35.5 1.7 %collective-permute-start.11 = (bf16[16,2176]{1,0:T(8,128)(2,1)S(1)}, bf16[16,2176]{1,0:T(8,128)(2,1)S(1)}, u32[]{:S(2)}, u32[]{:S(2)}) collective-permute-start(bf16[16,2176]{1,0:T(8,128)(2,1)S(1)} %get-tuple-element.29), channel_id=1, source_target_pairs={{0,4},{4,0},{8,12},{12,8},{1,5},{5,1},{9,13},{13,9},{2,6},{6,2},{1... | collective-permute-start | bytes 208904 | tf_op jit(solution)/shard_map/ppermute | solution.py:35
  37.2 0.5 collective-permute-start.10
  37.8 1.3 %collective-permute-start.9 = (bf16[16,2176]{1,0:T(8,128)(2,1)S(1)}, bf16[16,2176]{1,0:T(8,128)(2,1)S(1)}, u32[]{:S(2)}, u32[]{:S(2)}) collective-permute-start(bf16[16,2176]{1,0:T(8,128)(2,1)S(1)} %get-tuple-element.29), channel_id=1, source_target_pairs={{0,8},{4,12},{8,0},{12,4},{1,9},{5,13},{9,1},{13,5},{2,10},{6,14},... | collective-permute-start | bytes 208904 | tf_op jit(solution)/shard_map/ppermute | solution.py:35
  39.1 0.8 %collective-permute-done.11 = bf16[16,2176]{1,0:T(8,128)(2,1)S(1)} collective-permute-done((bf16[16,2176]{1,0:T(8,128)(2,1)S(1)}, bf16[16,2176]{1,0:T(8,128)(2,1)S(1)}, u32[]{:S(2)}, u32[]{:S(2)}) %collective-permute-start.11) | collective-permute-done | bytes 69664 | tf_op jit(solution)/shard_map/ppermute | solution.py:35
  39.9 1.6 %collective-permute-start.14 = (bf16[32,2176]{1,0:T(8,128)(2,1)S(1)}, bf16[32,2176]{1,0:T(8,128)(2,1)S(1)}, u32[]{:S(2)}, u32[]{:S(2)}) collective-permute-start(bf16[32,2176]{1,0:T(8,128)(2,1)S(1)} %pad_maximum_fusion.1), channel_id=1, source_target_pairs={{0,2},{1,3},{2,0},{3,1},{4,6},{5,7},{6,4},{7,5},{8,10},{9,11},{10,... | collective-permute-start | bytes 417800 | tf_op jit(solution)/shard_map/ppermute | solution.py:35
  41.5 2.6 %collective-permute-done.10 = bf16[16,2176]{1,0:T(8,128)(2,1)S(1)} collective-permute-done((bf16[16,2176]{1,0:T(8,128)(2,1)S(1)}, bf16[16,2176]{1,0:T(8,128)(2,1)S(1)}, u32[]{:S(2)}, u32[]{:S(2)}) %collective-permute-start.10) | collective-permute-done | bytes 69664 | tf_op jit(solution)/shard_map/ppermute | solution.py:35
  44.1 2.0 %collective-permute-done.9 = bf16[16,2176]{1,0:T(8,128)(2,1)S(1)} collective-permute-done((bf16[16,2176]{1,0:T(8,128)(2,1)S(1)}, bf16[16,2176]{1,0:T(8,128)(2,1)S(1)}, u32[]{:S(2)}, u32[]{:S(2)}) %collective-permute-start.9) | collective-permute-done | bytes 69664 | tf_op jit(solution)/shard_map/ppermute | solution.py:35
  46.2 1.6 %collective-permute-start.12 = (bf16[32,2176]{1,0:T(8,128)(2,1)S(1)}, bf16[32,2176]{1,0:T(8,128)(2,1)S(1)}, u32[]{:S(2)}, u32[]{:S(2)}) collective-permute-start(bf16[32,2176]{1,0:T(8,128)(2,1)S(1)} %pad_maximum_fusion), channel_id=1, source_target_pairs={{0,2},{1,3},{2,0},{3,1},{4,6},{5,7},{6,4},{7,5},{8,10},{9,11},{10,... | collective-permute-start | bytes 417800 | tf_op jit(solution)/shard_map/ppermute | solution.py:35
  47.8 0.6 fusion.17.refs_1_
  48.4 0.7 %fusion.14.refs_0_ = f32[2,32,384]{2,1,0:T(8,128)S(1)} fusion(bf16[2048,2,384]{2,1,0:T(2,128)(2,1)S(1)} %bitcast.57, bf16[32,2176]{1,0:T(8,128)(2,1)S(1)} %collective-permute-done.14.rows), kind=kOutput, calls=%fused_computation.10 | convolution fusion | flops 100663296 | bytes 3375104 | tf_op jit(solution)/shard_map/nd,dgh->gnh/dot_general | solution.py:336
  49.1 0.7 %shard_map.118 = bf16[32,2048]{1,0:T(8,128)(2,1)S(1)} custom-call(bf16[32,2176]{1,0:T(8,128)(2,1)S(1)} %collective-permute-done.14.rows, f32[2,32,384]{2,1,0:T(8,128)S(1)} %fusion.14.refs_0_, f32[2,32,384]{2,1,0:T(8,128)S(1)} %fusion.17.refs_1_, bf16[1,384,2048]{2,1,0:T(8,128)(2,1)S(1)} %copy-done, bf16[1,384,2048]{2,1,0:T(8,128)(2,1)S(1)} %collective-permute-done.13.refs_3_), custom_call_target="tpu_custom_call" | custom-call | flops 100663296 | bytes 2097152 | tf_op jit(solution)/shard_map/pallas_call | solution.py:340
  49.8 0.6 collective-permute-start.15
  50.4 1.0 %collective-permute-done.12 = bf16[32,2176]{1,0:T(8,128)(2,1)S(1)} collective-permute-done((bf16[32,2176]{1,0:T(8,128)(2,1)S(1)}, bf16[32,2176]{1,0:T(8,128)(2,1)S(1)}, u32[]{:S(2)}, u32[]{:S(2)}) %collective-permute-start.12) | collective-permute-done | bytes 139296 | tf_op jit(solution)/shard_map/ppermute | solution.py:35
  51.4 0.6 fusion.11.refs_1_
  52.0 0.7 fusion.8.refs_0_
  52.7 0.8 %shard_map.117 = (f32[32,2048]{1,0:T(8,128)S(1)}, f32[32,2048]{1,0:T(8,128)S(1)}, bf16[32,2048]{1,0:T(8,128)(2,1)S(1)}) custom-call(bf16[96,2176]{1,0:T(8,128)(2,1)S(1)} %constant_dynamic-update-slice_fusion.rows, f32[2,96,384]{2,1,0:T(8,128)S(1)} %fusion.8.refs_0_, f32[2,96,384]{2,1,0:T(8,128)S(1)} %fusion.11.refs_1_, bf16[1,384,2048]{2,1,0:T(8,128)(2,1)S(1)} %copy-done, ...), custom_call_target="tpu_custom_call" | custom-call | flops 301989888 | bytes 2097152 | tf_op jit(solution)/shard_map/pallas_call | solution.py:340
  53.5 2.2 %collective-permute-start.16 = (bf16[32,2048]{1,0:T(8,128)(2,1)S(1)}, bf16[32,2048]{1,0:T(8,128)(2,1)S(1)}, u32[]{:S(2)}, u32[]{:S(2)}) collective-permute-start(bf16[32,2048]{1,0:T(8,128)(2,1)S(1)} %get-tuple-element.33), channel_id=1, source_target_pairs={{0,2},{1,3},{2,0},{3,1},{4,6},{5,7},{6,4},{7,5},{8,10},{9,11},{10,... | collective-permute-start | bytes 393224 | tf_op jit(solution)/shard_map/ppermute | solution.py:35
  55.7 0.1 collective-permute-start.19
  55.8 2.8 %collective-permute-done.16 = bf16[32,2048]{1,0:T(8,128)(2,1)S(1)} collective-permute-done((bf16[32,2048]{1,0:T(8,128)(2,1)S(1)}, bf16[32,2048]{1,0:T(8,128)(2,1)S(1)}, u32[]{:S(2)}, u32[]{:S(2)}) %collective-permute-start.16) | collective-permute-done | bytes 131104 | tf_op jit(solution)/shard_map/ppermute | solution.py:35
  58.7 0.1 collective-permute-start.17
  58.8 2.1 %collective-permute-start.18 = (bf16[16,2048]{1,0:T(8,128)(2,1)S(1)}, bf16[16,2048]{1,0:T(8,128)(2,1)S(1)}, u32[]{:S(2)}, u32[]{:S(2)}) collective-permute-start(bf16[16,2048]{1,0:T(8,128)(2,1)S(1)} %get-tuple-element.37), channel_id=1, source_target_pairs={{0,12},{4,8},{8,4},{12,0},{1,13},{5,9},{9,5},{13,1},{2,14},{6,10},... | collective-permute-start | bytes 196616 | tf_op jit(solution)/shard_map/ppermute | solution.py:35
  60.9 3.0 %collective-permute-done.17 = bf16[16,2048]{1,0:T(8,128)(2,1)S(1)} collective-permute-done((bf16[16,2048]{1,0:T(8,128)(2,1)S(1)}, bf16[16,2048]{1,0:T(8,128)(2,1)S(1)}, u32[]{:S(2)}, u32[]{:S(2)}) %collective-permute-start.17) | collective-permute-done | bytes 65568 | tf_op jit(solution)/shard_map/ppermute | solution.py:35
  63.9 1.0 %collective-permute-done.18 = bf16[16,2048]{1,0:T(8,128)(2,1)S(1)} collective-permute-done((bf16[16,2048]{1,0:T(8,128)(2,1)S(1)}, bf16[16,2048]{1,0:T(8,128)(2,1)S(1)}, u32[]{:S(2)}, u32[]{:S(2)}) %collective-permute-start.18) | collective-permute-done | bytes 65568 | tf_op jit(solution)/shard_map/ppermute | solution.py:35
  64.9 0.7 %fusion.24 = bf16[1,16,2048]{2,1,0:T(8,128)(2,1)} fusion(bf16[16,2048]{1,0:T(8,128)(2,1)S(1)} %collective-permute-done.19, bf16[16,2048]{1,0:T(8,128)(2,1)S(1)} %collective-permute-done.18, bf16[16,2048]{1,0:T(8,128)(2,1)S(1)} %collective-permute-done.17, f32[32,2048]{1,0:T(8,128)S(1)} %convert_add_fusion, bf16[16,2048]{1,0:T(8,128)(2,1)S(1)} %get-tuple-element.28), kind=kLoop, calls=%fused_computation.29 | loop fusion | flops 294912 | bytes 458752 | tf_op jit(solution)/shard_map/convert_element_type | solution.py:485
  (41 shorter events, 0.3 us)
Async XLA Ops:
  0.6 34.6 %collective-permute-start.8 = (bf16[1,2048,2,384]{3,2,1,0:T(2,128)(2,1)}, bf16[1,2048,2,384]{3,2,1,0:T(2,128)(2,1)S(1)}, u32[]{:S(2)}, u32[]{:S(2)}) collective-permute-start(bf16[1,2048,2,384]{3,2,1,0:T(2,128)(2,1)} %param.18), channel_id=1, source_target_pairs={{0,1},{1,0},{2,3},{3,2},{4,5},{5,4},{6,7},{7,6},{8,9},{9,8},{10,11... | collective-permute-start | bytes 9437192 | tf_op jit(solution)/shard_map/ppermute | solution.py:35
  2.2 8.9 %collective-permute-start.2 = (bf16[576,128]{1,0:T(8,128)(2,1)S(1)}, bf16[576,128]{1,0:T(8,128)(2,1)S(1)}, u32[]{:S(2)}, u32[]{:S(2)}) collective-permute-start(bf16[576,128]{1,0:T(8,128)(2,1)S(1)} %get-tuple-element.34.values), channel_id=1, source_target_pairs={{0,12},{4,0},{8,4},{12,8},{1,13},{5,1},{9,5},{13,9},{2,14},{6,2},{... | collective-permute-start | bytes 442376 | tf_op jit(solution)/shard_map/ppermute | solution.py:40
  6.8 8.6 %collective-permute-start = (bf16[576,128]{1,0:T(8,128)(2,1)S(1)}, bf16[576,128]{1,0:T(8,128)(2,1)S(1)}, u32[]{:S(2)}, u32[]{:S(2)}) collective-permute-start(bf16[576,128]{1,0:T(8,128)(2,1)S(1)} %get-tuple-element.35.keys), channel_id=1, source_target_pairs={{0,4},{4,8},{8,12},{12,0},{1,5},{5,9},{9,13},{13,1},{2,6},{6,10},{... | collective-permute-start | bytes 442376 | tf_op jit(solution)/shard_map/ppermute | solution.py:40
  6.8 14.9 %collective-permute-start.4 = (bf16[576,128]{1,0:T(8,128)(2,1)S(1)}, bf16[576,128]{1,0:T(8,128)(2,1)S(1)}, u32[]{:S(2)}, u32[]{:S(2)}) collective-permute-start(bf16[576,128]{1,0:T(8,128)(2,1)S(1)} %get-tuple-element.34.values), channel_id=1, source_target_pairs={{0,4},{4,8},{8,12},{12,0},{1,5},{5,9},{9,13},{13,1},{2,6},{6,10},{... | collective-permute-start | bytes 442376 | tf_op jit(solution)/shard_map/ppermute | solution.py:40
  6.9 14.9 %collective-permute-start.5 = (bf16[576,128]{1,0:T(8,128)(2,1)S(1)}, bf16[576,128]{1,0:T(8,128)(2,1)S(1)}, u32[]{:S(2)}, u32[]{:S(2)}) collective-permute-start(bf16[576,128]{1,0:T(8,128)(2,1)S(1)} %get-tuple-element.35.keys), channel_id=1, source_target_pairs={{0,12},{4,0},{8,4},{12,8},{1,13},{5,1},{9,5},{13,9},{2,14},{6,2},{... | collective-permute-start | bytes 442376 | tf_op jit(solution)/shard_map/ppermute | solution.py:40
  11.1 12.7 %collective-permute-start.3 = (bf16[576,128]{1,0:T(8,128)(2,1)S(1)}, bf16[576,128]{1,0:T(8,128)(2,1)S(1)}, u32[]{:S(2)}, u32[]{:S(2)}) collective-permute-start(bf16[576,128]{1,0:T(8,128)(2,1)S(1)} %collective-permute-done.2.refs_3_), channel_id=1, source_target_pairs={{0,12},{4,0},{8,4},{12,8},{1,13},{5,1},{9,5},{13,9},{2,14},{6,2},{... | collective-permute-start | bytes 442376 | tf_op jit(solution)/shard_map/ppermute | solution.py:40
  15.5 11.9 %collective-permute-start.1 = (bf16[576,128]{1,0:T(8,128)(2,1)S(1)}, bf16[576,128]{1,0:T(8,128)(2,1)S(1)}, u32[]{:S(2)}, u32[]{:S(2)}) collective-permute-start(bf16[576,128]{1,0:T(8,128)(2,1)S(1)} %collective-permute-done.refs_0_), channel_id=1, source_target_pairs={{0,4},{4,8},{8,12},{12,0},{1,5},{5,9},{9,13},{13,1},{2,6},{6,10},{... | collective-permute-start | bytes 442376 | tf_op jit(solution)/shard_map/ppermute | solution.py:40
  16.7 2.2 %copy-start.1 = (bf16[1024,2048]{1,0:T(8,128)(2,1)S(1)}, bf16[1024,2048]{1,0:T(8,128)(2,1)}, u32[]{:S(2)}) copy-start(bf16[1024,2048]{1,0:T(8,128)(2,1)} %weight.1) | copy-start | bytes 12582916
  18.9 0.9 %copy-start.3 = (bf16[1,64,1024]{2,1,0:T(8,128)(2,1)S(1)}, bf16[1,64,1024]{2,1,0:T(8,128)(2,1)}, u32[]{:S(2)}) copy-start(bf16[1,64,1024]{2,1,0:T(8,128)(2,1)} %param.10) | copy-start | bytes 393220
  19.8 0.7 copy-start.9
  20.4 1.3 %copy-start.4 = (bf16[1,64,1024]{2,1,0:T(8,128)(2,1)S(1)}, bf16[1,64,1024]{2,1,0:T(8,128)(2,1)}, u32[]{:S(2)}) copy-start(bf16[1,64,1024]{2,1,0:T(8,128)(2,1)} %param.10) | copy-start | bytes 393220
  20.4 6.9 %copy-start.2 = (bf16[1024,2048]{1,0:T(8,128)(2,1)S(1)}, bf16[1024,2048]{1,0:T(8,128)(2,1)}, u32[]{:S(2)}) copy-start(bf16[1024,2048]{1,0:T(8,128)(2,1)} %weight.1) | copy-start | bytes 12582916
  23.2 12.0 %copy-start.5 = (bf16[1,16,2048]{2,1,0:T(8,128)(2,1)S(1)}, bf16[1,16,2048]{2,1,0:T(8,128)(2,1)}, u32[]{:S(2)}) copy-start(bf16[1,16,2048]{2,1,0:T(8,128)(2,1)} %param.13) | copy-start | bytes 196612
  23.2 12.0 %copy-start.6 = (f32[2048]{0:T(1024)S(1)}, f32[2048]{0:T(1024)}, u32[]{:S(2)}) copy-start(f32[2048]{0:T(1024)} %param.15) | copy-start | bytes 24580
  23.3 12.0 %copy-start.7 = (s32[1,16,8]{1,2,0:T(8,128)S(1)}, s32[1,16,8]{1,2,0:T(8,128)}, u32[]{:S(2)}) copy-start(s32[1,16,8]{1,2,0:T(8,128)} %param.16) | copy-start | bytes 1540
  23.3 12.0 %copy-start.8 = (f32[1,16,8]{1,2,0:T(8,128)S(1)}, f32[1,16,8]{1,2,0:T(8,128)}, u32[]{:S(2)}) copy-start(f32[1,16,8]{1,2,0:T(8,128)} %param.17) | copy-start | bytes 1540
  29.5 7.7 %copy-start = (bf16[1,384,2048]{2,1,0:T(8,128)(2,1)S(1)}, bf16[1,384,2048]{2,1,0:T(8,128)(2,1)}, u32[]{:S(2)}) copy-start(bf16[1,384,2048]{2,1,0:T(8,128)(2,1)} %refs_2_.1) | copy-start | bytes 4718596
  29.5 1.3 %collective-permute-start.6 = (bf16[2,1,16,2048]{3,2,1,0:T(8,128)(2,1)S(1)}, bf16[2,1,16,2048]{3,2,1,0:T(8,128)(2,1)S(1)}, u32[]{:S(2)}, u32[]{:S(2)}) collective-permute-start(bf16[2,1,16,2048]{3,2,1,0:T(8,128)(2,1)S(1)} %bitcast.54), channel_id=1, source_target_pairs={{0,1},{1,0},{2,3},{3,2},{4,5},{5,4},{6,7},{7,6},{8,9},{9,8},{10,11... | collective-permute-start | bytes 393224 | tf_op jit(solution)/shard_map/ppermute | solution.py:35
  30.9 4.3 %collective-permute-start.7 = (bf16[1,1,16,2048]{3,2,1,0:T(8,128)(2,1)S(1)}, bf16[1,1,16,2048]{3,2,1,0:T(8,128)(2,1)S(1)}, u32[]{:S(2)}, u32[]{:S(2)}) collective-permute-start(bf16[1,1,16,2048]{3,2,1,0:T(8,128)(2,1)S(1)} %slice.79), channel_id=1, source_target_pairs={{0,2},{1,3},{2,0},{3,1},{4,6},{5,7},{6,4},{7,5},{8,10},{9,11},{10,... | collective-permute-start | bytes 196616 | tf_op jit(solution)/shard_map/ppermute | solution.py:35
  35.5 12.9 %copy-start.10 = (bf16[1,2048,2,384]{3,2,1,0:T(2,128)(2,1)S(1)}, bf16[1,2048,2,384]{3,2,1,0:T(2,128)(2,1)}, u32[]{:S(2)}) copy-start(bf16[1,2048,2,384]{3,2,1,0:T(2,128)(2,1)} %param.18) | copy-start | bytes 9437188
  35.5 4.4 %collective-permute-start.11 = (bf16[16,2176]{1,0:T(8,128)(2,1)S(1)}, bf16[16,2176]{1,0:T(8,128)(2,1)S(1)}, u32[]{:S(2)}, u32[]{:S(2)}) collective-permute-start(bf16[16,2176]{1,0:T(8,128)(2,1)S(1)} %get-tuple-element.29), channel_id=1, source_target_pairs={{0,4},{4,0},{8,12},{12,8},{1,5},{5,1},{9,13},{13,9},{2,6},{6,2},{1... | collective-permute-start | bytes 208904 | tf_op jit(solution)/shard_map/ppermute | solution.py:35
  37.2 11.9 %collective-permute-start.13 = (bf16[1,384,2048]{2,1,0:T(8,128)(2,1)S(1)}, bf16[1,384,2048]{2,1,0:T(8,128)(2,1)S(1)}, u32[]{:S(2)}, u32[]{:S(2)}) collective-permute-start(bf16[1,384,2048]{2,1,0:T(8,128)(2,1)S(1)} %copy-done), channel_id=1, source_target_pairs={{0,1},{1,0},{2,3},{3,2},{4,5},{5,4},{6,7},{7,6},{8,9},{9,8},{10,11... | collective-permute-start | bytes 4718600 | tf_op jit(solution)/shard_map/ppermute | solution.py:35
  37.2 6.9 %collective-permute-start.10 = (bf16[16,2176]{1,0:T(8,128)(2,1)S(1)}, bf16[16,2176]{1,0:T(8,128)(2,1)S(1)}, u32[]{:S(2)}, u32[]{:S(2)}) collective-permute-start(bf16[16,2176]{1,0:T(8,128)(2,1)S(1)} %get-tuple-element.29), channel_id=1, source_target_pairs={{0,12},{4,8},{8,4},{12,0},{1,13},{5,9},{9,5},{13,1},{2,14},{6,10},... | collective-permute-start | bytes 208904 | tf_op jit(solution)/shard_map/ppermute | solution.py:35
  37.8 8.4 %collective-permute-start.9 = (bf16[16,2176]{1,0:T(8,128)(2,1)S(1)}, bf16[16,2176]{1,0:T(8,128)(2,1)S(1)}, u32[]{:S(2)}, u32[]{:S(2)}) collective-permute-start(bf16[16,2176]{1,0:T(8,128)(2,1)S(1)} %get-tuple-element.29), channel_id=1, source_target_pairs={{0,8},{4,12},{8,0},{12,4},{1,9},{5,13},{9,1},{13,5},{2,10},{6,14},... | collective-permute-start | bytes 208904 | tf_op jit(solution)/shard_map/ppermute | solution.py:35
  39.9 7.8 %collective-permute-start.14 = (bf16[32,2176]{1,0:T(8,128)(2,1)S(1)}, bf16[32,2176]{1,0:T(8,128)(2,1)S(1)}, u32[]{:S(2)}, u32[]{:S(2)}) collective-permute-start(bf16[32,2176]{1,0:T(8,128)(2,1)S(1)} %pad_maximum_fusion.1), channel_id=1, source_target_pairs={{0,2},{1,3},{2,0},{3,1},{4,6},{5,7},{6,4},{7,5},{8,10},{9,11},{10,... | collective-permute-start | bytes 417800 | tf_op jit(solution)/shard_map/ppermute | solution.py:35
  46.2 5.2 %collective-permute-start.12 = (bf16[32,2176]{1,0:T(8,128)(2,1)S(1)}, bf16[32,2176]{1,0:T(8,128)(2,1)S(1)}, u32[]{:S(2)}, u32[]{:S(2)}) collective-permute-start(bf16[32,2176]{1,0:T(8,128)(2,1)S(1)} %pad_maximum_fusion), channel_id=1, source_target_pairs={{0,2},{1,3},{2,0},{3,1},{4,6},{5,7},{6,4},{7,5},{8,10},{9,11},{10,... | collective-permute-start | bytes 417800 | tf_op jit(solution)/shard_map/ppermute | solution.py:35
  49.8 5.9 %collective-permute-start.15 = (bf16[32,2048]{1,0:T(8,128)(2,1)S(1)}, bf16[32,2048]{1,0:T(8,128)(2,1)S(1)}, u32[]{:S(2)}, u32[]{:S(2)}) collective-permute-start(bf16[32,2048]{1,0:T(8,128)(2,1)S(1)} %shard_map.118), channel_id=1, source_target_pairs={{0,2},{1,3},{2,0},{3,1},{4,6},{5,7},{6,4},{7,5},{8,10},{9,11},{10,... | collective-permute-start | bytes 393224 | tf_op jit(solution)/shard_map/ppermute | solution.py:35
  53.5 5.2 %collective-permute-start.16 = (bf16[32,2048]{1,0:T(8,128)(2,1)S(1)}, bf16[32,2048]{1,0:T(8,128)(2,1)S(1)}, u32[]{:S(2)}, u32[]{:S(2)}) collective-permute-start(bf16[32,2048]{1,0:T(8,128)(2,1)S(1)} %get-tuple-element.33), channel_id=1, source_target_pairs={{0,2},{1,3},{2,0},{3,1},{4,6},{5,7},{6,4},{7,5},{8,10},{9,11},{10,... | collective-permute-start | bytes 393224 | tf_op jit(solution)/shard_map/ppermute | solution.py:35
  55.7 5.1 %collective-permute-start.19 = (bf16[16,2048]{1,0:T(8,128)(2,1)S(1)}, bf16[16,2048]{1,0:T(8,128)(2,1)S(1)}, u32[]{:S(2)}, u32[]{:S(2)}) collective-permute-start(bf16[16,2048]{1,0:T(8,128)(2,1)S(1)} %slice.78), channel_id=1, source_target_pairs={{0,4},{4,0},{8,12},{12,8},{1,5},{5,1},{9,13},{13,9},{2,6},{6,2},{1... | collective-permute-start | bytes 196616 | tf_op jit(solution)/shard_map/ppermute | solution.py:35
  58.7 5.2 %collective-permute-start.17 = (bf16[16,2048]{1,0:T(8,128)(2,1)S(1)}, bf16[16,2048]{1,0:T(8,128)(2,1)S(1)}, u32[]{:S(2)}, u32[]{:S(2)}) collective-permute-start(bf16[16,2048]{1,0:T(8,128)(2,1)S(1)} %get-tuple-element.36), channel_id=1, source_target_pairs={{0,8},{4,12},{8,0},{12,4},{1,9},{5,13},{9,1},{13,5},{2,10},{6,14},... | collective-permute-start | bytes 196616 | tf_op jit(solution)/shard_map/ppermute | solution.py:35
  58.8 6.2 %collective-permute-start.18 = (bf16[16,2048]{1,0:T(8,128)(2,1)S(1)}, bf16[16,2048]{1,0:T(8,128)(2,1)S(1)}, u32[]{:S(2)}, u32[]{:S(2)}) collective-permute-start(bf16[16,2048]{1,0:T(8,128)(2,1)S(1)} %get-tuple-element.37), channel_id=1, source_target_pairs={{0,12},{4,8},{8,4},{12,0},{1,13},{5,9},{9,5},{13,1},{2,14},{6,10},... | collective-permute-start | bytes 196616 | tf_op jit(solution)/shard_map/ppermute | solution.py:35

commit v13 on v12

--- a/solution.py
+++ b/solution.py
@@ -371,12 +371,11 @@
     far = strides(lax.axis_size("exp"))[:1]
     chunks = chunks_of(lax.axis_size("ctx"))
 
-    joined = [
-        jnp.concatenate(
-            [rows if offset == 0 else swap(rows, "ctx", offset) for offset in chunk], axis=0
-        )
-        for chunk in chunks
-    ]
+    joined, source = [], rows
+    for chunk in chunks:
+        blocks = [rows if offset == 0 else swap(source, "ctx", offset) for offset in chunk]
+        joined.append(jnp.concatenate(blocks, axis=0))
+        source, _ = lax.optimization_barrier((rows, blocks[-1]))
     crossed = []
     for piece in joined if far else []:
         crossed.append(swap(piece, "exp", far[0]))
@@ -388,7 +387,8 @@
         if far:
             other = first
             if number:
-                (other,) = expert_apply(crossed[number : number + 1], [jnp.bfloat16], weights)
+                piece = crossed[number]
+                (other,) = expert_apply([piece], [jnp.bfloat16], weights)
             value = value + swap(other, "exp", far[0]).astype(jnp.float32)
         for position, offset in enumerate(chunk):
             block = value[position * tokens : (position + 1) * tokens]

time: 65.8 us -> 66.3 us (level)
  starting transfers between devices: 27.9 us -> 30.3 us
  waiting for transfers between devices: 22 us -> 20.2 us
    ppermute x14, starting transfers between devices: 13.8 us -> 16.2 us  [swap(): lax.ppermute(value, axis, [(i, i ^ stride) for i in range(lax.axis_size(a...]
    ppermute x14, waiting for transfers between devices: 17.5 us -> 15.6 us  [swap(): lax.ppermute(value, axis, [(i, i ^ stride) for i in range(lax.axis_size(a...]
  transfers between devices with their start and end apart: 20 -> 20, of which waited for: 13 -> 15; matrix products, arithmetic and copies ran while one was open for 6% -> 6% of each run, Pallas kernels for 10% -> 10%
where the time goes in v13:
time: 66.3 us; the launch traced here: 66.1 us
  starting transfers between devices  30.3 us (46%)
  waiting for transfers between devices  20.2 us (30%)
  Pallas kernels  6.55 us (10%)
  local copies, waits for them, and re-layouts  4.91 us (7%)
  matrix products  2.58 us (4%)
  between operations  0.85 us (1%)
  other arithmetic  0.79 us (1%)
    ppermute x14, starting transfers between devices, swap(): lax.ppermute(value, axis, [(i, i ^ stride) for i in range(lax.axis_size(a...  16.2 us
    ppermute x14, waiting for transfers between devices, swap(): lax.ppermute(value, axis, [(i, i ^ stride) for i in range(lax.axis_size(a...  15.6 us
    ppermute x6, starting transfers between devices, shift(): lax.ppermute(value, axis, [(i, (i + step) % count) for i in range(count)])  14 us
    unnamed x27, local copies, waits for them, and re-layouts  4.83 us
    ppermute x6, waiting for transfers between devices, shift(): lax.ppermute(value, axis, [(i, (i + step) % count) for i in range(count)])  4.58 us
    dot_general x4, matrix products, expert_apply(): jnp.einsum('nd,dgh->gnh', rows[:, :width], gate_up[0], preferred_element_...  2.58 us
    pallas_call x1, Pallas kernels, attention(): pl.pallas_call(functools.partial(late_kernel, last[0], fresh_block), out_...  2.15 us
    pallas_call x1, Pallas kernels, attention(): pl.pallas_call(functools.partial(middle_kernel, [offset for offset, _, _...  1.43 us
  transfers between devices with their start and end apart: 20, of which 15 were waited for; matrix products, arithmetic and copies ran while one was open for 6% of the time, Pallas kernels for 10%

profile of v13, /device:TPU:0, one launch (start us, length us, event | category | flops | bytes accessed | tf_op | source)
XLA Modules:
  0.0 66.1 jit_solution(1789234515565271342)
XLA Ops:
  0.6 0.5 collective-permute-start.8
  1.1 1.0 %copy.34 = bf16[1,576,2,128]{3,1,2,0:T(8,128)(2,1)S(1)} copy(bf16[1,576,2,128]{3,2,1,0:T(2,128)(2,1)} %param.11) | data formatting | bytes 589824 | tf_op args[1]
  2.2 4.7 %collective-permute-start.2 = (bf16[576,128]{1,0:T(8,128)(2,1)S(1)}, bf16[576,128]{1,0:T(8,128)(2,1)S(1)}, u32[]{:S(2)}, u32[]{:S(2)}) collective-permute-start(bf16[576,128]{1,0:T(8,128)(2,1)S(1)} %get-tuple-element.36.values), channel_id=1, source_target_pairs={{0,12},{4,0},{8,4},{12,8},{1,13},{5,1},{9,5},{13,9},{2,14},{6,2},{... | collective-permute-start | bytes 442376 | tf_op jit(solution)/shard_map/ppermute | solution.py:40
  6.9 3.9 %collective-permute-start.5 = (bf16[576,128]{1,0:T(8,128)(2,1)S(1)}, bf16[576,128]{1,0:T(8,128)(2,1)S(1)}, u32[]{:S(2)}, u32[]{:S(2)}) collective-permute-start(bf16[576,128]{1,0:T(8,128)(2,1)S(1)} %get-tuple-element.37.keys), channel_id=1, source_target_pairs={{0,12},{4,0},{8,4},{12,8},{1,13},{5,1},{9,5},{13,9},{2,14},{6,2},{... | collective-permute-start | bytes 442376 | tf_op jit(solution)/shard_map/ppermute | solution.py:40
  10.7 0.3 collective-permute-done.2.refs_3_
  11.1 4.3 %collective-permute-start.3 = (bf16[576,128]{1,0:T(8,128)(2,1)S(1)}, bf16[576,128]{1,0:T(8,128)(2,1)S(1)}, u32[]{:S(2)}, u32[]{:S(2)}) collective-permute-start(bf16[576,128]{1,0:T(8,128)(2,1)S(1)} %collective-permute-done.2.refs_3_), channel_id=1, source_target_pairs={{0,12},{4,0},{8,4},{12,8},{1,13},{5,1},{9,5},{13,9},{2,14},{6,2},{... | collective-permute-start | bytes 442376 | tf_op jit(solution)/shard_map/ppermute | solution.py:40
  15.3 0.1 collective-permute-done.refs_0_
  15.5 1.2 %collective-permute-start.1 = (bf16[576,128]{1,0:T(8,128)(2,1)S(1)}, bf16[576,128]{1,0:T(8,128)(2,1)S(1)}, u32[]{:S(2)}, u32[]{:S(2)}) collective-permute-start(bf16[576,128]{1,0:T(8,128)(2,1)S(1)} %collective-permute-done.refs_0_), channel_id=1, source_target_pairs={{0,4},{4,8},{8,12},{12,0},{1,5},{5,9},{9,13},{13,1},{2,6},{6,10},{... | collective-permute-start | bytes 442376 | tf_op jit(solution)/shard_map/ppermute | solution.py:40
  16.7 2.2 %copy-done.1 = bf16[1024,2048]{1,0:T(8,128)(2,1)S(1)} copy-done((bf16[1024,2048]{1,0:T(8,128)(2,1)S(1)}, bf16[1024,2048]{1,0:T(8,128)(2,1)}, u32[]{:S(2)}) %copy-start.1) | copy-done | bytes 4194328
  18.9 0.9 %copy-done.3 = bf16[1,64,1024]{2,1,0:T(8,128)(2,1)S(1)} copy-done((bf16[1,64,1024]{2,1,0:T(8,128)(2,1)S(1)}, bf16[1,64,1024]{2,1,0:T(8,128)(2,1)}, u32[]{:S(2)}) %copy-start.3) | copy-done | bytes 131096
  19.8 0.7 copy-done.9
  20.4 1.3 %shard_map.113 = (f32[1,512]{1,0:T(1,128)S(1)}, f32[1,512]{1,0:T(1,128)S(1)}, f32[128,512]{1,0:T(8,128)S(1)}, s32[4,128]{1,0:T(4,128)S(1)}) custom-call(s32[4]{0:T(128)S(1)} %bitcast.55, bf16[64,1024]{1,0:T(8,128)(2,1)S(1)} %bitcast.46, bf16[576,128]{1,0:T(8,128)(2,1)S(1)} %get-tuple-element.37.keys, bf16[576,128]{1,0:T(8,128)(2,1)S(1)} %get-tuple-element.36.values, ...), custom_call_target="tpu_custom_call" | custom-call | flops 2415919104 | bytes 8388608 | tf_op jit(solution)/shard_map/pallas_call | solution.py:219
  21.8 1.4 %shard_map.114 = (f32[1,512]{1,0:T(1,128)S(1)}, f32[1,512]{1,0:T(1,128)S(1)}, f32[128,512]{1,0:T(8,128)S(1)}) custom-call(bf16[64,1024]{1,0:T(8,128)(2,1)S(1)} %bitcast.47, s32[4,128]{1,0:T(4,128)S(1)} %get-tuple-element.19.lengths, bf16[576,128]{1,0:T(8,128)(2,1)S(1)} %collective-permute-done.refs_0_, bf16[576,128]{1,0:T(8,128)(2,1)S(1)} %collective-permute-done.4.refs_1_, ...), custom_call_target="tpu_custom_call" | custom-call | flops 301989888 | bytes 2097152 | tf_op jit(solution)/shard_map/pallas_call | solution.py:234
  23.2 0.0 copy-start.6
  23.3 0.0 copy-start.7
  23.3 0.5 collective-permute-done.3.values
  23.7 3.6 %collective-permute-done.1.keys = bf16[576,128]{1,0:T(8,128)(2,1)S(1)} collective-permute-done((bf16[576,128]{1,0:T(8,128)(2,1)S(1)}, bf16[576,128]{1,0:T(8,128)(2,1)S(1)}, u32[]{:S(2)}, u32[]{:S(2)}) %collective-permute-start.1) | collective-permute-done | bytes 147488 | tf_op jit(solution)/shard_map/ppermute | solution.py:40
  27.4 2.2 %shard_map.115 = (bf16[64,1024]{1,0:T(8,128)(2,1)}, f32[32,2048]{1,0:T(8,128)S(1)}, bf16[32,2048]{1,0:T(8,128)(2,1)S(1)}) custom-call(bf16[64,1024]{1,0:T(8,128)(2,1)S(1)} %bitcast.48, bf16[576,128]{1,0:T(8,128)(2,1)S(1)} %collective-permute-done.1.keys, bf16[576,128]{1,0:T(8,128)(2,1)S(1)} %collective-permute-done.3.values, ...), custom_call_target="tpu_custom_call" | custom-call | flops 419430400 | bytes 6291456 | tf_op jit(solution)/shard_map/pallas_call | solution.py:251
  29.5 1.3 %collective-permute-done.6 = bf16[2,1,16,2048]{3,2,1,0:T(8,128)(2,1)S(1)} collective-permute-done((bf16[2,1,16,2048]{3,2,1,0:T(8,128)(2,1)S(1)}, bf16[2,1,16,2048]{3,2,1,0:T(8,128)(2,1)S(1)}, u32[]{:S(2)}, u32[]{:S(2)}) %collective-permute-start.6) | collective-permute-done | bytes 131104 | tf_op jit(solution)/shard_map/ppermute | solution.py:35
  30.9 1.6 %collective-permute-start.7 = (bf16[1,1,16,2048]{3,2,1,0:T(8,128)(2,1)S(1)}, bf16[1,1,16,2048]{3,2,1,0:T(8,128)(2,1)S(1)}, u32[]{:S(2)}, u32[]{:S(2)}) collective-permute-start(bf16[1,1,16,2048]{3,2,1,0:T(8,128)(2,1)S(1)} %slice.79), channel_id=1, source_target_pairs={{0,2},{1,3},{2,0},{3,1},{4,6},{5,7},{6,4},{7,5},{8,10},{9,11},{10,... | collective-permute-start | bytes 196616 | tf_op jit(solution)/shard_map/ppermute | solution.py:35
  32.5 2.7 %collective-permute-done.7 = bf16[1,1,16,2048]{3,2,1,0:T(8,128)(2,1)S(1)} collective-permute-done((bf16[1,1,16,2048]{3,2,1,0:T(8,128)(2,1)S(1)}, bf16[1,1,16,2048]{3,2,1,0:T(8,128)(2,1)S(1)}, u32[]{:S(2)}, u32[]{:S(2)}) %collective-permute-start.7) | collective-permute-done | bytes 65568 | tf_op jit(solution)/shard_map/ppermute | solution.py:35
  35.3 0.2 shard_map.116
  35.5 1.8 %collective-permute-start.10 = (bf16[16,2176]{1,0:T(8,128)(2,1)S(1)}, bf16[16,2176]{1,0:T(8,128)(2,1)S(1)}, u32[]{:S(2)}, u32[]{:S(2)}) collective-permute-start(bf16[16,2176]{1,0:T(8,128)(2,1)S(1)} %get-tuple-element.31), channel_id=1, source_target_pairs={{0,12},{4,8},{8,4},{12,0},{1,13},{5,9},{9,5},{13,1},{2,14},{6,10},... | collective-permute-start | bytes 208904 | tf_op jit(solution)/shard_map/ppermute | solution.py:35
  37.3 1.4 %collective-permute-start.9 = (bf16[16,2176]{1,0:T(8,128)(2,1)S(1)}, bf16[16,2176]{1,0:T(8,128)(2,1)S(1)}, u32[]{:S(2)}, u32[]{:S(2)}) collective-permute-start(bf16[16,2176]{1,0:T(8,128)(2,1)S(1)} %get-tuple-element.31), channel_id=1, source_target_pairs={{0,8},{4,12},{8,0},{12,4},{1,9},{5,13},{9,1},{13,5},{2,10},{6,14},... | collective-permute-start | bytes 208904 | tf_op jit(solution)/shard_map/ppermute | solution.py:35
  38.7 3.0 %collective-permute-done.10 = bf16[16,2176]{1,0:T(8,128)(2,1)S(1)} collective-permute-done((bf16[16,2176]{1,0:T(8,128)(2,1)S(1)}, bf16[16,2176]{1,0:T(8,128)(2,1)S(1)}, u32[]{:S(2)}, u32[]{:S(2)}) %collective-permute-start.10) | collective-permute-done | bytes 69664 | tf_op jit(solution)/shard_map/ppermute | solution.py:35
  41.7 2.3 %collective-permute-start.11 = (bf16[16,2176]{1,0:T(8,128)(2,1)S(1)}, bf16[16,2176]{1,0:T(8,128)(2,1)S(1)}, u32[]{:S(2)}, u32[]{:S(2)}) collective-permute-start(bf16[16,2176]{1,0:T(8,128)(2,1)S(1)} %get-tuple-element.31), channel_id=1, source_target_pairs={{0,4},{4,0},{8,12},{12,8},{1,5},{5,1},{9,13},{13,9},{2,6},{6,2},{1... | collective-permute-start | bytes 208904 | tf_op jit(solution)/shard_map/ppermute | solution.py:35
  44.1 0.2 collective-permute-done.9
  44.2 1.6 %collective-permute-start.12 = (bf16[32,2176]{1,0:T(8,128)(2,1)S(1)}, bf16[32,2176]{1,0:T(8,128)(2,1)S(1)}, u32[]{:S(2)}, u32[]{:S(2)}) collective-permute-start(bf16[32,2176]{1,0:T(8,128)(2,1)S(1)} %pad_maximum_fusion), channel_id=1, source_target_pairs={{0,2},{1,3},{2,0},{3,1},{4,6},{5,7},{6,4},{7,5},{8,10},{9,11},{10,... | collective-permute-start | bytes 417800 | tf_op jit(solution)/shard_map/ppermute | solution.py:35
  45.8 0.5 collective-permute-done.11
  46.4 1.6 %collective-permute-start.14 = (bf16[32,2176]{1,0:T(8,128)(2,1)S(1)}, bf16[32,2176]{1,0:T(8,128)(2,1)S(1)}, u32[]{:S(2)}, u32[]{:S(2)}) collective-permute-start(bf16[32,2176]{1,0:T(8,128)(2,1)S(1)} %pad_maximum_fusion.1), channel_id=1, source_target_pairs={{0,2},{1,3},{2,0},{3,1},{4,6},{5,7},{6,4},{7,5},{8,10},{9,11},{10,... | collective-permute-start | bytes 417800 | tf_op jit(solution)/shard_map/ppermute | solution.py:35
  47.9 2.5 %collective-permute-done.12 = bf16[32,2176]{1,0:T(8,128)(2,1)S(1)} collective-permute-done((bf16[32,2176]{1,0:T(8,128)(2,1)S(1)}, bf16[32,2176]{1,0:T(8,128)(2,1)S(1)}, u32[]{:S(2)}, u32[]{:S(2)}) %collective-permute-start.12) | collective-permute-done | bytes 139296 | tf_op jit(solution)/shard_map/ppermute | solution.py:35
  50.4 0.6 fusion.11.refs_1_
  51.1 0.7 fusion.8.refs_0_
  51.7 0.7 %shard_map.117 = (f32[32,2048]{1,0:T(8,128)S(1)}, f32[32,2048]{1,0:T(8,128)S(1)}, bf16[32,2048]{1,0:T(8,128)(2,1)S(1)}) custom-call(bf16[96,2176]{1,0:T(8,128)(2,1)S(1)} %constant_dynamic-update-slice_fusion.rows, f32[2,96,384]{2,1,0:T(8,128)S(1)} %fusion.8.refs_0_, f32[2,96,384]{2,1,0:T(8,128)S(1)} %fusion.11.refs_1_, bf16[1,384,2048]{2,1,0:T(8,128)(2,1)S(1)} %copy-done, ...), custom_call_target="tpu_custom_call" | custom-call | flops 301989888 | bytes 2097152 | tf_op jit(solution)/shard_map/pallas_call | solution.py:340
  52.5 1.6 %collective-permute-start.16 = (bf16[32,2048]{1,0:T(8,128)(2,1)S(1)}, bf16[32,2048]{1,0:T(8,128)(2,1)S(1)}, u32[]{:S(2)}, u32[]{:S(2)}) collective-permute-start(bf16[32,2048]{1,0:T(8,128)(2,1)S(1)} %get-tuple-element.35), channel_id=1, source_target_pairs={{0,2},{1,3},{2,0},{3,1},{4,6},{5,7},{6,4},{7,5},{8,10},{9,11},{10,... | collective-permute-start | bytes 393224 | tf_op jit(solution)/shard_map/ppermute | solution.py:35
  54.0 0.6 fusion.17.refs_1_
  54.7 0.6 fusion.14.refs_0_
  55.3 0.7 %shard_map.118 = bf16[32,2048]{1,0:T(8,128)(2,1)S(1)} custom-call(bf16[32,2176]{1,0:T(8,128)(2,1)S(1)} %collective-permute-done.14.rows, f32[2,32,384]{2,1,0:T(8,128)S(1)} %fusion.14.refs_0_, f32[2,32,384]{2,1,0:T(8,128)S(1)} %fusion.17.refs_1_, bf16[1,384,2048]{2,1,0:T(8,128)(2,1)S(1)} %copy-done, bf16[1,384,2048]{2,1,0:T(8,128)(2,1)S(1)} %collective-permute-done.13.refs_3_), custom_call_target="tpu_custom_call" | custom-call | flops 100663296 | bytes 2097152 | tf_op jit(solution)/shard_map/pallas_call | solution.py:340
  56.0 0.6 collective-permute-start.15
  56.6 1.4 %collective-permute-done.16 = bf16[32,2048]{1,0:T(8,128)(2,1)S(1)} collective-permute-done((bf16[32,2048]{1,0:T(8,128)(2,1)S(1)}, bf16[32,2048]{1,0:T(8,128)(2,1)S(1)}, u32[]{:S(2)}, u32[]{:S(2)}) %collective-permute-start.16) | collective-permute-done | bytes 131104 | tf_op jit(solution)/shard_map/ppermute | solution.py:35
  58.1 0.5 collective-permute-start.17
  58.5 2.3 %collective-permute-start.18 = (bf16[16,2048]{1,0:T(8,128)(2,1)S(1)}, bf16[16,2048]{1,0:T(8,128)(2,1)S(1)}, u32[]{:S(2)}, u32[]{:S(2)}) collective-permute-start(bf16[16,2048]{1,0:T(8,128)(2,1)S(1)} %get-tuple-element.39), channel_id=1, source_target_pairs={{0,12},{4,8},{8,4},{12,0},{1,13},{5,9},{9,5},{13,1},{2,14},{6,10},... | collective-permute-start | bytes 196616 | tf_op jit(solution)/shard_map/ppermute | solution.py:35
  60.8 0.2 collective-permute-done.15
  61.1 0.7 %collective-permute-start.19 = (bf16[16,2048]{1,0:T(8,128)(2,1)S(1)}, bf16[16,2048]{1,0:T(8,128)(2,1)S(1)}, u32[]{:S(2)}, u32[]{:S(2)}) collective-permute-start(bf16[16,2048]{1,0:T(8,128)(2,1)S(1)} %slice.78), channel_id=1, source_target_pairs={{0,4},{4,0},{8,12},{12,8},{1,5},{5,1},{9,13},{13,9},{2,6},{6,2},{1... | collective-permute-start | bytes 196616 | tf_op jit(solution)/shard_map/ppermute | solution.py:35
  61.8 1.9 %collective-permute-done.17 = bf16[16,2048]{1,0:T(8,128)(2,1)S(1)} collective-permute-done((bf16[16,2048]{1,0:T(8,128)(2,1)S(1)}, bf16[16,2048]{1,0:T(8,128)(2,1)S(1)}, u32[]{:S(2)}, u32[]{:S(2)}) %collective-permute-start.17) | collective-permute-done | bytes 65568 | tf_op jit(solution)/shard_map/ppermute | solution.py:35
  63.7 0.9 %collective-permute-done.18 = bf16[16,2048]{1,0:T(8,128)(2,1)S(1)} collective-permute-done((bf16[16,2048]{1,0:T(8,128)(2,1)S(1)}, bf16[16,2048]{1,0:T(8,128)(2,1)S(1)}, u32[]{:S(2)}, u32[]{:S(2)}) %collective-permute-start.18) | collective-permute-done | bytes 65568 | tf_op jit(solution)/shard_map/ppermute | solution.py:35
  64.6 0.8 %collective-permute-done.19 = bf16[16,2048]{1,0:T(8,128)(2,1)S(1)} collective-permute-done((bf16[16,2048]{1,0:T(8,128)(2,1)S(1)}, bf16[16,2048]{1,0:T(8,128)(2,1)S(1)}, u32[]{:S(2)}, u32[]{:S(2)}) %collective-permute-start.19) | collective-permute-done | bytes 65568 | tf_op jit(solution)/shard_map/ppermute | solution.py:35
  65.4 0.7 %fusion.24 = bf16[1,16,2048]{2,1,0:T(8,128)(2,1)} fusion(bf16[16,2048]{1,0:T(8,128)(2,1)S(1)} %collective-permute-done.19, bf16[16,2048]{1,0:T(8,128)(2,1)S(1)} %collective-permute-done.18, bf16[16,2048]{1,0:T(8,128)(2,1)S(1)} %collective-permute-done.17, f32[32,2048]{1,0:T(8,128)S(1)} %convert_add_fusion, bf16[16,2048]{1,0:T(8,128)(2,1)S(1)} %get-tuple-element.29), kind=kLoop, calls=%fused_computation.29 | loop fusion | flops 294912 | bytes 458752 | tf_op jit(solution)/shard_map/convert_element_type | solution.py:485
  (41 shorter events, 0.3 us)
Async XLA Ops:
  0.6 34.6 %collective-permute-start.8 = (bf16[1,2048,2,384]{3,2,1,0:T(2,128)(2,1)}, bf16[1,2048,2,384]{3,2,1,0:T(2,128)(2,1)S(1)}, u32[]{:S(2)}, u32[]{:S(2)}) collective-permute-start(bf16[1,2048,2,384]{3,2,1,0:T(2,128)(2,1)} %param.18), channel_id=1, source_target_pairs={{0,1},{1,0},{2,3},{3,2},{4,5},{5,4},{6,7},{7,6},{8,9},{9,8},{10,11... | collective-permute-start | bytes 9437192 | tf_op jit(solution)/shard_map/ppermute | solution.py:35
  2.2 8.9 %collective-permute-start.2 = (bf16[576,128]{1,0:T(8,128)(2,1)S(1)}, bf16[576,128]{1,0:T(8,128)(2,1)S(1)}, u32[]{:S(2)}, u32[]{:S(2)}) collective-permute-start(bf16[576,128]{1,0:T(8,128)(2,1)S(1)} %get-tuple-element.36.values), channel_id=1, source_target_pairs={{0,12},{4,0},{8,4},{12,8},{1,13},{5,1},{9,5},{13,9},{2,14},{6,2},{... | collective-permute-start | bytes 442376 | tf_op jit(solution)/shard_map/ppermute | solution.py:40
  6.8 8.6 %collective-permute-start = (bf16[576,128]{1,0:T(8,128)(2,1)S(1)}, bf16[576,128]{1,0:T(8,128)(2,1)S(1)}, u32[]{:S(2)}, u32[]{:S(2)}) collective-permute-start(bf16[576,128]{1,0:T(8,128)(2,1)S(1)} %get-tuple-element.37.keys), channel_id=1, source_target_pairs={{0,4},{4,8},{8,12},{12,0},{1,5},{5,9},{9,13},{13,1},{2,6},{6,10},{... | collective-permute-start | bytes 442376 | tf_op jit(solution)/shard_map/ppermute | solution.py:40
  6.8 14.9 %collective-permute-start.4 = (bf16[576,128]{1,0:T(8,128)(2,1)S(1)}, bf16[576,128]{1,0:T(8,128)(2,1)S(1)}, u32[]{:S(2)}, u32[]{:S(2)}) collective-permute-start(bf16[576,128]{1,0:T(8,128)(2,1)S(1)} %get-tuple-element.36.values), channel_id=1, source_target_pairs={{0,4},{4,8},{8,12},{12,0},{1,5},{5,9},{9,13},{13,1},{2,6},{6,10},{... | collective-permute-start | bytes 442376 | tf_op jit(solution)/shard_map/ppermute | solution.py:40
  6.9 14.9 %collective-permute-start.5 = (bf16[576,128]{1,0:T(8,128)(2,1)S(1)}, bf16[576,128]{1,0:T(8,128)(2,1)S(1)}, u32[]{:S(2)}, u32[]{:S(2)}) collective-permute-start(bf16[576,128]{1,0:T(8,128)(2,1)S(1)} %get-tuple-element.37.keys), channel_id=1, source_target_pairs={{0,12},{4,0},{8,4},{12,8},{1,13},{5,1},{9,5},{13,9},{2,14},{6,2},{... | collective-permute-start | bytes 442376 | tf_op jit(solution)/shard_map/ppermute | solution.py:40
  11.1 12.7 %collective-permute-start.3 = (bf16[576,128]{1,0:T(8,128)(2,1)S(1)}, bf16[576,128]{1,0:T(8,128)(2,1)S(1)}, u32[]{:S(2)}, u32[]{:S(2)}) collective-permute-start(bf16[576,128]{1,0:T(8,128)(2,1)S(1)} %collective-permute-done.2.refs_3_), channel_id=1, source_target_pairs={{0,12},{4,0},{8,4},{12,8},{1,13},{5,1},{9,5},{13,9},{2,14},{6,2},{... | collective-permute-start | bytes 442376 | tf_op jit(solution)/shard_map/ppermute | solution.py:40
  15.5 11.9 %collective-permute-start.1 = (bf16[576,128]{1,0:T(8,128)(2,1)S(1)}, bf16[576,128]{1,0:T(8,128)(2,1)S(1)}, u32[]{:S(2)}, u32[]{:S(2)}) collective-permute-start(bf16[576,128]{1,0:T(8,128)(2,1)S(1)} %collective-permute-done.refs_0_), channel_id=1, source_target_pairs={{0,4},{4,8},{8,12},{12,0},{1,5},{5,9},{9,13},{13,1},{2,6},{6,10},{... | collective-permute-start | bytes 442376 | tf_op jit(solution)/shard_map/ppermute | solution.py:40
  16.7 2.2 %copy-start.1 = (bf16[1024,2048]{1,0:T(8,128)(2,1)S(1)}, bf16[1024,2048]{1,0:T(8,128)(2,1)}, u32[]{:S(2)}) copy-start(bf16[1024,2048]{1,0:T(8,128)(2,1)} %weight.1) | copy-start | bytes 12582916
  18.9 0.9 %copy-start.3 = (bf16[1,64,1024]{2,1,0:T(8,128)(2,1)S(1)}, bf16[1,64,1024]{2,1,0:T(8,128)(2,1)}, u32[]{:S(2)}) copy-start(bf16[1,64,1024]{2,1,0:T(8,128)(2,1)} %param.10) | copy-start | bytes 393220
  19.8 0.7 copy-start.9
  20.4 1.3 %copy-start.4 = (bf16[1,64,1024]{2,1,0:T(8,128)(2,1)S(1)}, bf16[1,64,1024]{2,1,0:T(8,128)(2,1)}, u32[]{:S(2)}) copy-start(bf16[1,64,1024]{2,1,0:T(8,128)(2,1)} %param.10) | copy-start | bytes 393220
  20.4 6.9 %copy-start.2 = (bf16[1024,2048]{1,0:T(8,128)(2,1)S(1)}, bf16[1024,2048]{1,0:T(8,128)(2,1)}, u32[]{:S(2)}) copy-start(bf16[1024,2048]{1,0:T(8,128)(2,1)} %weight.1) | copy-start | bytes 12582916
  23.2 12.0 %copy-start.5 = (bf16[1,16,2048]{2,1,0:T(8,128)(2,1)S(1)}, bf16[1,16,2048]{2,1,0:T(8,128)(2,1)}, u32[]{:S(2)}) copy-start(bf16[1,16,2048]{2,1,0:T(8,128)(2,1)} %param.13) | copy-start | bytes 196612
  23.2 12.0 %copy-start.6 = (f32[2048]{0:T(1024)S(1)}, f32[2048]{0:T(1024)}, u32[]{:S(2)}) copy-start(f32[2048]{0:T(1024)} %param.15) | copy-start | bytes 24580
  23.3 12.0 %copy-start.7 = (s32[1,16,8]{1,2,0:T(8,128)S(1)}, s32[1,16,8]{1,2,0:T(8,128)}, u32[]{:S(2)}) copy-start(s32[1,16,8]{1,2,0:T(8,128)} %param.16) | copy-start | bytes 1540
  23.3 12.0 %copy-start.8 = (f32[1,16,8]{1,2,0:T(8,128)S(1)}, f32[1,16,8]{1,2,0:T(8,128)}, u32[]{:S(2)}) copy-start(f32[1,16,8]{1,2,0:T(8,128)} %param.17) | copy-start | bytes 1540
  29.5 9.2 %copy-start = (bf16[1,384,2048]{2,1,0:T(8,128)(2,1)S(1)}, bf16[1,384,2048]{2,1,0:T(8,128)(2,1)}, u32[]{:S(2)}) copy-start(bf16[1,384,2048]{2,1,0:T(8,128)(2,1)} %refs_2_.1) | copy-start | bytes 4718596
  29.5 1.3 %collective-permute-start.6 = (bf16[2,1,16,2048]{3,2,1,0:T(8,128)(2,1)S(1)}, bf16[2,1,16,2048]{3,2,1,0:T(8,128)(2,1)S(1)}, u32[]{:S(2)}, u32[]{:S(2)}) collective-permute-start(bf16[2,1,16,2048]{3,2,1,0:T(8,128)(2,1)S(1)} %bitcast.54), channel_id=1, source_target_pairs={{0,1},{1,0},{2,3},{3,2},{4,5},{5,4},{6,7},{7,6},{8,9},{9,8},{10,11... | collective-permute-start | bytes 393224 | tf_op jit(solution)/shard_map/ppermute | solution.py:35
  30.9 4.3 %collective-permute-start.7 = (bf16[1,1,16,2048]{3,2,1,0:T(8,128)(2,1)S(1)}, bf16[1,1,16,2048]{3,2,1,0:T(8,128)(2,1)S(1)}, u32[]{:S(2)}, u32[]{:S(2)}) collective-permute-start(bf16[1,1,16,2048]{3,2,1,0:T(8,128)(2,1)S(1)} %slice.79), channel_id=1, source_target_pairs={{0,2},{1,3},{2,0},{3,1},{4,6},{5,7},{6,4},{7,5},{8,10},{9,11},{10,... | collective-permute-start | bytes 196616 | tf_op jit(solution)/shard_map/ppermute | solution.py:35
  35.5 15.5 %copy-start.10 = (bf16[1,2048,2,384]{3,2,1,0:T(2,128)(2,1)S(1)}, bf16[1,2048,2,384]{3,2,1,0:T(2,128)(2,1)}, u32[]{:S(2)}) copy-start(bf16[1,2048,2,384]{3,2,1,0:T(2,128)(2,1)} %param.18) | copy-start | bytes 9437188
  35.5 6.2 %collective-permute-start.10 = (bf16[16,2176]{1,0:T(8,128)(2,1)S(1)}, bf16[16,2176]{1,0:T(8,128)(2,1)S(1)}, u32[]{:S(2)}, u32[]{:S(2)}) collective-permute-start(bf16[16,2176]{1,0:T(8,128)(2,1)S(1)} %get-tuple-element.31), channel_id=1, source_target_pairs={{0,12},{4,8},{8,4},{12,0},{1,13},{5,9},{9,5},{13,1},{2,14},{6,10},... | collective-permute-start | bytes 208904 | tf_op jit(solution)/shard_map/ppermute | solution.py:35
  37.3 6.9 %collective-permute-start.9 = (bf16[16,2176]{1,0:T(8,128)(2,1)S(1)}, bf16[16,2176]{1,0:T(8,128)(2,1)S(1)}, u32[]{:S(2)}, u32[]{:S(2)}) collective-permute-start(bf16[16,2176]{1,0:T(8,128)(2,1)S(1)} %get-tuple-element.31), channel_id=1, source_target_pairs={{0,8},{4,12},{8,0},{12,4},{1,9},{5,13},{9,1},{13,5},{2,10},{6,14},... | collective-permute-start | bytes 208904 | tf_op jit(solution)/shard_map/ppermute | solution.py:35
  38.7 13.0 %collective-permute-start.13 = (bf16[1,384,2048]{2,1,0:T(8,128)(2,1)S(1)}, bf16[1,384,2048]{2,1,0:T(8,128)(2,1)S(1)}, u32[]{:S(2)}, u32[]{:S(2)}) collective-permute-start(bf16[1,384,2048]{2,1,0:T(8,128)(2,1)S(1)} %copy-done), channel_id=1, source_target_pairs={{0,1},{1,0},{2,3},{3,2},{4,5},{5,4},{6,7},{7,6},{8,9},{9,8},{10,11... | collective-permute-start | bytes 4718600 | tf_op jit(solution)/shard_map/ppermute | solution.py:35
  41.7 4.6 %collective-permute-start.11 = (bf16[16,2176]{1,0:T(8,128)(2,1)S(1)}, bf16[16,2176]{1,0:T(8,128)(2,1)S(1)}, u32[]{:S(2)}, u32[]{:S(2)}) collective-permute-start(bf16[16,2176]{1,0:T(8,128)(2,1)S(1)} %get-tuple-element.31), channel_id=1, source_target_pairs={{0,4},{4,0},{8,12},{12,8},{1,5},{5,1},{9,13},{13,9},{2,6},{6,2},{1... | collective-permute-start | bytes 208904 | tf_op jit(solution)/shard_map/ppermute | solution.py:35
  44.2 6.1 %collective-permute-start.12 = (bf16[32,2176]{1,0:T(8,128)(2,1)S(1)}, bf16[32,2176]{1,0:T(8,128)(2,1)S(1)}, u32[]{:S(2)}, u32[]{:S(2)}) collective-permute-start(bf16[32,2176]{1,0:T(8,128)(2,1)S(1)} %pad_maximum_fusion), channel_id=1, source_target_pairs={{0,2},{1,3},{2,0},{3,1},{4,6},{5,7},{6,4},{7,5},{8,10},{9,11},{10,... | collective-permute-start | bytes 417800 | tf_op jit(solution)/shard_map/ppermute | solution.py:35
  46.4 7.7 %collective-permute-start.14 = (bf16[32,2176]{1,0:T(8,128)(2,1)S(1)}, bf16[32,2176]{1,0:T(8,128)(2,1)S(1)}, u32[]{:S(2)}, u32[]{:S(2)}) collective-permute-start(bf16[32,2176]{1,0:T(8,128)(2,1)S(1)} %pad_maximum_fusion.1), channel_id=1, source_target_pairs={{0,2},{1,3},{2,0},{3,1},{4,6},{5,7},{6,4},{7,5},{8,10},{9,11},{10,... | collective-permute-start | bytes 417800 | tf_op jit(solution)/shard_map/ppermute | solution.py:35
  52.5 5.6 %collective-permute-start.16 = (bf16[32,2048]{1,0:T(8,128)(2,1)S(1)}, bf16[32,2048]{1,0:T(8,128)(2,1)S(1)}, u32[]{:S(2)}, u32[]{:S(2)}) collective-permute-start(bf16[32,2048]{1,0:T(8,128)(2,1)S(1)} %get-tuple-element.35), channel_id=1, source_target_pairs={{0,2},{1,3},{2,0},{3,1},{4,6},{5,7},{6,4},{7,5},{8,10},{9,11},{10,... | collective-permute-start | bytes 393224 | tf_op jit(solution)/shard_map/ppermute | solution.py:35
  56.0 5.0 %collective-permute-start.15 = (bf16[32,2048]{1,0:T(8,128)(2,1)S(1)}, bf16[32,2048]{1,0:T(8,128)(2,1)S(1)}, u32[]{:S(2)}, u32[]{:S(2)}) collective-permute-start(bf16[32,2048]{1,0:T(8,128)(2,1)S(1)} %shard_map.118), channel_id=1, source_target_pairs={{0,2},{1,3},{2,0},{3,1},{4,6},{5,7},{6,4},{7,5},{8,10},{9,11},{10,... | collective-permute-start | bytes 393224 | tf_op jit(solution)/shard_map/ppermute | solution.py:35
  58.1 5.6 %collective-permute-start.17 = (bf16[16,2048]{1,0:T(8,128)(2,1)S(1)}, bf16[16,2048]{1,0:T(8,128)(2,1)S(1)}, u32[]{:S(2)}, u32[]{:S(2)}) collective-permute-start(bf16[16,2048]{1,0:T(8,128)(2,1)S(1)} %get-tuple-element.38), channel_id=1, source_target_pairs={{0,8},{4,12},{8,0},{12,4},{1,9},{5,13},{9,1},{13,5},{2,10},{6,14},... | collective-permute-start | bytes 196616 | tf_op jit(solution)/shard_map/ppermute | solution.py:35
  58.5 6.1 %collective-permute-start.18 = (bf16[16,2048]{1,0:T(8,128)(2,1)S(1)}, bf16[16,2048]{1,0:T(8,128)(2,1)S(1)}, u32[]{:S(2)}, u32[]{:S(2)}) collective-permute-start(bf16[16,2048]{1,0:T(8,128)(2,1)S(1)} %get-tuple-element.39), channel_id=1, source_target_pairs={{0,12},{4,8},{8,4},{12,0},{1,13},{5,9},{9,5},{13,1},{2,14},{6,10},... | collective-permute-start | bytes 196616 | tf_op jit(solution)/shard_map/ppermute | solution.py:35
  61.1 4.3 %collective-permute-start.19 = (bf16[16,2048]{1,0:T(8,128)(2,1)S(1)}, bf16[16,2048]{1,0:T(8,128)(2,1)S(1)}, u32[]{:S(2)}, u32[]{:S(2)}) collective-permute-start(bf16[16,2048]{1,0:T(8,128)(2,1)S(1)} %slice.78), channel_id=1, source_target_pairs={{0,4},{4,0},{8,12},{12,8},{1,5},{5,1},{9,13},{13,9},{2,6},{6,2},{1... | collective-permute-start | bytes 196616 | tf_op jit(solution)/shard_map/ppermute | solution.py:35

commit v14 on v12

--- a/solution.py
+++ b/solution.py
@@ -55,7 +55,7 @@
     )
 
 
-def page_partial(stacked, keys, values, page, length, place, fresh_block):
+def page_weights(stacked, keys, page, length, place, fresh_block):
     rows, page_size = stacked.shape[0], keys.shape[0]
     slab_size = page_size - fresh_block
     scores = lax.dot_general(
@@ -77,13 +77,18 @@
     peak = jnp.max(masked, axis=0, keepdims=True)
     weights = jnp.exp((masked - peak) * (HEAD**-0.5))
     total = jnp.sum(weights, axis=0, keepdims=True)
-    summed = lax.dot_general(
-        values,
-        weights.astype(jnp.bfloat16),
-        (((0,), (0,)), ((), ())),
-        preferred_element_type=jnp.float32,
-    )
-    return peak, total, summed
+    return peak, total, weights.astype(jnp.bfloat16)
+
+
+def weighted(values, weights):
+    return lax.dot_general(
+        values, weights, (((0,), (0,)), ((), ())), preferred_element_type=jnp.float32
+    )
+
+
+def page_partial(stacked, keys, values, page, length, place, fresh_block):
+    peak, total, weights = page_weights(stacked, keys, page, length, place, fresh_block)
+    return peak, total, weighted(values, weights)
 
 
 def merge(first, second):
@@ -141,13 +146,23 @@
         out[...] = value
 
 
+def weights_kernel(offset, fresh_block, queries, keys, lengths, peak_out, total_out, weights_out):
+    peak_out[...], total_out[...], weights_out[...] = page_weights(
+        stack_heads(queries[...]),
+        keys[...],
+        page_at(offset),
+        lengths[offset : offset + 1, :],
+        lax.axis_index("ctx"),
+        fresh_block,
+    )
+
+
 def late_kernel(
-    offset,
     fresh_block,
-    queries,
-    keys,
     values,
-    lengths,
+    last_peak,
+    last_total,
+    weights,
     peak,
     total,
     summed,
@@ -157,16 +172,7 @@
     *rest,
 ):
     send_out, blocks = rest[:-1], rest[-1]
-    page = page_at(offset)
-    part = page_partial(
-        stack_heads(queries[...]),
-        keys[...],
-        values[...],
-        page,
-        lengths[offset : offset + 1, :],
-        lax.axis_index("ctx"),
-        fresh_block,
-    )
+    part = (last_peak[...], last_total[...], weighted(values[...], weights[...]))
     state = merge((peak[...], total[...], summed[...]), part)
     result = jnp.transpose(state[2] / state[1])
     context = jnp.concatenate(
@@ -203,14 +209,14 @@
     left_keys, left_values = own_keys, own_values
     right_keys, right_values = own_keys, own_values
     for step in range(1, (count - 1) // 2 + 1):
+        right_keys = shift(right_keys, "ctx", -1)
+        left_values = shift(left_values, "ctx", 1)
+        right_values = shift(right_values, "ctx", -1)
         left_keys = shift(left_keys, "ctx", 1)
-        right_values = shift(right_values, "ctx", -1)
-        left_values = shift(left_values, "ctx", 1)
-        right_keys = shift(right_keys, "ctx", -1)
         held.append((count - step, left_keys, left_values))
         held.append((step, right_keys, right_values))
     if count % 2 == 0:
-        last = (count // 2, shift(left_keys, "ctx", 1), shift(right_values, "ctx", -1))
+        last = (count // 2, shift(right_keys, "ctx", -1), shift(left_values, "ctx", 1))
     else:
         last = held.pop()
     page_flops = 4 * rows * pages.shape[0] * HEAD
@@ -248,8 +254,18 @@
     ]
     if exp_count > 1:
         shapes.append(jax.ShapeDtypeStruct(half, jnp.bfloat16))
+    last_weights = pl.pallas_call(
+        functools.partial(weights_kernel, last[0], fresh_block),
+        out_shape=(line, line, jax.ShapeDtypeStruct((pages.shape[0], rows), jnp.bfloat16)),
+        in_specs=whole_specs(3),
+        out_specs=tuple(whole_specs(3)),
+        compiler_params=LIMIT,
+        cost_estimate=pl.CostEstimate(
+            flops=page_flops, bytes_accessed=1 << 20, transcendentals=0
+        ),
+    )(queries, last[1], page_lengths)
     outs = pl.pallas_call(
-        functools.partial(late_kernel, last[0], fresh_block),
+        functools.partial(late_kernel, fresh_block),
         out_shape=shapes,
         in_specs=whole_specs(8),
         out_specs=whole_specs(len(shapes)),
@@ -260,7 +276,7 @@
             bytes_accessed=6 << 20,
             transcendentals=0,
         ),
-    )(queries, last[1], last[2], page_lengths, *state, out_weight)
+    )(last[2], *last_weights, *state, out_weight)
     return outs[0], outs[1], outs[2:]
 
 

time: 65.8 us -> 65.3 us (level)
    pallas_call x1 -> x2, Pallas kernels: 2.15 us -> 2.29 us  [the longest x1 1.68 us: attention(): pl.pallas_call(functools.partial(late_kernel, fresh_block), out_shape=sha...]
where the time goes in v14:
time: 65.3 us; the launch traced here: 65.1 us
  starting transfers between devices  27.8 us (43%)
  waiting for transfers between devices  21.4 us (33%)
  Pallas kernels  6.69 us (10%)
  local copies, waits for them, and re-layouts  4.91 us (8%)
  matrix products  2.61 us (4%)
  between operations  0.87 us (1%)
  other arithmetic  0.78 us (1%)
    ppermute x14, waiting for transfers between devices, swap(): lax.ppermute(value, axis, [(i, i ^ stride) for i in range(lax.axis_size(a...  17.4 us
    ppermute x6, starting transfers between devices, shift(): lax.ppermute(value, axis, [(i, (i + step) % count) for i in range(count)])  14 us
    ppermute x14, starting transfers between devices, swap(): lax.ppermute(value, axis, [(i, i ^ stride) for i in range(lax.axis_size(a...  13.8 us
    unnamed x27, local copies, waits for them, and re-layouts  4.83 us
    ppermute x6, waiting for transfers between devices, shift(): lax.ppermute(value, axis, [(i, (i + step) % count) for i in range(count)])  3.97 us
    dot_general x4, matrix products, expert_apply(): jnp.einsum('nd,dgh->gnh', rows[:, :width], gate_up[0], preferred_element_...  2.61 us
    pallas_call x1, Pallas kernels, attention(): pl.pallas_call(functools.partial(late_kernel, fresh_block), out_shape=sha...  1.68 us
    pallas_call x1, Pallas kernels, attention(): pl.pallas_call(functools.partial(middle_kernel, [offset for offset, _, _...  1.43 us
  transfers between devices with their start and end apart: 20, of which 13 were waited for; matrix products, arithmetic and copies ran while one was open for 6% of the time, Pallas kernels for 10%

profile of v14, /device:TPU:0, one launch (start us, length us, event | category | flops | bytes accessed | tf_op | source)
XLA Modules:
  0.0 65.1 jit_solution(16037141086291825934)
XLA Ops:
  0.6 0.5 collective-permute-start.8
  1.1 1.0 %copy.34 = bf16[1,576,2,128]{3,1,2,0:T(8,128)(2,1)S(1)} copy(bf16[1,576,2,128]{3,2,1,0:T(2,128)(2,1)} %param.11) | data formatting | bytes 589824 | tf_op args[1]
  2.2 4.7 %collective-permute-start.2 = (bf16[576,128]{1,0:T(8,128)(2,1)S(1)}, bf16[576,128]{1,0:T(8,128)(2,1)S(1)}, u32[]{:S(2)}, u32[]{:S(2)}) collective-permute-start(bf16[576,128]{1,0:T(8,128)(2,1)S(1)} %get-tuple-element.40.keys), channel_id=1, source_target_pairs={{0,12},{4,0},{8,4},{12,8},{1,13},{5,1},{9,5},{13,9},{2,14},{6,2},{... | collective-permute-start | bytes 442376 | tf_op jit(solution)/shard_map/ppermute | solution.py:40
  6.9 3.9 %collective-permute-start.5 = (bf16[576,128]{1,0:T(8,128)(2,1)S(1)}, bf16[576,128]{1,0:T(8,128)(2,1)S(1)}, u32[]{:S(2)}, u32[]{:S(2)}) collective-permute-start(bf16[576,128]{1,0:T(8,128)(2,1)S(1)} %get-tuple-element.41.values), channel_id=1, source_target_pairs={{0,12},{4,0},{8,4},{12,8},{1,13},{5,1},{9,5},{13,9},{2,14},{6,2},{... | collective-permute-start | bytes 442376 | tf_op jit(solution)/shard_map/ppermute | solution.py:40
  10.7 0.3 collective-permute-done.2.refs_2_
  11.1 4.3 %collective-permute-start.3 = (bf16[576,128]{1,0:T(8,128)(2,1)S(1)}, bf16[576,128]{1,0:T(8,128)(2,1)S(1)}, u32[]{:S(2)}, u32[]{:S(2)}) collective-permute-start(bf16[576,128]{1,0:T(8,128)(2,1)S(1)} %collective-permute-done.2.refs_2_), channel_id=1, source_target_pairs={{0,12},{4,0},{8,4},{12,8},{1,13},{5,1},{9,5},{13,9},{2,14},{6,2},{... | collective-permute-start | bytes 442376 | tf_op jit(solution)/shard_map/ppermute | solution.py:40
  15.3 0.1 collective-permute-done.refs_1_
  15.5 1.2 %collective-permute-start.1 = (bf16[576,128]{1,0:T(8,128)(2,1)S(1)}, bf16[576,128]{1,0:T(8,128)(2,1)S(1)}, u32[]{:S(2)}, u32[]{:S(2)}) collective-permute-start(bf16[576,128]{1,0:T(8,128)(2,1)S(1)} %collective-permute-done.refs_1_), channel_id=1, source_target_pairs={{0,4},{4,8},{8,12},{12,0},{1,5},{5,9},{9,13},{13,1},{2,6},{6,10},{... | collective-permute-start | bytes 442376 | tf_op jit(solution)/shard_map/ppermute | solution.py:40
  16.7 2.2 %copy-done.1 = bf16[1024,2048]{1,0:T(8,128)(2,1)S(1)} copy-done((bf16[1024,2048]{1,0:T(8,128)(2,1)S(1)}, bf16[1024,2048]{1,0:T(8,128)(2,1)}, u32[]{:S(2)}) %copy-start.1) | copy-done | bytes 4194328
  18.9 0.9 %copy-done.7 = bf16[1,64,1024]{2,1,0:T(8,128)(2,1)S(1)} copy-done((bf16[1,64,1024]{2,1,0:T(8,128)(2,1)S(1)}, bf16[1,64,1024]{2,1,0:T(8,128)(2,1)}, u32[]{:S(2)}) %copy-start.7) | copy-done | bytes 131096
  19.8 0.7 %copy-done.9 = s32[1,4]{1,0:T(1,128)S(1)} copy-done((s32[1,4]{1,0:T(1,128)S(1)}, s32[1,4]{1,0:T(1,128)}, u32[]{:S(2)}) %copy-start.9) | copy-done | bytes 40
  20.4 1.3 %shard_map.113 = (f32[1,512]{1,0:T(1,128)S(1)}, f32[1,512]{1,0:T(1,128)S(1)}, f32[128,512]{1,0:T(8,128)S(1)}, s32[4,128]{1,0:T(4,128)S(1)}) custom-call(s32[4]{0:T(128)S(1)} %bitcast.55, bf16[64,1024]{1,0:T(8,128)(2,1)S(1)} %bitcast.51, bf16[576,128]{1,0:T(8,128)(2,1)S(1)} %get-tuple-element.40.keys, bf16[576,128]{1,0:T(8,128)(2,1)S(1)} %get-tuple-element.41.values, ...), custom_call_target="tpu_custom_call" | custom-call | flops 2415919104 | bytes 8388608 | tf_op jit(solution)/shard_map/pallas_call | solution.py:225
  21.8 1.4 %shard_map.115 = (f32[1,512]{1,0:T(1,128)S(1)}, f32[1,512]{1,0:T(1,128)S(1)}, f32[128,512]{1,0:T(8,128)S(1)}) custom-call(bf16[64,1024]{1,0:T(8,128)(2,1)S(1)} %bitcast.52, s32[4,128]{1,0:T(4,128)S(1)} %get-tuple-element.21.lengths, bf16[576,128]{1,0:T(8,128)(2,1)S(1)} %collective-permute-done.4.refs_0_, bf16[576,128]{1,0:T(8,128)(2,1)S(1)} %collective-permute-done.refs_1_, ...), custom_call_target="tpu_custom_call" | custom-call | flops 301989888 | bytes 2097152 | tf_op jit(solution)/shard_map/pallas_call | solution.py:240
  23.2 0.5 collective-permute-done.3.keys
  23.7 0.6 shard_map.114
  24.4 0.0 copy-start.4
  24.4 0.0 copy-start.5
  24.4 3.0 %collective-permute-done.1.values = bf16[576,128]{1,0:T(8,128)(2,1)S(1)} collective-permute-done((bf16[576,128]{1,0:T(8,128)(2,1)S(1)}, bf16[576,128]{1,0:T(8,128)(2,1)S(1)}, u32[]{:S(2)}, u32[]{:S(2)}) %collective-permute-start.1) | collective-permute-done | bytes 147488 | tf_op jit(solution)/shard_map/ppermute | solution.py:40
  27.4 1.7 %shard_map.116 = (bf16[64,1024]{1,0:T(8,128)(2,1)}, f32[32,2048]{1,0:T(8,128)S(1)}, bf16[32,2048]{1,0:T(8,128)(2,1)S(1)}) custom-call(bf16[576,128]{1,0:T(8,128)(2,1)S(1)} %collective-permute-done.1.values, f32[1,512]{1,0:T(1,128)S(1)} %get-tuple-element.22.last_peak, f32[1,512]{1,0:T(1,128)S(1)} %get-tuple-element.23.last_total, ...), custom_call_target="tpu_custom_call" | custom-call | flops 419430400 | bytes 6291456 | tf_op jit(solution)/shard_map/pallas_call | solution.py:267
  29.0 1.3 %collective-permute-done.6 = bf16[2,1,16,2048]{3,2,1,0:T(8,128)(2,1)S(1)} collective-permute-done((bf16[2,1,16,2048]{3,2,1,0:T(8,128)(2,1)S(1)}, bf16[2,1,16,2048]{3,2,1,0:T(8,128)(2,1)S(1)}, u32[]{:S(2)}, u32[]{:S(2)}) %collective-permute-start.6) | collective-permute-done | bytes 131104 | tf_op jit(solution)/shard_map/ppermute | solution.py:35
  30.4 1.6 %collective-permute-start.7 = (bf16[1,1,16,2048]{3,2,1,0:T(8,128)(2,1)S(1)}, bf16[1,1,16,2048]{3,2,1,0:T(8,128)(2,1)S(1)}, u32[]{:S(2)}, u32[]{:S(2)}) collective-permute-start(bf16[1,1,16,2048]{3,2,1,0:T(8,128)(2,1)S(1)} %slice.79), channel_id=1, source_target_pairs={{0,2},{1,3},{2,0},{3,1},{4,6},{5,7},{6,4},{7,5},{8,10},{9,11},{10,... | collective-permute-start | bytes 196616 | tf_op jit(solution)/shard_map/ppermute | solution.py:35
  32.0 2.8 %collective-permute-done.7 = bf16[1,1,16,2048]{3,2,1,0:T(8,128)(2,1)S(1)} collective-permute-done((bf16[1,1,16,2048]{3,2,1,0:T(8,128)(2,1)S(1)}, bf16[1,1,16,2048]{3,2,1,0:T(8,128)(2,1)S(1)}, u32[]{:S(2)}, u32[]{:S(2)}) %collective-permute-start.7) | collective-permute-done | bytes 65568 | tf_op jit(solution)/shard_map/ppermute | solution.py:35
  34.8 0.2 shard_map.117
  35.1 0.0 copy-start.10
  35.1 1.7 %collective-permute-start.11 = (bf16[16,2176]{1,0:T(8,128)(2,1)S(1)}, bf16[16,2176]{1,0:T(8,128)(2,1)S(1)}, u32[]{:S(2)}, u32[]{:S(2)}) collective-permute-start(bf16[16,2176]{1,0:T(8,128)(2,1)S(1)} %get-tuple-element.35), channel_id=1, source_target_pairs={{0,4},{4,0},{8,12},{12,8},{1,5},{5,1},{9,13},{13,9},{2,6},{6,2},{1... | collective-permute-start | bytes 208904 | tf_op jit(solution)/shard_map/ppermute | solution.py:35
  36.8 0.5 collective-permute-start.10
  37.3 1.3 %collective-permute-start.9 = (bf16[16,2176]{1,0:T(8,128)(2,1)S(1)}, bf16[16,2176]{1,0:T(8,128)(2,1)S(1)}, u32[]{:S(2)}, u32[]{:S(2)}) collective-permute-start(bf16[16,2176]{1,0:T(8,128)(2,1)S(1)} %get-tuple-element.35), channel_id=1, source_target_pairs={{0,8},{4,12},{8,0},{12,4},{1,9},{5,13},{9,1},{13,5},{2,10},{6,14},... | collective-permute-start | bytes 208904 | tf_op jit(solution)/shard_map/ppermute | solution.py:35
  38.6 0.8 %collective-permute-done.11 = bf16[16,2176]{1,0:T(8,128)(2,1)S(1)} collective-permute-done((bf16[16,2176]{1,0:T(8,128)(2,1)S(1)}, bf16[16,2176]{1,0:T(8,128)(2,1)S(1)}, u32[]{:S(2)}, u32[]{:S(2)}) %collective-permute-start.11) | collective-permute-done | bytes 69664 | tf_op jit(solution)/shard_map/ppermute | solution.py:35
  39.5 1.6 %collective-permute-start.14 = (bf16[32,2176]{1,0:T(8,128)(2,1)S(1)}, bf16[32,2176]{1,0:T(8,128)(2,1)S(1)}, u32[]{:S(2)}, u32[]{:S(2)}) collective-permute-start(bf16[32,2176]{1,0:T(8,128)(2,1)S(1)} %pad_maximum_fusion.1), channel_id=1, source_target_pairs={{0,2},{1,3},{2,0},{3,1},{4,6},{5,7},{6,4},{7,5},{8,10},{9,11},{10,... | collective-permute-start | bytes 417800 | tf_op jit(solution)/shard_map/ppermute | solution.py:35
  41.0 2.6 %collective-permute-done.10 = bf16[16,2176]{1,0:T(8,128)(2,1)S(1)} collective-permute-done((bf16[16,2176]{1,0:T(8,128)(2,1)S(1)}, bf16[16,2176]{1,0:T(8,128)(2,1)S(1)}, u32[]{:S(2)}, u32[]{:S(2)}) %collective-permute-start.10) | collective-permute-done | bytes 69664 | tf_op jit(solution)/shard_map/ppermute | solution.py:35
  43.6 2.0 %collective-permute-done.9 = bf16[16,2176]{1,0:T(8,128)(2,1)S(1)} collective-permute-done((bf16[16,2176]{1,0:T(8,128)(2,1)S(1)}, bf16[16,2176]{1,0:T(8,128)(2,1)S(1)}, u32[]{:S(2)}, u32[]{:S(2)}) %collective-permute-start.9) | collective-permute-done | bytes 69664 | tf_op jit(solution)/shard_map/ppermute | solution.py:35
  45.7 1.6 %collective-permute-start.12 = (bf16[32,2176]{1,0:T(8,128)(2,1)S(1)}, bf16[32,2176]{1,0:T(8,128)(2,1)S(1)}, u32[]{:S(2)}, u32[]{:S(2)}) collective-permute-start(bf16[32,2176]{1,0:T(8,128)(2,1)S(1)} %pad_maximum_fusion), channel_id=1, source_target_pairs={{0,2},{1,3},{2,0},{3,1},{4,6},{5,7},{6,4},{7,5},{8,10},{9,11},{10,... | collective-permute-start | bytes 417800 | tf_op jit(solution)/shard_map/ppermute | solution.py:35
  47.3 0.6 fusion.17.refs_1_
  47.9 0.7 %fusion.14.refs_0_ = f32[2,32,384]{2,1,0:T(8,128)S(1)} fusion(bf16[2048,2,384]{2,1,0:T(2,128)(2,1)S(1)} %bitcast.57, bf16[32,2176]{1,0:T(8,128)(2,1)S(1)} %collective-permute-done.14.rows), kind=kOutput, calls=%fused_computation.10 | convolution fusion | flops 100663296 | bytes 3375104 | tf_op jit(solution)/shard_map/nd,dgh->gnh/dot_general | solution.py:352
  48.6 0.7 %shard_map.119 = bf16[32,2048]{1,0:T(8,128)(2,1)S(1)} custom-call(bf16[32,2176]{1,0:T(8,128)(2,1)S(1)} %collective-permute-done.14.rows, f32[2,32,384]{2,1,0:T(8,128)S(1)} %fusion.14.refs_0_, f32[2,32,384]{2,1,0:T(8,128)S(1)} %fusion.17.refs_1_, bf16[1,384,2048]{2,1,0:T(8,128)(2,1)S(1)} %copy-done, bf16[1,384,2048]{2,1,0:T(8,128)(2,1)S(1)} %collective-permute-done.13.refs_3_), custom_call_target="tpu_custom_call" | custom-call | flops 100663296 | bytes 2097152 | tf_op jit(solution)/shard_map/pallas_call | solution.py:356
  49.3 0.6 collective-permute-start.15
  49.9 1.0 %collective-permute-done.12 = bf16[32,2176]{1,0:T(8,128)(2,1)S(1)} collective-permute-done((bf16[32,2176]{1,0:T(8,128)(2,1)S(1)}, bf16[32,2176]{1,0:T(8,128)(2,1)S(1)}, u32[]{:S(2)}, u32[]{:S(2)}) %collective-permute-start.12) | collective-permute-done | bytes 139296 | tf_op jit(solution)/shard_map/ppermute | solution.py:35
  50.9 0.7 fusion.11.refs_1_
  51.6 0.7 %fusion.8.refs_0_ = f32[2,96,384]{2,1,0:T(8,128)S(1)} fusion(bf16[2048,2,384]{2,1,0:T(2,128)(2,1)S(1)} %bitcast.58, bf16[96,2176]{1,0:T(8,128)(2,1)S(1)} %constant_dynamic-update-slice_fusion.rows), kind=kOutput, calls=%fused_computation.8 | convolution fusion | flops 301989888 | bytes 3833856 | tf_op jit(solution)/shard_map/nd,dgh->gnh/dot_general | solution.py:352
  52.3 0.7 %shard_map.118 = (f32[32,2048]{1,0:T(8,128)S(1)}, f32[32,2048]{1,0:T(8,128)S(1)}, bf16[32,2048]{1,0:T(8,128)(2,1)S(1)}) custom-call(bf16[96,2176]{1,0:T(8,128)(2,1)S(1)} %constant_dynamic-update-slice_fusion.rows, f32[2,96,384]{2,1,0:T(8,128)S(1)} %fusion.8.refs_0_, f32[2,96,384]{2,1,0:T(8,128)S(1)} %fusion.11.refs_1_, bf16[1,384,2048]{2,1,0:T(8,128)(2,1)S(1)} %copy-done, ...), custom_call_target="tpu_custom_call" | custom-call | flops 301989888 | bytes 2097152 | tf_op jit(solution)/shard_map/pallas_call | solution.py:356
  53.0 2.2 %collective-permute-start.16 = (bf16[32,2048]{1,0:T(8,128)(2,1)S(1)}, bf16[32,2048]{1,0:T(8,128)(2,1)S(1)}, u32[]{:S(2)}, u32[]{:S(2)}) collective-permute-start(bf16[32,2048]{1,0:T(8,128)(2,1)S(1)} %get-tuple-element.39), channel_id=1, source_target_pairs={{0,2},{1,3},{2,0},{3,1},{4,6},{5,7},{6,4},{7,5},{8,10},{9,11},{10,... | collective-permute-start | bytes 393224 | tf_op jit(solution)/shard_map/ppermute | solution.py:35
  55.2 0.1 collective-permute-start.19
  55.3 2.8 %collective-permute-done.16 = bf16[32,2048]{1,0:T(8,128)(2,1)S(1)} collective-permute-done((bf16[32,2048]{1,0:T(8,128)(2,1)S(1)}, bf16[32,2048]{1,0:T(8,128)(2,1)S(1)}, u32[]{:S(2)}, u32[]{:S(2)}) %collective-permute-start.16) | collective-permute-done | bytes 131104 | tf_op jit(solution)/shard_map/ppermute | solution.py:35
  58.2 0.1 collective-permute-start.17
  58.2 2.2 %collective-permute-start.18 = (bf16[16,2048]{1,0:T(8,128)(2,1)S(1)}, bf16[16,2048]{1,0:T(8,128)(2,1)S(1)}, u32[]{:S(2)}, u32[]{:S(2)}) collective-permute-start(bf16[16,2048]{1,0:T(8,128)(2,1)S(1)} %get-tuple-element.43), channel_id=1, source_target_pairs={{0,12},{4,8},{8,4},{12,0},{1,13},{5,9},{9,5},{13,1},{2,14},{6,10},... | collective-permute-start | bytes 196616 | tf_op jit(solution)/shard_map/ppermute | solution.py:35
  60.4 3.0 %collective-permute-done.17 = bf16[16,2048]{1,0:T(8,128)(2,1)S(1)} collective-permute-done((bf16[16,2048]{1,0:T(8,128)(2,1)S(1)}, bf16[16,2048]{1,0:T(8,128)(2,1)S(1)}, u32[]{:S(2)}, u32[]{:S(2)}) %collective-permute-start.17) | collective-permute-done | bytes 65568 | tf_op jit(solution)/shard_map/ppermute | solution.py:35
  63.4 1.0 %collective-permute-done.18 = bf16[16,2048]{1,0:T(8,128)(2,1)S(1)} collective-permute-done((bf16[16,2048]{1,0:T(8,128)(2,1)S(1)}, bf16[16,2048]{1,0:T(8,128)(2,1)S(1)}, u32[]{:S(2)}, u32[]{:S(2)}) %collective-permute-start.18) | collective-permute-done | bytes 65568 | tf_op jit(solution)/shard_map/ppermute | solution.py:35
  64.4 0.7 %fusion.24 = bf16[1,16,2048]{2,1,0:T(8,128)(2,1)} fusion(bf16[16,2048]{1,0:T(8,128)(2,1)S(1)} %collective-permute-done.19, bf16[16,2048]{1,0:T(8,128)(2,1)S(1)} %collective-permute-done.18, bf16[16,2048]{1,0:T(8,128)(2,1)S(1)} %collective-permute-done.17, f32[32,2048]{1,0:T(8,128)S(1)} %convert_add_fusion, bf16[16,2048]{1,0:T(8,128)(2,1)S(1)} %get-tuple-element.34), kind=kLoop, calls=%fused_computation.29 | loop fusion | flops 294912 | bytes 458752 | tf_op jit(solution)/shard_map/convert_element_type | solution.py:501
  (42 shorter events, 0.3 us)
Async XLA Ops:
  0.6 34.1 %collective-permute-start.8 = (bf16[1,2048,2,384]{3,2,1,0:T(2,128)(2,1)}, bf16[1,2048,2,384]{3,2,1,0:T(2,128)(2,1)S(1)}, u32[]{:S(2)}, u32[]{:S(2)}) collective-permute-start(bf16[1,2048,2,384]{3,2,1,0:T(2,128)(2,1)} %param.18), channel_id=1, source_target_pairs={{0,1},{1,0},{2,3},{3,2},{4,5},{5,4},{6,7},{7,6},{8,9},{9,8},{10,11... | collective-permute-start | bytes 9437192 | tf_op jit(solution)/shard_map/ppermute | solution.py:35
  2.2 8.9 %collective-permute-start.2 = (bf16[576,128]{1,0:T(8,128)(2,1)S(1)}, bf16[576,128]{1,0:T(8,128)(2,1)S(1)}, u32[]{:S(2)}, u32[]{:S(2)}) collective-permute-start(bf16[576,128]{1,0:T(8,128)(2,1)S(1)} %get-tuple-element.40.keys), channel_id=1, source_target_pairs={{0,12},{4,0},{8,4},{12,8},{1,13},{5,1},{9,5},{13,9},{2,14},{6,2},{... | collective-permute-start | bytes 442376 | tf_op jit(solution)/shard_map/ppermute | solution.py:40
  6.8 8.6 %collective-permute-start = (bf16[576,128]{1,0:T(8,128)(2,1)S(1)}, bf16[576,128]{1,0:T(8,128)(2,1)S(1)}, u32[]{:S(2)}, u32[]{:S(2)}) collective-permute-start(bf16[576,128]{1,0:T(8,128)(2,1)S(1)} %get-tuple-element.41.values), channel_id=1, source_target_pairs={{0,4},{4,8},{8,12},{12,0},{1,5},{5,9},{9,13},{13,1},{2,6},{6,10},{... | collective-permute-start | bytes 442376 | tf_op jit(solution)/shard_map/ppermute | solution.py:40
  6.8 14.9 %collective-permute-start.4 = (bf16[576,128]{1,0:T(8,128)(2,1)S(1)}, bf16[576,128]{1,0:T(8,128)(2,1)S(1)}, u32[]{:S(2)}, u32[]{:S(2)}) collective-permute-start(bf16[576,128]{1,0:T(8,128)(2,1)S(1)} %get-tuple-element.40.keys), channel_id=1, source_target_pairs={{0,4},{4,8},{8,12},{12,0},{1,5},{5,9},{9,13},{13,1},{2,6},{6,10},{... | collective-permute-start | bytes 442376 | tf_op jit(solution)/shard_map/ppermute | solution.py:40
  6.9 14.9 %collective-permute-start.5 = (bf16[576,128]{1,0:T(8,128)(2,1)S(1)}, bf16[576,128]{1,0:T(8,128)(2,1)S(1)}, u32[]{:S(2)}, u32[]{:S(2)}) collective-permute-start(bf16[576,128]{1,0:T(8,128)(2,1)S(1)} %get-tuple-element.41.values), channel_id=1, source_target_pairs={{0,12},{4,0},{8,4},{12,8},{1,13},{5,1},{9,5},{13,9},{2,14},{6,2},{... | collective-permute-start | bytes 442376 | tf_op jit(solution)/shard_map/ppermute | solution.py:40
  11.1 12.7 %collective-permute-start.3 = (bf16[576,128]{1,0:T(8,128)(2,1)S(1)}, bf16[576,128]{1,0:T(8,128)(2,1)S(1)}, u32[]{:S(2)}, u32[]{:S(2)}) collective-permute-start(bf16[576,128]{1,0:T(8,128)(2,1)S(1)} %collective-permute-done.2.refs_2_), channel_id=1, source_target_pairs={{0,12},{4,0},{8,4},{12,8},{1,13},{5,1},{9,5},{13,9},{2,14},{6,2},{... | collective-permute-start | bytes 442376 | tf_op jit(solution)/shard_map/ppermute | solution.py:40
  15.5 11.9 %collective-permute-start.1 = (bf16[576,128]{1,0:T(8,128)(2,1)S(1)}, bf16[576,128]{1,0:T(8,128)(2,1)S(1)}, u32[]{:S(2)}, u32[]{:S(2)}) collective-permute-start(bf16[576,128]{1,0:T(8,128)(2,1)S(1)} %collective-permute-done.refs_1_), channel_id=1, source_target_pairs={{0,4},{4,8},{8,12},{12,0},{1,5},{5,9},{9,13},{13,1},{2,6},{6,10},{... | collective-permute-start | bytes 442376 | tf_op jit(solution)/shard_map/ppermute | solution.py:40
  16.7 2.2 %copy-start.1 = (bf16[1024,2048]{1,0:T(8,128)(2,1)S(1)}, bf16[1024,2048]{1,0:T(8,128)(2,1)}, u32[]{:S(2)}) copy-start(bf16[1024,2048]{1,0:T(8,128)(2,1)} %weight.1) | copy-start | bytes 12582916
  18.9 0.9 %copy-start.7 = (bf16[1,64,1024]{2,1,0:T(8,128)(2,1)S(1)}, bf16[1,64,1024]{2,1,0:T(8,128)(2,1)}, u32[]{:S(2)}) copy-start(bf16[1,64,1024]{2,1,0:T(8,128)(2,1)} %param.10) | copy-start | bytes 393220
  19.8 0.7 %copy-start.9 = (s32[1,4]{1,0:T(1,128)S(1)}, s32[1,4]{1,0:T(1,128)}, u32[]{:S(2)}) copy-start(s32[1,4]{1,0:T(1,128)} %param.12) | copy-start | bytes 52
  20.4 1.3 %copy-start.8 = (bf16[1,64,1024]{2,1,0:T(8,128)(2,1)S(1)}, bf16[1,64,1024]{2,1,0:T(8,128)(2,1)}, u32[]{:S(2)}) copy-start(bf16[1,64,1024]{2,1,0:T(8,128)(2,1)} %param.10) | copy-start | bytes 393220
  20.4 6.9 %copy-start.2 = (bf16[1024,2048]{1,0:T(8,128)(2,1)S(1)}, bf16[1024,2048]{1,0:T(8,128)(2,1)}, u32[]{:S(2)}) copy-start(bf16[1024,2048]{1,0:T(8,128)(2,1)} %weight.1) | copy-start | bytes 12582916
  24.3 10.4 %copy-start.3 = (bf16[1,16,2048]{2,1,0:T(8,128)(2,1)S(1)}, bf16[1,16,2048]{2,1,0:T(8,128)(2,1)}, u32[]{:S(2)}) copy-start(bf16[1,16,2048]{2,1,0:T(8,128)(2,1)} %param.13) | copy-start | bytes 196612
  24.4 10.4 %copy-start.4 = (f32[2048]{0:T(1024)S(1)}, f32[2048]{0:T(1024)}, u32[]{:S(2)}) copy-start(f32[2048]{0:T(1024)} %param.15) | copy-start | bytes 24580
  24.4 10.4 %copy-start.5 = (s32[1,16,8]{1,2,0:T(8,128)S(1)}, s32[1,16,8]{1,2,0:T(8,128)}, u32[]{:S(2)}) copy-start(s32[1,16,8]{1,2,0:T(8,128)} %param.16) | copy-start | bytes 1540
  24.4 10.4 %copy-start.6 = (f32[1,16,8]{1,2,0:T(8,128)S(1)}, f32[1,16,8]{1,2,0:T(8,128)}, u32[]{:S(2)}) copy-start(f32[1,16,8]{1,2,0:T(8,128)} %param.17) | copy-start | bytes 1540
  29.0 7.7 %copy-start = (bf16[1,384,2048]{2,1,0:T(8,128)(2,1)S(1)}, bf16[1,384,2048]{2,1,0:T(8,128)(2,1)}, u32[]{:S(2)}) copy-start(bf16[1,384,2048]{2,1,0:T(8,128)(2,1)} %refs_2_.1) | copy-start | bytes 4718596
  29.0 1.3 %collective-permute-start.6 = (bf16[2,1,16,2048]{3,2,1,0:T(8,128)(2,1)S(1)}, bf16[2,1,16,2048]{3,2,1,0:T(8,128)(2,1)S(1)}, u32[]{:S(2)}, u32[]{:S(2)}) collective-permute-start(bf16[2,1,16,2048]{3,2,1,0:T(8,128)(2,1)S(1)} %bitcast.54), channel_id=1, source_target_pairs={{0,1},{1,0},{2,3},{3,2},{4,5},{5,4},{6,7},{7,6},{8,9},{9,8},{10,11... | collective-permute-start | bytes 393224 | tf_op jit(solution)/shard_map/ppermute | solution.py:35
  30.4 4.3 %collective-permute-start.7 = (bf16[1,1,16,2048]{3,2,1,0:T(8,128)(2,1)S(1)}, bf16[1,1,16,2048]{3,2,1,0:T(8,128)(2,1)S(1)}, u32[]{:S(2)}, u32[]{:S(2)}) collective-permute-start(bf16[1,1,16,2048]{3,2,1,0:T(8,128)(2,1)S(1)} %slice.79), channel_id=1, source_target_pairs={{0,2},{1,3},{2,0},{3,1},{4,6},{5,7},{6,4},{7,5},{8,10},{9,11},{10,... | collective-permute-start | bytes 196616 | tf_op jit(solution)/shard_map/ppermute | solution.py:35
  35.1 12.9 %copy-start.10 = (bf16[1,2048,2,384]{3,2,1,0:T(2,128)(2,1)S(1)}, bf16[1,2048,2,384]{3,2,1,0:T(2,128)(2,1)}, u32[]{:S(2)}) copy-start(bf16[1,2048,2,384]{3,2,1,0:T(2,128)(2,1)} %param.18) | copy-start | bytes 9437188
  35.1 4.4 %collective-permute-start.11 = (bf16[16,2176]{1,0:T(8,128)(2,1)S(1)}, bf16[16,2176]{1,0:T(8,128)(2,1)S(1)}, u32[]{:S(2)}, u32[]{:S(2)}) collective-permute-start(bf16[16,2176]{1,0:T(8,128)(2,1)S(1)} %get-tuple-element.35), channel_id=1, source_target_pairs={{0,4},{4,0},{8,12},{12,8},{1,5},{5,1},{9,13},{13,9},{2,6},{6,2},{1... | collective-permute-start | bytes 208904 | tf_op jit(solution)/shard_map/ppermute | solution.py:35
  36.8 11.9 %collective-permute-start.13 = (bf16[1,384,2048]{2,1,0:T(8,128)(2,1)S(1)}, bf16[1,384,2048]{2,1,0:T(8,128)(2,1)S(1)}, u32[]{:S(2)}, u32[]{:S(2)}) collective-permute-start(bf16[1,384,2048]{2,1,0:T(8,128)(2,1)S(1)} %copy-done), channel_id=1, source_target_pairs={{0,1},{1,0},{2,3},{3,2},{4,5},{5,4},{6,7},{7,6},{8,9},{9,8},{10,11... | collective-permute-start | bytes 4718600 | tf_op jit(solution)/shard_map/ppermute | solution.py:35
  36.8 6.9 %collective-permute-start.10 = (bf16[16,2176]{1,0:T(8,128)(2,1)S(1)}, bf16[16,2176]{1,0:T(8,128)(2,1)S(1)}, u32[]{:S(2)}, u32[]{:S(2)}) collective-permute-start(bf16[16,2176]{1,0:T(8,128)(2,1)S(1)} %get-tuple-element.35), channel_id=1, source_target_pairs={{0,12},{4,8},{8,4},{12,0},{1,13},{5,9},{9,5},{13,1},{2,14},{6,10},... | collective-permute-start | bytes 208904 | tf_op jit(solution)/shard_map/ppermute | solution.py:35
  37.3 8.4 %collective-permute-start.9 = (bf16[16,2176]{1,0:T(8,128)(2,1)S(1)}, bf16[16,2176]{1,0:T(8,128)(2,1)S(1)}, u32[]{:S(2)}, u32[]{:S(2)}) collective-permute-start(bf16[16,2176]{1,0:T(8,128)(2,1)S(1)} %get-tuple-element.35), channel_id=1, source_target_pairs={{0,8},{4,12},{8,0},{12,4},{1,9},{5,13},{9,1},{13,5},{2,10},{6,14},... | collective-permute-start | bytes 208904 | tf_op jit(solution)/shard_map/ppermute | solution.py:35
  39.5 7.8 %collective-permute-start.14 = (bf16[32,2176]{1,0:T(8,128)(2,1)S(1)}, bf16[32,2176]{1,0:T(8,128)(2,1)S(1)}, u32[]{:S(2)}, u32[]{:S(2)}) collective-permute-start(bf16[32,2176]{1,0:T(8,128)(2,1)S(1)} %pad_maximum_fusion.1), channel_id=1, source_target_pairs={{0,2},{1,3},{2,0},{3,1},{4,6},{5,7},{6,4},{7,5},{8,10},{9,11},{10,... | collective-permute-start | bytes 417800 | tf_op jit(solution)/shard_map/ppermute | solution.py:35
  45.7 5.2 %collective-permute-start.12 = (bf16[32,2176]{1,0:T(8,128)(2,1)S(1)}, bf16[32,2176]{1,0:T(8,128)(2,1)S(1)}, u32[]{:S(2)}, u32[]{:S(2)}) collective-permute-start(bf16[32,2176]{1,0:T(8,128)(2,1)S(1)} %pad_maximum_fusion), channel_id=1, source_target_pairs={{0,2},{1,3},{2,0},{3,1},{4,6},{5,7},{6,4},{7,5},{8,10},{9,11},{10,... | collective-permute-start | bytes 417800 | tf_op jit(solution)/shard_map/ppermute | solution.py:35
  49.3 5.9 %collective-permute-start.15 = (bf16[32,2048]{1,0:T(8,128)(2,1)S(1)}, bf16[32,2048]{1,0:T(8,128)(2,1)S(1)}, u32[]{:S(2)}, u32[]{:S(2)}) collective-permute-start(bf16[32,2048]{1,0:T(8,128)(2,1)S(1)} %shard_map.119), channel_id=1, source_target_pairs={{0,2},{1,3},{2,0},{3,1},{4,6},{5,7},{6,4},{7,5},{8,10},{9,11},{10,... | collective-permute-start | bytes 393224 | tf_op jit(solution)/shard_map/ppermute | solution.py:35
  53.0 5.1 %collective-permute-start.16 = (bf16[32,2048]{1,0:T(8,128)(2,1)S(1)}, bf16[32,2048]{1,0:T(8,128)(2,1)S(1)}, u32[]{:S(2)}, u32[]{:S(2)}) collective-permute-start(bf16[32,2048]{1,0:T(8,128)(2,1)S(1)} %get-tuple-element.39), channel_id=1, source_target_pairs={{0,2},{1,3},{2,0},{3,1},{4,6},{5,7},{6,4},{7,5},{8,10},{9,11},{10,... | collective-permute-start | bytes 393224 | tf_op jit(solution)/shard_map/ppermute | solution.py:35
  55.2 5.2 %collective-permute-start.19 = (bf16[16,2048]{1,0:T(8,128)(2,1)S(1)}, bf16[16,2048]{1,0:T(8,128)(2,1)S(1)}, u32[]{:S(2)}, u32[]{:S(2)}) collective-permute-start(bf16[16,2048]{1,0:T(8,128)(2,1)S(1)} %slice.78), channel_id=1, source_target_pairs={{0,4},{4,0},{8,12},{12,8},{1,5},{5,1},{9,13},{13,9},{2,6},{6,2},{1... | collective-permute-start | bytes 196616 | tf_op jit(solution)/shard_map/ppermute | solution.py:35
  58.2 5.2 %collective-permute-start.17 = (bf16[16,2048]{1,0:T(8,128)(2,1)S(1)}, bf16[16,2048]{1,0:T(8,128)(2,1)S(1)}, u32[]{:S(2)}, u32[]{:S(2)}) collective-permute-start(bf16[16,2048]{1,0:T(8,128)(2,1)S(1)} %get-tuple-element.42), channel_id=1, source_target_pairs={{0,8},{4,12},{8,0},{12,4},{1,9},{5,13},{9,1},{13,5},{2,10},{6,14},... | collective-permute-start | bytes 196616 | tf_op jit(solution)/shard_map/ppermute | solution.py:35
  58.2 6.2 %collective-permute-start.18 = (bf16[16,2048]{1,0:T(8,128)(2,1)S(1)}, bf16[16,2048]{1,0:T(8,128)(2,1)S(1)}, u32[]{:S(2)}, u32[]{:S(2)}) collective-permute-start(bf16[16,2048]{1,0:T(8,128)(2,1)S(1)} %get-tuple-element.43), channel_id=1, source_target_pairs={{0,12},{4,8},{8,4},{12,0},{1,13},{5,9},{9,5},{13,1},{2,14},{6,10},... | collective-permute-start | bytes 196616 | tf_op jit(solution)/shard_map/ppermute | solution.py:35

commit v15 on v14

--- a/solution.py
+++ b/solution.py
@@ -387,15 +387,18 @@
     far = strides(lax.axis_size("exp"))[:1]
     chunks = chunks_of(lax.axis_size("ctx"))
 
-    joined = [
-        jnp.concatenate(
-            [rows if offset == 0 else swap(rows, "ctx", offset) for offset in chunk], axis=0
-        )
+    blocks = [
+        [rows if offset == 0 else swap(rows, "ctx", offset) for offset in chunk]
         for chunk in chunks
     ]
+    joined = [jnp.concatenate(parts, axis=0) for parts in blocks]
     crossed = []
-    for piece in joined if far else []:
-        crossed.append(swap(piece, "exp", far[0]))
+    if far:
+        near = swap(joined[-1], "exp", far[0])
+        for parts in blocks[:-1]:
+            parts[0], _ = lax.optimization_barrier((parts[0], near))
+            crossed.append(jnp.concatenate([swap(part, "exp", far[0]) for part in parts], axis=0))
+        crossed.append(near)
     *homes, first = expert_apply(
         joined + (crossed or joined)[:1], [jnp.float32] * len(joined) + [jnp.bfloat16], weights
     )

time: 65.3 us -> 65.8 us (level)
  starting transfers between devices: 27.8 us -> 32.7 us
  waiting for transfers between devices: 21.4 us -> 17.1 us
    ppermute x14 -> x15, starting transfers between devices: 13.8 us -> 18.7 us  [swap(): lax.ppermute(value, axis, [(i, i ^ stride) for i in range(lax.axis_size(a...]
    ppermute x14 -> x15, waiting for transfers between devices: 17.4 us -> 13.1 us  [swap(): lax.ppermute(value, axis, [(i, i ^ stride) for i in range(lax.axis_size(a...]
    unnamed x27 -> x28, local copies, waits for them, and re-layouts: 4.83 us -> 4.84 us
  transfers between devices with their start and end apart: 20 -> 21, of which waited for: 13 -> 14; matrix products, arithmetic and copies ran while one was open for 6% -> 6% of each run, Pallas kernels for 10% -> 10%
where the time goes in v15:
time: 65.8 us; the launch traced here: 65.6 us
  starting transfers between devices  32.7 us (50%)
  waiting for transfers between devices  17.1 us (26%)
  Pallas kernels  6.69 us (10%)
  local copies, waits for them, and re-layouts  4.91 us (7%)
  matrix products  2.61 us (4%)
  between operations  0.85 us (1%)
  other arithmetic  0.77 us (1%)
    ppermute x15, starting transfers between devices, swap(): lax.ppermute(value, axis, [(i, i ^ stride) for i in range(lax.axis_size(a...  18.7 us
    ppermute x6, starting transfers between devices, shift(): lax.ppermute(value, axis, [(i, (i + step) % count) for i in range(count)])  14 us
    ppermute x15, waiting for transfers between devices, swap(): lax.ppermute(value, axis, [(i, i ^ stride) for i in range(lax.axis_size(a...  13.1 us
    unnamed x28, local copies, waits for them, and re-layouts  4.84 us
    ppermute x6, waiting for transfers between devices, shift(): lax.ppermute(value, axis, [(i, (i + step) % count) for i in range(count)])  3.97 us
    dot_general x4, matrix products, expert_apply(): jnp.einsum('nd,dgh->gnh', rows[:, :width], gate_up[0], preferred_element_...  2.61 us
    pallas_call x1, Pallas kernels, attention(): pl.pallas_call(functools.partial(late_kernel, fresh_block), out_shape=sha...  1.68 us
    pallas_call x1, Pallas kernels, attention(): pl.pallas_call(functools.partial(middle_kernel, [offset for offset, _, _...  1.43 us
  transfers between devices with their start and end apart: 21, of which 14 were waited for; matrix products, arithmetic and copies ran while one was open for 6% of the time, Pallas kernels for 10%

profile of v15, /device:TPU:0, one launch (start us, length us, event | category | flops | bytes accessed | tf_op | source)
XLA Modules:
  0.0 65.6 jit_solution(10320749190078486924)
XLA Ops:
  0.6 0.5 collective-permute-start.8
  1.1 1.0 %copy.34 = bf16[1,576,2,128]{3,1,2,0:T(8,128)(2,1)S(1)} copy(bf16[1,576,2,128]{3,2,1,0:T(2,128)(2,1)} %param.11) | data formatting | bytes 589824 | tf_op args[1]
  2.2 4.7 %collective-permute-start.2 = (bf16[576,128]{1,0:T(8,128)(2,1)S(1)}, bf16[576,128]{1,0:T(8,128)(2,1)S(1)}, u32[]{:S(2)}, u32[]{:S(2)}) collective-permute-start(bf16[576,128]{1,0:T(8,128)(2,1)S(1)} %get-tuple-element.42.keys), channel_id=1, source_target_pairs={{0,12},{4,0},{8,4},{12,8},{1,13},{5,1},{9,5},{13,9},{2,14},{6,2},{... | collective-permute-start | bytes 442376 | tf_op jit(solution)/shard_map/ppermute | solution.py:40
  6.9 3.9 %collective-permute-start.5 = (bf16[576,128]{1,0:T(8,128)(2,1)S(1)}, bf16[576,128]{1,0:T(8,128)(2,1)S(1)}, u32[]{:S(2)}, u32[]{:S(2)}) collective-permute-start(bf16[576,128]{1,0:T(8,128)(2,1)S(1)} %get-tuple-element.43.values), channel_id=1, source_target_pairs={{0,12},{4,0},{8,4},{12,8},{1,13},{5,1},{9,5},{13,9},{2,14},{6,2},{... | collective-permute-start | bytes 442376 | tf_op jit(solution)/shard_map/ppermute | solution.py:40
  10.7 0.3 collective-permute-done.2.refs_2_
  11.1 4.3 %collective-permute-start.3 = (bf16[576,128]{1,0:T(8,128)(2,1)S(1)}, bf16[576,128]{1,0:T(8,128)(2,1)S(1)}, u32[]{:S(2)}, u32[]{:S(2)}) collective-permute-start(bf16[576,128]{1,0:T(8,128)(2,1)S(1)} %collective-permute-done.2.refs_2_), channel_id=1, source_target_pairs={{0,12},{4,0},{8,4},{12,8},{1,13},{5,1},{9,5},{13,9},{2,14},{6,2},{... | collective-permute-start | bytes 442376 | tf_op jit(solution)/shard_map/ppermute | solution.py:40
  15.3 0.1 collective-permute-done.refs_1_
  15.5 1.2 %collective-permute-start.1 = (bf16[576,128]{1,0:T(8,128)(2,1)S(1)}, bf16[576,128]{1,0:T(8,128)(2,1)S(1)}, u32[]{:S(2)}, u32[]{:S(2)}) collective-permute-start(bf16[576,128]{1,0:T(8,128)(2,1)S(1)} %collective-permute-done.refs_1_), channel_id=1, source_target_pairs={{0,4},{4,8},{8,12},{12,0},{1,5},{5,9},{9,13},{13,1},{2,6},{6,10},{... | collective-permute-start | bytes 442376 | tf_op jit(solution)/shard_map/ppermute | solution.py:40
  16.7 2.2 %copy-done.1 = bf16[1024,2048]{1,0:T(8,128)(2,1)S(1)} copy-done((bf16[1024,2048]{1,0:T(8,128)(2,1)S(1)}, bf16[1024,2048]{1,0:T(8,128)(2,1)}, u32[]{:S(2)}) %copy-start.1) | copy-done | bytes 4194328
  18.9 0.9 %copy-done.7 = bf16[1,64,1024]{2,1,0:T(8,128)(2,1)S(1)} copy-done((bf16[1,64,1024]{2,1,0:T(8,128)(2,1)S(1)}, bf16[1,64,1024]{2,1,0:T(8,128)(2,1)}, u32[]{:S(2)}) %copy-start.7) | copy-done | bytes 131096
  19.8 0.7 copy-done.9
  20.4 1.3 %shard_map.113 = (f32[1,512]{1,0:T(1,128)S(1)}, f32[1,512]{1,0:T(1,128)S(1)}, f32[128,512]{1,0:T(8,128)S(1)}, s32[4,128]{1,0:T(4,128)S(1)}) custom-call(s32[4]{0:T(128)S(1)} %bitcast.55, bf16[64,1024]{1,0:T(8,128)(2,1)S(1)} %bitcast.51, bf16[576,128]{1,0:T(8,128)(2,1)S(1)} %get-tuple-element.42.keys, bf16[576,128]{1,0:T(8,128)(2,1)S(1)} %get-tuple-element.43.values, ...), custom_call_target="tpu_custom_call" | custom-call | flops 2415919104 | bytes 8388608 | tf_op jit(solution)/shard_map/pallas_call | solution.py:225
  21.8 1.4 %shard_map.115 = (f32[1,512]{1,0:T(1,128)S(1)}, f32[1,512]{1,0:T(1,128)S(1)}, f32[128,512]{1,0:T(8,128)S(1)}) custom-call(bf16[64,1024]{1,0:T(8,128)(2,1)S(1)} %bitcast.52, s32[4,128]{1,0:T(4,128)S(1)} %get-tuple-element.22.lengths, bf16[576,128]{1,0:T(8,128)(2,1)S(1)} %collective-permute-done.4.refs_0_, bf16[576,128]{1,0:T(8,128)(2,1)S(1)} %collective-permute-done.refs_1_, ...), custom_call_target="tpu_custom_call" | custom-call | flops 301989888 | bytes 2097152 | tf_op jit(solution)/shard_map/pallas_call | solution.py:240
  23.2 0.5 collective-permute-done.3.keys
  23.7 0.6 shard_map.114
  24.4 0.0 copy-start.4
  24.4 3.0 %collective-permute-done.1.values = bf16[576,128]{1,0:T(8,128)(2,1)S(1)} collective-permute-done((bf16[576,128]{1,0:T(8,128)(2,1)S(1)}, bf16[576,128]{1,0:T(8,128)(2,1)S(1)}, u32[]{:S(2)}, u32[]{:S(2)}) %collective-permute-start.1) | collective-permute-done | bytes 147488 | tf_op jit(solution)/shard_map/ppermute | solution.py:40
  27.4 1.7 %shard_map.116 = (bf16[64,1024]{1,0:T(8,128)(2,1)}, f32[32,2048]{1,0:T(8,128)S(1)}, bf16[32,2048]{1,0:T(8,128)(2,1)S(1)}) custom-call(bf16[576,128]{1,0:T(8,128)(2,1)S(1)} %collective-permute-done.1.values, f32[1,512]{1,0:T(1,128)S(1)} %get-tuple-element.23.last_peak, f32[1,512]{1,0:T(1,128)S(1)} %get-tuple-element.24.last_total, ...), custom_call_target="tpu_custom_call" | custom-call | flops 419430400 | bytes 6291456 | tf_op jit(solution)/shard_map/pallas_call | solution.py:267
  29.0 1.3 %collective-permute-done.6 = bf16[2,1,16,2048]{3,2,1,0:T(8,128)(2,1)S(1)} collective-permute-done((bf16[2,1,16,2048]{3,2,1,0:T(8,128)(2,1)S(1)}, bf16[2,1,16,2048]{3,2,1,0:T(8,128)(2,1)S(1)}, u32[]{:S(2)}, u32[]{:S(2)}) %collective-permute-start.6) | collective-permute-done | bytes 131104 | tf_op jit(solution)/shard_map/ppermute | solution.py:35
  30.4 1.6 %collective-permute-start.7 = (bf16[1,1,16,2048]{3,2,1,0:T(8,128)(2,1)S(1)}, bf16[1,1,16,2048]{3,2,1,0:T(8,128)(2,1)S(1)}, u32[]{:S(2)}, u32[]{:S(2)}) collective-permute-start(bf16[1,1,16,2048]{3,2,1,0:T(8,128)(2,1)S(1)} %slice.79), channel_id=1, source_target_pairs={{0,2},{1,3},{2,0},{3,1},{4,6},{5,7},{6,4},{7,5},{8,10},{9,11},{10,... | collective-permute-start | bytes 196616 | tf_op jit(solution)/shard_map/ppermute | solution.py:35
  32.0 2.8 %collective-permute-done.7 = bf16[1,1,16,2048]{3,2,1,0:T(8,128)(2,1)S(1)} collective-permute-done((bf16[1,1,16,2048]{3,2,1,0:T(8,128)(2,1)S(1)}, bf16[1,1,16,2048]{3,2,1,0:T(8,128)(2,1)S(1)}, u32[]{:S(2)}, u32[]{:S(2)}) %collective-permute-start.7) | collective-permute-done | bytes 65568 | tf_op jit(solution)/shard_map/ppermute | solution.py:35
  34.8 0.2 shard_map.117
  35.1 1.7 %collective-permute-start.11 = (bf16[16,2176]{1,0:T(8,128)(2,1)S(1)}, bf16[16,2176]{1,0:T(8,128)(2,1)S(1)}, u32[]{:S(2)}, u32[]{:S(2)}) collective-permute-start(bf16[16,2176]{1,0:T(8,128)(2,1)S(1)} %get-tuple-element.36), channel_id=1, source_target_pairs={{0,4},{4,0},{8,12},{12,8},{1,5},{5,1},{9,13},{13,9},{2,6},{6,2},{1... | collective-permute-start | bytes 208904 | tf_op jit(solution)/shard_map/ppermute | solution.py:35
  36.8 0.5 collective-permute-start.10
  37.3 1.3 %collective-permute-start.9 = (bf16[16,2176]{1,0:T(8,128)(2,1)S(1)}, bf16[16,2176]{1,0:T(8,128)(2,1)S(1)}, u32[]{:S(2)}, u32[]{:S(2)}) collective-permute-start(bf16[16,2176]{1,0:T(8,128)(2,1)S(1)} %get-tuple-element.36), channel_id=1, source_target_pairs={{0,8},{4,12},{8,0},{12,4},{1,9},{5,13},{9,1},{13,5},{2,10},{6,14},... | collective-permute-start | bytes 208904 | tf_op jit(solution)/shard_map/ppermute | solution.py:35
  38.6 0.8 %collective-permute-done.11 = bf16[16,2176]{1,0:T(8,128)(2,1)S(1)} collective-permute-done((bf16[16,2176]{1,0:T(8,128)(2,1)S(1)}, bf16[16,2176]{1,0:T(8,128)(2,1)S(1)}, u32[]{:S(2)}, u32[]{:S(2)}) %collective-permute-start.11) | collective-permute-done | bytes 69664 | tf_op jit(solution)/shard_map/ppermute | solution.py:35
  39.5 1.6 %collective-permute-start.12 = (bf16[32,2176]{1,0:T(8,128)(2,1)S(1)}, bf16[32,2176]{1,0:T(8,128)(2,1)S(1)}, u32[]{:S(2)}, u32[]{:S(2)}) collective-permute-start(bf16[32,2176]{1,0:T(8,128)(2,1)S(1)} %pad_maximum_fusion), channel_id=1, source_target_pairs={{0,2},{1,3},{2,0},{3,1},{4,6},{5,7},{6,4},{7,5},{8,10},{9,11},{10,... | collective-permute-start | bytes 417800 | tf_op jit(solution)/shard_map/ppermute | solution.py:35
  41.0 2.6 %collective-permute-done.10 = bf16[16,2176]{1,0:T(8,128)(2,1)S(1)} collective-permute-done((bf16[16,2176]{1,0:T(8,128)(2,1)S(1)}, bf16[16,2176]{1,0:T(8,128)(2,1)S(1)}, u32[]{:S(2)}, u32[]{:S(2)}) %collective-permute-start.10) | collective-permute-done | bytes 69664 | tf_op jit(solution)/shard_map/ppermute | solution.py:35
  43.6 1.5 %collective-permute-start.14 = (bf16[16,2176]{1,0:T(8,128)(2,1)S(1)}, bf16[16,2176]{1,0:T(8,128)(2,1)S(1)}, u32[]{:S(2)}, u32[]{:S(2)}) collective-permute-start(bf16[16,2176]{1,0:T(8,128)(2,1)S(1)} %collective-permute-done.10), channel_id=1, source_target_pairs={{0,2},{1,3},{2,0},{3,1},{4,6},{5,7},{6,4},{7,5},{8,10},{9,11},{10,... | collective-permute-start | bytes 208904 | tf_op jit(solution)/shard_map/ppermute | solution.py:35
  45.1 0.5 collective-permute-done.9
  45.7 1.6 %collective-permute-start.13 = (bf16[16,2176]{1,0:T(8,128)(2,1)S(1)}, bf16[16,2176]{1,0:T(8,128)(2,1)S(1)}, u32[]{:S(2)}, u32[]{:S(2)}) collective-permute-start(bf16[16,2176]{1,0:T(8,128)(2,1)S(1)} %collective-permute-done.9), channel_id=1, source_target_pairs={{0,2},{1,3},{2,0},{3,1},{4,6},{5,7},{6,4},{7,5},{8,10},{9,11},{10,... | collective-permute-start | bytes 208904 | tf_op jit(solution)/shard_map/ppermute | solution.py:35
  47.3 0.6 fusion.17.refs_1_
  47.9 0.7 %fusion.14.refs_0_ = f32[2,32,384]{2,1,0:T(8,128)S(1)} fusion(bf16[2048,2,384]{2,1,0:T(2,128)(2,1)S(1)} %bitcast.57, bf16[32,2176]{1,0:T(8,128)(2,1)S(1)} %collective-permute-done.12.rows), kind=kOutput, calls=%fused_computation.10 | convolution fusion | flops 100663296 | bytes 3375104 | tf_op jit(solution)/shard_map/nd,dgh->gnh/dot_general | solution.py:352
  48.6 0.7 %shard_map.119 = bf16[32,2048]{1,0:T(8,128)(2,1)S(1)} custom-call(bf16[32,2176]{1,0:T(8,128)(2,1)S(1)} %collective-permute-done.12.rows, f32[2,32,384]{2,1,0:T(8,128)S(1)} %fusion.14.refs_0_, f32[2,32,384]{2,1,0:T(8,128)S(1)} %fusion.17.refs_1_, bf16[1,384,2048]{2,1,0:T(8,128)(2,1)S(1)} %copy-done, bf16[1,384,2048]{2,1,0:T(8,128)(2,1)S(1)} %collective-permute-done.15.refs_3_), custom_call_target="tpu_custom_call" | custom-call | flops 100663296 | bytes 2097152 | tf_op jit(solution)/shard_map/pallas_call | solution.py:356
  49.3 0.6 collective-permute-start.16
  49.9 0.2 collective-permute-done.13
  50.1 0.7 fusion.11.refs_1_
  50.8 0.7 %fusion.8.refs_0_ = f32[2,96,384]{2,1,0:T(8,128)S(1)} fusion(bf16[2048,2,384]{2,1,0:T(2,128)(2,1)S(1)} %bitcast.58, bf16[96,2176]{1,0:T(8,128)(2,1)S(1)} %constant_dynamic-update-slice_fusion.rows), kind=kOutput, calls=%fused_computation.8 | convolution fusion | flops 301989888 | bytes 3833856 | tf_op jit(solution)/shard_map/nd,dgh->gnh/dot_general | solution.py:352
  51.4 0.7 %shard_map.118 = (f32[32,2048]{1,0:T(8,128)S(1)}, f32[32,2048]{1,0:T(8,128)S(1)}, bf16[32,2048]{1,0:T(8,128)(2,1)S(1)}) custom-call(bf16[96,2176]{1,0:T(8,128)(2,1)S(1)} %constant_dynamic-update-slice_fusion.rows, f32[2,96,384]{2,1,0:T(8,128)S(1)} %fusion.8.refs_0_, f32[2,96,384]{2,1,0:T(8,128)S(1)} %fusion.11.refs_1_, bf16[1,384,2048]{2,1,0:T(8,128)(2,1)S(1)} %copy-done, ...), custom_call_target="tpu_custom_call" | custom-call | flops 301989888 | bytes 2097152 | tf_op jit(solution)/shard_map/pallas_call | solution.py:356
  52.2 1.6 %collective-permute-start.17 = (bf16[32,2048]{1,0:T(8,128)(2,1)S(1)}, bf16[32,2048]{1,0:T(8,128)(2,1)S(1)}, u32[]{:S(2)}, u32[]{:S(2)}) collective-permute-start(bf16[32,2048]{1,0:T(8,128)(2,1)S(1)} %get-tuple-element.41), channel_id=1, source_target_pairs={{0,2},{1,3},{2,0},{3,1},{4,6},{5,7},{6,4},{7,5},{8,10},{9,11},{10,... | collective-permute-start | bytes 393224 | tf_op jit(solution)/shard_map/ppermute | solution.py:35
  53.8 1.2 %collective-permute-done.16 = bf16[32,2048]{1,0:T(8,128)(2,1)S(1)} collective-permute-done((bf16[32,2048]{1,0:T(8,128)(2,1)S(1)}, bf16[32,2048]{1,0:T(8,128)(2,1)S(1)}, u32[]{:S(2)}, u32[]{:S(2)}) %collective-permute-start.16) | collective-permute-done | bytes 131104 | tf_op jit(solution)/shard_map/ppermute | solution.py:35
  55.0 1.6 %collective-permute-start.20 = (bf16[16,2048]{1,0:T(8,128)(2,1)S(1)}, bf16[16,2048]{1,0:T(8,128)(2,1)S(1)}, u32[]{:S(2)}, u32[]{:S(2)}) collective-permute-start(bf16[16,2048]{1,0:T(8,128)(2,1)S(1)} %slice.78), channel_id=1, source_target_pairs={{0,4},{4,0},{8,12},{12,8},{1,5},{5,1},{9,13},{13,9},{2,6},{6,2},{1... | collective-permute-start | bytes 196616 | tf_op jit(solution)/shard_map/ppermute | solution.py:35
  56.6 0.6 collective-permute-done.17
  57.3 1.1 %collective-permute-start.18 = (bf16[16,2048]{1,0:T(8,128)(2,1)S(1)}, bf16[16,2048]{1,0:T(8,128)(2,1)S(1)}, u32[]{:S(2)}, u32[]{:S(2)}) collective-permute-start(bf16[16,2048]{1,0:T(8,128)(2,1)S(1)} %get-tuple-element.44), channel_id=1, source_target_pairs={{0,8},{4,12},{8,0},{12,4},{1,9},{5,13},{9,1},{13,5},{2,10},{6,14},... | collective-permute-start | bytes 196616 | tf_op jit(solution)/shard_map/ppermute | solution.py:35
  58.3 3.7 %collective-permute-start.19 = (bf16[16,2048]{1,0:T(8,128)(2,1)S(1)}, bf16[16,2048]{1,0:T(8,128)(2,1)S(1)}, u32[]{:S(2)}, u32[]{:S(2)}) collective-permute-start(bf16[16,2048]{1,0:T(8,128)(2,1)S(1)} %get-tuple-element.45), channel_id=1, source_target_pairs={{0,12},{4,8},{8,4},{12,0},{1,13},{5,9},{9,5},{13,1},{2,14},{6,10},... | collective-permute-start | bytes 196616 | tf_op jit(solution)/shard_map/ppermute | solution.py:35
  62.0 0.5 collective-permute-done.18
  62.5 2.4 %collective-permute-done.19 = bf16[16,2048]{1,0:T(8,128)(2,1)S(1)} collective-permute-done((bf16[16,2048]{1,0:T(8,128)(2,1)S(1)}, bf16[16,2048]{1,0:T(8,128)(2,1)S(1)}, u32[]{:S(2)}, u32[]{:S(2)}) %collective-permute-start.19) | collective-permute-done | bytes 65568 | tf_op jit(solution)/shard_map/ppermute | solution.py:35
  64.9 0.7 %fusion.24 = bf16[1,16,2048]{2,1,0:T(8,128)(2,1)} fusion(bf16[16,2048]{1,0:T(8,128)(2,1)S(1)} %collective-permute-done.20, bf16[16,2048]{1,0:T(8,128)(2,1)S(1)} %collective-permute-done.19, bf16[16,2048]{1,0:T(8,128)(2,1)S(1)} %collective-permute-done.18, f32[32,2048]{1,0:T(8,128)S(1)} %convert_add_fusion, bf16[16,2048]{1,0:T(8,128)(2,1)S(1)} %get-tuple-element.35), kind=kLoop, calls=%fused_computation.28 | loop fusion | flops 294912 | bytes 458752 | tf_op jit(solution)/shard_map/convert_element_type | solution.py:504
  (44 shorter events, 0.3 us)
Async XLA Ops:
  0.6 34.1 %collective-permute-start.8 = (bf16[1,2048,2,384]{3,2,1,0:T(2,128)(2,1)}, bf16[1,2048,2,384]{3,2,1,0:T(2,128)(2,1)S(1)}, u32[]{:S(2)}, u32[]{:S(2)}) collective-permute-start(bf16[1,2048,2,384]{3,2,1,0:T(2,128)(2,1)} %param.18), channel_id=1, source_target_pairs={{0,1},{1,0},{2,3},{3,2},{4,5},{5,4},{6,7},{7,6},{8,9},{9,8},{10,11... | collective-permute-start | bytes 9437192 | tf_op jit(solution)/shard_map/ppermute | solution.py:35
  2.2 8.9 %collective-permute-start.2 = (bf16[576,128]{1,0:T(8,128)(2,1)S(1)}, bf16[576,128]{1,0:T(8,128)(2,1)S(1)}, u32[]{:S(2)}, u32[]{:S(2)}) collective-permute-start(bf16[576,128]{1,0:T(8,128)(2,1)S(1)} %get-tuple-element.42.keys), channel_id=1, source_target_pairs={{0,12},{4,0},{8,4},{12,8},{1,13},{5,1},{9,5},{13,9},{2,14},{6,2},{... | collective-permute-start | bytes 442376 | tf_op jit(solution)/shard_map/ppermute | solution.py:40
  6.8 8.6 %collective-permute-start = (bf16[576,128]{1,0:T(8,128)(2,1)S(1)}, bf16[576,128]{1,0:T(8,128)(2,1)S(1)}, u32[]{:S(2)}, u32[]{:S(2)}) collective-permute-start(bf16[576,128]{1,0:T(8,128)(2,1)S(1)} %get-tuple-element.43.values), channel_id=1, source_target_pairs={{0,4},{4,8},{8,12},{12,0},{1,5},{5,9},{9,13},{13,1},{2,6},{6,10},{... | collective-permute-start | bytes 442376 | tf_op jit(solution)/shard_map/ppermute | solution.py:40
  6.8 14.9 %collective-permute-start.4 = (bf16[576,128]{1,0:T(8,128)(2,1)S(1)}, bf16[576,128]{1,0:T(8,128)(2,1)S(1)}, u32[]{:S(2)}, u32[]{:S(2)}) collective-permute-start(bf16[576,128]{1,0:T(8,128)(2,1)S(1)} %get-tuple-element.42.keys), channel_id=1, source_target_pairs={{0,4},{4,8},{8,12},{12,0},{1,5},{5,9},{9,13},{13,1},{2,6},{6,10},{... | collective-permute-start | bytes 442376 | tf_op jit(solution)/shard_map/ppermute | solution.py:40
  6.9 14.9 %collective-permute-start.5 = (bf16[576,128]{1,0:T(8,128)(2,1)S(1)}, bf16[576,128]{1,0:T(8,128)(2,1)S(1)}, u32[]{:S(2)}, u32[]{:S(2)}) collective-permute-start(bf16[576,128]{1,0:T(8,128)(2,1)S(1)} %get-tuple-element.43.values), channel_id=1, source_target_pairs={{0,12},{4,0},{8,4},{12,8},{1,13},{5,1},{9,5},{13,9},{2,14},{6,2},{... | collective-permute-start | bytes 442376 | tf_op jit(solution)/shard_map/ppermute | solution.py:40
  11.1 12.7 %collective-permute-start.3 = (bf16[576,128]{1,0:T(8,128)(2,1)S(1)}, bf16[576,128]{1,0:T(8,128)(2,1)S(1)}, u32[]{:S(2)}, u32[]{:S(2)}) collective-permute-start(bf16[576,128]{1,0:T(8,128)(2,1)S(1)} %collective-permute-done.2.refs_2_), channel_id=1, source_target_pairs={{0,12},{4,0},{8,4},{12,8},{1,13},{5,1},{9,5},{13,9},{2,14},{6,2},{... | collective-permute-start | bytes 442376 | tf_op jit(solution)/shard_map/ppermute | solution.py:40
  15.5 11.9 %collective-permute-start.1 = (bf16[576,128]{1,0:T(8,128)(2,1)S(1)}, bf16[576,128]{1,0:T(8,128)(2,1)S(1)}, u32[]{:S(2)}, u32[]{:S(2)}) collective-permute-start(bf16[576,128]{1,0:T(8,128)(2,1)S(1)} %collective-permute-done.refs_1_), channel_id=1, source_target_pairs={{0,4},{4,8},{8,12},{12,0},{1,5},{5,9},{9,13},{13,1},{2,6},{6,10},{... | collective-permute-start | bytes 442376 | tf_op jit(solution)/shard_map/ppermute | solution.py:40
  16.7 2.2 %copy-start.1 = (bf16[1024,2048]{1,0:T(8,128)(2,1)S(1)}, bf16[1024,2048]{1,0:T(8,128)(2,1)}, u32[]{:S(2)}) copy-start(bf16[1024,2048]{1,0:T(8,128)(2,1)} %weight.1) | copy-start | bytes 12582916
  18.9 0.9 %copy-start.7 = (bf16[1,64,1024]{2,1,0:T(8,128)(2,1)S(1)}, bf16[1,64,1024]{2,1,0:T(8,128)(2,1)}, u32[]{:S(2)}) copy-start(bf16[1,64,1024]{2,1,0:T(8,128)(2,1)} %param.10) | copy-start | bytes 393220
  19.8 0.7 copy-start.9
  20.4 1.3 %copy-start.8 = (bf16[1,64,1024]{2,1,0:T(8,128)(2,1)S(1)}, bf16[1,64,1024]{2,1,0:T(8,128)(2,1)}, u32[]{:S(2)}) copy-start(bf16[1,64,1024]{2,1,0:T(8,128)(2,1)} %param.10) | copy-start | bytes 393220
  20.4 6.9 %copy-start.2 = (bf16[1024,2048]{1,0:T(8,128)(2,1)S(1)}, bf16[1024,2048]{1,0:T(8,128)(2,1)}, u32[]{:S(2)}) copy-start(bf16[1024,2048]{1,0:T(8,128)(2,1)} %weight.1) | copy-start | bytes 12582916
  24.3 10.4 %copy-start.3 = (bf16[1,16,2048]{2,1,0:T(8,128)(2,1)S(1)}, bf16[1,16,2048]{2,1,0:T(8,128)(2,1)}, u32[]{:S(2)}) copy-start(bf16[1,16,2048]{2,1,0:T(8,128)(2,1)} %param.13) | copy-start | bytes 196612
  24.4 10.4 %copy-start.4 = (f32[2048]{0:T(1024)S(1)}, f32[2048]{0:T(1024)}, u32[]{:S(2)}) copy-start(f32[2048]{0:T(1024)} %param.15) | copy-start | bytes 24580
  24.4 10.4 %copy-start.5 = (s32[1,16,8]{1,2,0:T(8,128)S(1)}, s32[1,16,8]{1,2,0:T(8,128)}, u32[]{:S(2)}) copy-start(s32[1,16,8]{1,2,0:T(8,128)} %param.16) | copy-start | bytes 1540
  24.4 10.4 %copy-start.6 = (f32[1,16,8]{1,2,0:T(8,128)S(1)}, f32[1,16,8]{1,2,0:T(8,128)}, u32[]{:S(2)}) copy-start(f32[1,16,8]{1,2,0:T(8,128)} %param.17) | copy-start | bytes 1540
  29.0 7.7 %copy-start = (bf16[1,384,2048]{2,1,0:T(8,128)(2,1)S(1)}, bf16[1,384,2048]{2,1,0:T(8,128)(2,1)}, u32[]{:S(2)}) copy-start(bf16[1,384,2048]{2,1,0:T(8,128)(2,1)} %refs_2_.1) | copy-start | bytes 4718596
  29.0 1.3 %collective-permute-start.6 = (bf16[2,1,16,2048]{3,2,1,0:T(8,128)(2,1)S(1)}, bf16[2,1,16,2048]{3,2,1,0:T(8,128)(2,1)S(1)}, u32[]{:S(2)}, u32[]{:S(2)}) collective-permute-start(bf16[2,1,16,2048]{3,2,1,0:T(8,128)(2,1)S(1)} %bitcast.54), channel_id=1, source_target_pairs={{0,1},{1,0},{2,3},{3,2},{4,5},{5,4},{6,7},{7,6},{8,9},{9,8},{10,11... | collective-permute-start | bytes 393224 | tf_op jit(solution)/shard_map/ppermute | solution.py:35
  30.4 4.3 %collective-permute-start.7 = (bf16[1,1,16,2048]{3,2,1,0:T(8,128)(2,1)S(1)}, bf16[1,1,16,2048]{3,2,1,0:T(8,128)(2,1)S(1)}, u32[]{:S(2)}, u32[]{:S(2)}) collective-permute-start(bf16[1,1,16,2048]{3,2,1,0:T(8,128)(2,1)S(1)} %slice.79), channel_id=1, source_target_pairs={{0,2},{1,3},{2,0},{3,1},{4,6},{5,7},{6,4},{7,5},{8,10},{9,11},{10,... | collective-permute-start | bytes 196616 | tf_op jit(solution)/shard_map/ppermute | solution.py:35
  34.8 13.1 %copy-start.10 = (bf16[1,2048,2,384]{3,2,1,0:T(2,128)(2,1)S(1)}, bf16[1,2048,2,384]{3,2,1,0:T(2,128)(2,1)}, u32[]{:S(2)}) copy-start(bf16[1,2048,2,384]{3,2,1,0:T(2,128)(2,1)} %param.18) | copy-start | bytes 9437188
  35.1 4.4 %collective-permute-start.11 = (bf16[16,2176]{1,0:T(8,128)(2,1)S(1)}, bf16[16,2176]{1,0:T(8,128)(2,1)S(1)}, u32[]{:S(2)}, u32[]{:S(2)}) collective-permute-start(bf16[16,2176]{1,0:T(8,128)(2,1)S(1)} %get-tuple-element.36), channel_id=1, source_target_pairs={{0,4},{4,0},{8,12},{12,8},{1,5},{5,1},{9,13},{13,9},{2,6},{6,2},{1... | collective-permute-start | bytes 208904 | tf_op jit(solution)/shard_map/ppermute | solution.py:35
  36.8 11.8 %collective-permute-start.15 = (bf16[1,384,2048]{2,1,0:T(8,128)(2,1)S(1)}, bf16[1,384,2048]{2,1,0:T(8,128)(2,1)S(1)}, u32[]{:S(2)}, u32[]{:S(2)}) collective-permute-start(bf16[1,384,2048]{2,1,0:T(8,128)(2,1)S(1)} %copy-done), channel_id=1, source_target_pairs={{0,1},{1,0},{2,3},{3,2},{4,5},{5,4},{6,7},{7,6},{8,9},{9,8},{10,11... | collective-permute-start | bytes 4718600 | tf_op jit(solution)/shard_map/ppermute | solution.py:35
  36.8 6.9 %collective-permute-start.10 = (bf16[16,2176]{1,0:T(8,128)(2,1)S(1)}, bf16[16,2176]{1,0:T(8,128)(2,1)S(1)}, u32[]{:S(2)}, u32[]{:S(2)}) collective-permute-start(bf16[16,2176]{1,0:T(8,128)(2,1)S(1)} %get-tuple-element.36), channel_id=1, source_target_pairs={{0,12},{4,8},{8,4},{12,0},{1,13},{5,9},{9,5},{13,1},{2,14},{6,10},... | collective-permute-start | bytes 208904 | tf_op jit(solution)/shard_map/ppermute | solution.py:35
  37.3 8.4 %collective-permute-start.9 = (bf16[16,2176]{1,0:T(8,128)(2,1)S(1)}, bf16[16,2176]{1,0:T(8,128)(2,1)S(1)}, u32[]{:S(2)}, u32[]{:S(2)}) collective-permute-start(bf16[16,2176]{1,0:T(8,128)(2,1)S(1)} %get-tuple-element.36), channel_id=1, source_target_pairs={{0,8},{4,12},{8,0},{12,4},{1,9},{5,13},{9,1},{13,5},{2,10},{6,14},... | collective-permute-start | bytes 208904 | tf_op jit(solution)/shard_map/ppermute | solution.py:35
  39.5 6.3 %collective-permute-start.12 = (bf16[32,2176]{1,0:T(8,128)(2,1)S(1)}, bf16[32,2176]{1,0:T(8,128)(2,1)S(1)}, u32[]{:S(2)}, u32[]{:S(2)}) collective-permute-start(bf16[32,2176]{1,0:T(8,128)(2,1)S(1)} %pad_maximum_fusion), channel_id=1, source_target_pairs={{0,2},{1,3},{2,0},{3,1},{4,6},{5,7},{6,4},{7,5},{8,10},{9,11},{10,... | collective-permute-start | bytes 417800 | tf_op jit(solution)/shard_map/ppermute | solution.py:35
  43.6 6.5 %collective-permute-start.14 = (bf16[16,2176]{1,0:T(8,128)(2,1)S(1)}, bf16[16,2176]{1,0:T(8,128)(2,1)S(1)}, u32[]{:S(2)}, u32[]{:S(2)}) collective-permute-start(bf16[16,2176]{1,0:T(8,128)(2,1)S(1)} %collective-permute-done.10), channel_id=1, source_target_pairs={{0,2},{1,3},{2,0},{3,1},{4,6},{5,7},{6,4},{7,5},{8,10},{9,11},{10,... | collective-permute-start | bytes 208904 | tf_op jit(solution)/shard_map/ppermute | solution.py:35
  45.7 4.4 %collective-permute-start.13 = (bf16[16,2176]{1,0:T(8,128)(2,1)S(1)}, bf16[16,2176]{1,0:T(8,128)(2,1)S(1)}, u32[]{:S(2)}, u32[]{:S(2)}) collective-permute-start(bf16[16,2176]{1,0:T(8,128)(2,1)S(1)} %collective-permute-done.9), channel_id=1, source_target_pairs={{0,2},{1,3},{2,0},{3,1},{4,6},{5,7},{6,4},{7,5},{8,10},{9,11},{10,... | collective-permute-start | bytes 208904 | tf_op jit(solution)/shard_map/ppermute | solution.py:35
  49.3 5.7 %collective-permute-start.16 = (bf16[32,2048]{1,0:T(8,128)(2,1)S(1)}, bf16[32,2048]{1,0:T(8,128)(2,1)S(1)}, u32[]{:S(2)}, u32[]{:S(2)}) collective-permute-start(bf16[32,2048]{1,0:T(8,128)(2,1)S(1)} %shard_map.119), channel_id=1, source_target_pairs={{0,2},{1,3},{2,0},{3,1},{4,6},{5,7},{6,4},{7,5},{8,10},{9,11},{10,... | collective-permute-start | bytes 393224 | tf_op jit(solution)/shard_map/ppermute | solution.py:35
  52.2 5.0 %collective-permute-start.17 = (bf16[32,2048]{1,0:T(8,128)(2,1)S(1)}, bf16[32,2048]{1,0:T(8,128)(2,1)S(1)}, u32[]{:S(2)}, u32[]{:S(2)}) collective-permute-start(bf16[32,2048]{1,0:T(8,128)(2,1)S(1)} %get-tuple-element.41), channel_id=1, source_target_pairs={{0,2},{1,3},{2,0},{3,1},{4,6},{5,7},{6,4},{7,5},{8,10},{9,11},{10,... | collective-permute-start | bytes 393224 | tf_op jit(solution)/shard_map/ppermute | solution.py:35
  55.0 7.0 %collective-permute-start.20 = (bf16[16,2048]{1,0:T(8,128)(2,1)S(1)}, bf16[16,2048]{1,0:T(8,128)(2,1)S(1)}, u32[]{:S(2)}, u32[]{:S(2)}) collective-permute-start(bf16[16,2048]{1,0:T(8,128)(2,1)S(1)} %slice.78), channel_id=1, source_target_pairs={{0,4},{4,0},{8,12},{12,8},{1,5},{5,1},{9,13},{13,9},{2,6},{6,2},{1... | collective-permute-start | bytes 196616 | tf_op jit(solution)/shard_map/ppermute | solution.py:35
  57.3 5.2 %collective-permute-start.18 = (bf16[16,2048]{1,0:T(8,128)(2,1)S(1)}, bf16[16,2048]{1,0:T(8,128)(2,1)S(1)}, u32[]{:S(2)}, u32[]{:S(2)}) collective-permute-start(bf16[16,2048]{1,0:T(8,128)(2,1)S(1)} %get-tuple-element.44), channel_id=1, source_target_pairs={{0,8},{4,12},{8,0},{12,4},{1,9},{5,13},{9,1},{13,5},{2,10},{6,14},... | collective-permute-start | bytes 196616 | tf_op jit(solution)/shard_map/ppermute | solution.py:35
  58.3 6.6 %collective-permute-start.19 = (bf16[16,2048]{1,0:T(8,128)(2,1)S(1)}, bf16[16,2048]{1,0:T(8,128)(2,1)S(1)}, u32[]{:S(2)}, u32[]{:S(2)}) collective-permute-start(bf16[16,2048]{1,0:T(8,128)(2,1)S(1)} %get-tuple-element.45), channel_id=1, source_target_pairs={{0,12},{4,8},{8,4},{12,0},{1,13},{5,9},{9,5},{13,1},{2,14},{6,10},... | collective-permute-start | bytes 196616 | tf_op jit(solution)/shard_map/ppermute | solution.py:35

commit v16 on v14

--- a/solution.py
+++ b/solution.py
@@ -209,14 +209,15 @@
     left_keys, left_values = own_keys, own_values
     right_keys, right_values = own_keys, own_values
     for step in range(1, (count - 1) // 2 + 1):
+        left_keys = shift(left_keys, "ctx", 1)
+        right_values = shift(right_values, "ctx", -1)
+        left_values = shift(left_values, "ctx", 1)
+        right_keys, _ = lax.optimization_barrier((right_keys, left_keys))
         right_keys = shift(right_keys, "ctx", -1)
-        left_values = shift(left_values, "ctx", 1)
-        right_values = shift(right_values, "ctx", -1)
-        left_keys = shift(left_keys, "ctx", 1)
         held.append((count - step, left_keys, left_values))
         held.append((step, right_keys, right_values))
     if count % 2 == 0:
-        last = (count // 2, shift(right_keys, "ctx", -1), shift(left_values, "ctx", 1))
+        last = (count // 2, shift(left_keys, "ctx", 1), shift(right_values, "ctx", -1))
     else:
         last = held.pop()
     page_flops = 4 * rows * pages.shape[0] * HEAD

time: 65.3 us -> 65.8 us (level)
  waiting for transfers between devices: 21.4 us -> 22.7 us
  starting transfers between devices: 27.8 us -> 27 us
    ppermute x6, waiting for transfers between devices: 3.97 us -> 4.69 us  [shift(): lax.ppermute(value, axis, [(i, (i + step) % count) for i in range(count)])]
  transfers between devices with their start and end apart: 20 -> 20, of which waited for: 13 -> 10; matrix products, arithmetic and copies ran while one was open for 6% -> 6% of each run, Pallas kernels for 10% -> 10%
where the time goes in v16:
time: 65.8 us; the launch traced here: 65.6 us
  starting transfers between devices  27 us (41%)
  waiting for transfers between devices  22.7 us (34%)
  Pallas kernels  6.7 us (10%)
  local copies, waits for them, and re-layouts  4.91 us (7%)
  matrix products  2.61 us (4%)
  between operations  0.9 us (1%)
  other arithmetic  0.78 us (1%)
    ppermute x14, waiting for transfers between devices, swap(): lax.ppermute(value, axis, [(i, i ^ stride) for i in range(lax.axis_size(a...  18 us
    ppermute x6, starting transfers between devices, shift(): lax.ppermute(value, axis, [(i, (i + step) % count) for i in range(count)])  13.6 us
    ppermute x14, starting transfers between devices, swap(): lax.ppermute(value, axis, [(i, i ^ stride) for i in range(lax.axis_size(a...  13.4 us
    unnamed x27, local copies, waits for them, and re-layouts  4.83 us
    ppermute x6, waiting for transfers between devices, shift(): lax.ppermute(value, axis, [(i, (i + step) % count) for i in range(count)])  4.69 us
    dot_general x4, matrix products, expert_apply(): jnp.einsum('nd,dgh->gnh', rows[:, :width], gate_up[0], preferred_element_...  2.61 us
    pallas_call x1, Pallas kernels, attention(): pl.pallas_call(functools.partial(late_kernel, fresh_block), out_shape=sha...  1.68 us
    pallas_call x2, Pallas kernels, expert_apply(): pl.pallas_call(functools.partial(down_kernel, [offset for offset, _, _ in...  1.43 us
  transfers between devices with their start and end apart: 20, of which 10 were waited for; matrix products, arithmetic and copies ran while one was open for 6% of the time, Pallas kernels for 10%

profile of v16, /device:TPU:0, one launch (start us, length us, event | category | flops | bytes accessed | tf_op | source)
XLA Modules:
  0.0 65.6 jit_solution(5132555089462875216)
XLA Ops:
  0.6 0.5 collective-permute-start.8
  1.1 1.0 %copy.34 = bf16[1,576,2,128]{3,1,2,0:T(8,128)(2,1)S(1)} copy(bf16[1,576,2,128]{3,2,1,0:T(2,128)(2,1)} %param.11) | data formatting | bytes 589824 | tf_op args[1]
  2.2 2.6 %collective-permute-start.2 = (bf16[576,128]{1,0:T(8,128)(2,1)S(1)}, bf16[576,128]{1,0:T(8,128)(2,1)S(1)}, u32[]{:S(2)}, u32[]{:S(2)}) collective-permute-start(bf16[576,128]{1,0:T(8,128)(2,1)S(1)} %get-tuple-element.26.keys), channel_id=1, source_target_pairs={{0,4},{4,8},{8,12},{12,0},{1,5},{5,9},{9,13},{13,1},{2,6},{6,10},{... | collective-permute-start | bytes 442376 | tf_op jit(solution)/shard_map/ppermute | solution.py:40
  4.8 2.1 %collective-permute-start = (bf16[576,128]{1,0:T(8,128)(2,1)S(1)}, bf16[576,128]{1,0:T(8,128)(2,1)S(1)}, u32[]{:S(2)}, u32[]{:S(2)}) collective-permute-start(bf16[576,128]{1,0:T(8,128)(2,1)S(1)} %get-tuple-element.43.values), channel_id=1, source_target_pairs={{0,12},{4,0},{8,4},{12,8},{1,13},{5,1},{9,5},{13,9},{2,14},{6,2},{... | collective-permute-start | bytes 442376 | tf_op jit(solution)/shard_map/ppermute | solution.py:40
  6.9 4.7 %collective-permute-done.2.refs_0_ = bf16[576,128]{1,0:T(8,128)(2,1)S(1)} collective-permute-done((bf16[576,128]{1,0:T(8,128)(2,1)S(1)}, bf16[576,128]{1,0:T(8,128)(2,1)S(1)}, u32[]{:S(2)}, u32[]{:S(2)}) %collective-permute-start.2) | collective-permute-done | bytes 147488 | tf_op jit(solution)/shard_map/ppermute | solution.py:40
  11.6 5.1 %collective-permute-start.5 = (bf16[576,128]{1,0:T(8,128)(2,1)S(1)}, bf16[576,128]{1,0:T(8,128)(2,1)S(1)}, u32[]{:S(2)}, u32[]{:S(2)}) collective-permute-start(bf16[576,128]{1,0:T(8,128)(2,1)S(1)} %get-tuple-element.26.keys), channel_id=1, source_target_pairs={{0,12},{4,0},{8,4},{12,8},{1,13},{5,1},{9,5},{13,9},{2,14},{6,2},{... | collective-permute-start | bytes 442376 | tf_op jit(solution)/shard_map/ppermute | solution.py:40
  16.7 3.8 %collective-permute-start.1 = (bf16[576,128]{1,0:T(8,128)(2,1)S(1)}, bf16[576,128]{1,0:T(8,128)(2,1)S(1)}, u32[]{:S(2)}, u32[]{:S(2)}) collective-permute-start(bf16[576,128]{1,0:T(8,128)(2,1)S(1)} %collective-permute-done.refs_3_), channel_id=1, source_target_pairs={{0,12},{4,0},{8,4},{12,8},{1,13},{5,1},{9,5},{13,9},{2,14},{6,2},{... | collective-permute-start | bytes 442376 | tf_op jit(solution)/shard_map/ppermute | solution.py:40
  20.5 2.2 %copy-done.1 = bf16[1024,2048]{1,0:T(8,128)(2,1)S(1)} copy-done((bf16[1024,2048]{1,0:T(8,128)(2,1)S(1)}, bf16[1024,2048]{1,0:T(8,128)(2,1)}, u32[]{:S(2)}) %copy-start.1) | copy-done | bytes 4194328
  22.7 0.9 %copy-done.7 = bf16[1,64,1024]{2,1,0:T(8,128)(2,1)S(1)} copy-done((bf16[1,64,1024]{2,1,0:T(8,128)(2,1)S(1)}, bf16[1,64,1024]{2,1,0:T(8,128)(2,1)}, u32[]{:S(2)}) %copy-start.7) | copy-done | bytes 131096
  23.6 0.7 copy-done.9
  24.2 1.3 %shard_map.113 = (f32[1,512]{1,0:T(1,128)S(1)}, f32[1,512]{1,0:T(1,128)S(1)}, f32[128,512]{1,0:T(8,128)S(1)}, s32[4,128]{1,0:T(4,128)S(1)}) custom-call(s32[4]{0:T(128)S(1)} %bitcast.55, bf16[64,1024]{1,0:T(8,128)(2,1)S(1)} %bitcast.51, bf16[576,128]{1,0:T(8,128)(2,1)S(1)} %get-tuple-element.26.keys, bf16[576,128]{1,0:T(8,128)(2,1)S(1)} %get-tuple-element.43.values, ...), custom_call_target="tpu_custom_call" | custom-call | flops 2415919104 | bytes 8388608 | tf_op jit(solution)/shard_map/pallas_call | solution.py:226
  25.6 0.6 shard_map.114
  26.2 1.4 %shard_map.115 = (f32[1,512]{1,0:T(1,128)S(1)}, f32[1,512]{1,0:T(1,128)S(1)}, f32[128,512]{1,0:T(8,128)S(1)}) custom-call(bf16[64,1024]{1,0:T(8,128)(2,1)S(1)} %bitcast.53, s32[4,128]{1,0:T(4,128)S(1)} %get-tuple-element.22.lengths, bf16[576,128]{1,0:T(8,128)(2,1)S(1)} %collective-permute-done.2.refs_0_, ...), custom_call_target="tpu_custom_call" | custom-call | flops 301989888 | bytes 2097152 | tf_op jit(solution)/shard_map/pallas_call | solution.py:241
  27.6 0.0 copy-start.3
  27.6 0.0 copy-start.4
  27.7 0.0 copy-start.5
  27.7 0.0 copy-start.6
  27.7 1.7 %shard_map.116 = (bf16[64,1024]{1,0:T(8,128)(2,1)}, f32[32,2048]{1,0:T(8,128)S(1)}, bf16[32,2048]{1,0:T(8,128)(2,1)S(1)}) custom-call(bf16[576,128]{1,0:T(8,128)(2,1)S(1)} %collective-permute-done.1.values, f32[1,512]{1,0:T(1,128)S(1)} %get-tuple-element.23.last_peak, f32[1,512]{1,0:T(1,128)S(1)} %get-tuple-element.24.last_total, ...), custom_call_target="tpu_custom_call" | custom-call | flops 419430400 | bytes 6291456 | tf_op jit(solution)/shard_map/pallas_call | solution.py:268
  29.4 1.3 %collective-permute-done.6 = bf16[2,1,16,2048]{3,2,1,0:T(8,128)(2,1)S(1)} collective-permute-done((bf16[2,1,16,2048]{3,2,1,0:T(8,128)(2,1)S(1)}, bf16[2,1,16,2048]{3,2,1,0:T(8,128)(2,1)S(1)}, u32[]{:S(2)}, u32[]{:S(2)}) %collective-permute-start.6) | collective-permute-done | bytes 131104 | tf_op jit(solution)/shard_map/ppermute | solution.py:35
  30.8 1.6 %collective-permute-start.7 = (bf16[1,1,16,2048]{3,2,1,0:T(8,128)(2,1)S(1)}, bf16[1,1,16,2048]{3,2,1,0:T(8,128)(2,1)S(1)}, u32[]{:S(2)}, u32[]{:S(2)}) collective-permute-start(bf16[1,1,16,2048]{3,2,1,0:T(8,128)(2,1)S(1)} %slice.79), channel_id=1, source_target_pairs={{0,2},{1,3},{2,0},{3,1},{4,6},{5,7},{6,4},{7,5},{8,10},{9,11},{10,... | collective-permute-start | bytes 196616 | tf_op jit(solution)/shard_map/ppermute | solution.py:35
  32.4 2.8 %collective-permute-done.7 = bf16[1,1,16,2048]{3,2,1,0:T(8,128)(2,1)S(1)} collective-permute-done((bf16[1,1,16,2048]{3,2,1,0:T(8,128)(2,1)S(1)}, bf16[1,1,16,2048]{3,2,1,0:T(8,128)(2,1)S(1)}, u32[]{:S(2)}, u32[]{:S(2)}) %collective-permute-start.7) | collective-permute-done | bytes 65568 | tf_op jit(solution)/shard_map/ppermute | solution.py:35
  35.1 0.2 shard_map.117
  35.4 0.0 copy-start.10
  35.4 0.1 collective-permute-start.11
  35.5 0.1 collective-permute-start.13
  35.6 2.1 %collective-permute-start.10 = (bf16[16,2176]{1,0:T(8,128)(2,1)S(1)}, bf16[16,2176]{1,0:T(8,128)(2,1)S(1)}, u32[]{:S(2)}, u32[]{:S(2)}) collective-permute-start(bf16[16,2176]{1,0:T(8,128)(2,1)S(1)} %get-tuple-element.37), channel_id=1, source_target_pairs={{0,12},{4,8},{8,4},{12,0},{1,13},{5,9},{9,5},{13,1},{2,14},{6,10},... | collective-permute-start | bytes 208904 | tf_op jit(solution)/shard_map/ppermute | solution.py:35
  37.7 1.3 %collective-permute-start.9 = (bf16[16,2176]{1,0:T(8,128)(2,1)S(1)}, bf16[16,2176]{1,0:T(8,128)(2,1)S(1)}, u32[]{:S(2)}, u32[]{:S(2)}) collective-permute-start(bf16[16,2176]{1,0:T(8,128)(2,1)S(1)} %get-tuple-element.37), channel_id=1, source_target_pairs={{0,8},{4,12},{8,0},{12,4},{1,9},{5,13},{9,1},{13,5},{2,10},{6,14},... | collective-permute-start | bytes 208904 | tf_op jit(solution)/shard_map/ppermute | solution.py:35
  39.0 0.8 %collective-permute-done.11 = bf16[16,2176]{1,0:T(8,128)(2,1)S(1)} collective-permute-done((bf16[16,2176]{1,0:T(8,128)(2,1)S(1)}, bf16[16,2176]{1,0:T(8,128)(2,1)S(1)}, u32[]{:S(2)}, u32[]{:S(2)}) %collective-permute-start.11) | collective-permute-done | bytes 69664 | tf_op jit(solution)/shard_map/ppermute | solution.py:35
  39.8 1.6 %collective-permute-start.14 = (bf16[32,2176]{1,0:T(8,128)(2,1)S(1)}, bf16[32,2176]{1,0:T(8,128)(2,1)S(1)}, u32[]{:S(2)}, u32[]{:S(2)}) collective-permute-start(bf16[32,2176]{1,0:T(8,128)(2,1)S(1)} %pad_maximum_fusion.1), channel_id=1, source_target_pairs={{0,2},{1,3},{2,0},{3,1},{4,6},{5,7},{6,4},{7,5},{8,10},{9,11},{10,... | collective-permute-start | bytes 417800 | tf_op jit(solution)/shard_map/ppermute | solution.py:35
  41.3 1.2 %collective-permute-done.10 = bf16[16,2176]{1,0:T(8,128)(2,1)S(1)} collective-permute-done((bf16[16,2176]{1,0:T(8,128)(2,1)S(1)}, bf16[16,2176]{1,0:T(8,128)(2,1)S(1)}, u32[]{:S(2)}, u32[]{:S(2)}) %collective-permute-start.10) | collective-permute-done | bytes 69664 | tf_op jit(solution)/shard_map/ppermute | solution.py:35
  42.5 3.5 %collective-permute-done.9 = bf16[16,2176]{1,0:T(8,128)(2,1)S(1)} collective-permute-done((bf16[16,2176]{1,0:T(8,128)(2,1)S(1)}, bf16[16,2176]{1,0:T(8,128)(2,1)S(1)}, u32[]{:S(2)}, u32[]{:S(2)}) %collective-permute-start.9) | collective-permute-done | bytes 69664 | tf_op jit(solution)/shard_map/ppermute | solution.py:35
  46.0 1.6 %collective-permute-start.12 = (bf16[32,2176]{1,0:T(8,128)(2,1)S(1)}, bf16[32,2176]{1,0:T(8,128)(2,1)S(1)}, u32[]{:S(2)}, u32[]{:S(2)}) collective-permute-start(bf16[32,2176]{1,0:T(8,128)(2,1)S(1)} %pad_maximum_fusion), channel_id=1, source_target_pairs={{0,2},{1,3},{2,0},{3,1},{4,6},{5,7},{6,4},{7,5},{8,10},{9,11},{10,... | collective-permute-start | bytes 417800 | tf_op jit(solution)/shard_map/ppermute | solution.py:35
  47.6 0.6 fusion.17.refs_1_
  48.3 0.7 %fusion.14.refs_0_ = f32[2,32,384]{2,1,0:T(8,128)S(1)} fusion(bf16[2048,2,384]{2,1,0:T(2,128)(2,1)S(1)} %bitcast.57, bf16[32,2176]{1,0:T(8,128)(2,1)S(1)} %collective-permute-done.14.rows), kind=kOutput, calls=%fused_computation.10 | convolution fusion | flops 100663296 | bytes 3375104 | tf_op jit(solution)/shard_map/nd,dgh->gnh/dot_general | solution.py:353
  48.9 0.7 %shard_map.119 = bf16[32,2048]{1,0:T(8,128)(2,1)S(1)} custom-call(bf16[32,2176]{1,0:T(8,128)(2,1)S(1)} %collective-permute-done.14.rows, f32[2,32,384]{2,1,0:T(8,128)S(1)} %fusion.14.refs_0_, f32[2,32,384]{2,1,0:T(8,128)S(1)} %fusion.17.refs_1_, bf16[1,384,2048]{2,1,0:T(8,128)(2,1)S(1)} %copy-done, bf16[1,384,2048]{2,1,0:T(8,128)(2,1)S(1)} %collective-permute-done.13.refs_3_), custom_call_target="tpu_custom_call" | custom-call | flops 100663296 | bytes 2097152 | tf_op jit(solution)/shard_map/pallas_call | solution.py:357
  49.6 0.6 collective-permute-start.15
  50.2 1.2 %collective-permute-done.12 = bf16[32,2176]{1,0:T(8,128)(2,1)S(1)} collective-permute-done((bf16[32,2176]{1,0:T(8,128)(2,1)S(1)}, bf16[32,2176]{1,0:T(8,128)(2,1)S(1)}, u32[]{:S(2)}, u32[]{:S(2)}) %collective-permute-start.12) | collective-permute-done | bytes 139296 | tf_op jit(solution)/shard_map/ppermute | solution.py:35
  51.4 0.6 fusion.11.refs_1_
  52.1 0.7 fusion.8.refs_0_
  52.7 0.8 %shard_map.118 = (f32[32,2048]{1,0:T(8,128)S(1)}, f32[32,2048]{1,0:T(8,128)S(1)}, bf16[32,2048]{1,0:T(8,128)(2,1)S(1)}) custom-call(bf16[96,2176]{1,0:T(8,128)(2,1)S(1)} %constant_dynamic-update-slice_fusion.rows, f32[2,96,384]{2,1,0:T(8,128)S(1)} %fusion.8.refs_0_, f32[2,96,384]{2,1,0:T(8,128)S(1)} %fusion.11.refs_1_, bf16[1,384,2048]{2,1,0:T(8,128)(2,1)S(1)} %copy-done, ...), custom_call_target="tpu_custom_call" | custom-call | flops 301989888 | bytes 2097152 | tf_op jit(solution)/shard_map/pallas_call | solution.py:357
  53.5 2.1 %collective-permute-start.16 = (bf16[32,2048]{1,0:T(8,128)(2,1)S(1)}, bf16[32,2048]{1,0:T(8,128)(2,1)S(1)}, u32[]{:S(2)}, u32[]{:S(2)}) collective-permute-start(bf16[32,2048]{1,0:T(8,128)(2,1)S(1)} %get-tuple-element.41), channel_id=1, source_target_pairs={{0,2},{1,3},{2,0},{3,1},{4,6},{5,7},{6,4},{7,5},{8,10},{9,11},{10,... | collective-permute-start | bytes 393224 | tf_op jit(solution)/shard_map/ppermute | solution.py:35
  55.7 0.1 collective-permute-start.19
  55.8 2.8 %collective-permute-done.16 = bf16[32,2048]{1,0:T(8,128)(2,1)S(1)} collective-permute-done((bf16[32,2048]{1,0:T(8,128)(2,1)S(1)}, bf16[32,2048]{1,0:T(8,128)(2,1)S(1)}, u32[]{:S(2)}, u32[]{:S(2)}) %collective-permute-start.16) | collective-permute-done | bytes 131104 | tf_op jit(solution)/shard_map/ppermute | solution.py:35
  58.6 0.1 collective-permute-start.17
  58.7 1.8 %collective-permute-start.18 = (bf16[16,2048]{1,0:T(8,128)(2,1)S(1)}, bf16[16,2048]{1,0:T(8,128)(2,1)S(1)}, u32[]{:S(2)}, u32[]{:S(2)}) collective-permute-start(bf16[16,2048]{1,0:T(8,128)(2,1)S(1)} %get-tuple-element.45), channel_id=1, source_target_pairs={{0,12},{4,8},{8,4},{12,0},{1,13},{5,9},{9,5},{13,1},{2,14},{6,10},... | collective-permute-start | bytes 196616 | tf_op jit(solution)/shard_map/ppermute | solution.py:35
  60.5 3.3 %collective-permute-done.17 = bf16[16,2048]{1,0:T(8,128)(2,1)S(1)} collective-permute-done((bf16[16,2048]{1,0:T(8,128)(2,1)S(1)}, bf16[16,2048]{1,0:T(8,128)(2,1)S(1)}, u32[]{:S(2)}, u32[]{:S(2)}) %collective-permute-start.17) | collective-permute-done | bytes 65568 | tf_op jit(solution)/shard_map/ppermute | solution.py:35
  63.9 1.1 %collective-permute-done.18 = bf16[16,2048]{1,0:T(8,128)(2,1)S(1)} collective-permute-done((bf16[16,2048]{1,0:T(8,128)(2,1)S(1)}, bf16[16,2048]{1,0:T(8,128)(2,1)S(1)}, u32[]{:S(2)}, u32[]{:S(2)}) %collective-permute-start.18) | collective-permute-done | bytes 65568 | tf_op jit(solution)/shard_map/ppermute | solution.py:35
  64.9 0.7 %fusion.24 = bf16[1,16,2048]{2,1,0:T(8,128)(2,1)} fusion(bf16[16,2048]{1,0:T(8,128)(2,1)S(1)} %collective-permute-done.19, bf16[16,2048]{1,0:T(8,128)(2,1)S(1)} %collective-permute-done.18, bf16[16,2048]{1,0:T(8,128)(2,1)S(1)} %collective-permute-done.17, f32[32,2048]{1,0:T(8,128)S(1)} %convert_add_fusion, bf16[16,2048]{1,0:T(8,128)(2,1)S(1)} %get-tuple-element.36), kind=kLoop, calls=%fused_computation.29 | loop fusion | flops 294912 | bytes 458752 | tf_op jit(solution)/shard_map/convert_element_type | solution.py:502
  (42 shorter events, 0.3 us)
Async XLA Ops:
  0.6 34.5 %collective-permute-start.8 = (bf16[1,2048,2,384]{3,2,1,0:T(2,128)(2,1)}, bf16[1,2048,2,384]{3,2,1,0:T(2,128)(2,1)S(1)}, u32[]{:S(2)}, u32[]{:S(2)}) collective-permute-start(bf16[1,2048,2,384]{3,2,1,0:T(2,128)(2,1)} %param.18), channel_id=1, source_target_pairs={{0,1},{1,0},{2,3},{3,2},{4,5},{5,4},{6,7},{7,6},{8,9},{9,8},{10,11... | collective-permute-start | bytes 9437192 | tf_op jit(solution)/shard_map/ppermute | solution.py:35
  2.2 9.4 %collective-permute-start.2 = (bf16[576,128]{1,0:T(8,128)(2,1)S(1)}, bf16[576,128]{1,0:T(8,128)(2,1)S(1)}, u32[]{:S(2)}, u32[]{:S(2)}) collective-permute-start(bf16[576,128]{1,0:T(8,128)(2,1)S(1)} %get-tuple-element.26.keys), channel_id=1, source_target_pairs={{0,4},{4,8},{8,12},{12,0},{1,5},{5,9},{9,13},{13,1},{2,6},{6,10},{... | collective-permute-start | bytes 442376 | tf_op jit(solution)/shard_map/ppermute | solution.py:40
  4.8 11.8 %collective-permute-start = (bf16[576,128]{1,0:T(8,128)(2,1)S(1)}, bf16[576,128]{1,0:T(8,128)(2,1)S(1)}, u32[]{:S(2)}, u32[]{:S(2)}) collective-permute-start(bf16[576,128]{1,0:T(8,128)(2,1)S(1)} %get-tuple-element.43.values), channel_id=1, source_target_pairs={{0,12},{4,0},{8,4},{12,8},{1,13},{5,1},{9,5},{13,9},{2,14},{6,2},{... | collective-permute-start | bytes 442376 | tf_op jit(solution)/shard_map/ppermute | solution.py:40
  6.9 19.3 %collective-permute-start.4 = (bf16[576,128]{1,0:T(8,128)(2,1)S(1)}, bf16[576,128]{1,0:T(8,128)(2,1)S(1)}, u32[]{:S(2)}, u32[]{:S(2)}) collective-permute-start(bf16[576,128]{1,0:T(8,128)(2,1)S(1)} %get-tuple-element.43.values), channel_id=1, source_target_pairs={{0,4},{4,8},{8,12},{12,0},{1,5},{5,9},{9,13},{13,1},{2,6},{6,10},{... | collective-permute-start | bytes 442376 | tf_op jit(solution)/shard_map/ppermute | solution.py:40
  11.6 14.6 %collective-permute-start.5 = (bf16[576,128]{1,0:T(8,128)(2,1)S(1)}, bf16[576,128]{1,0:T(8,128)(2,1)S(1)}, u32[]{:S(2)}, u32[]{:S(2)}) collective-permute-start(bf16[576,128]{1,0:T(8,128)(2,1)S(1)} %get-tuple-element.26.keys), channel_id=1, source_target_pairs={{0,12},{4,0},{8,4},{12,8},{1,13},{5,1},{9,5},{13,9},{2,14},{6,2},{... | collective-permute-start | bytes 442376 | tf_op jit(solution)/shard_map/ppermute | solution.py:40
  16.6 8.9 %collective-permute-start.3 = (bf16[576,128]{1,0:T(8,128)(2,1)S(1)}, bf16[576,128]{1,0:T(8,128)(2,1)S(1)}, u32[]{:S(2)}, u32[]{:S(2)}) collective-permute-start(bf16[576,128]{1,0:T(8,128)(2,1)S(1)} %collective-permute-done.2.refs_0_), channel_id=1, source_target_pairs={{0,4},{4,8},{8,12},{12,0},{1,5},{5,9},{9,13},{13,1},{2,6},{6,10},{... | collective-permute-start | bytes 442376 | tf_op jit(solution)/shard_map/ppermute | solution.py:40
  16.7 11.0 %collective-permute-start.1 = (bf16[576,128]{1,0:T(8,128)(2,1)S(1)}, bf16[576,128]{1,0:T(8,128)(2,1)S(1)}, u32[]{:S(2)}, u32[]{:S(2)}) collective-permute-start(bf16[576,128]{1,0:T(8,128)(2,1)S(1)} %collective-permute-done.refs_3_), channel_id=1, source_target_pairs={{0,12},{4,0},{8,4},{12,8},{1,13},{5,1},{9,5},{13,9},{2,14},{6,2},{... | collective-permute-start | bytes 442376 | tf_op jit(solution)/shard_map/ppermute | solution.py:40
  20.5 2.2 %copy-start.1 = (bf16[1024,2048]{1,0:T(8,128)(2,1)S(1)}, bf16[1024,2048]{1,0:T(8,128)(2,1)}, u32[]{:S(2)}) copy-start(bf16[1024,2048]{1,0:T(8,128)(2,1)} %weight.1) | copy-start | bytes 12582916
  22.7 0.9 %copy-start.7 = (bf16[1,64,1024]{2,1,0:T(8,128)(2,1)S(1)}, bf16[1,64,1024]{2,1,0:T(8,128)(2,1)}, u32[]{:S(2)}) copy-start(bf16[1,64,1024]{2,1,0:T(8,128)(2,1)} %param.10) | copy-start | bytes 393220
  23.6 0.7 copy-start.9
  24.2 1.3 %copy-start.8 = (bf16[1,64,1024]{2,1,0:T(8,128)(2,1)S(1)}, bf16[1,64,1024]{2,1,0:T(8,128)(2,1)}, u32[]{:S(2)}) copy-start(bf16[1,64,1024]{2,1,0:T(8,128)(2,1)} %param.10) | copy-start | bytes 393220
  24.2 3.5 %copy-start.2 = (bf16[1024,2048]{1,0:T(8,128)(2,1)S(1)}, bf16[1024,2048]{1,0:T(8,128)(2,1)}, u32[]{:S(2)}) copy-start(bf16[1024,2048]{1,0:T(8,128)(2,1)} %weight.1) | copy-start | bytes 12582916
  27.6 7.5 %copy-start.3 = (bf16[1,16,2048]{2,1,0:T(8,128)(2,1)S(1)}, bf16[1,16,2048]{2,1,0:T(8,128)(2,1)}, u32[]{:S(2)}) copy-start(bf16[1,16,2048]{2,1,0:T(8,128)(2,1)} %param.13) | copy-start | bytes 196612
  27.6 7.5 %copy-start.4 = (f32[2048]{0:T(1024)S(1)}, f32[2048]{0:T(1024)}, u32[]{:S(2)}) copy-start(f32[2048]{0:T(1024)} %param.15) | copy-start | bytes 24580
  27.7 7.5 %copy-start.5 = (s32[1,16,8]{1,2,0:T(8,128)S(1)}, s32[1,16,8]{1,2,0:T(8,128)}, u32[]{:S(2)}) copy-start(s32[1,16,8]{1,2,0:T(8,128)} %param.16) | copy-start | bytes 1540
  27.7 7.5 %copy-start.6 = (f32[1,16,8]{1,2,0:T(8,128)S(1)}, f32[1,16,8]{1,2,0:T(8,128)}, u32[]{:S(2)}) copy-start(f32[1,16,8]{1,2,0:T(8,128)} %param.17) | copy-start | bytes 1540
  29.4 6.1 %copy-start = (bf16[1,384,2048]{2,1,0:T(8,128)(2,1)S(1)}, bf16[1,384,2048]{2,1,0:T(8,128)(2,1)}, u32[]{:S(2)}) copy-start(bf16[1,384,2048]{2,1,0:T(8,128)(2,1)} %refs_2_.1) | copy-start | bytes 4718596
  29.4 1.3 %collective-permute-start.6 = (bf16[2,1,16,2048]{3,2,1,0:T(8,128)(2,1)S(1)}, bf16[2,1,16,2048]{3,2,1,0:T(8,128)(2,1)S(1)}, u32[]{:S(2)}, u32[]{:S(2)}) collective-permute-start(bf16[2,1,16,2048]{3,2,1,0:T(8,128)(2,1)S(1)} %bitcast.54), channel_id=1, source_target_pairs={{0,1},{1,0},{2,3},{3,2},{4,5},{5,4},{6,7},{7,6},{8,9},{9,8},{10,11... | collective-permute-start | bytes 393224 | tf_op jit(solution)/shard_map/ppermute | solution.py:35
  30.8 4.3 %collective-permute-start.7 = (bf16[1,1,16,2048]{3,2,1,0:T(8,128)(2,1)S(1)}, bf16[1,1,16,2048]{3,2,1,0:T(8,128)(2,1)S(1)}, u32[]{:S(2)}, u32[]{:S(2)}) collective-permute-start(bf16[1,1,16,2048]{3,2,1,0:T(8,128)(2,1)S(1)} %slice.79), channel_id=1, source_target_pairs={{0,2},{1,3},{2,0},{3,1},{4,6},{5,7},{6,4},{7,5},{8,10},{9,11},{10,... | collective-permute-start | bytes 196616 | tf_op jit(solution)/shard_map/ppermute | solution.py:35
  35.4 12.9 %copy-start.10 = (bf16[1,2048,2,384]{3,2,1,0:T(2,128)(2,1)S(1)}, bf16[1,2048,2,384]{3,2,1,0:T(2,128)(2,1)}, u32[]{:S(2)}) copy-start(bf16[1,2048,2,384]{3,2,1,0:T(2,128)(2,1)} %param.18) | copy-start | bytes 9437188
  35.4 4.4 %collective-permute-start.11 = (bf16[16,2176]{1,0:T(8,128)(2,1)S(1)}, bf16[16,2176]{1,0:T(8,128)(2,1)S(1)}, u32[]{:S(2)}, u32[]{:S(2)}) collective-permute-start(bf16[16,2176]{1,0:T(8,128)(2,1)S(1)} %get-tuple-element.37), channel_id=1, source_target_pairs={{0,4},{4,0},{8,12},{12,8},{1,5},{5,1},{9,13},{13,9},{2,6},{6,2},{1... | collective-permute-start | bytes 208904 | tf_op jit(solution)/shard_map/ppermute | solution.py:35
  35.5 13.5 %collective-permute-start.13 = (bf16[1,384,2048]{2,1,0:T(8,128)(2,1)S(1)}, bf16[1,384,2048]{2,1,0:T(8,128)(2,1)S(1)}, u32[]{:S(2)}, u32[]{:S(2)}) collective-permute-start(bf16[1,384,2048]{2,1,0:T(8,128)(2,1)S(1)} %copy-done), channel_id=1, source_target_pairs={{0,1},{1,0},{2,3},{3,2},{4,5},{5,4},{6,7},{7,6},{8,9},{9,8},{10,11... | collective-permute-start | bytes 4718600 | tf_op jit(solution)/shard_map/ppermute | solution.py:35
  35.6 6.9 %collective-permute-start.10 = (bf16[16,2176]{1,0:T(8,128)(2,1)S(1)}, bf16[16,2176]{1,0:T(8,128)(2,1)S(1)}, u32[]{:S(2)}, u32[]{:S(2)}) collective-permute-start(bf16[16,2176]{1,0:T(8,128)(2,1)S(1)} %get-tuple-element.37), channel_id=1, source_target_pairs={{0,12},{4,8},{8,4},{12,0},{1,13},{5,9},{9,5},{13,1},{2,14},{6,10},... | collective-permute-start | bytes 208904 | tf_op jit(solution)/shard_map/ppermute | solution.py:35
  37.7 8.3 %collective-permute-start.9 = (bf16[16,2176]{1,0:T(8,128)(2,1)S(1)}, bf16[16,2176]{1,0:T(8,128)(2,1)S(1)}, u32[]{:S(2)}, u32[]{:S(2)}) collective-permute-start(bf16[16,2176]{1,0:T(8,128)(2,1)S(1)} %get-tuple-element.37), channel_id=1, source_target_pairs={{0,8},{4,12},{8,0},{12,4},{1,9},{5,13},{9,1},{13,5},{2,10},{6,14},... | collective-permute-start | bytes 208904 | tf_op jit(solution)/shard_map/ppermute | solution.py:35
  39.8 7.8 %collective-permute-start.14 = (bf16[32,2176]{1,0:T(8,128)(2,1)S(1)}, bf16[32,2176]{1,0:T(8,128)(2,1)S(1)}, u32[]{:S(2)}, u32[]{:S(2)}) collective-permute-start(bf16[32,2176]{1,0:T(8,128)(2,1)S(1)} %pad_maximum_fusion.1), channel_id=1, source_target_pairs={{0,2},{1,3},{2,0},{3,1},{4,6},{5,7},{6,4},{7,5},{8,10},{9,11},{10,... | collective-permute-start | bytes 417800 | tf_op jit(solution)/shard_map/ppermute | solution.py:35
  46.0 5.4 %collective-permute-start.12 = (bf16[32,2176]{1,0:T(8,128)(2,1)S(1)}, bf16[32,2176]{1,0:T(8,128)(2,1)S(1)}, u32[]{:S(2)}, u32[]{:S(2)}) collective-permute-start(bf16[32,2176]{1,0:T(8,128)(2,1)S(1)} %pad_maximum_fusion), channel_id=1, source_target_pairs={{0,2},{1,3},{2,0},{3,1},{4,6},{5,7},{6,4},{7,5},{8,10},{9,11},{10,... | collective-permute-start | bytes 417800 | tf_op jit(solution)/shard_map/ppermute | solution.py:35
  49.6 6.0 %collective-permute-start.15 = (bf16[32,2048]{1,0:T(8,128)(2,1)S(1)}, bf16[32,2048]{1,0:T(8,128)(2,1)S(1)}, u32[]{:S(2)}, u32[]{:S(2)}) collective-permute-start(bf16[32,2048]{1,0:T(8,128)(2,1)S(1)} %shard_map.119), channel_id=1, source_target_pairs={{0,2},{1,3},{2,0},{3,1},{4,6},{5,7},{6,4},{7,5},{8,10},{9,11},{10,... | collective-permute-start | bytes 393224 | tf_op jit(solution)/shard_map/ppermute | solution.py:35
  53.5 5.1 %collective-permute-start.16 = (bf16[32,2048]{1,0:T(8,128)(2,1)S(1)}, bf16[32,2048]{1,0:T(8,128)(2,1)S(1)}, u32[]{:S(2)}, u32[]{:S(2)}) collective-permute-start(bf16[32,2048]{1,0:T(8,128)(2,1)S(1)} %get-tuple-element.41), channel_id=1, source_target_pairs={{0,2},{1,3},{2,0},{3,1},{4,6},{5,7},{6,4},{7,5},{8,10},{9,11},{10,... | collective-permute-start | bytes 393224 | tf_op jit(solution)/shard_map/ppermute | solution.py:35
  55.7 4.8 %collective-permute-start.19 = (bf16[16,2048]{1,0:T(8,128)(2,1)S(1)}, bf16[16,2048]{1,0:T(8,128)(2,1)S(1)}, u32[]{:S(2)}, u32[]{:S(2)}) collective-permute-start(bf16[16,2048]{1,0:T(8,128)(2,1)S(1)} %slice.78), channel_id=1, source_target_pairs={{0,4},{4,0},{8,12},{12,8},{1,5},{5,1},{9,13},{13,9},{2,6},{6,2},{1... | collective-permute-start | bytes 196616 | tf_op jit(solution)/shard_map/ppermute | solution.py:35
  58.6 5.2 %collective-permute-start.17 = (bf16[16,2048]{1,0:T(8,128)(2,1)S(1)}, bf16[16,2048]{1,0:T(8,128)(2,1)S(1)}, u32[]{:S(2)}, u32[]{:S(2)}) collective-permute-start(bf16[16,2048]{1,0:T(8,128)(2,1)S(1)} %get-tuple-element.44), channel_id=1, source_target_pairs={{0,8},{4,12},{8,0},{12,4},{1,9},{5,13},{9,1},{13,5},{2,10},{6,14},... | collective-permute-start | bytes 196616 | tf_op jit(solution)/shard_map/ppermute | solution.py:35
  58.7 6.2 %collective-permute-start.18 = (bf16[16,2048]{1,0:T(8,128)(2,1)S(1)}, bf16[16,2048]{1,0:T(8,128)(2,1)S(1)}, u32[]{:S(2)}, u32[]{:S(2)}) collective-permute-start(bf16[16,2048]{1,0:T(8,128)(2,1)S(1)} %get-tuple-element.45), channel_id=1, source_target_pairs={{0,12},{4,8},{8,4},{12,0},{1,13},{5,9},{9,5},{13,1},{2,14},{6,10},... | collective-permute-start | bytes 196616 | tf_op jit(solution)/shard_map/ppermute | solution.py:35

commit v17 on v16

--- a/solution.py
+++ b/solution.py
@@ -105,6 +105,10 @@
 def page_at(offset):
     count = lax.axis_size("ctx")
     return lax.rem(lax.axis_index("ctx") + offset + count, count)
+
+
+def hold_kernel(weight, out):
+    out[...] = jnp.zeros(out.shape, out.dtype)
 
 
 def first_kernel(fresh_block, count, lengths, queries, keys, values, *refs):
@@ -205,14 +209,23 @@
     exp_count = lax.axis_size("exp")
     model_width = out_weight.shape[1]
     own_keys, own_values = pages[:, 0], pages[:, 1]
+    weight_held = pl.pallas_call(
+        hold_kernel,
+        out_shape=jax.ShapeDtypeStruct((8, HEAD), jnp.float32),
+        in_specs=[pl.BlockSpec(memory_space=pl.ANY)],
+        out_specs=whole_specs(1)[0],
+        compiler_params=LIMIT,
+        cost_estimate=pl.CostEstimate(flops=4 << 30, bytes_accessed=4 << 20, transcendentals=0),
+    )(out_weight)
     held = []
     left_keys, left_values = own_keys, own_values
     right_keys, right_values = own_keys, own_values
     for step in range(1, (count - 1) // 2 + 1):
         left_keys = shift(left_keys, "ctx", 1)
         right_values = shift(right_values, "ctx", -1)
+        left_values, _ = lax.optimization_barrier((left_values, weight_held))
         left_values = shift(left_values, "ctx", 1)
-        right_keys, _ = lax.optimization_barrier((right_keys, left_keys))
+        right_keys, _ = lax.optimization_barrier((right_keys, (left_keys, weight_held)))
         right_keys = shift(right_keys, "ctx", -1)
         held.append((count - step, left_keys, left_values))
         held.append((step, right_keys, right_values))
@@ -234,7 +247,7 @@
         cost_estimate=pl.CostEstimate(
             flops=16 * page_flops, bytes_accessed=8 << 20, transcendentals=0
         ),
-    )(lengths, queries, own_keys, own_values, out_weight)
+    )(lengths, queries, own_keys, own_values, weight_held)
     for start in range(0, len(held), 2):
         group = held[start : start + 2]
         operands = [part for _, keys, values in group for part in (keys, values)]

time: 65.8 us -> 65.3 us (level)
  local copies, waits for them, and re-layouts: 4.91 us -> 3.35 us
  waiting for transfers between devices: 22.7 us -> 23.7 us
    unnamed x27 -> x25, local copies, waits for them, and re-layouts: 4.83 us -> 3.28 us
    ppermute x6, waiting for transfers between devices: 4.69 us -> 5.95 us  [shift(): lax.ppermute(value, axis, [(i, (i + step) % count) for i in range(count)])]
  transfers between devices with their start and end apart: 20 -> 20, of which waited for: 10 -> 11; matrix products, arithmetic and copies ran while one was open for 6% -> 6% of each run, Pallas kernels for 10% -> 10%
where the time goes in v17:
time: 65.3 us; the launch traced here: 65.2 us
  starting transfers between devices  27.1 us (42%)
  waiting for transfers between devices  23.7 us (36%)
  Pallas kernels  6.71 us (10%)
  local copies, waits for them, and re-layouts  3.35 us (5%)
  matrix products  2.61 us (4%)
  between operations  0.87 us (1%)
  other arithmetic  0.78 us (1%)
    ppermute x14, waiting for transfers between devices, swap(): lax.ppermute(value, axis, [(i, i ^ stride) for i in range(lax.axis_size(a...  17.8 us
    ppermute x14, starting transfers between devices, swap(): lax.ppermute(value, axis, [(i, i ^ stride) for i in range(lax.axis_size(a...  14 us
    ppermute x6, starting transfers between devices, shift(): lax.ppermute(value, axis, [(i, (i + step) % count) for i in range(count)])  13.1 us
    ppermute x6, waiting for transfers between devices, shift(): lax.ppermute(value, axis, [(i, (i + step) % count) for i in range(count)])  5.95 us
    unnamed x25, local copies, waits for them, and re-layouts  3.28 us
    dot_general x4, matrix products, expert_apply(): jnp.einsum('nd,dgh->gnh', rows[:, :width], gate_up[0], preferred_element_...  2.61 us
    pallas_call x1, Pallas kernels, attention(): pl.pallas_call(functools.partial(late_kernel, fresh_block), out_shape=sha...  1.69 us
    pallas_call x2, Pallas kernels, expert_apply(): pl.pallas_call(functools.partial(down_kernel, [offset for offset, _, _ in...  1.43 us
  transfers between devices with their start and end apart: 20, of which 11 were waited for; matrix products, arithmetic and copies ran while one was open for 6% of the time, Pallas kernels for 10%

profile of v17, /device:TPU:0, one launch (start us, length us, event | category | flops | bytes accessed | tf_op | source)
XLA Modules:
  0.0 65.2 jit_solution(6185677786527048096)
XLA Ops:
  0.6 0.5 collective-permute-start.8
  1.1 1.0 %copy.34 = bf16[1,576,2,128]{3,1,2,0:T(8,128)(2,1)S(1)} copy(bf16[1,576,2,128]{3,2,1,0:T(2,128)(2,1)} %param.11) | data formatting | bytes 589824 | tf_op args[1]
  2.2 2.6 %collective-permute-start.2 = (bf16[576,128]{1,0:T(8,128)(2,1)S(1)}, bf16[576,128]{1,0:T(8,128)(2,1)S(1)}, u32[]{:S(2)}, u32[]{:S(2)}) collective-permute-start(bf16[576,128]{1,0:T(8,128)(2,1)S(1)} %get-tuple-element.28.keys), channel_id=1, source_target_pairs={{0,4},{4,8},{8,12},{12,0},{1,5},{5,9},{9,13},{13,1},{2,6},{6,10},{... | collective-permute-start | bytes 442376 | tf_op jit(solution)/shard_map/ppermute | solution.py:40
  4.8 2.1 %collective-permute-start = (bf16[576,128]{1,0:T(8,128)(2,1)S(1)}, bf16[576,128]{1,0:T(8,128)(2,1)S(1)}, u32[]{:S(2)}, u32[]{:S(2)}) collective-permute-start(bf16[576,128]{1,0:T(8,128)(2,1)S(1)} %get-tuple-element.27.values), channel_id=1, source_target_pairs={{0,12},{4,0},{8,4},{12,8},{1,13},{5,1},{9,5},{13,9},{2,14},{6,2},{... | collective-permute-start | bytes 442376 | tf_op jit(solution)/shard_map/ppermute | solution.py:40
  6.9 2.2 %copy-done.1 = bf16[1024,2048]{1,0:T(8,128)(2,1)S(1)} copy-done((bf16[1024,2048]{1,0:T(8,128)(2,1)S(1)}, bf16[1024,2048]{1,0:T(8,128)(2,1)}, u32[]{:S(2)}) %copy-start.1) | copy-done | bytes 4194328
  9.1 2.5 %collective-permute-done.2.refs_0_ = bf16[576,128]{1,0:T(8,128)(2,1)S(1)} collective-permute-done((bf16[576,128]{1,0:T(8,128)(2,1)S(1)}, bf16[576,128]{1,0:T(8,128)(2,1)S(1)}, u32[]{:S(2)}, u32[]{:S(2)}) %collective-permute-start.2) | collective-permute-done | bytes 147488 | tf_op jit(solution)/shard_map/ppermute | solution.py:40
  11.6 4.5 %collective-permute-start.5 = (bf16[576,128]{1,0:T(8,128)(2,1)S(1)}, bf16[576,128]{1,0:T(8,128)(2,1)S(1)}, u32[]{:S(2)}, u32[]{:S(2)}) collective-permute-start(bf16[576,128]{1,0:T(8,128)(2,1)S(1)} %get-tuple-element.28.keys), channel_id=1, source_target_pairs={{0,12},{4,0},{8,4},{12,8},{1,13},{5,1},{9,5},{13,9},{2,14},{6,2},{... | collective-permute-start | bytes 442376 | tf_op jit(solution)/shard_map/ppermute | solution.py:40
  16.1 0.0 collective-permute-start.3
  16.1 3.8 %collective-permute-start.1 = (bf16[576,128]{1,0:T(8,128)(2,1)S(1)}, bf16[576,128]{1,0:T(8,128)(2,1)S(1)}, u32[]{:S(2)}, u32[]{:S(2)}) collective-permute-start(bf16[576,128]{1,0:T(8,128)(2,1)S(1)} %collective-permute-done.refs_3_), channel_id=1, source_target_pairs={{0,12},{4,0},{8,4},{12,8},{1,13},{5,1},{9,5},{13,9},{2,14},{6,2},{... | collective-permute-start | bytes 442376 | tf_op jit(solution)/shard_map/ppermute | solution.py:40
  19.9 1.3 %shard_map.114 = (f32[1,512]{1,0:T(1,128)S(1)}, f32[1,512]{1,0:T(1,128)S(1)}, f32[128,512]{1,0:T(8,128)S(1)}, s32[4,128]{1,0:T(4,128)S(1)}) custom-call(s32[4]{0:T(128)S(1)} %bitcast.55, bf16[64,1024]{1,0:T(8,128)(2,1)S(1)} %bitcast.51, bf16[576,128]{1,0:T(8,128)(2,1)S(1)} %get-tuple-element.28.keys, bf16[576,128]{1,0:T(8,128)(2,1)S(1)} %get-tuple-element.27.values, ...), custom_call_target="tpu_custom_call" | custom-call | flops 2415919104 | bytes 8388608 | tf_op jit(solution)/shard_map/pallas_call | solution.py:239
  21.3 3.5 %collective-permute-done.3.keys = bf16[576,128]{1,0:T(8,128)(2,1)S(1)} collective-permute-done((bf16[576,128]{1,0:T(8,128)(2,1)S(1)}, bf16[576,128]{1,0:T(8,128)(2,1)S(1)}, u32[]{:S(2)}, u32[]{:S(2)}) %collective-permute-start.3) | collective-permute-done | bytes 147488 | tf_op jit(solution)/shard_map/ppermute | solution.py:40
  24.7 0.6 shard_map.115
  25.3 0.0 collective-permute-done.4.refs_1_
  25.4 1.4 %shard_map.116 = (f32[1,512]{1,0:T(1,128)S(1)}, f32[1,512]{1,0:T(1,128)S(1)}, f32[128,512]{1,0:T(8,128)S(1)}) custom-call(bf16[64,1024]{1,0:T(8,128)(2,1)S(1)} %bitcast.53, s32[4,128]{1,0:T(4,128)S(1)} %get-tuple-element.23.lengths, bf16[576,128]{1,0:T(8,128)(2,1)S(1)} %collective-permute-done.2.refs_0_, ...), custom_call_target="tpu_custom_call" | custom-call | flops 301989888 | bytes 2097152 | tf_op jit(solution)/shard_map/pallas_call | solution.py:254
  26.8 0.0 copy-start.3
  26.8 0.0 copy-start.4
  26.8 0.0 copy-start.5
  26.8 0.0 copy-start.6
  26.9 1.7 %shard_map.117 = (bf16[64,1024]{1,0:T(8,128)(2,1)}, f32[32,2048]{1,0:T(8,128)S(1)}, bf16[32,2048]{1,0:T(8,128)(2,1)S(1)}) custom-call(bf16[576,128]{1,0:T(8,128)(2,1)S(1)} %collective-permute-done.1.values, f32[1,512]{1,0:T(1,128)S(1)} %get-tuple-element.24.last_peak, f32[1,512]{1,0:T(1,128)S(1)} %get-tuple-element.25.last_total, ...), custom_call_target="tpu_custom_call" | custom-call | flops 419430400 | bytes 6291456 | tf_op jit(solution)/shard_map/pallas_call | solution.py:281
  28.5 1.3 %collective-permute-done.6 = bf16[2,1,16,2048]{3,2,1,0:T(8,128)(2,1)S(1)} collective-permute-done((bf16[2,1,16,2048]{3,2,1,0:T(8,128)(2,1)S(1)}, bf16[2,1,16,2048]{3,2,1,0:T(8,128)(2,1)S(1)}, u32[]{:S(2)}, u32[]{:S(2)}) %collective-permute-start.6) | collective-permute-done | bytes 131104 | tf_op jit(solution)/shard_map/ppermute | solution.py:35
  29.9 1.6 %collective-permute-start.7 = (bf16[1,1,16,2048]{3,2,1,0:T(8,128)(2,1)S(1)}, bf16[1,1,16,2048]{3,2,1,0:T(8,128)(2,1)S(1)}, u32[]{:S(2)}, u32[]{:S(2)}) collective-permute-start(bf16[1,1,16,2048]{3,2,1,0:T(8,128)(2,1)S(1)} %slice.79), channel_id=1, source_target_pairs={{0,2},{1,3},{2,0},{3,1},{4,6},{5,7},{6,4},{7,5},{8,10},{9,11},{10,... | collective-permute-start | bytes 196616 | tf_op jit(solution)/shard_map/ppermute | solution.py:35
  31.5 2.8 %collective-permute-done.7 = bf16[1,1,16,2048]{3,2,1,0:T(8,128)(2,1)S(1)} collective-permute-done((bf16[1,1,16,2048]{3,2,1,0:T(8,128)(2,1)S(1)}, bf16[1,1,16,2048]{3,2,1,0:T(8,128)(2,1)S(1)}, u32[]{:S(2)}, u32[]{:S(2)}) %collective-permute-start.7) | collective-permute-done | bytes 65568 | tf_op jit(solution)/shard_map/ppermute | solution.py:35
  34.3 0.2 shard_map.118
  34.6 0.0 copy-start.9
  34.6 0.9 %collective-permute-start.11 = (bf16[16,2176]{1,0:T(8,128)(2,1)S(1)}, bf16[16,2176]{1,0:T(8,128)(2,1)S(1)}, u32[]{:S(2)}, u32[]{:S(2)}) collective-permute-start(bf16[16,2176]{1,0:T(8,128)(2,1)S(1)} %get-tuple-element.39), channel_id=1, source_target_pairs={{0,4},{4,0},{8,12},{12,8},{1,5},{5,1},{9,13},{13,9},{2,6},{6,2},{1... | collective-permute-start | bytes 208904 | tf_op jit(solution)/shard_map/ppermute | solution.py:35
  35.5 2.1 %collective-permute-start.10 = (bf16[16,2176]{1,0:T(8,128)(2,1)S(1)}, bf16[16,2176]{1,0:T(8,128)(2,1)S(1)}, u32[]{:S(2)}, u32[]{:S(2)}) collective-permute-start(bf16[16,2176]{1,0:T(8,128)(2,1)S(1)} %get-tuple-element.39), channel_id=1, source_target_pairs={{0,12},{4,8},{8,4},{12,0},{1,13},{5,9},{9,5},{13,1},{2,14},{6,10},... | collective-permute-start | bytes 208904 | tf_op jit(solution)/shard_map/ppermute | solution.py:35
  37.6 0.5 collective-permute-start.9
  38.1 0.8 %collective-permute-done.11 = bf16[16,2176]{1,0:T(8,128)(2,1)S(1)} collective-permute-done((bf16[16,2176]{1,0:T(8,128)(2,1)S(1)}, bf16[16,2176]{1,0:T(8,128)(2,1)S(1)}, u32[]{:S(2)}, u32[]{:S(2)}) %collective-permute-start.11) | collective-permute-done | bytes 69664 | tf_op jit(solution)/shard_map/ppermute | solution.py:35
  39.0 1.6 %collective-permute-start.14 = (bf16[32,2176]{1,0:T(8,128)(2,1)S(1)}, bf16[32,2176]{1,0:T(8,128)(2,1)S(1)}, u32[]{:S(2)}, u32[]{:S(2)}) collective-permute-start(bf16[32,2176]{1,0:T(8,128)(2,1)S(1)} %pad_maximum_fusion.1), channel_id=1, source_target_pairs={{0,2},{1,3},{2,0},{3,1},{4,6},{5,7},{6,4},{7,5},{8,10},{9,11},{10,... | collective-permute-start | bytes 417800 | tf_op jit(solution)/shard_map/ppermute | solution.py:35
  40.5 1.9 %collective-permute-done.10 = bf16[16,2176]{1,0:T(8,128)(2,1)S(1)} collective-permute-done((bf16[16,2176]{1,0:T(8,128)(2,1)S(1)}, bf16[16,2176]{1,0:T(8,128)(2,1)S(1)}, u32[]{:S(2)}, u32[]{:S(2)}) %collective-permute-start.10) | collective-permute-done | bytes 69664 | tf_op jit(solution)/shard_map/ppermute | solution.py:35
  42.4 2.8 %collective-permute-done.9 = bf16[16,2176]{1,0:T(8,128)(2,1)S(1)} collective-permute-done((bf16[16,2176]{1,0:T(8,128)(2,1)S(1)}, bf16[16,2176]{1,0:T(8,128)(2,1)S(1)}, u32[]{:S(2)}, u32[]{:S(2)}) %collective-permute-start.9) | collective-permute-done | bytes 69664 | tf_op jit(solution)/shard_map/ppermute | solution.py:35
  45.2 1.6 %collective-permute-start.12 = (bf16[32,2176]{1,0:T(8,128)(2,1)S(1)}, bf16[32,2176]{1,0:T(8,128)(2,1)S(1)}, u32[]{:S(2)}, u32[]{:S(2)}) collective-permute-start(bf16[32,2176]{1,0:T(8,128)(2,1)S(1)} %pad_maximum_fusion), channel_id=1, source_target_pairs={{0,2},{1,3},{2,0},{3,1},{4,6},{5,7},{6,4},{7,5},{8,10},{9,11},{10,... | collective-permute-start | bytes 417800 | tf_op jit(solution)/shard_map/ppermute | solution.py:35
  46.8 0.6 fusion.17.refs_1_
  47.4 0.7 %fusion.14.refs_0_ = f32[2,32,384]{2,1,0:T(8,128)S(1)} fusion(bf16[2048,2,384]{2,1,0:T(2,128)(2,1)S(1)} %bitcast.57, bf16[32,2176]{1,0:T(8,128)(2,1)S(1)} %collective-permute-done.14.rows), kind=kOutput, calls=%fused_computation.10 | convolution fusion | flops 100663296 | bytes 3375104 | tf_op jit(solution)/shard_map/nd,dgh->gnh/dot_general | solution.py:366
  48.1 0.7 %shard_map.120 = bf16[32,2048]{1,0:T(8,128)(2,1)S(1)} custom-call(bf16[32,2176]{1,0:T(8,128)(2,1)S(1)} %collective-permute-done.14.rows, f32[2,32,384]{2,1,0:T(8,128)S(1)} %fusion.14.refs_0_, f32[2,32,384]{2,1,0:T(8,128)S(1)} %fusion.17.refs_1_, bf16[1,384,2048]{2,1,0:T(8,128)(2,1)S(1)} %copy-done, bf16[1,384,2048]{2,1,0:T(8,128)(2,1)S(1)} %collective-permute-done.13.refs_3_), custom_call_target="tpu_custom_call" | custom-call | flops 100663296 | bytes 2097152 | tf_op jit(solution)/shard_map/pallas_call | solution.py:370
  48.8 0.6 collective-permute-start.15
  49.4 1.4 %collective-permute-done.12 = bf16[32,2176]{1,0:T(8,128)(2,1)S(1)} collective-permute-done((bf16[32,2176]{1,0:T(8,128)(2,1)S(1)}, bf16[32,2176]{1,0:T(8,128)(2,1)S(1)}, u32[]{:S(2)}, u32[]{:S(2)}) %collective-permute-start.12) | collective-permute-done | bytes 139296 | tf_op jit(solution)/shard_map/ppermute | solution.py:35
  50.8 0.6 fusion.11.refs_1_
  51.5 0.7 %fusion.8.refs_0_ = f32[2,96,384]{2,1,0:T(8,128)S(1)} fusion(bf16[2048,2,384]{2,1,0:T(2,128)(2,1)S(1)} %bitcast.58, bf16[96,2176]{1,0:T(8,128)(2,1)S(1)} %constant_dynamic-update-slice_fusion.rows), kind=kOutput, calls=%fused_computation.8 | convolution fusion | flops 301989888 | bytes 3833856 | tf_op jit(solution)/shard_map/nd,dgh->gnh/dot_general | solution.py:366
  52.1 0.8 %shard_map.119 = (f32[32,2048]{1,0:T(8,128)S(1)}, f32[32,2048]{1,0:T(8,128)S(1)}, bf16[32,2048]{1,0:T(8,128)(2,1)S(1)}) custom-call(bf16[96,2176]{1,0:T(8,128)(2,1)S(1)} %constant_dynamic-update-slice_fusion.rows, f32[2,96,384]{2,1,0:T(8,128)S(1)} %fusion.8.refs_0_, f32[2,96,384]{2,1,0:T(8,128)S(1)} %fusion.11.refs_1_, bf16[1,384,2048]{2,1,0:T(8,128)(2,1)S(1)} %copy-done, ...), custom_call_target="tpu_custom_call" | custom-call | flops 301989888 | bytes 2097152 | tf_op jit(solution)/shard_map/pallas_call | solution.py:370
  52.9 2.1 %collective-permute-start.16 = (bf16[32,2048]{1,0:T(8,128)(2,1)S(1)}, bf16[32,2048]{1,0:T(8,128)(2,1)S(1)}, u32[]{:S(2)}, u32[]{:S(2)}) collective-permute-start(bf16[32,2048]{1,0:T(8,128)(2,1)S(1)} %get-tuple-element.43), channel_id=1, source_target_pairs={{0,2},{1,3},{2,0},{3,1},{4,6},{5,7},{6,4},{7,5},{8,10},{9,11},{10,... | collective-permute-start | bytes 393224 | tf_op jit(solution)/shard_map/ppermute | solution.py:35
  55.0 0.1 collective-permute-start.19
  55.1 2.8 %collective-permute-done.16 = bf16[32,2048]{1,0:T(8,128)(2,1)S(1)} collective-permute-done((bf16[32,2048]{1,0:T(8,128)(2,1)S(1)}, bf16[32,2048]{1,0:T(8,128)(2,1)S(1)}, u32[]{:S(2)}, u32[]{:S(2)}) %collective-permute-start.16) | collective-permute-done | bytes 131104 | tf_op jit(solution)/shard_map/ppermute | solution.py:35
  58.0 0.4 collective-permute-start.17
  58.4 2.1 %collective-permute-start.18 = (bf16[16,2048]{1,0:T(8,128)(2,1)S(1)}, bf16[16,2048]{1,0:T(8,128)(2,1)S(1)}, u32[]{:S(2)}, u32[]{:S(2)}) collective-permute-start(bf16[16,2048]{1,0:T(8,128)(2,1)S(1)} %get-tuple-element.47), channel_id=1, source_target_pairs={{0,12},{4,8},{8,4},{12,0},{1,13},{5,9},{9,5},{13,1},{2,14},{6,10},... | collective-permute-start | bytes 196616 | tf_op jit(solution)/shard_map/ppermute | solution.py:35
  60.5 2.9 %collective-permute-done.17 = bf16[16,2048]{1,0:T(8,128)(2,1)S(1)} collective-permute-done((bf16[16,2048]{1,0:T(8,128)(2,1)S(1)}, bf16[16,2048]{1,0:T(8,128)(2,1)S(1)}, u32[]{:S(2)}, u32[]{:S(2)}) %collective-permute-start.17) | collective-permute-done | bytes 65568 | tf_op jit(solution)/shard_map/ppermute | solution.py:35
  63.4 1.1 %collective-permute-done.18 = bf16[16,2048]{1,0:T(8,128)(2,1)S(1)} collective-permute-done((bf16[16,2048]{1,0:T(8,128)(2,1)S(1)}, bf16[16,2048]{1,0:T(8,128)(2,1)S(1)}, u32[]{:S(2)}, u32[]{:S(2)}) %collective-permute-start.18) | collective-permute-done | bytes 65568 | tf_op jit(solution)/shard_map/ppermute | solution.py:35
  64.5 0.7 %fusion.24 = bf16[1,16,2048]{2,1,0:T(8,128)(2,1)} fusion(bf16[16,2048]{1,0:T(8,128)(2,1)S(1)} %collective-permute-done.19, bf16[16,2048]{1,0:T(8,128)(2,1)S(1)} %collective-permute-done.18, bf16[16,2048]{1,0:T(8,128)(2,1)S(1)} %collective-permute-done.17, f32[32,2048]{1,0:T(8,128)S(1)} %convert_add_fusion, bf16[16,2048]{1,0:T(8,128)(2,1)S(1)} %get-tuple-element.38), kind=kLoop, calls=%fused_computation.29 | loop fusion | flops 294912 | bytes 458752 | tf_op jit(solution)/shard_map/convert_element_type | solution.py:515
  (41 shorter events, 0.3 us)
Async XLA Ops:
  0.6 33.6 %collective-permute-start.8 = (bf16[1,2048,2,384]{3,2,1,0:T(2,128)(2,1)}, bf16[1,2048,2,384]{3,2,1,0:T(2,128)(2,1)S(1)}, u32[]{:S(2)}, u32[]{:S(2)}) collective-permute-start(bf16[1,2048,2,384]{3,2,1,0:T(2,128)(2,1)} %param.18), channel_id=1, source_target_pairs={{0,1},{1,0},{2,3},{3,2},{4,5},{5,4},{6,7},{7,6},{8,9},{9,8},{10,11... | collective-permute-start | bytes 9437192 | tf_op jit(solution)/shard_map/ppermute | solution.py:35
  2.2 9.4 %collective-permute-start.2 = (bf16[576,128]{1,0:T(8,128)(2,1)S(1)}, bf16[576,128]{1,0:T(8,128)(2,1)S(1)}, u32[]{:S(2)}, u32[]{:S(2)}) collective-permute-start(bf16[576,128]{1,0:T(8,128)(2,1)S(1)} %get-tuple-element.28.keys), channel_id=1, source_target_pairs={{0,4},{4,8},{8,12},{12,0},{1,5},{5,9},{9,13},{13,1},{2,6},{6,10},{... | collective-permute-start | bytes 442376 | tf_op jit(solution)/shard_map/ppermute | solution.py:40
  4.8 11.3 %collective-permute-start = (bf16[576,128]{1,0:T(8,128)(2,1)S(1)}, bf16[576,128]{1,0:T(8,128)(2,1)S(1)}, u32[]{:S(2)}, u32[]{:S(2)}) collective-permute-start(bf16[576,128]{1,0:T(8,128)(2,1)S(1)} %get-tuple-element.27.values), channel_id=1, source_target_pairs={{0,12},{4,0},{8,4},{12,8},{1,13},{5,1},{9,5},{13,9},{2,14},{6,2},{... | collective-permute-start | bytes 442376 | tf_op jit(solution)/shard_map/ppermute | solution.py:40
  6.9 2.2 %copy-start.1 = (bf16[1024,2048]{1,0:T(8,128)(2,1)S(1)}, bf16[1024,2048]{1,0:T(8,128)(2,1)}, u32[]{:S(2)}) copy-start(bf16[1024,2048]{1,0:T(8,128)(2,1)} %weight.3) | copy-start | bytes 12582916
  9.1 10.8 %copy-start.7 = (bf16[1,64,1024]{2,1,0:T(8,128)(2,1)S(1)}, bf16[1,64,1024]{2,1,0:T(8,128)(2,1)}, u32[]{:S(2)}) copy-start(bf16[1,64,1024]{2,1,0:T(8,128)(2,1)} %param.10) | copy-start | bytes 393220
  9.1 10.8 %copy-start.8 = (s32[1,4]{1,0:T(1,128)S(1)}, s32[1,4]{1,0:T(1,128)}, u32[]{:S(2)}) copy-start(s32[1,4]{1,0:T(1,128)} %param.12) | copy-start | bytes 52
  9.1 16.2 %collective-permute-start.4 = (bf16[576,128]{1,0:T(8,128)(2,1)S(1)}, bf16[576,128]{1,0:T(8,128)(2,1)S(1)}, u32[]{:S(2)}, u32[]{:S(2)}) collective-permute-start(bf16[576,128]{1,0:T(8,128)(2,1)S(1)} %get-tuple-element.27.values), channel_id=1, source_target_pairs={{0,4},{4,8},{8,12},{12,0},{1,5},{5,9},{9,13},{13,1},{2,6},{6,10},{... | collective-permute-start | bytes 442376 | tf_op jit(solution)/shard_map/ppermute | solution.py:40
  11.6 13.8 %collective-permute-start.5 = (bf16[576,128]{1,0:T(8,128)(2,1)S(1)}, bf16[576,128]{1,0:T(8,128)(2,1)S(1)}, u32[]{:S(2)}, u32[]{:S(2)}) collective-permute-start(bf16[576,128]{1,0:T(8,128)(2,1)S(1)} %get-tuple-element.28.keys), channel_id=1, source_target_pairs={{0,12},{4,0},{8,4},{12,8},{1,13},{5,1},{9,5},{13,9},{2,14},{6,2},{... | collective-permute-start | bytes 442376 | tf_op jit(solution)/shard_map/ppermute | solution.py:40
  16.1 8.6 %collective-permute-start.3 = (bf16[576,128]{1,0:T(8,128)(2,1)S(1)}, bf16[576,128]{1,0:T(8,128)(2,1)S(1)}, u32[]{:S(2)}, u32[]{:S(2)}) collective-permute-start(bf16[576,128]{1,0:T(8,128)(2,1)S(1)} %collective-permute-done.2.refs_0_), channel_id=1, source_target_pairs={{0,4},{4,8},{8,12},{12,0},{1,5},{5,9},{9,13},{13,1},{2,6},{6,10},{... | collective-permute-start | bytes 442376 | tf_op jit(solution)/shard_map/ppermute | solution.py:40
  16.1 10.7 %collective-permute-start.1 = (bf16[576,128]{1,0:T(8,128)(2,1)S(1)}, bf16[576,128]{1,0:T(8,128)(2,1)S(1)}, u32[]{:S(2)}, u32[]{:S(2)}) collective-permute-start(bf16[576,128]{1,0:T(8,128)(2,1)S(1)} %collective-permute-done.refs_3_), channel_id=1, source_target_pairs={{0,12},{4,0},{8,4},{12,8},{1,13},{5,1},{9,5},{13,9},{2,14},{6,2},{... | collective-permute-start | bytes 442376 | tf_op jit(solution)/shard_map/ppermute | solution.py:40
  19.9 6.9 %copy-start.2 = (bf16[1024,2048]{1,0:T(8,128)(2,1)S(1)}, bf16[1024,2048]{1,0:T(8,128)(2,1)}, u32[]{:S(2)}) copy-start(bf16[1024,2048]{1,0:T(8,128)(2,1)} %weight.3) | copy-start | bytes 12582916
  26.8 7.5 %copy-start.3 = (bf16[1,16,2048]{2,1,0:T(8,128)(2,1)S(1)}, bf16[1,16,2048]{2,1,0:T(8,128)(2,1)}, u32[]{:S(2)}) copy-start(bf16[1,16,2048]{2,1,0:T(8,128)(2,1)} %param.13) | copy-start | bytes 196612
  26.8 7.5 %copy-start.4 = (f32[2048]{0:T(1024)S(1)}, f32[2048]{0:T(1024)}, u32[]{:S(2)}) copy-start(f32[2048]{0:T(1024)} %param.15) | copy-start | bytes 24580
  26.8 7.5 %copy-start.5 = (s32[1,16,8]{1,2,0:T(8,128)S(1)}, s32[1,16,8]{1,2,0:T(8,128)}, u32[]{:S(2)}) copy-start(s32[1,16,8]{1,2,0:T(8,128)} %param.16) | copy-start | bytes 1540
  26.8 7.5 %copy-start.6 = (f32[1,16,8]{1,2,0:T(8,128)S(1)}, f32[1,16,8]{1,2,0:T(8,128)}, u32[]{:S(2)}) copy-start(f32[1,16,8]{1,2,0:T(8,128)} %param.17) | copy-start | bytes 1540
  28.5 6.9 %copy-start = (bf16[1,384,2048]{2,1,0:T(8,128)(2,1)S(1)}, bf16[1,384,2048]{2,1,0:T(8,128)(2,1)}, u32[]{:S(2)}) copy-start(bf16[1,384,2048]{2,1,0:T(8,128)(2,1)} %refs_2_.1) | copy-start | bytes 4718596
  28.5 1.3 %collective-permute-start.6 = (bf16[2,1,16,2048]{3,2,1,0:T(8,128)(2,1)S(1)}, bf16[2,1,16,2048]{3,2,1,0:T(8,128)(2,1)S(1)}, u32[]{:S(2)}, u32[]{:S(2)}) collective-permute-start(bf16[2,1,16,2048]{3,2,1,0:T(8,128)(2,1)S(1)} %bitcast.54), channel_id=1, source_target_pairs={{0,1},{1,0},{2,3},{3,2},{4,5},{5,4},{6,7},{7,6},{8,9},{9,8},{10,11... | collective-permute-start | bytes 393224 | tf_op jit(solution)/shard_map/ppermute | solution.py:35
  29.9 4.3 %collective-permute-start.7 = (bf16[1,1,16,2048]{3,2,1,0:T(8,128)(2,1)S(1)}, bf16[1,1,16,2048]{3,2,1,0:T(8,128)(2,1)S(1)}, u32[]{:S(2)}, u32[]{:S(2)}) collective-permute-start(bf16[1,1,16,2048]{3,2,1,0:T(8,128)(2,1)S(1)} %slice.79), channel_id=1, source_target_pairs={{0,2},{1,3},{2,0},{3,1},{4,6},{5,7},{6,4},{7,5},{8,10},{9,11},{10,... | collective-permute-start | bytes 196616 | tf_op jit(solution)/shard_map/ppermute | solution.py:35
  34.6 12.9 %copy-start.9 = (bf16[1,2048,2,384]{3,2,1,0:T(2,128)(2,1)S(1)}, bf16[1,2048,2,384]{3,2,1,0:T(2,128)(2,1)}, u32[]{:S(2)}) copy-start(bf16[1,2048,2,384]{3,2,1,0:T(2,128)(2,1)} %param.18) | copy-start | bytes 9437188
  34.6 4.4 %collective-permute-start.11 = (bf16[16,2176]{1,0:T(8,128)(2,1)S(1)}, bf16[16,2176]{1,0:T(8,128)(2,1)S(1)}, u32[]{:S(2)}, u32[]{:S(2)}) collective-permute-start(bf16[16,2176]{1,0:T(8,128)(2,1)S(1)} %get-tuple-element.39), channel_id=1, source_target_pairs={{0,4},{4,0},{8,12},{12,8},{1,5},{5,1},{9,13},{13,9},{2,6},{6,2},{1... | collective-permute-start | bytes 208904 | tf_op jit(solution)/shard_map/ppermute | solution.py:35
  35.5 12.6 %collective-permute-start.13 = (bf16[1,384,2048]{2,1,0:T(8,128)(2,1)S(1)}, bf16[1,384,2048]{2,1,0:T(8,128)(2,1)S(1)}, u32[]{:S(2)}, u32[]{:S(2)}) collective-permute-start(bf16[1,384,2048]{2,1,0:T(8,128)(2,1)S(1)} %copy-done), channel_id=1, source_target_pairs={{0,1},{1,0},{2,3},{3,2},{4,5},{5,4},{6,7},{7,6},{8,9},{9,8},{10,11... | collective-permute-start | bytes 4718600 | tf_op jit(solution)/shard_map/ppermute | solution.py:35
  35.5 6.9 %collective-permute-start.10 = (bf16[16,2176]{1,0:T(8,128)(2,1)S(1)}, bf16[16,2176]{1,0:T(8,128)(2,1)S(1)}, u32[]{:S(2)}, u32[]{:S(2)}) collective-permute-start(bf16[16,2176]{1,0:T(8,128)(2,1)S(1)} %get-tuple-element.39), channel_id=1, source_target_pairs={{0,12},{4,8},{8,4},{12,0},{1,13},{5,9},{9,5},{13,1},{2,14},{6,10},... | collective-permute-start | bytes 208904 | tf_op jit(solution)/shard_map/ppermute | solution.py:35
  37.6 7.5 %collective-permute-start.9 = (bf16[16,2176]{1,0:T(8,128)(2,1)S(1)}, bf16[16,2176]{1,0:T(8,128)(2,1)S(1)}, u32[]{:S(2)}, u32[]{:S(2)}) collective-permute-start(bf16[16,2176]{1,0:T(8,128)(2,1)S(1)} %get-tuple-element.39), channel_id=1, source_target_pairs={{0,8},{4,12},{8,0},{12,4},{1,9},{5,13},{9,1},{13,5},{2,10},{6,14},... | collective-permute-start | bytes 208904 | tf_op jit(solution)/shard_map/ppermute | solution.py:35
  39.0 7.8 %collective-permute-start.14 = (bf16[32,2176]{1,0:T(8,128)(2,1)S(1)}, bf16[32,2176]{1,0:T(8,128)(2,1)S(1)}, u32[]{:S(2)}, u32[]{:S(2)}) collective-permute-start(bf16[32,2176]{1,0:T(8,128)(2,1)S(1)} %pad_maximum_fusion.1), channel_id=1, source_target_pairs={{0,2},{1,3},{2,0},{3,1},{4,6},{5,7},{6,4},{7,5},{8,10},{9,11},{10,... | collective-permute-start | bytes 417800 | tf_op jit(solution)/shard_map/ppermute | solution.py:35
  45.2 5.6 %collective-permute-start.12 = (bf16[32,2176]{1,0:T(8,128)(2,1)S(1)}, bf16[32,2176]{1,0:T(8,128)(2,1)S(1)}, u32[]{:S(2)}, u32[]{:S(2)}) collective-permute-start(bf16[32,2176]{1,0:T(8,128)(2,1)S(1)} %pad_maximum_fusion), channel_id=1, source_target_pairs={{0,2},{1,3},{2,0},{3,1},{4,6},{5,7},{6,4},{7,5},{8,10},{9,11},{10,... | collective-permute-start | bytes 417800 | tf_op jit(solution)/shard_map/ppermute | solution.py:35
  48.8 6.2 %collective-permute-start.15 = (bf16[32,2048]{1,0:T(8,128)(2,1)S(1)}, bf16[32,2048]{1,0:T(8,128)(2,1)S(1)}, u32[]{:S(2)}, u32[]{:S(2)}) collective-permute-start(bf16[32,2048]{1,0:T(8,128)(2,1)S(1)} %shard_map.120), channel_id=1, source_target_pairs={{0,2},{1,3},{2,0},{3,1},{4,6},{5,7},{6,4},{7,5},{8,10},{9,11},{10,... | collective-permute-start | bytes 393224 | tf_op jit(solution)/shard_map/ppermute | solution.py:35
  52.9 5.0 %collective-permute-start.16 = (bf16[32,2048]{1,0:T(8,128)(2,1)S(1)}, bf16[32,2048]{1,0:T(8,128)(2,1)S(1)}, u32[]{:S(2)}, u32[]{:S(2)}) collective-permute-start(bf16[32,2048]{1,0:T(8,128)(2,1)S(1)} %get-tuple-element.43), channel_id=1, source_target_pairs={{0,2},{1,3},{2,0},{3,1},{4,6},{5,7},{6,4},{7,5},{8,10},{9,11},{10,... | collective-permute-start | bytes 393224 | tf_op jit(solution)/shard_map/ppermute | solution.py:35
  55.0 5.5 %collective-permute-start.19 = (bf16[16,2048]{1,0:T(8,128)(2,1)S(1)}, bf16[16,2048]{1,0:T(8,128)(2,1)S(1)}, u32[]{:S(2)}, u32[]{:S(2)}) collective-permute-start(bf16[16,2048]{1,0:T(8,128)(2,1)S(1)} %slice.78), channel_id=1, source_target_pairs={{0,4},{4,0},{8,12},{12,8},{1,5},{5,1},{9,13},{13,9},{2,6},{6,2},{1... | collective-permute-start | bytes 196616 | tf_op jit(solution)/shard_map/ppermute | solution.py:35
  58.0 5.4 %collective-permute-start.17 = (bf16[16,2048]{1,0:T(8,128)(2,1)S(1)}, bf16[16,2048]{1,0:T(8,128)(2,1)S(1)}, u32[]{:S(2)}, u32[]{:S(2)}) collective-permute-start(bf16[16,2048]{1,0:T(8,128)(2,1)S(1)} %get-tuple-element.46), channel_id=1, source_target_pairs={{0,8},{4,12},{8,0},{12,4},{1,9},{5,13},{9,1},{13,5},{2,10},{6,14},... | collective-permute-start | bytes 196616 | tf_op jit(solution)/shard_map/ppermute | solution.py:35
  58.4 6.1 %collective-permute-start.18 = (bf16[16,2048]{1,0:T(8,128)(2,1)S(1)}, bf16[16,2048]{1,0:T(8,128)(2,1)S(1)}, u32[]{:S(2)}, u32[]{:S(2)}) collective-permute-start(bf16[16,2048]{1,0:T(8,128)(2,1)S(1)} %get-tuple-element.47), channel_id=1, source_target_pairs={{0,12},{4,8},{8,4},{12,0},{1,13},{5,9},{9,5},{13,1},{2,14},{6,10},... | collective-permute-start | bytes 196616 | tf_op jit(solution)/shard_map/ppermute | solution.py:35

commit v18 on v17

--- a/solution.py
+++ b/solution.py
@@ -268,6 +268,7 @@
     ]
     if exp_count > 1:
         shapes.append(jax.ShapeDtypeStruct(half, jnp.bfloat16))
+    last_keys, _ = lax.optimization_barrier((last[1], state))
     last_weights = pl.pallas_call(
         functools.partial(weights_kernel, last[0], fresh_block),
         out_shape=(line, line, jax.ShapeDtypeStruct((pages.shape[0], rows), jnp.bfloat16)),
@@ -277,7 +278,7 @@
         cost_estimate=pl.CostEstimate(
             flops=page_flops, bytes_accessed=1 << 20, transcendentals=0
         ),
-    )(queries, last[1], page_lengths)
+    )(queries, last_keys, page_lengths)
     outs = pl.pallas_call(
         functools.partial(late_kernel, fresh_block),
         out_shape=shapes,

time: 65.3 us -> 64.9 us (level)
  transfers between devices with their start and end apart: 20 -> 20, of which waited for: 11 -> 13; matrix products, arithmetic and copies ran while one was open for 6% -> 6% of each run, Pallas kernels for 10% -> 10%
where the time goes in v18:
time: 64.9 us; the launch traced here: 64.7 us
  starting transfers between devices  26.7 us (41%)
  waiting for transfers between devices  23.7 us (37%)
  Pallas kernels  6.7 us (10%)
  local copies, waits for them, and re-layouts  3.35 us (5%)
  matrix products  2.61 us (4%)
  between operations  0.86 us (1%)
  other arithmetic  0.78 us (1%)
    ppermute x14, waiting for transfers between devices, swap(): lax.ppermute(value, axis, [(i, i ^ stride) for i in range(lax.axis_size(a...  18 us
    ppermute x14, starting transfers between devices, swap(): lax.ppermute(value, axis, [(i, i ^ stride) for i in range(lax.axis_size(a...  13.7 us
    ppermute x6, starting transfers between devices, shift(): lax.ppermute(value, axis, [(i, (i + step) % count) for i in range(count)])  13.1 us
    ppermute x6, waiting for transfers between devices, shift(): lax.ppermute(value, axis, [(i, (i + step) % count) for i in range(count)])  5.72 us
    unnamed x25, local copies, waits for them, and re-layouts  3.27 us
    dot_general x4, matrix products, expert_apply(): jnp.einsum('nd,dgh->gnh', rows[:, :width], gate_up[0], preferred_element_...  2.61 us
    pallas_call x1, Pallas kernels, attention(): pl.pallas_call(functools.partial(late_kernel, fresh_block), out_shape=sha...  1.68 us
    pallas_call x2, Pallas kernels, expert_apply(): pl.pallas_call(functools.partial(down_kernel, [offset for offset, _, _ in...  1.44 us
  transfers between devices with their start and end apart: 20, of which 13 were waited for; matrix products, arithmetic and copies ran while one was open for 6% of the time, Pallas kernels for 10%

profile of v18, /device:TPU:0, one launch (start us, length us, event | category | flops | bytes accessed | tf_op | source)
XLA Modules:
  0.0 64.7 jit_solution(14880162324073605368)
XLA Ops:
  0.6 0.5 collective-permute-start.8
  1.1 1.0 %copy.34 = bf16[1,576,2,128]{3,1,2,0:T(8,128)(2,1)S(1)} copy(bf16[1,576,2,128]{3,2,1,0:T(2,128)(2,1)} %param.11) | data formatting | bytes 589824 | tf_op args[1]
  2.2 2.6 %collective-permute-start.2 = (bf16[576,128]{1,0:T(8,128)(2,1)S(1)}, bf16[576,128]{1,0:T(8,128)(2,1)S(1)}, u32[]{:S(2)}, u32[]{:S(2)}) collective-permute-start(bf16[576,128]{1,0:T(8,128)(2,1)S(1)} %get-tuple-element.26.keys), channel_id=1, source_target_pairs={{0,4},{4,8},{8,12},{12,0},{1,5},{5,9},{9,13},{13,1},{2,6},{6,10},{... | collective-permute-start | bytes 442376 | tf_op jit(solution)/shard_map/ppermute | solution.py:40
  4.8 2.1 %collective-permute-start = (bf16[576,128]{1,0:T(8,128)(2,1)S(1)}, bf16[576,128]{1,0:T(8,128)(2,1)S(1)}, u32[]{:S(2)}, u32[]{:S(2)}) collective-permute-start(bf16[576,128]{1,0:T(8,128)(2,1)S(1)} %get-tuple-element.25.values), channel_id=1, source_target_pairs={{0,12},{4,0},{8,4},{12,8},{1,13},{5,1},{9,5},{13,9},{2,14},{6,2},{... | collective-permute-start | bytes 442376 | tf_op jit(solution)/shard_map/ppermute | solution.py:40
  6.9 2.2 %copy-done.1 = bf16[1024,2048]{1,0:T(8,128)(2,1)S(1)} copy-done((bf16[1024,2048]{1,0:T(8,128)(2,1)S(1)}, bf16[1024,2048]{1,0:T(8,128)(2,1)}, u32[]{:S(2)}) %copy-start.1) | copy-done | bytes 4194328
  9.1 0.0 collective-permute-start.4
  9.1 2.5 %collective-permute-done.2.refs_0_ = bf16[576,128]{1,0:T(8,128)(2,1)S(1)} collective-permute-done((bf16[576,128]{1,0:T(8,128)(2,1)S(1)}, bf16[576,128]{1,0:T(8,128)(2,1)S(1)}, u32[]{:S(2)}, u32[]{:S(2)}) %collective-permute-start.2) | collective-permute-done | bytes 147488 | tf_op jit(solution)/shard_map/ppermute | solution.py:40
  11.6 4.5 %collective-permute-start.5 = (bf16[576,128]{1,0:T(8,128)(2,1)S(1)}, bf16[576,128]{1,0:T(8,128)(2,1)S(1)}, u32[]{:S(2)}, u32[]{:S(2)}) collective-permute-start(bf16[576,128]{1,0:T(8,128)(2,1)S(1)} %get-tuple-element.26.keys), channel_id=1, source_target_pairs={{0,12},{4,0},{8,4},{12,8},{1,13},{5,1},{9,5},{13,9},{2,14},{6,2},{... | collective-permute-start | bytes 442376 | tf_op jit(solution)/shard_map/ppermute | solution.py:40
  16.1 3.8 %collective-permute-start.1 = (bf16[576,128]{1,0:T(8,128)(2,1)S(1)}, bf16[576,128]{1,0:T(8,128)(2,1)S(1)}, u32[]{:S(2)}, u32[]{:S(2)}) collective-permute-start(bf16[576,128]{1,0:T(8,128)(2,1)S(1)} %collective-permute-done.refs_3_), channel_id=1, source_target_pairs={{0,12},{4,0},{8,4},{12,8},{1,13},{5,1},{9,5},{13,9},{2,14},{6,2},{... | collective-permute-start | bytes 442376 | tf_op jit(solution)/shard_map/ppermute | solution.py:40
  19.9 1.3 %shard_map.114 = (f32[1,512]{1,0:T(1,128)S(1)}, f32[1,512]{1,0:T(1,128)S(1)}, f32[128,512]{1,0:T(8,128)S(1)}, s32[4,128]{1,0:T(4,128)S(1)}) custom-call(s32[4]{0:T(128)S(1)} %bitcast.55, bf16[64,1024]{1,0:T(8,128)(2,1)S(1)} %bitcast.51, bf16[576,128]{1,0:T(8,128)(2,1)S(1)} %get-tuple-element.26.keys, bf16[576,128]{1,0:T(8,128)(2,1)S(1)} %get-tuple-element.25.values, ...), custom_call_target="tpu_custom_call" | custom-call | flops 2415919104 | bytes 8388608 | tf_op jit(solution)/shard_map/pallas_call | solution.py:239
  21.3 0.1 collective-permute-done.5.refs_2_
  21.3 1.4 %shard_map.115 = (f32[1,512]{1,0:T(1,128)S(1)}, f32[1,512]{1,0:T(1,128)S(1)}, f32[128,512]{1,0:T(8,128)S(1)}) custom-call(bf16[64,1024]{1,0:T(8,128)(2,1)S(1)} %bitcast.52, s32[4,128]{1,0:T(4,128)S(1)} %get-tuple-element.24.lengths, bf16[576,128]{1,0:T(8,128)(2,1)S(1)} %collective-permute-done.2.refs_0_, ...), custom_call_target="tpu_custom_call" | custom-call | flops 301989888 | bytes 2097152 | tf_op jit(solution)/shard_map/pallas_call | solution.py:254
  22.8 2.0 %collective-permute-done.3.keys = bf16[576,128]{1,0:T(8,128)(2,1)S(1)} collective-permute-done((bf16[576,128]{1,0:T(8,128)(2,1)S(1)}, bf16[576,128]{1,0:T(8,128)(2,1)S(1)}, u32[]{:S(2)}, u32[]{:S(2)}) %collective-permute-start.3) | collective-permute-done | bytes 147488 | tf_op jit(solution)/shard_map/ppermute | solution.py:40
  24.7 0.6 shard_map.116
  25.3 0.0 copy-start.4
  25.4 0.0 copy-start.5
  25.4 0.0 copy-start.6
  25.4 1.2 %collective-permute-done.1.values = bf16[576,128]{1,0:T(8,128)(2,1)S(1)} collective-permute-done((bf16[576,128]{1,0:T(8,128)(2,1)S(1)}, bf16[576,128]{1,0:T(8,128)(2,1)S(1)}, u32[]{:S(2)}, u32[]{:S(2)}) %collective-permute-start.1) | collective-permute-done | bytes 147488 | tf_op jit(solution)/shard_map/ppermute | solution.py:40
  26.6 1.7 %shard_map.117 = (bf16[64,1024]{1,0:T(8,128)(2,1)}, f32[32,2048]{1,0:T(8,128)S(1)}, bf16[32,2048]{1,0:T(8,128)(2,1)S(1)}) custom-call(bf16[576,128]{1,0:T(8,128)(2,1)S(1)} %collective-permute-done.1.values, f32[1,512]{1,0:T(1,128)S(1)} %get-tuple-element.34.last_peak, f32[1,512]{1,0:T(1,128)S(1)} %get-tuple-element.35.last_total, ...), custom_call_target="tpu_custom_call" | custom-call | flops 419430400 | bytes 6291456 | tf_op jit(solution)/shard_map/pallas_call | solution.py:282
  28.3 1.3 %collective-permute-done.6 = bf16[2,1,16,2048]{3,2,1,0:T(8,128)(2,1)S(1)} collective-permute-done((bf16[2,1,16,2048]{3,2,1,0:T(8,128)(2,1)S(1)}, bf16[2,1,16,2048]{3,2,1,0:T(8,128)(2,1)S(1)}, u32[]{:S(2)}, u32[]{:S(2)}) %collective-permute-start.6) | collective-permute-done | bytes 131104 | tf_op jit(solution)/shard_map/ppermute | solution.py:35
  29.7 1.6 %collective-permute-start.7 = (bf16[1,1,16,2048]{3,2,1,0:T(8,128)(2,1)S(1)}, bf16[1,1,16,2048]{3,2,1,0:T(8,128)(2,1)S(1)}, u32[]{:S(2)}, u32[]{:S(2)}) collective-permute-start(bf16[1,1,16,2048]{3,2,1,0:T(8,128)(2,1)S(1)} %slice.79), channel_id=1, source_target_pairs={{0,2},{1,3},{2,0},{3,1},{4,6},{5,7},{6,4},{7,5},{8,10},{9,11},{10,... | collective-permute-start | bytes 196616 | tf_op jit(solution)/shard_map/ppermute | solution.py:35
  31.2 2.8 %collective-permute-done.7 = bf16[1,1,16,2048]{3,2,1,0:T(8,128)(2,1)S(1)} collective-permute-done((bf16[1,1,16,2048]{3,2,1,0:T(8,128)(2,1)S(1)}, bf16[1,1,16,2048]{3,2,1,0:T(8,128)(2,1)S(1)}, u32[]{:S(2)}, u32[]{:S(2)}) %collective-permute-start.7) | collective-permute-done | bytes 65568 | tf_op jit(solution)/shard_map/ppermute | solution.py:35
  34.0 0.2 shard_map.118
  34.3 0.0 copy-start.9
  34.3 1.2 %collective-permute-start.11 = (bf16[16,2176]{1,0:T(8,128)(2,1)S(1)}, bf16[16,2176]{1,0:T(8,128)(2,1)S(1)}, u32[]{:S(2)}, u32[]{:S(2)}) collective-permute-start(bf16[16,2176]{1,0:T(8,128)(2,1)S(1)} %get-tuple-element.41), channel_id=1, source_target_pairs={{0,4},{4,0},{8,12},{12,8},{1,5},{5,1},{9,13},{13,9},{2,6},{6,2},{1... | collective-permute-start | bytes 208904 | tf_op jit(solution)/shard_map/ppermute | solution.py:35
  35.5 1.6 %collective-permute-start.10 = (bf16[16,2176]{1,0:T(8,128)(2,1)S(1)}, bf16[16,2176]{1,0:T(8,128)(2,1)S(1)}, u32[]{:S(2)}, u32[]{:S(2)}) collective-permute-start(bf16[16,2176]{1,0:T(8,128)(2,1)S(1)} %get-tuple-element.41), channel_id=1, source_target_pairs={{0,12},{4,8},{8,4},{12,0},{1,13},{5,9},{9,5},{13,1},{2,14},{6,10},... | collective-permute-start | bytes 208904 | tf_op jit(solution)/shard_map/ppermute | solution.py:35
  37.1 0.8 %collective-permute-start.9 = (bf16[16,2176]{1,0:T(8,128)(2,1)S(1)}, bf16[16,2176]{1,0:T(8,128)(2,1)S(1)}, u32[]{:S(2)}, u32[]{:S(2)}) collective-permute-start(bf16[16,2176]{1,0:T(8,128)(2,1)S(1)} %get-tuple-element.41), channel_id=1, source_target_pairs={{0,8},{4,12},{8,0},{12,4},{1,9},{5,13},{9,1},{13,5},{2,10},{6,14},... | collective-permute-start | bytes 208904 | tf_op jit(solution)/shard_map/ppermute | solution.py:35
  37.9 0.8 %collective-permute-done.11 = bf16[16,2176]{1,0:T(8,128)(2,1)S(1)} collective-permute-done((bf16[16,2176]{1,0:T(8,128)(2,1)S(1)}, bf16[16,2176]{1,0:T(8,128)(2,1)S(1)}, u32[]{:S(2)}, u32[]{:S(2)}) %collective-permute-start.11) | collective-permute-done | bytes 69664 | tf_op jit(solution)/shard_map/ppermute | solution.py:35
  38.7 1.6 %collective-permute-start.14 = (bf16[32,2176]{1,0:T(8,128)(2,1)S(1)}, bf16[32,2176]{1,0:T(8,128)(2,1)S(1)}, u32[]{:S(2)}, u32[]{:S(2)}) collective-permute-start(bf16[32,2176]{1,0:T(8,128)(2,1)S(1)} %pad_maximum_fusion.1), channel_id=1, source_target_pairs={{0,2},{1,3},{2,0},{3,1},{4,6},{5,7},{6,4},{7,5},{8,10},{9,11},{10,... | collective-permute-start | bytes 417800 | tf_op jit(solution)/shard_map/ppermute | solution.py:35
  40.2 2.1 %collective-permute-done.10 = bf16[16,2176]{1,0:T(8,128)(2,1)S(1)} collective-permute-done((bf16[16,2176]{1,0:T(8,128)(2,1)S(1)}, bf16[16,2176]{1,0:T(8,128)(2,1)S(1)}, u32[]{:S(2)}, u32[]{:S(2)}) %collective-permute-start.10) | collective-permute-done | bytes 69664 | tf_op jit(solution)/shard_map/ppermute | solution.py:35
  42.4 2.5 %collective-permute-done.9 = bf16[16,2176]{1,0:T(8,128)(2,1)S(1)} collective-permute-done((bf16[16,2176]{1,0:T(8,128)(2,1)S(1)}, bf16[16,2176]{1,0:T(8,128)(2,1)S(1)}, u32[]{:S(2)}, u32[]{:S(2)}) %collective-permute-start.9) | collective-permute-done | bytes 69664 | tf_op jit(solution)/shard_map/ppermute | solution.py:35
  44.9 1.6 %collective-permute-start.12 = (bf16[32,2176]{1,0:T(8,128)(2,1)S(1)}, bf16[32,2176]{1,0:T(8,128)(2,1)S(1)}, u32[]{:S(2)}, u32[]{:S(2)}) collective-permute-start(bf16[32,2176]{1,0:T(8,128)(2,1)S(1)} %pad_maximum_fusion), channel_id=1, source_target_pairs={{0,2},{1,3},{2,0},{3,1},{4,6},{5,7},{6,4},{7,5},{8,10},{9,11},{10,... | collective-permute-start | bytes 417800 | tf_op jit(solution)/shard_map/ppermute | solution.py:35
  46.5 0.6 %fusion.17.refs_1_ = f32[2,32,384]{2,1,0:T(8,128)S(1)} fusion(bf16[2048,2,384]{2,1,0:T(2,128)(2,1)S(1)} %bitcast.43, bf16[32,2176]{1,0:T(8,128)(2,1)S(1)} %collective-permute-done.14.rows), kind=kOutput, calls=%fused_computation.11 | convolution fusion | flops 100663296 | bytes 3375104 | tf_op jit(solution)/shard_map/nd,dgh->gnh/dot_general | solution.py:367
  47.2 0.7 %fusion.14.refs_0_ = f32[2,32,384]{2,1,0:T(8,128)S(1)} fusion(bf16[2048,2,384]{2,1,0:T(2,128)(2,1)S(1)} %bitcast.57, bf16[32,2176]{1,0:T(8,128)(2,1)S(1)} %collective-permute-done.14.rows), kind=kOutput, calls=%fused_computation.10 | convolution fusion | flops 100663296 | bytes 3375104 | tf_op jit(solution)/shard_map/nd,dgh->gnh/dot_general | solution.py:367
  47.8 0.7 %shard_map.120 = bf16[32,2048]{1,0:T(8,128)(2,1)S(1)} custom-call(bf16[32,2176]{1,0:T(8,128)(2,1)S(1)} %collective-permute-done.14.rows, f32[2,32,384]{2,1,0:T(8,128)S(1)} %fusion.14.refs_0_, f32[2,32,384]{2,1,0:T(8,128)S(1)} %fusion.17.refs_1_, bf16[1,384,2048]{2,1,0:T(8,128)(2,1)S(1)} %copy-done, bf16[1,384,2048]{2,1,0:T(8,128)(2,1)S(1)} %collective-permute-done.13.refs_3_), custom_call_target="tpu_custom_call" | custom-call | flops 100663296 | bytes 2097152 | tf_op jit(solution)/shard_map/pallas_call | solution.py:371
  48.5 0.6 collective-permute-start.15
  49.1 1.5 %collective-permute-done.12 = bf16[32,2176]{1,0:T(8,128)(2,1)S(1)} collective-permute-done((bf16[32,2176]{1,0:T(8,128)(2,1)S(1)}, bf16[32,2176]{1,0:T(8,128)(2,1)S(1)}, u32[]{:S(2)}, u32[]{:S(2)}) %collective-permute-start.12) | collective-permute-done | bytes 139296 | tf_op jit(solution)/shard_map/ppermute | solution.py:35
  50.6 0.7 %fusion.11.refs_1_ = f32[2,96,384]{2,1,0:T(8,128)S(1)} fusion(bf16[2048,2,384]{2,1,0:T(2,128)(2,1)S(1)} %bitcast.44, bf16[96,2176]{1,0:T(8,128)(2,1)S(1)} %constant_dynamic-update-slice_fusion.rows), kind=kOutput, calls=%fused_computation.9 | convolution fusion | flops 301989888 | bytes 3833856 | tf_op jit(solution)/shard_map/nd,dgh->gnh/dot_general | solution.py:367
  51.3 0.7 %fusion.8.refs_0_ = f32[2,96,384]{2,1,0:T(8,128)S(1)} fusion(bf16[2048,2,384]{2,1,0:T(2,128)(2,1)S(1)} %bitcast.58, bf16[96,2176]{1,0:T(8,128)(2,1)S(1)} %constant_dynamic-update-slice_fusion.rows), kind=kOutput, calls=%fused_computation.8 | convolution fusion | flops 301989888 | bytes 3833856 | tf_op jit(solution)/shard_map/nd,dgh->gnh/dot_general | solution.py:367
  51.9 0.8 %shard_map.119 = (f32[32,2048]{1,0:T(8,128)S(1)}, f32[32,2048]{1,0:T(8,128)S(1)}, bf16[32,2048]{1,0:T(8,128)(2,1)S(1)}) custom-call(bf16[96,2176]{1,0:T(8,128)(2,1)S(1)} %constant_dynamic-update-slice_fusion.rows, f32[2,96,384]{2,1,0:T(8,128)S(1)} %fusion.8.refs_0_, f32[2,96,384]{2,1,0:T(8,128)S(1)} %fusion.11.refs_1_, bf16[1,384,2048]{2,1,0:T(8,128)(2,1)S(1)} %copy-done, ...), custom_call_target="tpu_custom_call" | custom-call | flops 301989888 | bytes 2097152 | tf_op jit(solution)/shard_map/pallas_call | solution.py:371
  52.7 2.1 %collective-permute-start.16 = (bf16[32,2048]{1,0:T(8,128)(2,1)S(1)}, bf16[32,2048]{1,0:T(8,128)(2,1)S(1)}, u32[]{:S(2)}, u32[]{:S(2)}) collective-permute-start(bf16[32,2048]{1,0:T(8,128)(2,1)S(1)} %get-tuple-element.45), channel_id=1, source_target_pairs={{0,2},{1,3},{2,0},{3,1},{4,6},{5,7},{6,4},{7,5},{8,10},{9,11},{10,... | collective-permute-start | bytes 393224 | tf_op jit(solution)/shard_map/ppermute | solution.py:35
  54.8 0.1 collective-permute-start.19
  54.9 2.8 %collective-permute-done.16 = bf16[32,2048]{1,0:T(8,128)(2,1)S(1)} collective-permute-done((bf16[32,2048]{1,0:T(8,128)(2,1)S(1)}, bf16[32,2048]{1,0:T(8,128)(2,1)S(1)}, u32[]{:S(2)}, u32[]{:S(2)}) %collective-permute-start.16) | collective-permute-done | bytes 131104 | tf_op jit(solution)/shard_map/ppermute | solution.py:35
  57.8 0.1 collective-permute-start.17
  57.9 2.1 %collective-permute-start.18 = (bf16[16,2048]{1,0:T(8,128)(2,1)S(1)}, bf16[16,2048]{1,0:T(8,128)(2,1)S(1)}, u32[]{:S(2)}, u32[]{:S(2)}) collective-permute-start(bf16[16,2048]{1,0:T(8,128)(2,1)S(1)} %get-tuple-element.49), channel_id=1, source_target_pairs={{0,12},{4,8},{8,4},{12,0},{1,13},{5,9},{9,5},{13,1},{2,14},{6,10},... | collective-permute-start | bytes 196616 | tf_op jit(solution)/shard_map/ppermute | solution.py:35
  60.0 3.1 %collective-permute-done.17 = bf16[16,2048]{1,0:T(8,128)(2,1)S(1)} collective-permute-done((bf16[16,2048]{1,0:T(8,128)(2,1)S(1)}, bf16[16,2048]{1,0:T(8,128)(2,1)S(1)}, u32[]{:S(2)}, u32[]{:S(2)}) %collective-permute-start.17) | collective-permute-done | bytes 65568 | tf_op jit(solution)/shard_map/ppermute | solution.py:35
  63.0 1.0 %collective-permute-done.18 = bf16[16,2048]{1,0:T(8,128)(2,1)S(1)} collective-permute-done((bf16[16,2048]{1,0:T(8,128)(2,1)S(1)}, bf16[16,2048]{1,0:T(8,128)(2,1)S(1)}, u32[]{:S(2)}, u32[]{:S(2)}) %collective-permute-start.18) | collective-permute-done | bytes 65568 | tf_op jit(solution)/shard_map/ppermute | solution.py:35
  64.0 0.7 %fusion.24 = bf16[1,16,2048]{2,1,0:T(8,128)(2,1)} fusion(bf16[16,2048]{1,0:T(8,128)(2,1)S(1)} %collective-permute-done.19, bf16[16,2048]{1,0:T(8,128)(2,1)S(1)} %collective-permute-done.18, bf16[16,2048]{1,0:T(8,128)(2,1)S(1)} %collective-permute-done.17, f32[32,2048]{1,0:T(8,128)S(1)} %convert_add_fusion, bf16[16,2048]{1,0:T(8,128)(2,1)S(1)} %get-tuple-element.40), kind=kLoop, calls=%fused_computation.29 | loop fusion | flops 294912 | bytes 458752 | tf_op jit(solution)/shard_map/convert_element_type | solution.py:516
  (41 shorter events, 0.3 us)
Async XLA Ops:
  0.6 33.4 %collective-permute-start.8 = (bf16[1,2048,2,384]{3,2,1,0:T(2,128)(2,1)}, bf16[1,2048,2,384]{3,2,1,0:T(2,128)(2,1)S(1)}, u32[]{:S(2)}, u32[]{:S(2)}) collective-permute-start(bf16[1,2048,2,384]{3,2,1,0:T(2,128)(2,1)} %param.18), channel_id=1, source_target_pairs={{0,1},{1,0},{2,3},{3,2},{4,5},{5,4},{6,7},{7,6},{8,9},{9,8},{10,11... | collective-permute-start | bytes 9437192 | tf_op jit(solution)/shard_map/ppermute | solution.py:35
  2.2 9.4 %collective-permute-start.2 = (bf16[576,128]{1,0:T(8,128)(2,1)S(1)}, bf16[576,128]{1,0:T(8,128)(2,1)S(1)}, u32[]{:S(2)}, u32[]{:S(2)}) collective-permute-start(bf16[576,128]{1,0:T(8,128)(2,1)S(1)} %get-tuple-element.26.keys), channel_id=1, source_target_pairs={{0,4},{4,8},{8,12},{12,0},{1,5},{5,9},{9,13},{13,1},{2,6},{6,10},{... | collective-permute-start | bytes 442376 | tf_op jit(solution)/shard_map/ppermute | solution.py:40
  4.8 11.3 %collective-permute-start = (bf16[576,128]{1,0:T(8,128)(2,1)S(1)}, bf16[576,128]{1,0:T(8,128)(2,1)S(1)}, u32[]{:S(2)}, u32[]{:S(2)}) collective-permute-start(bf16[576,128]{1,0:T(8,128)(2,1)S(1)} %get-tuple-element.25.values), channel_id=1, source_target_pairs={{0,12},{4,0},{8,4},{12,8},{1,13},{5,1},{9,5},{13,9},{2,14},{6,2},{... | collective-permute-start | bytes 442376 | tf_op jit(solution)/shard_map/ppermute | solution.py:40
  6.9 2.2 %copy-start.1 = (bf16[1024,2048]{1,0:T(8,128)(2,1)S(1)}, bf16[1024,2048]{1,0:T(8,128)(2,1)}, u32[]{:S(2)}) copy-start(bf16[1024,2048]{1,0:T(8,128)(2,1)} %weight.3) | copy-start | bytes 12582916
  9.1 10.8 %copy-start.7 = (bf16[1,64,1024]{2,1,0:T(8,128)(2,1)S(1)}, bf16[1,64,1024]{2,1,0:T(8,128)(2,1)}, u32[]{:S(2)}) copy-start(bf16[1,64,1024]{2,1,0:T(8,128)(2,1)} %param.10) | copy-start | bytes 393220
  9.1 10.8 %copy-start.8 = (s32[1,4]{1,0:T(1,128)S(1)}, s32[1,4]{1,0:T(1,128)}, u32[]{:S(2)}) copy-start(s32[1,4]{1,0:T(1,128)} %param.12) | copy-start | bytes 52
  9.1 12.1 %collective-permute-start.4 = (bf16[576,128]{1,0:T(8,128)(2,1)S(1)}, bf16[576,128]{1,0:T(8,128)(2,1)S(1)}, u32[]{:S(2)}, u32[]{:S(2)}) collective-permute-start(bf16[576,128]{1,0:T(8,128)(2,1)S(1)} %get-tuple-element.25.values), channel_id=1, source_target_pairs={{0,4},{4,8},{8,12},{12,0},{1,5},{5,9},{9,13},{13,1},{2,6},{6,10},{... | collective-permute-start | bytes 442376 | tf_op jit(solution)/shard_map/ppermute | solution.py:40
  11.6 9.7 %collective-permute-start.5 = (bf16[576,128]{1,0:T(8,128)(2,1)S(1)}, bf16[576,128]{1,0:T(8,128)(2,1)S(1)}, u32[]{:S(2)}, u32[]{:S(2)}) collective-permute-start(bf16[576,128]{1,0:T(8,128)(2,1)S(1)} %get-tuple-element.26.keys), channel_id=1, source_target_pairs={{0,12},{4,0},{8,4},{12,8},{1,13},{5,1},{9,5},{13,9},{2,14},{6,2},{... | collective-permute-start | bytes 442376 | tf_op jit(solution)/shard_map/ppermute | solution.py:40
  16.1 8.6 %collective-permute-start.3 = (bf16[576,128]{1,0:T(8,128)(2,1)S(1)}, bf16[576,128]{1,0:T(8,128)(2,1)S(1)}, u32[]{:S(2)}, u32[]{:S(2)}) collective-permute-start(bf16[576,128]{1,0:T(8,128)(2,1)S(1)} %collective-permute-done.2.refs_0_), channel_id=1, source_target_pairs={{0,4},{4,8},{8,12},{12,0},{1,5},{5,9},{9,13},{13,1},{2,6},{6,10},{... | collective-permute-start | bytes 442376 | tf_op jit(solution)/shard_map/ppermute | solution.py:40
  16.1 10.5 %collective-permute-start.1 = (bf16[576,128]{1,0:T(8,128)(2,1)S(1)}, bf16[576,128]{1,0:T(8,128)(2,1)S(1)}, u32[]{:S(2)}, u32[]{:S(2)}) collective-permute-start(bf16[576,128]{1,0:T(8,128)(2,1)S(1)} %collective-permute-done.refs_3_), channel_id=1, source_target_pairs={{0,12},{4,0},{8,4},{12,8},{1,13},{5,1},{9,5},{13,9},{2,14},{6,2},{... | collective-permute-start | bytes 442376 | tf_op jit(solution)/shard_map/ppermute | solution.py:40
  19.9 6.7 %copy-start.2 = (bf16[1024,2048]{1,0:T(8,128)(2,1)S(1)}, bf16[1024,2048]{1,0:T(8,128)(2,1)}, u32[]{:S(2)}) copy-start(bf16[1024,2048]{1,0:T(8,128)(2,1)} %weight.3) | copy-start | bytes 12582916
  25.3 8.7 %copy-start.3 = (bf16[1,16,2048]{2,1,0:T(8,128)(2,1)S(1)}, bf16[1,16,2048]{2,1,0:T(8,128)(2,1)}, u32[]{:S(2)}) copy-start(bf16[1,16,2048]{2,1,0:T(8,128)(2,1)} %param.13) | copy-start | bytes 196612
  25.3 8.7 %copy-start.4 = (f32[2048]{0:T(1024)S(1)}, f32[2048]{0:T(1024)}, u32[]{:S(2)}) copy-start(f32[2048]{0:T(1024)} %param.15) | copy-start | bytes 24580
  25.4 8.7 %copy-start.5 = (s32[1,16,8]{1,2,0:T(8,128)S(1)}, s32[1,16,8]{1,2,0:T(8,128)}, u32[]{:S(2)}) copy-start(s32[1,16,8]{1,2,0:T(8,128)} %param.16) | copy-start | bytes 1540
  25.4 8.7 %copy-start.6 = (f32[1,16,8]{1,2,0:T(8,128)S(1)}, f32[1,16,8]{1,2,0:T(8,128)}, u32[]{:S(2)}) copy-start(f32[1,16,8]{1,2,0:T(8,128)} %param.17) | copy-start | bytes 1540
  28.3 7.2 %copy-start = (bf16[1,384,2048]{2,1,0:T(8,128)(2,1)S(1)}, bf16[1,384,2048]{2,1,0:T(8,128)(2,1)}, u32[]{:S(2)}) copy-start(bf16[1,384,2048]{2,1,0:T(8,128)(2,1)} %refs_2_.1) | copy-start | bytes 4718596
  28.3 1.3 %collective-permute-start.6 = (bf16[2,1,16,2048]{3,2,1,0:T(8,128)(2,1)S(1)}, bf16[2,1,16,2048]{3,2,1,0:T(8,128)(2,1)S(1)}, u32[]{:S(2)}, u32[]{:S(2)}) collective-permute-start(bf16[2,1,16,2048]{3,2,1,0:T(8,128)(2,1)S(1)} %bitcast.54), channel_id=1, source_target_pairs={{0,1},{1,0},{2,3},{3,2},{4,5},{5,4},{6,7},{7,6},{8,9},{9,8},{10,11... | collective-permute-start | bytes 393224 | tf_op jit(solution)/shard_map/ppermute | solution.py:35
  29.7 4.3 %collective-permute-start.7 = (bf16[1,1,16,2048]{3,2,1,0:T(8,128)(2,1)S(1)}, bf16[1,1,16,2048]{3,2,1,0:T(8,128)(2,1)S(1)}, u32[]{:S(2)}, u32[]{:S(2)}) collective-permute-start(bf16[1,1,16,2048]{3,2,1,0:T(8,128)(2,1)S(1)} %slice.79), channel_id=1, source_target_pairs={{0,2},{1,3},{2,0},{3,1},{4,6},{5,7},{6,4},{7,5},{8,10},{9,11},{10,... | collective-permute-start | bytes 196616 | tf_op jit(solution)/shard_map/ppermute | solution.py:35
  34.3 12.9 %copy-start.9 = (bf16[1,2048,2,384]{3,2,1,0:T(2,128)(2,1)S(1)}, bf16[1,2048,2,384]{3,2,1,0:T(2,128)(2,1)}, u32[]{:S(2)}) copy-start(bf16[1,2048,2,384]{3,2,1,0:T(2,128)(2,1)} %param.18) | copy-start | bytes 9437188
  34.3 4.4 %collective-permute-start.11 = (bf16[16,2176]{1,0:T(8,128)(2,1)S(1)}, bf16[16,2176]{1,0:T(8,128)(2,1)S(1)}, u32[]{:S(2)}, u32[]{:S(2)}) collective-permute-start(bf16[16,2176]{1,0:T(8,128)(2,1)S(1)} %get-tuple-element.41), channel_id=1, source_target_pairs={{0,4},{4,0},{8,12},{12,8},{1,5},{5,1},{9,13},{13,9},{2,6},{6,2},{1... | collective-permute-start | bytes 208904 | tf_op jit(solution)/shard_map/ppermute | solution.py:35
  35.5 12.3 %collective-permute-start.13 = (bf16[1,384,2048]{2,1,0:T(8,128)(2,1)S(1)}, bf16[1,384,2048]{2,1,0:T(8,128)(2,1)S(1)}, u32[]{:S(2)}, u32[]{:S(2)}) collective-permute-start(bf16[1,384,2048]{2,1,0:T(8,128)(2,1)S(1)} %copy-done), channel_id=1, source_target_pairs={{0,1},{1,0},{2,3},{3,2},{4,5},{5,4},{6,7},{7,6},{8,9},{9,8},{10,11... | collective-permute-start | bytes 4718600 | tf_op jit(solution)/shard_map/ppermute | solution.py:35
  35.5 6.9 %collective-permute-start.10 = (bf16[16,2176]{1,0:T(8,128)(2,1)S(1)}, bf16[16,2176]{1,0:T(8,128)(2,1)S(1)}, u32[]{:S(2)}, u32[]{:S(2)}) collective-permute-start(bf16[16,2176]{1,0:T(8,128)(2,1)S(1)} %get-tuple-element.41), channel_id=1, source_target_pairs={{0,12},{4,8},{8,4},{12,0},{1,13},{5,9},{9,5},{13,1},{2,14},{6,10},... | collective-permute-start | bytes 208904 | tf_op jit(solution)/shard_map/ppermute | solution.py:35
  37.1 7.8 %collective-permute-start.9 = (bf16[16,2176]{1,0:T(8,128)(2,1)S(1)}, bf16[16,2176]{1,0:T(8,128)(2,1)S(1)}, u32[]{:S(2)}, u32[]{:S(2)}) collective-permute-start(bf16[16,2176]{1,0:T(8,128)(2,1)S(1)} %get-tuple-element.41), channel_id=1, source_target_pairs={{0,8},{4,12},{8,0},{12,4},{1,9},{5,13},{9,1},{13,5},{2,10},{6,14},... | collective-permute-start | bytes 208904 | tf_op jit(solution)/shard_map/ppermute | solution.py:35
  38.7 7.8 %collective-permute-start.14 = (bf16[32,2176]{1,0:T(8,128)(2,1)S(1)}, bf16[32,2176]{1,0:T(8,128)(2,1)S(1)}, u32[]{:S(2)}, u32[]{:S(2)}) collective-permute-start(bf16[32,2176]{1,0:T(8,128)(2,1)S(1)} %pad_maximum_fusion.1), channel_id=1, source_target_pairs={{0,2},{1,3},{2,0},{3,1},{4,6},{5,7},{6,4},{7,5},{8,10},{9,11},{10,... | collective-permute-start | bytes 417800 | tf_op jit(solution)/shard_map/ppermute | solution.py:35
  44.9 5.7 %collective-permute-start.12 = (bf16[32,2176]{1,0:T(8,128)(2,1)S(1)}, bf16[32,2176]{1,0:T(8,128)(2,1)S(1)}, u32[]{:S(2)}, u32[]{:S(2)}) collective-permute-start(bf16[32,2176]{1,0:T(8,128)(2,1)S(1)} %pad_maximum_fusion), channel_id=1, source_target_pairs={{0,2},{1,3},{2,0},{3,1},{4,6},{5,7},{6,4},{7,5},{8,10},{9,11},{10,... | collective-permute-start | bytes 417800 | tf_op jit(solution)/shard_map/ppermute | solution.py:35
  48.5 6.2 %collective-permute-start.15 = (bf16[32,2048]{1,0:T(8,128)(2,1)S(1)}, bf16[32,2048]{1,0:T(8,128)(2,1)S(1)}, u32[]{:S(2)}, u32[]{:S(2)}) collective-permute-start(bf16[32,2048]{1,0:T(8,128)(2,1)S(1)} %shard_map.120), channel_id=1, source_target_pairs={{0,2},{1,3},{2,0},{3,1},{4,6},{5,7},{6,4},{7,5},{8,10},{9,11},{10,... | collective-permute-start | bytes 393224 | tf_op jit(solution)/shard_map/ppermute | solution.py:35
  52.7 5.0 %collective-permute-start.16 = (bf16[32,2048]{1,0:T(8,128)(2,1)S(1)}, bf16[32,2048]{1,0:T(8,128)(2,1)S(1)}, u32[]{:S(2)}, u32[]{:S(2)}) collective-permute-start(bf16[32,2048]{1,0:T(8,128)(2,1)S(1)} %get-tuple-element.45), channel_id=1, source_target_pairs={{0,2},{1,3},{2,0},{3,1},{4,6},{5,7},{6,4},{7,5},{8,10},{9,11},{10,... | collective-permute-start | bytes 393224 | tf_op jit(solution)/shard_map/ppermute | solution.py:35
  54.8 5.1 %collective-permute-start.19 = (bf16[16,2048]{1,0:T(8,128)(2,1)S(1)}, bf16[16,2048]{1,0:T(8,128)(2,1)S(1)}, u32[]{:S(2)}, u32[]{:S(2)}) collective-permute-start(bf16[16,2048]{1,0:T(8,128)(2,1)S(1)} %slice.78), channel_id=1, source_target_pairs={{0,4},{4,0},{8,12},{12,8},{1,5},{5,1},{9,13},{13,9},{2,6},{6,2},{1... | collective-permute-start | bytes 196616 | tf_op jit(solution)/shard_map/ppermute | solution.py:35
  57.8 5.3 %collective-permute-start.17 = (bf16[16,2048]{1,0:T(8,128)(2,1)S(1)}, bf16[16,2048]{1,0:T(8,128)(2,1)S(1)}, u32[]{:S(2)}, u32[]{:S(2)}) collective-permute-start(bf16[16,2048]{1,0:T(8,128)(2,1)S(1)} %get-tuple-element.48), channel_id=1, source_target_pairs={{0,8},{4,12},{8,0},{12,4},{1,9},{5,13},{9,1},{13,5},{2,10},{6,14},... | collective-permute-start | bytes 196616 | tf_op jit(solution)/shard_map/ppermute | solution.py:35
  57.9 6.2 %collective-permute-start.18 = (bf16[16,2048]{1,0:T(8,128)(2,1)S(1)}, bf16[16,2048]{1,0:T(8,128)(2,1)S(1)}, u32[]{:S(2)}, u32[]{:S(2)}) collective-permute-start(bf16[16,2048]{1,0:T(8,128)(2,1)S(1)} %get-tuple-element.49), channel_id=1, source_target_pairs={{0,12},{4,8},{8,4},{12,0},{1,13},{5,9},{9,5},{13,1},{2,14},{6,10},... | collective-permute-start | bytes 196616 | tf_op jit(solution)/shard_map/ppermute | solution.py:35

commit v19 on v18

--- a/solution.py
+++ b/solution.py
@@ -402,15 +402,18 @@
     far = strides(lax.axis_size("exp"))[:1]
     chunks = chunks_of(lax.axis_size("ctx"))
 
-    joined = [
-        jnp.concatenate(
-            [rows if offset == 0 else swap(rows, "ctx", offset) for offset in chunk], axis=0
-        )
+    blocks = [
+        [rows if offset == 0 else swap(rows, "ctx", offset) for offset in chunk]
         for chunk in chunks
     ]
+    joined = [jnp.concatenate(parts, axis=0) for parts in blocks]
     crossed = []
-    for piece in joined if far else []:
-        crossed.append(swap(piece, "exp", far[0]))
+    if far:
+        near = swap(joined[-1], "exp", far[0])
+        for parts in blocks[:-1]:
+            parts[0], _ = lax.optimization_barrier((parts[0], near))
+            crossed.append(jnp.concatenate([swap(part, "exp", far[0]) for part in parts], axis=0))
+        crossed.append(near)
     *homes, first = expert_apply(
         joined + (crossed or joined)[:1], [jnp.float32] * len(joined) + [jnp.bfloat16], weights
     )

time: 64.9 us -> 65.7 us (1.012)
  starting transfers between devices: 26.7 us -> 30.9 us
  waiting for transfers between devices: 23.7 us -> 20.3 us
    ppermute x14 -> x15, starting transfers between devices: 13.7 us -> 17.8 us  [swap(): lax.ppermute(value, axis, [(i, i ^ stride) for i in range(lax.axis_size(a...]
    ppermute x14 -> x15, waiting for transfers between devices: 18 us -> 14.6 us  [swap(): lax.ppermute(value, axis, [(i, i ^ stride) for i in range(lax.axis_size(a...]
    unnamed x25 -> x26, local copies, waits for them, and re-layouts: 3.27 us -> 3.29 us
  transfers between devices with their start and end apart: 20 -> 21, of which waited for: 13 -> 14; matrix products, arithmetic and copies ran while one was open for 6% -> 6% of each run, Pallas kernels for 10% -> 10%
where the time goes in v19:
time: 65.7 us; the launch traced here: 65.5 us
  starting transfers between devices  30.9 us (47%)
  waiting for transfers between devices  20.3 us (31%)
  Pallas kernels  6.7 us (10%)
  local copies, waits for them, and re-layouts  3.36 us (5%)
  matrix products  2.61 us (4%)
  between operations  0.84 us (1%)
  other arithmetic  0.77 us (1%)
    ppermute x15, starting transfers between devices, swap(): lax.ppermute(value, axis, [(i, i ^ stride) for i in range(lax.axis_size(a...  17.8 us
    ppermute x15, waiting for transfers between devices, swap(): lax.ppermute(value, axis, [(i, i ^ stride) for i in range(lax.axis_size(a...  14.6 us
    ppermute x6, starting transfers between devices, shift(): lax.ppermute(value, axis, [(i, (i + step) % count) for i in range(count)])  13.1 us
    ppermute x6, waiting for transfers between devices, shift(): lax.ppermute(value, axis, [(i, (i + step) % count) for i in range(count)])  5.72 us
    unnamed x26, local copies, waits for them, and re-layouts  3.29 us
    dot_general x4, matrix products, expert_apply(): jnp.einsum('nd,dgh->gnh', rows[:, :width], gate_up[0], preferred_element_...  2.61 us
    pallas_call x1, Pallas kernels, attention(): pl.pallas_call(functools.partial(late_kernel, fresh_block), out_shape=sha...  1.68 us
    pallas_call x2, Pallas kernels, expert_apply(): pl.pallas_call(functools.partial(down_kernel, [offset for offset, _, _ in...  1.44 us
  transfers between devices with their start and end apart: 21, of which 14 were waited for; matrix products, arithmetic and copies ran while one was open for 6% of the time, Pallas kernels for 10%

profile of v19, /device:TPU:0, one launch (start us, length us, event | category | flops | bytes accessed | tf_op | source)
XLA Modules:
  0.0 65.5 jit_solution(9472207494068213705)
XLA Ops:
  0.6 0.5 collective-permute-start.8
  1.1 1.0 %copy.34 = bf16[1,576,2,128]{3,1,2,0:T(8,128)(2,1)S(1)} copy(bf16[1,576,2,128]{3,2,1,0:T(2,128)(2,1)} %param.11) | data formatting | bytes 589824 | tf_op args[1]
  2.2 2.6 %collective-permute-start.2 = (bf16[576,128]{1,0:T(8,128)(2,1)S(1)}, bf16[576,128]{1,0:T(8,128)(2,1)S(1)}, u32[]{:S(2)}, u32[]{:S(2)}) collective-permute-start(bf16[576,128]{1,0:T(8,128)(2,1)S(1)} %get-tuple-element.27.keys), channel_id=1, source_target_pairs={{0,4},{4,8},{8,12},{12,0},{1,5},{5,9},{9,13},{13,1},{2,6},{6,10},{... | collective-permute-start | bytes 442376 | tf_op jit(solution)/shard_map/ppermute | solution.py:40
  4.8 2.1 %collective-permute-start = (bf16[576,128]{1,0:T(8,128)(2,1)S(1)}, bf16[576,128]{1,0:T(8,128)(2,1)S(1)}, u32[]{:S(2)}, u32[]{:S(2)}) collective-permute-start(bf16[576,128]{1,0:T(8,128)(2,1)S(1)} %get-tuple-element.26.values), channel_id=1, source_target_pairs={{0,12},{4,0},{8,4},{12,8},{1,13},{5,1},{9,5},{13,9},{2,14},{6,2},{... | collective-permute-start | bytes 442376 | tf_op jit(solution)/shard_map/ppermute | solution.py:40
  6.9 2.2 %copy-done.1 = bf16[1024,2048]{1,0:T(8,128)(2,1)S(1)} copy-done((bf16[1024,2048]{1,0:T(8,128)(2,1)S(1)}, bf16[1024,2048]{1,0:T(8,128)(2,1)}, u32[]{:S(2)}) %copy-start.1) | copy-done | bytes 4194328
  9.1 2.5 %collective-permute-done.2.refs_0_ = bf16[576,128]{1,0:T(8,128)(2,1)S(1)} collective-permute-done((bf16[576,128]{1,0:T(8,128)(2,1)S(1)}, bf16[576,128]{1,0:T(8,128)(2,1)S(1)}, u32[]{:S(2)}, u32[]{:S(2)}) %collective-permute-start.2) | collective-permute-done | bytes 147488 | tf_op jit(solution)/shard_map/ppermute | solution.py:40
  11.6 4.5 %collective-permute-start.5 = (bf16[576,128]{1,0:T(8,128)(2,1)S(1)}, bf16[576,128]{1,0:T(8,128)(2,1)S(1)}, u32[]{:S(2)}, u32[]{:S(2)}) collective-permute-start(bf16[576,128]{1,0:T(8,128)(2,1)S(1)} %get-tuple-element.27.keys), channel_id=1, source_target_pairs={{0,12},{4,0},{8,4},{12,8},{1,13},{5,1},{9,5},{13,9},{2,14},{6,2},{... | collective-permute-start | bytes 442376 | tf_op jit(solution)/shard_map/ppermute | solution.py:40
  16.1 3.8 %collective-permute-start.1 = (bf16[576,128]{1,0:T(8,128)(2,1)S(1)}, bf16[576,128]{1,0:T(8,128)(2,1)S(1)}, u32[]{:S(2)}, u32[]{:S(2)}) collective-permute-start(bf16[576,128]{1,0:T(8,128)(2,1)S(1)} %collective-permute-done.refs_3_), channel_id=1, source_target_pairs={{0,12},{4,0},{8,4},{12,8},{1,13},{5,1},{9,5},{13,9},{2,14},{6,2},{... | collective-permute-start | bytes 442376 | tf_op jit(solution)/shard_map/ppermute | solution.py:40
  19.9 1.3 %shard_map.114 = (f32[1,512]{1,0:T(1,128)S(1)}, f32[1,512]{1,0:T(1,128)S(1)}, f32[128,512]{1,0:T(8,128)S(1)}, s32[4,128]{1,0:T(4,128)S(1)}) custom-call(s32[4]{0:T(128)S(1)} %bitcast.55, bf16[64,1024]{1,0:T(8,128)(2,1)S(1)} %bitcast.51, bf16[576,128]{1,0:T(8,128)(2,1)S(1)} %get-tuple-element.27.keys, bf16[576,128]{1,0:T(8,128)(2,1)S(1)} %get-tuple-element.26.values, ...), custom_call_target="tpu_custom_call" | custom-call | flops 2415919104 | bytes 8388608 | tf_op jit(solution)/shard_map/pallas_call | solution.py:239
  21.3 0.1 collective-permute-done.5.refs_2_
  21.3 1.4 %shard_map.115 = (f32[1,512]{1,0:T(1,128)S(1)}, f32[1,512]{1,0:T(1,128)S(1)}, f32[128,512]{1,0:T(8,128)S(1)}) custom-call(bf16[64,1024]{1,0:T(8,128)(2,1)S(1)} %bitcast.52, s32[4,128]{1,0:T(4,128)S(1)} %get-tuple-element.25.lengths, bf16[576,128]{1,0:T(8,128)(2,1)S(1)} %collective-permute-done.2.refs_0_, ...), custom_call_target="tpu_custom_call" | custom-call | flops 301989888 | bytes 2097152 | tf_op jit(solution)/shard_map/pallas_call | solution.py:254
  22.8 2.0 %collective-permute-done.3.keys = bf16[576,128]{1,0:T(8,128)(2,1)S(1)} collective-permute-done((bf16[576,128]{1,0:T(8,128)(2,1)S(1)}, bf16[576,128]{1,0:T(8,128)(2,1)S(1)}, u32[]{:S(2)}, u32[]{:S(2)}) %collective-permute-start.3) | collective-permute-done | bytes 147488 | tf_op jit(solution)/shard_map/ppermute | solution.py:40
  24.7 0.6 shard_map.116
  25.3 0.0 copy-start.4
  25.4 0.0 copy-start.5
  25.4 0.0 copy-start.6
  25.4 1.2 %collective-permute-done.1.values = bf16[576,128]{1,0:T(8,128)(2,1)S(1)} collective-permute-done((bf16[576,128]{1,0:T(8,128)(2,1)S(1)}, bf16[576,128]{1,0:T(8,128)(2,1)S(1)}, u32[]{:S(2)}, u32[]{:S(2)}) %collective-permute-start.1) | collective-permute-done | bytes 147488 | tf_op jit(solution)/shard_map/ppermute | solution.py:40
  26.6 1.7 %shard_map.117 = (bf16[64,1024]{1,0:T(8,128)(2,1)}, f32[32,2048]{1,0:T(8,128)S(1)}, bf16[32,2048]{1,0:T(8,128)(2,1)S(1)}) custom-call(bf16[576,128]{1,0:T(8,128)(2,1)S(1)} %collective-permute-done.1.values, f32[1,512]{1,0:T(1,128)S(1)} %get-tuple-element.35.last_peak, f32[1,512]{1,0:T(1,128)S(1)} %get-tuple-element.36.last_total, ...), custom_call_target="tpu_custom_call" | custom-call | flops 419430400 | bytes 6291456 | tf_op jit(solution)/shard_map/pallas_call | solution.py:282
  28.3 1.3 %collective-permute-done.6 = bf16[2,1,16,2048]{3,2,1,0:T(8,128)(2,1)S(1)} collective-permute-done((bf16[2,1,16,2048]{3,2,1,0:T(8,128)(2,1)S(1)}, bf16[2,1,16,2048]{3,2,1,0:T(8,128)(2,1)S(1)}, u32[]{:S(2)}, u32[]{:S(2)}) %collective-permute-start.6) | collective-permute-done | bytes 131104 | tf_op jit(solution)/shard_map/ppermute | solution.py:35
  29.7 1.6 %collective-permute-start.7 = (bf16[1,1,16,2048]{3,2,1,0:T(8,128)(2,1)S(1)}, bf16[1,1,16,2048]{3,2,1,0:T(8,128)(2,1)S(1)}, u32[]{:S(2)}, u32[]{:S(2)}) collective-permute-start(bf16[1,1,16,2048]{3,2,1,0:T(8,128)(2,1)S(1)} %slice.79), channel_id=1, source_target_pairs={{0,2},{1,3},{2,0},{3,1},{4,6},{5,7},{6,4},{7,5},{8,10},{9,11},{10,... | collective-permute-start | bytes 196616 | tf_op jit(solution)/shard_map/ppermute | solution.py:35
  31.2 2.8 %collective-permute-done.7 = bf16[1,1,16,2048]{3,2,1,0:T(8,128)(2,1)S(1)} collective-permute-done((bf16[1,1,16,2048]{3,2,1,0:T(8,128)(2,1)S(1)}, bf16[1,1,16,2048]{3,2,1,0:T(8,128)(2,1)S(1)}, u32[]{:S(2)}, u32[]{:S(2)}) %collective-permute-start.7) | collective-permute-done | bytes 65568 | tf_op jit(solution)/shard_map/ppermute | solution.py:35
  34.0 0.2 shard_map.118
  34.3 1.2 %collective-permute-start.11 = (bf16[16,2176]{1,0:T(8,128)(2,1)S(1)}, bf16[16,2176]{1,0:T(8,128)(2,1)S(1)}, u32[]{:S(2)}, u32[]{:S(2)}) collective-permute-start(bf16[16,2176]{1,0:T(8,128)(2,1)S(1)} %get-tuple-element.42), channel_id=1, source_target_pairs={{0,4},{4,0},{8,12},{12,8},{1,5},{5,1},{9,13},{13,9},{2,6},{6,2},{1... | collective-permute-start | bytes 208904 | tf_op jit(solution)/shard_map/ppermute | solution.py:35
  35.5 1.6 %collective-permute-start.10 = (bf16[16,2176]{1,0:T(8,128)(2,1)S(1)}, bf16[16,2176]{1,0:T(8,128)(2,1)S(1)}, u32[]{:S(2)}, u32[]{:S(2)}) collective-permute-start(bf16[16,2176]{1,0:T(8,128)(2,1)S(1)} %get-tuple-element.42), channel_id=1, source_target_pairs={{0,12},{4,8},{8,4},{12,0},{1,13},{5,9},{9,5},{13,1},{2,14},{6,10},... | collective-permute-start | bytes 208904 | tf_op jit(solution)/shard_map/ppermute | solution.py:35
  37.1 0.8 %collective-permute-start.9 = (bf16[16,2176]{1,0:T(8,128)(2,1)S(1)}, bf16[16,2176]{1,0:T(8,128)(2,1)S(1)}, u32[]{:S(2)}, u32[]{:S(2)}) collective-permute-start(bf16[16,2176]{1,0:T(8,128)(2,1)S(1)} %get-tuple-element.42), channel_id=1, source_target_pairs={{0,8},{4,12},{8,0},{12,4},{1,9},{5,13},{9,1},{13,5},{2,10},{6,14},... | collective-permute-start | bytes 208904 | tf_op jit(solution)/shard_map/ppermute | solution.py:35
  37.9 0.8 %collective-permute-done.11 = bf16[16,2176]{1,0:T(8,128)(2,1)S(1)} collective-permute-done((bf16[16,2176]{1,0:T(8,128)(2,1)S(1)}, bf16[16,2176]{1,0:T(8,128)(2,1)S(1)}, u32[]{:S(2)}, u32[]{:S(2)}) %collective-permute-start.11) | collective-permute-done | bytes 69664 | tf_op jit(solution)/shard_map/ppermute | solution.py:35
  38.7 1.6 %collective-permute-start.12 = (bf16[32,2176]{1,0:T(8,128)(2,1)S(1)}, bf16[32,2176]{1,0:T(8,128)(2,1)S(1)}, u32[]{:S(2)}, u32[]{:S(2)}) collective-permute-start(bf16[32,2176]{1,0:T(8,128)(2,1)S(1)} %pad_maximum_fusion), channel_id=1, source_target_pairs={{0,2},{1,3},{2,0},{3,1},{4,6},{5,7},{6,4},{7,5},{8,10},{9,11},{10,... | collective-permute-start | bytes 417800 | tf_op jit(solution)/shard_map/ppermute | solution.py:35
  40.2 2.1 %collective-permute-done.10 = bf16[16,2176]{1,0:T(8,128)(2,1)S(1)} collective-permute-done((bf16[16,2176]{1,0:T(8,128)(2,1)S(1)}, bf16[16,2176]{1,0:T(8,128)(2,1)S(1)}, u32[]{:S(2)}, u32[]{:S(2)}) %collective-permute-start.10) | collective-permute-done | bytes 69664 | tf_op jit(solution)/shard_map/ppermute | solution.py:35
  42.4 1.5 %collective-permute-start.14 = (bf16[16,2176]{1,0:T(8,128)(2,1)S(1)}, bf16[16,2176]{1,0:T(8,128)(2,1)S(1)}, u32[]{:S(2)}, u32[]{:S(2)}) collective-permute-start(bf16[16,2176]{1,0:T(8,128)(2,1)S(1)} %collective-permute-done.10), channel_id=1, source_target_pairs={{0,2},{1,3},{2,0},{3,1},{4,6},{5,7},{6,4},{7,5},{8,10},{9,11},{10,... | collective-permute-start | bytes 208904 | tf_op jit(solution)/shard_map/ppermute | solution.py:35
  43.9 1.0 %collective-permute-done.9 = bf16[16,2176]{1,0:T(8,128)(2,1)S(1)} collective-permute-done((bf16[16,2176]{1,0:T(8,128)(2,1)S(1)}, bf16[16,2176]{1,0:T(8,128)(2,1)S(1)}, u32[]{:S(2)}, u32[]{:S(2)}) %collective-permute-start.9) | collective-permute-done | bytes 69664 | tf_op jit(solution)/shard_map/ppermute | solution.py:35
  45.0 1.6 %collective-permute-start.13 = (bf16[16,2176]{1,0:T(8,128)(2,1)S(1)}, bf16[16,2176]{1,0:T(8,128)(2,1)S(1)}, u32[]{:S(2)}, u32[]{:S(2)}) collective-permute-start(bf16[16,2176]{1,0:T(8,128)(2,1)S(1)} %collective-permute-done.9), channel_id=1, source_target_pairs={{0,2},{1,3},{2,0},{3,1},{4,6},{5,7},{6,4},{7,5},{8,10},{9,11},{10,... | collective-permute-start | bytes 208904 | tf_op jit(solution)/shard_map/ppermute | solution.py:35
  46.5 0.6 fusion.17.refs_1_
  47.2 0.7 %fusion.14.refs_0_ = f32[2,32,384]{2,1,0:T(8,128)S(1)} fusion(bf16[2048,2,384]{2,1,0:T(2,128)(2,1)S(1)} %bitcast.57, bf16[32,2176]{1,0:T(8,128)(2,1)S(1)} %collective-permute-done.12.rows), kind=kOutput, calls=%fused_computation.10 | convolution fusion | flops 100663296 | bytes 3375104 | tf_op jit(solution)/shard_map/nd,dgh->gnh/dot_general | solution.py:367
  47.8 0.7 %shard_map.120 = bf16[32,2048]{1,0:T(8,128)(2,1)S(1)} custom-call(bf16[32,2176]{1,0:T(8,128)(2,1)S(1)} %collective-permute-done.12.rows, f32[2,32,384]{2,1,0:T(8,128)S(1)} %fusion.14.refs_0_, f32[2,32,384]{2,1,0:T(8,128)S(1)} %fusion.17.refs_1_, bf16[1,384,2048]{2,1,0:T(8,128)(2,1)S(1)} %copy-done, bf16[1,384,2048]{2,1,0:T(8,128)(2,1)S(1)} %collective-permute-done.15.refs_3_), custom_call_target="tpu_custom_call" | custom-call | flops 100663296 | bytes 2097152 | tf_op jit(solution)/shard_map/pallas_call | solution.py:371
  48.5 0.6 collective-permute-start.16
  49.1 0.2 collective-permute-done.13
  49.4 0.7 fusion.11.refs_1_
  50.0 0.7 %fusion.8.refs_0_ = f32[2,96,384]{2,1,0:T(8,128)S(1)} fusion(bf16[2048,2,384]{2,1,0:T(2,128)(2,1)S(1)} %bitcast.58, bf16[96,2176]{1,0:T(8,128)(2,1)S(1)} %constant_dynamic-update-slice_fusion.rows), kind=kOutput, calls=%fused_computation.8 | convolution fusion | flops 301989888 | bytes 3833856 | tf_op jit(solution)/shard_map/nd,dgh->gnh/dot_general | solution.py:367
  50.7 0.8 %shard_map.119 = (f32[32,2048]{1,0:T(8,128)S(1)}, f32[32,2048]{1,0:T(8,128)S(1)}, bf16[32,2048]{1,0:T(8,128)(2,1)S(1)}) custom-call(bf16[96,2176]{1,0:T(8,128)(2,1)S(1)} %constant_dynamic-update-slice_fusion.rows, f32[2,96,384]{2,1,0:T(8,128)S(1)} %fusion.8.refs_0_, f32[2,96,384]{2,1,0:T(8,128)S(1)} %fusion.11.refs_1_, bf16[1,384,2048]{2,1,0:T(8,128)(2,1)S(1)} %copy-done, ...), custom_call_target="tpu_custom_call" | custom-call | flops 301989888 | bytes 2097152 | tf_op jit(solution)/shard_map/pallas_call | solution.py:371
  51.4 1.6 %collective-permute-start.17 = (bf16[32,2048]{1,0:T(8,128)(2,1)S(1)}, bf16[32,2048]{1,0:T(8,128)(2,1)S(1)}, u32[]{:S(2)}, u32[]{:S(2)}) collective-permute-start(bf16[32,2048]{1,0:T(8,128)(2,1)S(1)} %get-tuple-element.47), channel_id=1, source_target_pairs={{0,2},{1,3},{2,0},{3,1},{4,6},{5,7},{6,4},{7,5},{8,10},{9,11},{10,... | collective-permute-start | bytes 393224 | tf_op jit(solution)/shard_map/ppermute | solution.py:35
  53.0 1.1 %collective-permute-done.16 = bf16[32,2048]{1,0:T(8,128)(2,1)S(1)} collective-permute-done((bf16[32,2048]{1,0:T(8,128)(2,1)S(1)}, bf16[32,2048]{1,0:T(8,128)(2,1)S(1)}, u32[]{:S(2)}, u32[]{:S(2)}) %collective-permute-start.16) | collective-permute-done | bytes 131104 | tf_op jit(solution)/shard_map/ppermute | solution.py:35
  54.1 1.7 %collective-permute-start.20 = (bf16[16,2048]{1,0:T(8,128)(2,1)S(1)}, bf16[16,2048]{1,0:T(8,128)(2,1)S(1)}, u32[]{:S(2)}, u32[]{:S(2)}) collective-permute-start(bf16[16,2048]{1,0:T(8,128)(2,1)S(1)} %slice.78), channel_id=1, source_target_pairs={{0,4},{4,0},{8,12},{12,8},{1,5},{5,1},{9,13},{13,9},{2,6},{6,2},{1... | collective-permute-start | bytes 196616 | tf_op jit(solution)/shard_map/ppermute | solution.py:35
  55.8 0.7 %collective-permute-done.17 = bf16[32,2048]{1,0:T(8,128)(2,1)S(1)} collective-permute-done((bf16[32,2048]{1,0:T(8,128)(2,1)S(1)}, bf16[32,2048]{1,0:T(8,128)(2,1)S(1)}, u32[]{:S(2)}, u32[]{:S(2)}) %collective-permute-start.17) | collective-permute-done | bytes 131104 | tf_op jit(solution)/shard_map/ppermute | solution.py:35
  56.6 2.2 %collective-permute-start.18 = (bf16[16,2048]{1,0:T(8,128)(2,1)S(1)}, bf16[16,2048]{1,0:T(8,128)(2,1)S(1)}, u32[]{:S(2)}, u32[]{:S(2)}) collective-permute-start(bf16[16,2048]{1,0:T(8,128)(2,1)S(1)} %get-tuple-element.50), channel_id=1, source_target_pairs={{0,8},{4,12},{8,0},{12,4},{1,9},{5,13},{9,1},{13,5},{2,10},{6,14},... | collective-permute-start | bytes 196616 | tf_op jit(solution)/shard_map/ppermute | solution.py:35
  58.8 1.6 %collective-permute-start.19 = (bf16[16,2048]{1,0:T(8,128)(2,1)S(1)}, bf16[16,2048]{1,0:T(8,128)(2,1)S(1)}, u32[]{:S(2)}, u32[]{:S(2)}) collective-permute-start(bf16[16,2048]{1,0:T(8,128)(2,1)S(1)} %get-tuple-element.51), channel_id=1, source_target_pairs={{0,12},{4,8},{8,4},{12,0},{1,13},{5,9},{9,5},{13,1},{2,14},{6,10},... | collective-permute-start | bytes 196616 | tf_op jit(solution)/shard_map/ppermute | solution.py:35
  60.4 2.5 %collective-permute-done.18 = bf16[16,2048]{1,0:T(8,128)(2,1)S(1)} collective-permute-done((bf16[16,2048]{1,0:T(8,128)(2,1)S(1)}, bf16[16,2048]{1,0:T(8,128)(2,1)S(1)}, u32[]{:S(2)}, u32[]{:S(2)}) %collective-permute-start.18) | collective-permute-done | bytes 65568 | tf_op jit(solution)/shard_map/ppermute | solution.py:35
  62.9 2.0 %collective-permute-done.19 = bf16[16,2048]{1,0:T(8,128)(2,1)S(1)} collective-permute-done((bf16[16,2048]{1,0:T(8,128)(2,1)S(1)}, bf16[16,2048]{1,0:T(8,128)(2,1)S(1)}, u32[]{:S(2)}, u32[]{:S(2)}) %collective-permute-start.19) | collective-permute-done | bytes 65568 | tf_op jit(solution)/shard_map/ppermute | solution.py:35
  64.9 0.7 %fusion.24 = bf16[1,16,2048]{2,1,0:T(8,128)(2,1)} fusion(bf16[16,2048]{1,0:T(8,128)(2,1)S(1)} %collective-permute-done.20, bf16[16,2048]{1,0:T(8,128)(2,1)S(1)} %collective-permute-done.19, bf16[16,2048]{1,0:T(8,128)(2,1)S(1)} %collective-permute-done.18, f32[32,2048]{1,0:T(8,128)S(1)} %convert_add_fusion, bf16[16,2048]{1,0:T(8,128)(2,1)S(1)} %get-tuple-element.41), kind=kLoop, calls=%fused_computation.28 | loop fusion | flops 294912 | bytes 458752 | tf_op jit(solution)/shard_map/convert_element_type | solution.py:519
  (43 shorter events, 0.3 us)
Async XLA Ops:
  0.6 33.4 %collective-permute-start.8 = (bf16[1,2048,2,384]{3,2,1,0:T(2,128)(2,1)}, bf16[1,2048,2,384]{3,2,1,0:T(2,128)(2,1)S(1)}, u32[]{:S(2)}, u32[]{:S(2)}) collective-permute-start(bf16[1,2048,2,384]{3,2,1,0:T(2,128)(2,1)} %param.18), channel_id=1, source_target_pairs={{0,1},{1,0},{2,3},{3,2},{4,5},{5,4},{6,7},{7,6},{8,9},{9,8},{10,11... | collective-permute-start | bytes 9437192 | tf_op jit(solution)/shard_map/ppermute | solution.py:35
  2.2 9.4 %collective-permute-start.2 = (bf16[576,128]{1,0:T(8,128)(2,1)S(1)}, bf16[576,128]{1,0:T(8,128)(2,1)S(1)}, u32[]{:S(2)}, u32[]{:S(2)}) collective-permute-start(bf16[576,128]{1,0:T(8,128)(2,1)S(1)} %get-tuple-element.27.keys), channel_id=1, source_target_pairs={{0,4},{4,8},{8,12},{12,0},{1,5},{5,9},{9,13},{13,1},{2,6},{6,10},{... | collective-permute-start | bytes 442376 | tf_op jit(solution)/shard_map/ppermute | solution.py:40
  4.8 11.3 %collective-permute-start = (bf16[576,128]{1,0:T(8,128)(2,1)S(1)}, bf16[576,128]{1,0:T(8,128)(2,1)S(1)}, u32[]{:S(2)}, u32[]{:S(2)}) collective-permute-start(bf16[576,128]{1,0:T(8,128)(2,1)S(1)} %get-tuple-element.26.values), channel_id=1, source_target_pairs={{0,12},{4,0},{8,4},{12,8},{1,13},{5,1},{9,5},{13,9},{2,14},{6,2},{... | collective-permute-start | bytes 442376 | tf_op jit(solution)/shard_map/ppermute | solution.py:40
  6.9 2.2 %copy-start.1 = (bf16[1024,2048]{1,0:T(8,128)(2,1)S(1)}, bf16[1024,2048]{1,0:T(8,128)(2,1)}, u32[]{:S(2)}) copy-start(bf16[1024,2048]{1,0:T(8,128)(2,1)} %weight.3) | copy-start | bytes 12582916
  9.1 10.8 %copy-start.7 = (bf16[1,64,1024]{2,1,0:T(8,128)(2,1)S(1)}, bf16[1,64,1024]{2,1,0:T(8,128)(2,1)}, u32[]{:S(2)}) copy-start(bf16[1,64,1024]{2,1,0:T(8,128)(2,1)} %param.10) | copy-start | bytes 393220
  9.1 10.8 %copy-start.8 = (s32[1,4]{1,0:T(1,128)S(1)}, s32[1,4]{1,0:T(1,128)}, u32[]{:S(2)}) copy-start(s32[1,4]{1,0:T(1,128)} %param.12) | copy-start | bytes 52
  9.1 12.1 %collective-permute-start.4 = (bf16[576,128]{1,0:T(8,128)(2,1)S(1)}, bf16[576,128]{1,0:T(8,128)(2,1)S(1)}, u32[]{:S(2)}, u32[]{:S(2)}) collective-permute-start(bf16[576,128]{1,0:T(8,128)(2,1)S(1)} %get-tuple-element.26.values), channel_id=1, source_target_pairs={{0,4},{4,8},{8,12},{12,0},{1,5},{5,9},{9,13},{13,1},{2,6},{6,10},{... | collective-permute-start | bytes 442376 | tf_op jit(solution)/shard_map/ppermute | solution.py:40
  11.6 9.7 %collective-permute-start.5 = (bf16[576,128]{1,0:T(8,128)(2,1)S(1)}, bf16[576,128]{1,0:T(8,128)(2,1)S(1)}, u32[]{:S(2)}, u32[]{:S(2)}) collective-permute-start(bf16[576,128]{1,0:T(8,128)(2,1)S(1)} %get-tuple-element.27.keys), channel_id=1, source_target_pairs={{0,12},{4,0},{8,4},{12,8},{1,13},{5,1},{9,5},{13,9},{2,14},{6,2},{... | collective-permute-start | bytes 442376 | tf_op jit(solution)/shard_map/ppermute | solution.py:40
  16.1 8.6 %collective-permute-start.3 = (bf16[576,128]{1,0:T(8,128)(2,1)S(1)}, bf16[576,128]{1,0:T(8,128)(2,1)S(1)}, u32[]{:S(2)}, u32[]{:S(2)}) collective-permute-start(bf16[576,128]{1,0:T(8,128)(2,1)S(1)} %collective-permute-done.2.refs_0_), channel_id=1, source_target_pairs={{0,4},{4,8},{8,12},{12,0},{1,5},{5,9},{9,13},{13,1},{2,6},{6,10},{... | collective-permute-start | bytes 442376 | tf_op jit(solution)/shard_map/ppermute | solution.py:40
  16.1 10.5 %collective-permute-start.1 = (bf16[576,128]{1,0:T(8,128)(2,1)S(1)}, bf16[576,128]{1,0:T(8,128)(2,1)S(1)}, u32[]{:S(2)}, u32[]{:S(2)}) collective-permute-start(bf16[576,128]{1,0:T(8,128)(2,1)S(1)} %collective-permute-done.refs_3_), channel_id=1, source_target_pairs={{0,12},{4,0},{8,4},{12,8},{1,13},{5,1},{9,5},{13,9},{2,14},{6,2},{... | collective-permute-start | bytes 442376 | tf_op jit(solution)/shard_map/ppermute | solution.py:40
  19.9 6.7 %copy-start.2 = (bf16[1024,2048]{1,0:T(8,128)(2,1)S(1)}, bf16[1024,2048]{1,0:T(8,128)(2,1)}, u32[]{:S(2)}) copy-start(bf16[1024,2048]{1,0:T(8,128)(2,1)} %weight.3) | copy-start | bytes 12582916
  25.3 8.7 %copy-start.3 = (bf16[1,16,2048]{2,1,0:T(8,128)(2,1)S(1)}, bf16[1,16,2048]{2,1,0:T(8,128)(2,1)}, u32[]{:S(2)}) copy-start(bf16[1,16,2048]{2,1,0:T(8,128)(2,1)} %param.13) | copy-start | bytes 196612
  25.3 8.7 %copy-start.4 = (f32[2048]{0:T(1024)S(1)}, f32[2048]{0:T(1024)}, u32[]{:S(2)}) copy-start(f32[2048]{0:T(1024)} %param.15) | copy-start | bytes 24580
  25.4 8.7 %copy-start.5 = (s32[1,16,8]{1,2,0:T(8,128)S(1)}, s32[1,16,8]{1,2,0:T(8,128)}, u32[]{:S(2)}) copy-start(s32[1,16,8]{1,2,0:T(8,128)} %param.16) | copy-start | bytes 1540
  25.4 8.7 %copy-start.6 = (f32[1,16,8]{1,2,0:T(8,128)S(1)}, f32[1,16,8]{1,2,0:T(8,128)}, u32[]{:S(2)}) copy-start(f32[1,16,8]{1,2,0:T(8,128)} %param.17) | copy-start | bytes 1540
  28.3 7.2 %copy-start = (bf16[1,384,2048]{2,1,0:T(8,128)(2,1)S(1)}, bf16[1,384,2048]{2,1,0:T(8,128)(2,1)}, u32[]{:S(2)}) copy-start(bf16[1,384,2048]{2,1,0:T(8,128)(2,1)} %refs_2_.1) | copy-start | bytes 4718596
  28.3 1.3 %collective-permute-start.6 = (bf16[2,1,16,2048]{3,2,1,0:T(8,128)(2,1)S(1)}, bf16[2,1,16,2048]{3,2,1,0:T(8,128)(2,1)S(1)}, u32[]{:S(2)}, u32[]{:S(2)}) collective-permute-start(bf16[2,1,16,2048]{3,2,1,0:T(8,128)(2,1)S(1)} %bitcast.54), channel_id=1, source_target_pairs={{0,1},{1,0},{2,3},{3,2},{4,5},{5,4},{6,7},{7,6},{8,9},{9,8},{10,11... | collective-permute-start | bytes 393224 | tf_op jit(solution)/shard_map/ppermute | solution.py:35
  29.7 4.3 %collective-permute-start.7 = (bf16[1,1,16,2048]{3,2,1,0:T(8,128)(2,1)S(1)}, bf16[1,1,16,2048]{3,2,1,0:T(8,128)(2,1)S(1)}, u32[]{:S(2)}, u32[]{:S(2)}) collective-permute-start(bf16[1,1,16,2048]{3,2,1,0:T(8,128)(2,1)S(1)} %slice.79), channel_id=1, source_target_pairs={{0,2},{1,3},{2,0},{3,1},{4,6},{5,7},{6,4},{7,5},{8,10},{9,11},{10,... | collective-permute-start | bytes 196616 | tf_op jit(solution)/shard_map/ppermute | solution.py:35
  34.0 13.1 %copy-start.9 = (bf16[1,2048,2,384]{3,2,1,0:T(2,128)(2,1)S(1)}, bf16[1,2048,2,384]{3,2,1,0:T(2,128)(2,1)}, u32[]{:S(2)}) copy-start(bf16[1,2048,2,384]{3,2,1,0:T(2,128)(2,1)} %param.18) | copy-start | bytes 9437188
  34.3 4.4 %collective-permute-start.11 = (bf16[16,2176]{1,0:T(8,128)(2,1)S(1)}, bf16[16,2176]{1,0:T(8,128)(2,1)S(1)}, u32[]{:S(2)}, u32[]{:S(2)}) collective-permute-start(bf16[16,2176]{1,0:T(8,128)(2,1)S(1)} %get-tuple-element.42), channel_id=1, source_target_pairs={{0,4},{4,0},{8,12},{12,8},{1,5},{5,1},{9,13},{13,9},{2,6},{6,2},{1... | collective-permute-start | bytes 208904 | tf_op jit(solution)/shard_map/ppermute | solution.py:35
  35.5 12.3 %collective-permute-start.15 = (bf16[1,384,2048]{2,1,0:T(8,128)(2,1)S(1)}, bf16[1,384,2048]{2,1,0:T(8,128)(2,1)S(1)}, u32[]{:S(2)}, u32[]{:S(2)}) collective-permute-start(bf16[1,384,2048]{2,1,0:T(8,128)(2,1)S(1)} %copy-done), channel_id=1, source_target_pairs={{0,1},{1,0},{2,3},{3,2},{4,5},{5,4},{6,7},{7,6},{8,9},{9,8},{10,11... | collective-permute-start | bytes 4718600 | tf_op jit(solution)/shard_map/ppermute | solution.py:35
  35.5 6.9 %collective-permute-start.10 = (bf16[16,2176]{1,0:T(8,128)(2,1)S(1)}, bf16[16,2176]{1,0:T(8,128)(2,1)S(1)}, u32[]{:S(2)}, u32[]{:S(2)}) collective-permute-start(bf16[16,2176]{1,0:T(8,128)(2,1)S(1)} %get-tuple-element.42), channel_id=1, source_target_pairs={{0,12},{4,8},{8,4},{12,0},{1,13},{5,9},{9,5},{13,1},{2,14},{6,10},... | collective-permute-start | bytes 208904 | tf_op jit(solution)/shard_map/ppermute | solution.py:35
  37.1 7.8 %collective-permute-start.9 = (bf16[16,2176]{1,0:T(8,128)(2,1)S(1)}, bf16[16,2176]{1,0:T(8,128)(2,1)S(1)}, u32[]{:S(2)}, u32[]{:S(2)}) collective-permute-start(bf16[16,2176]{1,0:T(8,128)(2,1)S(1)} %get-tuple-element.42), channel_id=1, source_target_pairs={{0,8},{4,12},{8,0},{12,4},{1,9},{5,13},{9,1},{13,5},{2,10},{6,14},... | collective-permute-start | bytes 208904 | tf_op jit(solution)/shard_map/ppermute | solution.py:35
  38.7 6.3 %collective-permute-start.12 = (bf16[32,2176]{1,0:T(8,128)(2,1)S(1)}, bf16[32,2176]{1,0:T(8,128)(2,1)S(1)}, u32[]{:S(2)}, u32[]{:S(2)}) collective-permute-start(bf16[32,2176]{1,0:T(8,128)(2,1)S(1)} %pad_maximum_fusion), channel_id=1, source_target_pairs={{0,2},{1,3},{2,0},{3,1},{4,6},{5,7},{6,4},{7,5},{8,10},{9,11},{10,... | collective-permute-start | bytes 417800 | tf_op jit(solution)/shard_map/ppermute | solution.py:35
  42.4 7.0 %collective-permute-start.14 = (bf16[16,2176]{1,0:T(8,128)(2,1)S(1)}, bf16[16,2176]{1,0:T(8,128)(2,1)S(1)}, u32[]{:S(2)}, u32[]{:S(2)}) collective-permute-start(bf16[16,2176]{1,0:T(8,128)(2,1)S(1)} %collective-permute-done.10), channel_id=1, source_target_pairs={{0,2},{1,3},{2,0},{3,1},{4,6},{5,7},{6,4},{7,5},{8,10},{9,11},{10,... | collective-permute-start | bytes 208904 | tf_op jit(solution)/shard_map/ppermute | solution.py:35
  45.0 4.4 %collective-permute-start.13 = (bf16[16,2176]{1,0:T(8,128)(2,1)S(1)}, bf16[16,2176]{1,0:T(8,128)(2,1)S(1)}, u32[]{:S(2)}, u32[]{:S(2)}) collective-permute-start(bf16[16,2176]{1,0:T(8,128)(2,1)S(1)} %collective-permute-done.9), channel_id=1, source_target_pairs={{0,2},{1,3},{2,0},{3,1},{4,6},{5,7},{6,4},{7,5},{8,10},{9,11},{10,... | collective-permute-start | bytes 208904 | tf_op jit(solution)/shard_map/ppermute | solution.py:35
  48.5 5.6 %collective-permute-start.16 = (bf16[32,2048]{1,0:T(8,128)(2,1)S(1)}, bf16[32,2048]{1,0:T(8,128)(2,1)S(1)}, u32[]{:S(2)}, u32[]{:S(2)}) collective-permute-start(bf16[32,2048]{1,0:T(8,128)(2,1)S(1)} %shard_map.120), channel_id=1, source_target_pairs={{0,2},{1,3},{2,0},{3,1},{4,6},{5,7},{6,4},{7,5},{8,10},{9,11},{10,... | collective-permute-start | bytes 393224 | tf_op jit(solution)/shard_map/ppermute | solution.py:35
  51.4 5.1 %collective-permute-start.17 = (bf16[32,2048]{1,0:T(8,128)(2,1)S(1)}, bf16[32,2048]{1,0:T(8,128)(2,1)S(1)}, u32[]{:S(2)}, u32[]{:S(2)}) collective-permute-start(bf16[32,2048]{1,0:T(8,128)(2,1)S(1)} %get-tuple-element.47), channel_id=1, source_target_pairs={{0,2},{1,3},{2,0},{3,1},{4,6},{5,7},{6,4},{7,5},{8,10},{9,11},{10,... | collective-permute-start | bytes 393224 | tf_op jit(solution)/shard_map/ppermute | solution.py:35
  54.1 6.2 %collective-permute-start.20 = (bf16[16,2048]{1,0:T(8,128)(2,1)S(1)}, bf16[16,2048]{1,0:T(8,128)(2,1)S(1)}, u32[]{:S(2)}, u32[]{:S(2)}) collective-permute-start(bf16[16,2048]{1,0:T(8,128)(2,1)S(1)} %slice.78), channel_id=1, source_target_pairs={{0,4},{4,0},{8,12},{12,8},{1,5},{5,1},{9,13},{13,9},{2,6},{6,2},{1... | collective-permute-start | bytes 196616 | tf_op jit(solution)/shard_map/ppermute | solution.py:35
  56.6 6.3 %collective-permute-start.18 = (bf16[16,2048]{1,0:T(8,128)(2,1)S(1)}, bf16[16,2048]{1,0:T(8,128)(2,1)S(1)}, u32[]{:S(2)}, u32[]{:S(2)}) collective-permute-start(bf16[16,2048]{1,0:T(8,128)(2,1)S(1)} %get-tuple-element.50), channel_id=1, source_target_pairs={{0,8},{4,12},{8,0},{12,4},{1,9},{5,13},{9,1},{13,5},{2,10},{6,14},... | collective-permute-start | bytes 196616 | tf_op jit(solution)/shard_map/ppermute | solution.py:35
  58.8 6.1 %collective-permute-start.19 = (bf16[16,2048]{1,0:T(8,128)(2,1)S(1)}, bf16[16,2048]{1,0:T(8,128)(2,1)S(1)}, u32[]{:S(2)}, u32[]{:S(2)}) collective-permute-start(bf16[16,2048]{1,0:T(8,128)(2,1)S(1)} %get-tuple-element.51), channel_id=1, source_target_pairs={{0,12},{4,8},{8,4},{12,0},{1,13},{5,9},{9,5},{13,1},{2,14},{6,10},... | collective-permute-start | bytes 196616 | tf_op jit(solution)/shard_map/ppermute | solution.py:35
